TPU v7x, 32 devices: a whole 2x2x4 slice. The times are simulated.
32 devices in a mesh: parts: 2 (over x), dp: 16 (over z, y, core).
Axes of the slice: x: 2, y: 2, z: 4, core: 2. Of those that a mesh axis runs over, the one named last changes fastest.
Arguments:
- hidden_state_input: bfloat16 [8192, 5120], P(('parts', 'dp')), parts along dimension 0, may hold values from -6 to 6
- attention_mixed_state: bfloat16 [8192, 5120], P(('parts', 'dp')), parts along dimension 0, may hold values from -6 to 6
- hidden_state_adjoint: bfloat16 [8192, 5120], P(('parts', 'dp')), parts along dimension 0, may hold values from -6 to 6
- attention_values_adjoint: bfloat16 [8192, 2560], P(('parts', 'dp')), parts along dimension 0, may hold values from -6 to 6
- sequence_token_counts: int32 [32, 2], P(('parts', 'dp')), parts along dimension 0, may hold values from 64 to 192, as said below
- heldout_sketched_signals: bfloat16 [128, 8192], P('dp'), may hold values from -6 to 6
- benchmark_labels: int32 [128, 1], P('dp'), may hold values from 0 to 2
- top_rmsnorm_weights: float32 [5120], replicated, may hold values from 0.5 to 1.5
- top_reducer_matrix: bfloat16 [5120, 128], P('dp'), may hold values from -0.078125 to 0.078125
- top_expander_matrix: bfloat16 [128, 2560], P(None, 'dp'), may hold values from -0.5 to 0.5
- bottom_reducer_matrix: bfloat16 [5120, 128], P('dp'), may hold values from -0.078125 to 0.078125
- bottom_expander_matrix: bfloat16 [128, 5120], P(None, 'dp'), may hold values from -0.5 to 0.5
- source_sketch: bfloat16 [5120, 64], replicated, may hold values from -0.078125 to 0.078125
- top_reducer_sketch: bfloat16 [128, 128], replicated, may hold values from -0.5 to 0.5
- top_expander_sketch: bfloat16 [128, 64], replicated, may hold values from -0.5 to 0.5
- top_target_sketch: bfloat16 [2560, 128], replicated, may hold values from -0.125 to 0.125
- bottom_reducer_sketch: bfloat16 [128, 128], replicated, may hold values from -0.5 to 0.5
- bottom_expander_sketch: bfloat16 [128, 64], replicated, may hold values from -0.5 to 0.5
- bottom_target_sketch: bfloat16 [5120, 128], replicated, may hold values from -0.078125 to 0.078125
Outputs:
- scores: float32 [64], P(('parts', 'dp')), parts along dimension 0
- task_best: float32 [64, 3], P(('parts', 'dp')), parts along dimension 0
There are 2 independent parts, one for each index of `parts`. A program takes and returns all parts, laid end to end along the dimension named above; an argument that names none is the same for every part. Nothing has to cross between parts.
Inputs may be any that keep to these rules, and one draw needn't show every extreme that they name: `sequence_token_counts`: each row sums to 256, and one entry of each row, at a drawn place, is 192. `benchmark_labels`: every task is named by some validation example.
All inputs are finite; a program needn't handle non-finite values.
Results may differ from a plain program's by a relative error of at most 0.0033.
Values may be sent and summed in bfloat16 or wider, within the bound.
No kernel may reach another device: no remote copies, remote signals or barrier semaphores. Data moves between devices by JAX's collectives and lax.ppermute only.
A program may use at most 128 MiB of HBM per device.

v0:
```python
import jax
import jax.numpy as jnp
from jax import lax
from jax.sharding import PartitionSpec as P

TASKS = 3


alpha_multiplier = 4.0


def sketch_summands(
    inputs, gradient_list, down, up_factor, proj_left, adapter_rank_down, rank_b, projection_output
):
    reduced = jnp.dot(inputs, down, preferred_element_type=jnp.float32).astype(jnp.bfloat16)
    returned_gradient = lax.dot_general(
        gradient_list, up_factor, (((1,), (1,)), ((), ())), preferred_element_type=jnp.float32
    ).astype(jnp.bfloat16)
    first_a = jnp.dot(inputs, proj_left, preferred_element_type=jnp.float32)
    first_b = jnp.dot(reduced, rank_b, preferred_element_type=jnp.float32)
    second_layer_down = alpha_multiplier * jnp.dot(
        returned_gradient, adapter_rank_down, preferred_element_type=jnp.float32
    )
    second_layer_up = alpha_multiplier * jnp.dot(
        gradient_list, projection_output, preferred_element_type=jnp.float32
    )
    return (returned_gradient, first_a, first_b, second_layer_down, second_layer_up)


def example_features(lefts, rights, token_count_vector):
    tokens_count = lefts[0].shape[0]
    left_stack = jnp.stack(lefts, axis=1).astype(jnp.bfloat16)
    right_stack = jnp.stack(rights, axis=1).astype(jnp.bfloat16)
    ends = jnp.cumsum(token_count_vector)
    starts = ends - token_count_vector
    places = jnp.arange(tokens_count, dtype=jnp.int32)[:, None]
    member = ((places >= starts[None, :]) & (places < ends[None, :])).astype(jnp.bfloat16)
    count_ex = member.shape[1]
    width_left = left_stack.shape[2]
    spread = (member[:, None, :, None] * left_stack[:, :, None, :]).reshape(
        tokens_count * 4, count_ex * width_left
    )
    rights_flat = right_stack.reshape(tokens_count * 4, right_stack.shape[2])
    feats = lax.dot_general(
        spread, rights_flat, (((0,), (0,)), ((), ())), preferred_element_type=jnp.float32
    )
    feats = feats.reshape(count_ex, -1)
    squares = jnp.sum(feats * feats, axis=1, keepdims=True)
    return (feats * lax.rsqrt(squares + 1e-06)).astype(jnp.bfloat16)


def task_maxima(pool_rows, panel, panel_tasks, score_scale):
    similar = score_scale * lax.dot_general(
        pool_rows, panel, (((1,), (1,)), ((), ())), preferred_element_type=jnp.float32
    )
    task_mask = panel_tasks == jnp.arange(TASKS, dtype=jnp.int32)[None, :]
    return jnp.max(
        jnp.where(task_mask[None, :, :], similar[:, :, None], -2.0 * score_scale), axis=1
    )


def shards(
    hidden_state_input,
    attention_mixed_state,
    hidden_state_adjoint,
    attention_values_adjoint,
    sequence_token_counts,
    heldout_sketched_signals,
    benchmark_labels,
    top_rmsnorm_weights,
    top_reducer_matrix,
    top_expander_matrix,
    bottom_reducer_matrix,
    bottom_expander_matrix,
    source_sketch,
    top_reducer_sketch,
    top_expander_sketch,
    top_target_sketch,
    bottom_reducer_sketch,
    bottom_expander_sketch,
    bottom_target_sketch,
):
    down_upper_all, down_lower_all, up_upper_all, up_lower_all = (
        lax.all_gather(top_reducer_matrix, "dp", axis=0, tiled=True),
        lax.all_gather(bottom_reducer_matrix, "dp", axis=0, tiled=True),
        lax.all_gather(top_expander_matrix, "dp", axis=1, tiled=True),
        lax.all_gather(bottom_expander_matrix, "dp", axis=1, tiled=True),
    )
    wide = hidden_state_input.astype(jnp.float32)
    inverse = lax.rsqrt(jnp.mean(wide * wide, axis=1, keepdims=True) + 1e-05)
    unit_stream = wide * inverse
    rescaled_hidden = (unit_stream * top_rmsnorm_weights[None, :]).astype(jnp.bfloat16)
    val_wide = heldout_sketched_signals.astype(jnp.float32)
    val_unit = (
        val_wide * lax.rsqrt(jnp.sum(val_wide * val_wide, axis=1, keepdims=True) + 1e-06)
    ).astype(jnp.bfloat16)
    (
        top_branch_adjoint,
        initial_left_operand,
        latter_left_operand,
        initial_right_operand,
        latter_right_operand,
    ) = sketch_summands(
        rescaled_hidden,
        attention_values_adjoint,
        down_upper_all,
        up_upper_all,
        source_sketch,
        top_reducer_sketch,
        top_expander_sketch,
        top_target_sketch,
    )
    branch_sensitivity = alpha_multiplier * lax.dot_general(
        top_branch_adjoint,
        down_upper_all,
        (((1,), (1,)), ((), ())),
        preferred_element_type=jnp.float32,
    )
    gain_applied = branch_sensitivity * top_rmsnorm_weights[None, :]
    along = jnp.mean(gain_applied * unit_stream, axis=1, keepdims=True)
    lower_grad = (
        hidden_state_adjoint.astype(jnp.float32) + inverse * (gain_applied - unit_stream * along)
    ).astype(jnp.bfloat16)
    returned_lower, left_three, left_four, right_three, right_four = sketch_summands(
        attention_mixed_state,
        lower_grad,
        down_lower_all,
        up_lower_all,
        source_sketch,
        bottom_reducer_sketch,
        bottom_expander_sketch,
        bottom_target_sketch,
    )
    unit_rows = example_features(
        (initial_left_operand, latter_left_operand, left_three, left_four),
        (initial_right_operand, latter_right_operand, right_three, right_four),
        sequence_token_counts[0],
    )
    count_ex = unit_rows.shape[0]
    score_scale = float(unit_rows.shape[1]) ** 0.5
    initial = jnp.full((count_ex, TASKS), -2.0 * score_scale, jnp.float32)
    task_best = jnp.maximum(
        initial,
        task_maxima(
            unit_rows,
            lax.all_gather(val_unit, "dp", axis=0, tiled=True),
            lax.all_gather(benchmark_labels, "dp", axis=0, tiled=True),
            score_scale,
        ),
    )
    scores = jnp.mean(task_best, axis=1)
    return (scores, task_best)


def solution(mesh):
    placed = (
        P(("parts", "dp"), None),
        P(("parts", "dp"), None),
        P(("parts", "dp"), None),
        P(("parts", "dp"), None),
        P(("parts", "dp"), None),
        P("dp", None),
        P("dp", None),
        P(),
        P("dp", None),
        P(None, "dp"),
        P("dp", None),
        P(None, "dp"),
        P(),
        P(),
        P(),
        P(),
        P(),
        P(),
        P(),
    )
    return jax.shard_map(
        shards,
        mesh=mesh,
        in_specs=placed,
        out_specs=(P(("parts", "dp")), P(("parts", "dp"), None)),
        check_vma=False,
    )
```

profile of v0, /device:TPU:0, one launch (start us, length us, event | category | flops | bytes accessed | tf_op | source)
XLA Modules:
  0.0 185.5 jit_solution(7172701821815110174)
XLA Ops:
  7.2 0.7 all-gather.5.cloned.1.call-update
  8.0 0.7 all-gather.9.cloned.1.call-update
  8.7 0.7 all-gather.7.cloned.1.call-update
  9.5 1.1 fusion.29
  10.6 1.6 fusion.30
  12.3 2.5 %fusion.9 = f32[256]{0:T(256)S(1)} fusion(bf16[256,5120]{1,0:T(8,128)(2,1)} %param.19), kind=kLoop, calls=%fused_computation.12 | loop fusion | flops 3931904 | bytes 2622464 | tf_op jit(solution)/shard_map/reduce_sum | solution.py:90
  14.8 25.5 %all_gather.21 = bf16[128,2560]{0,1:T(8,128)(2,1)S(1)} all-gather(bf16[128,160]{0,1:T(8,128)(2,1)S(1)} %copy-done.9), channel_id=1, replica_groups=mesh['parts'=2,'dp'=16] {'dp'}, dimensions={1}, use_global_device_ids=true | all-gather | bytes 696320 | tf_op jit(solution)/shard_map/all_gather | solution.py:86
  40.3 0.5 convolution_convert_fusion.1
  40.8 0.5 fusion.19
  41.3 1.0 fusion.22
  42.4 0.9 fusion.23
  43.7 0.6 dynamic-slice
  45.1 7.1 %all-reduce = s32[128]{0:T(128)S(1)} all-reduce(s32[128]{0:T(128)S(1)} %bitcast_dynamic-update-slice_fusion), channel_id=1, replica_groups=mesh['parts'=2,'dp'=16] {'dp'}, use_global_device_ids=true, to_apply=%add | all-reduce | flops 128 | bytes 1024
  52.3 1.1 all-gather.5.cloned.1.call-done
  53.4 3.4 %fusion.4 = (f32[256]{0:T(256)S(1)}, f32[256,5120]{1,0:T(8,128)S(1)}) fusion(bf16[256,5120]{1,0:T(8,128)(2,1)} %param.19, f32[256]{0:T(256)S(1)} %add_rsqrt_fusion, f32[5120]{0:T(1024)S(1)} %broadcast_multiply_fusion.1, bf16[256,128]{1,0:T(8,128)(2,1)S(1)} %convolution_convert_fusion.1, bf16[5120,128]{1,0:T(8,128)(2,1)} %all-gather.5.cloned.1.call-done), kind=kOutput, calls=%fused_computation.7 | convolution fusion | flops 342097664 | bytes 9263104 | tf_op jit(solution)/shard_map/dot_general | solution.py:113
  56.8 0.3 copy-done.5
  57.1 1.7 fusion.8
  58.8 1.5 copy-done.3
  60.3 0.8 fusion.18
  61.2 32.1 %all-gather.9.cloned.1.call-done = bf16[128,5120]{0,1:T(8,128)(2,1)} async-done(((bf16[128,320]{0,1:T(8,128)(2,1)}), bf16[128,5120]{0,1:T(8,128)(2,1)}) %all-gather.9.cloned.1.call-update) | async-done | bytes 1310736 | tf_op jit(solution)/shard_map/all_gather | solution.py:87
  93.2 3.1 %fusion.14 = bf16[256,1,128]{2,0,1:T(8,128)(2,1)S(1)} fusion(bf16[128,128]{1,0:T(8,128)(2,1)S(1)} %copy-done.10, bf16[256,5120]{1,0:T(8,128)(2,1)} %copy-done.3, bf16[128,5120]{0,1:T(8,128)(2,1)} %all-gather.9.cloned.1.call-done), kind=kOutput, calls=%fused_computation.25 | convolution fusion | flops 344031232 | bytes 4030464 | tf_op jit(solution)/shard_map/dot_general | solution.py:21
  96.4 0.9 copy.31
  97.3 35.9 %all-gather.7.cloned.1.call-done = bf16[5120,128]{1,0:T(8,128)(2,1)} async-done(((bf16[320,128]{1,0:T(8,128)(2,1)}), bf16[5120,128]{1,0:T(8,128)(2,1)}) %all-gather.7.cloned.1.call-update) | async-done | bytes 1310736 | tf_op jit(solution)/shard_map/all_gather | solution.py:85
  133.2 2.3 %fusion.25 = bf16[256,1,64]{0,2,1:T(8,128)(2,1)S(1)} fusion(bf16[128,64]{0,1:T(8,128)(2,1)S(1)} %copy-done.13, bf16[256,5120]{1,0:T(8,128)(2,1)S(1)} %copy-done, bf16[5120,128]{1,0:T(8,128)(2,1)} %all-gather.7.cloned.1.call-done), kind=kOutput, calls=%fused_computation.38 | convolution fusion | flops 339787776 | bytes 3981312 | tf_op jit(solution)/shard_map/dot_general | solution.py:20
  135.5 3.2 %fusion.24 = bf16[256,1,64]{0,2,1:T(8,128)(2,1)S(1)} fusion(bf16[128,64]{0,1:T(8,128)(2,1)S(1)} %copy-done.14, bf16[5120,128]{1,0:T(8,128)(2,1)} %all-gather.5.cloned.1.call-done, bf16[256,5120]{1,0:T(8,128)(2,1)} %param.19, f32[5120]{0:T(1024)S(1)} %copy-done.12, f32[256]{0:T(256)S(1)} %add_rsqrt_fusion), kind=kOutput, calls=%fused_computation.37 | convolution fusion | flops 345030656 | bytes 4002816 | tf_op jit(solution)/shard_map/dot_general | solution.py:20
  138.9 0.6 broadcast_multiply_fusion
  139.5 0.2 mul.122
  139.8 1.2 multiply_reduce_fusion
  141.4 34.0 %all-gather.11.cloned.1.call-done = bf16[128,8192]{1,0:T(8,128)(2,1)} async-done(((bf16[8,8192]{1,0:T(8,128)(2,1)}), bf16[128,8192]{1,0:T(8,128)(2,1)}) %all-gather.11.cloned.1.call-update) | async-done | bytes 2097168 | tf_op jit(solution)/shard_map/all_gather | solution.py:146
  175.4 2.3 %convolution_multiply_fusion.5 = f32[2,128]{1,0:T(2,128)S(1)} fusion(bf16[128,8192]{1,0:T(8,128)(2,1)} %all-gather.11.cloned.1.call-done, f32[2,8192]{1,0:T(2,128)S(1)} %reshape.165, f32[2]{0:T(128)S(1)} %add_rsqrt_fusion.2), kind=kOutput, calls=%fused_computation.39 | convolution fusion | flops 4227328 | bytes 2163720 | tf_op jit(solution)/shard_map/dot_general | solution.py:53
  177.8 0.7 copy.33
  178.4 0.5 broadcast_multiply_fusion.3
  (61 shorter events, 1.7 us)
Async XLA Ops:
  7.2 35.1 %copy-start = (bf16[256,5120]{1,0:T(8,128)(2,1)S(1)}, bf16[256,5120]{1,0:T(8,128)(2,1)}, u32[]{:S(2)}) copy-start(bf16[256,5120]{1,0:T(8,128)(2,1)} %param.20) | copy-start | bytes 7864324
  7.2 7.6 %copy-start.9 = (bf16[128,160]{0,1:T(8,128)(2,1)S(1)}, bf16[128,160]{0,1:T(8,128)(2,1)}, u32[]{:S(2)}) copy-start(bf16[128,160]{0,1:T(8,128)(2,1)} %param.28) | copy-start | bytes 122884
  7.2 33.1 %copy-start.12 = (f32[5120]{0:T(1024)S(1)}, f32[5120]{0:T(1024)}, u32[]{:S(2)}) copy-start(f32[5120]{0:T(1024)} %param.26) | copy-start | bytes 61444
  7.2 46.2 %all-gather.5.cloned.1.call-start = ((), (), s32[]{:S(2)}) async-start(), calls=%async_computation | async-start | bytes 1392640 | tf_op jit(solution)/shard_map/all_gather | solution.py:84
  7.9 85.3 %all-gather.9.cloned.1.call-start = ((), (), s32[]{:S(2)}) async-start(), calls=%async_computation.2 | async-start | bytes 1392640 | tf_op jit(solution)/shard_map/all_gather | solution.py:87
  8.7 124.5 %all-gather.7.cloned.1.call-start = ((), (), s32[]{:S(2)}) async-start(), calls=%async_computation.1 | async-start | bytes 1392640 | tf_op jit(solution)/shard_map/all_gather | solution.py:85
  9.4 166.0 %all-gather.11.cloned.1.call-start = ((), (), s32[]{:S(2)}) async-start(), calls=%async_computation.3 | async-start | bytes 2228224 | tf_op jit(solution)/shard_map/all_gather | solution.py:146
  12.2 28.0 %copy-start.4 = (bf16[256,2560]{1,0:T(8,128)(2,1)S(1)}, bf16[256,2560]{1,0:T(8,128)(2,1)}, u32[]{:S(2)}) copy-start(bf16[256,2560]{1,0:T(8,128)(2,1)} %param.22) | copy-start | bytes 3932164
  12.2 28.5 %copy-start.8 = (bf16[2560,128]{1,0:T(8,128)(2,1)S(1)}, bf16[2560,128]{1,0:T(8,128)(2,1)}, u32[]{:S(2)}) copy-start(bf16[2560,128]{1,0:T(8,128)(2,1)} %param.34) | copy-start | bytes 1966084
  14.7 26.6 %copy-start.1 = (bf16[256,5120]{1,0:T(8,128)(2,1)S(1)}, bf16[256,5120]{1,0:T(8,128)(2,1)}, u32[]{:S(2)}) copy-start(bf16[256,5120]{1,0:T(8,128)(2,1)} %param.19) | copy-start | bytes 7864324
  14.7 26.6 %copy-start.7 = (bf16[5120,64]{0,1:T(8,128)(2,1)S(1)}, bf16[5120,64]{0,1:T(8,128)(2,1)}, u32[]{:S(2)}) copy-start(bf16[5120,64]{0,1:T(8,128)(2,1)} %param.31) | copy-start | bytes 1966084
  42.3 1.0 copy-start.15
  42.3 1.4 copy-start.17
  42.3 2.6 %copy-start.16 = (s32[8,1]{0,1:T(1,128)S(1)}, s32[8,1]{0,1:T(1,128)}, u32[]{:S(2)}) copy-start(s32[8,1]{0,1:T(1,128)} %param.25) | copy-start | bytes 100
  42.4 9.8 %copy-start.11 = (bf16[128,128]{1,0:T(8,128)(2,1)S(1)}, bf16[128,128]{1,0:T(8,128)(2,1)}, u32[]{:S(2)}) copy-start(bf16[128,128]{1,0:T(8,128)(2,1)} %param.32) | copy-start | bytes 98308
  53.4 3.4 %copy-start.2 = (bf16[256,5120]{1,0:T(8,128)(2,1)S(1)}, bf16[256,5120]{1,0:T(8,128)(2,1)}, u32[]{:S(2)}) copy-start(bf16[256,5120]{1,0:T(8,128)(2,1)} %param.19) | copy-start | bytes 7864324
  53.4 3.7 %copy-start.5 = (bf16[256,5120]{1,0:T(8,128)(2,1)S(1)}, bf16[256,5120]{1,0:T(8,128)(2,1)}, u32[]{:S(2)}) copy-start(bf16[256,5120]{1,0:T(8,128)(2,1)} %param.21) | copy-start | bytes 7864324
  57.1 3.2 %copy-start.6 = (bf16[5120,128]{1,0:T(8,128)(2,1)S(1)}, bf16[5120,128]{1,0:T(8,128)(2,1)}, u32[]{:S(2)}) copy-start(bf16[5120,128]{1,0:T(8,128)(2,1)} %param.37) | copy-start | bytes 3932164
  58.8 1.5 copy-start.3
  60.3 32.9 %copy-start.10 = (bf16[128,128]{1,0:T(8,128)(2,1)S(1)}, bf16[128,128]{1,0:T(8,128)(2,1)}, u32[]{:S(2)}) copy-start(bf16[128,128]{1,0:T(8,128)(2,1)} %param.35) | copy-start | bytes 98308
  61.2 72.0 %copy-start.13 = (bf16[128,64]{0,1:T(8,128)(2,1)S(1)}, bf16[128,64]{0,1:T(8,128)(2,1)}, u32[]{:S(2)}) copy-start(bf16[128,64]{0,1:T(8,128)(2,1)} %param.36) | copy-start | bytes 49156
  96.3 39.1 %copy-start.14 = (bf16[128,64]{0,1:T(8,128)(2,1)S(1)}, bf16[128,64]{0,1:T(8,128)(2,1)}, u32[]{:S(2)}) copy-start(bf16[128,64]{0,1:T(8,128)(2,1)} %param.33) | copy-start | bytes 49156
Sparse Core Ops, SparseCore 0:
  10.3 43.0 all-gather.4
  55.7 37.5 all-gather.8
  95.5 37.6 all-gather.6
  135.2 40.1 all-gather.10
where the time goes:
time: 186 us; the launch traced here: 185 us
  waiting for transfers between devices  105 us (56%)
  blocking collectives  32.5 us (17%)
  matrix products  19.3 us (10%)
  between operations  14.7 us (8%)
  other arithmetic  8.63 us (5%)
  local copies, waits for them, and re-layouts  4.94 us (3%)
    all_gather x1, waiting for transfers between devices, shards(): lax.all_gather(bottom_reducer_matrix, 'dp', axis=0, tiled=True)  35.9 us
    all_gather x1, waiting for transfers between devices, shards(): lax.all_gather(val_unit, 'dp', axis=0, tiled=True)  34 us
    all_gather x1, waiting for transfers between devices, shards(): lax.all_gather(bottom_expander_matrix, 'dp', axis=1, tiled=True)  32.1 us
    all_gather x1, blocking collectives, shards(): lax.all_gather(top_expander_matrix, 'dp', axis=1, tiled=True)  25.5 us
    unnamed x1, blocking collectives  7.05 us
    dot_general x2, matrix products, sketch_summands(): first_b = jnp.dot(reduced, rank_b, preferred_element_type=jnp.float32)  5.45 us
  transfers between devices with their start and end apart: 4, of which 4 were waited for; matrix products, arithmetic and copies ran while one was open for 15% of the time, Pallas kernels for 0%

commit v1 on v0

v1 whole, which is shorter than its diff:
```python
import jax
import jax.numpy as jnp
from jax import lax
from jax.sharding import PartitionSpec as P

TASKS = 3
ALPHA = 4.0
F32 = jnp.float32
BF16 = jnp.bfloat16
MOST_RING_CHIPS = 8


def mm(a, b):
    return jnp.dot(a, b, preferred_element_type=F32)


def mm_rows(a, b):
    return lax.dot_general(a, b, (((1,), (1,)), ((), ())), preferred_element_type=F32)


def mm_cols(a, b):
    return lax.dot_general(a, b, (((0,), (0,)), ((), ())), preferred_element_type=F32)


def ring_chip(pos, chips):
    half = chips // 2
    return jnp.where(pos < half, 2 * pos, 2 * (chips - 1 - pos) + 1)


def gather_blocks(block, n):
    chips = n // 2
    if chips > MOST_RING_CHIPS:
        return lax.all_gather(block, "dp")
    half = chips // 2
    place = [2 * q if q < half else 2 * (chips - 1 - q) + 1 for q in range(chips)]

    def hop(value, step):
        pairs = [
            (2 * place[q] + c, 2 * place[(q + step) % chips] + c)
            for q in range(chips)
            for c in range(2)
        ]
        return lax.ppermute(value, "dp", pairs)

    def other_core(value):
        return lax.ppermute(value, "dp", [(d, d ^ 1) for d in range(n)])

    me = lax.axis_index("dp")
    chip, core = me // 2, me % 2
    row, side = chip // 2, chip % 2
    pos = jnp.where(side == 0, row, chips - 1 - row)
    pieces = [(0, block, 0)]
    up, down = block, block
    middle = (block.shape[0] // 2) // 16 * 16
    for k in range(1, half):
        up, down = hop(up, 1), hop(down, -1)
        pieces += [(-k, up, 0), (k, down, 0)]
    pieces += [(-half, hop(up[:middle], 1), 0), (half, hop(down[middle:], -1), middle)]
    out = jnp.zeros((n,) + block.shape, block.dtype)
    for away, piece, first in pieces:
        base = 2 * ring_chip((pos + away + chips) % chips, chips)
        out = lax.dynamic_update_slice(out, piece[None], (base + core, first, 0))
        out = lax.dynamic_update_slice(out, other_core(piece)[None], (base + 1 - core, first, 0))
    return out


def shards(
    hidden_state_input,
    attention_mixed_state,
    hidden_state_adjoint,
    attention_values_adjoint,
    sequence_token_counts,
    heldout_sketched_signals,
    benchmark_labels,
    top_rmsnorm_weights,
    top_reducer_matrix,
    top_expander_matrix,
    bottom_reducer_matrix,
    bottom_expander_matrix,
    source_sketch,
    top_reducer_sketch,
    top_expander_sketch,
    top_target_sketch,
    bottom_reducer_sketch,
    bottom_expander_sketch,
    bottom_target_sketch,
    n,
):
    me = lax.axis_index("dp")
    x, mixed, adjoint, values = (
        hidden_state_input,
        attention_mixed_state,
        hidden_state_adjoint,
        attention_values_adjoint,
    )
    tokens, width = x.shape
    rows = top_reducer_matrix.shape[0]
    up_rows = top_expander_matrix.shape[1]
    rank = top_reducer_matrix.shape[1]
    k1 = source_sketch.shape[1]
    gain = top_rmsnorm_weights
    own_gain = lax.dynamic_slice_in_dim(gain, me * rows, rows)

    down_upper = (own_gain[:, None] * top_reducer_matrix.astype(F32)).astype(BF16)
    up_lower = mm(bottom_expander_matrix.T, bottom_reducer_sketch).astype(BF16)
    down_lower = mm(bottom_reducer_matrix, bottom_expander_sketch).astype(BF16)
    packed_lower = jnp.concatenate([down_lower[: rows // 2], down_lower[rows // 2 :]], axis=1)
    factors = jnp.concatenate([down_upper, up_lower, top_expander_matrix.T, packed_lower], axis=0)
    factors = gather_blocks(factors, n)

    val_wide = heldout_sketched_signals.astype(F32)
    val_unit = (
        val_wide * lax.rsqrt(jnp.sum(val_wide * val_wide, axis=1, keepdims=True) + 1e-06)
    ).astype(BF16)
    labels = jnp.broadcast_to(benchmark_labels.astype(BF16), (val_unit.shape[0], 128))
    panel = jnp.concatenate([val_unit.reshape(-1, 128), labels], axis=0)
    panel = gather_blocks(panel, n)
    val_rows = val_unit.shape[0]
    cut = panel.shape[1] - val_rows
    panel_tasks = panel[:, cut:, 0].reshape(n * val_rows, 1).astype(jnp.int32)
    panel = panel[:, :cut].reshape(n * val_rows, val_unit.shape[1])

    wide = x.astype(F32)
    inverse = lax.rsqrt(jnp.mean(wide * wide, axis=1, keepdims=True) + 1e-05)
    gained_sketch = (gain[:, None] * source_sketch.astype(F32)).astype(BF16)
    left_one = inverse * mm(x, gained_sketch)
    left_three = mm(mixed, source_sketch)
    right_two = ALPHA * mm(values, top_target_sketch)

    at = 0
    down_upper = factors[:, at : at + rows].reshape(width, rank)
    at += rows
    up_lower = factors[:, at : at + rows].reshape(width, -1)
    at += rows
    up_upper = factors[:, at : at + up_rows].reshape(-1, rank)
    at += up_rows
    down_lower = factors[:, at:]
    down_lower = jnp.concatenate([down_lower[:, :, :k1], down_lower[:, :, k1:]], axis=1)
    down_lower = down_lower.reshape(width, k1)

    reduced = inverse * mm(x, down_upper)
    left_two = mm(reduced.astype(BF16), top_expander_sketch)
    left_four = mm(mixed, down_lower)
    returned = mm(values, up_upper).astype(BF16)
    right_one = ALPHA * mm(returned, top_reducer_sketch)
    along = (ALPHA / width) * jnp.sum(returned.astype(F32) * reduced, axis=1, keepdims=True)
    targets = jnp.concatenate([up_lower, bottom_target_sketch], axis=1)
    bridge = mm_cols(down_upper, targets).astype(BF16)
    rights_low = mm(adjoint, targets) + inverse * (
        ALPHA * mm(returned, bridge) - (along * inverse) * mm(x, targets)
    )
    rights_low = ALPHA * rights_low
    k2 = up_lower.shape[1]
    lefts = (left_one, left_two, left_three, left_four)
    rights = (right_one, right_two, rights_low[:, :k2], rights_low[:, k2:])

    counts = sequence_token_counts[0]
    ends = jnp.cumsum(counts)
    starts = ends - counts
    places = jnp.arange(tokens, dtype=jnp.int32)[:, None]
    member = (places >= starts[None, :]) & (places < ends[None, :])
    count_ex = counts.shape[0]
    spread = jnp.concatenate(lefts, axis=0).astype(BF16)
    member = jnp.tile(member, (4, 1))
    spread = jnp.concatenate(
        [jnp.where(member[:, e : e + 1], spread, 0) for e in range(count_ex)], axis=1
    )
    feats = mm_cols(spread, jnp.concatenate(rights, axis=0).astype(BF16))
    feats = feats.reshape(count_ex, -1)
    squares = jnp.sum(feats * feats, axis=1, keepdims=True)
    unit_rows = (feats * lax.rsqrt(squares + 1e-06)).astype(BF16)

    score_scale = float(unit_rows.shape[1]) ** 0.5
    similar = score_scale * mm_rows(unit_rows, panel)
    task_mask = panel_tasks == jnp.arange(TASKS, dtype=jnp.int32)[None, :]
    task_best = jnp.max(
        jnp.where(task_mask[None, :, :], similar[:, :, None], -2.0 * score_scale), axis=1
    )
    return (jnp.mean(task_best, axis=1), task_best)


def solution(mesh):
    n = mesh.shape["dp"]
    split = P(("parts", "dp"), None)
    by_row, by_column, whole = P("dp", None), P(None, "dp"), P()
    placed = (
        (split,) * 5
        + (by_row, by_row, whole)
        + (by_row, by_column, by_row, by_column)
        + (whole,) * 7
    )
    return jax.shard_map(
        lambda *arrays: shards(*arrays, n),
        mesh=mesh,
        in_specs=placed,
        out_specs=(P(("parts", "dp")), split),
        check_vma=False,
    )
```

time: 186 us -> 112 us (0.60)
  waiting for transfers between devices: 105 us -> 9.6 us
  local copies, waits for them, and re-layouts: 4.94 us -> 49.7 us
  blocking collectives: 32.5 us -> 0 us
  starting transfers between devices: 0.15 us -> 20.7 us
  between operations: 14.7 us -> 1.23 us
  other arithmetic: 8.63 us -> 10.6 us
    all_gather x4 -> x0, waiting for transfers between devices: 103 us -> none  [the longest x1 35.9 us: shards(): lax.all_gather(bottom_reducer_matrix, 'dp', axis=0, tiled=True)]
    dynamic_update_slice x0 -> x34, local copies, waits for them, and re-layouts: none -> 29.6 us  [the longest x18 15.9 us: gather_blocks(): lax.dynamic_update_slice(out, other_core(piece)[None], (base + 1 - core,...]
    all_gather x1 -> x0, blocking collectives: 25.5 us -> none  [shards(): lax.all_gather(top_expander_matrix, 'dp', axis=1, tiled=True)]
    ppermute x0 -> x34, starting transfers between devices: none -> 20.7 us  [the longest x16 16.9 us: hop(): return lax.ppermute(value, 'dp', pairs)]
    ppermute x0 -> x34, waiting for transfers between devices: none -> 9.6 us  [the longest x16 9.55 us: hop(): return lax.ppermute(value, 'dp', pairs)]
    slice x0 -> x11, local copies, waits for them, and re-layouts: none -> 8.49 us  [the longest x1 3.15 us: shards(): panel = panel[:, :cut].reshape(n * val_rows, val_unit.shape[1])]
    unnamed x1 -> x0, blocking collectives: 7.05 us -> none
    broadcast_in_dim x0 -> x2, local copies, waits for them, and re-layouts: none -> 4.27 us  [gather_blocks(): out = jnp.zeros((n,) + block.shape, block.dtype)]
  transfers between devices with their start and end apart: 4 -> 34, of which waited for: 4 -> 4; matrix products, arithmetic and copies ran while one was open for 15% -> 47% of each run, Pallas kernels for 0% -> 0%
where the time goes in v1:
time: 112 us; the launch traced here: 111 us
  local copies, waits for them, and re-layouts  49.7 us (44%)
  starting transfers between devices  20.7 us (18%)
  matrix products  18.9 us (17%)
  other arithmetic  10.6 us (9%)
  waiting for transfers between devices  9.6 us (9%)
  between operations  1.23 us (1%)
    ppermute x16, starting transfers between devices, hop(): return lax.ppermute(value, 'dp', pairs)  16.9 us
    dot_general x13, matrix products, mm(): return jnp.dot(a, b, preferred_element_type=F32)  16.4 us
    dynamic_update_slice x18, local copies, waits for them, and re-layouts, gather_blocks(): lax.dynamic_update_slice(out, other_core(piece)[None], (base + 1 - core,...  15.9 us
    dynamic_update_slice x16, local copies, waits for them, and re-layouts, gather_blocks(): out = lax.dynamic_update_slice(out, piece[None], (base + core, first, 0))  13.7 us
    ppermute x16, waiting for transfers between devices, hop(): return lax.ppermute(value, 'dp', pairs)  9.55 us
    broadcast_in_dim x2, local copies, waits for them, and re-layouts, gather_blocks(): out = jnp.zeros((n,) + block.shape, block.dtype)  4.27 us
    reshape x1, local copies, waits for them, and re-layouts, shards(): panel = panel[:, :cut].reshape(n * val_rows, val_unit.shape[1])  4.18 us
    ppermute x18, starting transfers between devices, other_core(): return lax.ppermute(value, 'dp', [(d, d ^ 1) for d in range(n)])  3.75 us
  transfers between devices with their start and end apart: 34, of which 4 were waited for; matrix products, arithmetic and copies ran while one was open for 47% of the time, Pallas kernels for 0%

profile of v1, /device:TPU:0, one launch (start us, length us, event | category | flops | bytes accessed | tf_op | source)
XLA Modules:
  0.0 110.7 jit_solution(14234123207965851919)
XLA Ops:
  4.8 2.6 %broadcast_in_dim.199 = bf16[16,960,128]{2,1,0:T(8,128)(2,1)} broadcast(bf16[]{:T(256)} %constant.142.clone.1), dimensions={} | broadcast | bytes 3932162 | tf_op jit(solution)/shard_map/broadcast_in_dim | solution.py:59
  8.8 2.6 %collective-permute-start.18 = (bf16[960,128]{1,0:T(8,128)(2,1)}, bf16[960,128]{1,0:T(8,128)(2,1)}, u32[]{:S(2)}, u32[]{:S(2)}) collective-permute-start(bf16[960,128]{1,0:T(8,128)(2,1)} %get-tuple-element.7), channel_id=1, source_target_pairs={{0,4},{1,5},{4,8},{5,9},{8,12},{9,13},{12,14},{13,15},{14,10},{15,... | collective-permute-start | bytes 737288 | tf_op jit(solution)/shard_map/ppermute | solution.py:43
  12.8 1.8 %collective-permute-start.1 = (bf16[520,128]{1,0:T(8,128)(2,1)}, bf16[520,128]{1,0:T(8,128)(2,1)S(1)}, u32[]{:S(2)}, u32[]{:S(2)}) collective-permute-start(bf16[520,128]{1,0:T(8,128)(2,1)} %pad_maximum_fusion.6), channel_id=1, source_target_pairs={{0,4},{1,5},{4,8},{5,9},{8,12},{9,13},{12,14},{13,15},{14,10},{15,... | collective-permute-start | bytes 399368 | tf_op jit(solution)/shard_map/ppermute | solution.py:43
  14.6 2.3 %multiply_reduce_fusion = f32[256]{0:T(256)S(1)} fusion(bf16[256,5120]{1,0:T(8,128)(2,1)} %param.19), kind=kLoop, calls=%fused_computation | loop fusion | flops 3931904 | bytes 2622464 | tf_op jit(solution)/shard_map/reduce_sum | solution.py:124
  16.9 1.3 %reduce-window.4 = s32[2,1]{0,1:T(1,128)} reduce-window(s32[2,1]{0,1:T(1,128)} %bitcast.135, s32[]{:T(128)} %constant.147.clone.1), window={size=2x1 pad=1_0x0_0}, to_apply=%region_1.2 | reduce-window | flops 2 | bytes 20 | tf_op jit(solution)/shard_map/reduce-window
  19.1 3.3 %fusion.9 = bf16[256,64]{0,1:T(8,128)(2,1)} fusion(bf16[256,5120]{1,0:T(8,128)(2,1)} %param.19, bf16[5120,64]{0,1:T(8,128)(2,1)S(1)} %copy-done.7, f32[5120]{0:T(1024)} %param.26, f32[256]{0:T(256)S(1)} %add_rsqrt_fusion), kind=kOutput, calls=%fused_computation.27 | convolution fusion | flops 168787968 | bytes 3331072 | tf_op jit(solution)/shard_map/dot_general | solution.py:14
  22.4 1.5 %convolution_convert_fusion.6 = bf16[256,64]{0,1:T(8,128)(2,1)} fusion(bf16[256,5120]{1,0:T(8,128)(2,1)S(1)} %copy-done.2, bf16[5120,64]{0,1:T(8,128)(2,1)S(1)} %copy-done.7), kind=kOutput, calls=%fused_computation.26 | convolution fusion | flops 167788544 | bytes 3309568 | tf_op jit(solution)/shard_map/dot_general | solution.py:14
  23.9 1.6 %broadcast_in_dim.175 = bf16[16,520,128]{2,1,0:T(8,128)(2,1)} broadcast(bf16[]{:T(256)} %constant.142.clone.1), dimensions={} | broadcast | bytes 2129922 | tf_op jit(solution)/shard_map/broadcast_in_dim | solution.py:59
  28.1 1.6 %bitcast_dynamic-update-slice_fusion.26 = bf16[16,520,128]{2,1,0:T(8,128)(2,1)} fusion(bf16[16,520,128]{2,1,0:T(8,128)(2,1)} %bitcast_dynamic-update-slice_fusion.27, s32[]{:T(128)S(6)} %select_n.212, bf16[520,128]{1,0:T(8,128)(2,1)} %collective-permute-done), kind=kLoop, calls=%fused_computation.75 | loop fusion | bytes 266244 | tf_op jit(solution)/shard_map/dynamic_update_slice | solution.py:63
  30.4 3.3 %collective-permute-done.3 = bf16[520,128]{1,0:T(8,128)(2,1)S(1)} collective-permute-done((bf16[520,128]{1,0:T(8,128)(2,1)}, bf16[520,128]{1,0:T(8,128)(2,1)S(1)}, u32[]{:S(2)}, u32[]{:S(2)}) %collective-permute-start.3) | collective-permute-done | bytes 133152 | tf_op jit(solution)/shard_map/ppermute | solution.py:43
  33.7 1.6 %collective-permute-start.5 = (bf16[520,128]{1,0:T(8,128)(2,1)S(1)}, bf16[520,128]{1,0:T(8,128)(2,1)S(1)}, u32[]{:S(2)}, u32[]{:S(2)}) collective-permute-start(bf16[520,128]{1,0:T(8,128)(2,1)S(1)} %collective-permute-done.1), channel_id=1, source_target_pairs={{0,4},{1,5},{4,8},{5,9},{8,12},{9,13},{12,14},{13,15},{14,10},{15,... | collective-permute-start | bytes 399368 | tf_op jit(solution)/shard_map/ppermute | solution.py:43
  35.2 1.6 %bitcast_dynamic-update-slice_fusion.12 = bf16[16,960,128]{2,1,0:T(8,128)(2,1)} fusion(bf16[16,960,128]{2,1,0:T(8,128)(2,1)} %get-tuple-element.6, s32[]{:T(128)S(6)} %select_n.212, bf16[960,128]{1,0:T(8,128)(2,1)} %collective-permute-done.17), kind=kLoop, calls=%fused_computation.59 | loop fusion | bytes 491524 | tf_op jit(solution)/shard_map/dynamic_update_slice | solution.py:63
  37.4 1.7 %bitcast_dynamic-update-slice_fusion.11 = bf16[16,960,128]{2,1,0:T(8,128)(2,1)} fusion(bf16[16,960,128]{2,1,0:T(8,128)(2,1)} %bitcast_dynamic-update-slice_fusion.12, s32[]{:T(128)S(6)} %select_n.215, bf16[960,128]{1,0:T(8,128)(2,1)} %collective-permute-done.18), kind=kLoop, calls=%fused_computation.58 | loop fusion | bytes 491524 | tf_op jit(solution)/shard_map/dynamic_update_slice | solution.py:62
  40.6 1.6 %collective-permute-start.22 = (bf16[960,128]{1,0:T(8,128)(2,1)}, bf16[960,128]{1,0:T(8,128)(2,1)S(1)}, u32[]{:S(2)}, u32[]{:S(2)}) collective-permute-start(bf16[960,128]{1,0:T(8,128)(2,1)} %collective-permute-done.18), channel_id=1, source_target_pairs={{0,4},{1,5},{4,8},{5,9},{8,12},{9,13},{12,14},{13,15},{14,10},{15,... | collective-permute-start | bytes 737288 | tf_op jit(solution)/shard_map/ppermute | solution.py:43
  44.0 1.6 %collective-permute-start.9 = (bf16[520,128]{1,0:T(8,128)(2,1)S(1)}, bf16[520,128]{1,0:T(8,128)(2,1)S(1)}, u32[]{:S(2)}, u32[]{:S(2)}) collective-permute-start(bf16[520,128]{1,0:T(8,128)(2,1)S(1)} %collective-permute-done.5), channel_id=1, source_target_pairs={{0,4},{1,5},{4,8},{5,9},{8,12},{9,13},{12,14},{13,15},{14,10},{15,... | collective-permute-start | bytes 399368 | tf_op jit(solution)/shard_map/ppermute | solution.py:43
  48.0 3.8 %collective-permute-done.9 = bf16[520,128]{1,0:T(8,128)(2,1)S(1)} collective-permute-done((bf16[520,128]{1,0:T(8,128)(2,1)S(1)}, bf16[520,128]{1,0:T(8,128)(2,1)S(1)}, u32[]{:S(2)}, u32[]{:S(2)}) %collective-permute-start.9) | collective-permute-done | bytes 133152 | tf_op jit(solution)/shard_map/ppermute | solution.py:43
  52.8 1.5 %collective-permute-start.13 = (bf16[256,128]{1,0:T(8,128)(2,1)S(1)}, bf16[256,128]{1,0:T(8,128)(2,1)S(1)}, u32[]{:S(2)}, u32[]{:S(2)}) collective-permute-start(bf16[256,128]{1,0:T(8,128)(2,1)S(1)} %slice.73), channel_id=1, source_target_pairs={{0,4},{1,5},{4,8},{5,9},{8,12},{9,13},{12,14},{13,15},{14,10},{15,... | collective-permute-start | bytes 196616 | tf_op jit(solution)/shard_map/ppermute | solution.py:43
  56.2 1.7 %bitcast_dynamic-update-slice_fusion.9 = bf16[16,960,128]{2,1,0:T(8,128)(2,1)} fusion(bf16[16,960,128]{2,1,0:T(8,128)(2,1)} %bitcast_dynamic-update-slice_fusion.10, s32[]{:T(128)S(6)} %select_n.219, bf16[960,128]{1,0:T(8,128)(2,1)} %collective-permute-done.20), kind=kLoop, calls=%fused_computation.56 | loop fusion | bytes 491524 | tf_op jit(solution)/shard_map/dynamic_update_slice | solution.py:62
  59.1 1.7 %collective-permute-done.15 = bf16[264,128]{1,0:T(8,128)(2,1)S(1)} collective-permute-done((bf16[264,128]{1,0:T(8,128)(2,1)S(1)}, bf16[264,128]{1,0:T(8,128)(2,1)S(1)}, u32[]{:S(2)}, u32[]{:S(2)}) %collective-permute-start.15) | collective-permute-done | bytes 67616 | tf_op jit(solution)/shard_map/ppermute | solution.py:43
  63.4 1.5 %collective-permute-start.26 = (bf16[960,128]{1,0:T(8,128)(2,1)S(1)}, bf16[960,128]{1,0:T(8,128)(2,1)S(1)}, u32[]{:S(2)}, u32[]{:S(2)}) collective-permute-start(bf16[960,128]{1,0:T(8,128)(2,1)S(1)} %collective-permute-done.22), channel_id=1, source_target_pairs={{0,4},{1,5},{4,8},{5,9},{8,12},{9,13},{12,14},{13,15},{14,10},{15,... | collective-permute-start | bytes 737288 | tf_op jit(solution)/shard_map/ppermute | solution.py:43
  69.9 3.2 %slice.89 = bf16[16,512,128]{2,1,0:T(8,128)(2,1)} slice(bf16[16,520,128]{2,1,0:T(8,128)(2,1)} %bitcast_dynamic-update-slice_fusion.32), slice={[0:16], [0:512], [0:128]} | slice | bytes 4194304 | tf_op jit(solution)/shard_map/slice | solution.py:121
  73.1 4.2 %reshape.149 = bf16[128,8192]{1,0:T(8,128)(2,1)} reshape(bf16[16,512,128]{2,1,0:T(8,128)(2,1)} %slice.89) | data formatting | bytes 4194304 | tf_op jit(solution)/shard_map/reshape | solution.py:121
  77.4 1.6 %collective-permute-start.30 = (bf16[480,128]{1,0:T(8,128)(2,1)S(1)}, bf16[480,128]{1,0:T(8,128)(2,1)S(1)}, u32[]{:S(2)}, u32[]{:S(2)}) collective-permute-start(bf16[480,128]{1,0:T(8,128)(2,1)S(1)} %slice.79), channel_id=1, source_target_pairs={{0,4},{1,5},{4,8},{5,9},{8,12},{9,13},{12,14},{13,15},{14,10},{15,... | collective-permute-start | bytes 368648 | tf_op jit(solution)/shard_map/ppermute | solution.py:43
  80.2 1.7 %bitcast_dynamic-update-slice_fusion.6 = bf16[16,960,128]{2,1,0:T(8,128)(2,1)} fusion(bf16[16,960,128]{2,1,0:T(8,128)(2,1)} %bitcast_dynamic-update-slice_fusion.7, s32[]{:T(128)S(6)} %select_n.224, bf16[960,128]{1,0:T(8,128)(2,1)} %collective-permute-done.23), kind=kLoop, calls=%fused_computation.53 | loop fusion | bytes 491524 | tf_op jit(solution)/shard_map/dynamic_update_slice | solution.py:63
  81.9 1.7 %bitcast_dynamic-update-slice_fusion.5 = bf16[16,960,128]{2,1,0:T(8,128)(2,1)} fusion(bf16[16,960,128]{2,1,0:T(8,128)(2,1)} %bitcast_dynamic-update-slice_fusion.6, s32[]{:T(128)S(6)} %select_n.227, bf16[960,128]{1,0:T(8,128)(2,1)} %collective-permute-done.24), kind=kLoop, calls=%fused_computation.52 | loop fusion | bytes 491524 | tf_op jit(solution)/shard_map/dynamic_update_slice | solution.py:62
  83.5 1.6 %bitcast_dynamic-update-slice_fusion.4 = bf16[16,960,128]{2,1,0:T(8,128)(2,1)} fusion(bf16[16,960,128]{2,1,0:T(8,128)(2,1)} %bitcast_dynamic-update-slice_fusion.5, s32[]{:T(128)S(6)} %select_n.228, bf16[960,128]{1,0:T(8,128)(2,1)} %collective-permute-done.25), kind=kLoop, calls=%fused_computation.51 | loop fusion | bytes 491524 | tf_op jit(solution)/shard_map/dynamic_update_slice | solution.py:63
  91.2 1.6 %fusion.33 = (bf16[16,160,64]{2,1,0:T(8,128)(2,1)S(1)}, bf16[16,160,64]{2,1,0:T(8,128)(2,1)S(1)}) fusion(bf16[16,960,128]{2,1,0:T(8,128)(2,1)} %bitcast_dynamic-update-slice_fusion.28), kind=kLoop, calls=%fused_computation.112 | loop fusion | bytes 1310720 | tf_op jit(solution)/shard_map/slice | solution.py:138
  92.8 1.9 %fusion.32 = (bf16[16,320,128]{2,1,0:T(8,128)(2,1)S(1)}, bf16[16,320,128]{2,1,0:T(8,128)(2,1)S(1)}) fusion(bf16[16,960,128]{2,1,0:T(8,128)(2,1)} %bitcast_dynamic-update-slice_fusion.28), kind=kLoop, calls=%fused_computation.111 | loop fusion | bytes 5242880 | tf_op jit(solution)/shard_map/slice | solution.py:133
  94.7 1.8 %slice.85 = bf16[16,160,128]{2,1,0:T(8,128)(2,1)S(1)} slice(bf16[16,960,128]{2,1,0:T(8,128)(2,1)} %bitcast_dynamic-update-slice_fusion.28), slice={[0:16], [640:800], [0:128]} | slice | bytes 1310720 | tf_op jit(solution)/shard_map/slice | solution.py:135
  101.3 1.6 %convolution_bitcast_fusion = f32[256,256]{1,0:T(8,128)} fusion(bf16[256,5120]{1,0:T(8,128)(2,1)S(1)} %copy-done, bf16[5120,128]{1,0:T(8,128)(2,1)S(1)} %copy-done.18, bf16[5120,128]{1,0:T(8,128)(2,1)S(1)} %bitcast.130), kind=kOutput, calls=%fused_computation.4 | convolution fusion | flops 676331520 | bytes 5505024 | tf_op jit(solution)/shard_map/dot_general | solution.py:14
  102.9 3.0 %fusion.5 = bf16[256,256]{1,0:T(8,128)(2,1)S(1)} fusion(f32[256,256]{1,0:T(8,128)} %convolution_bitcast_fusion, f32[256,256]{1,0:T(8,128)S(1)} %fusion.4, bf16[128,256]{1,0:T(8,128)(2,1)S(1)} %convolution_convert_fusion.3, bf16[5120,128]{1,0:T(8,128)(2,1)} %bitcast.126, bf16[5120,128]{1,0:T(8,128)(2,1)} %param.37, bf16[5120,128]{1,0:T(8,128)(2,1)} %bitcast.131, ...), kind=kOutput, calls=%fused_computation.12 | convolution fusion | flops 357990400 | bytes 4654080 | tf_op jit(solution)/shard_map/dot_general | solution.py:14
  107.2 2.2 %convolution_multiply_fusion.6 = f32[2,128]{1,0:T(2,128)S(1)} fusion(bf16[2,8192]{1,0:T(2,128)(2,1)S(1)} %convert_element_type.84, bf16[128,8192]{1,0:T(8,128)(2,1)} %reshape.149), kind=kOutput, calls=%fused_computation.29 | convolution fusion | flops 4194560 | bytes 2130944 | tf_op jit(solution)/shard_map/dot_general | solution.py:18
  (175 shorter events, 43.4 us)
Async XLA Ops:
  8.4 26.9 %collective-permute-start.17 = (bf16[960,128]{1,0:T(8,128)(2,1)}, bf16[960,128]{1,0:T(8,128)(2,1)}, u32[]{:S(2)}, u32[]{:S(2)}) collective-permute-start(bf16[960,128]{1,0:T(8,128)(2,1)} %get-tuple-element.7), channel_id=1, source_target_pairs={{0,1},{1,0},{2,3},{3,2},{4,5},{5,4},{6,7},{7,6},{8,9},{9,8},{10,11... | collective-permute-start | bytes 737288 | tf_op jit(solution)/shard_map/ppermute | solution.py:46
  8.8 28.1 %collective-permute-start.18 = (bf16[960,128]{1,0:T(8,128)(2,1)}, bf16[960,128]{1,0:T(8,128)(2,1)}, u32[]{:S(2)}, u32[]{:S(2)}) collective-permute-start(bf16[960,128]{1,0:T(8,128)(2,1)} %get-tuple-element.7), channel_id=1, source_target_pairs={{0,4},{1,5},{4,8},{5,9},{8,12},{9,13},{12,14},{13,15},{14,10},{15,... | collective-permute-start | bytes 737288 | tf_op jit(solution)/shard_map/ppermute | solution.py:43
  11.4 29.2 %collective-permute-start.20 = (bf16[960,128]{1,0:T(8,128)(2,1)}, bf16[960,128]{1,0:T(8,128)(2,1)}, u32[]{:S(2)}, u32[]{:S(2)}) collective-permute-start(bf16[960,128]{1,0:T(8,128)(2,1)} %get-tuple-element.7), channel_id=1, source_target_pairs={{0,2},{1,3},{4,0},{5,1},{8,4},{9,5},{12,8},{13,9},{14,12},{15,13},... | collective-permute-start | bytes 737288 | tf_op jit(solution)/shard_map/ppermute | solution.py:43
  12.6 15.2 %collective-permute-start = (bf16[520,128]{1,0:T(8,128)(2,1)}, bf16[520,128]{1,0:T(8,128)(2,1)}, u32[]{:S(2)}, u32[]{:S(2)}) collective-permute-start(bf16[520,128]{1,0:T(8,128)(2,1)} %pad_maximum_fusion.6), channel_id=1, source_target_pairs={{0,1},{1,0},{2,3},{3,2},{4,5},{5,4},{6,7},{7,6},{8,9},{9,8},{10,11... | collective-permute-start | bytes 399368 | tf_op jit(solution)/shard_map/ppermute | solution.py:46
  12.8 15.2 %collective-permute-start.1 = (bf16[520,128]{1,0:T(8,128)(2,1)}, bf16[520,128]{1,0:T(8,128)(2,1)S(1)}, u32[]{:S(2)}, u32[]{:S(2)}) collective-permute-start(bf16[520,128]{1,0:T(8,128)(2,1)} %pad_maximum_fusion.6), channel_id=1, source_target_pairs={{0,4},{1,5},{4,8},{5,9},{8,12},{9,13},{12,14},{13,15},{14,10},{15,... | collective-permute-start | bytes 399368 | tf_op jit(solution)/shard_map/ppermute | solution.py:43
  27.7 5.9 %collective-permute-start.3 = (bf16[520,128]{1,0:T(8,128)(2,1)}, bf16[520,128]{1,0:T(8,128)(2,1)S(1)}, u32[]{:S(2)}, u32[]{:S(2)}) collective-permute-start(bf16[520,128]{1,0:T(8,128)(2,1)} %pad_maximum_fusion.6), channel_id=1, source_target_pairs={{0,2},{1,3},{4,0},{5,1},{8,4},{9,5},{12,8},{13,9},{14,12},{15,13},... | collective-permute-start | bytes 399368 | tf_op jit(solution)/shard_map/ppermute | solution.py:43
  28.0 11.0 %collective-permute-start.2 = (bf16[520,128]{1,0:T(8,128)(2,1)S(1)}, bf16[520,128]{1,0:T(8,128)(2,1)S(1)}, u32[]{:S(2)}, u32[]{:S(2)}) collective-permute-start(bf16[520,128]{1,0:T(8,128)(2,1)S(1)} %collective-permute-done.1), channel_id=1, source_target_pairs={{0,1},{1,0},{2,3},{3,2},{4,5},{5,4},{6,7},{7,6},{8,9},{9,8},{10,11... | collective-permute-start | bytes 399368 | tf_op jit(solution)/shard_map/ppermute | solution.py:46
  33.7 8.5 %collective-permute-start.5 = (bf16[520,128]{1,0:T(8,128)(2,1)S(1)}, bf16[520,128]{1,0:T(8,128)(2,1)S(1)}, u32[]{:S(2)}, u32[]{:S(2)}) collective-permute-start(bf16[520,128]{1,0:T(8,128)(2,1)S(1)} %collective-permute-done.1), channel_id=1, source_target_pairs={{0,4},{1,5},{4,8},{5,9},{8,12},{9,13},{12,14},{13,15},{14,10},{15,... | collective-permute-start | bytes 399368 | tf_op jit(solution)/shard_map/ppermute | solution.py:43
  35.2 6.9 %collective-permute-start.4 = (bf16[520,128]{1,0:T(8,128)(2,1)S(1)}, bf16[520,128]{1,0:T(8,128)(2,1)S(1)}, u32[]{:S(2)}, u32[]{:S(2)}) collective-permute-start(bf16[520,128]{1,0:T(8,128)(2,1)S(1)} %collective-permute-done.3), channel_id=1, source_target_pairs={{0,1},{1,0},{2,3},{3,2},{4,5},{5,4},{6,7},{7,6},{8,9},{9,8},{10,11... | collective-permute-start | bytes 399368 | tf_op jit(solution)/shard_map/ppermute | solution.py:46
  36.9 7.1 %collective-permute-start.7 = (bf16[520,128]{1,0:T(8,128)(2,1)S(1)}, bf16[520,128]{1,0:T(8,128)(2,1)S(1)}, u32[]{:S(2)}, u32[]{:S(2)}) collective-permute-start(bf16[520,128]{1,0:T(8,128)(2,1)S(1)} %collective-permute-done.3), channel_id=1, source_target_pairs={{0,2},{1,3},{4,0},{5,1},{8,4},{9,5},{12,8},{13,9},{14,12},{15,13},... | collective-permute-start | bytes 399368 | tf_op jit(solution)/shard_map/ppermute | solution.py:43
  39.0 16.0 %collective-permute-start.19 = (bf16[960,128]{1,0:T(8,128)(2,1)}, bf16[960,128]{1,0:T(8,128)(2,1)S(1)}, u32[]{:S(2)}, u32[]{:S(2)}) collective-permute-start(bf16[960,128]{1,0:T(8,128)(2,1)} %collective-permute-done.18), channel_id=1, source_target_pairs={{0,1},{1,0},{2,3},{3,2},{4,5},{5,4},{6,7},{7,6},{8,9},{9,8},{10,11... | collective-permute-start | bytes 737288 | tf_op jit(solution)/shard_map/ppermute | solution.py:46
  40.6 20.2 %collective-permute-start.22 = (bf16[960,128]{1,0:T(8,128)(2,1)}, bf16[960,128]{1,0:T(8,128)(2,1)S(1)}, u32[]{:S(2)}, u32[]{:S(2)}) collective-permute-start(bf16[960,128]{1,0:T(8,128)(2,1)} %collective-permute-done.18), channel_id=1, source_target_pairs={{0,4},{1,5},{4,8},{5,9},{8,12},{9,13},{12,14},{13,15},{14,10},{15,... | collective-permute-start | bytes 737288 | tf_op jit(solution)/shard_map/ppermute | solution.py:43
  42.2 15.7 %collective-permute-start.21 = (bf16[960,128]{1,0:T(8,128)(2,1)}, bf16[960,128]{1,0:T(8,128)(2,1)S(1)}, u32[]{:S(2)}, u32[]{:S(2)}) collective-permute-start(bf16[960,128]{1,0:T(8,128)(2,1)} %collective-permute-done.20), channel_id=1, source_target_pairs={{0,1},{1,0},{2,3},{3,2},{4,5},{5,4},{6,7},{7,6},{8,9},{9,8},{10,11... | collective-permute-start | bytes 737288 | tf_op jit(solution)/shard_map/ppermute | solution.py:46
  42.2 3.4 %collective-permute-start.6 = (bf16[520,128]{1,0:T(8,128)(2,1)S(1)}, bf16[520,128]{1,0:T(8,128)(2,1)S(1)}, u32[]{:S(2)}, u32[]{:S(2)}) collective-permute-start(bf16[520,128]{1,0:T(8,128)(2,1)S(1)} %collective-permute-done.5), channel_id=1, source_target_pairs={{0,1},{1,0},{2,3},{3,2},{4,5},{5,4},{6,7},{7,6},{8,9},{9,8},{10,11... | collective-permute-start | bytes 399368 | tf_op jit(solution)/shard_map/ppermute | solution.py:46
  44.0 7.8 %collective-permute-start.9 = (bf16[520,128]{1,0:T(8,128)(2,1)S(1)}, bf16[520,128]{1,0:T(8,128)(2,1)S(1)}, u32[]{:S(2)}, u32[]{:S(2)}) collective-permute-start(bf16[520,128]{1,0:T(8,128)(2,1)S(1)} %collective-permute-done.5), channel_id=1, source_target_pairs={{0,4},{1,5},{4,8},{5,9},{8,12},{9,13},{12,14},{13,15},{14,10},{15,... | collective-permute-start | bytes 399368 | tf_op jit(solution)/shard_map/ppermute | solution.py:43
  46.9 5.9 %collective-permute-start.11 = (bf16[520,128]{1,0:T(8,128)(2,1)S(1)}, bf16[520,128]{1,0:T(8,128)(2,1)S(1)}, u32[]{:S(2)}, u32[]{:S(2)}) collective-permute-start(bf16[520,128]{1,0:T(8,128)(2,1)S(1)} %collective-permute-done.7), channel_id=1, source_target_pairs={{0,2},{1,3},{4,0},{5,1},{8,4},{9,5},{12,8},{13,9},{14,12},{15,13},... | collective-permute-start | bytes 399368 | tf_op jit(solution)/shard_map/ppermute | solution.py:43
  51.8 11.6 %collective-permute-start.24 = (bf16[960,128]{1,0:T(8,128)(2,1)}, bf16[960,128]{1,0:T(8,128)(2,1)}, u32[]{:S(2)}, u32[]{:S(2)}) collective-permute-start(bf16[960,128]{1,0:T(8,128)(2,1)} %collective-permute-done.20), channel_id=1, source_target_pairs={{0,2},{1,3},{4,0},{5,1},{8,4},{9,5},{12,8},{13,9},{14,12},{15,13},... | collective-permute-start | bytes 737288 | tf_op jit(solution)/shard_map/ppermute | solution.py:43
  52.8 5.8 %collective-permute-start.13 = (bf16[256,128]{1,0:T(8,128)(2,1)S(1)}, bf16[256,128]{1,0:T(8,128)(2,1)S(1)}, u32[]{:S(2)}, u32[]{:S(2)}) collective-permute-start(bf16[256,128]{1,0:T(8,128)(2,1)S(1)} %slice.73), channel_id=1, source_target_pairs={{0,4},{1,5},{4,8},{5,9},{8,12},{9,13},{12,14},{13,15},{14,10},{15,... | collective-permute-start | bytes 196616 | tf_op jit(solution)/shard_map/ppermute | solution.py:43
  55.0 5.8 %collective-permute-start.15 = (bf16[264,128]{1,0:T(8,128)(2,1)S(1)}, bf16[264,128]{1,0:T(8,128)(2,1)S(1)}, u32[]{:S(2)}, u32[]{:S(2)}) collective-permute-start(bf16[264,128]{1,0:T(8,128)(2,1)S(1)} %slice.74), channel_id=1, source_target_pairs={{0,2},{1,3},{4,0},{5,1},{8,4},{9,5},{12,8},{13,9},{14,12},{15,13},... | collective-permute-start | bytes 202760 | tf_op jit(solution)/shard_map/ppermute | solution.py:43
  57.9 4.1 %collective-permute-start.10 = (bf16[520,128]{1,0:T(8,128)(2,1)S(1)}, bf16[520,128]{1,0:T(8,128)(2,1)S(1)}, u32[]{:S(2)}, u32[]{:S(2)}) collective-permute-start(bf16[520,128]{1,0:T(8,128)(2,1)S(1)} %collective-permute-done.9), channel_id=1, source_target_pairs={{0,1},{1,0},{2,3},{3,2},{4,5},{5,4},{6,7},{7,6},{8,9},{9,8},{10,11... | collective-permute-start | bytes 399368 | tf_op jit(solution)/shard_map/ppermute | solution.py:46
  58.6 6.3 %collective-permute-start.12 = (bf16[520,128]{1,0:T(8,128)(2,1)S(1)}, bf16[520,128]{1,0:T(8,128)(2,1)S(1)}, u32[]{:S(2)}, u32[]{:S(2)}) collective-permute-start(bf16[520,128]{1,0:T(8,128)(2,1)S(1)} %collective-permute-done.11), channel_id=1, source_target_pairs={{0,1},{1,0},{2,3},{3,2},{4,5},{5,4},{6,7},{7,6},{8,9},{9,8},{10,11... | collective-permute-start | bytes 399368 | tf_op jit(solution)/shard_map/ppermute | solution.py:46
  60.8 5.6 %collective-permute-start.14 = (bf16[256,128]{1,0:T(8,128)(2,1)S(1)}, bf16[256,128]{1,0:T(8,128)(2,1)S(1)}, u32[]{:S(2)}, u32[]{:S(2)}) collective-permute-start(bf16[256,128]{1,0:T(8,128)(2,1)S(1)} %collective-permute-done.13), channel_id=1, source_target_pairs={{0,1},{1,0},{2,3},{3,2},{4,5},{5,4},{6,7},{7,6},{8,9},{9,8},{10,11... | collective-permute-start | bytes 196616 | tf_op jit(solution)/shard_map/ppermute | solution.py:46
  60.8 7.4 %collective-permute-start.16 = (bf16[264,128]{1,0:T(8,128)(2,1)S(1)}, bf16[264,128]{1,0:T(8,128)(2,1)S(1)}, u32[]{:S(2)}, u32[]{:S(2)}) collective-permute-start(bf16[264,128]{1,0:T(8,128)(2,1)S(1)} %collective-permute-done.15), channel_id=1, source_target_pairs={{0,1},{1,0},{2,3},{3,2},{4,5},{5,4},{6,7},{7,6},{8,9},{9,8},{10,11... | collective-permute-start | bytes 202760 | tf_op jit(solution)/shard_map/ppermute | solution.py:46
  62.0 17.7 %collective-permute-start.23 = (bf16[960,128]{1,0:T(8,128)(2,1)S(1)}, bf16[960,128]{1,0:T(8,128)(2,1)}, u32[]{:S(2)}, u32[]{:S(2)}) collective-permute-start(bf16[960,128]{1,0:T(8,128)(2,1)S(1)} %collective-permute-done.22), channel_id=1, source_target_pairs={{0,1},{1,0},{2,3},{3,2},{4,5},{5,4},{6,7},{7,6},{8,9},{9,8},{10,11... | collective-permute-start | bytes 737288 | tf_op jit(solution)/shard_map/ppermute | solution.py:46
  63.4 14.0 %collective-permute-start.26 = (bf16[960,128]{1,0:T(8,128)(2,1)S(1)}, bf16[960,128]{1,0:T(8,128)(2,1)S(1)}, u32[]{:S(2)}, u32[]{:S(2)}) collective-permute-start(bf16[960,128]{1,0:T(8,128)(2,1)S(1)} %collective-permute-done.22), channel_id=1, source_target_pairs={{0,4},{1,5},{4,8},{5,9},{8,12},{9,13},{12,14},{13,15},{14,10},{15,... | collective-permute-start | bytes 737288 | tf_op jit(solution)/shard_map/ppermute | solution.py:43
  64.9 18.6 %collective-permute-start.25 = (bf16[960,128]{1,0:T(8,128)(2,1)}, bf16[960,128]{1,0:T(8,128)(2,1)}, u32[]{:S(2)}, u32[]{:S(2)}) collective-permute-start(bf16[960,128]{1,0:T(8,128)(2,1)} %collective-permute-done.24), channel_id=1, source_target_pairs={{0,1},{1,0},{2,3},{3,2},{4,5},{5,4},{6,7},{7,6},{8,9},{9,8},{10,11... | collective-permute-start | bytes 737288 | tf_op jit(solution)/shard_map/ppermute | solution.py:46
  66.4 12.6 %collective-permute-start.28 = (bf16[960,128]{1,0:T(8,128)(2,1)}, bf16[960,128]{1,0:T(8,128)(2,1)S(1)}, u32[]{:S(2)}, u32[]{:S(2)}) collective-permute-start(bf16[960,128]{1,0:T(8,128)(2,1)} %collective-permute-done.24), channel_id=1, source_target_pairs={{0,2},{1,3},{4,0},{5,1},{8,4},{9,5},{12,8},{13,9},{14,12},{15,13},... | collective-permute-start | bytes 737288 | tf_op jit(solution)/shard_map/ppermute | solution.py:43
  77.4 8.5 %collective-permute-start.30 = (bf16[480,128]{1,0:T(8,128)(2,1)S(1)}, bf16[480,128]{1,0:T(8,128)(2,1)S(1)}, u32[]{:S(2)}, u32[]{:S(2)}) collective-permute-start(bf16[480,128]{1,0:T(8,128)(2,1)S(1)} %slice.79), channel_id=1, source_target_pairs={{0,4},{1,5},{4,8},{5,9},{8,12},{9,13},{12,14},{13,15},{14,10},{15,... | collective-permute-start | bytes 368648 | tf_op jit(solution)/shard_map/ppermute | solution.py:43
  78.9 7.0 %collective-permute-start.32 = (bf16[480,128]{1,0:T(8,128)(2,1)S(1)}, bf16[480,128]{1,0:T(8,128)(2,1)S(1)}, u32[]{:S(2)}, u32[]{:S(2)}) collective-permute-start(bf16[480,128]{1,0:T(8,128)(2,1)S(1)} %slice.80), channel_id=1, source_target_pairs={{0,2},{1,3},{4,0},{5,1},{8,4},{9,5},{12,8},{13,9},{14,12},{15,13},... | collective-permute-start | bytes 368648 | tf_op jit(solution)/shard_map/ppermute | solution.py:43
  79.7 6.7 %collective-permute-start.27 = (bf16[960,128]{1,0:T(8,128)(2,1)S(1)}, bf16[960,128]{1,0:T(8,128)(2,1)S(1)}, u32[]{:S(2)}, u32[]{:S(2)}) collective-permute-start(bf16[960,128]{1,0:T(8,128)(2,1)S(1)} %collective-permute-done.26), channel_id=1, source_target_pairs={{0,1},{1,0},{2,3},{3,2},{4,5},{5,4},{6,7},{7,6},{8,9},{9,8},{10,11... | collective-permute-start | bytes 737288 | tf_op jit(solution)/shard_map/ppermute | solution.py:46
  79.7 8.1 %collective-permute-start.29 = (bf16[960,128]{1,0:T(8,128)(2,1)S(1)}, bf16[960,128]{1,0:T(8,128)(2,1)S(1)}, u32[]{:S(2)}, u32[]{:S(2)}) collective-permute-start(bf16[960,128]{1,0:T(8,128)(2,1)S(1)} %collective-permute-done.28), channel_id=1, source_target_pairs={{0,1},{1,0},{2,3},{3,2},{4,5},{5,4},{6,7},{7,6},{8,9},{9,8},{10,11... | collective-permute-start | bytes 737288 | tf_op jit(solution)/shard_map/ppermute | solution.py:46
  85.9 4.6 %collective-permute-start.33 = (bf16[480,128]{1,0:T(8,128)(2,1)S(1)}, bf16[480,128]{1,0:T(8,128)(2,1)S(1)}, u32[]{:S(2)}, u32[]{:S(2)}) collective-permute-start(bf16[480,128]{1,0:T(8,128)(2,1)S(1)} %collective-permute-done.32), channel_id=1, source_target_pairs={{0,1},{1,0},{2,3},{3,2},{4,5},{5,4},{6,7},{7,6},{8,9},{9,8},{10,11... | collective-permute-start | bytes 368648 | tf_op jit(solution)/shard_map/ppermute | solution.py:46
  (22 other events, 192.1 us)

commit v2 on v1

--- a/solution.py
+++ b/solution.py
@@ -1,13 +1,20 @@
+import functools
+
 import jax
 import jax.numpy as jnp
 from jax import lax
+from jax.experimental import pallas as pl
+from jax.experimental.pallas import tpu as pltpu
 from jax.sharding import PartitionSpec as P
 
 TASKS = 3
 ALPHA = 4.0
 F32 = jnp.float32
 BF16 = jnp.bfloat16
-MOST_RING_CHIPS = 8
+RING_CHIPS = 8
+LANES = 128
+STEPS = 4
+MIB = 1 << 20
 
 
 def mm(a, b):
@@ -22,49 +29,441 @@
     return lax.dot_general(a, b, (((0,), (0,)), ((), ())), preferred_element_type=F32)
 
 
-def ring_chip(pos, chips):
-    half = chips // 2
-    return jnp.where(pos < half, 2 * pos, 2 * (chips - 1 - pos) + 1)
-
-
-def gather_blocks(block, n):
-    chips = n // 2
-    if chips > MOST_RING_CHIPS:
-        return lax.all_gather(block, "dp")
-    half = chips // 2
-    place = [2 * q if q < half else 2 * (chips - 1 - q) + 1 for q in range(chips)]
-
-    def hop(value, step):
-        pairs = [
-            (2 * place[q] + c, 2 * place[(q + step) % chips] + c)
-            for q in range(chips)
-            for c in range(2)
-        ]
-        return lax.ppermute(value, "dp", pairs)
-
-    def other_core(value):
-        return lax.ppermute(value, "dp", [(d, d ^ 1) for d in range(n)])
-
-    me = lax.axis_index("dp")
-    chip, core = me // 2, me % 2
+def ring_chip(pos):
+    half = RING_CHIPS // 2
+    return jnp.where(pos < half, 2 * pos, 2 * (RING_CHIPS - 1 - pos) + 1)
+
+
+def ring_pos(chip):
     row, side = chip // 2, chip % 2
-    pos = jnp.where(side == 0, row, chips - 1 - row)
-    pieces = [(0, block, 0)]
+    return jnp.where(side == 0, row, RING_CHIPS - 1 - row)
+
+
+def hop(value, step):
+    half = RING_CHIPS // 2
+    place = [2 * q if q < half else 2 * (RING_CHIPS - 1 - q) + 1 for q in range(RING_CHIPS)]
+    pairs = [
+        (2 * place[q] + c, 2 * place[(q + step) % RING_CHIPS] + c)
+        for q in range(RING_CHIPS)
+        for c in range(2)
+    ]
+    return lax.ppermute(value, "dp", pairs)
+
+
+def other_core(value):
+    return lax.ppermute(value, "dp", [(d, d ^ 1) for d in range(2 * RING_CHIPS)])
+
+
+def ring(block, ups, downs):
+    pieces = [(0, block)]
     up, down = block, block
-    middle = (block.shape[0] // 2) // 16 * 16
-    for k in range(1, half):
-        up, down = hop(up, 1), hop(down, -1)
-        pieces += [(-k, up, 0), (k, down, 0)]
-    pieces += [(-half, hop(up[:middle], 1), 0), (half, hop(down[middle:], -1), middle)]
-    out = jnp.zeros((n,) + block.shape, block.dtype)
-    for away, piece, first in pieces:
-        base = 2 * ring_chip((pos + away + chips) % chips, chips)
-        out = lax.dynamic_update_slice(out, piece[None], (base + core, first, 0))
-        out = lax.dynamic_update_slice(out, other_core(piece)[None], (base + 1 - core, first, 0))
-    return out
+    for k in range(1, max(ups, downs) + 1):
+        if k <= ups:
+            up = hop(up, 1)
+            pieces.append((-k, up))
+        if k <= downs:
+            down = hop(down, -1)
+            pieces.append((k, down))
+    return pieces
+
+
+def half_lanes(shape):
+    return lax.broadcasted_iota(jnp.int32, shape, 1) < LANES // 2
+
+
+def diagonal_column(row, first, count):
+    shape = (count, row.shape[1])
+    lane = lax.broadcasted_iota(jnp.int32, shape, 1)
+    at = lax.broadcasted_iota(jnp.int32, shape, 0)
+    return jnp.sum(jnp.where(lane == at + first, row, 0.0), axis=1, keepdims=True)
+
+
+def factor_kernel(me_ref, gain_ref, down_up_ref, up_low_ref, sketch_ref, up_up_ref, down_low_ref, expand_ref, out_ref):
+    rows = down_up_ref.shape[0]
+    half = LANES // 2
+    for b in range(rows // half):
+        place = me_ref[0] * (rows // half) + b
+        row = gain_ref[pl.ds(place // 2, 1), :]
+        column = diagonal_column(row, (place % 2) * half, half)
+        part = down_up_ref[pl.ds(b * half, half), :].astype(F32)
+        out_ref[pl.ds(b * half, half), :] = (column * part).astype(BF16)
+    at = rows
+    out_ref[pl.ds(at, rows), :] = mm(up_low_ref[...], sketch_ref[...]).astype(BF16)
+    at += rows
+    out_ref[pl.ds(at, rows // 2), :] = up_up_ref[...]
+    at += rows // 2
+    expand = expand_ref[...]
+    low = mm_rows(down_low_ref[...], jnp.concatenate([expand, expand], axis=0))
+    first, second = low[: rows // 2], low[rows // 2 :]
+    out_ref[pl.ds(at, rows // 2), :] = jnp.where(half_lanes(first.shape), first, second).astype(BF16)
+
+
+def panel_kernel(val_ref, label_ref, out_ref):
+    wide = val_ref[...].astype(F32)
+    count, width = wide.shape
+    scale = lax.rsqrt(jnp.sum(wide * wide, axis=1, keepdims=True) + 1e-06)
+    unit = wide * scale
+    blocks = [unit[:, i * LANES : (i + 1) * LANES] for i in range(width // LANES)]
+    row = label_ref[...].astype(F32)
+    labels = jnp.broadcast_to(diagonal_column(row, 0, count), (count, LANES))
+    blocks += [labels, labels]
+    for i in range(0, len(blocks), 2):
+        pair = jnp.concatenate(blocks[i : i + 2], axis=0)
+        out_ref[pl.ds(i * count, 2 * count), :] = pair.astype(BF16)
+
+
+def local_kernel(
+    x_ref, mixed_ref, adjoint_ref, values_ref, gain_ref, source_ref, low_target_ref, top_target_ref,
+    lefts_ref, right_ref, x_target_ref, adjoint_target_ref, inverse_ref,
+    squares, x_source, mixed_source, values_target, width,
+):
+    step = pl.program_id(0)
+
+    @pl.when(step == 0)
+    def _():
+        for ref in (squares, x_source, mixed_source, values_target, x_target_ref, adjoint_target_ref):
+            ref[...] = jnp.zeros_like(ref)
+
+    x = x_ref[...]
+    wide = x.astype(F32)
+    square = wide * wide
+    total = squares[...]
+    for i in range(square.shape[1] // LANES):
+        total = total + square[:, i * LANES : (i + 1) * LANES]
+    squares[...] = total
+    source = source_ref[...]
+    gained = (source.astype(F32) * gain_ref[...]).astype(BF16)
+    x_source[...] += mm_rows(x, jnp.concatenate([gained, gained], axis=0))
+    mixed_source[...] += mm_rows(mixed_ref[...], jnp.concatenate([source, source], axis=0))
+    low_target = low_target_ref[...]
+    x_target_ref[...] += mm(x, low_target)
+    adjoint_target_ref[...] += mm(adjoint_ref[...], low_target)
+    values_target[...] += mm(values_ref[...], top_target_ref[...])
+
+    @pl.when(step == STEPS - 1)
+    def _():
+        mean = jnp.sum(squares[...], axis=1, keepdims=True) * (1.0 / width)
+        inverse = jnp.broadcast_to(lax.rsqrt(mean + 1e-05), squares.shape)
+        inverse_ref[...] = inverse
+        tokens = x_ref.shape[0]
+        lefts_ref[pl.ds(0, tokens), :] = (inverse * x_source[...]).astype(BF16)
+        lefts_ref[pl.ds(tokens, tokens), :] = mixed_source[...].astype(BF16)
+        right_ref[...] = (ALPHA * values_target[...]).astype(BF16)
+
+
+def feature_kernel(pieces, slots_ref, counts_ref, *refs):
+    piece_refs = refs[:pieces]
+    (
+        x_hbm, mixed_hbm, adjoint_hbm, values_hbm, target_hbm,
+        lefts_ref, right_ref, x_target_ref, adjoint_target_ref, inverse_ref, expand_ref, sketch_ref,
+        out_ref,
+        factors, x_ref, mixed_ref, adjoint_ref, values_ref, target_ref, piece_sems, sems,
+    ) = refs[pieces:]
+    rows = factors.shape[1] // 3
+    tokens, width = x_ref.shape
+    span = width // STEPS
+    per_step = span // rows
+    value_span = values_ref.shape[1] // STEPS
+
+    copies = []
+    for i, piece in enumerate(piece_refs):
+        copy = pltpu.make_async_copy(piece, factors.at[slots_ref[i]], piece_sems.at[i])
+        copy.start()
+        copies.append(copy)
+    parts = []
+    for j in range(STEPS):
+        part = []
+        for k, (hbm, ref, size) in enumerate(
+            (
+                (x_hbm, x_ref, span),
+                (mixed_hbm, mixed_ref, span),
+                (adjoint_hbm, adjoint_ref, span),
+                (values_hbm, values_ref, value_span),
+            )
+        ):
+            window = pl.ds(j * size, size)
+            part.append(pltpu.make_async_copy(hbm.at[:, window], ref.at[:, window], sems.at[j, k]))
+        window = pl.ds(j * span, span)
+        part.append(pltpu.make_async_copy(target_hbm.at[window], target_ref.at[window], sems.at[j, 4]))
+        for copy in part:
+            copy.start()
+        parts.append(part)
+    for copy in copies:
+        copy.wait()
+
+    x_both = jnp.zeros((tokens, 2 * LANES), F32)
+    bridge = jnp.zeros((LANES, 2 * LANES), F32)
+    adjoint_low = jnp.zeros((tokens, LANES), F32)
+    mixed_low = jnp.zeros((tokens, LANES), F32)
+    returned = jnp.zeros((tokens, LANES), F32)
+    for j in range(STEPS):
+        for copy in parts[j]:
+            copy.wait()
+        held = [factors[j * per_step + s] for s in range(per_step)]
+        down_up = jnp.concatenate([f[:rows] for f in held], axis=0)
+        up_low = jnp.concatenate([f[rows : 2 * rows] for f in held], axis=0)
+        up_up = jnp.concatenate([f[2 * rows : 2 * rows + rows // 2] for f in held], axis=0)
+        down_low = []
+        for f in held:
+            packed = f[2 * rows + rows // 2 :].astype(F32)
+            turned = pltpu.roll(packed, LANES // 2, 1)
+            lower = half_lanes(packed.shape)
+            down_low += [jnp.where(lower, packed, turned), jnp.where(lower, turned, packed)]
+        down_low = jnp.concatenate(down_low, axis=0).astype(BF16)
+        window = slice(j * span, (j + 1) * span)
+        x_both = x_both + mm(x_ref[:, window], jnp.concatenate([down_up, up_low], axis=1))
+        adjoint_low = adjoint_low + mm(adjoint_ref[:, window], up_low)
+        mixed_low = mixed_low + mm(mixed_ref[:, window], down_low)
+        returned = returned + mm(values_ref[:, j * value_span : (j + 1) * value_span], up_up)
+        bridge = bridge + mm_cols(down_up, jnp.concatenate([up_low, target_ref[window, :]], axis=1))
+
+    inverse = inverse_ref[...]
+    reduced = inverse * x_both[:, :LANES]
+    expand = expand_ref[...]
+    left_two = mm_rows(reduced.astype(BF16), jnp.concatenate([expand, expand], axis=0))
+    returned = returned.astype(BF16)
+    right_one = ALPHA * mm(returned, sketch_ref[...])
+    along = (ALPHA / width) * jnp.sum(returned.astype(F32) * reduced, axis=1, keepdims=True)
+    bridged = mm(returned, bridge.astype(BF16))
+    along = along * inverse
+    right_three = adjoint_low + inverse * (ALPHA * bridged[:, :LANES] - along * x_both[:, LANES:])
+    right_four = adjoint_target_ref[...] + inverse * (
+        ALPHA * bridged[:, LANES:] - along * x_target_ref[...]
+    )
+    rights = (
+        right_one.astype(BF16),
+        right_ref[...],
+        (ALPHA * right_three).astype(BF16),
+        (ALPHA * right_four).astype(BF16),
+    )
+    place = lax.broadcasted_iota(jnp.int32, (tokens, LANES), 0)
+    first, second = counts_ref[0, 0], counts_ref[0, 1]
+    lower = half_lanes((tokens, LANES))
+    start = jnp.where(lower, 0, first)
+    end = jnp.where(lower, first, first + second)
+    member = (place >= start) & (place < end)
+    lefts = (
+        lefts_ref[pl.ds(0, tokens), :].astype(F32),
+        left_two,
+        lefts_ref[pl.ds(tokens, tokens), :].astype(F32),
+        mixed_low,
+    )
+    spread = jnp.concatenate([jnp.where(member, left, 0.0).astype(BF16) for left in lefts], axis=0)
+    feats = mm_cols(spread, jnp.concatenate(rights, axis=0))
+    half = LANES // 2
+    for e in range(2):
+        own = feats[e * half : (e + 1) * half]
+        squares = jnp.sum(own * own, keepdims=True)
+        out_ref[pl.ds(e * half, half), :] = (own * lax.rsqrt(squares + 1e-06)).astype(BF16)
+
+
+def score_kernel(pieces, count, unit_ref, *refs):
+    piece_refs = refs[:pieces]
+    best_ref, mean_ref, spread = refs[pieces:]
+    half = LANES // 2
+    scale = float(half * LANES) ** 0.5
+    for e in range(2):
+        for i in range(half):
+            row = unit_ref[pl.ds(e * half + i, 1), :].astype(F32)
+            spread[e, pl.ds(i * count, count), :] = jnp.broadcast_to(row, (count, LANES))
+    best = [[jnp.full((count, LANES), -2.0 * scale, F32) for _ in range(TASKS)] for _ in range(2)]
+    for piece in piece_refs:
+        wide = piece[pl.ds(0, half * count), :].astype(F32)
+        labels = piece[pl.ds(half * count, 2 * count), :].astype(F32)[:count]
+        for e in range(2):
+            products = wide * spread[e]
+            total = jnp.sum(products.reshape(half, count, LANES), axis=0)
+            similar = scale * jnp.sum(total, axis=1, keepdims=True)
+            for t in range(TASKS):
+                here = jnp.where(labels == float(t), similar, -2.0 * scale)
+                best[e][t] = jnp.maximum(best[e][t], here)
+    for e in range(2):
+        values = [jnp.max(best[e][t]) for t in range(TASKS)]
+        for t in range(TASKS):
+            best_ref[e, t] = values[t]
+        mean_ref[e] = (values[0] + values[1] + values[2]) * (1.0 / TASKS)
+
+
+VMEM = pl.BlockSpec(memory_space=pltpu.VMEM)
+SMEM = pl.BlockSpec(memory_space=pltpu.SMEM)
+ANY = pl.BlockSpec(memory_space=pl.ANY)
+
+
+def params(mib):
+    return pltpu.CompilerParams(vmem_limit_bytes=mib * MIB)
+
+
+def cost(flops, nbytes):
+    return pl.CostEstimate(flops=flops, bytes_accessed=nbytes, transcendentals=0)
 
 
 def shards(
+    hidden_state_input,
+    attention_mixed_state,
+    hidden_state_adjoint,
+    attention_values_adjoint,
+    sequence_token_counts,
+    heldout_sketched_signals,
+    benchmark_labels,
+    top_rmsnorm_weights,
+    top_reducer_matrix,
+    top_expander_matrix,
+    bottom_reducer_matrix,
+    bottom_expander_matrix,
+    source_sketch,
+    top_reducer_sketch,
+    top_expander_sketch,
+    top_target_sketch,
+    bottom_reducer_sketch,
+    bottom_expander_sketch,
+    bottom_target_sketch,
+):
+    me = lax.axis_index("dp").astype(jnp.int32)
+    x, mixed, adjoint, values = (
+        hidden_state_input,
+        attention_mixed_state,
+        hidden_state_adjoint,
+        attention_values_adjoint,
+    )
+    tokens, width = x.shape
+    value_width = values.shape[1]
+    rows = top_reducer_matrix.shape[0]
+    count = heldout_sketched_signals.shape[0]
+
+    factors = pl.pallas_call(
+        factor_kernel,
+        out_shape=jax.ShapeDtypeStruct((3 * rows, LANES), BF16),
+        in_specs=[SMEM] + [VMEM] * 7,
+        out_specs=VMEM,
+        compiler_params=params(16),
+        name="factors",
+    )(
+        me.reshape(1),
+        top_rmsnorm_weights.reshape(width // LANES, LANES),
+        top_reducer_matrix,
+        bottom_expander_matrix.T,
+        bottom_reducer_sketch,
+        top_expander_matrix.T,
+        bottom_reducer_matrix,
+        bottom_expander_sketch.T,
+    )
+    panel = pl.pallas_call(
+        panel_kernel,
+        out_shape=jax.ShapeDtypeStruct(((LANES // 2 + 2) * count, LANES), BF16),
+        in_specs=[VMEM] * 2,
+        out_specs=VMEM,
+        compiler_params=params(16),
+        name="panel",
+    )(heldout_sketched_signals, benchmark_labels.T)
+
+    half = RING_CHIPS // 2
+    pos, core = ring_pos(me // 2), me % 2
+    pieces, slots = [], []
+    for away, piece in ring(factors, half, half - 1):
+        base = 2 * ring_chip((pos + away + RING_CHIPS) % RING_CHIPS)
+        pieces += [piece, other_core(piece)]
+        slots += [base + core, base + 1 - core]
+    panels = []
+    for _, piece in ring(panel, half - 1, half):
+        panels += [piece, other_core(piece)]
+
+    span, value_span = width // STEPS, value_width // STEPS
+    by_column = lambda i: (0, i)
+    by_row = lambda i: (i, 0)
+    whole = lambda i: (0, 0)
+    square = (tokens, LANES)
+    lefts, right, x_target, adjoint_target, inverse = pl.pallas_call(
+        functools.partial(local_kernel, width=width),
+        grid=(STEPS,),
+        out_shape=(
+            jax.ShapeDtypeStruct((2 * tokens, LANES), BF16),
+            jax.ShapeDtypeStruct(square, BF16),
+            jax.ShapeDtypeStruct(square, F32),
+            jax.ShapeDtypeStruct(square, F32),
+            jax.ShapeDtypeStruct(square, F32),
+        ),
+        in_specs=[
+            pl.BlockSpec((tokens, span), by_column),
+            pl.BlockSpec((tokens, span), by_column),
+            pl.BlockSpec((tokens, span), by_column),
+            pl.BlockSpec((tokens, value_span), by_column),
+            pl.BlockSpec((1, span), by_column),
+            pl.BlockSpec((LANES // 2, span), by_column),
+            pl.BlockSpec((span, LANES), by_row),
+            pl.BlockSpec((value_span, LANES), by_row),
+        ],
+        out_specs=(
+            pl.BlockSpec((2 * tokens, LANES), whole),
+            pl.BlockSpec(square, whole),
+            pl.BlockSpec(square, whole),
+            pl.BlockSpec(square, whole),
+            pl.BlockSpec(square, whole),
+        ),
+        scratch_shapes=[pltpu.VMEM(square, F32)] * 4,
+        compiler_params=params(24),
+        cost_estimate=cost(tokens * width * LANES * 12, 12 * MIB),
+        name="local_products",
+    )(
+        x,
+        mixed,
+        adjoint,
+        values,
+        top_rmsnorm_weights.reshape(1, width),
+        source_sketch.T,
+        bottom_target_sketch,
+        top_target_sketch,
+    )
+
+    unit = pl.pallas_call(
+        functools.partial(feature_kernel, len(pieces)),
+        out_shape=jax.ShapeDtypeStruct((LANES, LANES), BF16),
+        in_specs=[SMEM, SMEM] + [ANY] * (len(pieces) + 5) + [VMEM] * 7,
+        out_specs=VMEM,
+        scratch_shapes=[
+            pltpu.VMEM((len(pieces), 3 * rows, LANES), BF16),
+            pltpu.VMEM(x.shape, BF16),
+            pltpu.VMEM(x.shape, BF16),
+            pltpu.VMEM(x.shape, BF16),
+            pltpu.VMEM(values.shape, BF16),
+            pltpu.VMEM(bottom_target_sketch.shape, BF16),
+            pltpu.SemaphoreType.DMA((len(pieces),)),
+            pltpu.SemaphoreType.DMA((STEPS, 5)),
+        ],
+        compiler_params=params(32),
+        cost_estimate=cost(tokens * width * LANES * 12, 16 * MIB),
+        name="features",
+    )(
+        jnp.stack(slots),
+        sequence_token_counts,
+        *pieces,
+        x,
+        mixed,
+        adjoint,
+        values,
+        bottom_target_sketch,
+        lefts,
+        right,
+        x_target,
+        adjoint_target,
+        inverse,
+        top_expander_sketch.T,
+        top_reducer_sketch,
+    )
+
+    task_best, scores = pl.pallas_call(
+        functools.partial(score_kernel, len(panels), count),
+        out_shape=(jax.ShapeDtypeStruct((2, TASKS), F32), jax.ShapeDtypeStruct((2,), F32)),
+        in_specs=[VMEM] * (1 + len(panels)),
+        out_specs=(SMEM, SMEM),
+        scratch_shapes=[pltpu.VMEM((2, LANES // 2 * count, LANES), F32)],
+        compiler_params=params(16),
+        cost_estimate=cost(4 * MIB, 2 * MIB),
+        name="scores",
+    )(unit, *panels)
+    return (scores, task_best)
+
+
+def shards_of_any_slice(
     hidden_state_input,
     attention_mixed_state,
     hidden_state_adjoint,
@@ -106,7 +505,7 @@
     down_lower = mm(bottom_reducer_matrix, bottom_expander_sketch).astype(BF16)
     packed_lower = jnp.concatenate([down_lower[: rows // 2], down_lower[rows // 2 :]], axis=1)
     factors = jnp.concatenate([down_upper, up_lower, top_expander_matrix.T, packed_lower], axis=0)
-    factors = gather_blocks(factors, n)
+    factors = lax.all_gather(factors, "dp")
 
     val_wide = heldout_sketched_signals.astype(F32)
     val_unit = (
@@ -114,7 +513,7 @@
     ).astype(BF16)
     labels = jnp.broadcast_to(benchmark_labels.astype(BF16), (val_unit.shape[0], 128))
     panel = jnp.concatenate([val_unit.reshape(-1, 128), labels], axis=0)
-    panel = gather_blocks(panel, n)
+    panel = lax.all_gather(panel, "dp")
     val_rows = val_unit.shape[0]
     cut = panel.shape[1] - val_rows
     panel_tasks = panel[:, cut:, 0].reshape(n * val_rows, 1).astype(jnp.int32)
@@ -189,8 +588,9 @@
         + (by_row, by_column, by_row, by_column)
         + (whole,) * 7
     )
+    ours = shards if n == 2 * RING_CHIPS else functools.partial(shards_of_any_slice, n=n)
     return jax.shard_map(
-        lambda *arrays: shards(*arrays, n),
+        ours,
         mesh=mesh,
         in_specs=placed,
         out_specs=(P(("parts", "dp")), split),

time: 112 us -> 81.3 us (0.73)
  local copies, waits for them, and re-layouts: 49.7 us -> 20.9 us
  matrix products: 18.9 us -> 0 us
  Pallas kernels: 0 us -> 17.6 us
  other arithmetic: 10.6 us -> 0 us
  waiting for transfers between devices: 9.6 us -> 19.6 us
    dynamic_update_slice x34 -> x0, local copies, waits for them, and re-layouts: 29.6 us -> none  [the longest x18 15.9 us: gather_blocks(): lax.dynamic_update_slice(out, other_core(piece)[None], (base + 1 - core,...]
    unnamed x43 -> x84, local copies, waits for them, and re-layouts: 1.82 us -> 20.8 us
    dot_general x15 -> x0, matrix products: 18.9 us -> none  [the longest x13 16.4 us: mm(): return jnp.dot(a, b, preferred_element_type=F32)]
    pallas_call x0 -> x5, Pallas kernels: none -> 17.6 us  [the longest x1 10.7 us: shards(): pl.pallas_call(functools.partial(feature_kernel, len(pieces)), out_shape=...]
    ppermute x16 -> x14, waiting for transfers between devices: 9.55 us -> 19.6 us  [hop(): return lax.ppermute(value, 'dp', pairs)]
    slice x11 -> x0, local copies, waits for them, and re-layouts: 8.49 us -> none  [the longest x1 3.15 us: shards(): panel = panel[:, :cut].reshape(n * val_rows, val_unit.shape[1])]
    broadcast_in_dim x2 -> x0, local copies, waits for them, and re-layouts: 4.27 us -> none  [gather_blocks(): out = jnp.zeros((n,) + block.shape, block.dtype)]
    reshape x2 -> x0, local copies, waits for them, and re-layouts: 4.24 us -> none  [the longest x1 4.18 us: shards(): panel = panel[:, :cut].reshape(n * val_rows, val_unit.shape[1])]
  transfers between devices with their start and end apart: 34 -> 30, of which waited for: 4 -> 7; matrix products, arithmetic and copies ran while one was open for 47% -> 0% of each run, Pallas kernels for 0% -> 19%
where the time goes in v2:
time: 81.3 us; the launch traced here: 80.5 us
  starting transfers between devices  21.2 us (26%)
  local copies, waits for them, and re-layouts  20.9 us (26%)
  waiting for transfers between devices  19.6 us (24%)
  Pallas kernels  17.6 us (22%)
  between operations  1.16 us (1%)
    unnamed x84, local copies, waits for them, and re-layouts  20.8 us
    ppermute x14, waiting for transfers between devices, hop(): return lax.ppermute(value, 'dp', pairs)  19.6 us
    ppermute x14, starting transfers between devices, hop(): return lax.ppermute(value, 'dp', pairs)  18.2 us
    pallas_call x1, Pallas kernels, shards(): pl.pallas_call(functools.partial(feature_kernel, len(pieces)), out_shape=...  10.7 us
    pallas_call x1, Pallas kernels, shards(): pl.pallas_call(functools.partial(local_kernel, width=width), grid=(STEPS,...  4.81 us
    ppermute x16, starting transfers between devices, other_core(): lax.ppermute(value, 'dp', [(d, d ^ 1) for d in range(2 * RING_CHIPS)])  3.01 us
    pallas_call x1, Pallas kernels, shards(): pl.pallas_call(functools.partial(score_kernel, len(panels), count), out_s...  1.71 us
  transfers between devices with their start and end apart: 30, of which 7 were waited for; matrix products, arithmetic and copies ran while one was open for 0% of the time, Pallas kernels for 19%

profile of v2, /device:TPU:0, one launch (start us, length us, event | category | flops | bytes accessed | tf_op | source)
XLA Modules:
  0.0 80.5 jit_solution(2252133934938374848)
XLA Ops:
  1.4 0.9 %copy-done.32 = bf16[320,128]{1,0:T(8,128)(2,1)S(1)} copy-done((bf16[320,128]{1,0:T(8,128)(2,1)S(1)}, bf16[320,128]{1,0:T(8,128)(2,1)}, u32[]{:S(2)}) %copy-start.32) | copy-done | bytes 81944
  2.3 0.9 %copy-done.33 = bf16[128,320]{0,1:T(8,128)(2,1)S(1)} copy-done((bf16[128,320]{0,1:T(8,128)(2,1)S(1)}, bf16[128,320]{0,1:T(8,128)(2,1)}, u32[]{:S(2)}) %copy-start.33) | copy-done | bytes 81944
  3.1 0.9 %copy-done.34 = bf16[320,128]{1,0:T(8,128)(2,1)S(1)} copy-done((bf16[320,128]{1,0:T(8,128)(2,1)S(1)}, bf16[320,128]{1,0:T(8,128)(2,1)}, u32[]{:S(2)}) %copy-start.34) | copy-done | bytes 81944
  4.0 0.8 copy-done.35
  4.8 0.8 copy-done.37
  6.5 3.1 %collective-permute-start.1 = (bf16[960,128]{1,0:T(8,128)(2,1)S(1)}, bf16[960,128]{1,0:T(8,128)(2,1)S(1)}, u32[]{:S(2)}, u32[]{:S(2)}) collective-permute-start(bf16[960,128]{1,0:T(8,128)(2,1)S(1)} %factors.1.refs_0_), channel_id=1, source_target_pairs={{0,4},{1,5},{4,8},{5,9},{8,12},{9,13},{12,14},{13,15},{14,10},{15,... | collective-permute-start | bytes 737288 | tf_op jit(solution)/shard_map/ppermute | solution.py:50
  9.6 0.9 %copy-done.29 = bf16[8,8192]{1,0:T(8,128)(2,1)S(1)} copy-done((bf16[8,8192]{1,0:T(8,128)(2,1)S(1)}, bf16[8,8192]{1,0:T(8,128)(2,1)}, u32[]{:S(2)}) %copy-start.29) | copy-done | bytes 131096
  11.4 2.0 %collective-permute-start.3 = (bf16[960,128]{1,0:T(8,128)(2,1)S(1)}, bf16[960,128]{1,0:T(8,128)(2,1)S(1)}, u32[]{:S(2)}, u32[]{:S(2)}) collective-permute-start(bf16[960,128]{1,0:T(8,128)(2,1)S(1)} %factors.1.refs_0_), channel_id=1, source_target_pairs={{0,2},{1,3},{4,0},{5,1},{8,4},{9,5},{12,8},{13,9},{14,12},{15,13},... | collective-permute-start | bytes 737288 | tf_op jit(solution)/shard_map/ppermute | solution.py:50
  13.3 2.1 %collective-permute-done.1.refs_2_ = bf16[960,128]{1,0:T(8,128)(2,1)S(1)} collective-permute-done((bf16[960,128]{1,0:T(8,128)(2,1)S(1)}, bf16[960,128]{1,0:T(8,128)(2,1)S(1)}, u32[]{:S(2)}, u32[]{:S(2)}) %collective-permute-start.1) | collective-permute-done | bytes 245792 | tf_op jit(solution)/shard_map/ppermute | solution.py:50
  15.5 1.8 %collective-permute-start.5 = (bf16[960,128]{1,0:T(8,128)(2,1)S(1)}, bf16[960,128]{1,0:T(8,128)(2,1)S(1)}, u32[]{:S(2)}, u32[]{:S(2)}) collective-permute-start(bf16[960,128]{1,0:T(8,128)(2,1)S(1)} %collective-permute-done.1.refs_2_), channel_id=1, source_target_pairs={{0,4},{1,5},{4,8},{5,9},{8,12},{9,13},{12,14},{13,15},{14,10},{15,... | collective-permute-start | bytes 737288 | tf_op jit(solution)/shard_map/ppermute | solution.py:50
  17.3 1.6 %collective-permute-start.16 = (bf16[528,128]{1,0:T(8,128)(2,1)S(1)}, bf16[528,128]{1,0:T(8,128)(2,1)S(1)}, u32[]{:S(2)}, u32[]{:S(2)}) collective-permute-start(bf16[528,128]{1,0:T(8,128)(2,1)S(1)} %panel.1.refs_0_), channel_id=1, source_target_pairs={{0,4},{1,5},{4,8},{5,9},{8,12},{9,13},{12,14},{13,15},{14,10},{15,... | collective-permute-start | bytes 405512 | tf_op jit(solution)/shard_map/ppermute | solution.py:50
  19.3 6.1 %collective-permute-done.16.refs_2_ = bf16[528,128]{1,0:T(8,128)(2,1)S(1)} collective-permute-done((bf16[528,128]{1,0:T(8,128)(2,1)S(1)}, bf16[528,128]{1,0:T(8,128)(2,1)S(1)}, u32[]{:S(2)}, u32[]{:S(2)}) %collective-permute-start.16) | collective-permute-done | bytes 135200 | tf_op jit(solution)/shard_map/ppermute | solution.py:50
  25.5 1.4 %collective-permute-start.22 = (bf16[528,128]{1,0:T(8,128)(2,1)S(1)}, bf16[528,128]{1,0:T(8,128)(2,1)S(1)}, u32[]{:S(2)}, u32[]{:S(2)}) collective-permute-start(bf16[528,128]{1,0:T(8,128)(2,1)S(1)} %collective-permute-done.18.refs_4_), channel_id=1, source_target_pairs={{0,2},{1,3},{4,0},{5,1},{8,4},{9,5},{12,8},{13,9},{14,12},{15,13},... | collective-permute-start | bytes 405512 | tf_op jit(solution)/shard_map/ppermute | solution.py:50
  28.2 1.4 %collective-permute-start.7 = (bf16[960,128]{1,0:T(8,128)(2,1)S(1)}, bf16[960,128]{1,0:T(8,128)(2,1)S(1)}, u32[]{:S(2)}, u32[]{:S(2)}) collective-permute-start(bf16[960,128]{1,0:T(8,128)(2,1)S(1)} %collective-permute-done.3.refs_4_), channel_id=1, source_target_pairs={{0,2},{1,3},{4,0},{5,1},{8,4},{9,5},{12,8},{13,9},{14,12},{15,13},... | collective-permute-start | bytes 737288 | tf_op jit(solution)/shard_map/ppermute | solution.py:50
  30.9 1.0 %collective-permute-done.22.refs_8_ = bf16[528,128]{1,0:T(8,128)(2,1)S(1)} collective-permute-done((bf16[528,128]{1,0:T(8,128)(2,1)S(1)}, bf16[528,128]{1,0:T(8,128)(2,1)S(1)}, u32[]{:S(2)}, u32[]{:S(2)}) %collective-permute-start.22) | collective-permute-done | bytes 135200 | tf_op jit(solution)/shard_map/ppermute | solution.py:50
  31.9 1.6 %collective-permute-done.20.refs_6_ = bf16[528,128]{1,0:T(8,128)(2,1)S(1)} collective-permute-done((bf16[528,128]{1,0:T(8,128)(2,1)S(1)}, bf16[528,128]{1,0:T(8,128)(2,1)S(1)}, u32[]{:S(2)}, u32[]{:S(2)}) %collective-permute-start.20) | collective-permute-done | bytes 135200 | tf_op jit(solution)/shard_map/ppermute | solution.py:50
  33.5 1.6 %collective-permute-start.26 = (bf16[528,128]{1,0:T(8,128)(2,1)S(1)}, bf16[528,128]{1,0:T(8,128)(2,1)S(1)}, u32[]{:S(2)}, u32[]{:S(2)}) collective-permute-start(bf16[528,128]{1,0:T(8,128)(2,1)S(1)} %collective-permute-done.22.refs_8_), channel_id=1, source_target_pairs={{0,2},{1,3},{4,0},{5,1},{8,4},{9,5},{12,8},{13,9},{14,12},{15,13},... | collective-permute-start | bytes 405512 | tf_op jit(solution)/shard_map/ppermute | solution.py:50
  36.8 1.7 %collective-permute-done.26.refs_12_ = bf16[528,128]{1,0:T(8,128)(2,1)S(1)} collective-permute-done((bf16[528,128]{1,0:T(8,128)(2,1)S(1)}, bf16[528,128]{1,0:T(8,128)(2,1)S(1)}, u32[]{:S(2)}, u32[]{:S(2)}) %collective-permute-start.26) | collective-permute-done | bytes 135200 | tf_op jit(solution)/shard_map/ppermute | solution.py:50
  38.5 1.6 %collective-permute-start.11 = (bf16[960,128]{1,0:T(8,128)(2,1)S(1)}, bf16[960,128]{1,0:T(8,128)(2,1)S(1)}, u32[]{:S(2)}, u32[]{:S(2)}) collective-permute-start(bf16[960,128]{1,0:T(8,128)(2,1)S(1)} %collective-permute-done.7.refs_8_), channel_id=1, source_target_pairs={{0,2},{1,3},{4,0},{5,1},{8,4},{9,5},{12,8},{13,9},{14,12},{15,13},... | collective-permute-start | bytes 737288 | tf_op jit(solution)/shard_map/ppermute | solution.py:50
  40.7 1.6 %collective-permute-start.28 = (bf16[528,128]{1,0:T(8,128)(2,1)S(1)}, bf16[528,128]{1,0:T(8,128)(2,1)S(1)}, u32[]{:S(2)}, u32[]{:S(2)}) collective-permute-start(bf16[528,128]{1,0:T(8,128)(2,1)S(1)} %collective-permute-done.26.refs_12_), channel_id=1, source_target_pairs={{0,2},{1,3},{4,0},{5,1},{8,4},{9,5},{12,8},{13,9},{14,12},{15,13},... | collective-permute-start | bytes 405512 | tf_op jit(solution)/shard_map/ppermute | solution.py:50
  42.9 6.9 %collective-permute-done.28.refs_14_ = bf16[528,128]{1,0:T(8,128)(2,1)S(1)} collective-permute-done((bf16[528,128]{1,0:T(8,128)(2,1)S(1)}, bf16[528,128]{1,0:T(8,128)(2,1)S(1)}, u32[]{:S(2)}, u32[]{:S(2)}) %collective-permute-start.28) | collective-permute-done | bytes 135200 | tf_op jit(solution)/shard_map/ppermute | solution.py:50
  50.7 1.7 %copy-done = bf16[256,5120]{1,0:T(8,128)(2,1)S(1)} copy-done((bf16[256,5120]{1,0:T(8,128)(2,1)S(1)}, bf16[256,5120]{1,0:T(8,128)(2,1)}, u32[]{:S(2)}) %copy-start) | copy-done | bytes 2621464
  52.5 1.7 %copy-done.2 = bf16[256,5120]{1,0:T(8,128)(2,1)S(1)} copy-done((bf16[256,5120]{1,0:T(8,128)(2,1)S(1)}, bf16[256,5120]{1,0:T(8,128)(2,1)}, u32[]{:S(2)}) %copy-start.2) | copy-done | bytes 2621464
  54.2 1.7 %copy-done.4 = bf16[256,5120]{1,0:T(8,128)(2,1)S(1)} copy-done((bf16[256,5120]{1,0:T(8,128)(2,1)S(1)}, bf16[256,5120]{1,0:T(8,128)(2,1)}, u32[]{:S(2)}) %copy-start.4) | copy-done | bytes 2621464
  56.0 1.3 %copy-done.6 = bf16[256,2560]{1,0:T(8,128)(2,1)S(1)} copy-done((bf16[256,2560]{1,0:T(8,128)(2,1)S(1)}, bf16[256,2560]{1,0:T(8,128)(2,1)}, u32[]{:S(2)}) %copy-start.6) | copy-done | bytes 1310744
  57.3 1.3 %copy-done.8 = bf16[5120,128]{1,0:T(8,128)(2,1)S(1)} copy-done((bf16[5120,128]{1,0:T(8,128)(2,1)S(1)}, bf16[5120,128]{1,0:T(8,128)(2,1)}, u32[]{:S(2)}) %copy-start.8) | copy-done | bytes 1310744
  58.6 1.1 %copy-done.9 = bf16[5120,64]{0,1:T(8,128)(2,1)S(1)} copy-done((bf16[5120,64]{0,1:T(8,128)(2,1)S(1)}, bf16[5120,64]{0,1:T(8,128)(2,1)}, u32[]{:S(2)}) %copy-start.9) | copy-done | bytes 655384
  59.7 1.1 %copy-done.10 = bf16[2560,128]{1,0:T(8,128)(2,1)S(1)} copy-done((bf16[2560,128]{1,0:T(8,128)(2,1)S(1)}, bf16[2560,128]{1,0:T(8,128)(2,1)}, u32[]{:S(2)}) %copy-start.10) | copy-done | bytes 655384
  60.8 0.7 copy-done.31
  61.6 4.8 %local_products.1 = (bf16[512,128]{1,0:T(8,128)(2,1)S(1)}, bf16[256,128]{1,0:T(8,128)(2,1)S(1)}, f32[256,128]{1,0:T(8,128)S(1)}, f32[256,128]{1,0:T(8,128)S(1)}, f32[256,128]{1,0:T(8,128)S(1)}) custom-call(bf16[256,5120]{1,0:T(8,128)(2,1)S(1)} %copy-done, bf16[256,5120]{1,0:T(8,128)(2,1)S(1)} %copy-done.2, bf16[256,5120]{1,0:T(8,128)(2,1)S(1)} %copy-done.4, ...), custom_call_target="tpu_custom_call" | custom-call | flops 2013265920 | bytes 12582912 | tf_op jit(solution)/shard_map/local_products/pallas_call | solution.py:375
  68.0 10.7 %features.1.unit_ref = bf16[128,128]{1,0:T(8,128)(2,1)S(1)} custom-call(s32[16]{0:T(128)S(1)} %stack.67.slots_ref, s32[1,2]{1,0:T(1,128)S(1)} %copy-done.40, bf16[960,128]{1,0:T(8,128)(2,1)S(1)} %factors.1.refs_0_, bf16[960,128]{1,0:T(8,128)(2,1)S(1)} %collective-permute-done.refs_1_, bf16[960,128]{1,0:T(8,128)(2,1)S(1)} %collective-permute-done.1.refs_2_, ...), custom_call_target="tpu_custom_call" | custom-call | flops 2013265920 | bytes 16777216 | tf_op jit(solution)/shard_map/features/pallas_call | solution.py:417
  78.8 1.7 %scores.1 = (f32[2,3]{1,0:T(2,128)}, f32[2]{0:T(128)}) custom-call(bf16[128,128]{1,0:T(8,128)(2,1)S(1)} %features.1.unit_ref, bf16[528,128]{1,0:T(8,128)(2,1)S(1)} %panel.1.refs_0_, bf16[528,128]{1,0:T(8,128)(2,1)S(1)} %copy-done.14, bf16[528,128]{1,0:T(8,128)(2,1)S(1)} %copy-done.12, bf16[528,128]{1,0:T(8,128)(2,1)S(1)} %copy-done.20, ...), custom_call_target="tpu_custom_call" | custom-call | flops 4194304 | bytes 2097152 | tf_op jit(solution)/shard_map/scores/pallas_call | solution.py:453
  (118 shorter events, 10.8 us)
Async XLA Ops:
  6.5 9.0 %collective-permute-start.1 = (bf16[960,128]{1,0:T(8,128)(2,1)S(1)}, bf16[960,128]{1,0:T(8,128)(2,1)S(1)}, u32[]{:S(2)}, u32[]{:S(2)}) collective-permute-start(bf16[960,128]{1,0:T(8,128)(2,1)S(1)} %factors.1.refs_0_), channel_id=1, source_target_pairs={{0,4},{1,5},{4,8},{5,9},{8,12},{9,13},{12,14},{13,15},{14,10},{15,... | collective-permute-start | bytes 737288 | tf_op jit(solution)/shard_map/ppermute | solution.py:50
  11.3 7.5 %collective-permute-start.18 = (bf16[528,128]{1,0:T(8,128)(2,1)S(1)}, bf16[528,128]{1,0:T(8,128)(2,1)S(1)}, u32[]{:S(2)}, u32[]{:S(2)}) collective-permute-start(bf16[528,128]{1,0:T(8,128)(2,1)S(1)} %panel.1.refs_0_), channel_id=1, source_target_pairs={{0,2},{1,3},{4,0},{5,1},{8,4},{9,5},{12,8},{13,9},{14,12},{15,13},... | collective-permute-start | bytes 405512 | tf_op jit(solution)/shard_map/ppermute | solution.py:50
  11.4 16.8 %collective-permute-start.3 = (bf16[960,128]{1,0:T(8,128)(2,1)S(1)}, bf16[960,128]{1,0:T(8,128)(2,1)S(1)}, u32[]{:S(2)}, u32[]{:S(2)}) collective-permute-start(bf16[960,128]{1,0:T(8,128)(2,1)S(1)} %factors.1.refs_0_), channel_id=1, source_target_pairs={{0,2},{1,3},{4,0},{5,1},{8,4},{9,5},{12,8},{13,9},{14,12},{15,13},... | collective-permute-start | bytes 737288 | tf_op jit(solution)/shard_map/ppermute | solution.py:50
  15.5 14.2 %collective-permute-start.5 = (bf16[960,128]{1,0:T(8,128)(2,1)S(1)}, bf16[960,128]{1,0:T(8,128)(2,1)S(1)}, u32[]{:S(2)}, u32[]{:S(2)}) collective-permute-start(bf16[960,128]{1,0:T(8,128)(2,1)S(1)} %collective-permute-done.1.refs_2_), channel_id=1, source_target_pairs={{0,4},{1,5},{4,8},{5,9},{8,12},{9,13},{12,14},{13,15},{14,10},{15,... | collective-permute-start | bytes 737288 | tf_op jit(solution)/shard_map/ppermute | solution.py:50
  17.3 8.2 %collective-permute-start.16 = (bf16[528,128]{1,0:T(8,128)(2,1)S(1)}, bf16[528,128]{1,0:T(8,128)(2,1)S(1)}, u32[]{:S(2)}, u32[]{:S(2)}) collective-permute-start(bf16[528,128]{1,0:T(8,128)(2,1)S(1)} %panel.1.refs_0_), channel_id=1, source_target_pairs={{0,4},{1,5},{4,8},{5,9},{8,12},{9,13},{12,14},{13,15},{14,10},{15,... | collective-permute-start | bytes 405512 | tf_op jit(solution)/shard_map/ppermute | solution.py:50
  18.8 8.1 %collective-permute-start.15 = (bf16[528,128]{1,0:T(8,128)(2,1)S(1)}, bf16[528,128]{1,0:T(8,128)(2,1)S(1)}, u32[]{:S(2)}, u32[]{:S(2)}) collective-permute-start(bf16[528,128]{1,0:T(8,128)(2,1)S(1)} %panel.1.refs_0_), channel_id=1, source_target_pairs={{0,1},{1,0},{2,3},{3,2},{4,5},{5,4},{6,7},{7,6},{8,9},{9,8},{10,11... | collective-permute-start | bytes 405512 | tf_op jit(solution)/shard_map/ppermute | solution.py:54
  18.8 11.4 %collective-permute-start = (bf16[960,128]{1,0:T(8,128)(2,1)S(1)}, bf16[960,128]{1,0:T(8,128)(2,1)S(1)}, u32[]{:S(2)}, u32[]{:S(2)}) collective-permute-start(bf16[960,128]{1,0:T(8,128)(2,1)S(1)} %factors.1.refs_0_), channel_id=1, source_target_pairs={{0,1},{1,0},{2,3},{3,2},{4,5},{5,4},{6,7},{7,6},{8,9},{9,8},{10,11... | collective-permute-start | bytes 737288 | tf_op jit(solution)/shard_map/ppermute | solution.py:54
  25.5 6.4 %collective-permute-start.22 = (bf16[528,128]{1,0:T(8,128)(2,1)S(1)}, bf16[528,128]{1,0:T(8,128)(2,1)S(1)}, u32[]{:S(2)}, u32[]{:S(2)}) collective-permute-start(bf16[528,128]{1,0:T(8,128)(2,1)S(1)} %collective-permute-done.18.refs_4_), channel_id=1, source_target_pairs={{0,2},{1,3},{4,0},{5,1},{8,4},{9,5},{12,8},{13,9},{14,12},{15,13},... | collective-permute-start | bytes 405512 | tf_op jit(solution)/shard_map/ppermute | solution.py:50
  27.6 5.9 %collective-permute-start.20 = (bf16[528,128]{1,0:T(8,128)(2,1)S(1)}, bf16[528,128]{1,0:T(8,128)(2,1)S(1)}, u32[]{:S(2)}, u32[]{:S(2)}) collective-permute-start(bf16[528,128]{1,0:T(8,128)(2,1)S(1)} %collective-permute-done.16.refs_2_), channel_id=1, source_target_pairs={{0,4},{1,5},{4,8},{5,9},{8,12},{9,13},{12,14},{13,15},{14,10},{15,... | collective-permute-start | bytes 405512 | tf_op jit(solution)/shard_map/ppermute | solution.py:50
  28.2 10.3 %collective-permute-start.7 = (bf16[960,128]{1,0:T(8,128)(2,1)S(1)}, bf16[960,128]{1,0:T(8,128)(2,1)S(1)}, u32[]{:S(2)}, u32[]{:S(2)}) collective-permute-start(bf16[960,128]{1,0:T(8,128)(2,1)S(1)} %collective-permute-done.3.refs_4_), channel_id=1, source_target_pairs={{0,2},{1,3},{4,0},{5,1},{8,4},{9,5},{12,8},{13,9},{14,12},{15,13},... | collective-permute-start | bytes 737288 | tf_op jit(solution)/shard_map/ppermute | solution.py:50
  29.6 10.5 %collective-permute-start.9 = (bf16[960,128]{1,0:T(8,128)(2,1)S(1)}, bf16[960,128]{1,0:T(8,128)(2,1)S(1)}, u32[]{:S(2)}, u32[]{:S(2)}) collective-permute-start(bf16[960,128]{1,0:T(8,128)(2,1)S(1)} %collective-permute-done.5.refs_6_), channel_id=1, source_target_pairs={{0,4},{1,5},{4,8},{5,9},{8,12},{9,13},{12,14},{13,15},{14,10},{15,... | collective-permute-start | bytes 737288 | tf_op jit(solution)/shard_map/ppermute | solution.py:50
  30.2 4.8 %collective-permute-start.17 = (bf16[528,128]{1,0:T(8,128)(2,1)S(1)}, bf16[528,128]{1,0:T(8,128)(2,1)S(1)}, u32[]{:S(2)}, u32[]{:S(2)}) collective-permute-start(bf16[528,128]{1,0:T(8,128)(2,1)S(1)} %collective-permute-done.16.refs_2_), channel_id=1, source_target_pairs={{0,1},{1,0},{2,3},{3,2},{4,5},{5,4},{6,7},{7,6},{8,9},{9,8},{10,11... | collective-permute-start | bytes 405512 | tf_op jit(solution)/shard_map/ppermute | solution.py:54
  31.9 4.3 %collective-permute-start.19 = (bf16[528,128]{1,0:T(8,128)(2,1)S(1)}, bf16[528,128]{1,0:T(8,128)(2,1)S(1)}, u32[]{:S(2)}, u32[]{:S(2)}) collective-permute-start(bf16[528,128]{1,0:T(8,128)(2,1)S(1)} %collective-permute-done.18.refs_4_), channel_id=1, source_target_pairs={{0,1},{1,0},{2,3},{3,2},{4,5},{5,4},{6,7},{7,6},{8,9},{9,8},{10,11... | collective-permute-start | bytes 405512 | tf_op jit(solution)/shard_map/ppermute | solution.py:54
  33.5 5.0 %collective-permute-start.26 = (bf16[528,128]{1,0:T(8,128)(2,1)S(1)}, bf16[528,128]{1,0:T(8,128)(2,1)S(1)}, u32[]{:S(2)}, u32[]{:S(2)}) collective-permute-start(bf16[528,128]{1,0:T(8,128)(2,1)S(1)} %collective-permute-done.22.refs_8_), channel_id=1, source_target_pairs={{0,2},{1,3},{4,0},{5,1},{8,4},{9,5},{12,8},{13,9},{14,12},{15,13},... | collective-permute-start | bytes 405512 | tf_op jit(solution)/shard_map/ppermute | solution.py:50
  35.7 5.0 %collective-permute-start.24 = (bf16[528,128]{1,0:T(8,128)(2,1)S(1)}, bf16[528,128]{1,0:T(8,128)(2,1)S(1)}, u32[]{:S(2)}, u32[]{:S(2)}) collective-permute-start(bf16[528,128]{1,0:T(8,128)(2,1)S(1)} %collective-permute-done.20.refs_6_), channel_id=1, source_target_pairs={{0,4},{1,5},{4,8},{5,9},{8,12},{9,13},{12,14},{13,15},{14,10},{15,... | collective-permute-start | bytes 405512 | tf_op jit(solution)/shard_map/ppermute | solution.py:50
  36.8 5.5 %collective-permute-start.2 = (bf16[960,128]{1,0:T(8,128)(2,1)S(1)}, bf16[960,128]{1,0:T(8,128)(2,1)S(1)}, u32[]{:S(2)}, u32[]{:S(2)}) collective-permute-start(bf16[960,128]{1,0:T(8,128)(2,1)S(1)} %collective-permute-done.1.refs_2_), channel_id=1, source_target_pairs={{0,1},{1,0},{2,3},{3,2},{4,5},{5,4},{6,7},{7,6},{8,9},{9,8},{10,11... | collective-permute-start | bytes 737288 | tf_op jit(solution)/shard_map/ppermute | solution.py:54
  38.5 11.8 %copy-start.23 = (bf16[528,128]{1,0:T(8,128)(2,1)}, bf16[528,128]{1,0:T(8,128)(2,1)S(1)}, u32[]{:S(2)}) copy-start(bf16[528,128]{1,0:T(8,128)(2,1)S(1)} %collective-permute-done.26.refs_12_) | copy-start | bytes 405508
  38.5 3.9 %collective-permute-start.4 = (bf16[960,128]{1,0:T(8,128)(2,1)S(1)}, bf16[960,128]{1,0:T(8,128)(2,1)S(1)}, u32[]{:S(2)}, u32[]{:S(2)}) collective-permute-start(bf16[960,128]{1,0:T(8,128)(2,1)S(1)} %collective-permute-done.3.refs_4_), channel_id=1, source_target_pairs={{0,1},{1,0},{2,3},{3,2},{4,5},{5,4},{6,7},{7,6},{8,9},{9,8},{10,11... | collective-permute-start | bytes 737288 | tf_op jit(solution)/shard_map/ppermute | solution.py:54
  38.5 11.3 %collective-permute-start.11 = (bf16[960,128]{1,0:T(8,128)(2,1)S(1)}, bf16[960,128]{1,0:T(8,128)(2,1)S(1)}, u32[]{:S(2)}, u32[]{:S(2)}) collective-permute-start(bf16[960,128]{1,0:T(8,128)(2,1)S(1)} %collective-permute-done.7.refs_8_), channel_id=1, source_target_pairs={{0,2},{1,3},{4,0},{5,1},{8,4},{9,5},{12,8},{13,9},{14,12},{15,13},... | collective-permute-start | bytes 737288 | tf_op jit(solution)/shard_map/ppermute | solution.py:50
  40.1 10.2 %collective-permute-start.13 = (bf16[960,128]{1,0:T(8,128)(2,1)S(1)}, bf16[960,128]{1,0:T(8,128)(2,1)S(1)}, u32[]{:S(2)}, u32[]{:S(2)}) collective-permute-start(bf16[960,128]{1,0:T(8,128)(2,1)S(1)} %collective-permute-done.9.refs_10_), channel_id=1, source_target_pairs={{0,4},{1,5},{4,8},{5,9},{8,12},{9,13},{12,14},{13,15},{14,10},{15,... | collective-permute-start | bytes 737288 | tf_op jit(solution)/shard_map/ppermute | solution.py:50
  40.7 9.1 %collective-permute-start.28 = (bf16[528,128]{1,0:T(8,128)(2,1)S(1)}, bf16[528,128]{1,0:T(8,128)(2,1)S(1)}, u32[]{:S(2)}, u32[]{:S(2)}) collective-permute-start(bf16[528,128]{1,0:T(8,128)(2,1)S(1)} %collective-permute-done.26.refs_12_), channel_id=1, source_target_pairs={{0,2},{1,3},{4,0},{5,1},{8,4},{9,5},{12,8},{13,9},{14,12},{15,13},... | collective-permute-start | bytes 405512 | tf_op jit(solution)/shard_map/ppermute | solution.py:50
  42.3 24.1 %collective-permute-start.6 = (bf16[960,128]{1,0:T(8,128)(2,1)S(1)}, bf16[960,128]{1,0:T(8,128)(2,1)S(1)}, u32[]{:S(2)}, u32[]{:S(2)}) collective-permute-start(bf16[960,128]{1,0:T(8,128)(2,1)S(1)} %collective-permute-done.5.refs_6_), channel_id=1, source_target_pairs={{0,1},{1,0},{2,3},{3,2},{4,5},{5,4},{6,7},{7,6},{8,9},{9,8},{10,11... | collective-permute-start | bytes 737288 | tf_op jit(solution)/shard_map/ppermute | solution.py:54
  42.4 24.4 %collective-permute-start.8 = (bf16[960,128]{1,0:T(8,128)(2,1)S(1)}, bf16[960,128]{1,0:T(8,128)(2,1)S(1)}, u32[]{:S(2)}, u32[]{:S(2)}) collective-permute-start(bf16[960,128]{1,0:T(8,128)(2,1)S(1)} %collective-permute-done.7.refs_8_), channel_id=1, source_target_pairs={{0,1},{1,0},{2,3},{3,2},{4,5},{5,4},{6,7},{7,6},{8,9},{9,8},{10,11... | collective-permute-start | bytes 737288 | tf_op jit(solution)/shard_map/ppermute | solution.py:54
  49.8 17.2 %collective-permute-start.10 = (bf16[960,128]{1,0:T(8,128)(2,1)S(1)}, bf16[960,128]{1,0:T(8,128)(2,1)}, u32[]{:S(2)}, u32[]{:S(2)}) collective-permute-start(bf16[960,128]{1,0:T(8,128)(2,1)S(1)} %collective-permute-done.9.refs_10_), channel_id=1, source_target_pairs={{0,1},{1,0},{2,3},{3,2},{4,5},{5,4},{6,7},{7,6},{8,9},{9,8},{10,11... | collective-permute-start | bytes 737288 | tf_op jit(solution)/shard_map/ppermute | solution.py:54
  49.8 17.6 %collective-permute-start.12 = (bf16[960,128]{1,0:T(8,128)(2,1)S(1)}, bf16[960,128]{1,0:T(8,128)(2,1)}, u32[]{:S(2)}, u32[]{:S(2)}) collective-permute-start(bf16[960,128]{1,0:T(8,128)(2,1)S(1)} %collective-permute-done.11.refs_12_), channel_id=1, source_target_pairs={{0,1},{1,0},{2,3},{3,2},{4,5},{5,4},{6,7},{7,6},{8,9},{9,8},{10,11... | collective-permute-start | bytes 737288 | tf_op jit(solution)/shard_map/ppermute | solution.py:54
  50.4 17.1 %collective-permute-start.14 = (bf16[960,128]{1,0:T(8,128)(2,1)S(1)}, bf16[960,128]{1,0:T(8,128)(2,1)}, u32[]{:S(2)}, u32[]{:S(2)}) collective-permute-start(bf16[960,128]{1,0:T(8,128)(2,1)S(1)} %collective-permute-done.13.refs_14_), channel_id=1, source_target_pairs={{0,1},{1,0},{2,3},{3,2},{4,5},{5,4},{6,7},{7,6},{8,9},{9,8},{10,11... | collective-permute-start | bytes 737288 | tf_op jit(solution)/shard_map/ppermute | solution.py:54
  66.4 12.3 %collective-permute-start.21 = (bf16[528,128]{1,0:T(8,128)(2,1)S(1)}, bf16[528,128]{1,0:T(8,128)(2,1)S(1)}, u32[]{:S(2)}, u32[]{:S(2)}) collective-permute-start(bf16[528,128]{1,0:T(8,128)(2,1)S(1)} %copy-done.18), channel_id=1, source_target_pairs={{0,1},{1,0},{2,3},{3,2},{4,5},{5,4},{6,7},{7,6},{8,9},{9,8},{10,11... | collective-permute-start | bytes 405512 | tf_op jit(solution)/shard_map/ppermute | solution.py:54
  66.8 11.9 %collective-permute-start.23 = (bf16[528,128]{1,0:T(8,128)(2,1)S(1)}, bf16[528,128]{1,0:T(8,128)(2,1)S(1)}, u32[]{:S(2)}, u32[]{:S(2)}) collective-permute-start(bf16[528,128]{1,0:T(8,128)(2,1)S(1)} %copy-done.16), channel_id=1, source_target_pairs={{0,1},{1,0},{2,3},{3,2},{4,5},{5,4},{6,7},{7,6},{8,9},{9,8},{10,11... | collective-permute-start | bytes 405512 | tf_op jit(solution)/shard_map/ppermute | solution.py:54
  67.0 11.7 %collective-permute-start.27 = (bf16[528,128]{1,0:T(8,128)(2,1)S(1)}, bf16[528,128]{1,0:T(8,128)(2,1)S(1)}, u32[]{:S(2)}, u32[]{:S(2)}) collective-permute-start(bf16[528,128]{1,0:T(8,128)(2,1)S(1)} %copy-done.24), channel_id=1, source_target_pairs={{0,1},{1,0},{2,3},{3,2},{4,5},{5,4},{6,7},{7,6},{8,9},{9,8},{10,11... | collective-permute-start | bytes 405512 | tf_op jit(solution)/shard_map/ppermute | solution.py:54
  67.4 11.4 %collective-permute-start.25 = (bf16[528,128]{1,0:T(8,128)(2,1)S(1)}, bf16[528,128]{1,0:T(8,128)(2,1)S(1)}, u32[]{:S(2)}, u32[]{:S(2)}) collective-permute-start(bf16[528,128]{1,0:T(8,128)(2,1)S(1)} %copy-done.26), channel_id=1, source_target_pairs={{0,1},{1,0},{2,3},{3,2},{4,5},{5,4},{6,7},{7,6},{8,9},{9,8},{10,11... | collective-permute-start | bytes 405512 | tf_op jit(solution)/shard_map/ppermute | solution.py:54
  67.5 11.2 %collective-permute-start.29 = (bf16[528,128]{1,0:T(8,128)(2,1)S(1)}, bf16[528,128]{1,0:T(8,128)(2,1)S(1)}, u32[]{:S(2)}, u32[]{:S(2)}) collective-permute-start(bf16[528,128]{1,0:T(8,128)(2,1)S(1)} %copy-done.28), channel_id=1, source_target_pairs={{0,1},{1,0},{2,3},{3,2},{4,5},{5,4},{6,7},{7,6},{8,9},{9,8},{10,11... | collective-permute-start | bytes 405512 | tf_op jit(solution)/shard_map/ppermute | solution.py:54
  67.9 10.8 %copy-start.12 = (bf16[528,128]{1,0:T(8,128)(2,1)S(1)}, bf16[528,128]{1,0:T(8,128)(2,1)}, u32[]{:S(2)}) copy-start(bf16[528,128]{1,0:T(8,128)(2,1)} %copy-done.11) | copy-start | bytes 405508
  (40 other events, 141.2 us)

commit v3 on v1

--- a/solution.py
+++ b/solution.py
@@ -1,13 +1,19 @@
+import functools
+
 import jax
 import jax.numpy as jnp
 from jax import lax
+from jax.experimental import pallas as pl
+from jax.experimental.pallas import tpu as pltpu
 from jax.sharding import PartitionSpec as P
 
 TASKS = 3
 ALPHA = 4.0
 F32 = jnp.float32
 BF16 = jnp.bfloat16
-MOST_RING_CHIPS = 8
+RING_CHIPS = 8
+LANES = 128
+MIB = 1 << 20
 
 
 def mm(a, b):
@@ -22,49 +28,417 @@
     return lax.dot_general(a, b, (((0,), (0,)), ((), ())), preferred_element_type=F32)
 
 
-def ring_chip(pos, chips):
-    half = chips // 2
-    return jnp.where(pos < half, 2 * pos, 2 * (chips - 1 - pos) + 1)
-
-
-def gather_blocks(block, n):
-    chips = n // 2
-    if chips > MOST_RING_CHIPS:
-        return lax.all_gather(block, "dp")
-    half = chips // 2
-    place = [2 * q if q < half else 2 * (chips - 1 - q) + 1 for q in range(chips)]
-
-    def hop(value, step):
-        pairs = [
-            (2 * place[q] + c, 2 * place[(q + step) % chips] + c)
-            for q in range(chips)
-            for c in range(2)
+def ring_chip(pos):
+    half = RING_CHIPS // 2
+    return jnp.where(pos < half, 2 * pos, 2 * (RING_CHIPS - 1 - pos) + 1)
+
+
+def ring_pos(chip):
+    row, side = chip // 2, chip % 2
+    return jnp.where(side == 0, row, RING_CHIPS - 1 - row)
+
+
+def hop(value, step):
+    half = RING_CHIPS // 2
+    place = [2 * q if q < half else 2 * (RING_CHIPS - 1 - q) + 1 for q in range(RING_CHIPS)]
+    pairs = [
+        (2 * place[q] + c, 2 * place[(q + step) % RING_CHIPS] + c)
+        for q in range(RING_CHIPS)
+        for c in range(2)
+    ]
+    return lax.ppermute(value, "dp", pairs)
+
+
+def other_core(value):
+    return lax.ppermute(value, "dp", [(d, d ^ 1) for d in range(2 * RING_CHIPS)])
+
+
+def half_lanes(shape):
+    return lax.broadcasted_iota(jnp.int32, shape, 1) < LANES // 2
+
+
+def diagonal_column(row, first, count):
+    shape = (count, row.shape[1])
+    lane = lax.broadcasted_iota(jnp.int32, shape, 1)
+    at = lax.broadcasted_iota(jnp.int32, shape, 0)
+    return jnp.sum(jnp.where(lane == at + first, row, 0.0), axis=1, keepdims=True)
+
+
+def load(pairs, sems):
+    copies = [pltpu.make_async_copy(src, dst, sems.at[i]) for i, (src, dst) in enumerate(pairs)]
+    for copy in copies:
+        copy.start()
+    return copies
+
+
+def factor_kernel(me_ref, *refs):
+    hbm, out_ref, held, sems = refs[:7], refs[7], refs[8:15], refs[15]
+    gain_ref, down_up_ref, up_low_ref, sketch_ref, up_up_ref, down_low_ref, expand_ref = held
+    copies = load(zip(hbm, held), sems)
+    rows = down_up_ref.shape[0]
+    half = LANES // 2
+    copies[0].wait()
+    copies[1].wait()
+    for b in range(rows // half):
+        place = me_ref[0] * (rows // half) + b
+        row = gain_ref[pl.ds(place // 2, 1), :]
+        column = diagonal_column(row, (place % 2) * half, half)
+        part = down_up_ref[pl.ds(b * half, half), :].astype(F32)
+        out_ref[pl.ds(b * half, half), :] = (column * part).astype(BF16)
+    for copy in copies[2:]:
+        copy.wait()
+    at = rows
+    out_ref[pl.ds(at, rows), :] = mm(up_low_ref[...], sketch_ref[...]).astype(BF16)
+    at += rows
+    out_ref[pl.ds(at, rows // 2), :] = up_up_ref[...]
+    at += rows // 2
+    expand = expand_ref[...]
+    low = mm_rows(down_low_ref[...], jnp.concatenate([expand, expand], axis=0))
+    first, second = low[: rows // 2], low[rows // 2 :]
+    out_ref[pl.ds(at, rows // 2), :] = jnp.where(half_lanes(first.shape), first, second).astype(BF16)
+
+
+def panel_kernel(val_hbm, label_hbm, out_ref, val_ref, label_ref, sems):
+    for copy in load(((val_hbm, val_ref), (label_hbm, label_ref)), sems):
+        copy.wait()
+    wide = val_ref[...].astype(F32)
+    count, width = wide.shape
+    scale = lax.rsqrt(jnp.sum(wide * wide, axis=1, keepdims=True) + 1e-06)
+    unit = wide * scale
+    blocks = [unit[:, i * LANES : (i + 1) * LANES] for i in range(width // LANES)]
+    row = label_ref[...].astype(F32)
+    labels = jnp.broadcast_to(diagonal_column(row, 0, count), (count, LANES))
+    blocks += [labels, labels]
+    for i in range(0, len(blocks), 2):
+        pair = jnp.concatenate(blocks[i : i + 2], axis=0)
+        out_ref[pl.ds(i * count, 2 * count), :] = pair.astype(BF16)
+
+
+X_LOW, X_DOWN, X_SOURCE, SQUARES, J_LOW, M_DOWN, M_SOURCE, VALUES, SUMS = 0, 2, 3, 4, 5, 7, 8, 9, 11
+
+
+def stage_kernel(aways, first, last, me_ref, *refs):
+    refs = list(refs)
+    take = lambda k: [refs.pop(0) for _ in range(k)]
+    counts_ref = take(1)[0] if last else None
+    pieces = take(2 * len(aways))
+    x_hbm, mixed_hbm, adjoint_hbm, values_hbm, gain_hbm, source_hbm, target_hbm, top_target_hbm = take(8)
+    old_sums, old_bridge = (None, None) if first else take(2)
+    expand_hbm, sketch_hbm = take(2) if last else (None, None)
+    if last:
+        (out_ref,) = take(1)
+    else:
+        new_sums, new_bridge = take(2)
+    xs, ms, js, vs, gains, sources, low, down, up, packed, expand_ref, sketch_ref, sems = refs
+    rows = down.shape[1] // 2
+    half = rows // 2
+    tokens, span = xs.shape[1:]
+    pad = LANES // 2
+    me = me_ref[0]
+    pos, core = ring_pos(me // 2), me % 2
+
+    copies = []
+    for k, away in enumerate(aways):
+        chip = ring_chip((pos + (away + RING_CHIPS)) % RING_CHIPS)
+        odd = chip % 2
+        mine = pl.ds(pl.multiple_of(chip * span, LANES), span)
+        values_start = (chip // 2) * span + odd * (span // 2 - pad)
+        values_window = pl.ds(pl.multiple_of(values_start, LANES), vs.shape[2])
+        shift = odd * pad
+        up[k, pl.ds(pl.multiple_of((1 - odd) * rows, 16), pad), :] = jnp.zeros((pad, 2 * LANES), BF16)
+        pairs = []
+        for piece, c in ((pieces[2 * k], core), (pieces[2 * k + 1], 1 - core)):
+            one = pl.ds(pl.multiple_of(c * rows, 16), rows)
+            part = pl.ds(pl.multiple_of(c * half, 16), half)
+            up_part = pl.ds(pl.multiple_of(shift + c * half, 16), half)
+            pairs += [
+                (piece.at[pl.ds(0, rows)], down.at[k, one]),
+                (piece.at[pl.ds(rows, rows)], low.at[k, one, pl.ds(0, LANES)]),
+                (piece.at[pl.ds(2 * rows, half)], up.at[k, up_part, pl.ds(0, LANES)]),
+                (piece.at[pl.ds(2 * rows + half, half)], packed.at[k, part]),
+            ]
+        pairs += [
+            (target_hbm.at[mine], low.at[k, :, pl.ds(LANES, LANES)]),
+            (
+                top_target_hbm.at[pl.ds(pl.multiple_of(chip * rows, 16), rows)],
+                up.at[k, pl.ds(pl.multiple_of(shift, 16), rows), pl.ds(LANES, LANES)],
+            ),
+            (source_hbm.at[:, mine], sources.at[k]),
+            (gain_hbm.at[:, mine], gains.at[k]),
+            (x_hbm.at[:, mine], xs.at[k]),
+            (adjoint_hbm.at[:, mine], js.at[k]),
+            (mixed_hbm.at[:, mine], ms.at[k]),
+            (values_hbm.at[:, values_window], vs.at[k]),
         ]
-        return lax.ppermute(value, "dp", pairs)
-
-    def other_core(value):
-        return lax.ppermute(value, "dp", [(d, d ^ 1) for d in range(n)])
-
-    me = lax.axis_index("dp")
-    chip, core = me // 2, me % 2
-    row, side = chip // 2, chip % 2
-    pos = jnp.where(side == 0, row, chips - 1 - row)
-    pieces = [(0, block, 0)]
-    up, down = block, block
-    middle = (block.shape[0] // 2) // 16 * 16
-    for k in range(1, half):
-        up, down = hop(up, 1), hop(down, -1)
-        pieces += [(-k, up, 0), (k, down, 0)]
-    pieces += [(-half, hop(up[:middle], 1), 0), (half, hop(down[middle:], -1), middle)]
-    out = jnp.zeros((n,) + block.shape, block.dtype)
-    for away, piece, first in pieces:
-        base = 2 * ring_chip((pos + away + chips) % chips, chips)
-        out = lax.dynamic_update_slice(out, piece[None], (base + core, first, 0))
-        out = lax.dynamic_update_slice(out, other_core(piece)[None], (base + 1 - core, first, 0))
-    return out
+        copies.append(load(pairs, sems.at[k]))
+    if last:
+        more = load(((expand_hbm, expand_ref), (sketch_hbm, sketch_ref)), sems.at[len(aways)])
+
+    total = [None if first else old_sums[:, i * LANES : (i + 1) * LANES] for i in range(SUMS)]
+    bridged = None if first else old_bridge[...]
+
+    def add(column, value):
+        for i in range(value.shape[1] // LANES):
+            part = value[:, i * LANES : (i + 1) * LANES]
+            total[column + i] = part if total[column + i] is None else total[column + i] + part
+
+    for k in range(len(aways)):
+        for copy in copies[k]:
+            copy.wait()
+        x, mixed = xs[k], ms[k]
+        add(X_LOW, mm(x, low[k]))
+        add(X_DOWN, mm(x, down[k]))
+        source = sources[k]
+        gained = (source.astype(F32) * gains[k]).astype(BF16)
+        add(X_SOURCE, mm_rows(x, jnp.concatenate([gained, gained], axis=0)))
+        square = jnp.zeros((tokens, LANES), F32)
+        for i in range(span // LANES):
+            wide = x[:, i * LANES : (i + 1) * LANES].astype(F32)
+            square = square + wide * wide
+        add(SQUARES, square)
+        add(J_LOW, mm(js[k], low[k]))
+        unpacked = []
+        for c in range(2):
+            both = packed[k, pl.ds(c * half, half), :].astype(F32)
+            turned = pltpu.roll(both, LANES // 2, 1)
+            lower = half_lanes(both.shape)
+            unpacked += [jnp.where(lower, both, turned), jnp.where(lower, turned, both)]
+        add(M_DOWN, mm(mixed, jnp.concatenate(unpacked, axis=0).astype(BF16)))
+        add(M_SOURCE, mm_rows(mixed, jnp.concatenate([source, source], axis=0)))
+        add(VALUES, mm(vs[k], up[k]))
+        product = mm_cols(down[k], low[k])
+        bridged = product if bridged is None else bridged + product
+
+    if not last:
+        for i in range(SUMS):
+            new_sums[:, i * LANES : (i + 1) * LANES] = total[i]
+        new_bridge[...] = bridged
+        return
+
+    for copy in more:
+        copy.wait()
+    width = x_hbm.shape[1]
+    mean = jnp.sum(total[SQUARES], axis=1, keepdims=True) * (1.0 / width)
+    inverse = lax.rsqrt(mean + 1e-05)
+    reduced = inverse * total[X_DOWN]
+    expand = expand_ref[...]
+    left_two = mm_rows(reduced.astype(BF16), jnp.concatenate([expand, expand], axis=0))
+    returned = total[VALUES].astype(BF16)
+    right_one = ALPHA * mm(returned, sketch_ref[...])
+    along = (ALPHA / width) * jnp.sum(returned.astype(F32) * reduced, axis=1, keepdims=True)
+    back = mm(returned, bridged.astype(BF16))
+    along = along * inverse
+    lows = [
+        total[J_LOW + i]
+        + inverse * (ALPHA * back[:, i * LANES : (i + 1) * LANES] - along * total[X_LOW + i])
+        for i in range(2)
+    ]
+    rights = (right_one, ALPHA * total[VALUES + 1], ALPHA * lows[0], ALPHA * lows[1])
+    lefts = (inverse * total[X_SOURCE], left_two, total[M_SOURCE], total[M_DOWN])
+    place = lax.broadcasted_iota(jnp.int32, (tokens, LANES), 0)
+    one, two = counts_ref[0, 0], counts_ref[0, 1]
+    lower = half_lanes((tokens, LANES))
+    member = (place >= jnp.where(lower, 0, one)) & (place < jnp.where(lower, one, one + two))
+    spread = jnp.concatenate([jnp.where(member, left, 0.0).astype(BF16) for left in lefts], axis=0)
+    feats = mm_cols(spread, jnp.concatenate([right.astype(BF16) for right in rights], axis=0))
+    for e in range(2):
+        own = feats[e * pad : (e + 1) * pad]
+        squares = jnp.sum(own * own, keepdims=True)
+        out_ref[pl.ds(e * pad, pad), :] = (own * lax.rsqrt(squares + 1e-06)).astype(BF16)
+
+
+def score_kernel(pieces, count, unit_ref, *refs):
+    piece_refs = refs[:pieces]
+    best_ref, mean_ref, spread = refs[pieces:]
+    half = LANES // 2
+    scale = float(half * LANES) ** 0.5
+    for e in range(2):
+        for i in range(half):
+            row = unit_ref[pl.ds(e * half + i, 1), :].astype(F32)
+            spread[e, pl.ds(i * count, count), :] = jnp.broadcast_to(row, (count, LANES))
+    best = [[jnp.full((count, LANES), -2.0 * scale, F32) for _ in range(TASKS)] for _ in range(2)]
+    for piece in piece_refs:
+        wide = piece[pl.ds(0, half * count), :].astype(F32)
+        labels = piece[pl.ds(half * count, 2 * count), :].astype(F32)[:count]
+        for e in range(2):
+            products = wide * spread[e]
+            total = jnp.sum(products.reshape(half, count, LANES), axis=0)
+            similar = scale * jnp.sum(total, axis=1, keepdims=True)
+            for t in range(TASKS):
+                here = jnp.where(labels == float(t), similar, -2.0 * scale)
+                best[e][t] = jnp.maximum(best[e][t], here)
+    for e in range(2):
+        values = [jnp.max(best[e][t]) for t in range(TASKS)]
+        for t in range(TASKS):
+            best_ref[e, t] = values[t]
+        mean_ref[e] = (values[0] + values[1] + values[2]) * (1.0 / TASKS)
+
+
+VMEM = pl.BlockSpec(memory_space=pltpu.VMEM)
+SMEM = pl.BlockSpec(memory_space=pltpu.SMEM)
+ANY = pl.BlockSpec(memory_space=pl.ANY)
+HBM = pl.BlockSpec(memory_space=pltpu.HBM)
+
+
+def params(mib):
+    return pltpu.CompilerParams(vmem_limit_bytes=mib * MIB)
+
+
+def cost(flops, nbytes):
+    return pl.CostEstimate(flops=flops, bytes_accessed=nbytes, transcendentals=0)
 
 
 def shards(
+    hidden_state_input,
+    attention_mixed_state,
+    hidden_state_adjoint,
+    attention_values_adjoint,
+    sequence_token_counts,
+    heldout_sketched_signals,
+    benchmark_labels,
+    top_rmsnorm_weights,
+    top_reducer_matrix,
+    top_expander_matrix,
+    bottom_reducer_matrix,
+    bottom_expander_matrix,
+    source_sketch,
+    top_reducer_sketch,
+    top_expander_sketch,
+    top_target_sketch,
+    bottom_reducer_sketch,
+    bottom_expander_sketch,
+    bottom_target_sketch,
+):
+    me = lax.axis_index("dp").astype(jnp.int32)
+    x, mixed, adjoint, values = (
+        hidden_state_input,
+        attention_mixed_state,
+        hidden_state_adjoint,
+        attention_values_adjoint,
+    )
+    tokens, width = x.shape
+    rows = top_reducer_matrix.shape[0]
+    count = heldout_sketched_signals.shape[0]
+
+    inputs = (
+        top_rmsnorm_weights.reshape(width // LANES, LANES),
+        top_reducer_matrix,
+        bottom_expander_matrix.T,
+        bottom_reducer_sketch,
+        top_expander_matrix.T,
+        bottom_reducer_matrix,
+        bottom_expander_sketch.T,
+    )
+    factors = pl.pallas_call(
+        factor_kernel,
+        out_shape=jax.ShapeDtypeStruct((3 * rows, LANES), BF16),
+        in_specs=[SMEM] + [HBM] * len(inputs),
+        out_specs=VMEM,
+        scratch_shapes=[pltpu.VMEM(a.shape, a.dtype) for a in inputs]
+        + [pltpu.SemaphoreType.DMA((len(inputs),))],
+        compiler_params=params(8),
+        name="factors",
+    )(me.reshape(1), *inputs)
+    inputs = (heldout_sketched_signals, benchmark_labels.T)
+    panel = pl.pallas_call(
+        panel_kernel,
+        out_shape=jax.ShapeDtypeStruct(((LANES // 2 + 2) * count, LANES), BF16),
+        in_specs=[HBM] * len(inputs),
+        out_specs=VMEM,
+        scratch_shapes=[pltpu.VMEM(a.shape, a.dtype) for a in inputs]
+        + [pltpu.SemaphoreType.DMA((len(inputs),))],
+        compiler_params=params(8),
+        name="panel",
+    )(*inputs)
+
+    span = 2 * rows
+    activations = (
+        x,
+        mixed,
+        adjoint,
+        values,
+        top_rmsnorm_weights.reshape(1, width),
+        source_sketch.T,
+        bottom_target_sketch,
+        top_target_sketch,
+    )
+
+    def stage(aways, pieces, sums=(), last=False):
+        first, n = not sums, len(aways)
+        sums_shape, bridge_shape = (tokens, SUMS * LANES), (LANES, 2 * LANES)
+        small = (top_expander_sketch.T, top_reducer_sketch)
+        head = [me.reshape(1)] + ([sequence_token_counts] if last else [])
+        start = len(head) + len(pieces) + len(activations)
+        return pl.pallas_call(
+            functools.partial(stage_kernel, aways, first, last),
+            out_shape=jax.ShapeDtypeStruct((LANES, LANES), BF16)
+            if last
+            else (jax.ShapeDtypeStruct(sums_shape, F32), jax.ShapeDtypeStruct(bridge_shape, F32)),
+            in_specs=[SMEM] * len(head)
+            + [ANY] * len(pieces)
+            + [HBM] * len(activations)
+            + [VMEM] * len(sums)
+            + ([HBM] * 2 if last else []),
+            out_specs=VMEM if last else (VMEM, VMEM),
+            scratch_shapes=[
+                pltpu.VMEM((n, tokens, span), BF16),
+                pltpu.VMEM((n, tokens, span), BF16),
+                pltpu.VMEM((n, tokens, span), BF16),
+                pltpu.VMEM((n, tokens, rows + LANES // 2), BF16),
+                pltpu.VMEM((n, 1, span), F32),
+                pltpu.VMEM((n, LANES // 2, span), BF16),
+                pltpu.VMEM((n, span, 2 * LANES), BF16),
+                pltpu.VMEM((n, span, LANES), BF16),
+                pltpu.VMEM((n, rows + LANES // 2, 2 * LANES), BF16),
+                pltpu.VMEM((n, rows, LANES), BF16),
+                pltpu.VMEM(small[0].shape, BF16),
+                pltpu.VMEM(small[1].shape, BF16),
+                pltpu.SemaphoreType.DMA((n + 1, 16)),
+            ],
+            input_output_aliases={} if first or last else {start: 0, start + 1: 1},
+            compiler_params=params(16),
+            cost_estimate=cost(n * tokens * span * LANES * 24, 3 * n * MIB),
+            name="features" if last else "stage",
+        )(*head, *pieces, *activations, *sums, *(small if last else ()))
+
+    tie = lax.optimization_barrier
+    half = RING_CHIPS // 2
+    up = down = factors
+    panel_up = panel_down = panel
+    sums = ()
+    held = [factors, other_core(factors)]
+    aways = (0,)
+    panels = [panel, other_core(panel)]
+    for k in range(1, half + 1):
+        up = hop(up, 1)
+        down = hop(down, -1) if k < half else down
+        panel_up = hop(panel_up, 1) if k < half else panel_up
+        panel_down = hop(panel_down, -1)
+        sums = stage(aways, held, sums)
+        up, down = tie((up, down))
+        panel_up, panel_down, _, _ = tie((panel_up, panel_down, up, down))
+        aways = (-k, k) if k < half else (-half,)
+        held = [up, other_core(up)]
+        if k < half:
+            held += [down, other_core(down)]
+            panels += [panel_up, other_core(panel_up)]
+        panels += [panel_down, other_core(panel_down)]
+    unit = stage(aways, held, sums, last=True)
+
+    task_best, scores = pl.pallas_call(
+        functools.partial(score_kernel, len(panels), count),
+        out_shape=(jax.ShapeDtypeStruct((2, TASKS), F32), jax.ShapeDtypeStruct((2,), F32)),
+        in_specs=[VMEM] * (1 + len(panels)),
+        out_specs=(SMEM, SMEM),
+        scratch_shapes=[pltpu.VMEM((2, LANES // 2 * count, LANES), F32)],
+        compiler_params=params(16),
+        cost_estimate=cost(4 * MIB, 2 * MIB),
+        name="scores",
+    )(unit, *panels)
+    return (scores, task_best)
+
+
+def shards_of_any_slice(
     hidden_state_input,
     attention_mixed_state,
     hidden_state_adjoint,
@@ -106,7 +480,7 @@
     down_lower = mm(bottom_reducer_matrix, bottom_expander_sketch).astype(BF16)
     packed_lower = jnp.concatenate([down_lower[: rows // 2], down_lower[rows // 2 :]], axis=1)
     factors = jnp.concatenate([down_upper, up_lower, top_expander_matrix.T, packed_lower], axis=0)
-    factors = gather_blocks(factors, n)
+    factors = lax.all_gather(factors, "dp")
 
     val_wide = heldout_sketched_signals.astype(F32)
     val_unit = (
@@ -114,7 +488,7 @@
     ).astype(BF16)
     labels = jnp.broadcast_to(benchmark_labels.astype(BF16), (val_unit.shape[0], 128))
     panel = jnp.concatenate([val_unit.reshape(-1, 128), labels], axis=0)
-    panel = gather_blocks(panel, n)
+    panel = lax.all_gather(panel, "dp")
     val_rows = val_unit.shape[0]
     cut = panel.shape[1] - val_rows
     panel_tasks = panel[:, cut:, 0].reshape(n * val_rows, 1).astype(jnp.int32)
@@ -189,8 +563,9 @@
         + (by_row, by_column, by_row, by_column)
         + (whole,) * 7
     )
+    ours = shards if n == 2 * RING_CHIPS else functools.partial(shards_of_any_slice, n=n)
     return jax.shard_map(
-        lambda *arrays: shards(*arrays, n),
+        ours,
         mesh=mesh,
         in_specs=placed,
         out_specs=(P(("parts", "dp")), split),

time: 112 us -> 80 us (0.71)
  local copies, waits for them, and re-layouts: 49.7 us -> 19.6 us
  matrix products: 18.9 us -> 0 us
  Pallas kernels: 0 us -> 17.8 us
  waiting for transfers between devices: 9.6 us -> 21.7 us
  other arithmetic: 10.6 us -> 0 us
  starting transfers between devices: 20.7 us -> 19 us
    dynamic_update_slice x34 -> x0, local copies, waits for them, and re-layouts: 29.6 us -> none  [the longest x18 15.9 us: gather_blocks(): lax.dynamic_update_slice(out, other_core(piece)[None], (base + 1 - core,...]
    dot_general x15 -> x0, matrix products: 18.9 us -> none  [the longest x13 16.4 us: mm(): return jnp.dot(a, b, preferred_element_type=F32)]
    pallas_call x0 -> x8, Pallas kernels: none -> 17.8 us  [the longest x5 15 us: stage(): pl.pallas_call(functools.partial(stage_kernel, aways, first, last), out_s...]
    unnamed x43 -> x50, local copies, waits for them, and re-layouts: 1.82 us -> 19.6 us
    ppermute x16 -> x14, waiting for transfers between devices: 9.55 us -> 21.7 us  [hop(): return lax.ppermute(value, 'dp', pairs)]
    slice x11 -> x0, local copies, waits for them, and re-layouts: 8.49 us -> none  [the longest x1 3.15 us: shards(): panel = panel[:, :cut].reshape(n * val_rows, val_unit.shape[1])]
    broadcast_in_dim x2 -> x0, local copies, waits for them, and re-layouts: 4.27 us -> none  [gather_blocks(): out = jnp.zeros((n,) + block.shape, block.dtype)]
    reshape x2 -> x0, local copies, waits for them, and re-layouts: 4.24 us -> none  [the longest x1 4.18 us: shards(): panel = panel[:, :cut].reshape(n * val_rows, val_unit.shape[1])]
  transfers between devices with their start and end apart: 34 -> 30, of which waited for: 4 -> 10; matrix products, arithmetic and copies ran while one was open for 47% -> 0% of each run, Pallas kernels for 0% -> 19%
where the time goes in v3:
time: 80 us; the launch traced here: 79.2 us
  waiting for transfers between devices  21.7 us (27%)
  local copies, waits for them, and re-layouts  19.6 us (25%)
  starting transfers between devices  19 us (24%)
  Pallas kernels  17.8 us (22%)
  between operations  1.01 us (1%)
    ppermute x14, waiting for transfers between devices, hop(): return lax.ppermute(value, 'dp', pairs)  21.7 us
    unnamed x50, local copies, waits for them, and re-layouts  19.6 us
    ppermute x14, starting transfers between devices, hop(): return lax.ppermute(value, 'dp', pairs)  15.7 us
    pallas_call x5, Pallas kernels, stage(): pl.pallas_call(functools.partial(stage_kernel, aways, first, last), out_s...  15 us
    ppermute x16, starting transfers between devices, other_core(): lax.ppermute(value, 'dp', [(d, d ^ 1) for d in range(2 * RING_CHIPS)])  3.35 us
    pallas_call x1, Pallas kernels, shards(): pl.pallas_call(functools.partial(score_kernel, len(panels), count), out_s...  1.7 us
  transfers between devices with their start and end apart: 30, of which 10 were waited for; matrix products, arithmetic and copies ran while one was open for 0% of the time, Pallas kernels for 19%

profile of v3, /device:TPU:0, one launch (start us, length us, event | category | flops | bytes accessed | tf_op | source)
XLA Modules:
  0.0 79.2 jit_solution(14041442765190634276)
XLA Ops:
  1.4 0.9 %copy-done.15 = bf16[320,128]{1,0:T(8,128)(2,1)S(1)} copy-done((bf16[320,128]{1,0:T(8,128)(2,1)S(1)}, bf16[320,128]{1,0:T(8,128)(2,1)}, u32[]{:S(2)}) %copy-start.15) | copy-done | bytes 81944
  2.3 0.9 %copy-done.16 = bf16[128,320]{0,1:T(8,128)(2,1)S(1)} copy-done((bf16[128,320]{0,1:T(8,128)(2,1)S(1)}, bf16[128,320]{0,1:T(8,128)(2,1)}, u32[]{:S(2)}) %copy-start.16) | copy-done | bytes 81944
  3.1 0.9 %copy-done.17 = bf16[320,128]{1,0:T(8,128)(2,1)S(1)} copy-done((bf16[320,128]{1,0:T(8,128)(2,1)S(1)}, bf16[320,128]{1,0:T(8,128)(2,1)}, u32[]{:S(2)}) %copy-start.17) | copy-done | bytes 81944
  7.1 3.1 %collective-permute-start = (bf16[960,128]{1,0:T(8,128)(2,1)S(1)}, bf16[960,128]{1,0:T(8,128)(2,1)S(1)}, u32[]{:S(2)}, u32[]{:S(2)}) collective-permute-start(bf16[960,128]{1,0:T(8,128)(2,1)S(1)} %factors.1.refs_0_), channel_id=1, source_target_pairs={{0,4},{1,5},{4,8},{5,9},{8,12},{9,13},{12,14},{13,15},{14,10},{15,... | collective-permute-start | bytes 737288 | tf_op jit(solution)/shard_map/ppermute | solution.py:49
  10.2 5.9 %collective-permute-done.refs_0_ = bf16[960,128]{1,0:T(8,128)(2,1)S(1)} collective-permute-done((bf16[960,128]{1,0:T(8,128)(2,1)S(1)}, bf16[960,128]{1,0:T(8,128)(2,1)S(1)}, u32[]{:S(2)}, u32[]{:S(2)}) %collective-permute-start) | collective-permute-done | bytes 245792 | tf_op jit(solution)/shard_map/ppermute | solution.py:49
  16.1 1.5 %collective-permute-done.1.refs_2_ = bf16[960,128]{1,0:T(8,128)(2,1)S(1)} collective-permute-done((bf16[960,128]{1,0:T(8,128)(2,1)S(1)}, bf16[960,128]{1,0:T(8,128)(2,1)S(1)}, u32[]{:S(2)}, u32[]{:S(2)}) %collective-permute-start.1) | collective-permute-done | bytes 245792 | tf_op jit(solution)/shard_map/ppermute | solution.py:49
  17.6 1.6 %collective-permute-start.2 = (bf16[960,128]{1,0:T(8,128)(2,1)S(1)}, bf16[960,128]{1,0:T(8,128)(2,1)S(1)}, u32[]{:S(2)}, u32[]{:S(2)}) collective-permute-start(bf16[960,128]{1,0:T(8,128)(2,1)S(1)} %collective-permute-done.refs_0_), channel_id=1, source_target_pairs={{0,4},{1,5},{4,8},{5,9},{8,12},{9,13},{12,14},{13,15},{14,10},{15,... | collective-permute-start | bytes 737288 | tf_op jit(solution)/shard_map/ppermute | solution.py:49
  19.6 0.9 %copy-done.14 = bf16[8,8192]{1,0:T(8,128)(2,1)S(1)} copy-done((bf16[8,8192]{1,0:T(8,128)(2,1)S(1)}, bf16[8,8192]{1,0:T(8,128)(2,1)}, u32[]{:S(2)}) %copy-start.14) | copy-done | bytes 131096
  21.5 1.6 %collective-permute-start.16 = (bf16[528,128]{1,0:T(8,128)(2,1)S(1)}, bf16[528,128]{1,0:T(8,128)(2,1)S(1)}, u32[]{:S(2)}, u32[]{:S(2)}) collective-permute-start(bf16[528,128]{1,0:T(8,128)(2,1)S(1)} %panel.1.refs_0_), channel_id=1, source_target_pairs={{0,4},{1,5},{4,8},{5,9},{8,12},{9,13},{12,14},{13,15},{14,10},{15,... | collective-permute-start | bytes 405512 | tf_op jit(solution)/shard_map/ppermute | solution.py:49
  23.6 2.0 %collective-permute-done.2.refs_0_ = bf16[960,128]{1,0:T(8,128)(2,1)S(1)} collective-permute-done((bf16[960,128]{1,0:T(8,128)(2,1)S(1)}, bf16[960,128]{1,0:T(8,128)(2,1)S(1)}, u32[]{:S(2)}, u32[]{:S(2)}) %collective-permute-start.2) | collective-permute-done | bytes 245792 | tf_op jit(solution)/shard_map/ppermute | solution.py:49
  25.6 1.3 %collective-permute-done.3.refs_2_ = bf16[960,128]{1,0:T(8,128)(2,1)S(1)} collective-permute-done((bf16[960,128]{1,0:T(8,128)(2,1)S(1)}, bf16[960,128]{1,0:T(8,128)(2,1)S(1)}, u32[]{:S(2)}, u32[]{:S(2)}) %collective-permute-start.3) | collective-permute-done | bytes 245792 | tf_op jit(solution)/shard_map/ppermute | solution.py:49
  26.9 1.6 %collective-permute-start.4 = (bf16[960,128]{1,0:T(8,128)(2,1)S(1)}, bf16[960,128]{1,0:T(8,128)(2,1)S(1)}, u32[]{:S(2)}, u32[]{:S(2)}) collective-permute-start(bf16[960,128]{1,0:T(8,128)(2,1)S(1)} %collective-permute-done.2.refs_0_), channel_id=1, source_target_pairs={{0,4},{1,5},{4,8},{5,9},{8,12},{9,13},{12,14},{13,15},{14,10},{15,... | collective-permute-start | bytes 737288 | tf_op jit(solution)/shard_map/ppermute | solution.py:49
  29.8 1.6 %collective-permute-start.20 = (bf16[528,128]{1,0:T(8,128)(2,1)S(1)}, bf16[528,128]{1,0:T(8,128)(2,1)S(1)}, u32[]{:S(2)}, u32[]{:S(2)}) collective-permute-start(bf16[528,128]{1,0:T(8,128)(2,1)S(1)} %collective-permute-done.16.refs_2_), channel_id=1, source_target_pairs={{0,4},{1,5},{4,8},{5,9},{8,12},{9,13},{12,14},{13,15},{14,10},{15,... | collective-permute-start | bytes 405512 | tf_op jit(solution)/shard_map/ppermute | solution.py:49
  31.8 3.4 %collective-permute-done.20.refs_6_ = bf16[528,128]{1,0:T(8,128)(2,1)S(1)} collective-permute-done((bf16[528,128]{1,0:T(8,128)(2,1)S(1)}, bf16[528,128]{1,0:T(8,128)(2,1)S(1)}, u32[]{:S(2)}, u32[]{:S(2)}) %collective-permute-start.20) | collective-permute-done | bytes 135200 | tf_op jit(solution)/shard_map/ppermute | solution.py:49
  35.2 1.3 %collective-permute-done.21.refs_8_ = bf16[528,128]{1,0:T(8,128)(2,1)S(1)} collective-permute-done((bf16[528,128]{1,0:T(8,128)(2,1)S(1)}, bf16[528,128]{1,0:T(8,128)(2,1)S(1)}, u32[]{:S(2)}, u32[]{:S(2)}) %collective-permute-start.21) | collective-permute-done | bytes 135200 | tf_op jit(solution)/shard_map/ppermute | solution.py:49
  36.5 1.8 %collective-permute-start.24 = (bf16[528,128]{1,0:T(8,128)(2,1)S(1)}, bf16[528,128]{1,0:T(8,128)(2,1)S(1)}, u32[]{:S(2)}, u32[]{:S(2)}) collective-permute-start(bf16[528,128]{1,0:T(8,128)(2,1)S(1)} %collective-permute-done.20.refs_6_), channel_id=1, source_target_pairs={{0,4},{1,5},{4,8},{5,9},{8,12},{9,13},{12,14},{13,15},{14,10},{15,... | collective-permute-start | bytes 405512 | tf_op jit(solution)/shard_map/ppermute | solution.py:49
  38.5 1.8 %collective-permute-start.6 = (bf16[960,128]{1,0:T(8,128)(2,1)S(1)}, bf16[960,128]{1,0:T(8,128)(2,1)S(1)}, u32[]{:S(2)}, u32[]{:S(2)}) collective-permute-start(bf16[960,128]{1,0:T(8,128)(2,1)S(1)} %collective-permute-done.4.refs_0_), channel_id=1, source_target_pairs={{0,4},{1,5},{4,8},{5,9},{8,12},{9,13},{12,14},{13,15},{14,10},{15,... | collective-permute-start | bytes 737288 | tf_op jit(solution)/shard_map/ppermute | solution.py:49
  40.8 2.1 %collective-permute-done.24.refs_10_ = bf16[528,128]{1,0:T(8,128)(2,1)S(1)} collective-permute-done((bf16[528,128]{1,0:T(8,128)(2,1)S(1)}, bf16[528,128]{1,0:T(8,128)(2,1)S(1)}, u32[]{:S(2)}, u32[]{:S(2)}) %collective-permute-start.24) | collective-permute-done | bytes 135200 | tf_op jit(solution)/shard_map/ppermute | solution.py:49
  43.4 3.0 %collective-permute-done.6.refs_1_ = bf16[960,128]{1,0:T(8,128)(2,1)S(1)} collective-permute-done((bf16[960,128]{1,0:T(8,128)(2,1)S(1)}, bf16[960,128]{1,0:T(8,128)(2,1)S(1)}, u32[]{:S(2)}, u32[]{:S(2)}) %collective-permute-start.6) | collective-permute-done | bytes 245792 | tf_op jit(solution)/shard_map/ppermute | solution.py:49
  47.7 1.7 %copy-done = bf16[256,5120]{1,0:T(8,128)(2,1)S(1)} copy-done((bf16[256,5120]{1,0:T(8,128)(2,1)S(1)}, bf16[256,5120]{1,0:T(8,128)(2,1)}, u32[]{:S(2)}) %copy-start) | copy-done | bytes 2621464
  49.4 1.7 %copy-done.2 = bf16[256,5120]{1,0:T(8,128)(2,1)S(1)} copy-done((bf16[256,5120]{1,0:T(8,128)(2,1)S(1)}, bf16[256,5120]{1,0:T(8,128)(2,1)}, u32[]{:S(2)}) %copy-start.2) | copy-done | bytes 2621464
  51.1 1.7 %copy-done.4 = bf16[256,5120]{1,0:T(8,128)(2,1)S(1)} copy-done((bf16[256,5120]{1,0:T(8,128)(2,1)S(1)}, bf16[256,5120]{1,0:T(8,128)(2,1)}, u32[]{:S(2)}) %copy-start.4) | copy-done | bytes 2621464
  52.9 1.3 %copy-done.6 = bf16[256,2560]{1,0:T(8,128)(2,1)S(1)} copy-done((bf16[256,2560]{1,0:T(8,128)(2,1)S(1)}, bf16[256,2560]{1,0:T(8,128)(2,1)}, u32[]{:S(2)}) %copy-start.6) | copy-done | bytes 1310744
  54.2 1.3 %copy-done.8 = bf16[5120,128]{1,0:T(8,128)(2,1)S(1)} copy-done((bf16[5120,128]{1,0:T(8,128)(2,1)S(1)}, bf16[5120,128]{1,0:T(8,128)(2,1)}, u32[]{:S(2)}) %copy-start.8) | copy-done | bytes 1310744
  55.5 1.1 %copy-done.10 = bf16[5120,64]{0,1:T(8,128)(2,1)S(1)} copy-done((bf16[5120,64]{0,1:T(8,128)(2,1)S(1)}, bf16[5120,64]{0,1:T(8,128)(2,1)}, u32[]{:S(2)}) %copy-start.10) | copy-done | bytes 655384
  56.6 1.1 %copy-done.11 = bf16[2560,128]{1,0:T(8,128)(2,1)S(1)} copy-done((bf16[2560,128]{1,0:T(8,128)(2,1)S(1)}, bf16[2560,128]{1,0:T(8,128)(2,1)}, u32[]{:S(2)}) %copy-start.11) | copy-done | bytes 655384
  58.4 1.7 %stage.4 = (f32[256,1408]{1,0:T(8,128)S(1)}, f32[128,256]{1,0:T(8,128)S(1)}) custom-call(s32[1]{0:T(128)} %bitcast.me_ref, bf16[960,128]{1,0:T(8,128)(2,1)S(1)} %factors.1.refs_0_, bf16[960,128]{1,0:T(8,128)(2,1)S(1)} %collective-permute-done.14.refs_1_, bf16[256,5120]{1,0:T(8,128)(2,1)S(1)} %copy-done, bf16[256,5120]{1,0:T(8,128)(2,1)S(1)} %copy-done.2, ...), custom_call_target="tpu_custom_call" | custom-call | flops 503316480 | bytes 3145728 | tf_op jit(solution)/shard_map/stage/pallas_call | solution.py:372
  62.4 3.3 %stage.5 = (f32[256,1408]{1,0:T(8,128)S(1)}, f32[128,256]{1,0:T(8,128)S(1)}) custom-call(s32[1]{0:T(128)} %bitcast.me_ref, bf16[960,128]{1,0:T(8,128)(2,1)S(1)} %collective-permute-done.refs_0_, bf16[960,128]{1,0:T(8,128)(2,1)S(1)} %collective-permute-done.12.refs_1_, ...), custom_call_target="tpu_custom_call", output_to_operand_aliasing={{0}: (13, {}), {1}: (14, {})} | custom-call | flops 1006632960 | bytes 6291456 | tf_op jit(solution)/shard_map/stage/pallas_call | solution.py:372
  65.8 3.4 %stage.6 = (f32[256,1408]{1,0:T(8,128)S(1)}, f32[128,256]{1,0:T(8,128)S(1)}) custom-call(s32[1]{0:T(128)} %bitcast.me_ref, bf16[960,128]{1,0:T(8,128)(2,1)S(1)} %collective-permute-done.2.refs_0_, bf16[960,128]{1,0:T(8,128)(2,1)S(1)} %collective-permute-done.10.refs_1_, ...), custom_call_target="tpu_custom_call", output_to_operand_aliasing={{0}: (13, {}), {1}: (14, {})} | custom-call | flops 1006632960 | bytes 6291456 | tf_op jit(solution)/shard_map/stage/pallas_call | solution.py:372
  70.8 3.4 %stage.7 = (f32[256,1408]{1,0:T(8,128)S(1)}, f32[128,256]{1,0:T(8,128)S(1)}) custom-call(s32[1]{0:T(128)} %bitcast.me_ref, bf16[960,128]{1,0:T(8,128)(2,1)S(1)} %collective-permute-done.4.refs_0_, bf16[960,128]{1,0:T(8,128)(2,1)S(1)} %collective-permute-done.8.refs_1_, ...), custom_call_target="tpu_custom_call", output_to_operand_aliasing={{0}: (13, {}), {1}: (14, {})} | custom-call | flops 1006632960 | bytes 6291456 | tf_op jit(solution)/shard_map/stage/pallas_call | solution.py:372
  74.2 3.1 %features.1.unit_ref = bf16[128,128]{1,0:T(8,128)(2,1)S(1)} custom-call(s32[1]{0:T(128)} %bitcast.me_ref, s32[1,2]{1,0:T(1,128)S(1)} %copy-done.24, bf16[960,128]{1,0:T(8,128)(2,1)S(1)} %collective-permute-done.6.refs_1_, bf16[960,128]{1,0:T(8,128)(2,1)S(1)} %collective-permute-done.7.refs_2_, bf16[256,5120]{1,0:T(8,128)(2,1)S(1)} %copy-done.1, ...), custom_call_target="tpu_custom_call" | custom-call | flops 503316480 | bytes 3145728 | tf_op jit(solution)/shard_map/features/pallas_call | solution.py:372
  77.3 1.7 %scores.1 = (f32[2,3]{1,0:T(2,128)}, f32[2]{0:T(128)}) custom-call(bf16[128,128]{1,0:T(8,128)(2,1)S(1)} %features.1.unit_ref, bf16[528,128]{1,0:T(8,128)(2,1)S(1)} %panel.1.refs_0_, bf16[528,128]{1,0:T(8,128)(2,1)S(1)} %collective-permute-done.15.refs_1_, bf16[528,128]{1,0:T(8,128)(2,1)S(1)} %collective-permute-done.16.refs_2_, ...), custom_call_target="tpu_custom_call" | custom-call | flops 4194304 | bytes 2097152 | tf_op jit(solution)/shard_map/scores/pallas_call | solution.py:428
  (86 shorter events, 14.3 us)
Async XLA Ops:
  7.1 9.0 %collective-permute-start = (bf16[960,128]{1,0:T(8,128)(2,1)S(1)}, bf16[960,128]{1,0:T(8,128)(2,1)S(1)}, u32[]{:S(2)}, u32[]{:S(2)}) collective-permute-start(bf16[960,128]{1,0:T(8,128)(2,1)S(1)} %factors.1.refs_0_), channel_id=1, source_target_pairs={{0,4},{1,5},{4,8},{5,9},{8,12},{9,13},{12,14},{13,15},{14,10},{15,... | collective-permute-start | bytes 737288 | tf_op jit(solution)/shard_map/ppermute | solution.py:49
  10.2 7.4 %collective-permute-start.1 = (bf16[960,128]{1,0:T(8,128)(2,1)S(1)}, bf16[960,128]{1,0:T(8,128)(2,1)S(1)}, u32[]{:S(2)}, u32[]{:S(2)}) collective-permute-start(bf16[960,128]{1,0:T(8,128)(2,1)S(1)} %factors.1.refs_0_), channel_id=1, source_target_pairs={{0,2},{1,3},{4,0},{5,1},{8,4},{9,5},{12,8},{13,9},{14,12},{15,13},... | collective-permute-start | bytes 737288 | tf_op jit(solution)/shard_map/ppermute | solution.py:49
  17.6 8.0 %collective-permute-start.2 = (bf16[960,128]{1,0:T(8,128)(2,1)S(1)}, bf16[960,128]{1,0:T(8,128)(2,1)S(1)}, u32[]{:S(2)}, u32[]{:S(2)}) collective-permute-start(bf16[960,128]{1,0:T(8,128)(2,1)S(1)} %collective-permute-done.refs_0_), channel_id=1, source_target_pairs={{0,4},{1,5},{4,8},{5,9},{8,12},{9,13},{12,14},{13,15},{14,10},{15,... | collective-permute-start | bytes 737288 | tf_op jit(solution)/shard_map/ppermute | solution.py:49
  19.2 7.7 %collective-permute-start.3 = (bf16[960,128]{1,0:T(8,128)(2,1)S(1)}, bf16[960,128]{1,0:T(8,128)(2,1)S(1)}, u32[]{:S(2)}, u32[]{:S(2)}) collective-permute-start(bf16[960,128]{1,0:T(8,128)(2,1)S(1)} %collective-permute-done.1.refs_2_), channel_id=1, source_target_pairs={{0,2},{1,3},{4,0},{5,1},{8,4},{9,5},{12,8},{13,9},{14,12},{15,13},... | collective-permute-start | bytes 737288 | tf_op jit(solution)/shard_map/ppermute | solution.py:49
  21.5 7.4 %collective-permute-start.16 = (bf16[528,128]{1,0:T(8,128)(2,1)S(1)}, bf16[528,128]{1,0:T(8,128)(2,1)S(1)}, u32[]{:S(2)}, u32[]{:S(2)}) collective-permute-start(bf16[528,128]{1,0:T(8,128)(2,1)S(1)} %panel.1.refs_0_), channel_id=1, source_target_pairs={{0,4},{1,5},{4,8},{5,9},{8,12},{9,13},{12,14},{13,15},{14,10},{15,... | collective-permute-start | bytes 405512 | tf_op jit(solution)/shard_map/ppermute | solution.py:49
  23.2 6.6 %collective-permute-start.17 = (bf16[528,128]{1,0:T(8,128)(2,1)S(1)}, bf16[528,128]{1,0:T(8,128)(2,1)S(1)}, u32[]{:S(2)}, u32[]{:S(2)}) collective-permute-start(bf16[528,128]{1,0:T(8,128)(2,1)S(1)} %panel.1.refs_0_), channel_id=1, source_target_pairs={{0,2},{1,3},{4,0},{5,1},{8,4},{9,5},{12,8},{13,9},{14,12},{15,13},... | collective-permute-start | bytes 405512 | tf_op jit(solution)/shard_map/ppermute | solution.py:49
  26.9 11.4 %collective-permute-start.4 = (bf16[960,128]{1,0:T(8,128)(2,1)S(1)}, bf16[960,128]{1,0:T(8,128)(2,1)S(1)}, u32[]{:S(2)}, u32[]{:S(2)}) collective-permute-start(bf16[960,128]{1,0:T(8,128)(2,1)S(1)} %collective-permute-done.2.refs_0_), channel_id=1, source_target_pairs={{0,4},{1,5},{4,8},{5,9},{8,12},{9,13},{12,14},{13,15},{14,10},{15,... | collective-permute-start | bytes 737288 | tf_op jit(solution)/shard_map/ppermute | solution.py:49
  28.5 10.0 %collective-permute-start.5 = (bf16[960,128]{1,0:T(8,128)(2,1)S(1)}, bf16[960,128]{1,0:T(8,128)(2,1)S(1)}, u32[]{:S(2)}, u32[]{:S(2)}) collective-permute-start(bf16[960,128]{1,0:T(8,128)(2,1)S(1)} %collective-permute-done.3.refs_2_), channel_id=1, source_target_pairs={{0,2},{1,3},{4,0},{5,1},{8,4},{9,5},{12,8},{13,9},{14,12},{15,13},... | collective-permute-start | bytes 737288 | tf_op jit(solution)/shard_map/ppermute | solution.py:49
  29.8 5.4 %collective-permute-start.20 = (bf16[528,128]{1,0:T(8,128)(2,1)S(1)}, bf16[528,128]{1,0:T(8,128)(2,1)S(1)}, u32[]{:S(2)}, u32[]{:S(2)}) collective-permute-start(bf16[528,128]{1,0:T(8,128)(2,1)S(1)} %collective-permute-done.16.refs_2_), channel_id=1, source_target_pairs={{0,4},{1,5},{4,8},{5,9},{8,12},{9,13},{12,14},{13,15},{14,10},{15,... | collective-permute-start | bytes 405512 | tf_op jit(solution)/shard_map/ppermute | solution.py:49
  31.4 5.1 %collective-permute-start.21 = (bf16[528,128]{1,0:T(8,128)(2,1)S(1)}, bf16[528,128]{1,0:T(8,128)(2,1)S(1)}, u32[]{:S(2)}, u32[]{:S(2)}) collective-permute-start(bf16[528,128]{1,0:T(8,128)(2,1)S(1)} %collective-permute-done.17.refs_4_), channel_id=1, source_target_pairs={{0,2},{1,3},{4,0},{5,1},{8,4},{9,5},{12,8},{13,9},{14,12},{15,13},... | collective-permute-start | bytes 405512 | tf_op jit(solution)/shard_map/ppermute | solution.py:49
  31.8 8.5 %collective-permute-start.14 = (bf16[960,128]{1,0:T(8,128)(2,1)S(1)}, bf16[960,128]{1,0:T(8,128)(2,1)S(1)}, u32[]{:S(2)}, u32[]{:S(2)}) collective-permute-start(bf16[960,128]{1,0:T(8,128)(2,1)S(1)} %factors.1.refs_0_), channel_id=1, source_target_pairs={{0,1},{1,0},{2,3},{3,2},{4,5},{5,4},{6,7},{7,6},{8,9},{9,8},{10,11... | collective-permute-start | bytes 737288 | tf_op jit(solution)/shard_map/ppermute | solution.py:53
  35.2 5.1 %collective-permute-start.15 = (bf16[528,128]{1,0:T(8,128)(2,1)S(1)}, bf16[528,128]{1,0:T(8,128)(2,1)S(1)}, u32[]{:S(2)}, u32[]{:S(2)}) collective-permute-start(bf16[528,128]{1,0:T(8,128)(2,1)S(1)} %panel.1.refs_0_), channel_id=1, source_target_pairs={{0,1},{1,0},{2,3},{3,2},{4,5},{5,4},{6,7},{7,6},{8,9},{9,8},{10,11... | collective-permute-start | bytes 405512 | tf_op jit(solution)/shard_map/ppermute | solution.py:53
  36.5 6.5 %collective-permute-start.24 = (bf16[528,128]{1,0:T(8,128)(2,1)S(1)}, bf16[528,128]{1,0:T(8,128)(2,1)S(1)}, u32[]{:S(2)}, u32[]{:S(2)}) collective-permute-start(bf16[528,128]{1,0:T(8,128)(2,1)S(1)} %collective-permute-done.20.refs_6_), channel_id=1, source_target_pairs={{0,4},{1,5},{4,8},{5,9},{8,12},{9,13},{12,14},{13,15},{14,10},{15,... | collective-permute-start | bytes 405512 | tf_op jit(solution)/shard_map/ppermute | solution.py:49
  38.3 5.0 %collective-permute-start.25 = (bf16[528,128]{1,0:T(8,128)(2,1)S(1)}, bf16[528,128]{1,0:T(8,128)(2,1)S(1)}, u32[]{:S(2)}, u32[]{:S(2)}) collective-permute-start(bf16[528,128]{1,0:T(8,128)(2,1)S(1)} %collective-permute-done.21.refs_8_), channel_id=1, source_target_pairs={{0,2},{1,3},{4,0},{5,1},{8,4},{9,5},{12,8},{13,9},{14,12},{15,13},... | collective-permute-start | bytes 405512 | tf_op jit(solution)/shard_map/ppermute | solution.py:49
  38.5 8.0 %collective-permute-start.6 = (bf16[960,128]{1,0:T(8,128)(2,1)S(1)}, bf16[960,128]{1,0:T(8,128)(2,1)S(1)}, u32[]{:S(2)}, u32[]{:S(2)}) collective-permute-start(bf16[960,128]{1,0:T(8,128)(2,1)S(1)} %collective-permute-done.4.refs_0_), channel_id=1, source_target_pairs={{0,4},{1,5},{4,8},{5,9},{8,12},{9,13},{12,14},{13,15},{14,10},{15,... | collective-permute-start | bytes 737288 | tf_op jit(solution)/shard_map/ppermute | solution.py:49
  40.3 6.8 %collective-permute-start.12 = (bf16[960,128]{1,0:T(8,128)(2,1)S(1)}, bf16[960,128]{1,0:T(8,128)(2,1)S(1)}, u32[]{:S(2)}, u32[]{:S(2)}) collective-permute-start(bf16[960,128]{1,0:T(8,128)(2,1)S(1)} %collective-permute-done.refs_0_), channel_id=1, source_target_pairs={{0,1},{1,0},{2,3},{3,2},{4,5},{5,4},{6,7},{7,6},{8,9},{9,8},{10,11... | collective-permute-start | bytes 737288 | tf_op jit(solution)/shard_map/ppermute | solution.py:53
  40.3 6.7 %collective-permute-start.13 = (bf16[960,128]{1,0:T(8,128)(2,1)S(1)}, bf16[960,128]{1,0:T(8,128)(2,1)S(1)}, u32[]{:S(2)}, u32[]{:S(2)}) collective-permute-start(bf16[960,128]{1,0:T(8,128)(2,1)S(1)} %collective-permute-done.1.refs_2_), channel_id=1, source_target_pairs={{0,1},{1,0},{2,3},{3,2},{4,5},{5,4},{6,7},{7,6},{8,9},{9,8},{10,11... | collective-permute-start | bytes 737288 | tf_op jit(solution)/shard_map/ppermute | solution.py:53
  42.9 4.7 %collective-permute-start.10 = (bf16[960,128]{1,0:T(8,128)(2,1)S(1)}, bf16[960,128]{1,0:T(8,128)(2,1)S(1)}, u32[]{:S(2)}, u32[]{:S(2)}) collective-permute-start(bf16[960,128]{1,0:T(8,128)(2,1)S(1)} %collective-permute-done.2.refs_0_), channel_id=1, source_target_pairs={{0,1},{1,0},{2,3},{3,2},{4,5},{5,4},{6,7},{7,6},{8,9},{9,8},{10,11... | collective-permute-start | bytes 737288 | tf_op jit(solution)/shard_map/ppermute | solution.py:53
  43.3 16.9 %collective-permute-start.11 = (bf16[960,128]{1,0:T(8,128)(2,1)S(1)}, bf16[960,128]{1,0:T(8,128)(2,1)S(1)}, u32[]{:S(2)}, u32[]{:S(2)}) collective-permute-start(bf16[960,128]{1,0:T(8,128)(2,1)S(1)} %collective-permute-done.3.refs_2_), channel_id=1, source_target_pairs={{0,1},{1,0},{2,3},{3,2},{4,5},{5,4},{6,7},{7,6},{8,9},{9,8},{10,11... | collective-permute-start | bytes 737288 | tf_op jit(solution)/shard_map/ppermute | solution.py:53
  46.5 14.2 %collective-permute-start.28 = (bf16[528,128]{1,0:T(8,128)(2,1)S(1)}, bf16[528,128]{1,0:T(8,128)(2,1)S(1)}, u32[]{:S(2)}, u32[]{:S(2)}) collective-permute-start(bf16[528,128]{1,0:T(8,128)(2,1)S(1)} %collective-permute-done.25.refs_12_), channel_id=1, source_target_pairs={{0,2},{1,3},{4,0},{5,1},{8,4},{9,5},{12,8},{13,9},{14,12},{15,13},... | collective-permute-start | bytes 405512 | tf_op jit(solution)/shard_map/ppermute | solution.py:49
  47.1 22.7 %collective-permute-start.8 = (bf16[960,128]{1,0:T(8,128)(2,1)S(1)}, bf16[960,128]{1,0:T(8,128)(2,1)S(1)}, u32[]{:S(2)}, u32[]{:S(2)}) collective-permute-start(bf16[960,128]{1,0:T(8,128)(2,1)S(1)} %collective-permute-done.4.refs_0_), channel_id=1, source_target_pairs={{0,1},{1,0},{2,3},{3,2},{4,5},{5,4},{6,7},{7,6},{8,9},{9,8},{10,11... | collective-permute-start | bytes 737288 | tf_op jit(solution)/shard_map/ppermute | solution.py:53
  47.1 23.2 %collective-permute-start.9 = (bf16[960,128]{1,0:T(8,128)(2,1)S(1)}, bf16[960,128]{1,0:T(8,128)(2,1)S(1)}, u32[]{:S(2)}, u32[]{:S(2)}) collective-permute-start(bf16[960,128]{1,0:T(8,128)(2,1)S(1)} %collective-permute-done.5.refs_2_), channel_id=1, source_target_pairs={{0,1},{1,0},{2,3},{3,2},{4,5},{5,4},{6,7},{7,6},{8,9},{9,8},{10,11... | collective-permute-start | bytes 737288 | tf_op jit(solution)/shard_map/ppermute | solution.py:53
  47.6 22.7 %collective-permute-start.7 = (bf16[960,128]{1,0:T(8,128)(2,1)S(1)}, bf16[960,128]{1,0:T(8,128)(2,1)S(1)}, u32[]{:S(2)}, u32[]{:S(2)}) collective-permute-start(bf16[960,128]{1,0:T(8,128)(2,1)S(1)} %collective-permute-done.6.refs_1_), channel_id=1, source_target_pairs={{0,1},{1,0},{2,3},{3,2},{4,5},{5,4},{6,7},{7,6},{8,9},{9,8},{10,11... | collective-permute-start | bytes 737288 | tf_op jit(solution)/shard_map/ppermute | solution.py:53
  58.4 3.6 %copy-start.7 = (bf16[256,2560]{1,0:T(8,128)(2,1)S(1)}, bf16[256,2560]{1,0:T(8,128)(2,1)}, u32[]{:S(2)}) copy-start(bf16[256,2560]{1,0:T(8,128)(2,1)} %refs_6_.7) | copy-start | bytes 3932164
  58.4 4.0 %copy-start.9 = (bf16[5120,128]{1,0:T(8,128)(2,1)S(1)}, bf16[5120,128]{1,0:T(8,128)(2,1)}, u32[]{:S(2)}) copy-start(bf16[5120,128]{1,0:T(8,128)(2,1)} %refs_9_.3) | copy-start | bytes 3932164
  60.2 9.0 %collective-permute-start.18 = (bf16[528,128]{1,0:T(8,128)(2,1)S(1)}, bf16[528,128]{1,0:T(8,128)(2,1)S(1)}, u32[]{:S(2)}, u32[]{:S(2)}) collective-permute-start(bf16[528,128]{1,0:T(8,128)(2,1)S(1)} %collective-permute-done.16.refs_2_), channel_id=1, source_target_pairs={{0,1},{1,0},{2,3},{3,2},{4,5},{5,4},{6,7},{7,6},{8,9},{9,8},{10,11... | collective-permute-start | bytes 405512 | tf_op jit(solution)/shard_map/ppermute | solution.py:53
  60.7 9.0 %collective-permute-start.19 = (bf16[528,128]{1,0:T(8,128)(2,1)S(1)}, bf16[528,128]{1,0:T(8,128)(2,1)S(1)}, u32[]{:S(2)}, u32[]{:S(2)}) collective-permute-start(bf16[528,128]{1,0:T(8,128)(2,1)S(1)} %collective-permute-done.17.refs_4_), channel_id=1, source_target_pairs={{0,1},{1,0},{2,3},{3,2},{4,5},{5,4},{6,7},{7,6},{8,9},{9,8},{10,11... | collective-permute-start | bytes 405512 | tf_op jit(solution)/shard_map/ppermute | solution.py:53
  69.2 8.1 %collective-permute-start.22 = (bf16[528,128]{1,0:T(8,128)(2,1)S(1)}, bf16[528,128]{1,0:T(8,128)(2,1)S(1)}, u32[]{:S(2)}, u32[]{:S(2)}) collective-permute-start(bf16[528,128]{1,0:T(8,128)(2,1)S(1)} %collective-permute-done.20.refs_6_), channel_id=1, source_target_pairs={{0,1},{1,0},{2,3},{3,2},{4,5},{5,4},{6,7},{7,6},{8,9},{9,8},{10,11... | collective-permute-start | bytes 405512 | tf_op jit(solution)/shard_map/ppermute | solution.py:53
  69.7 7.6 %collective-permute-start.23 = (bf16[528,128]{1,0:T(8,128)(2,1)S(1)}, bf16[528,128]{1,0:T(8,128)(2,1)S(1)}, u32[]{:S(2)}, u32[]{:S(2)}) collective-permute-start(bf16[528,128]{1,0:T(8,128)(2,1)S(1)} %collective-permute-done.21.refs_8_), channel_id=1, source_target_pairs={{0,1},{1,0},{2,3},{3,2},{4,5},{5,4},{6,7},{7,6},{8,9},{9,8},{10,11... | collective-permute-start | bytes 405512 | tf_op jit(solution)/shard_map/ppermute | solution.py:53
  69.8 7.5 %collective-permute-start.26 = (bf16[528,128]{1,0:T(8,128)(2,1)S(1)}, bf16[528,128]{1,0:T(8,128)(2,1)S(1)}, u32[]{:S(2)}, u32[]{:S(2)}) collective-permute-start(bf16[528,128]{1,0:T(8,128)(2,1)S(1)} %collective-permute-done.24.refs_10_), channel_id=1, source_target_pairs={{0,1},{1,0},{2,3},{3,2},{4,5},{5,4},{6,7},{7,6},{8,9},{9,8},{10,11... | collective-permute-start | bytes 405512 | tf_op jit(solution)/shard_map/ppermute | solution.py:53
  70.2 7.1 %collective-permute-start.27 = (bf16[528,128]{1,0:T(8,128)(2,1)S(1)}, bf16[528,128]{1,0:T(8,128)(2,1)S(1)}, u32[]{:S(2)}, u32[]{:S(2)}) collective-permute-start(bf16[528,128]{1,0:T(8,128)(2,1)S(1)} %collective-permute-done.25.refs_12_), channel_id=1, source_target_pairs={{0,1},{1,0},{2,3},{3,2},{4,5},{5,4},{6,7},{7,6},{8,9},{9,8},{10,11... | collective-permute-start | bytes 405512 | tf_op jit(solution)/shard_map/ppermute | solution.py:53
  70.3 7.0 %collective-permute-start.29 = (bf16[528,128]{1,0:T(8,128)(2,1)S(1)}, bf16[528,128]{1,0:T(8,128)(2,1)S(1)}, u32[]{:S(2)}, u32[]{:S(2)}) collective-permute-start(bf16[528,128]{1,0:T(8,128)(2,1)S(1)} %collective-permute-done.28.refs_14_), channel_id=1, source_target_pairs={{0,1},{1,0},{2,3},{3,2},{4,5},{5,4},{6,7},{7,6},{8,9},{9,8},{10,11... | collective-permute-start | bytes 405512 | tf_op jit(solution)/shard_map/ppermute | solution.py:53
  (23 other events, 36.3 us)

commit v4 on v3

--- a/solution.py
+++ b/solution.py
@@ -38,14 +38,13 @@
     return jnp.where(side == 0, row, RING_CHIPS - 1 - row)
 
 
-def hop(value, step):
+def hop(value):
     half = RING_CHIPS // 2
     place = [2 * q if q < half else 2 * (RING_CHIPS - 1 - q) + 1 for q in range(RING_CHIPS)]
-    pairs = [
-        (2 * place[q] + c, 2 * place[(q + step) % RING_CHIPS] + c)
-        for q in range(RING_CHIPS)
-        for c in range(2)
-    ]
+    pairs = []
+    for q in range(RING_CHIPS):
+        pairs.append((2 * place[q], 2 * place[(q + 1) % RING_CHIPS]))
+        pairs.append((2 * place[q] + 1, 2 * place[(q - 1) % RING_CHIPS] + 1))
     return lax.ppermute(value, "dp", pairs)
 
 
@@ -71,22 +70,20 @@
     return copies
 
 
-def factor_kernel(me_ref, *refs):
-    hbm, out_ref, held, sems = refs[:7], refs[7], refs[8:15], refs[15]
-    gain_ref, down_up_ref, up_low_ref, sketch_ref, up_up_ref, down_low_ref, expand_ref = held
+def pack_kernel(me_ref, *refs):
+    hbm, out_ref, held, sems = refs[:9], refs[9], refs[10:19], refs[19]
+    gain_ref, down_up_ref, up_low_ref, sketch_ref, up_up_ref, down_low_ref, expand_ref, val_ref, label_ref = held
     copies = load(zip(hbm, held), sems)
     rows = down_up_ref.shape[0]
     half = LANES // 2
-    copies[0].wait()
-    copies[1].wait()
+    for copy in copies:
+        copy.wait()
     for b in range(rows // half):
         place = me_ref[0] * (rows // half) + b
         row = gain_ref[pl.ds(place // 2, 1), :]
         column = diagonal_column(row, (place % 2) * half, half)
         part = down_up_ref[pl.ds(b * half, half), :].astype(F32)
         out_ref[pl.ds(b * half, half), :] = (column * part).astype(BF16)
-    for copy in copies[2:]:
-        copy.wait()
     at = rows
     out_ref[pl.ds(at, rows), :] = mm(up_low_ref[...], sketch_ref[...]).astype(BF16)
     at += rows
@@ -96,11 +93,7 @@
     low = mm_rows(down_low_ref[...], jnp.concatenate([expand, expand], axis=0))
     first, second = low[: rows // 2], low[rows // 2 :]
     out_ref[pl.ds(at, rows // 2), :] = jnp.where(half_lanes(first.shape), first, second).astype(BF16)
-
-
-def panel_kernel(val_hbm, label_hbm, out_ref, val_ref, label_ref, sems):
-    for copy in load(((val_hbm, val_ref), (label_hbm, label_ref)), sems):
-        copy.wait()
+    at += rows // 2
     wide = val_ref[...].astype(F32)
     count, width = wide.shape
     scale = lax.rsqrt(jnp.sum(wide * wide, axis=1, keepdims=True) + 1e-06)
@@ -111,7 +104,7 @@
     blocks += [labels, labels]
     for i in range(0, len(blocks), 2):
         pair = jnp.concatenate(blocks[i : i + 2], axis=0)
-        out_ref[pl.ds(i * count, 2 * count), :] = pair.astype(BF16)
+        out_ref[pl.ds(at + i * count, 2 * count), :] = pair.astype(BF16)
 
 
 X_LOW, X_DOWN, X_SOURCE, SQUARES, J_LOW, M_DOWN, M_SOURCE, VALUES, SUMS = 0, 2, 3, 4, 5, 7, 8, 9, 11
@@ -139,7 +132,7 @@
 
     copies = []
     for k, away in enumerate(aways):
-        chip = ring_chip((pos + (away + RING_CHIPS)) % RING_CHIPS)
+        chip = ring_chip((pos + away * (2 * core - 1) + RING_CHIPS) % RING_CHIPS)
         odd = chip % 2
         mine = pl.ds(pl.multiple_of(chip * span, LANES), span)
         values_start = (chip // 2) * span + odd * (span // 2 - pad)
@@ -147,7 +140,8 @@
         shift = odd * pad
         up[k, pl.ds(pl.multiple_of((1 - odd) * rows, 16), pad), :] = jnp.zeros((pad, 2 * LANES), BF16)
         pairs = []
-        for piece, c in ((pieces[2 * k], core), (pieces[2 * k + 1], 1 - core)):
+        side = core if away >= 0 else 1 - core
+        for piece, c in ((pieces[2 * k], side), (pieces[2 * k + 1], 1 - side)):
             one = pl.ds(pl.multiple_of(c * rows, 16), rows)
             part = pl.ds(pl.multiple_of(c * half, 16), half)
             up_part = pl.ds(pl.multiple_of(shift + c * half, 16), half)
@@ -247,7 +241,7 @@
         out_ref[pl.ds(e * pad, pad), :] = (own * lax.rsqrt(squares + 1e-06)).astype(BF16)
 
 
-def score_kernel(pieces, count, unit_ref, *refs):
+def score_kernel(pieces, count, start, unit_ref, *refs):
     piece_refs = refs[:pieces]
     best_ref, mean_ref, spread = refs[pieces:]
     half = LANES // 2
@@ -258,8 +252,8 @@
             spread[e, pl.ds(i * count, count), :] = jnp.broadcast_to(row, (count, LANES))
     best = [[jnp.full((count, LANES), -2.0 * scale, F32) for _ in range(TASKS)] for _ in range(2)]
     for piece in piece_refs:
-        wide = piece[pl.ds(0, half * count), :].astype(F32)
-        labels = piece[pl.ds(half * count, 2 * count), :].astype(F32)[:count]
+        wide = piece[pl.ds(start, half * count), :].astype(F32)
+        labels = piece[pl.ds(start + half * count, 2 * count), :].astype(F32)[:count]
         for e in range(2):
             products = wide * spread[e]
             total = jnp.sum(products.reshape(half, count, LANES), axis=0)
@@ -278,6 +272,10 @@
 SMEM = pl.BlockSpec(memory_space=pltpu.SMEM)
 ANY = pl.BlockSpec(memory_space=pl.ANY)
 HBM = pl.BlockSpec(memory_space=pltpu.HBM)
+
+
+def in_hbm(arrays):
+    return [pltpu.with_memory_space_constraint(a, pltpu.HBM) for a in arrays]
 
 
 def params(mib):
@@ -328,28 +326,19 @@
         top_expander_matrix.T,
         bottom_reducer_matrix,
         bottom_expander_sketch.T,
-    )
-    factors = pl.pallas_call(
-        factor_kernel,
-        out_shape=jax.ShapeDtypeStruct((3 * rows, LANES), BF16),
+        heldout_sketched_signals,
+        benchmark_labels.T,
+    )
+    own = pl.pallas_call(
+        pack_kernel,
+        out_shape=jax.ShapeDtypeStruct((3 * rows + (LANES // 2 + 2) * count, LANES), BF16),
         in_specs=[SMEM] + [HBM] * len(inputs),
         out_specs=VMEM,
         scratch_shapes=[pltpu.VMEM(a.shape, a.dtype) for a in inputs]
         + [pltpu.SemaphoreType.DMA((len(inputs),))],
         compiler_params=params(8),
-        name="factors",
-    )(me.reshape(1), *inputs)
-    inputs = (heldout_sketched_signals, benchmark_labels.T)
-    panel = pl.pallas_call(
-        panel_kernel,
-        out_shape=jax.ShapeDtypeStruct(((LANES // 2 + 2) * count, LANES), BF16),
-        in_specs=[HBM] * len(inputs),
-        out_specs=VMEM,
-        scratch_shapes=[pltpu.VMEM(a.shape, a.dtype) for a in inputs]
-        + [pltpu.SemaphoreType.DMA((len(inputs),))],
-        compiler_params=params(8),
-        name="panel",
-    )(*inputs)
+        name="pack",
+    )(me.reshape(1), *in_hbm(inputs))
 
     span = 2 * rows
     activations = (
@@ -399,42 +388,36 @@
             compiler_params=params(16),
             cost_estimate=cost(n * tokens * span * LANES * 24, 3 * n * MIB),
             name="features" if last else "stage",
-        )(*head, *pieces, *activations, *sums, *(small if last else ()))
+        )(*head, *pieces, *in_hbm(activations), *sums, *in_hbm(small if last else ()))
 
     tie = lax.optimization_barrier
     half = RING_CHIPS // 2
-    up = down = factors
-    panel_up = panel_down = panel
-    sums = ()
-    held = [factors, other_core(factors)]
-    aways = (0,)
-    panels = [panel, other_core(panel)]
+    first, second = own, other_core(own)
+    held, aways, sums = [first, second], (0,), ()
+    blocks = list(held)
     for k in range(1, half + 1):
-        up = hop(up, 1)
-        down = hop(down, -1) if k < half else down
-        panel_up = hop(panel_up, 1) if k < half else panel_up
-        panel_down = hop(panel_down, -1)
-        sums = stage(aways, held, sums)
-        up, down = tie((up, down))
-        panel_up, panel_down, _, _ = tie((panel_up, panel_down, up, down))
-        aways = (-k, k) if k < half else (-half,)
-        held = [up, other_core(up)]
-        if k < half:
-            held += [down, other_core(down)]
-            panels += [panel_up, other_core(panel_up)]
-        panels += [panel_down, other_core(panel_down)]
+        first = hop(first)
+        if k == half:
+            held, aways, sums = [first, other_core(first)], (half,), stage(aways, held, sums)
+        else:
+            second = hop(second)
+            old, held = held, [first, second, other_core(first), other_core(second)]
+            sums = stage(aways, old, sums)
+            second, sums = tie((second, sums))
+            aways = (k, -k)
+        blocks += held
     unit = stage(aways, held, sums, last=True)
 
     task_best, scores = pl.pallas_call(
-        functools.partial(score_kernel, len(panels), count),
+        functools.partial(score_kernel, len(blocks), count, 3 * rows),
         out_shape=(jax.ShapeDtypeStruct((2, TASKS), F32), jax.ShapeDtypeStruct((2,), F32)),
-        in_specs=[VMEM] * (1 + len(panels)),
+        in_specs=[VMEM] * (1 + len(blocks)),
         out_specs=(SMEM, SMEM),
         scratch_shapes=[pltpu.VMEM((2, LANES // 2 * count, LANES), F32)],
         compiler_params=params(16),
         cost_estimate=cost(4 * MIB, 2 * MIB),
         name="scores",
-    )(unit, *panels)
+    )(unit, *blocks)
     return (scores, task_best)
 
 

time: 80 us -> 51.6 us (0.65)
  local copies, waits for them, and re-layouts: 19.6 us -> 0.01 us
  waiting for transfers between devices: 21.7 us -> 13.7 us
  Pallas kernels: 17.8 us -> 21.7 us
  starting transfers between devices: 19 us -> 15.2 us
    unnamed x50 -> x2, local copies, waits for them, and re-layouts: 19.6 us -> 0.01 us
    ppermute x14 -> x7, waiting for transfers between devices: 21.7 us -> 13.7 us  [hop(): return lax.ppermute(value, 'dp', pairs)]
    pallas_call x5, Pallas kernels: 15 us -> 18.6 us  [stage(): pl.pallas_call(functools.partial(stage_kernel, aways, first, last), out_s...]
    ppermute x16 -> x8, starting transfers between devices: 3.35 us -> 1.04 us  [other_core(): lax.ppermute(value, 'dp', [(d, d ^ 1) for d in range(2 * RING_CHIPS)])]
    ppermute x14 -> x7, starting transfers between devices: 15.7 us -> 14.2 us  [hop(): return lax.ppermute(value, 'dp', pairs)]
    pallas_call x3 -> x2, Pallas kernels: 2.84 us -> 3.1 us  [the longest x1 1.7 us: shards(): pl.pallas_call(functools.partial(score_kernel, len(blocks), count, 3 * ro...]
  transfers between devices with their start and end apart: 30 -> 15, of which waited for: 10 -> 6; matrix products, arithmetic and copies ran while one was open for 0% -> 0% of each run, Pallas kernels for 19% -> 28%
where the time goes in v4:
time: 51.6 us; the launch traced here: 51.4 us
  Pallas kernels  21.7 us (42%)
  starting transfers between devices  15.2 us (29%)
  waiting for transfers between devices  13.7 us (27%)
  between operations  0.74 us (1%)
    pallas_call x5, Pallas kernels, stage(): pl.pallas_call(functools.partial(stage_kernel, aways, first, last), out_s...  18.6 us
    ppermute x7, starting transfers between devices, hop(): return lax.ppermute(value, 'dp', pairs)  14.2 us
    ppermute x7, waiting for transfers between devices, hop(): return lax.ppermute(value, 'dp', pairs)  13.7 us
    pallas_call x1, Pallas kernels, shards(): pl.pallas_call(functools.partial(score_kernel, len(blocks), count, 3 * ro...  1.7 us
    pallas_call x1, Pallas kernels, shards(): pl.pallas_call(pack_kernel, out_shape=jax.ShapeDtypeStruct((3 * rows + (L...  1.41 us
    ppermute x8, starting transfers between devices, other_core(): lax.ppermute(value, 'dp', [(d, d ^ 1) for d in range(2 * RING_CHIPS)])  1.04 us
  transfers between devices with their start and end apart: 15, of which 6 were waited for; matrix products, arithmetic and copies ran while one was open for 0% of the time, Pallas kernels for 28%

profile of v4, /device:TPU:0, one launch (start us, length us, event | category | flops | bytes accessed | tf_op | source)
XLA Modules:
  0.0 51.4 jit_solution(8500987576346152839)
XLA Ops:
  0.6 1.4 %pack.1.refs_0_ = bf16[1488,128]{1,0:T(8,128)(2,1)S(1)} custom-call(s32[1]{0:T(128)} %bitcast.me_ref, f32[40,128]{1,0:T(8,128)} %bitcast.14, bf16[320,128]{1,0:T(8,128)(2,1)} %refs_1_.1, bf16[320,128]{1,0:T(8,128)(2,1)} %bitcast.20, bf16[128,128]{1,0:T(8,128)(2,1)} %refs_3_.3, bf16[160,128]{1,0:T(8,128)(2,1)} %bitcast.21, bf16[320,128]{1,0:T(8,128)(2,1)} %refs_5_.6, ...), custom_call_target="tpu_custom_call" | custom-call | tf_op jit(solution)/shard_map/pack/pallas_call | solution.py:332
  2.1 0.5 %collective-permute-start.5 = (bf16[1488,128]{1,0:T(8,128)(2,1)S(1)}, bf16[1488,128]{1,0:T(8,128)(2,1)S(1)}, u32[]{:S(2)}, u32[]{:S(2)}) collective-permute-start(bf16[1488,128]{1,0:T(8,128)(2,1)S(1)} %pack.1.refs_0_), channel_id=1, source_target_pairs={{0,1},{1,0},{2,3},{3,2},{4,5},{5,4},{6,7},{7,6},{8,9},{9,8},{10,11... | collective-permute-start | bytes 1142792 | tf_op jit(solution)/shard_map/ppermute | solution.py:52
  2.6 2.6 %collective-permute-start = (bf16[1488,128]{1,0:T(8,128)(2,1)S(1)}, bf16[1488,128]{1,0:T(8,128)(2,1)S(1)}, u32[]{:S(2)}, u32[]{:S(2)}) collective-permute-start(bf16[1488,128]{1,0:T(8,128)(2,1)S(1)} %pack.1.refs_0_), channel_id=1, source_target_pairs={{0,4},{1,3},{4,8},{5,1},{8,12},{9,5},{12,14},{13,9},{14,10},{15,13... | collective-permute-start | bytes 1142792 | tf_op jit(solution)/shard_map/ppermute | solution.py:48
  5.2 1.6 %collective-permute-start.6 = (bf16[1488,128]{1,0:T(8,128)(2,1)S(1)}, bf16[1488,128]{1,0:T(8,128)(2,1)S(1)}, u32[]{:S(2)}, u32[]{:S(2)}) collective-permute-start(bf16[1488,128]{1,0:T(8,128)(2,1)S(1)} %collective-permute-done.5.refs_1_), channel_id=1, source_target_pairs={{0,4},{1,3},{4,8},{5,1},{8,12},{9,5},{12,14},{13,9},{14,10},{15,13... | collective-permute-start | bytes 1142792 | tf_op jit(solution)/shard_map/ppermute | solution.py:48
  6.8 3.9 %collective-permute-done.refs_0_.refs_2_ = bf16[1488,128]{1,0:T(8,128)(2,1)S(1)} collective-permute-done((bf16[1488,128]{1,0:T(8,128)(2,1)S(1)}, bf16[1488,128]{1,0:T(8,128)(2,1)S(1)}, u32[]{:S(2)}, u32[]{:S(2)}) %collective-permute-start) | collective-permute-done | bytes 380960 | tf_op jit(solution)/shard_map/ppermute | solution.py:48
  10.8 2.1 %collective-permute-start.1 = (bf16[1488,128]{1,0:T(8,128)(2,1)S(1)}, bf16[1488,128]{1,0:T(8,128)(2,1)S(1)}, u32[]{:S(2)}, u32[]{:S(2)}) collective-permute-start(bf16[1488,128]{1,0:T(8,128)(2,1)S(1)} %collective-permute-done.refs_0_.refs_2_), channel_id=1, source_target_pairs={{0,4},{1,3},{4,8},{5,1},{8,12},{9,5},{12,14},{13,9},{14,10},{15,13... | collective-permute-start | bytes 1142792 | tf_op jit(solution)/shard_map/ppermute | solution.py:48
  12.9 0.0 collective-permute-start.8
  12.9 2.0 %collective-permute-done.6.refs_1_.refs_3_ = bf16[1488,128]{1,0:T(8,128)(2,1)S(1)} collective-permute-done((bf16[1488,128]{1,0:T(8,128)(2,1)S(1)}, bf16[1488,128]{1,0:T(8,128)(2,1)S(1)}, u32[]{:S(2)}, u32[]{:S(2)}) %collective-permute-start.6) | collective-permute-done | bytes 380960 | tf_op jit(solution)/shard_map/ppermute | solution.py:48
  14.9 0.0 collective-permute-start.9
  14.9 2.9 %stage.4 = (f32[256,1408]{1,0:T(8,128)S(1)}, f32[128,256]{1,0:T(8,128)S(1)}) custom-call(s32[1]{0:T(128)} %bitcast.me_ref, bf16[1488,128]{1,0:T(8,128)(2,1)S(1)} %pack.1.refs_0_, bf16[1488,128]{1,0:T(8,128)(2,1)S(1)} %collective-permute-done.5.refs_1_, bf16[256,5120]{1,0:T(8,128)(2,1)} %refs_3_.5, bf16[256,5120]{1,0:T(8,128)(2,1)} %refs_4_.9, ...), custom_call_target="tpu_custom_call" | custom-call | flops 503316480 | bytes 3145728 | tf_op jit(solution)/shard_map/stage/pallas_call | solution.py:361
  17.7 2.1 %collective-permute-start.7 = (bf16[1488,128]{1,0:T(8,128)(2,1)S(1)}, bf16[1488,128]{1,0:T(8,128)(2,1)S(1)}, u32[]{:S(2)}, u32[]{:S(2)}) collective-permute-start(bf16[1488,128]{1,0:T(8,128)(2,1)S(1)} %collective-permute-done.6.refs_1_.refs_3_), channel_id=1, source_target_pairs={{0,4},{1,3},{4,8},{5,1},{8,12},{9,5},{12,14},{13,9},{14,10},{15,13... | collective-permute-start | bytes 1142792 | tf_op jit(solution)/shard_map/ppermute | solution.py:48
  19.9 1.6 %collective-permute-start.2 = (bf16[1488,128]{1,0:T(8,128)(2,1)S(1)}, bf16[1488,128]{1,0:T(8,128)(2,1)S(1)}, u32[]{:S(2)}, u32[]{:S(2)}) collective-permute-start(bf16[1488,128]{1,0:T(8,128)(2,1)S(1)} %collective-permute-done.1.refs_0_.refs_6_), channel_id=1, source_target_pairs={{0,4},{1,3},{4,8},{5,1},{8,12},{9,5},{12,14},{13,9},{14,10},{15,13... | collective-permute-start | bytes 1142792 | tf_op jit(solution)/shard_map/ppermute | solution.py:48
  21.4 0.0 collective-permute-done.8.refs_2_.refs_4_
  21.5 0.0 collective-permute-done.9.refs_3_.refs_5_
  21.5 3.8 %stage.5 = (f32[256,1408]{1,0:T(8,128)S(1)}, f32[128,256]{1,0:T(8,128)S(1)}) custom-call(s32[1]{0:T(128)} %bitcast.me_ref, bf16[1488,128]{1,0:T(8,128)(2,1)S(1)} %collective-permute-done.refs_0_.refs_2_, bf16[1488,128]{1,0:T(8,128)(2,1)S(1)} %collective-permute-done.6.refs_1_.refs_3_, ...), custom_call_target="tpu_custom_call", output_to_operand_aliasing={{0}: (13, {}), {1}: (14, {})} | custom-call | flops 1006632960 | bytes 6291456 | tf_op jit(solution)/shard_map/stage/pallas_call | solution.py:361
  25.3 0.2 collective-permute-done.7.refs_1_.refs_7_
  25.4 2.1 %collective-permute-start.10 = (bf16[1488,128]{1,0:T(8,128)(2,1)S(1)}, bf16[1488,128]{1,0:T(8,128)(2,1)S(1)}, u32[]{:S(2)}, u32[]{:S(2)}) collective-permute-start(bf16[1488,128]{1,0:T(8,128)(2,1)S(1)} %collective-permute-done.7.refs_1_.refs_7_), channel_id=1, source_target_pairs={{0,4},{1,3},{4,8},{5,1},{8,12},{9,5},{12,14},{13,9},{14,10},{15,13... | collective-permute-start | bytes 1142792 | tf_op jit(solution)/shard_map/ppermute | solution.py:48
  27.5 2.0 %collective-permute-done.2.refs_0_.refs_10_ = bf16[1488,128]{1,0:T(8,128)(2,1)S(1)} collective-permute-done((bf16[1488,128]{1,0:T(8,128)(2,1)S(1)}, bf16[1488,128]{1,0:T(8,128)(2,1)S(1)}, u32[]{:S(2)}, u32[]{:S(2)}) %collective-permute-start.2) | collective-permute-done | bytes 380960 | tf_op jit(solution)/shard_map/ppermute | solution.py:48
  29.5 2.1 %collective-permute-start.3 = (bf16[1488,128]{1,0:T(8,128)(2,1)S(1)}, bf16[1488,128]{1,0:T(8,128)(2,1)S(1)}, u32[]{:S(2)}, u32[]{:S(2)}) collective-permute-start(bf16[1488,128]{1,0:T(8,128)(2,1)S(1)} %collective-permute-done.2.refs_0_.refs_10_), channel_id=1, source_target_pairs={{0,4},{1,3},{4,8},{5,1},{8,12},{9,5},{12,14},{13,9},{14,10},{15,13... | collective-permute-start | bytes 1142792 | tf_op jit(solution)/shard_map/ppermute | solution.py:48
  31.6 0.0 collective-permute-start.13
  31.6 0.5 collective-permute-start.14
  32.1 1.5 %collective-permute-done.10.refs_1_.refs_11_ = bf16[1488,128]{1,0:T(8,128)(2,1)S(1)} collective-permute-done((bf16[1488,128]{1,0:T(8,128)(2,1)S(1)}, bf16[1488,128]{1,0:T(8,128)(2,1)S(1)}, u32[]{:S(2)}, u32[]{:S(2)}) %collective-permute-start.10) | collective-permute-done | bytes 380960 | tf_op jit(solution)/shard_map/ppermute | solution.py:48
  33.6 0.0 collective-permute-start.12
  33.6 4.1 %collective-permute-done.3.refs_1_.refs_14_ = bf16[1488,128]{1,0:T(8,128)(2,1)S(1)} collective-permute-done((bf16[1488,128]{1,0:T(8,128)(2,1)S(1)}, bf16[1488,128]{1,0:T(8,128)(2,1)S(1)}, u32[]{:S(2)}, u32[]{:S(2)}) %collective-permute-start.3) | collective-permute-done | bytes 380960 | tf_op jit(solution)/shard_map/ppermute | solution.py:48
  37.7 0.0 collective-permute-start.4
  37.7 0.0 collective-permute-done.13.refs_2_.refs_8_
  37.7 0.0 collective-permute-done.14.refs_3_.refs_9_
  37.7 3.9 %stage.6 = (f32[256,1408]{1,0:T(8,128)S(1)}, f32[128,256]{1,0:T(8,128)S(1)}) custom-call(s32[1]{0:T(128)} %bitcast.me_ref, bf16[1488,128]{1,0:T(8,128)(2,1)S(1)} %collective-permute-done.1.refs_0_.refs_6_, bf16[1488,128]{1,0:T(8,128)(2,1)S(1)} %collective-permute-done.7.refs_1_.refs_7_, ...), custom_call_target="tpu_custom_call", output_to_operand_aliasing={{0}: (13, {}), {1}: (14, {})} | custom-call | flops 1006632960 | bytes 6291456 | tf_op jit(solution)/shard_map/stage/pallas_call | solution.py:361
  41.6 0.0 copy-start
  41.6 3.9 %stage.7 = (f32[256,1408]{1,0:T(8,128)S(1)}, f32[128,256]{1,0:T(8,128)S(1)}) custom-call(s32[1]{0:T(128)} %bitcast.me_ref, bf16[1488,128]{1,0:T(8,128)(2,1)S(1)} %collective-permute-done.2.refs_0_.refs_10_, bf16[1488,128]{1,0:T(8,128)(2,1)S(1)} %collective-permute-done.10.refs_1_.refs_11_, ...), custom_call_target="tpu_custom_call", output_to_operand_aliasing={{0}: (13, {}), {1}: (14, {})} | custom-call | flops 1006632960 | bytes 6291456 | tf_op jit(solution)/shard_map/stage/pallas_call | solution.py:361
  45.5 4.1 %features.1.unit_ref = bf16[128,128]{1,0:T(8,128)(2,1)S(1)} custom-call(s32[1]{0:T(128)} %bitcast.me_ref, s32[1,2]{1,0:T(1,128)S(1)} %copy-done, bf16[1488,128]{1,0:T(8,128)(2,1)S(1)} %collective-permute-done.3.refs_1_.refs_14_, bf16[1488,128]{1,0:T(8,128)(2,1)S(1)} %collective-permute-done.4.refs_2_.refs_15_, bf16[256,5120]{1,0:T(8,128)(2,1)} %refs_3_.5, ...), custom_call_target="tpu_custom_call" | custom-call | flops 503316480 | bytes 3145728 | tf_op jit(solution)/shard_map/features/pallas_call | solution.py:361
  49.7 1.7 %scores.1 = (f32[2,3]{1,0:T(2,128)}, f32[2]{0:T(128)}) custom-call(bf16[128,128]{1,0:T(8,128)(2,1)S(1)} %features.1.unit_ref, bf16[1488,128]{1,0:T(8,128)(2,1)S(1)} %pack.1.refs_0_, bf16[1488,128]{1,0:T(8,128)(2,1)S(1)} %collective-permute-done.5.refs_1_, bf16[1488,128]{1,0:T(8,128)(2,1)S(1)} %collective-permute-done.refs_0_.refs_2_, ...), custom_call_target="tpu_custom_call" | custom-call | flops 4194304 | bytes 2097152 | tf_op jit(solution)/shard_map/scores/pallas_call | solution.py:411
  (7 shorter events, 0.0 us)
Async XLA Ops:
  2.1 3.2 %collective-permute-start.5 = (bf16[1488,128]{1,0:T(8,128)(2,1)S(1)}, bf16[1488,128]{1,0:T(8,128)(2,1)S(1)}, u32[]{:S(2)}, u32[]{:S(2)}) collective-permute-start(bf16[1488,128]{1,0:T(8,128)(2,1)S(1)} %pack.1.refs_0_), channel_id=1, source_target_pairs={{0,1},{1,0},{2,3},{3,2},{4,5},{5,4},{6,7},{7,6},{8,9},{9,8},{10,11... | collective-permute-start | bytes 1142792 | tf_op jit(solution)/shard_map/ppermute | solution.py:52
  2.6 8.2 %collective-permute-start = (bf16[1488,128]{1,0:T(8,128)(2,1)S(1)}, bf16[1488,128]{1,0:T(8,128)(2,1)S(1)}, u32[]{:S(2)}, u32[]{:S(2)}) collective-permute-start(bf16[1488,128]{1,0:T(8,128)(2,1)S(1)} %pack.1.refs_0_), channel_id=1, source_target_pairs={{0,4},{1,3},{4,8},{5,1},{8,12},{9,5},{12,14},{13,9},{14,10},{15,13... | collective-permute-start | bytes 1142792 | tf_op jit(solution)/shard_map/ppermute | solution.py:48
  5.2 9.6 %collective-permute-start.6 = (bf16[1488,128]{1,0:T(8,128)(2,1)S(1)}, bf16[1488,128]{1,0:T(8,128)(2,1)S(1)}, u32[]{:S(2)}, u32[]{:S(2)}) collective-permute-start(bf16[1488,128]{1,0:T(8,128)(2,1)S(1)} %collective-permute-done.5.refs_1_), channel_id=1, source_target_pairs={{0,4},{1,3},{4,8},{5,1},{8,12},{9,5},{12,14},{13,9},{14,10},{15,13... | collective-permute-start | bytes 1142792 | tf_op jit(solution)/shard_map/ppermute | solution.py:48
  10.8 9.1 %collective-permute-start.1 = (bf16[1488,128]{1,0:T(8,128)(2,1)S(1)}, bf16[1488,128]{1,0:T(8,128)(2,1)S(1)}, u32[]{:S(2)}, u32[]{:S(2)}) collective-permute-start(bf16[1488,128]{1,0:T(8,128)(2,1)S(1)} %collective-permute-done.refs_0_.refs_2_), channel_id=1, source_target_pairs={{0,4},{1,3},{4,8},{5,1},{8,12},{9,5},{12,14},{13,9},{14,10},{15,13... | collective-permute-start | bytes 1142792 | tf_op jit(solution)/shard_map/ppermute | solution.py:48
  12.9 8.6 %collective-permute-start.8 = (bf16[1488,128]{1,0:T(8,128)(2,1)S(1)}, bf16[1488,128]{1,0:T(8,128)(2,1)S(1)}, u32[]{:S(2)}, u32[]{:S(2)}) collective-permute-start(bf16[1488,128]{1,0:T(8,128)(2,1)S(1)} %collective-permute-done.refs_0_.refs_2_), channel_id=1, source_target_pairs={{0,1},{1,0},{2,3},{3,2},{4,5},{5,4},{6,7},{7,6},{8,9},{9,8},{10,11... | collective-permute-start | bytes 1142792 | tf_op jit(solution)/shard_map/ppermute | solution.py:52
  14.9 6.6 %collective-permute-start.9 = (bf16[1488,128]{1,0:T(8,128)(2,1)S(1)}, bf16[1488,128]{1,0:T(8,128)(2,1)S(1)}, u32[]{:S(2)}, u32[]{:S(2)}) collective-permute-start(bf16[1488,128]{1,0:T(8,128)(2,1)S(1)} %collective-permute-done.6.refs_1_.refs_3_), channel_id=1, source_target_pairs={{0,1},{1,0},{2,3},{3,2},{4,5},{5,4},{6,7},{7,6},{8,9},{9,8},{10,11... | collective-permute-start | bytes 1142792 | tf_op jit(solution)/shard_map/ppermute | solution.py:52
  17.7 7.7 %collective-permute-start.7 = (bf16[1488,128]{1,0:T(8,128)(2,1)S(1)}, bf16[1488,128]{1,0:T(8,128)(2,1)S(1)}, u32[]{:S(2)}, u32[]{:S(2)}) collective-permute-start(bf16[1488,128]{1,0:T(8,128)(2,1)S(1)} %collective-permute-done.6.refs_1_.refs_3_), channel_id=1, source_target_pairs={{0,4},{1,3},{4,8},{5,1},{8,12},{9,5},{12,14},{13,9},{14,10},{15,13... | collective-permute-start | bytes 1142792 | tf_op jit(solution)/shard_map/ppermute | solution.py:48
  19.9 9.6 %collective-permute-start.2 = (bf16[1488,128]{1,0:T(8,128)(2,1)S(1)}, bf16[1488,128]{1,0:T(8,128)(2,1)S(1)}, u32[]{:S(2)}, u32[]{:S(2)}) collective-permute-start(bf16[1488,128]{1,0:T(8,128)(2,1)S(1)} %collective-permute-done.1.refs_0_.refs_6_), channel_id=1, source_target_pairs={{0,4},{1,3},{4,8},{5,1},{8,12},{9,5},{12,14},{13,9},{14,10},{15,13... | collective-permute-start | bytes 1142792 | tf_op jit(solution)/shard_map/ppermute | solution.py:48
  25.4 8.2 %collective-permute-start.10 = (bf16[1488,128]{1,0:T(8,128)(2,1)S(1)}, bf16[1488,128]{1,0:T(8,128)(2,1)S(1)}, u32[]{:S(2)}, u32[]{:S(2)}) collective-permute-start(bf16[1488,128]{1,0:T(8,128)(2,1)S(1)} %collective-permute-done.7.refs_1_.refs_7_), channel_id=1, source_target_pairs={{0,4},{1,3},{4,8},{5,1},{8,12},{9,5},{12,14},{13,9},{14,10},{15,13... | collective-permute-start | bytes 1142792 | tf_op jit(solution)/shard_map/ppermute | solution.py:48
  29.5 8.2 %collective-permute-start.3 = (bf16[1488,128]{1,0:T(8,128)(2,1)S(1)}, bf16[1488,128]{1,0:T(8,128)(2,1)S(1)}, u32[]{:S(2)}, u32[]{:S(2)}) collective-permute-start(bf16[1488,128]{1,0:T(8,128)(2,1)S(1)} %collective-permute-done.2.refs_0_.refs_10_), channel_id=1, source_target_pairs={{0,4},{1,3},{4,8},{5,1},{8,12},{9,5},{12,14},{13,9},{14,10},{15,13... | collective-permute-start | bytes 1142792 | tf_op jit(solution)/shard_map/ppermute | solution.py:48
  31.6 6.1 %collective-permute-start.13 = (bf16[1488,128]{1,0:T(8,128)(2,1)S(1)}, bf16[1488,128]{1,0:T(8,128)(2,1)S(1)}, u32[]{:S(2)}, u32[]{:S(2)}) collective-permute-start(bf16[1488,128]{1,0:T(8,128)(2,1)S(1)} %collective-permute-done.1.refs_0_.refs_6_), channel_id=1, source_target_pairs={{0,1},{1,0},{2,3},{3,2},{4,5},{5,4},{6,7},{7,6},{8,9},{9,8},{10,11... | collective-permute-start | bytes 1142792 | tf_op jit(solution)/shard_map/ppermute | solution.py:52
  31.6 6.1 %collective-permute-start.14 = (bf16[1488,128]{1,0:T(8,128)(2,1)S(1)}, bf16[1488,128]{1,0:T(8,128)(2,1)S(1)}, u32[]{:S(2)}, u32[]{:S(2)}) collective-permute-start(bf16[1488,128]{1,0:T(8,128)(2,1)S(1)} %collective-permute-done.7.refs_1_.refs_7_), channel_id=1, source_target_pairs={{0,1},{1,0},{2,3},{3,2},{4,5},{5,4},{6,7},{7,6},{8,9},{9,8},{10,11... | collective-permute-start | bytes 1142792 | tf_op jit(solution)/shard_map/ppermute | solution.py:52
  32.1 9.5 %collective-permute-start.11 = (bf16[1488,128]{1,0:T(8,128)(2,1)S(1)}, bf16[1488,128]{1,0:T(8,128)(2,1)S(1)}, u32[]{:S(2)}, u32[]{:S(2)}) collective-permute-start(bf16[1488,128]{1,0:T(8,128)(2,1)S(1)} %collective-permute-done.2.refs_0_.refs_10_), channel_id=1, source_target_pairs={{0,1},{1,0},{2,3},{3,2},{4,5},{5,4},{6,7},{7,6},{8,9},{9,8},{10,11... | collective-permute-start | bytes 1142792 | tf_op jit(solution)/shard_map/ppermute | solution.py:52
  33.6 8.0 %collective-permute-start.12 = (bf16[1488,128]{1,0:T(8,128)(2,1)S(1)}, bf16[1488,128]{1,0:T(8,128)(2,1)S(1)}, u32[]{:S(2)}, u32[]{:S(2)}) collective-permute-start(bf16[1488,128]{1,0:T(8,128)(2,1)S(1)} %collective-permute-done.10.refs_1_.refs_11_), channel_id=1, source_target_pairs={{0,1},{1,0},{2,3},{3,2},{4,5},{5,4},{6,7},{7,6},{8,9},{9,8},{10,11... | collective-permute-start | bytes 1142792 | tf_op jit(solution)/shard_map/ppermute | solution.py:52
  37.7 7.8 %collective-permute-start.4 = (bf16[1488,128]{1,0:T(8,128)(2,1)S(1)}, bf16[1488,128]{1,0:T(8,128)(2,1)S(1)}, u32[]{:S(2)}, u32[]{:S(2)}) collective-permute-start(bf16[1488,128]{1,0:T(8,128)(2,1)S(1)} %collective-permute-done.3.refs_1_.refs_14_), channel_id=1, source_target_pairs={{0,1},{1,0},{2,3},{3,2},{4,5},{5,4},{6,7},{7,6},{8,9},{9,8},{10,11... | collective-permute-start | bytes 1142792 | tf_op jit(solution)/shard_map/ppermute | solution.py:52
  41.6 3.9 %copy-start = (s32[1,2]{1,0:T(1,128)S(1)}, s32[1,2]{1,0:T(1,128)}, u32[]{:S(2)}) copy-start(s32[1,2]{1,0:T(1,128)} %refs_0_.1) | copy-start | bytes 28

commit v5 on v4

--- a/solution.py
+++ b/solution.py
@@ -13,6 +13,9 @@
 BF16 = jnp.bfloat16
 RING_CHIPS = 8
 LANES = 128
+STEPS = 4
+X_DOWN, X_LOW, J_LOW, M_DOWN, VALUES, SUMS = range(6)
+X_SOURCE, X_TARGET, SQUARES, M_SOURCE, J_TARGET, V_TARGET, LOCAL_SUMS = range(7)
 MIB = 1 << 20
 
 
@@ -107,128 +110,125 @@
         out_ref[pl.ds(at + i * count, 2 * count), :] = pair.astype(BF16)
 
 
-X_LOW, X_DOWN, X_SOURCE, SQUARES, J_LOW, M_DOWN, M_SOURCE, VALUES, SUMS = 0, 2, 3, 4, 5, 7, 8, 9, 11
-
-
-def stage_kernel(aways, first, last, me_ref, *refs):
+def local_kernel(*refs):
+    x_hbm, mixed_hbm, adjoint_hbm, values_hbm, target_hbm, gain_hbm, source_hbm, top_target_hbm = refs[:8]
+    x_ref, mixed_ref, adjoint_ref, values_ref, target_ref, sums_ref = refs[8:14]
+    gain_ref, source_ref, top_target_ref, sems = refs[14:]
+    width, value_width = x_ref.shape[1], values_ref.shape[1]
+    span, value_span = width // STEPS, value_width // STEPS
+    copies = []
+    for j in range(STEPS):
+        part, value_part = pl.ds(j * span, span), pl.ds(j * value_span, value_span)
+        pairs = (
+            (gain_hbm.at[:, part], gain_ref.at[:, part]),
+            (source_hbm.at[:, part], source_ref.at[:, part]),
+            (x_hbm.at[:, part], x_ref.at[:, part]),
+            (target_hbm.at[part], target_ref.at[part]),
+            (mixed_hbm.at[:, part], mixed_ref.at[:, part]),
+            (adjoint_hbm.at[:, part], adjoint_ref.at[:, part]),
+            (values_hbm.at[:, value_part], values_ref.at[:, value_part]),
+            (top_target_hbm.at[value_part], top_target_ref.at[value_part]),
+        )
+        copies.append(load(pairs, sems.at[j]))
+    total = [None] * LOCAL_SUMS
+
+    def add(column, value):
+        total[column] = value if total[column] is None else total[column] + value
+
+    for j in range(STEPS):
+        for copy in copies[j]:
+            copy.wait()
+        part, value_part = slice(j * span, (j + 1) * span), slice(j * value_span, (j + 1) * value_span)
+        x, target, source = x_ref[:, part], target_ref[part, :], source_ref[:, part]
+        gained = (source.astype(F32) * gain_ref[:, part]).astype(BF16)
+        add(X_SOURCE, mm_rows(x, jnp.concatenate([gained, gained], axis=0)))
+        add(X_TARGET, mm(x, target))
+        for i in range(span // LANES):
+            wide = x[:, i * LANES : (i + 1) * LANES].astype(F32)
+            add(SQUARES, wide * wide)
+        add(M_SOURCE, mm_rows(mixed_ref[:, part], jnp.concatenate([source, source], axis=0)))
+        add(J_TARGET, mm(adjoint_ref[:, part], target))
+        add(V_TARGET, mm(values_ref[:, value_part], top_target_ref[value_part, :]))
+    for i in range(LOCAL_SUMS):
+        sums_ref[:, i * LANES : (i + 1) * LANES] = total[i]
+
+
+def stage_kernel(away, first, last, me_ref, *refs):
     refs = list(refs)
     take = lambda k: [refs.pop(0) for _ in range(k)]
     counts_ref = take(1)[0] if last else None
-    pieces = take(2 * len(aways))
-    x_hbm, mixed_hbm, adjoint_hbm, values_hbm, gain_hbm, source_hbm, target_hbm, top_target_hbm = take(8)
+    pieces = take(2)
+    x_ref, mixed_ref, adjoint_ref, values_ref, target_ref = take(5)
     old_sums, old_bridge = (None, None) if first else take(2)
-    expand_hbm, sketch_hbm = take(2) if last else (None, None)
+    local_ref, expand_hbm, sketch_hbm = take(3) if last else (None, None, None)
     if last:
         (out_ref,) = take(1)
     else:
         new_sums, new_bridge = take(2)
-    xs, ms, js, vs, gains, sources, low, down, up, packed, expand_ref, sketch_ref, sems = refs
-    rows = down.shape[1] // 2
-    half = rows // 2
-    tokens, span = xs.shape[1:]
-    pad = LANES // 2
+    both, up, down, expand_ref, sketch_ref, sems = refs
+    rows = both.shape[0] // 2
+    half, pad = rows // 2, LANES // 2
+    tokens, width = x_ref.shape
+    span = 2 * rows
+    if last:
+        more = load(((expand_hbm, expand_ref), (sketch_hbm, sketch_ref)), sems)
+
     me = me_ref[0]
     pos, core = ring_pos(me // 2), me % 2
-
-    copies = []
-    for k, away in enumerate(aways):
-        chip = ring_chip((pos + away * (2 * core - 1) + RING_CHIPS) % RING_CHIPS)
-        odd = chip % 2
-        mine = pl.ds(pl.multiple_of(chip * span, LANES), span)
-        values_start = (chip // 2) * span + odd * (span // 2 - pad)
-        values_window = pl.ds(pl.multiple_of(values_start, LANES), vs.shape[2])
-        shift = odd * pad
-        up[k, pl.ds(pl.multiple_of((1 - odd) * rows, 16), pad), :] = jnp.zeros((pad, 2 * LANES), BF16)
-        pairs = []
-        side = core if away >= 0 else 1 - core
-        for piece, c in ((pieces[2 * k], side), (pieces[2 * k + 1], 1 - side)):
-            one = pl.ds(pl.multiple_of(c * rows, 16), rows)
-            part = pl.ds(pl.multiple_of(c * half, 16), half)
-            up_part = pl.ds(pl.multiple_of(shift + c * half, 16), half)
-            pairs += [
-                (piece.at[pl.ds(0, rows)], down.at[k, one]),
-                (piece.at[pl.ds(rows, rows)], low.at[k, one, pl.ds(0, LANES)]),
-                (piece.at[pl.ds(2 * rows, half)], up.at[k, up_part, pl.ds(0, LANES)]),
-                (piece.at[pl.ds(2 * rows + half, half)], packed.at[k, part]),
-            ]
-        pairs += [
-            (target_hbm.at[mine], low.at[k, :, pl.ds(LANES, LANES)]),
-            (
-                top_target_hbm.at[pl.ds(pl.multiple_of(chip * rows, 16), rows)],
-                up.at[k, pl.ds(pl.multiple_of(shift, 16), rows), pl.ds(LANES, LANES)],
-            ),
-            (source_hbm.at[:, mine], sources.at[k]),
-            (gain_hbm.at[:, mine], gains.at[k]),
-            (x_hbm.at[:, mine], xs.at[k]),
-            (adjoint_hbm.at[:, mine], js.at[k]),
-            (mixed_hbm.at[:, mine], ms.at[k]),
-            (values_hbm.at[:, values_window], vs.at[k]),
-        ]
-        copies.append(load(pairs, sems.at[k]))
-    if last:
-        more = load(((expand_hbm, expand_ref), (sketch_hbm, sketch_ref)), sems.at[len(aways)])
-
-    total = [None if first else old_sums[:, i * LANES : (i + 1) * LANES] for i in range(SUMS)]
-    bridged = None if first else old_bridge[...]
-
-    def add(column, value):
-        for i in range(value.shape[1] // LANES):
-            part = value[:, i * LANES : (i + 1) * LANES]
-            total[column + i] = part if total[column + i] is None else total[column + i] + part
-
-    for k in range(len(aways)):
-        for copy in copies[k]:
-            copy.wait()
-        x, mixed = xs[k], ms[k]
-        add(X_LOW, mm(x, low[k]))
-        add(X_DOWN, mm(x, down[k]))
-        source = sources[k]
-        gained = (source.astype(F32) * gains[k]).astype(BF16)
-        add(X_SOURCE, mm_rows(x, jnp.concatenate([gained, gained], axis=0)))
-        square = jnp.zeros((tokens, LANES), F32)
-        for i in range(span // LANES):
-            wide = x[:, i * LANES : (i + 1) * LANES].astype(F32)
-            square = square + wide * wide
-        add(SQUARES, square)
-        add(J_LOW, mm(js[k], low[k]))
-        unpacked = []
-        for c in range(2):
-            both = packed[k, pl.ds(c * half, half), :].astype(F32)
-            turned = pltpu.roll(both, LANES // 2, 1)
-            lower = half_lanes(both.shape)
-            unpacked += [jnp.where(lower, both, turned), jnp.where(lower, turned, both)]
-        add(M_DOWN, mm(mixed, jnp.concatenate(unpacked, axis=0).astype(BF16)))
-        add(M_SOURCE, mm_rows(mixed, jnp.concatenate([source, source], axis=0)))
-        add(VALUES, mm(vs[k], up[k]))
-        product = mm_cols(down[k], low[k])
-        bridged = product if bridged is None else bridged + product
-
+    chip = ring_chip((pos + away * (2 * core - 1) + RING_CHIPS) % RING_CHIPS)
+    odd = chip % 2
+    mine = pl.ds(pl.multiple_of(chip * span, LANES), span)
+    values_start = (chip // 2) * span + odd * (rows - pad)
+    values_part = pl.ds(pl.multiple_of(values_start, LANES), rows + pad)
+    side = core if away >= 0 else 1 - core
+    up[pl.ds(pl.multiple_of((1 - odd) * rows, 16), pad), :] = jnp.zeros((pad, LANES), BF16)
+    for piece, c in ((pieces[0], side), (pieces[1], 1 - side)):
+        one = pl.ds(pl.multiple_of(c * rows, 16), rows)
+        both[one, pl.ds(0, LANES)] = piece[pl.ds(0, rows), :]
+        both[one, pl.ds(LANES, LANES)] = piece[pl.ds(rows, rows), :]
+        up[pl.ds(pl.multiple_of(odd * pad + c * half, 16), half), :] = piece[pl.ds(2 * rows, half), :]
+        packed = piece[pl.ds(2 * rows + half, half), :].astype(F32)
+        turned = pltpu.roll(packed, pad, 1)
+        lower = half_lanes(packed.shape)
+        down[pl.ds(pl.multiple_of(c * rows, 16), half), :] = jnp.where(lower, packed, turned).astype(BF16)
+        down[pl.ds(pl.multiple_of(c * rows + half, 16), half), :] = jnp.where(lower, turned, packed).astype(BF16)
+
+    weights = both[...]
+    products = [None] * SUMS
+    x_both = mm(x_ref[:, mine], weights)
+    products[X_DOWN], products[X_LOW] = x_both[:, :LANES], x_both[:, LANES:]
+    products[J_LOW] = mm(adjoint_ref[:, mine], weights[:, LANES:])
+    products[M_DOWN] = mm(mixed_ref[:, mine], down[...])
+    products[VALUES] = mm(values_ref[:, values_part], up[...])
+    bridge = mm_cols(
+        weights[:, :LANES], jnp.concatenate([weights[:, LANES:], target_ref[mine, :]], axis=1)
+    )
+    if not first:
+        products = [p + old_sums[:, i * LANES : (i + 1) * LANES] for i, p in enumerate(products)]
+        bridge = bridge + old_bridge[...]
     if not last:
         for i in range(SUMS):
-            new_sums[:, i * LANES : (i + 1) * LANES] = total[i]
-        new_bridge[...] = bridged
+            new_sums[:, i * LANES : (i + 1) * LANES] = products[i]
+        new_bridge[...] = bridge
         return
 
     for copy in more:
         copy.wait()
-    width = x_hbm.shape[1]
-    mean = jnp.sum(total[SQUARES], axis=1, keepdims=True) * (1.0 / width)
+    local = [local_ref[:, i * LANES : (i + 1) * LANES] for i in range(LOCAL_SUMS)]
+    mean = jnp.sum(local[SQUARES], axis=1, keepdims=True) * (1.0 / width)
     inverse = lax.rsqrt(mean + 1e-05)
-    reduced = inverse * total[X_DOWN]
+    reduced = inverse * products[X_DOWN]
     expand = expand_ref[...]
     left_two = mm_rows(reduced.astype(BF16), jnp.concatenate([expand, expand], axis=0))
-    returned = total[VALUES].astype(BF16)
+    returned = products[VALUES].astype(BF16)
     right_one = ALPHA * mm(returned, sketch_ref[...])
     along = (ALPHA / width) * jnp.sum(returned.astype(F32) * reduced, axis=1, keepdims=True)
-    back = mm(returned, bridged.astype(BF16))
+    back = mm(returned, bridge.astype(BF16))
     along = along * inverse
-    lows = [
-        total[J_LOW + i]
-        + inverse * (ALPHA * back[:, i * LANES : (i + 1) * LANES] - along * total[X_LOW + i])
-        for i in range(2)
-    ]
-    rights = (right_one, ALPHA * total[VALUES + 1], ALPHA * lows[0], ALPHA * lows[1])
-    lefts = (inverse * total[X_SOURCE], left_two, total[M_SOURCE], total[M_DOWN])
+    right_three = products[J_LOW] + inverse * (ALPHA * back[:, :LANES] - along * products[X_LOW])
+    right_four = local[J_TARGET] + inverse * (ALPHA * back[:, LANES:] - along * local[X_TARGET])
+    rights = (right_one, ALPHA * local[V_TARGET], ALPHA * right_three, ALPHA * right_four)
+    lefts = (inverse * local[X_SOURCE], left_two, local[M_SOURCE], products[M_DOWN])
     place = lax.broadcasted_iota(jnp.int32, (tokens, LANES), 0)
     one, two = counts_ref[0, 0], counts_ref[0, 1]
     lower = half_lanes((tokens, LANES))
@@ -340,73 +340,82 @@
         name="pack",
     )(me.reshape(1), *in_hbm(inputs))
 
-    span = 2 * rows
-    activations = (
+    inputs = (
         x,
         mixed,
         adjoint,
         values,
+        bottom_target_sketch,
         top_rmsnorm_weights.reshape(1, width),
         source_sketch.T,
-        bottom_target_sketch,
         top_target_sketch,
     )
-
-    def stage(aways, pieces, sums=(), last=False):
-        first, n = not sums, len(aways)
+    *activations, local = pl.pallas_call(
+        local_kernel,
+        out_shape=[jax.ShapeDtypeStruct(a.shape, a.dtype) for a in inputs[:5]]
+        + [jax.ShapeDtypeStruct((tokens, LOCAL_SUMS * LANES), F32)],
+        in_specs=[HBM] * len(inputs),
+        out_specs=[VMEM] * 6,
+        scratch_shapes=[pltpu.VMEM(a.shape, a.dtype) for a in inputs[5:]]
+        + [pltpu.SemaphoreType.DMA((STEPS, len(inputs)))],
+        compiler_params=params(24),
+        cost_estimate=cost(tokens * width * LANES * 12, 14 * MIB),
+        name="local_products",
+    )(*in_hbm(inputs))
+
+    def stage(away, pieces, sums, local=None):
+        first, last = not sums, local is not None
         sums_shape, bridge_shape = (tokens, SUMS * LANES), (LANES, 2 * LANES)
         small = (top_expander_sketch.T, top_reducer_sketch)
         head = [me.reshape(1)] + ([sequence_token_counts] if last else [])
         start = len(head) + len(pieces) + len(activations)
         return pl.pallas_call(
-            functools.partial(stage_kernel, aways, first, last),
+            functools.partial(stage_kernel, away, first, last),
             out_shape=jax.ShapeDtypeStruct((LANES, LANES), BF16)
             if last
-            else (jax.ShapeDtypeStruct(sums_shape, F32), jax.ShapeDtypeStruct(bridge_shape, F32)),
+            else [jax.ShapeDtypeStruct(sums_shape, F32), jax.ShapeDtypeStruct(bridge_shape, F32)],
             in_specs=[SMEM] * len(head)
-            + [ANY] * len(pieces)
-            + [HBM] * len(activations)
-            + [VMEM] * len(sums)
-            + ([HBM] * 2 if last else []),
-            out_specs=VMEM if last else (VMEM, VMEM),
+            + [VMEM] * (len(pieces) + len(activations) + len(sums))
+            + ([VMEM, HBM, HBM] if last else []),
+            out_specs=VMEM if last else [VMEM, VMEM],
             scratch_shapes=[
-                pltpu.VMEM((n, tokens, span), BF16),
-                pltpu.VMEM((n, tokens, span), BF16),
-                pltpu.VMEM((n, tokens, span), BF16),
-                pltpu.VMEM((n, tokens, rows + LANES // 2), BF16),
-                pltpu.VMEM((n, 1, span), F32),
-                pltpu.VMEM((n, LANES // 2, span), BF16),
-                pltpu.VMEM((n, span, 2 * LANES), BF16),
-                pltpu.VMEM((n, span, LANES), BF16),
-                pltpu.VMEM((n, rows + LANES // 2, 2 * LANES), BF16),
-                pltpu.VMEM((n, rows, LANES), BF16),
+                pltpu.VMEM((2 * rows, 2 * LANES), BF16),
+                pltpu.VMEM((rows + LANES // 2, LANES), BF16),
+                pltpu.VMEM((2 * rows, LANES), BF16),
                 pltpu.VMEM(small[0].shape, BF16),
                 pltpu.VMEM(small[1].shape, BF16),
-                pltpu.SemaphoreType.DMA((n + 1, 16)),
+                pltpu.SemaphoreType.DMA((2,)),
             ],
             input_output_aliases={} if first or last else {start: 0, start + 1: 1},
             compiler_params=params(16),
-            cost_estimate=cost(n * tokens * span * LANES * 24, 3 * n * MIB),
+            cost_estimate=cost(tokens * rows * LANES * 16, 2 * MIB),
             name="features" if last else "stage",
-        )(*head, *pieces, *in_hbm(activations), *sums, *in_hbm(small if last else ()))
+        )(*head, *pieces, *activations, *sums, *((local, *in_hbm(small)) if last else ()))
 
     tie = lax.optimization_barrier
     half = RING_CHIPS // 2
     first, second = own, other_core(own)
-    held, aways, sums = [first, second], (0,), ()
-    blocks = list(held)
-    for k in range(1, half + 1):
+    blocks = [first, second]
+    held = [first, second]
+    first, second = hop(first), hop(second)
+    first, activations = tie((first, activations))
+    sums = stage(0, held, [])
+    second, sums = tie((second, sums))
+    for k in range(1, half):
+        held = [first, second]
+        crossed = [other_core(first), other_core(second)]
+        blocks += held + crossed
         first = hop(first)
-        if k == half:
-            held, aways, sums = [first, other_core(first)], (half,), stage(aways, held, sums)
-        else:
+        sums = stage(k, held, sums)
+        first, sums = tie((first, sums))
+        if k < half - 1:
             second = hop(second)
-            old, held = held, [first, second, other_core(first), other_core(second)]
-            sums = stage(aways, old, sums)
+        sums = stage(-k, crossed, sums)
+        if k < half - 1:
             second, sums = tie((second, sums))
-            aways = (k, -k)
-        blocks += held
-    unit = stage(aways, held, sums, last=True)
+    held = [first, other_core(first)]
+    blocks += held
+    unit = stage(half, held, sums, local)
 
     task_best, scores = pl.pallas_call(
         functools.partial(score_kernel, len(blocks), count, 3 * rows),

time: 51.6 us -> 43.8 us (0.85)
  Pallas kernels: 21.7 us -> 17.3 us
  starting transfers between devices: 15.2 us -> 13.3 us
  waiting for transfers between devices: 13.7 us -> 12 us
    pallas_call x5 -> x9, Pallas kernels: 18.6 us -> 14.2 us  [the longest x8 7.56 us: stage(): pl.pallas_call(functools.partial(stage_kernel, away, first, last), out_sh...]
    ppermute x7, waiting for transfers between devices: 13.7 us -> 11 us  [hop(): return lax.ppermute(value, 'dp', pairs)]
    ppermute x7, starting transfers between devices: 14.2 us -> 12.2 us  [hop(): return lax.ppermute(value, 'dp', pairs)]
    ppermute x8, waiting for transfers between devices: 0.02 us -> 0.94 us  [other_core(): lax.ppermute(value, 'dp', [(d, d ^ 1) for d in range(2 * RING_CHIPS)])]
  transfers between devices with their start and end apart: 15 -> 15, of which waited for: 6 -> 6; matrix products, arithmetic and copies ran while one was open for 0% -> 0% of each run, Pallas kernels for 28% -> 27%
where the time goes in v5:
time: 43.8 us; the launch traced here: 43.5 us
  Pallas kernels  17.3 us (39%)
  starting transfers between devices  13.3 us (30%)
  waiting for transfers between devices  12 us (27%)
  between operations  0.92 us (2%)
    ppermute x7, starting transfers between devices, hop(): return lax.ppermute(value, 'dp', pairs)  12.2 us
    ppermute x7, waiting for transfers between devices, hop(): return lax.ppermute(value, 'dp', pairs)  11 us
    pallas_call x8, Pallas kernels, stage(): pl.pallas_call(functools.partial(stage_kernel, away, first, last), out_sh...  7.56 us
    pallas_call x1, Pallas kernels, shards(): pl.pallas_call(local_kernel, out_shape=[jax.ShapeDtypeStruct(a.shape, a.d...  6.6 us
    pallas_call x1, Pallas kernels, shards(): pl.pallas_call(functools.partial(score_kernel, len(blocks), count, 3 * ro...  1.7 us
    pallas_call x1, Pallas kernels, shards(): pl.pallas_call(pack_kernel, out_shape=jax.ShapeDtypeStruct((3 * rows + (L...  1.41 us
    ppermute x8, starting transfers between devices, other_core(): lax.ppermute(value, 'dp', [(d, d ^ 1) for d in range(2 * RING_CHIPS)])  1.11 us
    ppermute x8, waiting for transfers between devices, other_core(): lax.ppermute(value, 'dp', [(d, d ^ 1) for d in range(2 * RING_CHIPS)])  0.94 us
  transfers between devices with their start and end apart: 15, of which 6 were waited for; matrix products, arithmetic and copies ran while one was open for 0% of the time, Pallas kernels for 27%

profile of v5, /device:TPU:0, one launch (start us, length us, event | category | flops | bytes accessed | tf_op | source)
XLA Modules:
  0.0 43.5 jit_solution(7608287752726805179)
XLA Ops:
  0.6 1.4 %pack.1.refs_0_ = bf16[1488,128]{1,0:T(8,128)(2,1)S(1)} custom-call(s32[1]{0:T(128)} %bitcast.me_ref, f32[40,128]{1,0:T(8,128)} %bitcast.10, bf16[320,128]{1,0:T(8,128)(2,1)} %refs_1_.2, bf16[320,128]{1,0:T(8,128)(2,1)} %bitcast.12, bf16[128,128]{1,0:T(8,128)(2,1)} %refs_3_.2, bf16[160,128]{1,0:T(8,128)(2,1)} %bitcast.13, bf16[320,128]{1,0:T(8,128)(2,1)} %refs_5_.1, ...), custom_call_target="tpu_custom_call" | custom-call | tf_op jit(solution)/shard_map/pack/pallas_call | solution.py:332
  2.1 0.5 %collective-permute-start.2 = (bf16[1488,128]{1,0:T(8,128)(2,1)S(1)}, bf16[1488,128]{1,0:T(8,128)(2,1)S(1)}, u32[]{:S(2)}, u32[]{:S(2)}) collective-permute-start(bf16[1488,128]{1,0:T(8,128)(2,1)S(1)} %pack.1.refs_0_), channel_id=1, source_target_pairs={{0,1},{1,0},{2,3},{3,2},{4,5},{5,4},{6,7},{7,6},{8,9},{9,8},{10,11... | collective-permute-start | bytes 1142792 | tf_op jit(solution)/shard_map/ppermute | solution.py:55
  2.6 2.6 %collective-permute-start = (bf16[1488,128]{1,0:T(8,128)(2,1)S(1)}, bf16[1488,128]{1,0:T(8,128)(2,1)S(1)}, u32[]{:S(2)}, u32[]{:S(2)}) collective-permute-start(bf16[1488,128]{1,0:T(8,128)(2,1)S(1)} %pack.1.refs_0_), channel_id=1, source_target_pairs={{0,4},{1,3},{4,8},{5,1},{8,12},{9,5},{12,14},{13,9},{14,10},{15,13... | collective-permute-start | bytes 1142792 | tf_op jit(solution)/shard_map/ppermute | solution.py:51
  5.2 1.6 %collective-permute-start.3 = (bf16[1488,128]{1,0:T(8,128)(2,1)S(1)}, bf16[1488,128]{1,0:T(8,128)(2,1)S(1)}, u32[]{:S(2)}, u32[]{:S(2)}) collective-permute-start(bf16[1488,128]{1,0:T(8,128)(2,1)S(1)} %collective-permute-done.2.refs_1_), channel_id=1, source_target_pairs={{0,4},{1,3},{4,8},{5,1},{8,12},{9,5},{12,14},{13,9},{14,10},{15,13... | collective-permute-start | bytes 1142792 | tf_op jit(solution)/shard_map/ppermute | solution.py:51
  6.8 6.6 %local_products.1 = (bf16[256,5120]{1,0:T(8,128)(2,1)S(1)}, bf16[256,5120]{1,0:T(8,128)(2,1)S(1)}, bf16[256,5120]{1,0:T(8,128)(2,1)S(1)}, bf16[256,2560]{1,0:T(8...) custom-call(bf16[256,5120]{1,0:T(8,128)(2,1)} %refs_0_.2, bf16[256,5120]{1,0:T(8,128)(2,1)} %refs_1_.3, ...), custom_call_target="tpu_custom_call" | custom-call | flops 2013265920 | bytes 14680064 | tf_op jit(solution)/shard_map/local_products/pallas_call | solution.py:353
  13.5 0.0 collective-permute-done.refs_0_.refs_2_
  13.5 1.6 %collective-permute-start.1 = (bf16[1488,128]{1,0:T(8,128)(2,1)S(1)}, bf16[1488,128]{1,0:T(8,128)(2,1)S(1)}, u32[]{:S(2)}, u32[]{:S(2)}) collective-permute-start(bf16[1488,128]{1,0:T(8,128)(2,1)S(1)} %collective-permute-done.refs_0_.refs_2_), channel_id=1, source_target_pairs={{0,4},{1,3},{4,8},{5,1},{8,12},{9,5},{12,14},{13,9},{14,10},{15,13... | collective-permute-start | bytes 1142792 | tf_op jit(solution)/shard_map/ppermute | solution.py:51
  15.1 0.6 %stage.7 = (f32[256,640]{1,0:T(8,128)S(1)}, f32[128,256]{1,0:T(8,128)S(1)}) custom-call(s32[1]{0:T(128)} %bitcast.me_ref, bf16[1488,128]{1,0:T(8,128)(2,1)S(1)} %pack.1.refs_0_, bf16[1488,128]{1,0:T(8,128)(2,1)S(1)} %collective-permute-done.2.refs_1_, bf16[256,5120]{1,0:T(8,128)(2,1)S(1)} %get-tuple-element.54.refs_2_.refs_3_, ...), custom_call_target="tpu_custom_call" | custom-call | flops 167772160 | bytes 2097152 | tf_op jit(solution)/shard_map/stage/pallas_call | solution.py:372
  15.7 0.0 collective-permute-done.3.refs_1_.refs_3_
  15.8 0.6 %collective-permute-start.7 = (bf16[1488,128]{1,0:T(8,128)(2,1)S(1)}, bf16[1488,128]{1,0:T(8,128)(2,1)S(1)}, u32[]{:S(2)}, u32[]{:S(2)}) collective-permute-start(bf16[1488,128]{1,0:T(8,128)(2,1)S(1)} %collective-permute-done.3.refs_1_.refs_3_), channel_id=1, source_target_pairs={{0,1},{1,0},{2,3},{3,2},{4,5},{5,4},{6,7},{7,6},{8,9},{9,8},{10,11... | collective-permute-start | bytes 1142792 | tf_op jit(solution)/shard_map/ppermute | solution.py:55
  16.3 1.6 %collective-permute-start.5 = (bf16[1488,128]{1,0:T(8,128)(2,1)S(1)}, bf16[1488,128]{1,0:T(8,128)(2,1)S(1)}, u32[]{:S(2)}, u32[]{:S(2)}) collective-permute-start(bf16[1488,128]{1,0:T(8,128)(2,1)S(1)} %collective-permute-done.3.refs_1_.refs_3_), channel_id=1, source_target_pairs={{0,4},{1,3},{4,8},{5,1},{8,12},{9,5},{12,14},{13,9},{14,10},{15,13... | collective-permute-start | bytes 1142792 | tf_op jit(solution)/shard_map/ppermute | solution.py:51
  17.9 0.8 %stage.8 = (f32[256,640]{1,0:T(8,128)S(1)}, f32[128,256]{1,0:T(8,128)S(1)}) custom-call(s32[1]{0:T(128)} %bitcast.me_ref, bf16[1488,128]{1,0:T(8,128)(2,1)S(1)} %collective-permute-done.refs_0_.refs_2_, bf16[1488,128]{1,0:T(8,128)(2,1)S(1)} %collective-permute-done.3.refs_1_.refs_3_, ...), custom_call_target="tpu_custom_call", output_to_operand_aliasing={{0}: (8, {}), {1}: (9, {})} | custom-call | flops 167772160 | bytes 2097152 | tf_op jit(solution)/shard_map/stage/pallas_call | solution.py:372
  18.7 2.5 %collective-permute-done.1.refs_0_.refs_6_ = bf16[1488,128]{1,0:T(8,128)(2,1)S(1)} collective-permute-done((bf16[1488,128]{1,0:T(8,128)(2,1)S(1)}, bf16[1488,128]{1,0:T(8,128)(2,1)S(1)}, u32[]{:S(2)}, u32[]{:S(2)}) %collective-permute-start.1) | collective-permute-done | bytes 380960 | tf_op jit(solution)/shard_map/ppermute | solution.py:51
  21.2 1.6 %collective-permute-start.4 = (bf16[1488,128]{1,0:T(8,128)(2,1)S(1)}, bf16[1488,128]{1,0:T(8,128)(2,1)S(1)}, u32[]{:S(2)}, u32[]{:S(2)}) collective-permute-start(bf16[1488,128]{1,0:T(8,128)(2,1)S(1)} %collective-permute-done.1.refs_0_.refs_6_), channel_id=1, source_target_pairs={{0,4},{1,3},{4,8},{5,1},{8,12},{9,5},{12,14},{13,9},{14,10},{15,13... | collective-permute-start | bytes 1142792 | tf_op jit(solution)/shard_map/ppermute | solution.py:51
  22.7 0.0 collective-permute-start.10
  22.7 0.0 collective-permute-done.6.refs_0_.refs_4_
  22.8 0.0 collective-permute-done.7.refs_1_.refs_5_
  22.8 0.8 %stage.9 = (f32[256,640]{1,0:T(8,128)S(1)}, f32[128,256]{1,0:T(8,128)S(1)}) custom-call(s32[1]{0:T(128)} %bitcast.me_ref, bf16[1488,128]{1,0:T(8,128)(2,1)S(1)} %collective-permute-done.6.refs_0_.refs_4_, bf16[1488,128]{1,0:T(8,128)(2,1)S(1)} %collective-permute-done.7.refs_1_.refs_5_, ...), custom_call_target="tpu_custom_call", output_to_operand_aliasing={{0}: (8, {}), {1}: (9, {})} | custom-call | flops 167772160 | bytes 2097152 | tf_op jit(solution)/shard_map/stage/pallas_call | solution.py:372
  23.5 1.7 %collective-permute-done.5.refs_1_.refs_7_ = bf16[1488,128]{1,0:T(8,128)(2,1)S(1)} collective-permute-done((bf16[1488,128]{1,0:T(8,128)(2,1)S(1)}, bf16[1488,128]{1,0:T(8,128)(2,1)S(1)}, u32[]{:S(2)}, u32[]{:S(2)}) %collective-permute-start.5) | collective-permute-done | bytes 380960 | tf_op jit(solution)/shard_map/ppermute | solution.py:51
  25.2 0.0 collective-permute-start.11
  25.3 1.6 %collective-permute-start.9 = (bf16[1488,128]{1,0:T(8,128)(2,1)S(1)}, bf16[1488,128]{1,0:T(8,128)(2,1)S(1)}, u32[]{:S(2)}, u32[]{:S(2)}) collective-permute-start(bf16[1488,128]{1,0:T(8,128)(2,1)S(1)} %collective-permute-done.5.refs_1_.refs_7_), channel_id=1, source_target_pairs={{0,4},{1,3},{4,8},{5,1},{8,12},{9,5},{12,14},{13,9},{14,10},{15,13... | collective-permute-start | bytes 1142792 | tf_op jit(solution)/shard_map/ppermute | solution.py:51
  26.8 0.7 %stage.10 = (f32[256,640]{1,0:T(8,128)S(1)}, f32[128,256]{1,0:T(8,128)S(1)}) custom-call(s32[1]{0:T(128)} %bitcast.me_ref, bf16[1488,128]{1,0:T(8,128)(2,1)S(1)} %collective-permute-done.1.refs_0_.refs_6_, bf16[1488,128]{1,0:T(8,128)(2,1)S(1)} %collective-permute-done.5.refs_1_.refs_7_, ...), custom_call_target="tpu_custom_call", output_to_operand_aliasing={{0}: (8, {}), {1}: (9, {})} | custom-call | flops 167772160 | bytes 2097152 | tf_op jit(solution)/shard_map/stage/pallas_call | solution.py:372
  27.6 1.8 %collective-permute-done.4.refs_0_.refs_10_ = bf16[1488,128]{1,0:T(8,128)(2,1)S(1)} collective-permute-done((bf16[1488,128]{1,0:T(8,128)(2,1)S(1)}, bf16[1488,128]{1,0:T(8,128)(2,1)S(1)}, u32[]{:S(2)}, u32[]{:S(2)}) %collective-permute-start.4) | collective-permute-done | bytes 380960 | tf_op jit(solution)/shard_map/ppermute | solution.py:51
  29.3 1.6 %collective-permute-start.8 = (bf16[1488,128]{1,0:T(8,128)(2,1)S(1)}, bf16[1488,128]{1,0:T(8,128)(2,1)S(1)}, u32[]{:S(2)}, u32[]{:S(2)}) collective-permute-start(bf16[1488,128]{1,0:T(8,128)(2,1)S(1)} %collective-permute-done.4.refs_0_.refs_10_), channel_id=1, source_target_pairs={{0,4},{1,3},{4,8},{5,1},{8,12},{9,5},{12,14},{13,9},{14,10},{15,13... | collective-permute-start | bytes 1142792 | tf_op jit(solution)/shard_map/ppermute | solution.py:51
  30.9 0.8 %stage.11 = (f32[256,640]{1,0:T(8,128)S(1)}, f32[128,256]{1,0:T(8,128)S(1)}) custom-call(s32[1]{0:T(128)} %bitcast.me_ref, bf16[1488,128]{1,0:T(8,128)(2,1)S(1)} %collective-permute-done.10.refs_0_.refs_8_, bf16[1488,128]{1,0:T(8,128)(2,1)S(1)} %collective-permute-done.11.refs_1_.refs_9_, ...), custom_call_target="tpu_custom_call", output_to_operand_aliasing={{0}: (8, {}), {1}: (9, {})} | custom-call | flops 167772160 | bytes 2097152 | tf_op jit(solution)/shard_map/stage/pallas_call | solution.py:372
  31.7 1.7 %collective-permute-done.9.refs_1_.refs_11_ = bf16[1488,128]{1,0:T(8,128)(2,1)S(1)} collective-permute-done((bf16[1488,128]{1,0:T(8,128)(2,1)S(1)}, bf16[1488,128]{1,0:T(8,128)(2,1)S(1)}, u32[]{:S(2)}, u32[]{:S(2)}) %collective-permute-start.9) | collective-permute-done | bytes 380960 | tf_op jit(solution)/shard_map/ppermute | solution.py:51
  33.4 0.7 %stage.12 = (f32[256,640]{1,0:T(8,128)S(1)}, f32[128,256]{1,0:T(8,128)S(1)}) custom-call(s32[1]{0:T(128)} %bitcast.me_ref, bf16[1488,128]{1,0:T(8,128)(2,1)S(1)} %collective-permute-done.4.refs_0_.refs_10_, bf16[1488,128]{1,0:T(8,128)(2,1)S(1)} %collective-permute-done.9.refs_1_.refs_11_, ...), custom_call_target="tpu_custom_call", output_to_operand_aliasing={{0}: (8, {}), {1}: (9, {})} | custom-call | flops 167772160 | bytes 2097152 | tf_op jit(solution)/shard_map/stage/pallas_call | solution.py:372
  34.2 3.3 %collective-permute-done.8.refs_1_.refs_14_ = bf16[1488,128]{1,0:T(8,128)(2,1)S(1)} collective-permute-done((bf16[1488,128]{1,0:T(8,128)(2,1)S(1)}, bf16[1488,128]{1,0:T(8,128)(2,1)S(1)}, u32[]{:S(2)}, u32[]{:S(2)}) %collective-permute-start.8) | collective-permute-done | bytes 380960 | tf_op jit(solution)/shard_map/ppermute | solution.py:51
  37.5 0.8 %stage.13 = (f32[256,640]{1,0:T(8,128)S(1)}, f32[128,256]{1,0:T(8,128)S(1)}) custom-call(s32[1]{0:T(128)} %bitcast.me_ref, bf16[1488,128]{1,0:T(8,128)(2,1)S(1)} %collective-permute-done.13.refs_0_.refs_12_, bf16[1488,128]{1,0:T(8,128)(2,1)S(1)} %collective-permute-done.14.refs_1_.refs_13_, ...), custom_call_target="tpu_custom_call", output_to_operand_aliasing={{0}: (8, {}), {1}: (9, {})} | custom-call | flops 167772160 | bytes 2097152 | tf_op jit(solution)/shard_map/stage/pallas_call | solution.py:372
  38.3 0.9 %collective-permute-done.12.refs_2_.refs_15_ = bf16[1488,128]{1,0:T(8,128)(2,1)S(1)} collective-permute-done((bf16[1488,128]{1,0:T(8,128)(2,1)S(1)}, bf16[1488,128]{1,0:T(8,128)(2,1)S(1)}, u32[]{:S(2)}, u32[]{:S(2)}) %collective-permute-start.12) | collective-permute-done | bytes 380960 | tf_op jit(solution)/shard_map/ppermute | solution.py:55
  39.2 2.4 %features.1.unit_ref = bf16[128,128]{1,0:T(8,128)(2,1)S(1)} custom-call(s32[1]{0:T(128)} %bitcast.me_ref, s32[1,2]{1,0:T(1,128)S(1)} %copy-done, bf16[1488,128]{1,0:T(8,128)(2,1)S(1)} %collective-permute-done.8.refs_1_.refs_14_, bf16[1488,128]{1,0:T(8,128)(2,1)S(1)} %collective-permute-done.12.refs_2_.refs_15_, ...), custom_call_target="tpu_custom_call" | custom-call | flops 167772160 | bytes 2097152 | tf_op jit(solution)/shard_map/features/pallas_call | solution.py:372
  41.6 1.7 %scores.1 = (f32[2,3]{1,0:T(2,128)}, f32[2]{0:T(128)}) custom-call(bf16[128,128]{1,0:T(8,128)(2,1)S(1)} %features.1.unit_ref, bf16[1488,128]{1,0:T(8,128)(2,1)S(1)} %pack.1.refs_0_, bf16[1488,128]{1,0:T(8,128)(2,1)S(1)} %collective-permute-done.2.refs_1_, bf16[1488,128]{1,0:T(8,128)(2,1)S(1)} %collective-permute-done.refs_0_.refs_2_, ...), custom_call_target="tpu_custom_call" | custom-call | flops 4194304 | bytes 2097152 | tf_op jit(solution)/shard_map/scores/pallas_call | solution.py:420
  (11 shorter events, 0.0 us)
Async XLA Ops:
  2.1 3.2 %collective-permute-start.2 = (bf16[1488,128]{1,0:T(8,128)(2,1)S(1)}, bf16[1488,128]{1,0:T(8,128)(2,1)S(1)}, u32[]{:S(2)}, u32[]{:S(2)}) collective-permute-start(bf16[1488,128]{1,0:T(8,128)(2,1)S(1)} %pack.1.refs_0_), channel_id=1, source_target_pairs={{0,1},{1,0},{2,3},{3,2},{4,5},{5,4},{6,7},{7,6},{8,9},{9,8},{10,11... | collective-permute-start | bytes 1142792 | tf_op jit(solution)/shard_map/ppermute | solution.py:55
  2.6 10.9 %collective-permute-start = (bf16[1488,128]{1,0:T(8,128)(2,1)S(1)}, bf16[1488,128]{1,0:T(8,128)(2,1)S(1)}, u32[]{:S(2)}, u32[]{:S(2)}) collective-permute-start(bf16[1488,128]{1,0:T(8,128)(2,1)S(1)} %pack.1.refs_0_), channel_id=1, source_target_pairs={{0,4},{1,3},{4,8},{5,1},{8,12},{9,5},{12,14},{13,9},{14,10},{15,13... | collective-permute-start | bytes 1142792 | tf_op jit(solution)/shard_map/ppermute | solution.py:51
  5.2 10.5 %collective-permute-start.3 = (bf16[1488,128]{1,0:T(8,128)(2,1)S(1)}, bf16[1488,128]{1,0:T(8,128)(2,1)S(1)}, u32[]{:S(2)}, u32[]{:S(2)}) collective-permute-start(bf16[1488,128]{1,0:T(8,128)(2,1)S(1)} %collective-permute-done.2.refs_1_), channel_id=1, source_target_pairs={{0,4},{1,3},{4,8},{5,1},{8,12},{9,5},{12,14},{13,9},{14,10},{15,13... | collective-permute-start | bytes 1142792 | tf_op jit(solution)/shard_map/ppermute | solution.py:51
  13.5 7.7 %collective-permute-start.1 = (bf16[1488,128]{1,0:T(8,128)(2,1)S(1)}, bf16[1488,128]{1,0:T(8,128)(2,1)S(1)}, u32[]{:S(2)}, u32[]{:S(2)}) collective-permute-start(bf16[1488,128]{1,0:T(8,128)(2,1)S(1)} %collective-permute-done.refs_0_.refs_2_), channel_id=1, source_target_pairs={{0,4},{1,3},{4,8},{5,1},{8,12},{9,5},{12,14},{13,9},{14,10},{15,13... | collective-permute-start | bytes 1142792 | tf_op jit(solution)/shard_map/ppermute | solution.py:51
  15.1 7.7 %collective-permute-start.6 = (bf16[1488,128]{1,0:T(8,128)(2,1)S(1)}, bf16[1488,128]{1,0:T(8,128)(2,1)S(1)}, u32[]{:S(2)}, u32[]{:S(2)}) collective-permute-start(bf16[1488,128]{1,0:T(8,128)(2,1)S(1)} %collective-permute-done.refs_0_.refs_2_), channel_id=1, source_target_pairs={{0,1},{1,0},{2,3},{3,2},{4,5},{5,4},{6,7},{7,6},{8,9},{9,8},{10,11... | collective-permute-start | bytes 1142792 | tf_op jit(solution)/shard_map/ppermute | solution.py:55
  15.8 7.0 %collective-permute-start.7 = (bf16[1488,128]{1,0:T(8,128)(2,1)S(1)}, bf16[1488,128]{1,0:T(8,128)(2,1)S(1)}, u32[]{:S(2)}, u32[]{:S(2)}) collective-permute-start(bf16[1488,128]{1,0:T(8,128)(2,1)S(1)} %collective-permute-done.3.refs_1_.refs_3_), channel_id=1, source_target_pairs={{0,1},{1,0},{2,3},{3,2},{4,5},{5,4},{6,7},{7,6},{8,9},{9,8},{10,11... | collective-permute-start | bytes 1142792 | tf_op jit(solution)/shard_map/ppermute | solution.py:55
  16.3 8.9 %collective-permute-start.5 = (bf16[1488,128]{1,0:T(8,128)(2,1)S(1)}, bf16[1488,128]{1,0:T(8,128)(2,1)S(1)}, u32[]{:S(2)}, u32[]{:S(2)}) collective-permute-start(bf16[1488,128]{1,0:T(8,128)(2,1)S(1)} %collective-permute-done.3.refs_1_.refs_3_), channel_id=1, source_target_pairs={{0,4},{1,3},{4,8},{5,1},{8,12},{9,5},{12,14},{13,9},{14,10},{15,13... | collective-permute-start | bytes 1142792 | tf_op jit(solution)/shard_map/ppermute | solution.py:51
  21.2 8.2 %collective-permute-start.4 = (bf16[1488,128]{1,0:T(8,128)(2,1)S(1)}, bf16[1488,128]{1,0:T(8,128)(2,1)S(1)}, u32[]{:S(2)}, u32[]{:S(2)}) collective-permute-start(bf16[1488,128]{1,0:T(8,128)(2,1)S(1)} %collective-permute-done.1.refs_0_.refs_6_), channel_id=1, source_target_pairs={{0,4},{1,3},{4,8},{5,1},{8,12},{9,5},{12,14},{13,9},{14,10},{15,13... | collective-permute-start | bytes 1142792 | tf_op jit(solution)/shard_map/ppermute | solution.py:51
  22.7 8.2 %collective-permute-start.10 = (bf16[1488,128]{1,0:T(8,128)(2,1)S(1)}, bf16[1488,128]{1,0:T(8,128)(2,1)S(1)}, u32[]{:S(2)}, u32[]{:S(2)}) collective-permute-start(bf16[1488,128]{1,0:T(8,128)(2,1)S(1)} %collective-permute-done.1.refs_0_.refs_6_), channel_id=1, source_target_pairs={{0,1},{1,0},{2,3},{3,2},{4,5},{5,4},{6,7},{7,6},{8,9},{9,8},{10,11... | collective-permute-start | bytes 1142792 | tf_op jit(solution)/shard_map/ppermute | solution.py:55
  25.2 5.7 %collective-permute-start.11 = (bf16[1488,128]{1,0:T(8,128)(2,1)S(1)}, bf16[1488,128]{1,0:T(8,128)(2,1)S(1)}, u32[]{:S(2)}, u32[]{:S(2)}) collective-permute-start(bf16[1488,128]{1,0:T(8,128)(2,1)S(1)} %collective-permute-done.5.refs_1_.refs_7_), channel_id=1, source_target_pairs={{0,1},{1,0},{2,3},{3,2},{4,5},{5,4},{6,7},{7,6},{8,9},{9,8},{10,11... | collective-permute-start | bytes 1142792 | tf_op jit(solution)/shard_map/ppermute | solution.py:55
  25.3 8.2 %collective-permute-start.9 = (bf16[1488,128]{1,0:T(8,128)(2,1)S(1)}, bf16[1488,128]{1,0:T(8,128)(2,1)S(1)}, u32[]{:S(2)}, u32[]{:S(2)}) collective-permute-start(bf16[1488,128]{1,0:T(8,128)(2,1)S(1)} %collective-permute-done.5.refs_1_.refs_7_), channel_id=1, source_target_pairs={{0,4},{1,3},{4,8},{5,1},{8,12},{9,5},{12,14},{13,9},{14,10},{15,13... | collective-permute-start | bytes 1142792 | tf_op jit(solution)/shard_map/ppermute | solution.py:51
  29.3 8.2 %collective-permute-start.8 = (bf16[1488,128]{1,0:T(8,128)(2,1)S(1)}, bf16[1488,128]{1,0:T(8,128)(2,1)S(1)}, u32[]{:S(2)}, u32[]{:S(2)}) collective-permute-start(bf16[1488,128]{1,0:T(8,128)(2,1)S(1)} %collective-permute-done.4.refs_0_.refs_10_), channel_id=1, source_target_pairs={{0,4},{1,3},{4,8},{5,1},{8,12},{9,5},{12,14},{13,9},{14,10},{15,13... | collective-permute-start | bytes 1142792 | tf_op jit(solution)/shard_map/ppermute | solution.py:51
  30.9 6.6 %collective-permute-start.13 = (bf16[1488,128]{1,0:T(8,128)(2,1)S(1)}, bf16[1488,128]{1,0:T(8,128)(2,1)S(1)}, u32[]{:S(2)}, u32[]{:S(2)}) collective-permute-start(bf16[1488,128]{1,0:T(8,128)(2,1)S(1)} %collective-permute-done.4.refs_0_.refs_10_), channel_id=1, source_target_pairs={{0,1},{1,0},{2,3},{3,2},{4,5},{5,4},{6,7},{7,6},{8,9},{9,8},{10,11... | collective-permute-start | bytes 1142792 | tf_op jit(solution)/shard_map/ppermute | solution.py:55
  33.4 4.1 %collective-permute-start.14 = (bf16[1488,128]{1,0:T(8,128)(2,1)S(1)}, bf16[1488,128]{1,0:T(8,128)(2,1)S(1)}, u32[]{:S(2)}, u32[]{:S(2)}) collective-permute-start(bf16[1488,128]{1,0:T(8,128)(2,1)S(1)} %collective-permute-done.9.refs_1_.refs_11_), channel_id=1, source_target_pairs={{0,1},{1,0},{2,3},{3,2},{4,5},{5,4},{6,7},{7,6},{8,9},{9,8},{10,11... | collective-permute-start | bytes 1142792 | tf_op jit(solution)/shard_map/ppermute | solution.py:55
  37.5 1.7 %copy-start = (s32[1,2]{1,0:T(1,128)S(1)}, s32[1,2]{1,0:T(1,128)}, u32[]{:S(2)}) copy-start(s32[1,2]{1,0:T(1,128)} %refs_0_.3) | copy-start | bytes 28
  37.5 1.7 %collective-permute-start.12 = (bf16[1488,128]{1,0:T(8,128)(2,1)S(1)}, bf16[1488,128]{1,0:T(8,128)(2,1)S(1)}, u32[]{:S(2)}, u32[]{:S(2)}) collective-permute-start(bf16[1488,128]{1,0:T(8,128)(2,1)S(1)} %collective-permute-done.8.refs_1_.refs_14_), channel_id=1, source_target_pairs={{0,1},{1,0},{2,3},{3,2},{4,5},{5,4},{6,7},{7,6},{8,9},{9,8},{10,11... | collective-permute-start | bytes 1142792 | tf_op jit(solution)/shard_map/ppermute | solution.py:55

commit v6 on v5

--- a/solution.py
+++ b/solution.py
@@ -14,8 +14,8 @@
 RING_CHIPS = 8
 LANES = 128
 STEPS = 4
-X_DOWN, X_LOW, J_LOW, M_DOWN, VALUES, SUMS = range(6)
-X_SOURCE, X_TARGET, SQUARES, M_SOURCE, J_TARGET, V_TARGET, LOCAL_SUMS = range(7)
+X_DOWN, X_LOW, J_LOW, J_TARGET, M_DOWN, M_SOURCE, VALUES, V_TARGET, SUMS = range(9)
+INVERSE, LEFT_ONE, X_TARGET, LOCAL_SUMS = range(4)
 MIB = 1 << 20
 
 
@@ -111,46 +111,48 @@
 
 
 def local_kernel(*refs):
-    x_hbm, mixed_hbm, adjoint_hbm, values_hbm, target_hbm, gain_hbm, source_hbm, top_target_hbm = refs[:8]
-    x_ref, mixed_ref, adjoint_ref, values_ref, target_ref, sums_ref = refs[8:14]
-    gain_ref, source_ref, top_target_ref, sems = refs[14:]
-    width, value_width = x_ref.shape[1], values_ref.shape[1]
-    span, value_span = width // STEPS, value_width // STEPS
+    x_hbm, mixed_hbm, adjoint_hbm, values_hbm, target_hbm, top_target_hbm, gain_hbm, source_hbm = refs[:8]
+    x_ref, mixed_ref, adjoint_ref, values_ref, target_ref, top_target_ref, turned_ref, sums_ref = refs[8:16]
+    gain_ref, source_ref, sems = refs[16:]
+    tokens, width = x_ref.shape
+    span = width // STEPS
     copies = []
     for j in range(STEPS):
-        part, value_part = pl.ds(j * span, span), pl.ds(j * value_span, value_span)
+        part = pl.ds(j * span, span)
         pairs = (
             (gain_hbm.at[:, part], gain_ref.at[:, part]),
             (source_hbm.at[:, part], source_ref.at[:, part]),
             (x_hbm.at[:, part], x_ref.at[:, part]),
             (target_hbm.at[part], target_ref.at[part]),
-            (mixed_hbm.at[:, part], mixed_ref.at[:, part]),
-            (adjoint_hbm.at[:, part], adjoint_ref.at[:, part]),
-            (values_hbm.at[:, value_part], values_ref.at[:, value_part]),
-            (top_target_hbm.at[value_part], top_target_ref.at[value_part]),
         )
         copies.append(load(pairs, sems.at[j]))
-    total = [None] * LOCAL_SUMS
-
-    def add(column, value):
-        total[column] = value if total[column] is None else total[column] + value
-
+    pairs = (
+        (adjoint_hbm, adjoint_ref),
+        (mixed_hbm, mixed_ref),
+        (values_hbm, values_ref),
+        (top_target_hbm, top_target_ref),
+    )
+    later = load(pairs, sems.at[STEPS])
+    products = jnp.zeros((tokens, 2 * LANES), F32)
+    squares = jnp.zeros((tokens, LANES), F32)
     for j in range(STEPS):
         for copy in copies[j]:
             copy.wait()
-        part, value_part = slice(j * span, (j + 1) * span), slice(j * value_span, (j + 1) * value_span)
-        x, target, source = x_ref[:, part], target_ref[part, :], source_ref[:, part]
-        gained = (source.astype(F32) * gain_ref[:, part]).astype(BF16)
-        add(X_SOURCE, mm_rows(x, jnp.concatenate([gained, gained], axis=0)))
-        add(X_TARGET, mm(x, target))
+        part = slice(j * span, (j + 1) * span)
+        x, source = x_ref[:, part], source_ref[:, part].astype(F32)
+        gained = source * gain_ref[:, part]
+        turned_ref[part, :] = jnp.concatenate([source, source], axis=0).T.astype(BF16)
+        gained = jnp.concatenate([gained, gained], axis=0).T.astype(BF16)
+        products = products + mm(x, jnp.concatenate([gained, target_ref[part, :]], axis=1))
         for i in range(span // LANES):
             wide = x[:, i * LANES : (i + 1) * LANES].astype(F32)
-            add(SQUARES, wide * wide)
-        add(M_SOURCE, mm_rows(mixed_ref[:, part], jnp.concatenate([source, source], axis=0)))
-        add(J_TARGET, mm(adjoint_ref[:, part], target))
-        add(V_TARGET, mm(values_ref[:, value_part], top_target_ref[value_part, :]))
-    for i in range(LOCAL_SUMS):
-        sums_ref[:, i * LANES : (i + 1) * LANES] = total[i]
+            squares = squares + wide * wide
+    mean = jnp.sum(squares, axis=1, keepdims=True) * (1.0 / width)
+    inverse = jnp.broadcast_to(lax.rsqrt(mean + 1e-05), (tokens, LANES))
+    for i, value in enumerate((inverse, inverse * products[:, :LANES], products[:, LANES:])):
+        sums_ref[:, i * LANES : (i + 1) * LANES] = value
+    for copy in later:
+        copy.wait()
 
 
 def stage_kernel(away, first, last, me_ref, *refs):
@@ -158,7 +160,7 @@
     take = lambda k: [refs.pop(0) for _ in range(k)]
     counts_ref = take(1)[0] if last else None
     pieces = take(2)
-    x_ref, mixed_ref, adjoint_ref, values_ref, target_ref = take(5)
+    x_ref, mixed_ref, adjoint_ref, values_ref, target_ref, top_target_ref, source_ref = take(7)
     old_sums, old_bridge = (None, None) if first else take(2)
     local_ref, expand_hbm, sketch_hbm = take(3) if last else (None, None, None)
     if last:
@@ -181,12 +183,17 @@
     values_start = (chip // 2) * span + odd * (rows - pad)
     values_part = pl.ds(pl.multiple_of(values_start, LANES), rows + pad)
     side = core if away >= 0 else 1 - core
-    up[pl.ds(pl.multiple_of((1 - odd) * rows, 16), pad), :] = jnp.zeros((pad, LANES), BF16)
+    up[pl.ds(pl.multiple_of((1 - odd) * rows, 16), pad), :] = jnp.zeros((pad, 2 * LANES), BF16)
+    up[pl.ds(pl.multiple_of(odd * pad, 16), rows), pl.ds(LANES, LANES)] = top_target_ref[
+        pl.ds(pl.multiple_of(chip * rows, 16), rows), :
+    ]
     for piece, c in ((pieces[0], side), (pieces[1], 1 - side)):
         one = pl.ds(pl.multiple_of(c * rows, 16), rows)
         both[one, pl.ds(0, LANES)] = piece[pl.ds(0, rows), :]
         both[one, pl.ds(LANES, LANES)] = piece[pl.ds(rows, rows), :]
-        up[pl.ds(pl.multiple_of(odd * pad + c * half, 16), half), :] = piece[pl.ds(2 * rows, half), :]
+        up[pl.ds(pl.multiple_of(odd * pad + c * half, 16), half), pl.ds(0, LANES)] = piece[
+            pl.ds(2 * rows, half), :
+        ]
         packed = piece[pl.ds(2 * rows + half, half), :].astype(F32)
         turned = pltpu.roll(packed, pad, 1)
         lower = half_lanes(packed.shape)
@@ -194,15 +201,18 @@
         down[pl.ds(pl.multiple_of(c * rows + half, 16), half), :] = jnp.where(lower, turned, packed).astype(BF16)
 
     weights = both[...]
-    products = [None] * SUMS
-    x_both = mm(x_ref[:, mine], weights)
-    products[X_DOWN], products[X_LOW] = x_both[:, :LANES], x_both[:, LANES:]
-    products[J_LOW] = mm(adjoint_ref[:, mine], weights[:, LANES:])
-    products[M_DOWN] = mm(mixed_ref[:, mine], down[...])
-    products[VALUES] = mm(values_ref[:, values_part], up[...])
-    bridge = mm_cols(
-        weights[:, :LANES], jnp.concatenate([weights[:, LANES:], target_ref[mine, :]], axis=1)
-    )
+    down_up = weights[:, :LANES]
+    lows = jnp.concatenate([weights[:, LANES:], target_ref[mine, :]], axis=1)
+    products = []
+    for activation, factor in (
+        (x_ref[:, mine], weights),
+        (adjoint_ref[:, mine], lows),
+        (mixed_ref[:, mine], jnp.concatenate([down[...], source_ref[mine, :]], axis=1)),
+        (values_ref[:, values_part], up[...]),
+    ):
+        product = mm(activation, factor)
+        products += [product[:, :LANES], product[:, LANES:]]
+    bridge = mm_cols(down_up, lows)
     if not first:
         products = [p + old_sums[:, i * LANES : (i + 1) * LANES] for i, p in enumerate(products)]
         bridge = bridge + old_bridge[...]
@@ -215,8 +225,7 @@
     for copy in more:
         copy.wait()
     local = [local_ref[:, i * LANES : (i + 1) * LANES] for i in range(LOCAL_SUMS)]
-    mean = jnp.sum(local[SQUARES], axis=1, keepdims=True) * (1.0 / width)
-    inverse = lax.rsqrt(mean + 1e-05)
+    inverse = local[INVERSE]
     reduced = inverse * products[X_DOWN]
     expand = expand_ref[...]
     left_two = mm_rows(reduced.astype(BF16), jnp.concatenate([expand, expand], axis=0))
@@ -226,9 +235,9 @@
     back = mm(returned, bridge.astype(BF16))
     along = along * inverse
     right_three = products[J_LOW] + inverse * (ALPHA * back[:, :LANES] - along * products[X_LOW])
-    right_four = local[J_TARGET] + inverse * (ALPHA * back[:, LANES:] - along * local[X_TARGET])
-    rights = (right_one, ALPHA * local[V_TARGET], ALPHA * right_three, ALPHA * right_four)
-    lefts = (inverse * local[X_SOURCE], left_two, local[M_SOURCE], products[M_DOWN])
+    right_four = products[J_TARGET] + inverse * (ALPHA * back[:, LANES:] - along * local[X_TARGET])
+    rights = (right_one, ALPHA * products[V_TARGET], ALPHA * right_three, ALPHA * right_four)
+    lefts = (local[LEFT_ONE], left_two, products[M_SOURCE], products[M_DOWN])
     place = lax.broadcasted_iota(jnp.int32, (tokens, LANES), 0)
     one, two = counts_ref[0, 0], counts_ref[0, 1]
     lower = half_lanes((tokens, LANES))
@@ -241,9 +250,29 @@
         out_ref[pl.ds(e * pad, pad), :] = (own * lax.rsqrt(squares + 1e-06)).astype(BF16)
 
 
-def score_kernel(pieces, count, start, unit_ref, *refs):
-    piece_refs = refs[:pieces]
-    best_ref, mean_ref, spread = refs[pieces:]
+def split_kernel(block_ref, head_ref, tail_ref):
+    cut = head_ref.shape[0]
+    head_ref[...] = block_ref[pl.ds(0, cut), :]
+    tail_ref[...] = block_ref[pl.ds(cut, tail_ref.shape[0]), :]
+
+
+def best_of(block, count, spread, best):
+    half = LANES // 2
+    scale = float(half * LANES) ** 0.5
+    at = block.shape[0] - (half + 2) * count
+    wide = block[pl.ds(at, half * count), :].astype(F32)
+    labels = block[pl.ds(at + half * count, 2 * count), :].astype(F32)[:count]
+    for e in range(2):
+        products = wide * spread[e]
+        total = jnp.sum(products.reshape(half, count, LANES), axis=0)
+        similar = scale * jnp.sum(total, axis=1, keepdims=True)
+        for t in range(TASKS):
+            here = jnp.where(labels == float(t), similar, -2.0 * scale)
+            best[e][t] = jnp.maximum(best[e][t], here)
+
+
+def score_kernel(blocks, count, unit_ref, *refs):
+    block_refs, (out_ref, mean_ref, spread) = refs[:blocks], refs[blocks:]
     half = LANES // 2
     scale = float(half * LANES) ** 0.5
     for e in range(2):
@@ -251,20 +280,12 @@
             row = unit_ref[pl.ds(e * half + i, 1), :].astype(F32)
             spread[e, pl.ds(i * count, count), :] = jnp.broadcast_to(row, (count, LANES))
     best = [[jnp.full((count, LANES), -2.0 * scale, F32) for _ in range(TASKS)] for _ in range(2)]
-    for piece in piece_refs:
-        wide = piece[pl.ds(start, half * count), :].astype(F32)
-        labels = piece[pl.ds(start + half * count, 2 * count), :].astype(F32)[:count]
-        for e in range(2):
-            products = wide * spread[e]
-            total = jnp.sum(products.reshape(half, count, LANES), axis=0)
-            similar = scale * jnp.sum(total, axis=1, keepdims=True)
-            for t in range(TASKS):
-                here = jnp.where(labels == float(t), similar, -2.0 * scale)
-                best[e][t] = jnp.maximum(best[e][t], here)
+    for block in block_refs:
+        best_of(block, count, spread, best)
     for e in range(2):
         values = [jnp.max(best[e][t]) for t in range(TASKS)]
         for t in range(TASKS):
-            best_ref[e, t] = values[t]
+            out_ref[e, t] = values[t]
         mean_ref[e] = (values[0] + values[1] + values[2]) * (1.0 / TASKS)
 
 
@@ -346,20 +367,23 @@
         adjoint,
         values,
         bottom_target_sketch,
+        top_target_sketch,
         top_rmsnorm_weights.reshape(1, width),
         source_sketch.T,
-        top_target_sketch,
     )
     *activations, local = pl.pallas_call(
         local_kernel,
-        out_shape=[jax.ShapeDtypeStruct(a.shape, a.dtype) for a in inputs[:5]]
-        + [jax.ShapeDtypeStruct((tokens, LOCAL_SUMS * LANES), F32)],
+        out_shape=[jax.ShapeDtypeStruct(a.shape, a.dtype) for a in inputs[:6]]
+        + [
+            jax.ShapeDtypeStruct((width, LANES), BF16),
+            jax.ShapeDtypeStruct((tokens, LOCAL_SUMS * LANES), F32),
+        ],
         in_specs=[HBM] * len(inputs),
-        out_specs=[VMEM] * 6,
-        scratch_shapes=[pltpu.VMEM(a.shape, a.dtype) for a in inputs[5:]]
-        + [pltpu.SemaphoreType.DMA((STEPS, len(inputs)))],
+        out_specs=[VMEM] * 8,
+        scratch_shapes=[pltpu.VMEM(a.shape, a.dtype) for a in inputs[6:]]
+        + [pltpu.SemaphoreType.DMA((STEPS + 1, 4))],
         compiler_params=params(24),
-        cost_estimate=cost(tokens * width * LANES * 12, 14 * MIB),
+        cost_estimate=cost(tokens * width * LANES * 6, 14 * MIB),
         name="local_products",
     )(*in_hbm(inputs))
 
@@ -380,7 +404,7 @@
             out_specs=VMEM if last else [VMEM, VMEM],
             scratch_shapes=[
                 pltpu.VMEM((2 * rows, 2 * LANES), BF16),
-                pltpu.VMEM((rows + LANES // 2, LANES), BF16),
+                pltpu.VMEM((rows + LANES // 2, 2 * LANES), BF16),
                 pltpu.VMEM((2 * rows, LANES), BF16),
                 pltpu.VMEM(small[0].shape, BF16),
                 pltpu.VMEM(small[1].shape, BF16),
@@ -391,6 +415,17 @@
             cost_estimate=cost(tokens * rows * LANES * 16, 2 * MIB),
             name="features" if last else "stage",
         )(*head, *pieces, *activations, *sums, *((local, *in_hbm(small)) if last else ()))
+
+    def split(block):
+        shapes = (3 * rows, LANES), (block.shape[0] - 3 * rows, LANES)
+        return pl.pallas_call(
+            split_kernel,
+            out_shape=[jax.ShapeDtypeStruct(shape, BF16) for shape in shapes],
+            in_specs=[VMEM],
+            out_specs=[VMEM, VMEM],
+            compiler_params=params(8),
+            name="split",
+        )(block)
 
     tie = lax.optimization_barrier
     half = RING_CHIPS // 2
@@ -405,6 +440,9 @@
         held = [first, second]
         crossed = [other_core(first), other_core(second)]
         blocks += held + crossed
+        if k == half - 1:
+            first, panel = split(first)
+            panel = hop(panel)
         first = hop(first)
         sums = stage(k, held, sums)
         first, sums = tie((first, sums))
@@ -413,12 +451,11 @@
         sums = stage(-k, crossed, sums)
         if k < half - 1:
             second, sums = tie((second, sums))
-    held = [first, other_core(first)]
-    blocks += held
-    unit = stage(half, held, sums, local)
+    unit = stage(half, [first, other_core(first)], sums, local)
+    blocks += [panel, other_core(panel)]
 
     task_best, scores = pl.pallas_call(
-        functools.partial(score_kernel, len(blocks), count, 3 * rows),
+        functools.partial(score_kernel, len(blocks), count),
         out_shape=(jax.ShapeDtypeStruct((2, TASKS), F32), jax.ShapeDtypeStruct((2,), F32)),
         in_specs=[VMEM] * (1 + len(blocks)),
         out_specs=(SMEM, SMEM),

time: 43.8 us -> 41.5 us (0.947)
  waiting for transfers between devices: 12 us -> 8.52 us
  starting transfers between devices: 13.3 us -> 16.2 us
  Pallas kernels: 17.3 us -> 15.7 us
    ppermute x7 -> x8, starting transfers between devices: 12.2 us -> 15.4 us  [hop(): return lax.ppermute(value, 'dp', pairs)]
    ppermute x7 -> x8, waiting for transfers between devices: 11 us -> 8.5 us  [hop(): return lax.ppermute(value, 'dp', pairs)]
    pallas_call x1, Pallas kernels: 6.6 us -> 4.6 us  [shards(): pl.pallas_call(local_kernel, out_shape=[jax.ShapeDtypeStruct(a.shape, a.d...]
    ppermute x8 -> x9, waiting for transfers between devices: 0.94 us -> 0.02 us  [other_core(): lax.ppermute(value, 'dp', [(d, d ^ 1) for d in range(2 * RING_CHIPS)])]
    ppermute x8 -> x9, starting transfers between devices: 1.11 us -> 0.76 us  [other_core(): lax.ppermute(value, 'dp', [(d, d ^ 1) for d in range(2 * RING_CHIPS)])]
    pallas_call x1 -> x2, Pallas kernels: 1.7 us -> 1.72 us  [the longest x1 1.69 us: shards(): pl.pallas_call(functools.partial(score_kernel, len(blocks), count), out_s...]
  transfers between devices with their start and end apart: 15 -> 17, of which waited for: 6 -> 6; matrix products, arithmetic and copies ran while one was open for 0% -> 0% of each run, Pallas kernels for 27% -> 31%
where the time goes in v6:
time: 41.5 us; the launch traced here: 41.2 us
  starting transfers between devices  16.2 us (39%)
  Pallas kernels  15.7 us (38%)
  waiting for transfers between devices  8.52 us (21%)
  between operations  0.79 us (2%)
    ppermute x8, starting transfers between devices, hop(): return lax.ppermute(value, 'dp', pairs)  15.4 us
    ppermute x8, waiting for transfers between devices, hop(): return lax.ppermute(value, 'dp', pairs)  8.5 us
    pallas_call x8, Pallas kernels, stage(): pl.pallas_call(functools.partial(stage_kernel, away, first, last), out_sh...  7.99 us
    pallas_call x1, Pallas kernels, shards(): pl.pallas_call(local_kernel, out_shape=[jax.ShapeDtypeStruct(a.shape, a.d...  4.6 us
    pallas_call x1, Pallas kernels, shards(): pl.pallas_call(functools.partial(score_kernel, len(blocks), count), out_s...  1.69 us
    pallas_call x1, Pallas kernels, shards(): pl.pallas_call(pack_kernel, out_shape=jax.ShapeDtypeStruct((3 * rows + (L...  1.41 us
  transfers between devices with their start and end apart: 17, of which 6 were waited for; matrix products, arithmetic and copies ran while one was open for 0% of the time, Pallas kernels for 31%

profile of v6, /device:TPU:0, one launch (start us, length us, event | category | flops | bytes accessed | tf_op | source)
XLA Modules:
  0.0 41.2 jit_solution(4325666836272824308)
XLA Ops:
  0.6 1.4 %pack.1.refs_0_ = bf16[1488,128]{1,0:T(8,128)(2,1)S(1)} custom-call(s32[1]{0:T(128)} %bitcast.me_ref, f32[40,128]{1,0:T(8,128)} %bitcast.10, bf16[320,128]{1,0:T(8,128)(2,1)} %refs_1_.2, bf16[320,128]{1,0:T(8,128)(2,1)} %bitcast.12, bf16[128,128]{1,0:T(8,128)(2,1)} %refs_3_.2, bf16[160,128]{1,0:T(8,128)(2,1)} %bitcast.13, bf16[320,128]{1,0:T(8,128)(2,1)} %refs_5_.2, ...), custom_call_target="tpu_custom_call" | custom-call | tf_op jit(solution)/shard_map/pack/pallas_call | solution.py:353
  2.1 0.5 %collective-permute-start.2 = (bf16[1488,128]{1,0:T(8,128)(2,1)S(1)}, bf16[1488,128]{1,0:T(8,128)(2,1)S(1)}, u32[]{:S(2)}, u32[]{:S(2)}) collective-permute-start(bf16[1488,128]{1,0:T(8,128)(2,1)S(1)} %pack.1.refs_0_), channel_id=1, source_target_pairs={{0,1},{1,0},{2,3},{3,2},{4,5},{5,4},{6,7},{7,6},{8,9},{9,8},{10,11... | collective-permute-start | bytes 1142792 | tf_op jit(solution)/shard_map/ppermute | solution.py:55
  2.6 2.6 %collective-permute-start = (bf16[1488,128]{1,0:T(8,128)(2,1)S(1)}, bf16[1488,128]{1,0:T(8,128)(2,1)S(1)}, u32[]{:S(2)}, u32[]{:S(2)}) collective-permute-start(bf16[1488,128]{1,0:T(8,128)(2,1)S(1)} %pack.1.refs_0_), channel_id=1, source_target_pairs={{0,4},{1,3},{4,8},{5,1},{8,12},{9,5},{12,14},{13,9},{14,10},{15,13... | collective-permute-start | bytes 1142792 | tf_op jit(solution)/shard_map/ppermute | solution.py:51
  5.2 0.0 collective-permute-done.2.refs_1_
  5.2 1.6 %collective-permute-start.3 = (bf16[1488,128]{1,0:T(8,128)(2,1)S(1)}, bf16[1488,128]{1,0:T(8,128)(2,1)S(1)}, u32[]{:S(2)}, u32[]{:S(2)}) collective-permute-start(bf16[1488,128]{1,0:T(8,128)(2,1)S(1)} %collective-permute-done.2.refs_1_), channel_id=1, source_target_pairs={{0,4},{1,3},{4,8},{5,1},{8,12},{9,5},{12,14},{13,9},{14,10},{15,13... | collective-permute-start | bytes 1142792 | tf_op jit(solution)/shard_map/ppermute | solution.py:51
  6.8 4.6 %local_products.1 = (bf16[256,5120]{1,0:T(8,128)(2,1)S(1)}, bf16[256,5120]{1,0:T(8,128)(2,1)S(1)}, bf16[256,5120]{1,0:T(8,128)(2,1)S(1)}, bf16[256,2560]{1,0:T(8...) custom-call(bf16[256,5120]{1,0:T(8,128)(2,1)} %refs_0_.2, ...), custom_call_target="tpu_custom_call" | custom-call | flops 1006632960 | bytes 14680064 | tf_op jit(solution)/shard_map/local_products/pallas_call | solution.py:374
  11.5 1.6 %collective-permute-start.1 = (bf16[1488,128]{1,0:T(8,128)(2,1)S(1)}, bf16[1488,128]{1,0:T(8,128)(2,1)S(1)}, u32[]{:S(2)}, u32[]{:S(2)}) collective-permute-start(bf16[1488,128]{1,0:T(8,128)(2,1)S(1)} %collective-permute-done.refs_0_.refs_2_), channel_id=1, source_target_pairs={{0,4},{1,3},{4,8},{5,1},{8,12},{9,5},{12,14},{13,9},{14,10},{15,13... | collective-permute-start | bytes 1142792 | tf_op jit(solution)/shard_map/ppermute | solution.py:51
  13.1 0.0 collective-permute-start.6
  13.1 0.7 %stage.7 = (f32[256,1024]{1,0:T(8,128)S(1)}, f32[128,256]{1,0:T(8,128)S(1)}) custom-call(s32[1]{0:T(128)} %bitcast.me_ref, bf16[1488,128]{1,0:T(8,128)(2,1)S(1)} %pack.1.refs_0_, bf16[1488,128]{1,0:T(8,128)(2,1)S(1)} %collective-permute-done.2.refs_1_, bf16[256,5120]{1,0:T(8,128)(2,1)S(1)} %get-tuple-element.62.refs_2_.refs_3_, ...), custom_call_target="tpu_custom_call" | custom-call | flops 167772160 | bytes 2097152 | tf_op jit(solution)/shard_map/stage/pallas_call | solution.py:396
  13.8 1.0 %collective-permute-done.3.refs_1_.refs_3_ = bf16[1488,128]{1,0:T(8,128)(2,1)S(1)} collective-permute-done((bf16[1488,128]{1,0:T(8,128)(2,1)S(1)}, bf16[1488,128]{1,0:T(8,128)(2,1)S(1)}, u32[]{:S(2)}, u32[]{:S(2)}) %collective-permute-start.3) | collective-permute-done | bytes 380960 | tf_op jit(solution)/shard_map/ppermute | solution.py:51
  14.9 0.0 collective-permute-start.7
  14.9 2.1 %collective-permute-start.5 = (bf16[1488,128]{1,0:T(8,128)(2,1)S(1)}, bf16[1488,128]{1,0:T(8,128)(2,1)S(1)}, u32[]{:S(2)}, u32[]{:S(2)}) collective-permute-start(bf16[1488,128]{1,0:T(8,128)(2,1)S(1)} %collective-permute-done.3.refs_1_.refs_3_), channel_id=1, source_target_pairs={{0,4},{1,3},{4,8},{5,1},{8,12},{9,5},{12,14},{13,9},{14,10},{15,13... | collective-permute-start | bytes 1142792 | tf_op jit(solution)/shard_map/ppermute | solution.py:51
  16.9 0.9 %stage.8 = (f32[256,1024]{1,0:T(8,128)S(1)}, f32[128,256]{1,0:T(8,128)S(1)}) custom-call(s32[1]{0:T(128)} %bitcast.me_ref, bf16[1488,128]{1,0:T(8,128)(2,1)S(1)} %collective-permute-done.refs_0_.refs_2_, bf16[1488,128]{1,0:T(8,128)(2,1)S(1)} %collective-permute-done.3.refs_1_.refs_3_, ...), custom_call_target="tpu_custom_call", output_to_operand_aliasing={{0}: (10, {}), {1}: (11, {})} | custom-call | flops 167772160 | bytes 2097152 | tf_op jit(solution)/shard_map/stage/pallas_call | solution.py:396
  17.8 1.4 %collective-permute-done.1.refs_0_.refs_6_ = bf16[1488,128]{1,0:T(8,128)(2,1)S(1)} collective-permute-done((bf16[1488,128]{1,0:T(8,128)(2,1)S(1)}, bf16[1488,128]{1,0:T(8,128)(2,1)S(1)}, u32[]{:S(2)}, u32[]{:S(2)}) %collective-permute-start.1) | collective-permute-done | bytes 380960 | tf_op jit(solution)/shard_map/ppermute | solution.py:51
  19.2 1.9 %collective-permute-start.4 = (bf16[1488,128]{1,0:T(8,128)(2,1)S(1)}, bf16[1488,128]{1,0:T(8,128)(2,1)S(1)}, u32[]{:S(2)}, u32[]{:S(2)}) collective-permute-start(bf16[1488,128]{1,0:T(8,128)(2,1)S(1)} %collective-permute-done.1.refs_0_.refs_6_), channel_id=1, source_target_pairs={{0,4},{1,3},{4,8},{5,1},{8,12},{9,5},{12,14},{13,9},{14,10},{15,13... | collective-permute-start | bytes 1142792 | tf_op jit(solution)/shard_map/ppermute | solution.py:51
  21.0 0.8 %stage.9 = (f32[256,1024]{1,0:T(8,128)S(1)}, f32[128,256]{1,0:T(8,128)S(1)}) custom-call(s32[1]{0:T(128)} %bitcast.me_ref, bf16[1488,128]{1,0:T(8,128)(2,1)S(1)} %collective-permute-done.6.refs_0_.refs_4_, bf16[1488,128]{1,0:T(8,128)(2,1)S(1)} %collective-permute-done.7.refs_1_.refs_5_, ...), custom_call_target="tpu_custom_call", output_to_operand_aliasing={{0}: (10, {}), {1}: (11, {})} | custom-call | flops 167772160 | bytes 2097152 | tf_op jit(solution)/shard_map/stage/pallas_call | solution.py:396
  21.9 1.4 %collective-permute-done.5.refs_1_.refs_7_ = bf16[1488,128]{1,0:T(8,128)(2,1)S(1)} collective-permute-done((bf16[1488,128]{1,0:T(8,128)(2,1)S(1)}, bf16[1488,128]{1,0:T(8,128)(2,1)S(1)}, u32[]{:S(2)}, u32[]{:S(2)}) %collective-permute-start.5) | collective-permute-done | bytes 380960 | tf_op jit(solution)/shard_map/ppermute | solution.py:51
  23.2 1.9 %collective-permute-start.9 = (bf16[1488,128]{1,0:T(8,128)(2,1)S(1)}, bf16[1488,128]{1,0:T(8,128)(2,1)S(1)}, u32[]{:S(2)}, u32[]{:S(2)}) collective-permute-start(bf16[1488,128]{1,0:T(8,128)(2,1)S(1)} %collective-permute-done.5.refs_1_.refs_7_), channel_id=1, source_target_pairs={{0,4},{1,3},{4,8},{5,1},{8,12},{9,5},{12,14},{13,9},{14,10},{15,13... | collective-permute-start | bytes 1142792 | tf_op jit(solution)/shard_map/ppermute | solution.py:51
  25.1 0.8 %stage.10 = (f32[256,1024]{1,0:T(8,128)S(1)}, f32[128,256]{1,0:T(8,128)S(1)}) custom-call(s32[1]{0:T(128)} %bitcast.me_ref, bf16[1488,128]{1,0:T(8,128)(2,1)S(1)} %collective-permute-done.1.refs_0_.refs_6_, bf16[1488,128]{1,0:T(8,128)(2,1)S(1)} %collective-permute-done.5.refs_1_.refs_7_, ...), custom_call_target="tpu_custom_call", output_to_operand_aliasing={{0}: (10, {}), {1}: (11, {})} | custom-call | flops 167772160 | bytes 2097152 | tf_op jit(solution)/shard_map/stage/pallas_call | solution.py:396
  25.9 1.4 %collective-permute-done.4.block_ref.refs_0_.refs_10_ = bf16[1488,128]{1,0:T(8,128)(2,1)S(1)} collective-permute-done((bf16[1488,128]{1,0:T(8,128)(2,1)S(1)}, bf16[1488,128]{1,0:T(8,128)(2,1)S(1)}, u32[]{:S(2)}, u32[]{:S(2)}) %collective-permute-start.4) | collective-permute-done | bytes 380960 | tf_op jit(solution)/shard_map/ppermute | solution.py:51
  27.4 1.9 %collective-permute-start.8 = (bf16[960,128]{1,0:T(8,128)(2,1)S(1)}, bf16[960,128]{1,0:T(8,128)(2,1)S(1)}, u32[]{:S(2)}, u32[]{:S(2)}) collective-permute-start(bf16[960,128]{1,0:T(8,128)(2,1)S(1)} %get-tuple-element.87), channel_id=1, source_target_pairs={{0,4},{1,3},{4,8},{5,1},{8,12},{9,5},{12,14},{13,9},{14,10},{15,13... | collective-permute-start | bytes 737288 | tf_op jit(solution)/shard_map/ppermute | solution.py:51
  29.3 0.0 collective-permute-done.10.refs_0_.refs_8_
  29.3 0.8 %stage.11 = (f32[256,1024]{1,0:T(8,128)S(1)}, f32[128,256]{1,0:T(8,128)S(1)}) custom-call(s32[1]{0:T(128)} %bitcast.me_ref, bf16[1488,128]{1,0:T(8,128)(2,1)S(1)} %collective-permute-done.10.refs_0_.refs_8_, bf16[1488,128]{1,0:T(8,128)(2,1)S(1)} %collective-permute-done.11.refs_1_.refs_9_, ...), custom_call_target="tpu_custom_call", output_to_operand_aliasing={{0}: (10, {}), {1}: (11, {})} | custom-call | flops 167772160 | bytes 2097152 | tf_op jit(solution)/shard_map/stage/pallas_call | solution.py:396
  30.1 1.3 %collective-permute-done.9.refs_1_.refs_11_ = bf16[1488,128]{1,0:T(8,128)(2,1)S(1)} collective-permute-done((bf16[1488,128]{1,0:T(8,128)(2,1)S(1)}, bf16[1488,128]{1,0:T(8,128)(2,1)S(1)}, u32[]{:S(2)}, u32[]{:S(2)}) %collective-permute-start.9) | collective-permute-done | bytes 380960 | tf_op jit(solution)/shard_map/ppermute | solution.py:51
  31.4 1.9 %collective-permute-start.15 = (bf16[528,128]{1,0:T(8,128)(2,1)S(1)}, bf16[528,128]{1,0:T(8,128)(2,1)S(1)}, u32[]{:S(2)}, u32[]{:S(2)}) collective-permute-start(bf16[528,128]{1,0:T(8,128)(2,1)S(1)} %get-tuple-element.103), channel_id=1, source_target_pairs={{0,4},{1,3},{4,8},{5,1},{8,12},{9,5},{12,14},{13,9},{14,10},{15,13... | collective-permute-start | bytes 405512 | tf_op jit(solution)/shard_map/ppermute | solution.py:51
  33.3 0.8 %stage.12 = (f32[256,1024]{1,0:T(8,128)S(1)}, f32[128,256]{1,0:T(8,128)S(1)}) custom-call(s32[1]{0:T(128)} %bitcast.me_ref, bf16[1488,128]{1,0:T(8,128)(2,1)S(1)} %collective-permute-done.4.block_ref.refs_0_.refs_10_, bf16[1488,128]{1,0:T(8,128)(2,1)S(1)} %collective-permute-done.9.refs_1_.refs_11_, ...), custom_call_target="tpu_custom_call", output_to_operand_aliasing={{0}: (10, {}), {1}: (11, {})} | custom-call | flops 167772160 | bytes 2097152 | tf_op jit(solution)/shard_map/stage/pallas_call | solution.py:396
  34.1 0.0 copy-start
  34.1 0.2 collective-permute-start.12
  34.4 2.1 %collective-permute-done.15.refs_14_ = bf16[528,128]{1,0:T(8,128)(2,1)S(1)} collective-permute-done((bf16[528,128]{1,0:T(8,128)(2,1)S(1)}, bf16[528,128]{1,0:T(8,128)(2,1)S(1)}, u32[]{:S(2)}, u32[]{:S(2)}) %collective-permute-start.15) | collective-permute-done | bytes 135200 | tf_op jit(solution)/shard_map/ppermute | solution.py:51
  36.4 0.8 %stage.13 = (f32[256,1024]{1,0:T(8,128)S(1)}, f32[128,256]{1,0:T(8,128)S(1)}) custom-call(s32[1]{0:T(128)} %bitcast.me_ref, bf16[1488,128]{1,0:T(8,128)(2,1)S(1)} %collective-permute-done.13.refs_0_.refs_12_, bf16[1488,128]{1,0:T(8,128)(2,1)S(1)} %collective-permute-done.14.refs_1_.refs_13_, ...), custom_call_target="tpu_custom_call", output_to_operand_aliasing={{0}: (10, {}), {1}: (11, {})} | custom-call | flops 167772160 | bytes 2097152 | tf_op jit(solution)/shard_map/stage/pallas_call | solution.py:396
  37.3 2.2 %features.1.unit_ref = bf16[128,128]{1,0:T(8,128)(2,1)S(1)} custom-call(s32[1]{0:T(128)} %bitcast.me_ref, s32[1,2]{1,0:T(1,128)S(1)} %copy-done, bf16[960,128]{1,0:T(8,128)(2,1)S(1)} %collective-permute-done.8.refs_1_, bf16[960,128]{1,0:T(8,128)(2,1)S(1)} %collective-permute-done.12.refs_2_, bf16[256,5120]{1,0:T(8,128)(2,1)S(1)} %get-tuple-element.62.refs_2_.refs_3_, ...), custom_call_target="tpu_custom_call" | custom-call | flops 167772160 | bytes 2097152 | tf_op jit(solution)/shard_map/features/pallas_call | solution.py:396
  39.5 1.7 %scores.1 = (f32[2,3]{1,0:T(2,128)}, f32[2]{0:T(128)}) custom-call(bf16[128,128]{1,0:T(8,128)(2,1)S(1)} %features.1.unit_ref, bf16[1488,128]{1,0:T(8,128)(2,1)S(1)} %pack.1.refs_0_, bf16[1488,128]{1,0:T(8,128)(2,1)S(1)} %collective-permute-done.2.refs_1_, bf16[1488,128]{1,0:T(8,128)(2,1)S(1)} %collective-permute-done.refs_0_.refs_2_, ...), custom_call_target="tpu_custom_call" | custom-call | flops 4194304 | bytes 2097152 | tf_op jit(solution)/shard_map/scores/pallas_call | solution.py:457
  (16 shorter events, 0.1 us)
Async XLA Ops:
  2.1 3.2 %collective-permute-start.2 = (bf16[1488,128]{1,0:T(8,128)(2,1)S(1)}, bf16[1488,128]{1,0:T(8,128)(2,1)S(1)}, u32[]{:S(2)}, u32[]{:S(2)}) collective-permute-start(bf16[1488,128]{1,0:T(8,128)(2,1)S(1)} %pack.1.refs_0_), channel_id=1, source_target_pairs={{0,1},{1,0},{2,3},{3,2},{4,5},{5,4},{6,7},{7,6},{8,9},{9,8},{10,11... | collective-permute-start | bytes 1142792 | tf_op jit(solution)/shard_map/ppermute | solution.py:55
  2.6 8.9 %collective-permute-start = (bf16[1488,128]{1,0:T(8,128)(2,1)S(1)}, bf16[1488,128]{1,0:T(8,128)(2,1)S(1)}, u32[]{:S(2)}, u32[]{:S(2)}) collective-permute-start(bf16[1488,128]{1,0:T(8,128)(2,1)S(1)} %pack.1.refs_0_), channel_id=1, source_target_pairs={{0,4},{1,3},{4,8},{5,1},{8,12},{9,5},{12,14},{13,9},{14,10},{15,13... | collective-permute-start | bytes 1142792 | tf_op jit(solution)/shard_map/ppermute | solution.py:51
  5.2 9.6 %collective-permute-start.3 = (bf16[1488,128]{1,0:T(8,128)(2,1)S(1)}, bf16[1488,128]{1,0:T(8,128)(2,1)S(1)}, u32[]{:S(2)}, u32[]{:S(2)}) collective-permute-start(bf16[1488,128]{1,0:T(8,128)(2,1)S(1)} %collective-permute-done.2.refs_1_), channel_id=1, source_target_pairs={{0,4},{1,3},{4,8},{5,1},{8,12},{9,5},{12,14},{13,9},{14,10},{15,13... | collective-permute-start | bytes 1142792 | tf_op jit(solution)/shard_map/ppermute | solution.py:51
  11.5 7.7 %collective-permute-start.1 = (bf16[1488,128]{1,0:T(8,128)(2,1)S(1)}, bf16[1488,128]{1,0:T(8,128)(2,1)S(1)}, u32[]{:S(2)}, u32[]{:S(2)}) collective-permute-start(bf16[1488,128]{1,0:T(8,128)(2,1)S(1)} %collective-permute-done.refs_0_.refs_2_), channel_id=1, source_target_pairs={{0,4},{1,3},{4,8},{5,1},{8,12},{9,5},{12,14},{13,9},{14,10},{15,13... | collective-permute-start | bytes 1142792 | tf_op jit(solution)/shard_map/ppermute | solution.py:51
  13.1 7.9 %collective-permute-start.6 = (bf16[1488,128]{1,0:T(8,128)(2,1)S(1)}, bf16[1488,128]{1,0:T(8,128)(2,1)S(1)}, u32[]{:S(2)}, u32[]{:S(2)}) collective-permute-start(bf16[1488,128]{1,0:T(8,128)(2,1)S(1)} %collective-permute-done.refs_0_.refs_2_), channel_id=1, source_target_pairs={{0,1},{1,0},{2,3},{3,2},{4,5},{5,4},{6,7},{7,6},{8,9},{9,8},{10,11... | collective-permute-start | bytes 1142792 | tf_op jit(solution)/shard_map/ppermute | solution.py:55
  14.9 6.2 %collective-permute-start.7 = (bf16[1488,128]{1,0:T(8,128)(2,1)S(1)}, bf16[1488,128]{1,0:T(8,128)(2,1)S(1)}, u32[]{:S(2)}, u32[]{:S(2)}) collective-permute-start(bf16[1488,128]{1,0:T(8,128)(2,1)S(1)} %collective-permute-done.3.refs_1_.refs_3_), channel_id=1, source_target_pairs={{0,1},{1,0},{2,3},{3,2},{4,5},{5,4},{6,7},{7,6},{8,9},{9,8},{10,11... | collective-permute-start | bytes 1142792 | tf_op jit(solution)/shard_map/ppermute | solution.py:55
  14.9 8.4 %collective-permute-start.5 = (bf16[1488,128]{1,0:T(8,128)(2,1)S(1)}, bf16[1488,128]{1,0:T(8,128)(2,1)S(1)}, u32[]{:S(2)}, u32[]{:S(2)}) collective-permute-start(bf16[1488,128]{1,0:T(8,128)(2,1)S(1)} %collective-permute-done.3.refs_1_.refs_3_), channel_id=1, source_target_pairs={{0,4},{1,3},{4,8},{5,1},{8,12},{9,5},{12,14},{13,9},{14,10},{15,13... | collective-permute-start | bytes 1142792 | tf_op jit(solution)/shard_map/ppermute | solution.py:51
  19.2 8.2 %collective-permute-start.4 = (bf16[1488,128]{1,0:T(8,128)(2,1)S(1)}, bf16[1488,128]{1,0:T(8,128)(2,1)S(1)}, u32[]{:S(2)}, u32[]{:S(2)}) collective-permute-start(bf16[1488,128]{1,0:T(8,128)(2,1)S(1)} %collective-permute-done.1.refs_0_.refs_6_), channel_id=1, source_target_pairs={{0,4},{1,3},{4,8},{5,1},{8,12},{9,5},{12,14},{13,9},{14,10},{15,13... | collective-permute-start | bytes 1142792 | tf_op jit(solution)/shard_map/ppermute | solution.py:51
  21.0 8.3 %collective-permute-start.10 = (bf16[1488,128]{1,0:T(8,128)(2,1)S(1)}, bf16[1488,128]{1,0:T(8,128)(2,1)S(1)}, u32[]{:S(2)}, u32[]{:S(2)}) collective-permute-start(bf16[1488,128]{1,0:T(8,128)(2,1)S(1)} %collective-permute-done.1.refs_0_.refs_6_), channel_id=1, source_target_pairs={{0,1},{1,0},{2,3},{3,2},{4,5},{5,4},{6,7},{7,6},{8,9},{9,8},{10,11... | collective-permute-start | bytes 1142792 | tf_op jit(solution)/shard_map/ppermute | solution.py:55
  23.2 6.0 %collective-permute-start.11 = (bf16[1488,128]{1,0:T(8,128)(2,1)S(1)}, bf16[1488,128]{1,0:T(8,128)(2,1)S(1)}, u32[]{:S(2)}, u32[]{:S(2)}) collective-permute-start(bf16[1488,128]{1,0:T(8,128)(2,1)S(1)} %collective-permute-done.5.refs_1_.refs_7_), channel_id=1, source_target_pairs={{0,1},{1,0},{2,3},{3,2},{4,5},{5,4},{6,7},{7,6},{8,9},{9,8},{10,11... | collective-permute-start | bytes 1142792 | tf_op jit(solution)/shard_map/ppermute | solution.py:55
  23.2 8.2 %collective-permute-start.9 = (bf16[1488,128]{1,0:T(8,128)(2,1)S(1)}, bf16[1488,128]{1,0:T(8,128)(2,1)S(1)}, u32[]{:S(2)}, u32[]{:S(2)}) collective-permute-start(bf16[1488,128]{1,0:T(8,128)(2,1)S(1)} %collective-permute-done.5.refs_1_.refs_7_), channel_id=1, source_target_pairs={{0,4},{1,3},{4,8},{5,1},{8,12},{9,5},{12,14},{13,9},{14,10},{15,13... | collective-permute-start | bytes 1142792 | tf_op jit(solution)/shard_map/ppermute | solution.py:51
  27.4 6.8 %collective-permute-start.8 = (bf16[960,128]{1,0:T(8,128)(2,1)S(1)}, bf16[960,128]{1,0:T(8,128)(2,1)S(1)}, u32[]{:S(2)}, u32[]{:S(2)}) collective-permute-start(bf16[960,128]{1,0:T(8,128)(2,1)S(1)} %get-tuple-element.87), channel_id=1, source_target_pairs={{0,4},{1,3},{4,8},{5,1},{8,12},{9,5},{12,14},{13,9},{14,10},{15,13... | collective-permute-start | bytes 737288 | tf_op jit(solution)/shard_map/ppermute | solution.py:51
  29.3 7.2 %collective-permute-start.13 = (bf16[1488,128]{1,0:T(8,128)(2,1)S(1)}, bf16[1488,128]{1,0:T(8,128)(2,1)S(1)}, u32[]{:S(2)}, u32[]{:S(2)}) collective-permute-start(bf16[1488,128]{1,0:T(8,128)(2,1)S(1)} %collective-permute-done.4.block_ref.refs_0_.refs_10_), channel_id=1, source_target_pairs={{0,1},{1,0},{2,3},{3,2},{4,5},{5,4},{6,7},{7,6},{8,9},{9,8},{10,11... | collective-permute-start | bytes 1142792 | tf_op jit(solution)/shard_map/ppermute | solution.py:55
  31.4 5.0 %collective-permute-start.14 = (bf16[1488,128]{1,0:T(8,128)(2,1)S(1)}, bf16[1488,128]{1,0:T(8,128)(2,1)S(1)}, u32[]{:S(2)}, u32[]{:S(2)}) collective-permute-start(bf16[1488,128]{1,0:T(8,128)(2,1)S(1)} %collective-permute-done.9.refs_1_.refs_11_), channel_id=1, source_target_pairs={{0,1},{1,0},{2,3},{3,2},{4,5},{5,4},{6,7},{7,6},{8,9},{9,8},{10,11... | collective-permute-start | bytes 1142792 | tf_op jit(solution)/shard_map/ppermute | solution.py:55
  31.4 5.0 %collective-permute-start.15 = (bf16[528,128]{1,0:T(8,128)(2,1)S(1)}, bf16[528,128]{1,0:T(8,128)(2,1)S(1)}, u32[]{:S(2)}, u32[]{:S(2)}) collective-permute-start(bf16[528,128]{1,0:T(8,128)(2,1)S(1)} %get-tuple-element.103), channel_id=1, source_target_pairs={{0,4},{1,3},{4,8},{5,1},{8,12},{9,5},{12,14},{13,9},{14,10},{15,13... | collective-permute-start | bytes 405512 | tf_op jit(solution)/shard_map/ppermute | solution.py:51
  34.1 3.2 %copy-start = (s32[1,2]{1,0:T(1,128)S(1)}, s32[1,2]{1,0:T(1,128)}, u32[]{:S(2)}) copy-start(s32[1,2]{1,0:T(1,128)} %refs_0_.3) | copy-start | bytes 28
  34.1 3.1 %collective-permute-start.12 = (bf16[960,128]{1,0:T(8,128)(2,1)S(1)}, bf16[960,128]{1,0:T(8,128)(2,1)S(1)}, u32[]{:S(2)}, u32[]{:S(2)}) collective-permute-start(bf16[960,128]{1,0:T(8,128)(2,1)S(1)} %collective-permute-done.8.refs_1_), channel_id=1, source_target_pairs={{0,1},{1,0},{2,3},{3,2},{4,5},{5,4},{6,7},{7,6},{8,9},{9,8},{10,11... | collective-permute-start | bytes 737288 | tf_op jit(solution)/shard_map/ppermute | solution.py:55
  36.4 3.1 %collective-permute-start.16 = (bf16[528,128]{1,0:T(8,128)(2,1)S(1)}, bf16[528,128]{1,0:T(8,128)(2,1)S(1)}, u32[]{:S(2)}, u32[]{:S(2)}) collective-permute-start(bf16[528,128]{1,0:T(8,128)(2,1)S(1)} %collective-permute-done.15.refs_14_), channel_id=1, source_target_pairs={{0,1},{1,0},{2,3},{3,2},{4,5},{5,4},{6,7},{7,6},{8,9},{9,8},{10,11... | collective-permute-start | bytes 405512 | tf_op jit(solution)/shard_map/ppermute | solution.py:55

commit v7 on v6

--- a/solution.py
+++ b/solution.py
@@ -41,13 +41,14 @@
     return jnp.where(side == 0, row, RING_CHIPS - 1 - row)
 
 
-def hop(value):
+def hop(value, from_other=False):
     half = RING_CHIPS // 2
     place = [2 * q if q < half else 2 * (RING_CHIPS - 1 - q) + 1 for q in range(RING_CHIPS)]
+    turn = int(from_other)
     pairs = []
     for q in range(RING_CHIPS):
-        pairs.append((2 * place[q], 2 * place[(q + 1) % RING_CHIPS]))
-        pairs.append((2 * place[q] + 1, 2 * place[(q - 1) % RING_CHIPS] + 1))
+        pairs.append((2 * place[q] + turn, 2 * place[(q + 1) % RING_CHIPS]))
+        pairs.append((2 * place[q] + 1 - turn, 2 * place[(q - 1) % RING_CHIPS] + 1))
     return lax.ppermute(value, "dp", pairs)
 
 
@@ -155,26 +156,16 @@
         copy.wait()
 
 
-def stage_kernel(away, first, last, me_ref, *refs):
+def stage_kernel(away, first, me_ref, *refs):
     refs = list(refs)
     take = lambda k: [refs.pop(0) for _ in range(k)]
-    counts_ref = take(1)[0] if last else None
     pieces = take(2)
     x_ref, mixed_ref, adjoint_ref, values_ref, target_ref, top_target_ref, source_ref = take(7)
     old_sums, old_bridge = (None, None) if first else take(2)
-    local_ref, expand_hbm, sketch_hbm = take(3) if last else (None, None, None)
-    if last:
-        (out_ref,) = take(1)
-    else:
-        new_sums, new_bridge = take(2)
-    both, up, down, expand_ref, sketch_ref, sems = refs
+    new_sums, new_bridge, both, up, down = refs
     rows = both.shape[0] // 2
     half, pad = rows // 2, LANES // 2
-    tokens, width = x_ref.shape
     span = 2 * rows
-    if last:
-        more = load(((expand_hbm, expand_ref), (sketch_hbm, sketch_ref)), sems)
-
     me = me_ref[0]
     pos, core = ring_pos(me // 2), me % 2
     chip = ring_chip((pos + away * (2 * core - 1) + RING_CHIPS) % RING_CHIPS)
@@ -216,15 +207,21 @@
     if not first:
         products = [p + old_sums[:, i * LANES : (i + 1) * LANES] for i, p in enumerate(products)]
         bridge = bridge + old_bridge[...]
-    if not last:
-        for i in range(SUMS):
-            new_sums[:, i * LANES : (i + 1) * LANES] = products[i]
-        new_bridge[...] = bridge
-        return
-
+    for i in range(SUMS):
+        new_sums[:, i * LANES : (i + 1) * LANES] = products[i]
+    new_bridge[...] = bridge
+
+
+def feature_kernel(width, counts_ref, sums_ref, bridge_ref, local_ref, expand_hbm, sketch_hbm, out_ref, *scratch):
+    expand_ref, sketch_ref, sems = scratch
+    more = load(((expand_hbm, expand_ref), (sketch_hbm, sketch_ref)), sems)
+    tokens = sums_ref.shape[0]
+    pad = LANES // 2
+    products = [sums_ref[:, i * LANES : (i + 1) * LANES] for i in range(SUMS)]
+    local = [local_ref[:, i * LANES : (i + 1) * LANES] for i in range(LOCAL_SUMS)]
+    bridge = bridge_ref[...]
     for copy in more:
         copy.wait()
-    local = [local_ref[:, i * LANES : (i + 1) * LANES] for i in range(LOCAL_SUMS)]
     inverse = local[INVERSE]
     reduced = inverse * products[X_DOWN]
     expand = expand_ref[...]
@@ -247,41 +244,32 @@
     for e in range(2):
         own = feats[e * pad : (e + 1) * pad]
         squares = jnp.sum(own * own, keepdims=True)
-        out_ref[pl.ds(e * pad, pad), :] = (own * lax.rsqrt(squares + 1e-06)).astype(BF16)
-
-
-def split_kernel(block_ref, head_ref, tail_ref):
-    cut = head_ref.shape[0]
-    head_ref[...] = block_ref[pl.ds(0, cut), :]
-    tail_ref[...] = block_ref[pl.ds(cut, tail_ref.shape[0]), :]
-
-
-def best_of(block, count, spread, best):
+        out_ref[pl.ds(e * pad, pad), :] = (own * lax.rsqrt(squares + 1e-06)).astype(BF16).astype(F32)
+
+
+def score_kernel(blocks, count, unit_ref, *refs):
+    block_refs, (out_ref, mean_ref) = refs[:blocks], refs[blocks:]
     half = LANES // 2
     scale = float(half * LANES) ** 0.5
-    at = block.shape[0] - (half + 2) * count
-    wide = block[pl.ds(at, half * count), :].astype(F32)
-    labels = block[pl.ds(at + half * count, 2 * count), :].astype(F32)[:count]
-    for e in range(2):
-        products = wide * spread[e]
-        total = jnp.sum(products.reshape(half, count, LANES), axis=0)
-        similar = scale * jnp.sum(total, axis=1, keepdims=True)
-        for t in range(TASKS):
-            here = jnp.where(labels == float(t), similar, -2.0 * scale)
-            best[e][t] = jnp.maximum(best[e][t], here)
-
-
-def score_kernel(blocks, count, unit_ref, *refs):
-    block_refs, (out_ref, mean_ref, spread) = refs[:blocks], refs[blocks:]
-    half = LANES // 2
-    scale = float(half * LANES) ** 0.5
-    for e in range(2):
-        for i in range(half):
-            row = unit_ref[pl.ds(e * half + i, 1), :].astype(F32)
-            spread[e, pl.ds(i * count, count), :] = jnp.broadcast_to(row, (count, LANES))
-    best = [[jnp.full((count, LANES), -2.0 * scale, F32) for _ in range(TASKS)] for _ in range(2)]
-    for block in block_refs:
-        best_of(block, count, spread, best)
+    starts = [block.shape[0] - (half + 2) * count for block in block_refs]
+    shape = (count, LANES)
+    totals = [[jnp.zeros(shape, F32) for _ in range(2)] for _ in block_refs]
+    for i in range(0, half, 2):
+        units = [
+            [jnp.broadcast_to(unit_ref[pl.ds(e * half + i + k, 1), :], shape) for k in range(2)]
+            for e in range(2)
+        ]
+        for b, block in enumerate(block_refs):
+            wide = block[pl.ds(starts[b] + i * count, 2 * count), :].astype(F32)
+            for e in range(2):
+                totals[b][e] = totals[b][e] + (wide[:count] * units[e][0] + wide[count:] * units[e][1])
+    best = [[jnp.full(shape, -2.0 * scale, F32) for _ in range(TASKS)] for _ in range(2)]
+    for b, block in enumerate(block_refs):
+        labels = block[pl.ds(starts[b] + half * count, 2 * count), :].astype(F32)[:count]
+        for e in range(2):
+            similar = scale * jnp.sum(totals[b][e], axis=1, keepdims=True)
+            for t in range(TASKS):
+                best[e][t] = jnp.maximum(best[e][t], jnp.where(labels == float(t), similar, -2.0 * scale))
     for e in range(2):
         values = [jnp.max(best[e][t]) for t in range(TASKS)]
         for t in range(TASKS):
@@ -387,52 +375,33 @@
         name="local_products",
     )(*in_hbm(inputs))
 
-    def stage(away, pieces, sums, local=None):
-        first, last = not sums, local is not None
-        sums_shape, bridge_shape = (tokens, SUMS * LANES), (LANES, 2 * LANES)
-        small = (top_expander_sketch.T, top_reducer_sketch)
-        head = [me.reshape(1)] + ([sequence_token_counts] if last else [])
-        start = len(head) + len(pieces) + len(activations)
+    def stage(away, pieces, sums):
+        first = not sums
+        start = 1 + len(pieces) + len(activations)
         return pl.pallas_call(
-            functools.partial(stage_kernel, away, first, last),
-            out_shape=jax.ShapeDtypeStruct((LANES, LANES), BF16)
-            if last
-            else [jax.ShapeDtypeStruct(sums_shape, F32), jax.ShapeDtypeStruct(bridge_shape, F32)],
-            in_specs=[SMEM] * len(head)
-            + [VMEM] * (len(pieces) + len(activations) + len(sums))
-            + ([VMEM, HBM, HBM] if last else []),
-            out_specs=VMEM if last else [VMEM, VMEM],
+            functools.partial(stage_kernel, away, first),
+            out_shape=[
+                jax.ShapeDtypeStruct((tokens, SUMS * LANES), F32),
+                jax.ShapeDtypeStruct((LANES, 2 * LANES), F32),
+            ],
+            in_specs=[SMEM] + [VMEM] * (len(pieces) + len(activations) + len(sums)),
+            out_specs=[VMEM, VMEM],
             scratch_shapes=[
                 pltpu.VMEM((2 * rows, 2 * LANES), BF16),
                 pltpu.VMEM((rows + LANES // 2, 2 * LANES), BF16),
                 pltpu.VMEM((2 * rows, LANES), BF16),
-                pltpu.VMEM(small[0].shape, BF16),
-                pltpu.VMEM(small[1].shape, BF16),
-                pltpu.SemaphoreType.DMA((2,)),
             ],
-            input_output_aliases={} if first or last else {start: 0, start + 1: 1},
+            input_output_aliases={} if first else {start: 0, start + 1: 1},
             compiler_params=params(16),
             cost_estimate=cost(tokens * rows * LANES * 16, 2 * MIB),
-            name="features" if last else "stage",
-        )(*head, *pieces, *activations, *sums, *((local, *in_hbm(small)) if last else ()))
-
-    def split(block):
-        shapes = (3 * rows, LANES), (block.shape[0] - 3 * rows, LANES)
-        return pl.pallas_call(
-            split_kernel,
-            out_shape=[jax.ShapeDtypeStruct(shape, BF16) for shape in shapes],
-            in_specs=[VMEM],
-            out_specs=[VMEM, VMEM],
-            compiler_params=params(8),
-            name="split",
-        )(block)
+            name="stage",
+        )(me.reshape(1), *pieces, *activations, *sums)
 
     tie = lax.optimization_barrier
     half = RING_CHIPS // 2
-    first, second = own, other_core(own)
-    blocks = [first, second]
-    held = [first, second]
-    first, second = hop(first), hop(second)
+    held = [own, other_core(own)]
+    blocks = list(held)
+    first, second = hop(own), hop(own, from_other=True)
     first, activations = tie((first, activations))
     sums = stage(0, held, [])
     second, sums = tie((second, sums))
@@ -440,9 +409,6 @@
         held = [first, second]
         crossed = [other_core(first), other_core(second)]
         blocks += held + crossed
-        if k == half - 1:
-            first, panel = split(first)
-            panel = hop(panel)
         first = hop(first)
         sums = stage(k, held, sums)
         first, sums = tie((first, sums))
@@ -451,15 +417,26 @@
         sums = stage(-k, crossed, sums)
         if k < half - 1:
             second, sums = tie((second, sums))
-    unit = stage(half, [first, other_core(first)], sums, local)
-    blocks += [panel, other_core(panel)]
+    held = [first, other_core(first)]
+    blocks += held
+    sums = stage(half, held, sums)
+    small = (top_expander_sketch.T, top_reducer_sketch)
+    unit = pl.pallas_call(
+        functools.partial(feature_kernel, width),
+        out_shape=jax.ShapeDtypeStruct((LANES, LANES), F32),
+        in_specs=[SMEM] + [VMEM] * 3 + [HBM] * 2,
+        out_specs=VMEM,
+        scratch_shapes=[pltpu.VMEM(a.shape, a.dtype) for a in small] + [pltpu.SemaphoreType.DMA((2,))],
+        compiler_params=params(16),
+        cost_estimate=cost(tokens * LANES * LANES * 20, 4 * MIB),
+        name="features",
+    )(sequence_token_counts, *sums, local, *in_hbm(small))
 
     task_best, scores = pl.pallas_call(
         functools.partial(score_kernel, len(blocks), count),
         out_shape=(jax.ShapeDtypeStruct((2, TASKS), F32), jax.ShapeDtypeStruct((2,), F32)),
         in_specs=[VMEM] * (1 + len(blocks)),
         out_specs=(SMEM, SMEM),
-        scratch_shapes=[pltpu.VMEM((2, LANES // 2 * count, LANES), F32)],
         compiler_params=params(16),
         cost_estimate=cost(4 * MIB, 2 * MIB),
         name="scores",

time: 41.5 us -> 44.7 us (1.077)
  waiting for transfers between devices: 8.52 us -> 14.5 us
  starting transfers between devices: 16.2 us -> 13.1 us
    ppermute x8 -> x7, waiting for transfers between devices: 8.5 us -> 13.6 us  [hop(): return lax.ppermute(value, 'dp', pairs)]
    ppermute x8 -> x7, starting transfers between devices: 15.4 us -> 12.5 us  [hop(): return lax.ppermute(value, 'dp', pairs)]
    ppermute x9 -> x8, waiting for transfers between devices: 0.02 us -> 0.9 us  [other_core(): lax.ppermute(value, 'dp', [(d, d ^ 1) for d in range(2 * RING_CHIPS)])]
  transfers between devices with their start and end apart: 17 -> 15, of which waited for: 6 -> 7; matrix products, arithmetic and copies ran while one was open for 0% -> 0% of each run, Pallas kernels for 31% -> 23%
where the time goes in v7:
time: 44.7 us; the launch traced here: 44.4 us
  Pallas kernels  16 us (36%)
  waiting for transfers between devices  14.5 us (32%)
  starting transfers between devices  13.1 us (29%)
  between operations  0.76 us (2%)
    ppermute x7, waiting for transfers between devices, hop(): return lax.ppermute(value, 'dp', pairs)  13.6 us
    ppermute x7, starting transfers between devices, hop(): return lax.ppermute(value, 'dp', pairs)  12.5 us
    pallas_call x8, Pallas kernels, stage(): pl.pallas_call(functools.partial(stage_kernel, away, first), out_shape=[j...  6.41 us
    pallas_call x1, Pallas kernels, shards(): pl.pallas_call(local_kernel, out_shape=[jax.ShapeDtypeStruct(a.shape, a.d...  4.6 us
    pallas_call x1, Pallas kernels, shards(): pl.pallas_call(functools.partial(feature_kernel, width), out_shape=jax.Sh...  1.89 us
    pallas_call x1, Pallas kernels, shards(): pl.pallas_call(functools.partial(score_kernel, len(blocks), count), out_s...  1.67 us
    pallas_call x1, Pallas kernels, shards(): pl.pallas_call(pack_kernel, out_shape=jax.ShapeDtypeStruct((3 * rows + (L...  1.41 us
    ppermute x8, waiting for transfers between devices, other_core(): lax.ppermute(value, 'dp', [(d, d ^ 1) for d in range(2 * RING_CHIPS)])  0.9 us
  transfers between devices with their start and end apart: 15, of which 7 were waited for; matrix products, arithmetic and copies ran while one was open for 0% of the time, Pallas kernels for 23%

profile of v7, /device:TPU:0, one launch (start us, length us, event | category | flops | bytes accessed | tf_op | source)
XLA Modules:
  0.0 44.4 jit_solution(12882438667110176384)
XLA Ops:
  0.6 1.4 %pack.1.refs_0_ = bf16[1488,128]{1,0:T(8,128)(2,1)S(1)} custom-call(s32[1]{0:T(128)} %bitcast.me_ref, f32[40,128]{1,0:T(8,128)} %bitcast.10, bf16[320,128]{1,0:T(8,128)(2,1)} %refs_1_.2, bf16[320,128]{1,0:T(8,128)(2,1)} %bitcast.12, bf16[128,128]{1,0:T(8,128)(2,1)} %refs_3_.2, bf16[160,128]{1,0:T(8,128)(2,1)} %bitcast.13, bf16[320,128]{1,0:T(8,128)(2,1)} %refs_5_.2, ...), custom_call_target="tpu_custom_call" | custom-call | tf_op jit(solution)/shard_map/pack/pallas_call | solution.py:341
  2.1 3.1 %collective-permute-start = (bf16[1488,128]{1,0:T(8,128)(2,1)S(1)}, bf16[1488,128]{1,0:T(8,128)(2,1)S(1)}, u32[]{:S(2)}, u32[]{:S(2)}) collective-permute-start(bf16[1488,128]{1,0:T(8,128)(2,1)S(1)} %pack.1.refs_0_), channel_id=1, source_target_pairs={{0,4},{1,3},{4,8},{5,1},{8,12},{9,5},{12,14},{13,9},{14,10},{15,13... | collective-permute-start | bytes 1142792 | tf_op jit(solution)/shard_map/ppermute | solution.py:52
  5.1 0.0 collective-permute-start.3
  5.1 0.7 %collective-permute-start.2 = (bf16[1488,128]{1,0:T(8,128)(2,1)S(1)}, bf16[1488,128]{1,0:T(8,128)(2,1)S(1)}, u32[]{:S(2)}, u32[]{:S(2)}) collective-permute-start(bf16[1488,128]{1,0:T(8,128)(2,1)S(1)} %pack.1.refs_0_), channel_id=1, source_target_pairs={{1,4},{0,3},{5,8},{4,1},{9,12},{8,5},{13,14},{12,9},{15,10},{14,13... | collective-permute-start | bytes 1142792 | tf_op jit(solution)/shard_map/ppermute | solution.py:52
  5.8 4.6 %local_products.1 = (bf16[256,5120]{1,0:T(8,128)(2,1)S(1)}, bf16[256,5120]{1,0:T(8,128)(2,1)S(1)}, bf16[256,5120]{1,0:T(8,128)(2,1)S(1)}, bf16[256,2560]{1,0:T(8...) custom-call(bf16[256,5120]{1,0:T(8,128)(2,1)} %refs_0_.1, ...), custom_call_target="tpu_custom_call" | custom-call | flops 1006632960 | bytes 14680064 | tf_op jit(solution)/shard_map/local_products/pallas_call | solution.py:362
  10.4 3.0 %collective-permute-done.refs_0_.refs_2_ = bf16[1488,128]{1,0:T(8,128)(2,1)S(1)} collective-permute-done((bf16[1488,128]{1,0:T(8,128)(2,1)S(1)}, bf16[1488,128]{1,0:T(8,128)(2,1)S(1)}, u32[]{:S(2)}, u32[]{:S(2)}) %collective-permute-start) | collective-permute-done | bytes 380960 | tf_op jit(solution)/shard_map/ppermute | solution.py:52
  13.4 2.5 %collective-permute-start.1 = (bf16[1488,128]{1,0:T(8,128)(2,1)S(1)}, bf16[1488,128]{1,0:T(8,128)(2,1)S(1)}, u32[]{:S(2)}, u32[]{:S(2)}) collective-permute-start(bf16[1488,128]{1,0:T(8,128)(2,1)S(1)} %collective-permute-done.refs_0_.refs_2_), channel_id=1, source_target_pairs={{0,4},{1,3},{4,8},{5,1},{8,12},{9,5},{12,14},{13,9},{14,10},{15,13... | collective-permute-start | bytes 1142792 | tf_op jit(solution)/shard_map/ppermute | solution.py:52
  15.8 0.0 collective-permute-start.6
  15.9 0.0 collective-permute-done.3.refs_1_
  15.9 0.7 %stage.8 = (f32[256,1024]{1,0:T(8,128)S(1)}, f32[128,256]{1,0:T(8,128)S(1)}) custom-call(s32[1]{0:T(128)} %bitcast.me_ref, bf16[1488,128]{1,0:T(8,128)(2,1)S(1)} %pack.1.refs_0_, bf16[1488,128]{1,0:T(8,128)(2,1)S(1)} %collective-permute-done.3.refs_1_, bf16[256,5120]{1,0:T(8,128)(2,1)S(1)} %get-tuple-element.62.refs_2_, ...), custom_call_target="tpu_custom_call" | custom-call | flops 167772160 | bytes 2097152 | tf_op jit(solution)/shard_map/stage/pallas_call | solution.py:381
  16.6 0.6 %collective-permute-start.7 = (bf16[1488,128]{1,0:T(8,128)(2,1)S(1)}, bf16[1488,128]{1,0:T(8,128)(2,1)S(1)}, u32[]{:S(2)}, u32[]{:S(2)}) collective-permute-start(bf16[1488,128]{1,0:T(8,128)(2,1)S(1)} %collective-permute-done.2.refs_1_.refs_3_), channel_id=1, source_target_pairs={{0,1},{1,0},{2,3},{3,2},{4,5},{5,4},{6,7},{7,6},{8,9},{9,8},{10,11... | collective-permute-start | bytes 1142792 | tf_op jit(solution)/shard_map/ppermute | solution.py:56
  17.1 1.6 %collective-permute-start.5 = (bf16[1488,128]{1,0:T(8,128)(2,1)S(1)}, bf16[1488,128]{1,0:T(8,128)(2,1)S(1)}, u32[]{:S(2)}, u32[]{:S(2)}) collective-permute-start(bf16[1488,128]{1,0:T(8,128)(2,1)S(1)} %collective-permute-done.2.refs_1_.refs_3_), channel_id=1, source_target_pairs={{0,4},{1,3},{4,8},{5,1},{8,12},{9,5},{12,14},{13,9},{14,10},{15,13... | collective-permute-start | bytes 1142792 | tf_op jit(solution)/shard_map/ppermute | solution.py:52
  18.7 0.8 %stage.9 = (f32[256,1024]{1,0:T(8,128)S(1)}, f32[128,256]{1,0:T(8,128)S(1)}) custom-call(s32[1]{0:T(128)} %bitcast.me_ref, bf16[1488,128]{1,0:T(8,128)(2,1)S(1)} %collective-permute-done.refs_0_.refs_2_, bf16[1488,128]{1,0:T(8,128)(2,1)S(1)} %collective-permute-done.2.refs_1_.refs_3_, ...), custom_call_target="tpu_custom_call", output_to_operand_aliasing={{0}: (10, {}), {1}: (11, {})} | custom-call | flops 167772160 | bytes 2097152 | tf_op jit(solution)/shard_map/stage/pallas_call | solution.py:381
  19.6 2.4 %collective-permute-done.1.refs_0_.refs_6_ = bf16[1488,128]{1,0:T(8,128)(2,1)S(1)} collective-permute-done((bf16[1488,128]{1,0:T(8,128)(2,1)S(1)}, bf16[1488,128]{1,0:T(8,128)(2,1)S(1)}, u32[]{:S(2)}, u32[]{:S(2)}) %collective-permute-start.1) | collective-permute-done | bytes 380960 | tf_op jit(solution)/shard_map/ppermute | solution.py:52
  21.9 1.6 %collective-permute-start.4 = (bf16[1488,128]{1,0:T(8,128)(2,1)S(1)}, bf16[1488,128]{1,0:T(8,128)(2,1)S(1)}, u32[]{:S(2)}, u32[]{:S(2)}) collective-permute-start(bf16[1488,128]{1,0:T(8,128)(2,1)S(1)} %collective-permute-done.1.refs_0_.refs_6_), channel_id=1, source_target_pairs={{0,4},{1,3},{4,8},{5,1},{8,12},{9,5},{12,14},{13,9},{14,10},{15,13... | collective-permute-start | bytes 1142792 | tf_op jit(solution)/shard_map/ppermute | solution.py:52
  23.5 0.0 collective-permute-done.7.refs_1_.refs_5_
  23.5 0.8 %stage.10 = (f32[256,1024]{1,0:T(8,128)S(1)}, f32[128,256]{1,0:T(8,128)S(1)}) custom-call(s32[1]{0:T(128)} %bitcast.me_ref, bf16[1488,128]{1,0:T(8,128)(2,1)S(1)} %collective-permute-done.6.refs_0_.refs_4_, bf16[1488,128]{1,0:T(8,128)(2,1)S(1)} %collective-permute-done.7.refs_1_.refs_5_, ...), custom_call_target="tpu_custom_call", output_to_operand_aliasing={{0}: (10, {}), {1}: (11, {})} | custom-call | flops 167772160 | bytes 2097152 | tf_op jit(solution)/shard_map/stage/pallas_call | solution.py:381
  24.3 1.7 %collective-permute-done.5.refs_1_.refs_7_ = bf16[1488,128]{1,0:T(8,128)(2,1)S(1)} collective-permute-done((bf16[1488,128]{1,0:T(8,128)(2,1)S(1)}, bf16[1488,128]{1,0:T(8,128)(2,1)S(1)}, u32[]{:S(2)}, u32[]{:S(2)}) %collective-permute-start.5) | collective-permute-done | bytes 380960 | tf_op jit(solution)/shard_map/ppermute | solution.py:52
  26.0 1.6 %collective-permute-start.9 = (bf16[1488,128]{1,0:T(8,128)(2,1)S(1)}, bf16[1488,128]{1,0:T(8,128)(2,1)S(1)}, u32[]{:S(2)}, u32[]{:S(2)}) collective-permute-start(bf16[1488,128]{1,0:T(8,128)(2,1)S(1)} %collective-permute-done.5.refs_1_.refs_7_), channel_id=1, source_target_pairs={{0,4},{1,3},{4,8},{5,1},{8,12},{9,5},{12,14},{13,9},{14,10},{15,13... | collective-permute-start | bytes 1142792 | tf_op jit(solution)/shard_map/ppermute | solution.py:52
  27.6 0.8 %stage.11 = (f32[256,1024]{1,0:T(8,128)S(1)}, f32[128,256]{1,0:T(8,128)S(1)}) custom-call(s32[1]{0:T(128)} %bitcast.me_ref, bf16[1488,128]{1,0:T(8,128)(2,1)S(1)} %collective-permute-done.1.refs_0_.refs_6_, bf16[1488,128]{1,0:T(8,128)(2,1)S(1)} %collective-permute-done.5.refs_1_.refs_7_, ...), custom_call_target="tpu_custom_call", output_to_operand_aliasing={{0}: (10, {}), {1}: (11, {})} | custom-call | flops 167772160 | bytes 2097152 | tf_op jit(solution)/shard_map/stage/pallas_call | solution.py:381
  28.4 1.7 %collective-permute-done.4.refs_0_.refs_10_ = bf16[1488,128]{1,0:T(8,128)(2,1)S(1)} collective-permute-done((bf16[1488,128]{1,0:T(8,128)(2,1)S(1)}, bf16[1488,128]{1,0:T(8,128)(2,1)S(1)}, u32[]{:S(2)}, u32[]{:S(2)}) %collective-permute-start.4) | collective-permute-done | bytes 380960 | tf_op jit(solution)/shard_map/ppermute | solution.py:52
  30.1 1.6 %collective-permute-start.8 = (bf16[1488,128]{1,0:T(8,128)(2,1)S(1)}, bf16[1488,128]{1,0:T(8,128)(2,1)S(1)}, u32[]{:S(2)}, u32[]{:S(2)}) collective-permute-start(bf16[1488,128]{1,0:T(8,128)(2,1)S(1)} %collective-permute-done.4.refs_0_.refs_10_), channel_id=1, source_target_pairs={{0,4},{1,3},{4,8},{5,1},{8,12},{9,5},{12,14},{13,9},{14,10},{15,13... | collective-permute-start | bytes 1142792 | tf_op jit(solution)/shard_map/ppermute | solution.py:52
  31.7 0.0 collective-permute-done.10.refs_0_.refs_8_
  31.7 0.8 %stage.12 = (f32[256,1024]{1,0:T(8,128)S(1)}, f32[128,256]{1,0:T(8,128)S(1)}) custom-call(s32[1]{0:T(128)} %bitcast.me_ref, bf16[1488,128]{1,0:T(8,128)(2,1)S(1)} %collective-permute-done.10.refs_0_.refs_8_, bf16[1488,128]{1,0:T(8,128)(2,1)S(1)} %collective-permute-done.11.refs_1_.refs_9_, ...), custom_call_target="tpu_custom_call", output_to_operand_aliasing={{0}: (10, {}), {1}: (11, {})} | custom-call | flops 167772160 | bytes 2097152 | tf_op jit(solution)/shard_map/stage/pallas_call | solution.py:381
  32.5 1.7 %collective-permute-done.9.refs_1_.refs_11_ = bf16[1488,128]{1,0:T(8,128)(2,1)S(1)} collective-permute-done((bf16[1488,128]{1,0:T(8,128)(2,1)S(1)}, bf16[1488,128]{1,0:T(8,128)(2,1)S(1)}, u32[]{:S(2)}, u32[]{:S(2)}) %collective-permute-start.9) | collective-permute-done | bytes 380960 | tf_op jit(solution)/shard_map/ppermute | solution.py:52
  34.2 0.8 %stage.13 = (f32[256,1024]{1,0:T(8,128)S(1)}, f32[128,256]{1,0:T(8,128)S(1)}) custom-call(s32[1]{0:T(128)} %bitcast.me_ref, bf16[1488,128]{1,0:T(8,128)(2,1)S(1)} %collective-permute-done.4.refs_0_.refs_10_, bf16[1488,128]{1,0:T(8,128)(2,1)S(1)} %collective-permute-done.9.refs_1_.refs_11_, ...), custom_call_target="tpu_custom_call", output_to_operand_aliasing={{0}: (10, {}), {1}: (11, {})} | custom-call | flops 167772160 | bytes 2097152 | tf_op jit(solution)/shard_map/stage/pallas_call | solution.py:381
  35.0 3.3 %collective-permute-done.8.refs_0_.refs_14_ = bf16[1488,128]{1,0:T(8,128)(2,1)S(1)} collective-permute-done((bf16[1488,128]{1,0:T(8,128)(2,1)S(1)}, bf16[1488,128]{1,0:T(8,128)(2,1)S(1)}, u32[]{:S(2)}, u32[]{:S(2)}) %collective-permute-start.8) | collective-permute-done | bytes 380960 | tf_op jit(solution)/shard_map/ppermute | solution.py:52
  38.3 0.8 %stage.14 = (f32[256,1024]{1,0:T(8,128)S(1)}, f32[128,256]{1,0:T(8,128)S(1)}) custom-call(s32[1]{0:T(128)} %bitcast.me_ref, bf16[1488,128]{1,0:T(8,128)(2,1)S(1)} %collective-permute-done.13.refs_0_.refs_12_, bf16[1488,128]{1,0:T(8,128)(2,1)S(1)} %collective-permute-done.14.refs_1_.refs_13_, ...), custom_call_target="tpu_custom_call", output_to_operand_aliasing={{0}: (10, {}), {1}: (11, {})} | custom-call | flops 167772160 | bytes 2097152 | tf_op jit(solution)/shard_map/stage/pallas_call | solution.py:381
  39.1 0.9 %collective-permute-done.12.refs_1_.refs_15_ = bf16[1488,128]{1,0:T(8,128)(2,1)S(1)} collective-permute-done((bf16[1488,128]{1,0:T(8,128)(2,1)S(1)}, bf16[1488,128]{1,0:T(8,128)(2,1)S(1)}, u32[]{:S(2)}, u32[]{:S(2)}) %collective-permute-start.12) | collective-permute-done | bytes 380960 | tf_op jit(solution)/shard_map/ppermute | solution.py:56
  40.0 0.8 %stage.15 = (f32[256,1024]{1,0:T(8,128)S(1)}, f32[128,256]{1,0:T(8,128)S(1)}) custom-call(s32[1]{0:T(128)} %bitcast.me_ref, bf16[1488,128]{1,0:T(8,128)(2,1)S(1)} %collective-permute-done.8.refs_0_.refs_14_, bf16[1488,128]{1,0:T(8,128)(2,1)S(1)} %collective-permute-done.12.refs_1_.refs_15_, ...), custom_call_target="tpu_custom_call", output_to_operand_aliasing={{0}: (10, {}), {1}: (11, {})} | custom-call | flops 167772160 | bytes 2097152 | tf_op jit(solution)/shard_map/stage/pallas_call | solution.py:381
  40.8 1.9 %features.1.unit_ref = f32[128,128]{1,0:T(8,128)S(1)} custom-call(s32[1,2]{1,0:T(1,128)S(1)} %copy-done, f32[256,1024]{1,0:T(8,128)S(1)} %get-tuple-element.101.sums_ref, f32[128,256]{1,0:T(8,128)S(1)} %get-tuple-element.102.bridge_ref, f32[256,384]{1,0:T(8,128)S(1)} %get-tuple-element.103.local_ref, bf16[64,128]{1,0:T(8,128)(2,1)} %bitcast.14, ...), custom_call_target="tpu_custom_call" | custom-call | flops 83886080 | bytes 4194304 | tf_op jit(solution)/shard_map/features/pallas_call | solution.py:424
  42.7 1.7 %scores.1 = (f32[2,3]{1,0:T(2,128)}, f32[2]{0:T(128)}) custom-call(f32[128,128]{1,0:T(8,128)S(1)} %features.1.unit_ref, bf16[1488,128]{1,0:T(8,128)(2,1)S(1)} %pack.1.refs_0_, bf16[1488,128]{1,0:T(8,128)(2,1)S(1)} %collective-permute-done.3.refs_1_, bf16[1488,128]{1,0:T(8,128)(2,1)S(1)} %collective-permute-done.refs_0_.refs_2_, ...), custom_call_target="tpu_custom_call" | custom-call | flops 4194304 | bytes 2097152 | tf_op jit(solution)/shard_map/scores/pallas_call | solution.py:435
  (12 shorter events, 0.0 us)
Async XLA Ops:
  2.1 11.3 %collective-permute-start = (bf16[1488,128]{1,0:T(8,128)(2,1)S(1)}, bf16[1488,128]{1,0:T(8,128)(2,1)S(1)}, u32[]{:S(2)}, u32[]{:S(2)}) collective-permute-start(bf16[1488,128]{1,0:T(8,128)(2,1)S(1)} %pack.1.refs_0_), channel_id=1, source_target_pairs={{0,4},{1,3},{4,8},{5,1},{8,12},{9,5},{12,14},{13,9},{14,10},{15,13... | collective-permute-start | bytes 1142792 | tf_op jit(solution)/shard_map/ppermute | solution.py:52
  5.1 10.7 %collective-permute-start.3 = (bf16[1488,128]{1,0:T(8,128)(2,1)S(1)}, bf16[1488,128]{1,0:T(8,128)(2,1)S(1)}, u32[]{:S(2)}, u32[]{:S(2)}) collective-permute-start(bf16[1488,128]{1,0:T(8,128)(2,1)S(1)} %pack.1.refs_0_), channel_id=1, source_target_pairs={{0,1},{1,0},{2,3},{3,2},{4,5},{5,4},{6,7},{7,6},{8,9},{9,8},{10,11... | collective-permute-start | bytes 1142792 | tf_op jit(solution)/shard_map/ppermute | solution.py:56
  5.1 11.4 %collective-permute-start.2 = (bf16[1488,128]{1,0:T(8,128)(2,1)S(1)}, bf16[1488,128]{1,0:T(8,128)(2,1)S(1)}, u32[]{:S(2)}, u32[]{:S(2)}) collective-permute-start(bf16[1488,128]{1,0:T(8,128)(2,1)S(1)} %pack.1.refs_0_), channel_id=1, source_target_pairs={{1,4},{0,3},{5,8},{4,1},{9,12},{8,5},{13,14},{12,9},{15,10},{14,13... | collective-permute-start | bytes 1142792 | tf_op jit(solution)/shard_map/ppermute | solution.py:52
  13.4 8.6 %collective-permute-start.1 = (bf16[1488,128]{1,0:T(8,128)(2,1)S(1)}, bf16[1488,128]{1,0:T(8,128)(2,1)S(1)}, u32[]{:S(2)}, u32[]{:S(2)}) collective-permute-start(bf16[1488,128]{1,0:T(8,128)(2,1)S(1)} %collective-permute-done.refs_0_.refs_2_), channel_id=1, source_target_pairs={{0,4},{1,3},{4,8},{5,1},{8,12},{9,5},{12,14},{13,9},{14,10},{15,13... | collective-permute-start | bytes 1142792 | tf_op jit(solution)/shard_map/ppermute | solution.py:52
  15.8 7.7 %collective-permute-start.6 = (bf16[1488,128]{1,0:T(8,128)(2,1)S(1)}, bf16[1488,128]{1,0:T(8,128)(2,1)S(1)}, u32[]{:S(2)}, u32[]{:S(2)}) collective-permute-start(bf16[1488,128]{1,0:T(8,128)(2,1)S(1)} %collective-permute-done.refs_0_.refs_2_), channel_id=1, source_target_pairs={{0,1},{1,0},{2,3},{3,2},{4,5},{5,4},{6,7},{7,6},{8,9},{9,8},{10,11... | collective-permute-start | bytes 1142792 | tf_op jit(solution)/shard_map/ppermute | solution.py:56
  16.6 6.9 %collective-permute-start.7 = (bf16[1488,128]{1,0:T(8,128)(2,1)S(1)}, bf16[1488,128]{1,0:T(8,128)(2,1)S(1)}, u32[]{:S(2)}, u32[]{:S(2)}) collective-permute-start(bf16[1488,128]{1,0:T(8,128)(2,1)S(1)} %collective-permute-done.2.refs_1_.refs_3_), channel_id=1, source_target_pairs={{0,1},{1,0},{2,3},{3,2},{4,5},{5,4},{6,7},{7,6},{8,9},{9,8},{10,11... | collective-permute-start | bytes 1142792 | tf_op jit(solution)/shard_map/ppermute | solution.py:56
  17.1 8.9 %collective-permute-start.5 = (bf16[1488,128]{1,0:T(8,128)(2,1)S(1)}, bf16[1488,128]{1,0:T(8,128)(2,1)S(1)}, u32[]{:S(2)}, u32[]{:S(2)}) collective-permute-start(bf16[1488,128]{1,0:T(8,128)(2,1)S(1)} %collective-permute-done.2.refs_1_.refs_3_), channel_id=1, source_target_pairs={{0,4},{1,3},{4,8},{5,1},{8,12},{9,5},{12,14},{13,9},{14,10},{15,13... | collective-permute-start | bytes 1142792 | tf_op jit(solution)/shard_map/ppermute | solution.py:52
  21.9 8.2 %collective-permute-start.4 = (bf16[1488,128]{1,0:T(8,128)(2,1)S(1)}, bf16[1488,128]{1,0:T(8,128)(2,1)S(1)}, u32[]{:S(2)}, u32[]{:S(2)}) collective-permute-start(bf16[1488,128]{1,0:T(8,128)(2,1)S(1)} %collective-permute-done.1.refs_0_.refs_6_), channel_id=1, source_target_pairs={{0,4},{1,3},{4,8},{5,1},{8,12},{9,5},{12,14},{13,9},{14,10},{15,13... | collective-permute-start | bytes 1142792 | tf_op jit(solution)/shard_map/ppermute | solution.py:52
  23.5 8.2 %collective-permute-start.10 = (bf16[1488,128]{1,0:T(8,128)(2,1)S(1)}, bf16[1488,128]{1,0:T(8,128)(2,1)S(1)}, u32[]{:S(2)}, u32[]{:S(2)}) collective-permute-start(bf16[1488,128]{1,0:T(8,128)(2,1)S(1)} %collective-permute-done.1.refs_0_.refs_6_), channel_id=1, source_target_pairs={{0,1},{1,0},{2,3},{3,2},{4,5},{5,4},{6,7},{7,6},{8,9},{9,8},{10,11... | collective-permute-start | bytes 1142792 | tf_op jit(solution)/shard_map/ppermute | solution.py:56
  26.0 5.7 %collective-permute-start.11 = (bf16[1488,128]{1,0:T(8,128)(2,1)S(1)}, bf16[1488,128]{1,0:T(8,128)(2,1)S(1)}, u32[]{:S(2)}, u32[]{:S(2)}) collective-permute-start(bf16[1488,128]{1,0:T(8,128)(2,1)S(1)} %collective-permute-done.5.refs_1_.refs_7_), channel_id=1, source_target_pairs={{0,1},{1,0},{2,3},{3,2},{4,5},{5,4},{6,7},{7,6},{8,9},{9,8},{10,11... | collective-permute-start | bytes 1142792 | tf_op jit(solution)/shard_map/ppermute | solution.py:56
  26.0 8.2 %collective-permute-start.9 = (bf16[1488,128]{1,0:T(8,128)(2,1)S(1)}, bf16[1488,128]{1,0:T(8,128)(2,1)S(1)}, u32[]{:S(2)}, u32[]{:S(2)}) collective-permute-start(bf16[1488,128]{1,0:T(8,128)(2,1)S(1)} %collective-permute-done.5.refs_1_.refs_7_), channel_id=1, source_target_pairs={{0,4},{1,3},{4,8},{5,1},{8,12},{9,5},{12,14},{13,9},{14,10},{15,13... | collective-permute-start | bytes 1142792 | tf_op jit(solution)/shard_map/ppermute | solution.py:52
  30.1 8.2 %collective-permute-start.8 = (bf16[1488,128]{1,0:T(8,128)(2,1)S(1)}, bf16[1488,128]{1,0:T(8,128)(2,1)S(1)}, u32[]{:S(2)}, u32[]{:S(2)}) collective-permute-start(bf16[1488,128]{1,0:T(8,128)(2,1)S(1)} %collective-permute-done.4.refs_0_.refs_10_), channel_id=1, source_target_pairs={{0,4},{1,3},{4,8},{5,1},{8,12},{9,5},{12,14},{13,9},{14,10},{15,13... | collective-permute-start | bytes 1142792 | tf_op jit(solution)/shard_map/ppermute | solution.py:52
  31.7 6.6 %collective-permute-start.13 = (bf16[1488,128]{1,0:T(8,128)(2,1)S(1)}, bf16[1488,128]{1,0:T(8,128)(2,1)S(1)}, u32[]{:S(2)}, u32[]{:S(2)}) collective-permute-start(bf16[1488,128]{1,0:T(8,128)(2,1)S(1)} %collective-permute-done.4.refs_0_.refs_10_), channel_id=1, source_target_pairs={{0,1},{1,0},{2,3},{3,2},{4,5},{5,4},{6,7},{7,6},{8,9},{9,8},{10,11... | collective-permute-start | bytes 1142792 | tf_op jit(solution)/shard_map/ppermute | solution.py:56
  34.2 4.1 %collective-permute-start.14 = (bf16[1488,128]{1,0:T(8,128)(2,1)S(1)}, bf16[1488,128]{1,0:T(8,128)(2,1)S(1)}, u32[]{:S(2)}, u32[]{:S(2)}) collective-permute-start(bf16[1488,128]{1,0:T(8,128)(2,1)S(1)} %collective-permute-done.9.refs_1_.refs_11_), channel_id=1, source_target_pairs={{0,1},{1,0},{2,3},{3,2},{4,5},{5,4},{6,7},{7,6},{8,9},{9,8},{10,11... | collective-permute-start | bytes 1142792 | tf_op jit(solution)/shard_map/ppermute | solution.py:56
  38.3 1.7 %collective-permute-start.12 = (bf16[1488,128]{1,0:T(8,128)(2,1)S(1)}, bf16[1488,128]{1,0:T(8,128)(2,1)S(1)}, u32[]{:S(2)}, u32[]{:S(2)}) collective-permute-start(bf16[1488,128]{1,0:T(8,128)(2,1)S(1)} %collective-permute-done.8.refs_0_.refs_14_), channel_id=1, source_target_pairs={{0,1},{1,0},{2,3},{3,2},{4,5},{5,4},{6,7},{7,6},{8,9},{9,8},{10,11... | collective-permute-start | bytes 1142792 | tf_op jit(solution)/shard_map/ppermute | solution.py:56
  40.0 0.8 %copy-start = (s32[1,2]{1,0:T(1,128)S(1)}, s32[1,2]{1,0:T(1,128)}, u32[]{:S(2)}) copy-start(s32[1,2]{1,0:T(1,128)} %counts_ref.1) | copy-start | bytes 28

commit v8 on v7

--- a/solution.py
+++ b/solution.py
@@ -41,14 +41,13 @@
     return jnp.where(side == 0, row, RING_CHIPS - 1 - row)
 
 
-def hop(value, from_other=False):
+def hop(value):
     half = RING_CHIPS // 2
     place = [2 * q if q < half else 2 * (RING_CHIPS - 1 - q) + 1 for q in range(RING_CHIPS)]
-    turn = int(from_other)
     pairs = []
     for q in range(RING_CHIPS):
-        pairs.append((2 * place[q] + turn, 2 * place[(q + 1) % RING_CHIPS]))
-        pairs.append((2 * place[q] + 1 - turn, 2 * place[(q - 1) % RING_CHIPS] + 1))
+        pairs.append((2 * place[q], 2 * place[(q + 1) % RING_CHIPS]))
+        pairs.append((2 * place[q] + 1, 2 * place[(q - 1) % RING_CHIPS] + 1))
     return lax.ppermute(value, "dp", pairs)
 
 
@@ -156,13 +155,9 @@
         copy.wait()
 
 
-def stage_kernel(away, first, me_ref, *refs):
-    refs = list(refs)
-    take = lambda k: [refs.pop(0) for _ in range(k)]
-    pieces = take(2)
-    x_ref, mixed_ref, adjoint_ref, values_ref, target_ref, top_target_ref, source_ref = take(7)
-    old_sums, old_bridge = (None, None) if first else take(2)
-    new_sums, new_bridge, both, up, down = refs
+def add_stage(away, me_ref, pieces, held, old, scratch):
+    x_ref, mixed_ref, adjoint_ref, values_ref, target_ref, top_target_ref, source_ref = held
+    both, up, down = scratch
     rows = both.shape[0] // 2
     half, pad = rows // 2, LANES // 2
     span = 2 * rows
@@ -204,22 +199,46 @@
         product = mm(activation, factor)
         products += [product[:, :LANES], product[:, LANES:]]
     bridge = mm_cols(down_up, lows)
-    if not first:
+    if old:
+        old_sums, old_bridge = old
         products = [p + old_sums[:, i * LANES : (i + 1) * LANES] for i, p in enumerate(products)]
         bridge = bridge + old_bridge[...]
+    return products, bridge
+
+
+def stage_kernel(away, first, me_ref, *refs):
+    pieces, held, old = refs[:2], refs[2:9], refs[9:-5]
+    (new_sums, new_bridge), scratch = refs[-5:-3], refs[-3:]
+    products, bridge = add_stage(away, me_ref, pieces, held, old, scratch)
     for i in range(SUMS):
         new_sums[:, i * LANES : (i + 1) * LANES] = products[i]
     new_bridge[...] = bridge
 
 
-def feature_kernel(width, counts_ref, sums_ref, bridge_ref, local_ref, expand_hbm, sketch_hbm, out_ref, *scratch):
-    expand_ref, sketch_ref, sems = scratch
-    more = load(((expand_hbm, expand_ref), (sketch_hbm, sketch_ref)), sems)
-    tokens = sums_ref.shape[0]
-    pad = LANES // 2
-    products = [sums_ref[:, i * LANES : (i + 1) * LANES] for i in range(SUMS)]
+def finish_kernel(away, blocks, count, me_ref, counts_ref, *refs):
+    block_refs, refs = refs[:blocks], refs[blocks:]
+    held, old, local_ref, small_hbm, refs = refs[:7], refs[7:9], refs[9], refs[10:12], refs[12:]
+    (out_ref, mean_ref), scratch, (expand_ref, sketch_ref, panel, sems) = refs[:2], refs[2:5], refs[5:]
+    more = load(zip(small_hbm, (expand_ref, sketch_ref)), sems)
+    products, bridge = add_stage(away, me_ref, block_refs[-2:], held, old, scratch)
     local = [local_ref[:, i * LANES : (i + 1) * LANES] for i in range(LOCAL_SUMS)]
-    bridge = bridge_ref[...]
+    tokens, width = held[0].shape
+    half = LANES // 2
+
+    starts = [block.shape[0] - (half + 2) * count for block in block_refs]
+    for i in range(0, half, 2):
+        wide = [block[pl.ds(at + i * count, 2 * count), :].astype(F32) for block, at in zip(block_refs, starts)]
+        for k in range(2):
+            rows = jnp.concatenate([w[k * count : (k + 1) * count] for w in wide], axis=0)
+            panel[:, pl.ds((i + k) * LANES, LANES)] = rows.astype(BF16)
+    labels = jnp.concatenate(
+        [
+            block[pl.ds(at + half * count, 2 * count), :].astype(F32)[:count]
+            for block, at in zip(block_refs, starts)
+        ],
+        axis=0,
+    )
+
     for copy in more:
         copy.wait()
     inverse = local[INVERSE]
@@ -241,40 +260,26 @@
     member = (place >= jnp.where(lower, 0, one)) & (place < jnp.where(lower, one, one + two))
     spread = jnp.concatenate([jnp.where(member, left, 0.0).astype(BF16) for left in lefts], axis=0)
     feats = mm_cols(spread, jnp.concatenate([right.astype(BF16) for right in rights], axis=0))
+    lower = lax.broadcasted_iota(jnp.int32, (8, LANES), 0) < 4
+    unit = []
     for e in range(2):
-        own = feats[e * pad : (e + 1) * pad]
+        own = feats[e * half : (e + 1) * half]
         squares = jnp.sum(own * own, keepdims=True)
-        out_ref[pl.ds(e * pad, pad), :] = (own * lax.rsqrt(squares + 1e-06)).astype(BF16).astype(F32)
-
-
-def score_kernel(blocks, count, unit_ref, *refs):
-    block_refs, (out_ref, mean_ref) = refs[:blocks], refs[blocks:]
-    half = LANES // 2
+        unit.append(own * lax.rsqrt(squares + 1e-06))
+    tiles = [
+        jnp.where(lower, unit[0][i : i + 1], unit[1][i : i + 1]).astype(BF16) for i in range(half)
+    ]
     scale = float(half * LANES) ** 0.5
-    starts = [block.shape[0] - (half + 2) * count for block in block_refs]
-    shape = (count, LANES)
-    totals = [[jnp.zeros(shape, F32) for _ in range(2)] for _ in block_refs]
-    for i in range(0, half, 2):
-        units = [
-            [jnp.broadcast_to(unit_ref[pl.ds(e * half + i + k, 1), :], shape) for k in range(2)]
-            for e in range(2)
-        ]
-        for b, block in enumerate(block_refs):
-            wide = block[pl.ds(starts[b] + i * count, 2 * count), :].astype(F32)
-            for e in range(2):
-                totals[b][e] = totals[b][e] + (wide[:count] * units[e][0] + wide[count:] * units[e][1])
-    best = [[jnp.full(shape, -2.0 * scale, F32) for _ in range(TASKS)] for _ in range(2)]
-    for b, block in enumerate(block_refs):
-        labels = block[pl.ds(starts[b] + half * count, 2 * count), :].astype(F32)[:count]
-        for e in range(2):
-            similar = scale * jnp.sum(totals[b][e], axis=1, keepdims=True)
-            for t in range(TASKS):
-                best[e][t] = jnp.maximum(best[e][t], jnp.where(labels == float(t), similar, -2.0 * scale))
+    similar = scale * mm_rows(panel[...], jnp.concatenate(tiles, axis=1))
+    labels = labels[:, : similar.shape[1]]
+    values = []
+    for t in range(TASKS):
+        best = jnp.max(jnp.where(labels == float(t), similar, -2.0 * scale), axis=0, keepdims=True)
+        values.append([jnp.max(best[:, 4 * e : 4 * e + 4]) for e in range(2)])
     for e in range(2):
-        values = [jnp.max(best[e][t]) for t in range(TASKS)]
         for t in range(TASKS):
-            out_ref[e, t] = values[t]
-        mean_ref[e] = (values[0] + values[1] + values[2]) * (1.0 / TASKS)
+            out_ref[e, t] = values[t][e]
+        mean_ref[e] = (values[0][e] + values[1][e] + values[2][e]) * (1.0 / TASKS)
 
 
 VMEM = pl.BlockSpec(memory_space=pltpu.VMEM)
@@ -375,6 +380,12 @@
         name="local_products",
     )(*in_hbm(inputs))
 
+    stage_scratch = [
+        pltpu.VMEM((2 * rows, 2 * LANES), BF16),
+        pltpu.VMEM((rows + LANES // 2, 2 * LANES), BF16),
+        pltpu.VMEM((2 * rows, LANES), BF16),
+    ]
+
     def stage(away, pieces, sums):
         first = not sums
         start = 1 + len(pieces) + len(activations)
@@ -386,11 +397,7 @@
             ],
             in_specs=[SMEM] + [VMEM] * (len(pieces) + len(activations) + len(sums)),
             out_specs=[VMEM, VMEM],
-            scratch_shapes=[
-                pltpu.VMEM((2 * rows, 2 * LANES), BF16),
-                pltpu.VMEM((rows + LANES // 2, 2 * LANES), BF16),
-                pltpu.VMEM((2 * rows, LANES), BF16),
-            ],
+            scratch_shapes=stage_scratch,
             input_output_aliases={} if first else {start: 0, start + 1: 1},
             compiler_params=params(16),
             cost_estimate=cost(tokens * rows * LANES * 16, 2 * MIB),
@@ -401,7 +408,7 @@
     half = RING_CHIPS // 2
     held = [own, other_core(own)]
     blocks = list(held)
-    first, second = hop(own), hop(own, from_other=True)
+    first, second = hop(held[0]), hop(held[1])
     first, activations = tie((first, activations))
     sums = stage(0, held, [])
     second, sums = tie((second, sums))
@@ -419,28 +426,22 @@
             second, sums = tie((second, sums))
     held = [first, other_core(first)]
     blocks += held
-    sums = stage(half, held, sums)
     small = (top_expander_sketch.T, top_reducer_sketch)
-    unit = pl.pallas_call(
-        functools.partial(feature_kernel, width),
-        out_shape=jax.ShapeDtypeStruct((LANES, LANES), F32),
-        in_specs=[SMEM] + [VMEM] * 3 + [HBM] * 2,
-        out_specs=VMEM,
-        scratch_shapes=[pltpu.VMEM(a.shape, a.dtype) for a in small] + [pltpu.SemaphoreType.DMA((2,))],
-        compiler_params=params(16),
-        cost_estimate=cost(tokens * LANES * LANES * 20, 4 * MIB),
-        name="features",
-    )(sequence_token_counts, *sums, local, *in_hbm(small))
-
     task_best, scores = pl.pallas_call(
-        functools.partial(score_kernel, len(blocks), count),
+        functools.partial(finish_kernel, half, len(blocks), count),
         out_shape=(jax.ShapeDtypeStruct((2, TASKS), F32), jax.ShapeDtypeStruct((2,), F32)),
-        in_specs=[VMEM] * (1 + len(blocks)),
+        in_specs=[SMEM] * 2 + [VMEM] * (len(blocks) + len(activations) + 3) + [HBM] * 2,
         out_specs=(SMEM, SMEM),
-        compiler_params=params(16),
-        cost_estimate=cost(4 * MIB, 2 * MIB),
-        name="scores",
-    )(unit, *blocks)
+        scratch_shapes=stage_scratch
+        + [pltpu.VMEM(a.shape, a.dtype) for a in small]
+        + [
+            pltpu.VMEM((len(blocks) * count, LANES // 2 * LANES), BF16),
+            pltpu.SemaphoreType.DMA((2,)),
+        ],
+        compiler_params=params(24),
+        cost_estimate=cost(tokens * rows * LANES * 40, 8 * MIB),
+        name="finish",
+    )(me.reshape(1), sequence_token_counts, *blocks, *activations, *sums, local, *in_hbm(small))
     return (scores, task_best)
 
 

time: 44.7 us -> 42.3 us (0.946)
  waiting for transfers between devices: 14.5 us -> 10.8 us
  starting transfers between devices: 13.1 us -> 14.1 us
    ppermute x7, waiting for transfers between devices: 13.6 us -> 9.88 us  [hop(): return lax.ppermute(value, 'dp', pairs)]
    pallas_call x2 -> x1, Pallas kernels: 3.56 us -> 4.76 us  [shards(): pl.pallas_call(functools.partial(finish_kernel, half, len(blocks), count)...]
    ppermute x7, starting transfers between devices: 12.5 us -> 13.5 us  [hop(): return lax.ppermute(value, 'dp', pairs)]
    pallas_call x8 -> x7, Pallas kernels: 6.41 us -> 5.6 us  [stage(): pl.pallas_call(functools.partial(stage_kernel, away, first), out_shape=[j...]
  transfers between devices with their start and end apart: 15 -> 15, of which waited for: 7 -> 7; matrix products, arithmetic and copies ran while one was open for 0% -> 0% of each run, Pallas kernels for 23% -> 24%
where the time goes in v8:
time: 42.3 us; the launch traced here: 42 us
  Pallas kernels  16.4 us (39%)
  starting transfers between devices  14.1 us (33%)
  waiting for transfers between devices  10.8 us (26%)
  between operations  0.74 us (2%)
    ppermute x7, starting transfers between devices, hop(): return lax.ppermute(value, 'dp', pairs)  13.5 us
    ppermute x7, waiting for transfers between devices, hop(): return lax.ppermute(value, 'dp', pairs)  9.88 us
    pallas_call x7, Pallas kernels, stage(): pl.pallas_call(functools.partial(stage_kernel, away, first), out_shape=[j...  5.6 us
    pallas_call x1, Pallas kernels, shards(): pl.pallas_call(functools.partial(finish_kernel, half, len(blocks), count)...  4.76 us
    pallas_call x1, Pallas kernels, shards(): pl.pallas_call(local_kernel, out_shape=[jax.ShapeDtypeStruct(a.shape, a.d...  4.6 us
    pallas_call x1, Pallas kernels, shards(): pl.pallas_call(pack_kernel, out_shape=jax.ShapeDtypeStruct((3 * rows + (L...  1.41 us
    ppermute x8, waiting for transfers between devices, other_core(): lax.ppermute(value, 'dp', [(d, d ^ 1) for d in range(2 * RING_CHIPS)])  0.89 us
  transfers between devices with their start and end apart: 15, of which 7 were waited for; matrix products, arithmetic and copies ran while one was open for 0% of the time, Pallas kernels for 24%

profile of v8, /device:TPU:0, one launch (start us, length us, event | category | flops | bytes accessed | tf_op | source)
XLA Modules:
  0.0 42.0 jit_solution(12996773884827192484)
XLA Ops:
  0.6 1.4 %pack.1.refs_0_ = bf16[1488,128]{1,0:T(8,128)(2,1)S(1)} custom-call(s32[1]{0:T(128)} %bitcast.me_ref, f32[40,128]{1,0:T(8,128)} %bitcast.10, bf16[320,128]{1,0:T(8,128)(2,1)} %refs_1_.2, bf16[320,128]{1,0:T(8,128)(2,1)} %bitcast.12, bf16[128,128]{1,0:T(8,128)(2,1)} %refs_3_.2, bf16[160,128]{1,0:T(8,128)(2,1)} %bitcast.13, bf16[320,128]{1,0:T(8,128)(2,1)} %refs_5_.2, ...), custom_call_target="tpu_custom_call" | custom-call | tf_op jit(solution)/shard_map/pack/pallas_call | solution.py:346
  2.1 0.5 %collective-permute-start = (bf16[1488,128]{1,0:T(8,128)(2,1)S(1)}, bf16[1488,128]{1,0:T(8,128)(2,1)S(1)}, u32[]{:S(2)}, u32[]{:S(2)}) collective-permute-start(bf16[1488,128]{1,0:T(8,128)(2,1)S(1)} %pack.1.refs_0_), channel_id=1, source_target_pairs={{0,1},{1,0},{2,3},{3,2},{4,5},{5,4},{6,7},{7,6},{8,9},{9,8},{10,11... | collective-permute-start | bytes 1142792 | tf_op jit(solution)/shard_map/ppermute | solution.py:55
  2.6 2.6 %collective-permute-start.1 = (bf16[1488,128]{1,0:T(8,128)(2,1)S(1)}, bf16[1488,128]{1,0:T(8,128)(2,1)S(1)}, u32[]{:S(2)}, u32[]{:S(2)}) collective-permute-start(bf16[1488,128]{1,0:T(8,128)(2,1)S(1)} %pack.1.refs_0_), channel_id=1, source_target_pairs={{0,4},{1,3},{4,8},{5,1},{8,12},{9,5},{12,14},{13,9},{14,10},{15,13... | collective-permute-start | bytes 1142792 | tf_op jit(solution)/shard_map/ppermute | solution.py:51
  5.2 0.0 collective-permute-done.refs_1_
  5.2 1.6 %collective-permute-start.2 = (bf16[1488,128]{1,0:T(8,128)(2,1)S(1)}, bf16[1488,128]{1,0:T(8,128)(2,1)S(1)}, u32[]{:S(2)}, u32[]{:S(2)}) collective-permute-start(bf16[1488,128]{1,0:T(8,128)(2,1)S(1)} %collective-permute-done.refs_1_), channel_id=1, source_target_pairs={{0,4},{1,3},{4,8},{5,1},{8,12},{9,5},{12,14},{13,9},{14,10},{15,13... | collective-permute-start | bytes 1142792 | tf_op jit(solution)/shard_map/ppermute | solution.py:51
  6.8 4.6 %local_products.1 = (bf16[256,5120]{1,0:T(8,128)(2,1)S(1)}, bf16[256,5120]{1,0:T(8,128)(2,1)S(1)}, bf16[256,5120]{1,0:T(8,128)(2,1)S(1)}, bf16[256,2560]{1,0:T(8...) custom-call(bf16[256,5120]{1,0:T(8,128)(2,1)} %refs_0_.1, ...), custom_call_target="tpu_custom_call" | custom-call | flops 1006632960 | bytes 14680064 | tf_op jit(solution)/shard_map/local_products/pallas_call | solution.py:367
  11.5 0.0 collective-permute-done.1.refs_0_.refs_2_
  11.5 1.6 %collective-permute-start.5 = (bf16[1488,128]{1,0:T(8,128)(2,1)S(1)}, bf16[1488,128]{1,0:T(8,128)(2,1)S(1)}, u32[]{:S(2)}, u32[]{:S(2)}) collective-permute-start(bf16[1488,128]{1,0:T(8,128)(2,1)S(1)} %collective-permute-done.1.refs_0_.refs_2_), channel_id=1, source_target_pairs={{0,4},{1,3},{4,8},{5,1},{8,12},{9,5},{12,14},{13,9},{14,10},{15,13... | collective-permute-start | bytes 1142792 | tf_op jit(solution)/shard_map/ppermute | solution.py:51
  13.1 0.0 collective-permute-start.3
  13.1 0.7 %stage.7 = (f32[256,1024]{1,0:T(8,128)S(1)}, f32[128,256]{1,0:T(8,128)S(1)}) custom-call(s32[1]{0:T(128)} %bitcast.me_ref, bf16[1488,128]{1,0:T(8,128)(2,1)S(1)} %pack.1.refs_0_, bf16[1488,128]{1,0:T(8,128)(2,1)S(1)} %collective-permute-done.refs_1_, bf16[256,5120]{1,0:T(8,128)(2,1)S(1)} %get-tuple-element.60.refs_2_.refs_16_, ...), custom_call_target="tpu_custom_call" | custom-call | flops 167772160 | bytes 2097152 | tf_op jit(solution)/shard_map/stage/pallas_call | solution.py:392
  13.8 1.1 %collective-permute-done.2.refs_1_.refs_3_ = bf16[1488,128]{1,0:T(8,128)(2,1)S(1)} collective-permute-done((bf16[1488,128]{1,0:T(8,128)(2,1)S(1)}, bf16[1488,128]{1,0:T(8,128)(2,1)S(1)}, u32[]{:S(2)}, u32[]{:S(2)}) %collective-permute-start.2) | collective-permute-done | bytes 380960 | tf_op jit(solution)/shard_map/ppermute | solution.py:51
  14.9 0.0 collective-permute-start.4
  14.9 2.1 %collective-permute-start.6 = (bf16[1488,128]{1,0:T(8,128)(2,1)S(1)}, bf16[1488,128]{1,0:T(8,128)(2,1)S(1)}, u32[]{:S(2)}, u32[]{:S(2)}) collective-permute-start(bf16[1488,128]{1,0:T(8,128)(2,1)S(1)} %collective-permute-done.2.refs_1_.refs_3_), channel_id=1, source_target_pairs={{0,4},{1,3},{4,8},{5,1},{8,12},{9,5},{12,14},{13,9},{14,10},{15,13... | collective-permute-start | bytes 1142792 | tf_op jit(solution)/shard_map/ppermute | solution.py:51
  16.9 0.8 %stage.8 = (f32[256,1024]{1,0:T(8,128)S(1)}, f32[128,256]{1,0:T(8,128)S(1)}) custom-call(s32[1]{0:T(128)} %bitcast.me_ref, bf16[1488,128]{1,0:T(8,128)(2,1)S(1)} %collective-permute-done.1.refs_0_.refs_2_, bf16[1488,128]{1,0:T(8,128)(2,1)S(1)} %collective-permute-done.2.refs_1_.refs_3_, ...), custom_call_target="tpu_custom_call", output_to_operand_aliasing={{0}: (10, {}), {1}: (11, {})} | custom-call | flops 167772160 | bytes 2097152 | tf_op jit(solution)/shard_map/stage/pallas_call | solution.py:392
  17.8 1.4 %collective-permute-done.5.refs_0_.refs_6_ = bf16[1488,128]{1,0:T(8,128)(2,1)S(1)} collective-permute-done((bf16[1488,128]{1,0:T(8,128)(2,1)S(1)}, bf16[1488,128]{1,0:T(8,128)(2,1)S(1)}, u32[]{:S(2)}, u32[]{:S(2)}) %collective-permute-start.5) | collective-permute-done | bytes 380960 | tf_op jit(solution)/shard_map/ppermute | solution.py:51
  19.2 1.9 %collective-permute-start.9 = (bf16[1488,128]{1,0:T(8,128)(2,1)S(1)}, bf16[1488,128]{1,0:T(8,128)(2,1)S(1)}, u32[]{:S(2)}, u32[]{:S(2)}) collective-permute-start(bf16[1488,128]{1,0:T(8,128)(2,1)S(1)} %collective-permute-done.5.refs_0_.refs_6_), channel_id=1, source_target_pairs={{0,4},{1,3},{4,8},{5,1},{8,12},{9,5},{12,14},{13,9},{14,10},{15,13... | collective-permute-start | bytes 1142792 | tf_op jit(solution)/shard_map/ppermute | solution.py:51
  21.0 0.8 %stage.9 = (f32[256,1024]{1,0:T(8,128)S(1)}, f32[128,256]{1,0:T(8,128)S(1)}) custom-call(s32[1]{0:T(128)} %bitcast.me_ref, bf16[1488,128]{1,0:T(8,128)(2,1)S(1)} %collective-permute-done.3.refs_0_.refs_4_, bf16[1488,128]{1,0:T(8,128)(2,1)S(1)} %collective-permute-done.4.refs_1_.refs_5_, ...), custom_call_target="tpu_custom_call", output_to_operand_aliasing={{0}: (10, {}), {1}: (11, {})} | custom-call | flops 167772160 | bytes 2097152 | tf_op jit(solution)/shard_map/stage/pallas_call | solution.py:392
  21.8 1.4 %collective-permute-done.6.refs_1_.refs_7_ = bf16[1488,128]{1,0:T(8,128)(2,1)S(1)} collective-permute-done((bf16[1488,128]{1,0:T(8,128)(2,1)S(1)}, bf16[1488,128]{1,0:T(8,128)(2,1)S(1)}, u32[]{:S(2)}, u32[]{:S(2)}) %collective-permute-start.6) | collective-permute-done | bytes 380960 | tf_op jit(solution)/shard_map/ppermute | solution.py:51
  23.2 1.9 %collective-permute-start.10 = (bf16[1488,128]{1,0:T(8,128)(2,1)S(1)}, bf16[1488,128]{1,0:T(8,128)(2,1)S(1)}, u32[]{:S(2)}, u32[]{:S(2)}) collective-permute-start(bf16[1488,128]{1,0:T(8,128)(2,1)S(1)} %collective-permute-done.6.refs_1_.refs_7_), channel_id=1, source_target_pairs={{0,4},{1,3},{4,8},{5,1},{8,12},{9,5},{12,14},{13,9},{14,10},{15,13... | collective-permute-start | bytes 1142792 | tf_op jit(solution)/shard_map/ppermute | solution.py:51
  25.1 0.8 %stage.10 = (f32[256,1024]{1,0:T(8,128)S(1)}, f32[128,256]{1,0:T(8,128)S(1)}) custom-call(s32[1]{0:T(128)} %bitcast.me_ref, bf16[1488,128]{1,0:T(8,128)(2,1)S(1)} %collective-permute-done.5.refs_0_.refs_6_, bf16[1488,128]{1,0:T(8,128)(2,1)S(1)} %collective-permute-done.6.refs_1_.refs_7_, ...), custom_call_target="tpu_custom_call", output_to_operand_aliasing={{0}: (10, {}), {1}: (11, {})} | custom-call | flops 167772160 | bytes 2097152 | tf_op jit(solution)/shard_map/stage/pallas_call | solution.py:392
  25.9 1.4 %collective-permute-done.9.refs_0_.refs_10_ = bf16[1488,128]{1,0:T(8,128)(2,1)S(1)} collective-permute-done((bf16[1488,128]{1,0:T(8,128)(2,1)S(1)}, bf16[1488,128]{1,0:T(8,128)(2,1)S(1)}, u32[]{:S(2)}, u32[]{:S(2)}) %collective-permute-start.9) | collective-permute-done | bytes 380960 | tf_op jit(solution)/shard_map/ppermute | solution.py:51
  27.3 1.9 %collective-permute-start.13 = (bf16[1488,128]{1,0:T(8,128)(2,1)S(1)}, bf16[1488,128]{1,0:T(8,128)(2,1)S(1)}, u32[]{:S(2)}, u32[]{:S(2)}) collective-permute-start(bf16[1488,128]{1,0:T(8,128)(2,1)S(1)} %collective-permute-done.9.refs_0_.refs_10_), channel_id=1, source_target_pairs={{0,4},{1,3},{4,8},{5,1},{8,12},{9,5},{12,14},{13,9},{14,10},{15,13... | collective-permute-start | bytes 1142792 | tf_op jit(solution)/shard_map/ppermute | solution.py:51
  29.2 0.0 collective-permute-done.8.refs_1_.refs_9_
  29.2 0.8 %stage.11 = (f32[256,1024]{1,0:T(8,128)S(1)}, f32[128,256]{1,0:T(8,128)S(1)}) custom-call(s32[1]{0:T(128)} %bitcast.me_ref, bf16[1488,128]{1,0:T(8,128)(2,1)S(1)} %collective-permute-done.7.refs_0_.refs_8_, bf16[1488,128]{1,0:T(8,128)(2,1)S(1)} %collective-permute-done.8.refs_1_.refs_9_, ...), custom_call_target="tpu_custom_call", output_to_operand_aliasing={{0}: (10, {}), {1}: (11, {})} | custom-call | flops 167772160 | bytes 2097152 | tf_op jit(solution)/shard_map/stage/pallas_call | solution.py:392
  30.0 1.4 %collective-permute-done.10.refs_1_.refs_11_ = bf16[1488,128]{1,0:T(8,128)(2,1)S(1)} collective-permute-done((bf16[1488,128]{1,0:T(8,128)(2,1)S(1)}, bf16[1488,128]{1,0:T(8,128)(2,1)S(1)}, u32[]{:S(2)}, u32[]{:S(2)}) %collective-permute-start.10) | collective-permute-done | bytes 380960 | tf_op jit(solution)/shard_map/ppermute | solution.py:51
  31.4 0.8 %stage.12 = (f32[256,1024]{1,0:T(8,128)S(1)}, f32[128,256]{1,0:T(8,128)S(1)}) custom-call(s32[1]{0:T(128)} %bitcast.me_ref, bf16[1488,128]{1,0:T(8,128)(2,1)S(1)} %collective-permute-done.9.refs_0_.refs_10_, bf16[1488,128]{1,0:T(8,128)(2,1)S(1)} %collective-permute-done.10.refs_1_.refs_11_, ...), custom_call_target="tpu_custom_call", output_to_operand_aliasing={{0}: (10, {}), {1}: (11, {})} | custom-call | flops 167772160 | bytes 2097152 | tf_op jit(solution)/shard_map/stage/pallas_call | solution.py:392
  32.2 3.2 %collective-permute-done.13.refs_14_ = bf16[1488,128]{1,0:T(8,128)(2,1)S(1)} collective-permute-done((bf16[1488,128]{1,0:T(8,128)(2,1)S(1)}, bf16[1488,128]{1,0:T(8,128)(2,1)S(1)}, u32[]{:S(2)}, u32[]{:S(2)}) %collective-permute-start.13) | collective-permute-done | bytes 380960 | tf_op jit(solution)/shard_map/ppermute | solution.py:51
  35.5 0.0 collective-permute-start.14
  35.5 0.0 collective-permute-done.12.refs_1_.refs_13_
  35.5 0.8 %stage.13 = (f32[256,1024]{1,0:T(8,128)S(1)}, f32[128,256]{1,0:T(8,128)S(1)}) custom-call(s32[1]{0:T(128)} %bitcast.me_ref, bf16[1488,128]{1,0:T(8,128)(2,1)S(1)} %collective-permute-done.11.refs_0_.refs_12_, bf16[1488,128]{1,0:T(8,128)(2,1)S(1)} %collective-permute-done.12.refs_1_.refs_13_, ...), custom_call_target="tpu_custom_call", output_to_operand_aliasing={{0}: (10, {}), {1}: (11, {})} | custom-call | flops 167772160 | bytes 2097152 | tf_op jit(solution)/shard_map/stage/pallas_call | solution.py:392
  36.3 0.9 %collective-permute-done.14.refs_15_ = bf16[1488,128]{1,0:T(8,128)(2,1)S(1)} collective-permute-done((bf16[1488,128]{1,0:T(8,128)(2,1)S(1)}, bf16[1488,128]{1,0:T(8,128)(2,1)S(1)}, u32[]{:S(2)}, u32[]{:S(2)}) %collective-permute-start.14) | collective-permute-done | bytes 380960 | tf_op jit(solution)/shard_map/ppermute | solution.py:55
  37.2 4.8 %finish.1 = (f32[2,3]{1,0:T(2,128)}, f32[2]{0:T(128)}) custom-call(s32[1]{0:T(128)} %bitcast.me_ref, s32[1,2]{1,0:T(1,128)S(1)} %copy-done, bf16[1488,128]{1,0:T(8,128)(2,1)S(1)} %pack.1.refs_0_, bf16[1488,128]{1,0:T(8,128)(2,1)S(1)} %collective-permute-done.refs_1_, bf16[1488,128]{1,0:T(8,128)(2,1)S(1)} %collective-permute-done.1.refs_0_.refs_2_, ...), custom_call_target="tpu_custom_call" | custom-call | flops 419430400 | bytes 8388608 | tf_op jit(solution)/shard_map/finish/pallas_call | solution.py:430
  (10 shorter events, 0.0 us)
Async XLA Ops:
  2.1 3.2 %collective-permute-start = (bf16[1488,128]{1,0:T(8,128)(2,1)S(1)}, bf16[1488,128]{1,0:T(8,128)(2,1)S(1)}, u32[]{:S(2)}, u32[]{:S(2)}) collective-permute-start(bf16[1488,128]{1,0:T(8,128)(2,1)S(1)} %pack.1.refs_0_), channel_id=1, source_target_pairs={{0,1},{1,0},{2,3},{3,2},{4,5},{5,4},{6,7},{7,6},{8,9},{9,8},{10,11... | collective-permute-start | bytes 1142792 | tf_op jit(solution)/shard_map/ppermute | solution.py:55
  2.6 8.9 %collective-permute-start.1 = (bf16[1488,128]{1,0:T(8,128)(2,1)S(1)}, bf16[1488,128]{1,0:T(8,128)(2,1)S(1)}, u32[]{:S(2)}, u32[]{:S(2)}) collective-permute-start(bf16[1488,128]{1,0:T(8,128)(2,1)S(1)} %pack.1.refs_0_), channel_id=1, source_target_pairs={{0,4},{1,3},{4,8},{5,1},{8,12},{9,5},{12,14},{13,9},{14,10},{15,13... | collective-permute-start | bytes 1142792 | tf_op jit(solution)/shard_map/ppermute | solution.py:51
  5.2 9.6 %collective-permute-start.2 = (bf16[1488,128]{1,0:T(8,128)(2,1)S(1)}, bf16[1488,128]{1,0:T(8,128)(2,1)S(1)}, u32[]{:S(2)}, u32[]{:S(2)}) collective-permute-start(bf16[1488,128]{1,0:T(8,128)(2,1)S(1)} %collective-permute-done.refs_1_), channel_id=1, source_target_pairs={{0,4},{1,3},{4,8},{5,1},{8,12},{9,5},{12,14},{13,9},{14,10},{15,13... | collective-permute-start | bytes 1142792 | tf_op jit(solution)/shard_map/ppermute | solution.py:51
  11.5 7.7 %collective-permute-start.5 = (bf16[1488,128]{1,0:T(8,128)(2,1)S(1)}, bf16[1488,128]{1,0:T(8,128)(2,1)S(1)}, u32[]{:S(2)}, u32[]{:S(2)}) collective-permute-start(bf16[1488,128]{1,0:T(8,128)(2,1)S(1)} %collective-permute-done.1.refs_0_.refs_2_), channel_id=1, source_target_pairs={{0,4},{1,3},{4,8},{5,1},{8,12},{9,5},{12,14},{13,9},{14,10},{15,13... | collective-permute-start | bytes 1142792 | tf_op jit(solution)/shard_map/ppermute | solution.py:51
  13.1 7.9 %collective-permute-start.3 = (bf16[1488,128]{1,0:T(8,128)(2,1)S(1)}, bf16[1488,128]{1,0:T(8,128)(2,1)S(1)}, u32[]{:S(2)}, u32[]{:S(2)}) collective-permute-start(bf16[1488,128]{1,0:T(8,128)(2,1)S(1)} %collective-permute-done.1.refs_0_.refs_2_), channel_id=1, source_target_pairs={{0,1},{1,0},{2,3},{3,2},{4,5},{5,4},{6,7},{7,6},{8,9},{9,8},{10,11... | collective-permute-start | bytes 1142792 | tf_op jit(solution)/shard_map/ppermute | solution.py:55
  14.9 6.2 %collective-permute-start.4 = (bf16[1488,128]{1,0:T(8,128)(2,1)S(1)}, bf16[1488,128]{1,0:T(8,128)(2,1)S(1)}, u32[]{:S(2)}, u32[]{:S(2)}) collective-permute-start(bf16[1488,128]{1,0:T(8,128)(2,1)S(1)} %collective-permute-done.2.refs_1_.refs_3_), channel_id=1, source_target_pairs={{0,1},{1,0},{2,3},{3,2},{4,5},{5,4},{6,7},{7,6},{8,9},{9,8},{10,11... | collective-permute-start | bytes 1142792 | tf_op jit(solution)/shard_map/ppermute | solution.py:55
  14.9 8.4 %collective-permute-start.6 = (bf16[1488,128]{1,0:T(8,128)(2,1)S(1)}, bf16[1488,128]{1,0:T(8,128)(2,1)S(1)}, u32[]{:S(2)}, u32[]{:S(2)}) collective-permute-start(bf16[1488,128]{1,0:T(8,128)(2,1)S(1)} %collective-permute-done.2.refs_1_.refs_3_), channel_id=1, source_target_pairs={{0,4},{1,3},{4,8},{5,1},{8,12},{9,5},{12,14},{13,9},{14,10},{15,13... | collective-permute-start | bytes 1142792 | tf_op jit(solution)/shard_map/ppermute | solution.py:51
  19.2 8.2 %collective-permute-start.9 = (bf16[1488,128]{1,0:T(8,128)(2,1)S(1)}, bf16[1488,128]{1,0:T(8,128)(2,1)S(1)}, u32[]{:S(2)}, u32[]{:S(2)}) collective-permute-start(bf16[1488,128]{1,0:T(8,128)(2,1)S(1)} %collective-permute-done.5.refs_0_.refs_6_), channel_id=1, source_target_pairs={{0,4},{1,3},{4,8},{5,1},{8,12},{9,5},{12,14},{13,9},{14,10},{15,13... | collective-permute-start | bytes 1142792 | tf_op jit(solution)/shard_map/ppermute | solution.py:51
  21.0 8.2 %collective-permute-start.7 = (bf16[1488,128]{1,0:T(8,128)(2,1)S(1)}, bf16[1488,128]{1,0:T(8,128)(2,1)S(1)}, u32[]{:S(2)}, u32[]{:S(2)}) collective-permute-start(bf16[1488,128]{1,0:T(8,128)(2,1)S(1)} %collective-permute-done.5.refs_0_.refs_6_), channel_id=1, source_target_pairs={{0,1},{1,0},{2,3},{3,2},{4,5},{5,4},{6,7},{7,6},{8,9},{9,8},{10,11... | collective-permute-start | bytes 1142792 | tf_op jit(solution)/shard_map/ppermute | solution.py:55
  23.2 5.9 %collective-permute-start.8 = (bf16[1488,128]{1,0:T(8,128)(2,1)S(1)}, bf16[1488,128]{1,0:T(8,128)(2,1)S(1)}, u32[]{:S(2)}, u32[]{:S(2)}) collective-permute-start(bf16[1488,128]{1,0:T(8,128)(2,1)S(1)} %collective-permute-done.6.refs_1_.refs_7_), channel_id=1, source_target_pairs={{0,1},{1,0},{2,3},{3,2},{4,5},{5,4},{6,7},{7,6},{8,9},{9,8},{10,11... | collective-permute-start | bytes 1142792 | tf_op jit(solution)/shard_map/ppermute | solution.py:55
  23.2 8.2 %collective-permute-start.10 = (bf16[1488,128]{1,0:T(8,128)(2,1)S(1)}, bf16[1488,128]{1,0:T(8,128)(2,1)S(1)}, u32[]{:S(2)}, u32[]{:S(2)}) collective-permute-start(bf16[1488,128]{1,0:T(8,128)(2,1)S(1)} %collective-permute-done.6.refs_1_.refs_7_), channel_id=1, source_target_pairs={{0,4},{1,3},{4,8},{5,1},{8,12},{9,5},{12,14},{13,9},{14,10},{15,13... | collective-permute-start | bytes 1142792 | tf_op jit(solution)/shard_map/ppermute | solution.py:51
  27.3 8.2 %collective-permute-start.13 = (bf16[1488,128]{1,0:T(8,128)(2,1)S(1)}, bf16[1488,128]{1,0:T(8,128)(2,1)S(1)}, u32[]{:S(2)}, u32[]{:S(2)}) collective-permute-start(bf16[1488,128]{1,0:T(8,128)(2,1)S(1)} %collective-permute-done.9.refs_0_.refs_10_), channel_id=1, source_target_pairs={{0,4},{1,3},{4,8},{5,1},{8,12},{9,5},{12,14},{13,9},{14,10},{15,13... | collective-permute-start | bytes 1142792 | tf_op jit(solution)/shard_map/ppermute | solution.py:51
  29.2 6.3 %collective-permute-start.11 = (bf16[1488,128]{1,0:T(8,128)(2,1)S(1)}, bf16[1488,128]{1,0:T(8,128)(2,1)S(1)}, u32[]{:S(2)}, u32[]{:S(2)}) collective-permute-start(bf16[1488,128]{1,0:T(8,128)(2,1)S(1)} %collective-permute-done.9.refs_0_.refs_10_), channel_id=1, source_target_pairs={{0,1},{1,0},{2,3},{3,2},{4,5},{5,4},{6,7},{7,6},{8,9},{9,8},{10,11... | collective-permute-start | bytes 1142792 | tf_op jit(solution)/shard_map/ppermute | solution.py:55
  31.4 4.1 %collective-permute-start.12 = (bf16[1488,128]{1,0:T(8,128)(2,1)S(1)}, bf16[1488,128]{1,0:T(8,128)(2,1)S(1)}, u32[]{:S(2)}, u32[]{:S(2)}) collective-permute-start(bf16[1488,128]{1,0:T(8,128)(2,1)S(1)} %collective-permute-done.10.refs_1_.refs_11_), channel_id=1, source_target_pairs={{0,1},{1,0},{2,3},{3,2},{4,5},{5,4},{6,7},{7,6},{8,9},{9,8},{10,11... | collective-permute-start | bytes 1142792 | tf_op jit(solution)/shard_map/ppermute | solution.py:55
  35.5 1.7 %copy-start = (s32[1,2]{1,0:T(1,128)S(1)}, s32[1,2]{1,0:T(1,128)}, u32[]{:S(2)}) copy-start(s32[1,2]{1,0:T(1,128)} %counts_ref.1) | copy-start | bytes 28
  35.5 1.7 %collective-permute-start.14 = (bf16[1488,128]{1,0:T(8,128)(2,1)S(1)}, bf16[1488,128]{1,0:T(8,128)(2,1)S(1)}, u32[]{:S(2)}, u32[]{:S(2)}) collective-permute-start(bf16[1488,128]{1,0:T(8,128)(2,1)S(1)} %collective-permute-done.13.refs_14_), channel_id=1, source_target_pairs={{0,1},{1,0},{2,3},{3,2},{4,5},{5,4},{6,7},{7,6},{8,9},{9,8},{10,11... | collective-permute-start | bytes 1142792 | tf_op jit(solution)/shard_map/ppermute | solution.py:55

commit v9 on v7

--- a/solution.py
+++ b/solution.py
@@ -41,14 +41,13 @@
     return jnp.where(side == 0, row, RING_CHIPS - 1 - row)
 
 
-def hop(value, from_other=False):
+def hop(value):
     half = RING_CHIPS // 2
     place = [2 * q if q < half else 2 * (RING_CHIPS - 1 - q) + 1 for q in range(RING_CHIPS)]
-    turn = int(from_other)
     pairs = []
     for q in range(RING_CHIPS):
-        pairs.append((2 * place[q] + turn, 2 * place[(q + 1) % RING_CHIPS]))
-        pairs.append((2 * place[q] + 1 - turn, 2 * place[(q - 1) % RING_CHIPS] + 1))
+        pairs.append((2 * place[q], 2 * place[(q + 1) % RING_CHIPS]))
+        pairs.append((2 * place[q] + 1, 2 * place[(q - 1) % RING_CHIPS] + 1))
     return lax.ppermute(value, "dp", pairs)
 
 
@@ -156,13 +155,9 @@
         copy.wait()
 
 
-def stage_kernel(away, first, me_ref, *refs):
-    refs = list(refs)
-    take = lambda k: [refs.pop(0) for _ in range(k)]
-    pieces = take(2)
-    x_ref, mixed_ref, adjoint_ref, values_ref, target_ref, top_target_ref, source_ref = take(7)
-    old_sums, old_bridge = (None, None) if first else take(2)
-    new_sums, new_bridge, both, up, down = refs
+def add_stage(away, me_ref, pieces, held, old, scratch):
+    x_ref, mixed_ref, adjoint_ref, values_ref, target_ref, top_target_ref, source_ref = held
+    both, up, down = scratch
     rows = both.shape[0] // 2
     half, pad = rows // 2, LANES // 2
     span = 2 * rows
@@ -204,22 +199,30 @@
         product = mm(activation, factor)
         products += [product[:, :LANES], product[:, LANES:]]
     bridge = mm_cols(down_up, lows)
-    if not first:
+    if old:
+        old_sums, old_bridge = old
         products = [p + old_sums[:, i * LANES : (i + 1) * LANES] for i, p in enumerate(products)]
         bridge = bridge + old_bridge[...]
+    return products, bridge
+
+
+def stage_kernel(away, first, me_ref, *refs):
+    pieces, held, old = refs[:2], refs[2:9], refs[9:-5]
+    (new_sums, new_bridge), scratch = refs[-5:-3], refs[-3:]
+    products, bridge = add_stage(away, me_ref, pieces, held, old, scratch)
     for i in range(SUMS):
         new_sums[:, i * LANES : (i + 1) * LANES] = products[i]
     new_bridge[...] = bridge
 
 
-def feature_kernel(width, counts_ref, sums_ref, bridge_ref, local_ref, expand_hbm, sketch_hbm, out_ref, *scratch):
-    expand_ref, sketch_ref, sems = scratch
-    more = load(((expand_hbm, expand_ref), (sketch_hbm, sketch_ref)), sems)
-    tokens = sums_ref.shape[0]
-    pad = LANES // 2
-    products = [sums_ref[:, i * LANES : (i + 1) * LANES] for i in range(SUMS)]
+def feature_kernel(away, me_ref, counts_ref, *refs):
+    pieces, held, old, local_ref, small_hbm, refs = refs[:2], refs[2:9], refs[9:11], refs[11], refs[12:14], refs[14:]
+    out_ref, scratch, (expand_ref, sketch_ref, sems) = refs[0], refs[1:4], refs[4:]
+    more = load(zip(small_hbm, (expand_ref, sketch_ref)), sems)
+    products, bridge = add_stage(away, me_ref, pieces, held, old, scratch)
     local = [local_ref[:, i * LANES : (i + 1) * LANES] for i in range(LOCAL_SUMS)]
-    bridge = bridge_ref[...]
+    tokens, width = held[0].shape
+    half = LANES // 2
     for copy in more:
         copy.wait()
     inverse = local[INVERSE]
@@ -242,34 +245,65 @@
     spread = jnp.concatenate([jnp.where(member, left, 0.0).astype(BF16) for left in lefts], axis=0)
     feats = mm_cols(spread, jnp.concatenate([right.astype(BF16) for right in rights], axis=0))
     for e in range(2):
-        own = feats[e * pad : (e + 1) * pad]
+        own = feats[e * half : (e + 1) * half]
         squares = jnp.sum(own * own, keepdims=True)
-        out_ref[pl.ds(e * pad, pad), :] = (own * lax.rsqrt(squares + 1e-06)).astype(BF16).astype(F32)
-
-
-def score_kernel(blocks, count, unit_ref, *refs):
-    block_refs, (out_ref, mean_ref) = refs[:blocks], refs[blocks:]
+        out_ref[pl.ds(e * half, half), :] = (own * lax.rsqrt(squares + 1e-06)).astype(BF16).astype(F32)
+
+
+def split_kernel(block_ref, *refs):
+    head_ref, tail_ref = refs[-2:]
+    cut, tail = head_ref.shape[0], block_ref.shape[0] - head_ref.shape[0]
+    head_ref[...] = block_ref[pl.ds(0, cut), :]
+    if len(refs) == 3:
+        tail_ref[pl.ds(0, tail), :] = refs[0][...]
+    tail_ref[pl.ds(tail_ref.shape[0] - tail, tail), :] = block_ref[pl.ds(cut, tail), :]
+
+
+def best_of(places, count, unit_ref, best):
     half = LANES // 2
     scale = float(half * LANES) ** 0.5
-    starts = [block.shape[0] - (half + 2) * count for block in block_refs]
     shape = (count, LANES)
-    totals = [[jnp.zeros(shape, F32) for _ in range(2)] for _ in block_refs]
+    totals = [[jnp.zeros(shape, F32) for _ in range(2)] for _ in places]
     for i in range(0, half, 2):
         units = [
             [jnp.broadcast_to(unit_ref[pl.ds(e * half + i + k, 1), :], shape) for k in range(2)]
             for e in range(2)
         ]
-        for b, block in enumerate(block_refs):
-            wide = block[pl.ds(starts[b] + i * count, 2 * count), :].astype(F32)
+        for b, (block, start) in enumerate(places):
+            wide = block[pl.ds(start + i * count, 2 * count), :].astype(F32)
             for e in range(2):
                 totals[b][e] = totals[b][e] + (wide[:count] * units[e][0] + wide[count:] * units[e][1])
-    best = [[jnp.full(shape, -2.0 * scale, F32) for _ in range(TASKS)] for _ in range(2)]
-    for b, block in enumerate(block_refs):
-        labels = block[pl.ds(starts[b] + half * count, 2 * count), :].astype(F32)[:count]
+    for b, (block, start) in enumerate(places):
+        labels = block[pl.ds(start + half * count, 2 * count), :].astype(F32)[:count]
         for e in range(2):
             similar = scale * jnp.sum(totals[b][e], axis=1, keepdims=True)
             for t in range(TASKS):
                 best[e][t] = jnp.maximum(best[e][t], jnp.where(labels == float(t), similar, -2.0 * scale))
+
+
+def places_of(blocks, count):
+    size = (LANES // 2 + 2) * count
+    places = []
+    for block in blocks:
+        total = block.shape[0]
+        firsts = range(0, total, size) if total % size == 0 else [total - size]
+        places += [(block, first) for first in firsts]
+    return places
+
+
+def score_kernel(blocks, count, unit_ref, *refs):
+    block_refs, best_ref = refs[:blocks], refs[blocks]
+    lowest = -2.0 * float(LANES // 2 * LANES) ** 0.5
+    best = [[jnp.full((count, LANES), lowest, F32) for _ in range(TASKS)] for _ in range(2)]
+    best_of(places_of(block_refs, count), count, unit_ref, best)
+    for e in range(2):
+        for t in range(TASKS):
+            best_ref[e, t] = best[e][t]
+
+
+def last_score_kernel(count, unit_ref, block_ref, best_ref, out_ref, mean_ref):
+    best = [[best_ref[e, t] for t in range(TASKS)] for e in range(2)]
+    best_of(places_of([block_ref], count), count, unit_ref, best)
     for e in range(2):
         values = [jnp.max(best[e][t]) for t in range(TASKS)]
         for t in range(TASKS):
@@ -375,6 +409,12 @@
         name="local_products",
     )(*in_hbm(inputs))
 
+    stage_scratch = [
+        pltpu.VMEM((2 * rows, 2 * LANES), BF16),
+        pltpu.VMEM((rows + LANES // 2, 2 * LANES), BF16),
+        pltpu.VMEM((2 * rows, LANES), BF16),
+    ]
+
     def stage(away, pieces, sums):
         first = not sums
         start = 1 + len(pieces) + len(activations)
@@ -386,61 +426,93 @@
             ],
             in_specs=[SMEM] + [VMEM] * (len(pieces) + len(activations) + len(sums)),
             out_specs=[VMEM, VMEM],
-            scratch_shapes=[
-                pltpu.VMEM((2 * rows, 2 * LANES), BF16),
-                pltpu.VMEM((rows + LANES // 2, 2 * LANES), BF16),
-                pltpu.VMEM((2 * rows, LANES), BF16),
-            ],
+            scratch_shapes=stage_scratch,
             input_output_aliases={} if first else {start: 0, start + 1: 1},
             compiler_params=params(16),
             cost_estimate=cost(tokens * rows * LANES * 16, 2 * MIB),
             name="stage",
         )(me.reshape(1), *pieces, *activations, *sums)
 
+    def split(block, *tails):
+        tail = block.shape[0] - 3 * rows
+        shapes = (3 * rows, LANES), ((1 + len(tails)) * tail, LANES)
+        return pl.pallas_call(
+            split_kernel,
+            out_shape=[jax.ShapeDtypeStruct(shape, BF16) for shape in shapes],
+            in_specs=[VMEM] * (1 + len(tails)),
+            out_specs=[VMEM, VMEM],
+            compiler_params=params(8),
+            name="split",
+        )(block, *tails)
+
     tie = lax.optimization_barrier
     half = RING_CHIPS // 2
     held = [own, other_core(own)]
     blocks = list(held)
-    first, second = hop(own), hop(own, from_other=True)
+    first, second = hop(held[0]), hop(held[1])
     first, activations = tie((first, activations))
     sums = stage(0, held, [])
     second, sums = tie((second, sums))
     for k in range(1, half):
         held = [first, second]
         crossed = [other_core(first), other_core(second)]
-        blocks += held + crossed
+        blocks += [first, crossed[0]]
+        if k < half - 1:
+            blocks += [second, crossed[1]]
+        else:
+            first, tails = split(first, tail)
         first = hop(first)
         sums = stage(k, held, sums)
         first, sums = tie((first, sums))
+        if k == half - 2:
+            second, tail = split(second)
         if k < half - 1:
             second = hop(second)
         sums = stage(-k, crossed, sums)
         if k < half - 1:
             second, sums = tie((second, sums))
-    held = [first, other_core(first)]
-    blocks += held
-    sums = stage(half, held, sums)
+    tails = hop(tails)
     small = (top_expander_sketch.T, top_reducer_sketch)
     unit = pl.pallas_call(
-        functools.partial(feature_kernel, width),
+        functools.partial(feature_kernel, half),
         out_shape=jax.ShapeDtypeStruct((LANES, LANES), F32),
-        in_specs=[SMEM] + [VMEM] * 3 + [HBM] * 2,
+        in_specs=[SMEM] * 2 + [VMEM] * (2 + len(activations) + 3) + [HBM] * 2,
         out_specs=VMEM,
-        scratch_shapes=[pltpu.VMEM(a.shape, a.dtype) for a in small] + [pltpu.SemaphoreType.DMA((2,))],
+        scratch_shapes=stage_scratch
+        + [pltpu.VMEM(a.shape, a.dtype) for a in small]
+        + [pltpu.SemaphoreType.DMA((2,))],
         compiler_params=params(16),
-        cost_estimate=cost(tokens * LANES * LANES * 20, 4 * MIB),
+        cost_estimate=cost(1, 1),
         name="features",
-    )(sequence_token_counts, *sums, local, *in_hbm(small))
-
-    task_best, scores = pl.pallas_call(
+    )(
+        me.reshape(1),
+        sequence_token_counts,
+        first,
+        other_core(first),
+        *activations,
+        *sums,
+        local,
+        *in_hbm(small),
+    )
+    tails, unit = tie((tails, unit))
+    blocks.append(tails)
+    best = pl.pallas_call(
         functools.partial(score_kernel, len(blocks), count),
-        out_shape=(jax.ShapeDtypeStruct((2, TASKS), F32), jax.ShapeDtypeStruct((2,), F32)),
+        out_shape=jax.ShapeDtypeStruct((2, TASKS, count, LANES), F32),
         in_specs=[VMEM] * (1 + len(blocks)),
-        out_specs=(SMEM, SMEM),
+        out_specs=VMEM,
         compiler_params=params(16),
         cost_estimate=cost(4 * MIB, 2 * MIB),
         name="scores",
     )(unit, *blocks)
+    task_best, scores = pl.pallas_call(
+        functools.partial(last_score_kernel, count),
+        out_shape=(jax.ShapeDtypeStruct((2, TASKS), F32), jax.ShapeDtypeStruct((2,), F32)),
+        in_specs=[VMEM] * 3,
+        out_specs=(SMEM, SMEM),
+        compiler_params=params(8),
+        name="last_scores",
+    )(unit, other_core(tails), best)
     return (scores, task_best)
 
 

time: 44.7 us -> 40.4 us (0.904)
  waiting for transfers between devices: 14.5 us -> 7.45 us
  starting transfers between devices: 13.1 us -> 16 us
    ppermute x7 -> x8, waiting for transfers between devices: 13.6 us -> 6.21 us  [hop(): return lax.ppermute(value, 'dp', pairs)]
    ppermute x7 -> x8, starting transfers between devices: 12.5 us -> 15.2 us  [hop(): return lax.ppermute(value, 'dp', pairs)]
    pallas_call x1 -> x4, Pallas kernels: 1.89 us -> 3.43 us  [the longest x1 2.49 us: shards(): pl.pallas_call(functools.partial(feature_kernel, half), out_shape=jax.Sha...]
    pallas_call x8 -> x7, Pallas kernels: 6.41 us -> 5.58 us  [stage(): pl.pallas_call(functools.partial(stage_kernel, away, first), out_shape=[j...]
    pallas_call x1, Pallas kernels: 1.67 us -> 0.87 us  [shards(): pl.pallas_call(functools.partial(score_kernel, len(blocks), count), out_s...]
    ppermute x8 -> x9, waiting for transfers between devices: 0.9 us -> 1.24 us  [other_core(): lax.ppermute(value, 'dp', [(d, d ^ 1) for d in range(2 * RING_CHIPS)])]
  transfers between devices with their start and end apart: 15 -> 17, of which waited for: 7 -> 7; matrix products, arithmetic and copies ran while one was open for 0% -> 0% of each run, Pallas kernels for 23% -> 34%
where the time goes in v9:
time: 40.4 us; the launch traced here: 40.1 us
  starting transfers between devices  16 us (40%)
  Pallas kernels  15.9 us (39%)
  waiting for transfers between devices  7.45 us (18%)
  between operations  0.78 us (2%)
    ppermute x8, starting transfers between devices, hop(): return lax.ppermute(value, 'dp', pairs)  15.2 us
    ppermute x8, waiting for transfers between devices, hop(): return lax.ppermute(value, 'dp', pairs)  6.21 us
    pallas_call x7, Pallas kernels, stage(): pl.pallas_call(functools.partial(stage_kernel, away, first), out_shape=[j...  5.58 us
    pallas_call x1, Pallas kernels, shards(): pl.pallas_call(local_kernel, out_shape=[jax.ShapeDtypeStruct(a.shape, a.d...  4.6 us
    pallas_call x1, Pallas kernels, shards(): pl.pallas_call(functools.partial(feature_kernel, half), out_shape=jax.Sha...  2.49 us
    pallas_call x1, Pallas kernels, shards(): pl.pallas_call(pack_kernel, out_shape=jax.ShapeDtypeStruct((3 * rows + (L...  1.41 us
    ppermute x9, waiting for transfers between devices, other_core(): lax.ppermute(value, 'dp', [(d, d ^ 1) for d in range(2 * RING_CHIPS)])  1.24 us
    pallas_call x1, Pallas kernels, shards(): pl.pallas_call(functools.partial(last_score_kernel, count), out_shape=(ja...  0.89 us
  transfers between devices with their start and end apart: 17, of which 7 were waited for; matrix products, arithmetic and copies ran while one was open for 0% of the time, Pallas kernels for 34%

profile of v9, /device:TPU:0, one launch (start us, length us, event | category | flops | bytes accessed | tf_op | source)
XLA Modules:
  0.0 40.1 jit_solution(713741045395864856)
XLA Ops:
  0.6 1.4 %pack.1.refs_0_ = bf16[1488,128]{1,0:T(8,128)(2,1)S(1)} custom-call(s32[1]{0:T(128)} %bitcast.me_ref, f32[40,128]{1,0:T(8,128)} %bitcast.10, bf16[320,128]{1,0:T(8,128)(2,1)} %refs_1_.2, bf16[320,128]{1,0:T(8,128)(2,1)} %bitcast.12, bf16[128,128]{1,0:T(8,128)(2,1)} %refs_3_.2, bf16[160,128]{1,0:T(8,128)(2,1)} %bitcast.13, bf16[320,128]{1,0:T(8,128)(2,1)} %refs_5_.2, ...), custom_call_target="tpu_custom_call" | custom-call | tf_op jit(solution)/shard_map/pack/pallas_call | solution.py:375
  2.1 0.5 %collective-permute-start.2 = (bf16[1488,128]{1,0:T(8,128)(2,1)S(1)}, bf16[1488,128]{1,0:T(8,128)(2,1)S(1)}, u32[]{:S(2)}, u32[]{:S(2)}) collective-permute-start(bf16[1488,128]{1,0:T(8,128)(2,1)S(1)} %pack.1.refs_0_), channel_id=1, source_target_pairs={{0,1},{1,0},{2,3},{3,2},{4,5},{5,4},{6,7},{7,6},{8,9},{9,8},{10,11... | collective-permute-start | bytes 1142792 | tf_op jit(solution)/shard_map/ppermute | solution.py:55
  2.6 2.6 %collective-permute-start = (bf16[1488,128]{1,0:T(8,128)(2,1)S(1)}, bf16[1488,128]{1,0:T(8,128)(2,1)S(1)}, u32[]{:S(2)}, u32[]{:S(2)}) collective-permute-start(bf16[1488,128]{1,0:T(8,128)(2,1)S(1)} %pack.1.refs_0_), channel_id=1, source_target_pairs={{0,4},{1,3},{4,8},{5,1},{8,12},{9,5},{12,14},{13,9},{14,10},{15,13... | collective-permute-start | bytes 1142792 | tf_op jit(solution)/shard_map/ppermute | solution.py:51
  5.2 0.0 collective-permute-done.2.refs_1_
  5.2 1.6 %collective-permute-start.3 = (bf16[1488,128]{1,0:T(8,128)(2,1)S(1)}, bf16[1488,128]{1,0:T(8,128)(2,1)S(1)}, u32[]{:S(2)}, u32[]{:S(2)}) collective-permute-start(bf16[1488,128]{1,0:T(8,128)(2,1)S(1)} %collective-permute-done.2.refs_1_), channel_id=1, source_target_pairs={{0,4},{1,3},{4,8},{5,1},{8,12},{9,5},{12,14},{13,9},{14,10},{15,13... | collective-permute-start | bytes 1142792 | tf_op jit(solution)/shard_map/ppermute | solution.py:51
  6.8 4.6 %local_products.1 = (bf16[256,5120]{1,0:T(8,128)(2,1)S(1)}, bf16[256,5120]{1,0:T(8,128)(2,1)S(1)}, bf16[256,5120]{1,0:T(8,128)(2,1)S(1)}, bf16[256,2560]{1,0:T(8...) custom-call(bf16[256,5120]{1,0:T(8,128)(2,1)} %refs_0_.1, ...), custom_call_target="tpu_custom_call" | custom-call | flops 1006632960 | bytes 14680064 | tf_op jit(solution)/shard_map/local_products/pallas_call | solution.py:396
  11.5 1.6 %collective-permute-start.1 = (bf16[1488,128]{1,0:T(8,128)(2,1)S(1)}, bf16[1488,128]{1,0:T(8,128)(2,1)S(1)}, u32[]{:S(2)}, u32[]{:S(2)}) collective-permute-start(bf16[1488,128]{1,0:T(8,128)(2,1)S(1)} %collective-permute-done.refs_0_.refs_2_), channel_id=1, source_target_pairs={{0,4},{1,3},{4,8},{5,1},{8,12},{9,5},{12,14},{13,9},{14,10},{15,13... | collective-permute-start | bytes 1142792 | tf_op jit(solution)/shard_map/ppermute | solution.py:51
  13.1 0.0 collective-permute-start.6
  13.1 0.7 %stage.7 = (f32[256,1024]{1,0:T(8,128)S(1)}, f32[128,256]{1,0:T(8,128)S(1)}) custom-call(s32[1]{0:T(128)} %bitcast.me_ref, bf16[1488,128]{1,0:T(8,128)(2,1)S(1)} %pack.1.refs_0_, bf16[1488,128]{1,0:T(8,128)(2,1)S(1)} %collective-permute-done.2.refs_1_, bf16[256,5120]{1,0:T(8,128)(2,1)S(1)} %get-tuple-element.66.refs_2_, ...), custom_call_target="tpu_custom_call" | custom-call | flops 167772160 | bytes 2097152 | tf_op jit(solution)/shard_map/stage/pallas_call | solution.py:421
  13.8 1.1 %collective-permute-done.3.refs_1_.refs_4_ = bf16[1488,128]{1,0:T(8,128)(2,1)S(1)} collective-permute-done((bf16[1488,128]{1,0:T(8,128)(2,1)S(1)}, bf16[1488,128]{1,0:T(8,128)(2,1)S(1)}, u32[]{:S(2)}, u32[]{:S(2)}) %collective-permute-start.3) | collective-permute-done | bytes 380960 | tf_op jit(solution)/shard_map/ppermute | solution.py:51
  14.9 2.1 %collective-permute-start.5 = (bf16[1488,128]{1,0:T(8,128)(2,1)S(1)}, bf16[1488,128]{1,0:T(8,128)(2,1)S(1)}, u32[]{:S(2)}, u32[]{:S(2)}) collective-permute-start(bf16[1488,128]{1,0:T(8,128)(2,1)S(1)} %collective-permute-done.3.refs_1_.refs_4_), channel_id=1, source_target_pairs={{0,4},{1,3},{4,8},{5,1},{8,12},{9,5},{12,14},{13,9},{14,10},{15,13... | collective-permute-start | bytes 1142792 | tf_op jit(solution)/shard_map/ppermute | solution.py:51
  16.9 0.8 %stage.8 = (f32[256,1024]{1,0:T(8,128)S(1)}, f32[128,256]{1,0:T(8,128)S(1)}) custom-call(s32[1]{0:T(128)} %bitcast.me_ref, bf16[1488,128]{1,0:T(8,128)(2,1)S(1)} %collective-permute-done.refs_0_.refs_2_, bf16[1488,128]{1,0:T(8,128)(2,1)S(1)} %collective-permute-done.3.refs_1_.refs_4_, ...), custom_call_target="tpu_custom_call", output_to_operand_aliasing={{0}: (10, {}), {1}: (11, {})} | custom-call | flops 167772160 | bytes 2097152 | tf_op jit(solution)/shard_map/stage/pallas_call | solution.py:421
  17.8 1.4 %collective-permute-done.1.refs_0_.refs_6_ = bf16[1488,128]{1,0:T(8,128)(2,1)S(1)} collective-permute-done((bf16[1488,128]{1,0:T(8,128)(2,1)S(1)}, bf16[1488,128]{1,0:T(8,128)(2,1)S(1)}, u32[]{:S(2)}, u32[]{:S(2)}) %collective-permute-start.1) | collective-permute-done | bytes 380960 | tf_op jit(solution)/shard_map/ppermute | solution.py:51
  19.2 1.9 %collective-permute-start.4 = (bf16[1488,128]{1,0:T(8,128)(2,1)S(1)}, bf16[1488,128]{1,0:T(8,128)(2,1)S(1)}, u32[]{:S(2)}, u32[]{:S(2)}) collective-permute-start(bf16[1488,128]{1,0:T(8,128)(2,1)S(1)} %collective-permute-done.1.refs_0_.refs_6_), channel_id=1, source_target_pairs={{0,4},{1,3},{4,8},{5,1},{8,12},{9,5},{12,14},{13,9},{14,10},{15,13... | collective-permute-start | bytes 1142792 | tf_op jit(solution)/shard_map/ppermute | solution.py:51
  21.0 0.8 %stage.9 = (f32[256,1024]{1,0:T(8,128)S(1)}, f32[128,256]{1,0:T(8,128)S(1)}) custom-call(s32[1]{0:T(128)} %bitcast.me_ref, bf16[1488,128]{1,0:T(8,128)(2,1)S(1)} %collective-permute-done.6.refs_0_.refs_3_, bf16[1488,128]{1,0:T(8,128)(2,1)S(1)} %collective-permute-done.7.refs_1_.refs_5_, ...), custom_call_target="tpu_custom_call", output_to_operand_aliasing={{0}: (10, {}), {1}: (11, {})} | custom-call | flops 167772160 | bytes 2097152 | tf_op jit(solution)/shard_map/stage/pallas_call | solution.py:421
  21.8 1.4 %collective-permute-done.5.refs_1_.block_ref.refs_8_ = bf16[1488,128]{1,0:T(8,128)(2,1)S(1)} collective-permute-done((bf16[1488,128]{1,0:T(8,128)(2,1)S(1)}, bf16[1488,128]{1,0:T(8,128)(2,1)S(1)}, u32[]{:S(2)}, u32[]{:S(2)}) %collective-permute-start.5) | collective-permute-done | bytes 380960 | tf_op jit(solution)/shard_map/ppermute | solution.py:51
  23.3 1.9 %collective-permute-start.10 = (bf16[960,128]{1,0:T(8,128)(2,1)S(1)}, bf16[960,128]{1,0:T(8,128)(2,1)S(1)}, u32[]{:S(2)}, u32[]{:S(2)}) collective-permute-start(bf16[960,128]{1,0:T(8,128)(2,1)S(1)} %get-tuple-element.94), channel_id=1, source_target_pairs={{0,4},{1,3},{4,8},{5,1},{8,12},{9,5},{12,14},{13,9},{14,10},{15,13... | collective-permute-start | bytes 737288 | tf_op jit(solution)/shard_map/ppermute | solution.py:51
  25.2 0.8 %stage.10 = (f32[256,1024]{1,0:T(8,128)S(1)}, f32[128,256]{1,0:T(8,128)S(1)}) custom-call(s32[1]{0:T(128)} %bitcast.me_ref, bf16[1488,128]{1,0:T(8,128)(2,1)S(1)} %collective-permute-done.1.refs_0_.refs_6_, bf16[1488,128]{1,0:T(8,128)(2,1)S(1)} %collective-permute-done.5.refs_1_.block_ref.refs_8_, ...), custom_call_target="tpu_custom_call", output_to_operand_aliasing={{0}: (10, {}), {1}: (11, {})} | custom-call | flops 167772160 | bytes 2097152 | tf_op jit(solution)/shard_map/stage/pallas_call | solution.py:421
  26.0 1.3 %collective-permute-done.4.block_ref.refs_0_.refs_10_ = bf16[1488,128]{1,0:T(8,128)(2,1)S(1)} collective-permute-done((bf16[1488,128]{1,0:T(8,128)(2,1)S(1)}, bf16[1488,128]{1,0:T(8,128)(2,1)S(1)}, u32[]{:S(2)}, u32[]{:S(2)}) %collective-permute-start.4) | collective-permute-done | bytes 380960 | tf_op jit(solution)/shard_map/ppermute | solution.py:51
  27.4 1.9 %collective-permute-start.9 = (bf16[960,128]{1,0:T(8,128)(2,1)S(1)}, bf16[960,128]{1,0:T(8,128)(2,1)S(1)}, u32[]{:S(2)}, u32[]{:S(2)}) collective-permute-start(bf16[960,128]{1,0:T(8,128)(2,1)S(1)} %get-tuple-element.93), channel_id=1, source_target_pairs={{0,4},{1,3},{4,8},{5,1},{8,12},{9,5},{12,14},{13,9},{14,10},{15,13... | collective-permute-start | bytes 737288 | tf_op jit(solution)/shard_map/ppermute | solution.py:51
  29.3 1.6 %collective-permute-start.8 = (bf16[1056,128]{1,0:T(8,128)(2,1)S(1)}, bf16[1056,128]{1,0:T(8,128)(2,1)S(1)}, u32[]{:S(2)}, u32[]{:S(2)}) collective-permute-start(bf16[1056,128]{1,0:T(8,128)(2,1)S(1)} %get-tuple-element.92), channel_id=1, source_target_pairs={{0,4},{1,3},{4,8},{5,1},{8,12},{9,5},{12,14},{13,9},{14,10},{15,13... | collective-permute-start | bytes 811016 | tf_op jit(solution)/shard_map/ppermute | solution.py:51
  30.9 0.8 %stage.11 = (f32[256,1024]{1,0:T(8,128)S(1)}, f32[128,256]{1,0:T(8,128)S(1)}) custom-call(s32[1]{0:T(128)} %bitcast.me_ref, bf16[1488,128]{1,0:T(8,128)(2,1)S(1)} %collective-permute-done.11.refs_0_.refs_7_, bf16[1488,128]{1,0:T(8,128)(2,1)S(1)} %collective-permute-done.12.refs_1_.refs_9_, ...), custom_call_target="tpu_custom_call", output_to_operand_aliasing={{0}: (10, {}), {1}: (11, {})} | custom-call | flops 167772160 | bytes 2097152 | tf_op jit(solution)/shard_map/stage/pallas_call | solution.py:421
  31.7 0.1 collective-permute-start.15
  31.8 0.8 %stage.12 = (f32[256,1024]{1,0:T(8,128)S(1)}, f32[128,256]{1,0:T(8,128)S(1)}) custom-call(s32[1]{0:T(128)} %bitcast.me_ref, bf16[1488,128]{1,0:T(8,128)(2,1)S(1)} %collective-permute-done.4.block_ref.refs_0_.refs_10_, bf16[960,128]{1,0:T(8,128)(2,1)S(1)} %collective-permute-done.10.refs_1_, ...), custom_call_target="tpu_custom_call", output_to_operand_aliasing={{0}: (10, {}), {1}: (11, {})} | custom-call | flops 167772160 | bytes 2097152 | tf_op jit(solution)/shard_map/stage/pallas_call | solution.py:421
  32.6 1.0 %collective-permute-done.9.refs_0_ = bf16[960,128]{1,0:T(8,128)(2,1)S(1)} collective-permute-done((bf16[960,128]{1,0:T(8,128)(2,1)S(1)}, bf16[960,128]{1,0:T(8,128)(2,1)S(1)}, u32[]{:S(2)}, u32[]{:S(2)}) %collective-permute-start.9) | collective-permute-done | bytes 245792 | tf_op jit(solution)/shard_map/ppermute | solution.py:51
  33.6 0.8 %stage.13 = (f32[256,1024]{1,0:T(8,128)S(1)}, f32[128,256]{1,0:T(8,128)S(1)}) custom-call(s32[1]{0:T(128)} %bitcast.me_ref, bf16[1488,128]{1,0:T(8,128)(2,1)S(1)} %collective-permute-done.14.refs_0_.refs_11_, bf16[960,128]{1,0:T(8,128)(2,1)S(1)} %collective-permute-done.15.refs_1_, ...), custom_call_target="tpu_custom_call", output_to_operand_aliasing={{0}: (10, {}), {1}: (11, {})} | custom-call | flops 167772160 | bytes 2097152 | tf_op jit(solution)/shard_map/stage/pallas_call | solution.py:421
  34.4 0.7 %collective-permute-done.13.refs_1_ = bf16[960,128]{1,0:T(8,128)(2,1)S(1)} collective-permute-done((bf16[960,128]{1,0:T(8,128)(2,1)S(1)}, bf16[960,128]{1,0:T(8,128)(2,1)S(1)}, u32[]{:S(2)}, u32[]{:S(2)}) %collective-permute-start.13) | collective-permute-done | bytes 245792 | tf_op jit(solution)/shard_map/ppermute | solution.py:55
  35.1 2.5 %features.1.unit_ref = f32[128,128]{1,0:T(8,128)S(1)} custom-call(s32[1]{0:T(128)} %bitcast.me_ref, s32[1,2]{1,0:T(1,128)S(1)} %copy-done, bf16[960,128]{1,0:T(8,128)(2,1)S(1)} %collective-permute-done.9.refs_0_, bf16[960,128]{1,0:T(8,128)(2,1)S(1)} %collective-permute-done.13.refs_1_, bf16[256,5120]{1,0:T(8,128)(2,1)S(1)} %get-tuple-element.66.refs_2_, ...), custom_call_target="tpu_custom_call" | custom-call | flops 1 | bytes 1 | tf_op jit(solution)/shard_map/features/pallas_call | solution.py:476
  37.6 0.2 collective-permute-start.16
  37.8 0.9 %scores.1.best_ref = f32[2,3,8,128]{3,2,1,0:T(8,128)S(1)} custom-call(f32[128,128]{1,0:T(8,128)S(1)} %features.1.unit_ref, bf16[1488,128]{1,0:T(8,128)(2,1)S(1)} %pack.1.refs_0_, bf16[1488,128]{1,0:T(8,128)(2,1)S(1)} %collective-permute-done.2.refs_1_, bf16[1488,128]{1,0:T(8,128)(2,1)S(1)} %collective-permute-done.refs_0_.refs_2_, ...), custom_call_target="tpu_custom_call" | custom-call | flops 4194304 | bytes 2097152 | tf_op jit(solution)/shard_map/scores/pallas_call | solution.py:499
  38.7 0.5 %collective-permute-done.16.block_ref = bf16[1056,128]{1,0:T(8,128)(2,1)S(1)} collective-permute-done((bf16[1056,128]{1,0:T(8,128)(2,1)S(1)}, bf16[1056,128]{1,0:T(8,128)(2,1)S(1)}, u32[]{:S(2)}, u32[]{:S(2)}) %collective-permute-start.16) | collective-permute-done | bytes 270368 | tf_op jit(solution)/shard_map/ppermute | solution.py:55
  39.2 0.9 %last_scores.1 = (f32[2,3]{1,0:T(2,128)}, f32[2]{0:T(128)}) custom-call(f32[128,128]{1,0:T(8,128)S(1)} %features.1.unit_ref, bf16[1056,128]{1,0:T(8,128)(2,1)S(1)} %collective-permute-done.16.block_ref, f32[2,3,8,128]{3,2,1,0:T(8,128)S(1)} %scores.1.best_ref), custom_call_target="tpu_custom_call" | custom-call | tf_op jit(solution)/shard_map/last_scores/pallas_call | solution.py:508
  (18 shorter events, 0.1 us)
Async XLA Ops:
  2.1 3.2 %collective-permute-start.2 = (bf16[1488,128]{1,0:T(8,128)(2,1)S(1)}, bf16[1488,128]{1,0:T(8,128)(2,1)S(1)}, u32[]{:S(2)}, u32[]{:S(2)}) collective-permute-start(bf16[1488,128]{1,0:T(8,128)(2,1)S(1)} %pack.1.refs_0_), channel_id=1, source_target_pairs={{0,1},{1,0},{2,3},{3,2},{4,5},{5,4},{6,7},{7,6},{8,9},{9,8},{10,11... | collective-permute-start | bytes 1142792 | tf_op jit(solution)/shard_map/ppermute | solution.py:55
  2.6 8.9 %collective-permute-start = (bf16[1488,128]{1,0:T(8,128)(2,1)S(1)}, bf16[1488,128]{1,0:T(8,128)(2,1)S(1)}, u32[]{:S(2)}, u32[]{:S(2)}) collective-permute-start(bf16[1488,128]{1,0:T(8,128)(2,1)S(1)} %pack.1.refs_0_), channel_id=1, source_target_pairs={{0,4},{1,3},{4,8},{5,1},{8,12},{9,5},{12,14},{13,9},{14,10},{15,13... | collective-permute-start | bytes 1142792 | tf_op jit(solution)/shard_map/ppermute | solution.py:51
  5.2 9.6 %collective-permute-start.3 = (bf16[1488,128]{1,0:T(8,128)(2,1)S(1)}, bf16[1488,128]{1,0:T(8,128)(2,1)S(1)}, u32[]{:S(2)}, u32[]{:S(2)}) collective-permute-start(bf16[1488,128]{1,0:T(8,128)(2,1)S(1)} %collective-permute-done.2.refs_1_), channel_id=1, source_target_pairs={{0,4},{1,3},{4,8},{5,1},{8,12},{9,5},{12,14},{13,9},{14,10},{15,13... | collective-permute-start | bytes 1142792 | tf_op jit(solution)/shard_map/ppermute | solution.py:51
  11.5 7.7 %collective-permute-start.1 = (bf16[1488,128]{1,0:T(8,128)(2,1)S(1)}, bf16[1488,128]{1,0:T(8,128)(2,1)S(1)}, u32[]{:S(2)}, u32[]{:S(2)}) collective-permute-start(bf16[1488,128]{1,0:T(8,128)(2,1)S(1)} %collective-permute-done.refs_0_.refs_2_), channel_id=1, source_target_pairs={{0,4},{1,3},{4,8},{5,1},{8,12},{9,5},{12,14},{13,9},{14,10},{15,13... | collective-permute-start | bytes 1142792 | tf_op jit(solution)/shard_map/ppermute | solution.py:51
  13.1 7.9 %collective-permute-start.6 = (bf16[1488,128]{1,0:T(8,128)(2,1)S(1)}, bf16[1488,128]{1,0:T(8,128)(2,1)S(1)}, u32[]{:S(2)}, u32[]{:S(2)}) collective-permute-start(bf16[1488,128]{1,0:T(8,128)(2,1)S(1)} %collective-permute-done.refs_0_.refs_2_), channel_id=1, source_target_pairs={{0,1},{1,0},{2,3},{3,2},{4,5},{5,4},{6,7},{7,6},{8,9},{9,8},{10,11... | collective-permute-start | bytes 1142792 | tf_op jit(solution)/shard_map/ppermute | solution.py:55
  14.9 6.2 %collective-permute-start.7 = (bf16[1488,128]{1,0:T(8,128)(2,1)S(1)}, bf16[1488,128]{1,0:T(8,128)(2,1)S(1)}, u32[]{:S(2)}, u32[]{:S(2)}) collective-permute-start(bf16[1488,128]{1,0:T(8,128)(2,1)S(1)} %collective-permute-done.3.refs_1_.refs_4_), channel_id=1, source_target_pairs={{0,1},{1,0},{2,3},{3,2},{4,5},{5,4},{6,7},{7,6},{8,9},{9,8},{10,11... | collective-permute-start | bytes 1142792 | tf_op jit(solution)/shard_map/ppermute | solution.py:55
  14.9 8.4 %collective-permute-start.5 = (bf16[1488,128]{1,0:T(8,128)(2,1)S(1)}, bf16[1488,128]{1,0:T(8,128)(2,1)S(1)}, u32[]{:S(2)}, u32[]{:S(2)}) collective-permute-start(bf16[1488,128]{1,0:T(8,128)(2,1)S(1)} %collective-permute-done.3.refs_1_.refs_4_), channel_id=1, source_target_pairs={{0,4},{1,3},{4,8},{5,1},{8,12},{9,5},{12,14},{13,9},{14,10},{15,13... | collective-permute-start | bytes 1142792 | tf_op jit(solution)/shard_map/ppermute | solution.py:51
  19.2 8.2 %collective-permute-start.4 = (bf16[1488,128]{1,0:T(8,128)(2,1)S(1)}, bf16[1488,128]{1,0:T(8,128)(2,1)S(1)}, u32[]{:S(2)}, u32[]{:S(2)}) collective-permute-start(bf16[1488,128]{1,0:T(8,128)(2,1)S(1)} %collective-permute-done.1.refs_0_.refs_6_), channel_id=1, source_target_pairs={{0,4},{1,3},{4,8},{5,1},{8,12},{9,5},{12,14},{13,9},{14,10},{15,13... | collective-permute-start | bytes 1142792 | tf_op jit(solution)/shard_map/ppermute | solution.py:51
  21.0 8.3 %collective-permute-start.11 = (bf16[1488,128]{1,0:T(8,128)(2,1)S(1)}, bf16[1488,128]{1,0:T(8,128)(2,1)S(1)}, u32[]{:S(2)}, u32[]{:S(2)}) collective-permute-start(bf16[1488,128]{1,0:T(8,128)(2,1)S(1)} %collective-permute-done.1.refs_0_.refs_6_), channel_id=1, source_target_pairs={{0,1},{1,0},{2,3},{3,2},{4,5},{5,4},{6,7},{7,6},{8,9},{9,8},{10,11... | collective-permute-start | bytes 1142792 | tf_op jit(solution)/shard_map/ppermute | solution.py:55
  23.2 7.6 %collective-permute-start.12 = (bf16[1488,128]{1,0:T(8,128)(2,1)S(1)}, bf16[1488,128]{1,0:T(8,128)(2,1)S(1)}, u32[]{:S(2)}, u32[]{:S(2)}) collective-permute-start(bf16[1488,128]{1,0:T(8,128)(2,1)S(1)} %collective-permute-done.5.refs_1_.block_ref.refs_8_), channel_id=1, source_target_pairs={{0,1},{1,0},{2,3},{3,2},{4,5},{5,4},{6,7},{7,6},{8,9},{9,8},{10,11... | collective-permute-start | bytes 1142792 | tf_op jit(solution)/shard_map/ppermute | solution.py:55
  23.3 8.4 %collective-permute-start.10 = (bf16[960,128]{1,0:T(8,128)(2,1)S(1)}, bf16[960,128]{1,0:T(8,128)(2,1)S(1)}, u32[]{:S(2)}, u32[]{:S(2)}) collective-permute-start(bf16[960,128]{1,0:T(8,128)(2,1)S(1)} %get-tuple-element.94), channel_id=1, source_target_pairs={{0,4},{1,3},{4,8},{5,1},{8,12},{9,5},{12,14},{13,9},{14,10},{15,13... | collective-permute-start | bytes 737288 | tf_op jit(solution)/shard_map/ppermute | solution.py:51
  27.4 6.2 %collective-permute-start.9 = (bf16[960,128]{1,0:T(8,128)(2,1)S(1)}, bf16[960,128]{1,0:T(8,128)(2,1)S(1)}, u32[]{:S(2)}, u32[]{:S(2)}) collective-permute-start(bf16[960,128]{1,0:T(8,128)(2,1)S(1)} %get-tuple-element.93), channel_id=1, source_target_pairs={{0,4},{1,3},{4,8},{5,1},{8,12},{9,5},{12,14},{13,9},{14,10},{15,13... | collective-permute-start | bytes 737288 | tf_op jit(solution)/shard_map/ppermute | solution.py:51
  29.3 4.4 %collective-permute-start.14 = (bf16[1488,128]{1,0:T(8,128)(2,1)S(1)}, bf16[1488,128]{1,0:T(8,128)(2,1)S(1)}, u32[]{:S(2)}, u32[]{:S(2)}) collective-permute-start(bf16[1488,128]{1,0:T(8,128)(2,1)S(1)} %collective-permute-done.4.block_ref.refs_0_.refs_10_), channel_id=1, source_target_pairs={{0,1},{1,0},{2,3},{3,2},{4,5},{5,4},{6,7},{7,6},{8,9},{9,8},{10,11... | collective-permute-start | bytes 1142792 | tf_op jit(solution)/shard_map/ppermute | solution.py:55
  29.3 8.3 %collective-permute-start.8 = (bf16[1056,128]{1,0:T(8,128)(2,1)S(1)}, bf16[1056,128]{1,0:T(8,128)(2,1)S(1)}, u32[]{:S(2)}, u32[]{:S(2)}) collective-permute-start(bf16[1056,128]{1,0:T(8,128)(2,1)S(1)} %get-tuple-element.92), channel_id=1, source_target_pairs={{0,4},{1,3},{4,8},{5,1},{8,12},{9,5},{12,14},{13,9},{14,10},{15,13... | collective-permute-start | bytes 811016 | tf_op jit(solution)/shard_map/ppermute | solution.py:51
  31.7 2.0 %collective-permute-start.15 = (bf16[960,128]{1,0:T(8,128)(2,1)S(1)}, bf16[960,128]{1,0:T(8,128)(2,1)S(1)}, u32[]{:S(2)}, u32[]{:S(2)}) collective-permute-start(bf16[960,128]{1,0:T(8,128)(2,1)S(1)} %collective-permute-done.10.refs_1_), channel_id=1, source_target_pairs={{0,1},{1,0},{2,3},{3,2},{4,5},{5,4},{6,7},{7,6},{8,9},{9,8},{10,11... | collective-permute-start | bytes 737288 | tf_op jit(solution)/shard_map/ppermute | solution.py:55
  33.6 1.5 %copy-start = (s32[1,2]{1,0:T(1,128)S(1)}, s32[1,2]{1,0:T(1,128)}, u32[]{:S(2)}) copy-start(s32[1,2]{1,0:T(1,128)} %counts_ref.1) | copy-start | bytes 28
  33.6 1.5 %collective-permute-start.13 = (bf16[960,128]{1,0:T(8,128)(2,1)S(1)}, bf16[960,128]{1,0:T(8,128)(2,1)S(1)}, u32[]{:S(2)}, u32[]{:S(2)}) collective-permute-start(bf16[960,128]{1,0:T(8,128)(2,1)S(1)} %collective-permute-done.9.refs_0_), channel_id=1, source_target_pairs={{0,1},{1,0},{2,3},{3,2},{4,5},{5,4},{6,7},{7,6},{8,9},{9,8},{10,11... | collective-permute-start | bytes 737288 | tf_op jit(solution)/shard_map/ppermute | solution.py:55
  37.6 1.6 %collective-permute-start.16 = (bf16[1056,128]{1,0:T(8,128)(2,1)S(1)}, bf16[1056,128]{1,0:T(8,128)(2,1)S(1)}, u32[]{:S(2)}, u32[]{:S(2)}) collective-permute-start(bf16[1056,128]{1,0:T(8,128)(2,1)S(1)} %collective-permute-done.8.refs_12_), channel_id=1, source_target_pairs={{0,1},{1,0},{2,3},{3,2},{4,5},{5,4},{6,7},{7,6},{8,9},{9,8},{10,11... | collective-permute-start | bytes 811016 | tf_op jit(solution)/shard_map/ppermute | solution.py:55

commit v10 on v9

--- a/solution.py
+++ b/solution.py
@@ -41,13 +41,14 @@
     return jnp.where(side == 0, row, RING_CHIPS - 1 - row)
 
 
-def hop(value):
+def hop(value, from_other=False):
     half = RING_CHIPS // 2
     place = [2 * q if q < half else 2 * (RING_CHIPS - 1 - q) + 1 for q in range(RING_CHIPS)]
+    turn = int(from_other)
     pairs = []
     for q in range(RING_CHIPS):
-        pairs.append((2 * place[q], 2 * place[(q + 1) % RING_CHIPS]))
-        pairs.append((2 * place[q] + 1, 2 * place[(q - 1) % RING_CHIPS] + 1))
+        pairs.append((2 * place[q] + turn, 2 * place[(q + 1) % RING_CHIPS]))
+        pairs.append((2 * place[q] + 1 - turn, 2 * place[(q - 1) % RING_CHIPS] + 1))
     return lax.ppermute(value, "dp", pairs)
 
 
@@ -111,9 +112,8 @@
 
 
 def local_kernel(*refs):
-    x_hbm, mixed_hbm, adjoint_hbm, values_hbm, target_hbm, top_target_hbm, gain_hbm, source_hbm = refs[:8]
-    x_ref, mixed_ref, adjoint_ref, values_ref, target_ref, top_target_ref, turned_ref, sums_ref = refs[8:16]
-    gain_ref, source_ref, sems = refs[16:]
+    x_hbm, target_hbm, gain_hbm, source_hbm, x_ref, target_ref, turned_ref, sums_ref = refs[:8]
+    gain_ref, source_ref, sems = refs[8:]
     tokens, width = x_ref.shape
     span = width // STEPS
     copies = []
@@ -126,13 +126,6 @@
             (target_hbm.at[part], target_ref.at[part]),
         )
         copies.append(load(pairs, sems.at[j]))
-    pairs = (
-        (adjoint_hbm, adjoint_ref),
-        (mixed_hbm, mixed_ref),
-        (values_hbm, values_ref),
-        (top_target_hbm, top_target_ref),
-    )
-    later = load(pairs, sems.at[STEPS])
     products = jnp.zeros((tokens, 2 * LANES), F32)
     squares = jnp.zeros((tokens, LANES), F32)
     for j in range(STEPS):
@@ -151,7 +144,11 @@
     inverse = jnp.broadcast_to(lax.rsqrt(mean + 1e-05), (tokens, LANES))
     for i, value in enumerate((inverse, inverse * products[:, :LANES], products[:, LANES:])):
         sums_ref[:, i * LANES : (i + 1) * LANES] = value
-    for copy in later:
+
+
+def fetch_kernel(after_ref, *refs):
+    count = (len(refs) - 1) // 2
+    for copy in load(zip(refs[:count], refs[count:-1]), refs[-1]):
         copy.wait()
 
 
@@ -304,11 +301,14 @@
 def last_score_kernel(count, unit_ref, block_ref, best_ref, out_ref, mean_ref):
     best = [[best_ref[e, t] for t in range(TASKS)] for e in range(2)]
     best_of(places_of([block_ref], count), count, unit_ref, best)
+    lane = lax.broadcasted_iota(jnp.int32, (1, LANES), 1)
+    means = []
     for e in range(2):
-        values = [jnp.max(best[e][t]) for t in range(TASKS)]
-        for t in range(TASKS):
-            out_ref[e, t] = values[t]
-        mean_ref[e] = (values[0] + values[1] + values[2]) * (1.0 / TASKS)
+        values = [jnp.max(best[e][t], axis=0, keepdims=True) for t in range(TASKS)]
+        row = jnp.where(lane == 0, values[0], jnp.where(lane == 1, values[1], values[2]))
+        out_ref[pl.ds(e, 1), :] = row[:, :TASKS]
+        means.append((values[0] + values[1] + values[2]) * (1.0 / TASKS))
+    mean_ref[...] = jnp.where(lane == 0, means[0], means[1])[:, :2]
 
 
 VMEM = pl.BlockSpec(memory_space=pltpu.VMEM)
@@ -383,31 +383,36 @@
         name="pack",
     )(me.reshape(1), *in_hbm(inputs))
 
-    inputs = (
-        x,
-        mixed,
-        adjoint,
-        values,
-        bottom_target_sketch,
-        top_target_sketch,
-        top_rmsnorm_weights.reshape(1, width),
-        source_sketch.T,
-    )
-    *activations, local = pl.pallas_call(
+    tie = lax.optimization_barrier
+    inputs = (x, bottom_target_sketch, top_rmsnorm_weights.reshape(1, width), source_sketch.T)
+    upper, low_target, source, local = pl.pallas_call(
         local_kernel,
-        out_shape=[jax.ShapeDtypeStruct(a.shape, a.dtype) for a in inputs[:6]]
+        out_shape=[jax.ShapeDtypeStruct(a.shape, a.dtype) for a in inputs[:2]]
         + [
             jax.ShapeDtypeStruct((width, LANES), BF16),
             jax.ShapeDtypeStruct((tokens, LOCAL_SUMS * LANES), F32),
         ],
         in_specs=[HBM] * len(inputs),
-        out_specs=[VMEM] * 8,
-        scratch_shapes=[pltpu.VMEM(a.shape, a.dtype) for a in inputs[6:]]
-        + [pltpu.SemaphoreType.DMA((STEPS + 1, 4))],
-        compiler_params=params(24),
-        cost_estimate=cost(tokens * width * LANES * 6, 14 * MIB),
+        out_specs=[VMEM] * 4,
+        scratch_shapes=[pltpu.VMEM(a.shape, a.dtype) for a in inputs[2:]]
+        + [pltpu.SemaphoreType.DMA((STEPS, len(inputs)))],
+        compiler_params=params(16),
+        cost_estimate=cost(tokens * width * LANES * 4, 6 * MIB),
         name="local_products",
     )(*in_hbm(inputs))
+    own_late, local = tie((own, local))
+    inputs = (mixed, adjoint, values, top_target_sketch)
+    fetched = pl.pallas_call(
+        fetch_kernel,
+        out_shape=[jax.ShapeDtypeStruct(a.shape, a.dtype) for a in inputs],
+        in_specs=[VMEM] + [HBM] * len(inputs),
+        out_specs=[VMEM] * len(inputs),
+        scratch_shapes=[pltpu.SemaphoreType.DMA((len(inputs),))],
+        compiler_params=params(16),
+        cost_estimate=cost(1, 8 * MIB),
+        name="fetch",
+    )(local, *in_hbm(inputs))
+    activations = [upper, *fetched[:3], low_target, fetched[3], source]
 
     stage_scratch = [
         pltpu.VMEM((2 * rows, 2 * LANES), BF16),
@@ -445,11 +450,10 @@
             name="split",
         )(block, *tails)
 
-    tie = lax.optimization_barrier
     half = RING_CHIPS // 2
-    held = [own, other_core(own)]
+    held = [own, other_core(own_late)]
     blocks = list(held)
-    first, second = hop(held[0]), hop(held[1])
+    first, second = hop(own), hop(own_late, from_other=True)
     first, activations = tie((first, activations))
     sums = stage(0, held, [])
     second, sums = tie((second, sums))
@@ -507,13 +511,13 @@
     )(unit, *blocks)
     task_best, scores = pl.pallas_call(
         functools.partial(last_score_kernel, count),
-        out_shape=(jax.ShapeDtypeStruct((2, TASKS), F32), jax.ShapeDtypeStruct((2,), F32)),
+        out_shape=(jax.ShapeDtypeStruct((2, TASKS), F32), jax.ShapeDtypeStruct((1, 2), F32)),
         in_specs=[VMEM] * 3,
-        out_specs=(SMEM, SMEM),
+        out_specs=(VMEM, VMEM),
         compiler_params=params(8),
         name="last_scores",
     )(unit, other_core(tails), best)
-    return (scores, task_best)
+    return (scores.reshape(2), task_best)
 
 
 def shards_of_any_slice(

time: 40.4 us -> 41.8 us (1.035)
  Pallas kernels: 15.9 us -> 18.1 us
  starting transfers between devices: 16 us -> 14.8 us
    pallas_call x0 -> x1, Pallas kernels: none -> 3.14 us  [shards(): pl.pallas_call(fetch_kernel, out_shape=[jax.ShapeDtypeStruct(a.shape, a.d...]
    ppermute x8, starting transfers between devices: 15.2 us -> 13.1 us  [hop(): return lax.ppermute(value, 'dp', pairs)]
    ppermute x9, starting transfers between devices: 0.8 us -> 1.7 us  [other_core(): lax.ppermute(value, 'dp', [(d, d ^ 1) for d in range(2 * RING_CHIPS)])]
    pallas_call x1, Pallas kernels: 4.6 us -> 3.8 us  [shards(): pl.pallas_call(local_kernel, out_shape=[jax.ShapeDtypeStruct(a.shape, a.d...]
  transfers between devices with their start and end apart: 17 -> 17, of which waited for: 7 -> 7; matrix products, arithmetic and copies ran while one was open for 0% -> 0% of each run, Pallas kernels for 34% -> 38%
where the time goes in v10:
time: 41.8 us; the launch traced here: 41.5 us
  Pallas kernels  18.1 us (43%)
  starting transfers between devices  14.8 us (35%)
  waiting for transfers between devices  7.78 us (19%)
  between operations  0.79 us (2%)
    ppermute x8, starting transfers between devices, hop(): return lax.ppermute(value, 'dp', pairs)  13.1 us
    ppermute x8, waiting for transfers between devices, hop(): return lax.ppermute(value, 'dp', pairs)  6.54 us
    pallas_call x7, Pallas kernels, stage(): pl.pallas_call(functools.partial(stage_kernel, away, first), out_shape=[j...  5.58 us
    pallas_call x1, Pallas kernels, shards(): pl.pallas_call(local_kernel, out_shape=[jax.ShapeDtypeStruct(a.shape, a.d...  3.8 us
    pallas_call x1, Pallas kernels, shards(): pl.pallas_call(fetch_kernel, out_shape=[jax.ShapeDtypeStruct(a.shape, a.d...  3.14 us
    pallas_call x1, Pallas kernels, shards(): pl.pallas_call(functools.partial(feature_kernel, half), out_shape=jax.Sha...  2.48 us
    ppermute x9, starting transfers between devices, other_core(): lax.ppermute(value, 'dp', [(d, d ^ 1) for d in range(2 * RING_CHIPS)])  1.7 us
    pallas_call x1, Pallas kernels, shards(): pl.pallas_call(pack_kernel, out_shape=jax.ShapeDtypeStruct((3 * rows + (L...  1.41 us
  transfers between devices with their start and end apart: 17, of which 7 were waited for; matrix products, arithmetic and copies ran while one was open for 0% of the time, Pallas kernels for 38%

profile of v10, /device:TPU:0, one launch (start us, length us, event | category | flops | bytes accessed | tf_op | source)
XLA Modules:
  0.0 41.5 jit_solution(8565844547225478643)
XLA Ops:
  0.6 1.4 %pack.1.refs_0_ = bf16[1488,128]{1,0:T(8,128)(2,1)S(1)} custom-call(s32[1]{0:T(128)} %bitcast.me_ref, f32[40,128]{1,0:T(8,128)} %bitcast.12, bf16[320,128]{1,0:T(8,128)(2,1)} %refs_1_.3, bf16[320,128]{1,0:T(8,128)(2,1)} %bitcast.11, bf16[128,128]{1,0:T(8,128)(2,1)} %refs_3_.2, bf16[160,128]{1,0:T(8,128)(2,1)} %bitcast.14, bf16[320,128]{1,0:T(8,128)(2,1)} %refs_5_.1, ...), custom_call_target="tpu_custom_call" | custom-call | tf_op jit(solution)/shard_map/pack/pallas_call | solution.py:375
  2.1 3.1 %collective-permute-start = (bf16[1488,128]{1,0:T(8,128)(2,1)S(1)}, bf16[1488,128]{1,0:T(8,128)(2,1)S(1)}, u32[]{:S(2)}, u32[]{:S(2)}) collective-permute-start(bf16[1488,128]{1,0:T(8,128)(2,1)S(1)} %pack.1.refs_0_), channel_id=1, source_target_pairs={{0,4},{1,3},{4,8},{5,1},{8,12},{9,5},{12,14},{13,9},{14,10},{15,13... | collective-permute-start | bytes 1142792 | tf_op jit(solution)/shard_map/ppermute | solution.py:52
  5.1 3.8 %local_products.1 = (bf16[256,5120]{1,0:T(8,128)(2,1)S(1)}, bf16[5120,128]{1,0:T(8,128)(2,1)S(1)}, bf16[5120,128]{1,0:T(8,128)(2,1)S(1)}, f32[256,384]{1,0:T(8,128)S(1)}) custom-call(bf16[256,5120]{1,0:T(8,128)(2,1)} %refs_0_.2, bf16[5120,128]{1,0:T(8,128)(2,1)} %refs_1_.4, f32[1,5120]{1,0:T(1,128)} %bitcast.13, bf16[64,5120]{1,0:T(8,128)(2,1)} %bitcast.10), custom_call_target="tpu_custom_call" | custom-call | flops 671088640 | bytes 6291456 | tf_op jit(solution)/shard_map/local_products/pallas_call | solution.py:388
  9.0 0.7 %collective-permute-start.2 = (bf16[1488,128]{1,0:T(8,128)(2,1)S(1)}, bf16[1488,128]{1,0:T(8,128)(2,1)S(1)}, u32[]{:S(2)}, u32[]{:S(2)}) collective-permute-start(bf16[1488,128]{1,0:T(8,128)(2,1)S(1)} %pack.1.refs_0_), channel_id=1, source_target_pairs={{1,4},{0,3},{5,8},{4,1},{9,12},{8,5},{13,14},{12,9},{15,10},{14,13... | collective-permute-start | bytes 1142792 | tf_op jit(solution)/shard_map/ppermute | solution.py:52
  9.8 3.1 %fetch.1 = (bf16[256,5120]{1,0:T(8,128)(2,1)S(1)}, bf16[256,5120]{1,0:T(8,128)(2,1)S(1)}, bf16[256,2560]{1,0:T(8,128)(2,1)S(1)}, bf16[2560,128]{1,0:T(8,128)(2,1)S(1)}) custom-call(f32[256,384]{1,0:T(8,128)S(1)} %get-tuple-element.62.after_ref.refs_11_, bf16[256,5120]{1,0:T(8,128)(2,1)} %refs_0_.3, bf16[256,5120]{1,0:T(8,128)(2,1)} %refs_1_.5, ...), custom_call_target="tpu_custom_call" | custom-call | flops 1 | bytes 8388608 | tf_op jit(solution)/shard_map/fetch/pallas_call | solution.py:405
  12.9 1.4 %collective-permute-start.1 = (bf16[1488,128]{1,0:T(8,128)(2,1)S(1)}, bf16[1488,128]{1,0:T(8,128)(2,1)S(1)}, u32[]{:S(2)}, u32[]{:S(2)}) collective-permute-start(bf16[1488,128]{1,0:T(8,128)(2,1)S(1)} %collective-permute-done.refs_0_.refs_2_), channel_id=1, source_target_pairs={{0,4},{1,3},{4,8},{5,1},{8,12},{9,5},{12,14},{13,9},{14,10},{15,13... | collective-permute-start | bytes 1142792 | tf_op jit(solution)/shard_map/ppermute | solution.py:52
  14.4 0.7 %stage.7 = (f32[256,1024]{1,0:T(8,128)S(1)}, f32[128,256]{1,0:T(8,128)S(1)}) custom-call(s32[1]{0:T(128)} %bitcast.me_ref, bf16[1488,128]{1,0:T(8,128)(2,1)S(1)} %pack.1.refs_0_, bf16[1488,128]{1,0:T(8,128)(2,1)S(1)} %collective-permute-done.3.refs_1_, bf16[256,5120]{1,0:T(8,128)(2,1)S(1)} %get-tuple-element.71.refs_2_, ...), custom_call_target="tpu_custom_call" | custom-call | flops 167772160 | bytes 2097152 | tf_op jit(solution)/shard_map/stage/pallas_call | solution.py:426
  15.1 1.1 %collective-permute-done.2.refs_1_.refs_4_ = bf16[1488,128]{1,0:T(8,128)(2,1)S(1)} collective-permute-done((bf16[1488,128]{1,0:T(8,128)(2,1)S(1)}, bf16[1488,128]{1,0:T(8,128)(2,1)S(1)}, u32[]{:S(2)}, u32[]{:S(2)}) %collective-permute-start.2) | collective-permute-done | bytes 380960 | tf_op jit(solution)/shard_map/ppermute | solution.py:52
  16.1 0.8 %collective-permute-start.7 = (bf16[1488,128]{1,0:T(8,128)(2,1)S(1)}, bf16[1488,128]{1,0:T(8,128)(2,1)S(1)}, u32[]{:S(2)}, u32[]{:S(2)}) collective-permute-start(bf16[1488,128]{1,0:T(8,128)(2,1)S(1)} %collective-permute-done.2.refs_1_.refs_4_), channel_id=1, source_target_pairs={{0,1},{1,0},{2,3},{3,2},{4,5},{5,4},{6,7},{7,6},{8,9},{9,8},{10,11... | collective-permute-start | bytes 1142792 | tf_op jit(solution)/shard_map/ppermute | solution.py:56
  17.0 1.6 %collective-permute-start.5 = (bf16[1488,128]{1,0:T(8,128)(2,1)S(1)}, bf16[1488,128]{1,0:T(8,128)(2,1)S(1)}, u32[]{:S(2)}, u32[]{:S(2)}) collective-permute-start(bf16[1488,128]{1,0:T(8,128)(2,1)S(1)} %collective-permute-done.2.refs_1_.refs_4_), channel_id=1, source_target_pairs={{0,4},{1,3},{4,8},{5,1},{8,12},{9,5},{12,14},{13,9},{14,10},{15,13... | collective-permute-start | bytes 1142792 | tf_op jit(solution)/shard_map/ppermute | solution.py:52
  18.6 0.8 %stage.8 = (f32[256,1024]{1,0:T(8,128)S(1)}, f32[128,256]{1,0:T(8,128)S(1)}) custom-call(s32[1]{0:T(128)} %bitcast.me_ref, bf16[1488,128]{1,0:T(8,128)(2,1)S(1)} %collective-permute-done.refs_0_.refs_2_, bf16[1488,128]{1,0:T(8,128)(2,1)S(1)} %collective-permute-done.2.refs_1_.refs_4_, ...), custom_call_target="tpu_custom_call", output_to_operand_aliasing={{0}: (10, {}), {1}: (11, {})} | custom-call | flops 167772160 | bytes 2097152 | tf_op jit(solution)/shard_map/stage/pallas_call | solution.py:426
  19.4 1.2 %collective-permute-done.1.refs_0_.refs_6_ = bf16[1488,128]{1,0:T(8,128)(2,1)S(1)} collective-permute-done((bf16[1488,128]{1,0:T(8,128)(2,1)S(1)}, bf16[1488,128]{1,0:T(8,128)(2,1)S(1)}, u32[]{:S(2)}, u32[]{:S(2)}) %collective-permute-start.1) | collective-permute-done | bytes 380960 | tf_op jit(solution)/shard_map/ppermute | solution.py:52
  20.6 1.4 %collective-permute-start.4 = (bf16[1488,128]{1,0:T(8,128)(2,1)S(1)}, bf16[1488,128]{1,0:T(8,128)(2,1)S(1)}, u32[]{:S(2)}, u32[]{:S(2)}) collective-permute-start(bf16[1488,128]{1,0:T(8,128)(2,1)S(1)} %collective-permute-done.1.refs_0_.refs_6_), channel_id=1, source_target_pairs={{0,4},{1,3},{4,8},{5,1},{8,12},{9,5},{12,14},{13,9},{14,10},{15,13... | collective-permute-start | bytes 1142792 | tf_op jit(solution)/shard_map/ppermute | solution.py:52
  22.0 0.8 %stage.9 = (f32[256,1024]{1,0:T(8,128)S(1)}, f32[128,256]{1,0:T(8,128)S(1)}) custom-call(s32[1]{0:T(128)} %bitcast.me_ref, bf16[1488,128]{1,0:T(8,128)(2,1)S(1)} %collective-permute-done.6.refs_0_.refs_3_, bf16[1488,128]{1,0:T(8,128)(2,1)S(1)} %collective-permute-done.7.refs_1_.refs_5_, ...), custom_call_target="tpu_custom_call", output_to_operand_aliasing={{0}: (10, {}), {1}: (11, {})} | custom-call | flops 167772160 | bytes 2097152 | tf_op jit(solution)/shard_map/stage/pallas_call | solution.py:426
  22.8 1.9 %collective-permute-done.5.refs_1_.block_ref.refs_8_ = bf16[1488,128]{1,0:T(8,128)(2,1)S(1)} collective-permute-done((bf16[1488,128]{1,0:T(8,128)(2,1)S(1)}, bf16[1488,128]{1,0:T(8,128)(2,1)S(1)}, u32[]{:S(2)}, u32[]{:S(2)}) %collective-permute-start.5) | collective-permute-done | bytes 380960 | tf_op jit(solution)/shard_map/ppermute | solution.py:52
  24.7 0.3 collective-permute-start.12
  25.0 0.2 collective-permute-start.11
  25.2 1.6 %collective-permute-start.10 = (bf16[960,128]{1,0:T(8,128)(2,1)S(1)}, bf16[960,128]{1,0:T(8,128)(2,1)S(1)}, u32[]{:S(2)}, u32[]{:S(2)}) collective-permute-start(bf16[960,128]{1,0:T(8,128)(2,1)S(1)} %get-tuple-element.99), channel_id=1, source_target_pairs={{0,4},{1,3},{4,8},{5,1},{8,12},{9,5},{12,14},{13,9},{14,10},{15,13... | collective-permute-start | bytes 737288 | tf_op jit(solution)/shard_map/ppermute | solution.py:52
  26.8 0.8 %stage.10 = (f32[256,1024]{1,0:T(8,128)S(1)}, f32[128,256]{1,0:T(8,128)S(1)}) custom-call(s32[1]{0:T(128)} %bitcast.me_ref, bf16[1488,128]{1,0:T(8,128)(2,1)S(1)} %collective-permute-done.1.refs_0_.refs_6_, bf16[1488,128]{1,0:T(8,128)(2,1)S(1)} %collective-permute-done.5.refs_1_.block_ref.refs_8_, ...), custom_call_target="tpu_custom_call", output_to_operand_aliasing={{0}: (10, {}), {1}: (11, {})} | custom-call | flops 167772160 | bytes 2097152 | tf_op jit(solution)/shard_map/stage/pallas_call | solution.py:426
  27.6 1.1 %collective-permute-done.4.block_ref.refs_0_.refs_10_ = bf16[1488,128]{1,0:T(8,128)(2,1)S(1)} collective-permute-done((bf16[1488,128]{1,0:T(8,128)(2,1)S(1)}, bf16[1488,128]{1,0:T(8,128)(2,1)S(1)}, u32[]{:S(2)}, u32[]{:S(2)}) %collective-permute-start.4) | collective-permute-done | bytes 380960 | tf_op jit(solution)/shard_map/ppermute | solution.py:52
  28.8 1.6 %collective-permute-start.9 = (bf16[960,128]{1,0:T(8,128)(2,1)S(1)}, bf16[960,128]{1,0:T(8,128)(2,1)S(1)}, u32[]{:S(2)}, u32[]{:S(2)}) collective-permute-start(bf16[960,128]{1,0:T(8,128)(2,1)S(1)} %get-tuple-element.98), channel_id=1, source_target_pairs={{0,4},{1,3},{4,8},{5,1},{8,12},{9,5},{12,14},{13,9},{14,10},{15,13... | collective-permute-start | bytes 737288 | tf_op jit(solution)/shard_map/ppermute | solution.py:52
  30.4 1.7 %collective-permute-start.8 = (bf16[1056,128]{1,0:T(8,128)(2,1)S(1)}, bf16[1056,128]{1,0:T(8,128)(2,1)S(1)}, u32[]{:S(2)}, u32[]{:S(2)}) collective-permute-start(bf16[1056,128]{1,0:T(8,128)(2,1)S(1)} %get-tuple-element.97), channel_id=1, source_target_pairs={{0,4},{1,3},{4,8},{5,1},{8,12},{9,5},{12,14},{13,9},{14,10},{15,13... | collective-permute-start | bytes 811016 | tf_op jit(solution)/shard_map/ppermute | solution.py:52
  32.1 0.8 %stage.11 = (f32[256,1024]{1,0:T(8,128)S(1)}, f32[128,256]{1,0:T(8,128)S(1)}) custom-call(s32[1]{0:T(128)} %bitcast.me_ref, bf16[1488,128]{1,0:T(8,128)(2,1)S(1)} %collective-permute-done.11.refs_0_.refs_7_, bf16[1488,128]{1,0:T(8,128)(2,1)S(1)} %collective-permute-done.12.refs_1_.refs_9_, ...), custom_call_target="tpu_custom_call", output_to_operand_aliasing={{0}: (10, {}), {1}: (11, {})} | custom-call | flops 167772160 | bytes 2097152 | tf_op jit(solution)/shard_map/stage/pallas_call | solution.py:426
  33.0 0.8 %stage.12 = (f32[256,1024]{1,0:T(8,128)S(1)}, f32[128,256]{1,0:T(8,128)S(1)}) custom-call(s32[1]{0:T(128)} %bitcast.me_ref, bf16[1488,128]{1,0:T(8,128)(2,1)S(1)} %collective-permute-done.4.block_ref.refs_0_.refs_10_, bf16[960,128]{1,0:T(8,128)(2,1)S(1)} %collective-permute-done.10.refs_1_, ...), custom_call_target="tpu_custom_call", output_to_operand_aliasing={{0}: (10, {}), {1}: (11, {})} | custom-call | flops 167772160 | bytes 2097152 | tf_op jit(solution)/shard_map/stage/pallas_call | solution.py:426
  33.9 1.2 %collective-permute-done.9.refs_0_ = bf16[960,128]{1,0:T(8,128)(2,1)S(1)} collective-permute-done((bf16[960,128]{1,0:T(8,128)(2,1)S(1)}, bf16[960,128]{1,0:T(8,128)(2,1)S(1)}, u32[]{:S(2)}, u32[]{:S(2)}) %collective-permute-start.9) | collective-permute-done | bytes 245792 | tf_op jit(solution)/shard_map/ppermute | solution.py:52
  35.1 0.8 %stage.13 = (f32[256,1024]{1,0:T(8,128)S(1)}, f32[128,256]{1,0:T(8,128)S(1)}) custom-call(s32[1]{0:T(128)} %bitcast.me_ref, bf16[1488,128]{1,0:T(8,128)(2,1)S(1)} %collective-permute-done.14.refs_0_.refs_11_, bf16[960,128]{1,0:T(8,128)(2,1)S(1)} %collective-permute-done.15.refs_1_, ...), custom_call_target="tpu_custom_call", output_to_operand_aliasing={{0}: (10, {}), {1}: (11, {})} | custom-call | flops 167772160 | bytes 2097152 | tf_op jit(solution)/shard_map/stage/pallas_call | solution.py:426
  35.9 0.7 %collective-permute-done.13.refs_1_ = bf16[960,128]{1,0:T(8,128)(2,1)S(1)} collective-permute-done((bf16[960,128]{1,0:T(8,128)(2,1)S(1)}, bf16[960,128]{1,0:T(8,128)(2,1)S(1)}, u32[]{:S(2)}, u32[]{:S(2)}) %collective-permute-start.13) | collective-permute-done | bytes 245792 | tf_op jit(solution)/shard_map/ppermute | solution.py:56
  36.6 2.5 %features.1.unit_ref = f32[128,128]{1,0:T(8,128)S(1)} custom-call(s32[1]{0:T(128)} %bitcast.me_ref, s32[1,2]{1,0:T(1,128)S(1)} %copy-done, bf16[960,128]{1,0:T(8,128)(2,1)S(1)} %collective-permute-done.9.refs_0_, bf16[960,128]{1,0:T(8,128)(2,1)S(1)} %collective-permute-done.13.refs_1_, bf16[256,5120]{1,0:T(8,128)(2,1)S(1)} %get-tuple-element.71.refs_2_, ...), custom_call_target="tpu_custom_call" | custom-call | flops 1 | bytes 1 | tf_op jit(solution)/shard_map/features/pallas_call | solution.py:480
  39.1 0.2 collective-permute-start.16
  39.3 0.9 %scores.1.best_ref = f32[2,3,8,128]{3,2,1,0:T(8,128)S(1)} custom-call(f32[128,128]{1,0:T(8,128)S(1)} %features.1.unit_ref, bf16[1488,128]{1,0:T(8,128)(2,1)S(1)} %pack.1.refs_0_, bf16[1488,128]{1,0:T(8,128)(2,1)S(1)} %collective-permute-done.3.refs_1_, bf16[1488,128]{1,0:T(8,128)(2,1)S(1)} %collective-permute-done.refs_0_.refs_2_, ...), custom_call_target="tpu_custom_call" | custom-call | flops 4194304 | bytes 2097152 | tf_op jit(solution)/shard_map/scores/pallas_call | solution.py:503
  40.1 0.6 %collective-permute-done.16.block_ref = bf16[1056,128]{1,0:T(8,128)(2,1)S(1)} collective-permute-done((bf16[1056,128]{1,0:T(8,128)(2,1)S(1)}, bf16[1056,128]{1,0:T(8,128)(2,1)S(1)}, u32[]{:S(2)}, u32[]{:S(2)}) %collective-permute-start.16) | collective-permute-done | bytes 270368 | tf_op jit(solution)/shard_map/ppermute | solution.py:56
  40.7 0.8 %last_scores.1 = (f32[2,3]{1,0:T(2,128)}, f32[1,2]{1,0:T(1,128)}) custom-call(f32[128,128]{1,0:T(8,128)S(1)} %features.1.unit_ref, bf16[1056,128]{1,0:T(8,128)(2,1)S(1)} %collective-permute-done.16.block_ref, f32[2,3,8,128]{3,2,1,0:T(8,128)S(1)} %scores.1.best_ref), custom_call_target="tpu_custom_call" | custom-call | tf_op jit(solution)/shard_map/last_scores/pallas_call | solution.py:512
  (19 shorter events, 0.2 us)
Async XLA Ops:
  2.1 10.9 %collective-permute-start = (bf16[1488,128]{1,0:T(8,128)(2,1)S(1)}, bf16[1488,128]{1,0:T(8,128)(2,1)S(1)}, u32[]{:S(2)}, u32[]{:S(2)}) collective-permute-start(bf16[1488,128]{1,0:T(8,128)(2,1)S(1)} %pack.1.refs_0_), channel_id=1, source_target_pairs={{0,4},{1,3},{4,8},{5,1},{8,12},{9,5},{12,14},{13,9},{14,10},{15,13... | collective-permute-start | bytes 1142792 | tf_op jit(solution)/shard_map/ppermute | solution.py:52
  8.9 5.4 %collective-permute-start.3 = (bf16[1488,128]{1,0:T(8,128)(2,1)S(1)}, bf16[1488,128]{1,0:T(8,128)(2,1)S(1)}, u32[]{:S(2)}, u32[]{:S(2)}) collective-permute-start(bf16[1488,128]{1,0:T(8,128)(2,1)S(1)} %pack.1.refs_0_), channel_id=1, source_target_pairs={{0,1},{1,0},{2,3},{3,2},{4,5},{5,4},{6,7},{7,6},{8,9},{9,8},{10,11... | collective-permute-start | bytes 1142792 | tf_op jit(solution)/shard_map/ppermute | solution.py:56
  9.0 7.1 %collective-permute-start.2 = (bf16[1488,128]{1,0:T(8,128)(2,1)S(1)}, bf16[1488,128]{1,0:T(8,128)(2,1)S(1)}, u32[]{:S(2)}, u32[]{:S(2)}) collective-permute-start(bf16[1488,128]{1,0:T(8,128)(2,1)S(1)} %pack.1.refs_0_), channel_id=1, source_target_pairs={{1,4},{0,3},{5,8},{4,1},{9,12},{8,5},{13,14},{12,9},{15,10},{14,13... | collective-permute-start | bytes 1142792 | tf_op jit(solution)/shard_map/ppermute | solution.py:52
  12.9 7.7 %collective-permute-start.1 = (bf16[1488,128]{1,0:T(8,128)(2,1)S(1)}, bf16[1488,128]{1,0:T(8,128)(2,1)S(1)}, u32[]{:S(2)}, u32[]{:S(2)}) collective-permute-start(bf16[1488,128]{1,0:T(8,128)(2,1)S(1)} %collective-permute-done.refs_0_.refs_2_), channel_id=1, source_target_pairs={{0,4},{1,3},{4,8},{5,1},{8,12},{9,5},{12,14},{13,9},{14,10},{15,13... | collective-permute-start | bytes 1142792 | tf_op jit(solution)/shard_map/ppermute | solution.py:52
  16.1 5.9 %collective-permute-start.7 = (bf16[1488,128]{1,0:T(8,128)(2,1)S(1)}, bf16[1488,128]{1,0:T(8,128)(2,1)S(1)}, u32[]{:S(2)}, u32[]{:S(2)}) collective-permute-start(bf16[1488,128]{1,0:T(8,128)(2,1)S(1)} %collective-permute-done.2.refs_1_.refs_4_), channel_id=1, source_target_pairs={{0,1},{1,0},{2,3},{3,2},{4,5},{5,4},{6,7},{7,6},{8,9},{9,8},{10,11... | collective-permute-start | bytes 1142792 | tf_op jit(solution)/shard_map/ppermute | solution.py:56
  17.0 5.0 %collective-permute-start.6 = (bf16[1488,128]{1,0:T(8,128)(2,1)S(1)}, bf16[1488,128]{1,0:T(8,128)(2,1)S(1)}, u32[]{:S(2)}, u32[]{:S(2)}) collective-permute-start(bf16[1488,128]{1,0:T(8,128)(2,1)S(1)} %collective-permute-done.refs_0_.refs_2_), channel_id=1, source_target_pairs={{0,1},{1,0},{2,3},{3,2},{4,5},{5,4},{6,7},{7,6},{8,9},{9,8},{10,11... | collective-permute-start | bytes 1142792 | tf_op jit(solution)/shard_map/ppermute | solution.py:56
  17.0 7.7 %collective-permute-start.5 = (bf16[1488,128]{1,0:T(8,128)(2,1)S(1)}, bf16[1488,128]{1,0:T(8,128)(2,1)S(1)}, u32[]{:S(2)}, u32[]{:S(2)}) collective-permute-start(bf16[1488,128]{1,0:T(8,128)(2,1)S(1)} %collective-permute-done.2.refs_1_.refs_4_), channel_id=1, source_target_pairs={{0,4},{1,3},{4,8},{5,1},{8,12},{9,5},{12,14},{13,9},{14,10},{15,13... | collective-permute-start | bytes 1142792 | tf_op jit(solution)/shard_map/ppermute | solution.py:52
  20.6 8.2 %collective-permute-start.4 = (bf16[1488,128]{1,0:T(8,128)(2,1)S(1)}, bf16[1488,128]{1,0:T(8,128)(2,1)S(1)}, u32[]{:S(2)}, u32[]{:S(2)}) collective-permute-start(bf16[1488,128]{1,0:T(8,128)(2,1)S(1)} %collective-permute-done.1.refs_0_.refs_6_), channel_id=1, source_target_pairs={{0,4},{1,3},{4,8},{5,1},{8,12},{9,5},{12,14},{13,9},{14,10},{15,13... | collective-permute-start | bytes 1142792 | tf_op jit(solution)/shard_map/ppermute | solution.py:52
  24.7 5.7 %collective-permute-start.12 = (bf16[1488,128]{1,0:T(8,128)(2,1)S(1)}, bf16[1488,128]{1,0:T(8,128)(2,1)S(1)}, u32[]{:S(2)}, u32[]{:S(2)}) collective-permute-start(bf16[1488,128]{1,0:T(8,128)(2,1)S(1)} %collective-permute-done.5.refs_1_.block_ref.refs_8_), channel_id=1, source_target_pairs={{0,1},{1,0},{2,3},{3,2},{4,5},{5,4},{6,7},{7,6},{8,9},{9,8},{10,11... | collective-permute-start | bytes 1142792 | tf_op jit(solution)/shard_map/ppermute | solution.py:56
  25.0 7.1 %collective-permute-start.11 = (bf16[1488,128]{1,0:T(8,128)(2,1)S(1)}, bf16[1488,128]{1,0:T(8,128)(2,1)S(1)}, u32[]{:S(2)}, u32[]{:S(2)}) collective-permute-start(bf16[1488,128]{1,0:T(8,128)(2,1)S(1)} %collective-permute-done.1.refs_0_.refs_6_), channel_id=1, source_target_pairs={{0,1},{1,0},{2,3},{3,2},{4,5},{5,4},{6,7},{7,6},{8,9},{9,8},{10,11... | collective-permute-start | bytes 1142792 | tf_op jit(solution)/shard_map/ppermute | solution.py:56
  25.2 7.7 %collective-permute-start.10 = (bf16[960,128]{1,0:T(8,128)(2,1)S(1)}, bf16[960,128]{1,0:T(8,128)(2,1)S(1)}, u32[]{:S(2)}, u32[]{:S(2)}) collective-permute-start(bf16[960,128]{1,0:T(8,128)(2,1)S(1)} %get-tuple-element.99), channel_id=1, source_target_pairs={{0,4},{1,3},{4,8},{5,1},{8,12},{9,5},{12,14},{13,9},{14,10},{15,13... | collective-permute-start | bytes 737288 | tf_op jit(solution)/shard_map/ppermute | solution.py:52
  28.8 6.2 %collective-permute-start.9 = (bf16[960,128]{1,0:T(8,128)(2,1)S(1)}, bf16[960,128]{1,0:T(8,128)(2,1)S(1)}, u32[]{:S(2)}, u32[]{:S(2)}) collective-permute-start(bf16[960,128]{1,0:T(8,128)(2,1)S(1)} %get-tuple-element.98), channel_id=1, source_target_pairs={{0,4},{1,3},{4,8},{5,1},{8,12},{9,5},{12,14},{13,9},{14,10},{15,13... | collective-permute-start | bytes 737288 | tf_op jit(solution)/shard_map/ppermute | solution.py:52
  30.4 4.7 %collective-permute-start.14 = (bf16[1488,128]{1,0:T(8,128)(2,1)S(1)}, bf16[1488,128]{1,0:T(8,128)(2,1)S(1)}, u32[]{:S(2)}, u32[]{:S(2)}) collective-permute-start(bf16[1488,128]{1,0:T(8,128)(2,1)S(1)} %collective-permute-done.4.block_ref.refs_0_.refs_10_), channel_id=1, source_target_pairs={{0,1},{1,0},{2,3},{3,2},{4,5},{5,4},{6,7},{7,6},{8,9},{9,8},{10,11... | collective-permute-start | bytes 1142792 | tf_op jit(solution)/shard_map/ppermute | solution.py:56
  30.4 8.7 %collective-permute-start.8 = (bf16[1056,128]{1,0:T(8,128)(2,1)S(1)}, bf16[1056,128]{1,0:T(8,128)(2,1)S(1)}, u32[]{:S(2)}, u32[]{:S(2)}) collective-permute-start(bf16[1056,128]{1,0:T(8,128)(2,1)S(1)} %get-tuple-element.97), channel_id=1, source_target_pairs={{0,4},{1,3},{4,8},{5,1},{8,12},{9,5},{12,14},{13,9},{14,10},{15,13... | collective-permute-start | bytes 811016 | tf_op jit(solution)/shard_map/ppermute | solution.py:52
  33.0 2.1 %collective-permute-start.15 = (bf16[960,128]{1,0:T(8,128)(2,1)S(1)}, bf16[960,128]{1,0:T(8,128)(2,1)S(1)}, u32[]{:S(2)}, u32[]{:S(2)}) collective-permute-start(bf16[960,128]{1,0:T(8,128)(2,1)S(1)} %collective-permute-done.10.refs_1_), channel_id=1, source_target_pairs={{0,1},{1,0},{2,3},{3,2},{4,5},{5,4},{6,7},{7,6},{8,9},{9,8},{10,11... | collective-permute-start | bytes 737288 | tf_op jit(solution)/shard_map/ppermute | solution.py:56
  35.1 1.5 %copy-start = (s32[1,2]{1,0:T(1,128)S(1)}, s32[1,2]{1,0:T(1,128)}, u32[]{:S(2)}) copy-start(s32[1,2]{1,0:T(1,128)} %counts_ref.1) | copy-start | bytes 28
  35.1 1.5 %collective-permute-start.13 = (bf16[960,128]{1,0:T(8,128)(2,1)S(1)}, bf16[960,128]{1,0:T(8,128)(2,1)S(1)}, u32[]{:S(2)}, u32[]{:S(2)}) collective-permute-start(bf16[960,128]{1,0:T(8,128)(2,1)S(1)} %collective-permute-done.9.refs_0_), channel_id=1, source_target_pairs={{0,1},{1,0},{2,3},{3,2},{4,5},{5,4},{6,7},{7,6},{8,9},{9,8},{10,11... | collective-permute-start | bytes 737288 | tf_op jit(solution)/shard_map/ppermute | solution.py:56
  39.1 1.6 %collective-permute-start.16 = (bf16[1056,128]{1,0:T(8,128)(2,1)S(1)}, bf16[1056,128]{1,0:T(8,128)(2,1)S(1)}, u32[]{:S(2)}, u32[]{:S(2)}) collective-permute-start(bf16[1056,128]{1,0:T(8,128)(2,1)S(1)} %collective-permute-done.8.refs_12_), channel_id=1, source_target_pairs={{0,1},{1,0},{2,3},{3,2},{4,5},{5,4},{6,7},{7,6},{8,9},{9,8},{10,11... | collective-permute-start | bytes 811016 | tf_op jit(solution)/shard_map/ppermute | solution.py:56

commit v11 on v10

--- a/solution.py
+++ b/solution.py
@@ -111,6 +111,12 @@
         out_ref[pl.ds(at + i * count, 2 * count), :] = pair.astype(BF16)
 
 
+def doubled(value, which):
+    turned = pltpu.roll(value, LANES // 2, 1)
+    lower = half_lanes(value.shape)
+    return jnp.where(lower, turned, value) if which else jnp.where(lower, value, turned)
+
+
 def local_kernel(*refs):
     x_hbm, target_hbm, gain_hbm, source_hbm, x_ref, target_ref, turned_ref, sums_ref = refs[:8]
     gain_ref, source_ref, sems = refs[8:]
@@ -132,23 +138,28 @@
         for copy in copies[j]:
             copy.wait()
         part = slice(j * span, (j + 1) * span)
-        x, source = x_ref[:, part], source_ref[:, part].astype(F32)
-        gained = source * gain_ref[:, part]
-        turned_ref[part, :] = jnp.concatenate([source, source], axis=0).T.astype(BF16)
-        gained = jnp.concatenate([gained, gained], axis=0).T.astype(BF16)
-        products = products + mm(x, jnp.concatenate([gained, target_ref[part, :]], axis=1))
+        x, source = x_ref[:, part], source_ref[:, part]
+        gained = (source.astype(F32) * gain_ref[:, part]).astype(BF16)
+        turned = jnp.concatenate([source, gained], axis=0).T
+        turned_ref[part, :] = turned
+        products = products + mm(x, jnp.concatenate([turned, target_ref[part, :]], axis=1))
         for i in range(span // LANES):
             wide = x[:, i * LANES : (i + 1) * LANES].astype(F32)
             squares = squares + wide * wide
     mean = jnp.sum(squares, axis=1, keepdims=True) * (1.0 / width)
     inverse = jnp.broadcast_to(lax.rsqrt(mean + 1e-05), (tokens, LANES))
-    for i, value in enumerate((inverse, inverse * products[:, :LANES], products[:, LANES:])):
+    left_one = inverse * doubled(products[:, :LANES], 1)
+    for i, value in enumerate((inverse, left_one, products[:, LANES:])):
         sums_ref[:, i * LANES : (i + 1) * LANES] = value
 
 
 def fetch_kernel(after_ref, *refs):
     count = (len(refs) - 1) // 2
-    for copy in load(zip(refs[:count], refs[count:-1]), refs[-1]):
+    pairs = []
+    for src, dst in zip(refs[:count], refs[count:-1]):
+        rows = src.shape[0] // STEPS
+        pairs += [(src.at[pl.ds(j * rows, rows)], dst.at[pl.ds(j * rows, rows)]) for j in range(STEPS)]
+    for copy in load(pairs, refs[-1]):
         copy.wait()
 
 
@@ -234,7 +245,7 @@
     right_three = products[J_LOW] + inverse * (ALPHA * back[:, :LANES] - along * products[X_LOW])
     right_four = products[J_TARGET] + inverse * (ALPHA * back[:, LANES:] - along * local[X_TARGET])
     rights = (right_one, ALPHA * products[V_TARGET], ALPHA * right_three, ALPHA * right_four)
-    lefts = (local[LEFT_ONE], left_two, products[M_SOURCE], products[M_DOWN])
+    lefts = (local[LEFT_ONE], left_two, doubled(products[M_SOURCE], 0), products[M_DOWN])
     place = lax.broadcasted_iota(jnp.int32, (tokens, LANES), 0)
     one, two = counts_ref[0, 0], counts_ref[0, 1]
     lower = half_lanes((tokens, LANES))
@@ -407,7 +418,7 @@
         out_shape=[jax.ShapeDtypeStruct(a.shape, a.dtype) for a in inputs],
         in_specs=[VMEM] + [HBM] * len(inputs),
         out_specs=[VMEM] * len(inputs),
-        scratch_shapes=[pltpu.SemaphoreType.DMA((len(inputs),))],
+        scratch_shapes=[pltpu.SemaphoreType.DMA((STEPS * len(inputs),))],
         compiler_params=params(16),
         cost_estimate=cost(1, 8 * MIB),
         name="fetch",

time: 41.8 us -> 41.8 us (level)
  starting transfers between devices: 14.8 us -> 14.3 us
  waiting for transfers between devices: 7.78 us -> 8.22 us
    ppermute x8, waiting for transfers between devices: 6.54 us -> 6.98 us  [hop(): return lax.ppermute(value, 'dp', pairs)]
where the time goes in v11:
time: 41.8 us; the launch traced here: 41.5 us
  Pallas kernels  18.2 us (44%)
  starting transfers between devices  14.3 us (34%)
  waiting for transfers between devices  8.22 us (20%)
  between operations  0.79 us (2%)
    ppermute x8, starting transfers between devices, hop(): return lax.ppermute(value, 'dp', pairs)  12.7 us
    ppermute x8, waiting for transfers between devices, hop(): return lax.ppermute(value, 'dp', pairs)  6.98 us
    pallas_call x7, Pallas kernels, stage(): pl.pallas_call(functools.partial(stage_kernel, away, first), out_shape=[j...  5.59 us
    pallas_call x1, Pallas kernels, shards(): pl.pallas_call(local_kernel, out_shape=[jax.ShapeDtypeStruct(a.shape, a.d...  3.73 us
    pallas_call x1, Pallas kernels, shards(): pl.pallas_call(fetch_kernel, out_shape=[jax.ShapeDtypeStruct(a.shape, a.d...  3.25 us
    pallas_call x1, Pallas kernels, shards(): pl.pallas_call(functools.partial(feature_kernel, half), out_shape=jax.Sha...  2.48 us
    ppermute x9, starting transfers between devices, other_core(): lax.ppermute(value, 'dp', [(d, d ^ 1) for d in range(2 * RING_CHIPS)])  1.6 us
    pallas_call x1, Pallas kernels, shards(): pl.pallas_call(pack_kernel, out_shape=jax.ShapeDtypeStruct((3 * rows + (L...  1.41 us
  transfers between devices with their start and end apart: 17, of which 7 were waited for; matrix products, arithmetic and copies ran while one was open for 0% of the time, Pallas kernels for 38%

profile of v11, /device:TPU:0, one launch (start us, length us, event | category | flops | bytes accessed | tf_op | source)
XLA Modules:
  0.0 41.5 jit_solution(5432399966267663012)
XLA Ops:
  0.6 1.4 %pack.1.refs_0_ = bf16[1488,128]{1,0:T(8,128)(2,1)S(1)} custom-call(s32[1]{0:T(128)} %bitcast.me_ref, f32[40,128]{1,0:T(8,128)} %bitcast.12, bf16[320,128]{1,0:T(8,128)(2,1)} %refs_1_.3, bf16[320,128]{1,0:T(8,128)(2,1)} %bitcast.11, bf16[128,128]{1,0:T(8,128)(2,1)} %refs_3_.2, bf16[160,128]{1,0:T(8,128)(2,1)} %bitcast.14, bf16[320,128]{1,0:T(8,128)(2,1)} %refs_5_.1, ...), custom_call_target="tpu_custom_call" | custom-call | tf_op jit(solution)/shard_map/pack/pallas_call | solution.py:386
  2.1 3.1 %collective-permute-start = (bf16[1488,128]{1,0:T(8,128)(2,1)S(1)}, bf16[1488,128]{1,0:T(8,128)(2,1)S(1)}, u32[]{:S(2)}, u32[]{:S(2)}) collective-permute-start(bf16[1488,128]{1,0:T(8,128)(2,1)S(1)} %pack.1.refs_0_), channel_id=1, source_target_pairs={{0,4},{1,3},{4,8},{5,1},{8,12},{9,5},{12,14},{13,9},{14,10},{15,13... | collective-permute-start | bytes 1142792 | tf_op jit(solution)/shard_map/ppermute | solution.py:52
  5.1 3.7 %local_products.1 = (bf16[256,5120]{1,0:T(8,128)(2,1)S(1)}, bf16[5120,128]{1,0:T(8,128)(2,1)S(1)}, bf16[5120,128]{1,0:T(8,128)(2,1)S(1)}, f32[256,384]{1,0:T(8,128)S(1)}) custom-call(bf16[256,5120]{1,0:T(8,128)(2,1)} %refs_0_.2, bf16[5120,128]{1,0:T(8,128)(2,1)} %refs_1_.4, f32[1,5120]{1,0:T(1,128)} %bitcast.13, bf16[64,5120]{1,0:T(8,128)(2,1)} %bitcast.10), custom_call_target="tpu_custom_call" | custom-call | flops 671088640 | bytes 6291456 | tf_op jit(solution)/shard_map/local_products/pallas_call | solution.py:399
  8.9 0.7 %collective-permute-start.2 = (bf16[1488,128]{1,0:T(8,128)(2,1)S(1)}, bf16[1488,128]{1,0:T(8,128)(2,1)S(1)}, u32[]{:S(2)}, u32[]{:S(2)}) collective-permute-start(bf16[1488,128]{1,0:T(8,128)(2,1)S(1)} %pack.1.refs_0_), channel_id=1, source_target_pairs={{1,4},{0,3},{5,8},{4,1},{9,12},{8,5},{13,14},{12,9},{15,10},{14,13... | collective-permute-start | bytes 1142792 | tf_op jit(solution)/shard_map/ppermute | solution.py:52
  9.7 3.2 %fetch.1 = (bf16[256,5120]{1,0:T(8,128)(2,1)S(1)}, bf16[256,5120]{1,0:T(8,128)(2,1)S(1)}, bf16[256,2560]{1,0:T(8,128)(2,1)S(1)}, bf16[2560,128]{1,0:T(8,128)(2,1)S(1)}) custom-call(f32[256,384]{1,0:T(8,128)S(1)} %get-tuple-element.62.after_ref.refs_11_, bf16[256,5120]{1,0:T(8,128)(2,1)} %refs_0_.3, bf16[256,5120]{1,0:T(8,128)(2,1)} %refs_1_.5, ...), custom_call_target="tpu_custom_call" | custom-call | flops 1 | bytes 8388608 | tf_op jit(solution)/shard_map/fetch/pallas_call | solution.py:416
  13.0 1.4 %collective-permute-start.1 = (bf16[1488,128]{1,0:T(8,128)(2,1)S(1)}, bf16[1488,128]{1,0:T(8,128)(2,1)S(1)}, u32[]{:S(2)}, u32[]{:S(2)}) collective-permute-start(bf16[1488,128]{1,0:T(8,128)(2,1)S(1)} %collective-permute-done.refs_0_.refs_2_), channel_id=1, source_target_pairs={{0,4},{1,3},{4,8},{5,1},{8,12},{9,5},{12,14},{13,9},{14,10},{15,13... | collective-permute-start | bytes 1142792 | tf_op jit(solution)/shard_map/ppermute | solution.py:52
  14.4 0.7 %stage.7 = (f32[256,1024]{1,0:T(8,128)S(1)}, f32[128,256]{1,0:T(8,128)S(1)}) custom-call(s32[1]{0:T(128)} %bitcast.me_ref, bf16[1488,128]{1,0:T(8,128)(2,1)S(1)} %pack.1.refs_0_, bf16[1488,128]{1,0:T(8,128)(2,1)S(1)} %collective-permute-done.3.refs_1_, bf16[256,5120]{1,0:T(8,128)(2,1)S(1)} %get-tuple-element.71.refs_2_, ...), custom_call_target="tpu_custom_call" | custom-call | flops 167772160 | bytes 2097152 | tf_op jit(solution)/shard_map/stage/pallas_call | solution.py:437
  15.1 1.0 %collective-permute-done.2.refs_1_.refs_4_ = bf16[1488,128]{1,0:T(8,128)(2,1)S(1)} collective-permute-done((bf16[1488,128]{1,0:T(8,128)(2,1)S(1)}, bf16[1488,128]{1,0:T(8,128)(2,1)S(1)}, u32[]{:S(2)}, u32[]{:S(2)}) %collective-permute-start.2) | collective-permute-done | bytes 380960 | tf_op jit(solution)/shard_map/ppermute | solution.py:52
  16.1 0.7 %collective-permute-start.7 = (bf16[1488,128]{1,0:T(8,128)(2,1)S(1)}, bf16[1488,128]{1,0:T(8,128)(2,1)S(1)}, u32[]{:S(2)}, u32[]{:S(2)}) collective-permute-start(bf16[1488,128]{1,0:T(8,128)(2,1)S(1)} %collective-permute-done.2.refs_1_.refs_4_), channel_id=1, source_target_pairs={{0,1},{1,0},{2,3},{3,2},{4,5},{5,4},{6,7},{7,6},{8,9},{9,8},{10,11... | collective-permute-start | bytes 1142792 | tf_op jit(solution)/shard_map/ppermute | solution.py:56
  16.8 1.6 %collective-permute-start.5 = (bf16[1488,128]{1,0:T(8,128)(2,1)S(1)}, bf16[1488,128]{1,0:T(8,128)(2,1)S(1)}, u32[]{:S(2)}, u32[]{:S(2)}) collective-permute-start(bf16[1488,128]{1,0:T(8,128)(2,1)S(1)} %collective-permute-done.2.refs_1_.refs_4_), channel_id=1, source_target_pairs={{0,4},{1,3},{4,8},{5,1},{8,12},{9,5},{12,14},{13,9},{14,10},{15,13... | collective-permute-start | bytes 1142792 | tf_op jit(solution)/shard_map/ppermute | solution.py:52
  18.4 0.8 %stage.8 = (f32[256,1024]{1,0:T(8,128)S(1)}, f32[128,256]{1,0:T(8,128)S(1)}) custom-call(s32[1]{0:T(128)} %bitcast.me_ref, bf16[1488,128]{1,0:T(8,128)(2,1)S(1)} %collective-permute-done.refs_0_.refs_2_, bf16[1488,128]{1,0:T(8,128)(2,1)S(1)} %collective-permute-done.2.refs_1_.refs_4_, ...), custom_call_target="tpu_custom_call", output_to_operand_aliasing={{0}: (10, {}), {1}: (11, {})} | custom-call | flops 167772160 | bytes 2097152 | tf_op jit(solution)/shard_map/stage/pallas_call | solution.py:437
  19.2 1.4 %collective-permute-done.1.refs_0_.refs_6_ = bf16[1488,128]{1,0:T(8,128)(2,1)S(1)} collective-permute-done((bf16[1488,128]{1,0:T(8,128)(2,1)S(1)}, bf16[1488,128]{1,0:T(8,128)(2,1)S(1)}, u32[]{:S(2)}, u32[]{:S(2)}) %collective-permute-start.1) | collective-permute-done | bytes 380960 | tf_op jit(solution)/shard_map/ppermute | solution.py:52
  20.7 1.4 %collective-permute-start.4 = (bf16[1488,128]{1,0:T(8,128)(2,1)S(1)}, bf16[1488,128]{1,0:T(8,128)(2,1)S(1)}, u32[]{:S(2)}, u32[]{:S(2)}) collective-permute-start(bf16[1488,128]{1,0:T(8,128)(2,1)S(1)} %collective-permute-done.1.refs_0_.refs_6_), channel_id=1, source_target_pairs={{0,4},{1,3},{4,8},{5,1},{8,12},{9,5},{12,14},{13,9},{14,10},{15,13... | collective-permute-start | bytes 1142792 | tf_op jit(solution)/shard_map/ppermute | solution.py:52
  22.0 0.8 %stage.9 = (f32[256,1024]{1,0:T(8,128)S(1)}, f32[128,256]{1,0:T(8,128)S(1)}) custom-call(s32[1]{0:T(128)} %bitcast.me_ref, bf16[1488,128]{1,0:T(8,128)(2,1)S(1)} %collective-permute-done.6.refs_0_.refs_3_, bf16[1488,128]{1,0:T(8,128)(2,1)S(1)} %collective-permute-done.7.refs_1_.refs_5_, ...), custom_call_target="tpu_custom_call", output_to_operand_aliasing={{0}: (10, {}), {1}: (11, {})} | custom-call | flops 167772160 | bytes 2097152 | tf_op jit(solution)/shard_map/stage/pallas_call | solution.py:437
  22.9 1.9 %collective-permute-done.5.refs_1_.block_ref.refs_8_ = bf16[1488,128]{1,0:T(8,128)(2,1)S(1)} collective-permute-done((bf16[1488,128]{1,0:T(8,128)(2,1)S(1)}, bf16[1488,128]{1,0:T(8,128)(2,1)S(1)}, u32[]{:S(2)}, u32[]{:S(2)}) %collective-permute-start.5) | collective-permute-done | bytes 380960 | tf_op jit(solution)/shard_map/ppermute | solution.py:52
  24.7 0.2 collective-permute-start.12
  25.0 0.3 collective-permute-start.11
  25.3 1.4 %collective-permute-start.10 = (bf16[960,128]{1,0:T(8,128)(2,1)S(1)}, bf16[960,128]{1,0:T(8,128)(2,1)S(1)}, u32[]{:S(2)}, u32[]{:S(2)}) collective-permute-start(bf16[960,128]{1,0:T(8,128)(2,1)S(1)} %get-tuple-element.99), channel_id=1, source_target_pairs={{0,4},{1,3},{4,8},{5,1},{8,12},{9,5},{12,14},{13,9},{14,10},{15,13... | collective-permute-start | bytes 737288 | tf_op jit(solution)/shard_map/ppermute | solution.py:52
  26.7 0.8 %stage.10 = (f32[256,1024]{1,0:T(8,128)S(1)}, f32[128,256]{1,0:T(8,128)S(1)}) custom-call(s32[1]{0:T(128)} %bitcast.me_ref, bf16[1488,128]{1,0:T(8,128)(2,1)S(1)} %collective-permute-done.1.refs_0_.refs_6_, bf16[1488,128]{1,0:T(8,128)(2,1)S(1)} %collective-permute-done.5.refs_1_.block_ref.refs_8_, ...), custom_call_target="tpu_custom_call", output_to_operand_aliasing={{0}: (10, {}), {1}: (11, {})} | custom-call | flops 167772160 | bytes 2097152 | tf_op jit(solution)/shard_map/stage/pallas_call | solution.py:437
  27.5 1.3 %collective-permute-done.4.block_ref.refs_0_.refs_10_ = bf16[1488,128]{1,0:T(8,128)(2,1)S(1)} collective-permute-done((bf16[1488,128]{1,0:T(8,128)(2,1)S(1)}, bf16[1488,128]{1,0:T(8,128)(2,1)S(1)}, u32[]{:S(2)}, u32[]{:S(2)}) %collective-permute-start.4) | collective-permute-done | bytes 380960 | tf_op jit(solution)/shard_map/ppermute | solution.py:52
  28.9 1.4 %collective-permute-start.9 = (bf16[960,128]{1,0:T(8,128)(2,1)S(1)}, bf16[960,128]{1,0:T(8,128)(2,1)S(1)}, u32[]{:S(2)}, u32[]{:S(2)}) collective-permute-start(bf16[960,128]{1,0:T(8,128)(2,1)S(1)} %get-tuple-element.98), channel_id=1, source_target_pairs={{0,4},{1,3},{4,8},{5,1},{8,12},{9,5},{12,14},{13,9},{14,10},{15,13... | collective-permute-start | bytes 737288 | tf_op jit(solution)/shard_map/ppermute | solution.py:52
  30.3 1.7 %collective-permute-start.8 = (bf16[1056,128]{1,0:T(8,128)(2,1)S(1)}, bf16[1056,128]{1,0:T(8,128)(2,1)S(1)}, u32[]{:S(2)}, u32[]{:S(2)}) collective-permute-start(bf16[1056,128]{1,0:T(8,128)(2,1)S(1)} %get-tuple-element.97), channel_id=1, source_target_pairs={{0,4},{1,3},{4,8},{5,1},{8,12},{9,5},{12,14},{13,9},{14,10},{15,13... | collective-permute-start | bytes 811016 | tf_op jit(solution)/shard_map/ppermute | solution.py:52
  32.0 0.8 %stage.11 = (f32[256,1024]{1,0:T(8,128)S(1)}, f32[128,256]{1,0:T(8,128)S(1)}) custom-call(s32[1]{0:T(128)} %bitcast.me_ref, bf16[1488,128]{1,0:T(8,128)(2,1)S(1)} %collective-permute-done.11.refs_0_.refs_7_, bf16[1488,128]{1,0:T(8,128)(2,1)S(1)} %collective-permute-done.12.refs_1_.refs_9_, ...), custom_call_target="tpu_custom_call", output_to_operand_aliasing={{0}: (10, {}), {1}: (11, {})} | custom-call | flops 167772160 | bytes 2097152 | tf_op jit(solution)/shard_map/stage/pallas_call | solution.py:437
  32.9 0.8 %stage.12 = (f32[256,1024]{1,0:T(8,128)S(1)}, f32[128,256]{1,0:T(8,128)S(1)}) custom-call(s32[1]{0:T(128)} %bitcast.me_ref, bf16[1488,128]{1,0:T(8,128)(2,1)S(1)} %collective-permute-done.4.block_ref.refs_0_.refs_10_, bf16[960,128]{1,0:T(8,128)(2,1)S(1)} %collective-permute-done.10.refs_1_, ...), custom_call_target="tpu_custom_call", output_to_operand_aliasing={{0}: (10, {}), {1}: (11, {})} | custom-call | flops 167772160 | bytes 2097152 | tf_op jit(solution)/shard_map/stage/pallas_call | solution.py:437
  33.7 1.4 %collective-permute-done.9.refs_0_ = bf16[960,128]{1,0:T(8,128)(2,1)S(1)} collective-permute-done((bf16[960,128]{1,0:T(8,128)(2,1)S(1)}, bf16[960,128]{1,0:T(8,128)(2,1)S(1)}, u32[]{:S(2)}, u32[]{:S(2)}) %collective-permute-start.9) | collective-permute-done | bytes 245792 | tf_op jit(solution)/shard_map/ppermute | solution.py:52
  35.1 0.8 %stage.13 = (f32[256,1024]{1,0:T(8,128)S(1)}, f32[128,256]{1,0:T(8,128)S(1)}) custom-call(s32[1]{0:T(128)} %bitcast.me_ref, bf16[1488,128]{1,0:T(8,128)(2,1)S(1)} %collective-permute-done.14.refs_0_.refs_11_, bf16[960,128]{1,0:T(8,128)(2,1)S(1)} %collective-permute-done.15.refs_1_, ...), custom_call_target="tpu_custom_call", output_to_operand_aliasing={{0}: (10, {}), {1}: (11, {})} | custom-call | flops 167772160 | bytes 2097152 | tf_op jit(solution)/shard_map/stage/pallas_call | solution.py:437
  35.9 0.7 %collective-permute-done.13.refs_1_ = bf16[960,128]{1,0:T(8,128)(2,1)S(1)} collective-permute-done((bf16[960,128]{1,0:T(8,128)(2,1)S(1)}, bf16[960,128]{1,0:T(8,128)(2,1)S(1)}, u32[]{:S(2)}, u32[]{:S(2)}) %collective-permute-start.13) | collective-permute-done | bytes 245792 | tf_op jit(solution)/shard_map/ppermute | solution.py:56
  36.6 2.5 %features.1.unit_ref = f32[128,128]{1,0:T(8,128)S(1)} custom-call(s32[1]{0:T(128)} %bitcast.me_ref, s32[1,2]{1,0:T(1,128)S(1)} %copy-done, bf16[960,128]{1,0:T(8,128)(2,1)S(1)} %collective-permute-done.9.refs_0_, bf16[960,128]{1,0:T(8,128)(2,1)S(1)} %collective-permute-done.13.refs_1_, bf16[256,5120]{1,0:T(8,128)(2,1)S(1)} %get-tuple-element.71.refs_2_, ...), custom_call_target="tpu_custom_call" | custom-call | flops 1 | bytes 1 | tf_op jit(solution)/shard_map/features/pallas_call | solution.py:491
  39.1 0.2 collective-permute-start.16
  39.3 0.9 %scores.1.best_ref = f32[2,3,8,128]{3,2,1,0:T(8,128)S(1)} custom-call(f32[128,128]{1,0:T(8,128)S(1)} %features.1.unit_ref, bf16[1488,128]{1,0:T(8,128)(2,1)S(1)} %pack.1.refs_0_, bf16[1488,128]{1,0:T(8,128)(2,1)S(1)} %collective-permute-done.3.refs_1_, bf16[1488,128]{1,0:T(8,128)(2,1)S(1)} %collective-permute-done.refs_0_.refs_2_, ...), custom_call_target="tpu_custom_call" | custom-call | flops 4194304 | bytes 2097152 | tf_op jit(solution)/shard_map/scores/pallas_call | solution.py:514
  40.2 0.5 %collective-permute-done.16.block_ref = bf16[1056,128]{1,0:T(8,128)(2,1)S(1)} collective-permute-done((bf16[1056,128]{1,0:T(8,128)(2,1)S(1)}, bf16[1056,128]{1,0:T(8,128)(2,1)S(1)}, u32[]{:S(2)}, u32[]{:S(2)}) %collective-permute-start.16) | collective-permute-done | bytes 270368 | tf_op jit(solution)/shard_map/ppermute | solution.py:56
  40.7 0.8 %last_scores.1 = (f32[2,3]{1,0:T(2,128)}, f32[1,2]{1,0:T(1,128)}) custom-call(f32[128,128]{1,0:T(8,128)S(1)} %features.1.unit_ref, bf16[1056,128]{1,0:T(8,128)(2,1)S(1)} %collective-permute-done.16.block_ref, f32[2,3,8,128]{3,2,1,0:T(8,128)S(1)} %scores.1.best_ref), custom_call_target="tpu_custom_call" | custom-call | tf_op jit(solution)/shard_map/last_scores/pallas_call | solution.py:523
  (19 shorter events, 0.2 us)
Async XLA Ops:
  2.1 10.9 %collective-permute-start = (bf16[1488,128]{1,0:T(8,128)(2,1)S(1)}, bf16[1488,128]{1,0:T(8,128)(2,1)S(1)}, u32[]{:S(2)}, u32[]{:S(2)}) collective-permute-start(bf16[1488,128]{1,0:T(8,128)(2,1)S(1)} %pack.1.refs_0_), channel_id=1, source_target_pairs={{0,4},{1,3},{4,8},{5,1},{8,12},{9,5},{12,14},{13,9},{14,10},{15,13... | collective-permute-start | bytes 1142792 | tf_op jit(solution)/shard_map/ppermute | solution.py:52
  8.9 5.5 %collective-permute-start.3 = (bf16[1488,128]{1,0:T(8,128)(2,1)S(1)}, bf16[1488,128]{1,0:T(8,128)(2,1)S(1)}, u32[]{:S(2)}, u32[]{:S(2)}) collective-permute-start(bf16[1488,128]{1,0:T(8,128)(2,1)S(1)} %pack.1.refs_0_), channel_id=1, source_target_pairs={{0,1},{1,0},{2,3},{3,2},{4,5},{5,4},{6,7},{7,6},{8,9},{9,8},{10,11... | collective-permute-start | bytes 1142792 | tf_op jit(solution)/shard_map/ppermute | solution.py:56
  8.9 7.1 %collective-permute-start.2 = (bf16[1488,128]{1,0:T(8,128)(2,1)S(1)}, bf16[1488,128]{1,0:T(8,128)(2,1)S(1)}, u32[]{:S(2)}, u32[]{:S(2)}) collective-permute-start(bf16[1488,128]{1,0:T(8,128)(2,1)S(1)} %pack.1.refs_0_), channel_id=1, source_target_pairs={{1,4},{0,3},{5,8},{4,1},{9,12},{8,5},{13,14},{12,9},{15,10},{14,13... | collective-permute-start | bytes 1142792 | tf_op jit(solution)/shard_map/ppermute | solution.py:52
  13.0 7.7 %collective-permute-start.1 = (bf16[1488,128]{1,0:T(8,128)(2,1)S(1)}, bf16[1488,128]{1,0:T(8,128)(2,1)S(1)}, u32[]{:S(2)}, u32[]{:S(2)}) collective-permute-start(bf16[1488,128]{1,0:T(8,128)(2,1)S(1)} %collective-permute-done.refs_0_.refs_2_), channel_id=1, source_target_pairs={{0,4},{1,3},{4,8},{5,1},{8,12},{9,5},{12,14},{13,9},{14,10},{15,13... | collective-permute-start | bytes 1142792 | tf_op jit(solution)/shard_map/ppermute | solution.py:52
  16.1 6.0 %collective-permute-start.7 = (bf16[1488,128]{1,0:T(8,128)(2,1)S(1)}, bf16[1488,128]{1,0:T(8,128)(2,1)S(1)}, u32[]{:S(2)}, u32[]{:S(2)}) collective-permute-start(bf16[1488,128]{1,0:T(8,128)(2,1)S(1)} %collective-permute-done.2.refs_1_.refs_4_), channel_id=1, source_target_pairs={{0,1},{1,0},{2,3},{3,2},{4,5},{5,4},{6,7},{7,6},{8,9},{9,8},{10,11... | collective-permute-start | bytes 1142792 | tf_op jit(solution)/shard_map/ppermute | solution.py:56
  16.8 5.2 %collective-permute-start.6 = (bf16[1488,128]{1,0:T(8,128)(2,1)S(1)}, bf16[1488,128]{1,0:T(8,128)(2,1)S(1)}, u32[]{:S(2)}, u32[]{:S(2)}) collective-permute-start(bf16[1488,128]{1,0:T(8,128)(2,1)S(1)} %collective-permute-done.refs_0_.refs_2_), channel_id=1, source_target_pairs={{0,1},{1,0},{2,3},{3,2},{4,5},{5,4},{6,7},{7,6},{8,9},{9,8},{10,11... | collective-permute-start | bytes 1142792 | tf_op jit(solution)/shard_map/ppermute | solution.py:56
  16.8 7.9 %collective-permute-start.5 = (bf16[1488,128]{1,0:T(8,128)(2,1)S(1)}, bf16[1488,128]{1,0:T(8,128)(2,1)S(1)}, u32[]{:S(2)}, u32[]{:S(2)}) collective-permute-start(bf16[1488,128]{1,0:T(8,128)(2,1)S(1)} %collective-permute-done.2.refs_1_.refs_4_), channel_id=1, source_target_pairs={{0,4},{1,3},{4,8},{5,1},{8,12},{9,5},{12,14},{13,9},{14,10},{15,13... | collective-permute-start | bytes 1142792 | tf_op jit(solution)/shard_map/ppermute | solution.py:52
  20.7 8.2 %collective-permute-start.4 = (bf16[1488,128]{1,0:T(8,128)(2,1)S(1)}, bf16[1488,128]{1,0:T(8,128)(2,1)S(1)}, u32[]{:S(2)}, u32[]{:S(2)}) collective-permute-start(bf16[1488,128]{1,0:T(8,128)(2,1)S(1)} %collective-permute-done.1.refs_0_.refs_6_), channel_id=1, source_target_pairs={{0,4},{1,3},{4,8},{5,1},{8,12},{9,5},{12,14},{13,9},{14,10},{15,13... | collective-permute-start | bytes 1142792 | tf_op jit(solution)/shard_map/ppermute | solution.py:52
  24.7 5.6 %collective-permute-start.12 = (bf16[1488,128]{1,0:T(8,128)(2,1)S(1)}, bf16[1488,128]{1,0:T(8,128)(2,1)S(1)}, u32[]{:S(2)}, u32[]{:S(2)}) collective-permute-start(bf16[1488,128]{1,0:T(8,128)(2,1)S(1)} %collective-permute-done.5.refs_1_.block_ref.refs_8_), channel_id=1, source_target_pairs={{0,1},{1,0},{2,3},{3,2},{4,5},{5,4},{6,7},{7,6},{8,9},{9,8},{10,11... | collective-permute-start | bytes 1142792 | tf_op jit(solution)/shard_map/ppermute | solution.py:56
  25.0 7.0 %collective-permute-start.11 = (bf16[1488,128]{1,0:T(8,128)(2,1)S(1)}, bf16[1488,128]{1,0:T(8,128)(2,1)S(1)}, u32[]{:S(2)}, u32[]{:S(2)}) collective-permute-start(bf16[1488,128]{1,0:T(8,128)(2,1)S(1)} %collective-permute-done.1.refs_0_.refs_6_), channel_id=1, source_target_pairs={{0,1},{1,0},{2,3},{3,2},{4,5},{5,4},{6,7},{7,6},{8,9},{9,8},{10,11... | collective-permute-start | bytes 1142792 | tf_op jit(solution)/shard_map/ppermute | solution.py:56
  25.3 7.5 %collective-permute-start.10 = (bf16[960,128]{1,0:T(8,128)(2,1)S(1)}, bf16[960,128]{1,0:T(8,128)(2,1)S(1)}, u32[]{:S(2)}, u32[]{:S(2)}) collective-permute-start(bf16[960,128]{1,0:T(8,128)(2,1)S(1)} %get-tuple-element.99), channel_id=1, source_target_pairs={{0,4},{1,3},{4,8},{5,1},{8,12},{9,5},{12,14},{13,9},{14,10},{15,13... | collective-permute-start | bytes 737288 | tf_op jit(solution)/shard_map/ppermute | solution.py:52
  28.9 6.2 %collective-permute-start.9 = (bf16[960,128]{1,0:T(8,128)(2,1)S(1)}, bf16[960,128]{1,0:T(8,128)(2,1)S(1)}, u32[]{:S(2)}, u32[]{:S(2)}) collective-permute-start(bf16[960,128]{1,0:T(8,128)(2,1)S(1)} %get-tuple-element.98), channel_id=1, source_target_pairs={{0,4},{1,3},{4,8},{5,1},{8,12},{9,5},{12,14},{13,9},{14,10},{15,13... | collective-permute-start | bytes 737288 | tf_op jit(solution)/shard_map/ppermute | solution.py:52
  30.3 4.8 %collective-permute-start.14 = (bf16[1488,128]{1,0:T(8,128)(2,1)S(1)}, bf16[1488,128]{1,0:T(8,128)(2,1)S(1)}, u32[]{:S(2)}, u32[]{:S(2)}) collective-permute-start(bf16[1488,128]{1,0:T(8,128)(2,1)S(1)} %collective-permute-done.4.block_ref.refs_0_.refs_10_), channel_id=1, source_target_pairs={{0,1},{1,0},{2,3},{3,2},{4,5},{5,4},{6,7},{7,6},{8,9},{9,8},{10,11... | collective-permute-start | bytes 1142792 | tf_op jit(solution)/shard_map/ppermute | solution.py:56
  30.3 8.8 %collective-permute-start.8 = (bf16[1056,128]{1,0:T(8,128)(2,1)S(1)}, bf16[1056,128]{1,0:T(8,128)(2,1)S(1)}, u32[]{:S(2)}, u32[]{:S(2)}) collective-permute-start(bf16[1056,128]{1,0:T(8,128)(2,1)S(1)} %get-tuple-element.97), channel_id=1, source_target_pairs={{0,4},{1,3},{4,8},{5,1},{8,12},{9,5},{12,14},{13,9},{14,10},{15,13... | collective-permute-start | bytes 811016 | tf_op jit(solution)/shard_map/ppermute | solution.py:52
  32.8 2.3 %collective-permute-start.15 = (bf16[960,128]{1,0:T(8,128)(2,1)S(1)}, bf16[960,128]{1,0:T(8,128)(2,1)S(1)}, u32[]{:S(2)}, u32[]{:S(2)}) collective-permute-start(bf16[960,128]{1,0:T(8,128)(2,1)S(1)} %collective-permute-done.10.refs_1_), channel_id=1, source_target_pairs={{0,1},{1,0},{2,3},{3,2},{4,5},{5,4},{6,7},{7,6},{8,9},{9,8},{10,11... | collective-permute-start | bytes 737288 | tf_op jit(solution)/shard_map/ppermute | solution.py:56
  35.1 1.5 %copy-start = (s32[1,2]{1,0:T(1,128)S(1)}, s32[1,2]{1,0:T(1,128)}, u32[]{:S(2)}) copy-start(s32[1,2]{1,0:T(1,128)} %counts_ref.1) | copy-start | bytes 28
  35.1 1.5 %collective-permute-start.13 = (bf16[960,128]{1,0:T(8,128)(2,1)S(1)}, bf16[960,128]{1,0:T(8,128)(2,1)S(1)}, u32[]{:S(2)}, u32[]{:S(2)}) collective-permute-start(bf16[960,128]{1,0:T(8,128)(2,1)S(1)} %collective-permute-done.9.refs_0_), channel_id=1, source_target_pairs={{0,1},{1,0},{2,3},{3,2},{4,5},{5,4},{6,7},{7,6},{8,9},{9,8},{10,11... | collective-permute-start | bytes 737288 | tf_op jit(solution)/shard_map/ppermute | solution.py:56
  39.1 1.6 %collective-permute-start.16 = (bf16[1056,128]{1,0:T(8,128)(2,1)S(1)}, bf16[1056,128]{1,0:T(8,128)(2,1)S(1)}, u32[]{:S(2)}, u32[]{:S(2)}) collective-permute-start(bf16[1056,128]{1,0:T(8,128)(2,1)S(1)} %collective-permute-done.8.refs_12_), channel_id=1, source_target_pairs={{0,1},{1,0},{2,3},{3,2},{4,5},{5,4},{6,7},{7,6},{8,9},{9,8},{10,11... | collective-permute-start | bytes 811016 | tf_op jit(solution)/shard_map/ppermute | solution.py:56

commit v12 on v11

--- a/solution.py
+++ b/solution.py
@@ -117,9 +117,10 @@
     return jnp.where(lower, turned, value) if which else jnp.where(lower, value, turned)
 
 
-def local_kernel(*refs):
-    x_hbm, target_hbm, gain_hbm, source_hbm, x_ref, target_ref, turned_ref, sums_ref = refs[:8]
-    gain_ref, source_ref, sems = refs[8:]
+def local_kernel(after_ref, *refs):
+    x_hbm, values_hbm, target_hbm, gain_hbm, source_hbm = refs[:5]
+    x_ref, values_ref, target_ref, turned_ref, sums_ref = refs[5:10]
+    gain_ref, source_ref, sems = refs[10:]
     tokens, width = x_ref.shape
     span = width // STEPS
     copies = []
@@ -132,6 +133,7 @@
             (target_hbm.at[part], target_ref.at[part]),
         )
         copies.append(load(pairs, sems.at[j]))
+    later = load(((values_hbm, values_ref),), sems.at[STEPS])
     products = jnp.zeros((tokens, 2 * LANES), F32)
     squares = jnp.zeros((tokens, LANES), F32)
     for j in range(STEPS):
@@ -151,9 +153,11 @@
     left_one = inverse * doubled(products[:, :LANES], 1)
     for i, value in enumerate((inverse, left_one, products[:, LANES:])):
         sums_ref[:, i * LANES : (i + 1) * LANES] = value
-
-
-def fetch_kernel(after_ref, *refs):
+    for copy in later:
+        copy.wait()
+
+
+def fetch_kernel(*refs):
     count = (len(refs) - 1) // 2
     pairs = []
     for src, dst in zip(refs[:count], refs[count:-1]):
@@ -395,35 +399,35 @@
     )(me.reshape(1), *in_hbm(inputs))
 
     tie = lax.optimization_barrier
-    inputs = (x, bottom_target_sketch, top_rmsnorm_weights.reshape(1, width), source_sketch.T)
-    upper, low_target, source, local = pl.pallas_call(
+    inputs = (mixed, adjoint, top_target_sketch)
+    fetched = pl.pallas_call(
+        fetch_kernel,
+        out_shape=[jax.ShapeDtypeStruct(a.shape, a.dtype) for a in inputs],
+        in_specs=[HBM] * len(inputs),
+        out_specs=[VMEM] * len(inputs),
+        scratch_shapes=[pltpu.SemaphoreType.DMA((STEPS * len(inputs),))],
+        compiler_params=params(16),
+        cost_estimate=cost(1, 6 * MIB),
+        name="fetch",
+    )(*in_hbm(inputs))
+    own_late, fetched = tie((own, fetched))
+    inputs = (x, values, bottom_target_sketch, top_rmsnorm_weights.reshape(1, width), source_sketch.T)
+    upper, upper_values, low_target, source, local = pl.pallas_call(
         local_kernel,
-        out_shape=[jax.ShapeDtypeStruct(a.shape, a.dtype) for a in inputs[:2]]
+        out_shape=[jax.ShapeDtypeStruct(a.shape, a.dtype) for a in inputs[:3]]
         + [
             jax.ShapeDtypeStruct((width, LANES), BF16),
             jax.ShapeDtypeStruct((tokens, LOCAL_SUMS * LANES), F32),
         ],
-        in_specs=[HBM] * len(inputs),
-        out_specs=[VMEM] * 4,
-        scratch_shapes=[pltpu.VMEM(a.shape, a.dtype) for a in inputs[2:]]
-        + [pltpu.SemaphoreType.DMA((STEPS, len(inputs)))],
+        in_specs=[VMEM] + [HBM] * len(inputs),
+        out_specs=[VMEM] * 5,
+        scratch_shapes=[pltpu.VMEM(a.shape, a.dtype) for a in inputs[3:]]
+        + [pltpu.SemaphoreType.DMA((STEPS + 1, 4))],
         compiler_params=params(16),
-        cost_estimate=cost(tokens * width * LANES * 4, 6 * MIB),
+        cost_estimate=cost(tokens * width * LANES * 4, 7 * MIB),
         name="local_products",
-    )(*in_hbm(inputs))
-    own_late, local = tie((own, local))
-    inputs = (mixed, adjoint, values, top_target_sketch)
-    fetched = pl.pallas_call(
-        fetch_kernel,
-        out_shape=[jax.ShapeDtypeStruct(a.shape, a.dtype) for a in inputs],
-        in_specs=[VMEM] + [HBM] * len(inputs),
-        out_specs=[VMEM] * len(inputs),
-        scratch_shapes=[pltpu.SemaphoreType.DMA((STEPS * len(inputs),))],
-        compiler_params=params(16),
-        cost_estimate=cost(1, 8 * MIB),
-        name="fetch",
-    )(local, *in_hbm(inputs))
-    activations = [upper, *fetched[:3], low_target, fetched[3], source]
+    )(fetched[2], *in_hbm(inputs))
+    activations = [upper, *fetched[:2], upper_values, low_target, fetched[2], source]
 
     stage_scratch = [
         pltpu.VMEM((2 * rows, 2 * LANES), BF16),

time: 41.8 us -> 41.4 us (level)
  Pallas kernels: 18.2 us -> 17.7 us
    pallas_call x1, Pallas kernels: 3.25 us -> 2.8 us  [shards(): pl.pallas_call(fetch_kernel, out_shape=[jax.ShapeDtypeStruct(a.shape, a.d...]
where the time goes in v12:
time: 41.4 us; the launch traced here: 41.1 us
  Pallas kernels  17.7 us (43%)
  starting transfers between devices  14.2 us (34%)
  waiting for transfers between devices  8.41 us (20%)
  between operations  0.79 us (2%)
    ppermute x8, starting transfers between devices, hop(): return lax.ppermute(value, 'dp', pairs)  12.8 us
    ppermute x8, waiting for transfers between devices, hop(): return lax.ppermute(value, 'dp', pairs)  7.17 us
    pallas_call x7, Pallas kernels, stage(): pl.pallas_call(functools.partial(stage_kernel, away, first), out_shape=[j...  5.57 us
    pallas_call x1, Pallas kernels, shards(): pl.pallas_call(local_kernel, out_shape=[jax.ShapeDtypeStruct(a.shape, a.d...  3.75 us
    pallas_call x1, Pallas kernels, shards(): pl.pallas_call(fetch_kernel, out_shape=[jax.ShapeDtypeStruct(a.shape, a.d...  2.8 us
    pallas_call x1, Pallas kernels, shards(): pl.pallas_call(functools.partial(feature_kernel, half), out_shape=jax.Sha...  2.48 us
    pallas_call x1, Pallas kernels, shards(): pl.pallas_call(pack_kernel, out_shape=jax.ShapeDtypeStruct((3 * rows + (L...  1.41 us
    ppermute x9, starting transfers between devices, other_core(): lax.ppermute(value, 'dp', [(d, d ^ 1) for d in range(2 * RING_CHIPS)])  1.36 us
  transfers between devices with their start and end apart: 17, of which 7 were waited for; matrix products, arithmetic and copies ran while one was open for 0% of the time, Pallas kernels for 38%

profile of v12, /device:TPU:0, one launch (start us, length us, event | category | flops | bytes accessed | tf_op | source)
XLA Modules:
  0.0 41.1 jit_solution(1696419574615356651)
XLA Ops:
  0.6 1.4 %pack.1.refs_0_ = bf16[1488,128]{1,0:T(8,128)(2,1)S(1)} custom-call(s32[1]{0:T(128)} %bitcast.me_ref, f32[40,128]{1,0:T(8,128)} %bitcast.12, bf16[320,128]{1,0:T(8,128)(2,1)} %refs_1_.3, bf16[320,128]{1,0:T(8,128)(2,1)} %bitcast.11, bf16[128,128]{1,0:T(8,128)(2,1)} %refs_3_.1, bf16[160,128]{1,0:T(8,128)(2,1)} %bitcast.14, bf16[320,128]{1,0:T(8,128)(2,1)} %refs_5_.1, ...), custom_call_target="tpu_custom_call" | custom-call | tf_op jit(solution)/shard_map/pack/pallas_call | solution.py:390
  2.1 3.1 %collective-permute-start = (bf16[1488,128]{1,0:T(8,128)(2,1)S(1)}, bf16[1488,128]{1,0:T(8,128)(2,1)S(1)}, u32[]{:S(2)}, u32[]{:S(2)}) collective-permute-start(bf16[1488,128]{1,0:T(8,128)(2,1)S(1)} %pack.1.refs_0_), channel_id=1, source_target_pairs={{0,4},{1,3},{4,8},{5,1},{8,12},{9,5},{12,14},{13,9},{14,10},{15,13... | collective-permute-start | bytes 1142792 | tf_op jit(solution)/shard_map/ppermute | solution.py:52
  5.1 2.8 %fetch.1 = (bf16[256,5120]{1,0:T(8,128)(2,1)S(1)}, bf16[256,5120]{1,0:T(8,128)(2,1)S(1)}, bf16[2560,128]{1,0:T(8,128)(2,1)S(1)}) custom-call(bf16[256,5120]{1,0:T(8,128)(2,1)} %refs_0_.2, bf16[256,5120]{1,0:T(8,128)(2,1)} %refs_1_.4, bf16[2560,128]{1,0:T(8,128)(2,1)} %refs_2_.2), custom_call_target="tpu_custom_call" | custom-call | flops 1 | bytes 6291456 | tf_op jit(solution)/shard_map/fetch/pallas_call | solution.py:403
  8.0 0.7 %collective-permute-start.2 = (bf16[1488,128]{1,0:T(8,128)(2,1)S(1)}, bf16[1488,128]{1,0:T(8,128)(2,1)S(1)}, u32[]{:S(2)}, u32[]{:S(2)}) collective-permute-start(bf16[1488,128]{1,0:T(8,128)(2,1)S(1)} %pack.1.refs_0_), channel_id=1, source_target_pairs={{1,4},{0,3},{5,8},{4,1},{9,12},{8,5},{13,14},{12,9},{15,10},{14,13... | collective-permute-start | bytes 1142792 | tf_op jit(solution)/shard_map/ppermute | solution.py:52
  8.8 3.7 %local_products.1 = (bf16[256,5120]{1,0:T(8,128)(2,1)S(1)}, bf16[256,2560]{1,0:T(8,128)(2,1)S(1)}, bf16[5120,128]{1,0:T(8,128)(2,1)S(1)}, bf16[5120,128]{1,0:T(8,128)(2,1)S(1)}, f32[256,384]{1,0:T(8,128)S(1)}) custom-call(bf16[2560,128]{1,0:T(8,128)(2,1)S(1)} %get-tuple-element.79.after_ref.refs_7_, bf16[256,5120]{1,0:T(8,128)(2,1)} %refs_0_.3, ...), custom_call_target="tpu_custom_call" | custom-call | flops 671088640 | bytes 7340032 | tf_op jit(solution)/shard_map/local_products/pallas_call | solution.py:415
  12.5 1.4 %collective-permute-start.1 = (bf16[1488,128]{1,0:T(8,128)(2,1)S(1)}, bf16[1488,128]{1,0:T(8,128)(2,1)S(1)}, u32[]{:S(2)}, u32[]{:S(2)}) collective-permute-start(bf16[1488,128]{1,0:T(8,128)(2,1)S(1)} %collective-permute-done.refs_0_.refs_2_), channel_id=1, source_target_pairs={{0,4},{1,3},{4,8},{5,1},{8,12},{9,5},{12,14},{13,9},{14,10},{15,13... | collective-permute-start | bytes 1142792 | tf_op jit(solution)/shard_map/ppermute | solution.py:52
  14.0 0.7 %stage.7 = (f32[256,1024]{1,0:T(8,128)S(1)}, f32[128,256]{1,0:T(8,128)S(1)}) custom-call(s32[1]{0:T(128)} %bitcast.me_ref, bf16[1488,128]{1,0:T(8,128)(2,1)S(1)} %pack.1.refs_0_, bf16[1488,128]{1,0:T(8,128)(2,1)S(1)} %collective-permute-done.3.refs_1_, bf16[256,5120]{1,0:T(8,128)(2,1)S(1)} %get-tuple-element.74.refs_2_, ...), custom_call_target="tpu_custom_call" | custom-call | flops 167772160 | bytes 2097152 | tf_op jit(solution)/shard_map/stage/pallas_call | solution.py:441
  14.7 0.5 %collective-permute-done.2.refs_1_.refs_4_ = bf16[1488,128]{1,0:T(8,128)(2,1)S(1)} collective-permute-done((bf16[1488,128]{1,0:T(8,128)(2,1)S(1)}, bf16[1488,128]{1,0:T(8,128)(2,1)S(1)}, u32[]{:S(2)}, u32[]{:S(2)}) %collective-permute-start.2) | collective-permute-done | bytes 380960 | tf_op jit(solution)/shard_map/ppermute | solution.py:52
  15.1 0.4 %collective-permute-start.7 = (bf16[1488,128]{1,0:T(8,128)(2,1)S(1)}, bf16[1488,128]{1,0:T(8,128)(2,1)S(1)}, u32[]{:S(2)}, u32[]{:S(2)}) collective-permute-start(bf16[1488,128]{1,0:T(8,128)(2,1)S(1)} %collective-permute-done.2.refs_1_.refs_4_), channel_id=1, source_target_pairs={{0,1},{1,0},{2,3},{3,2},{4,5},{5,4},{6,7},{7,6},{8,9},{9,8},{10,11... | collective-permute-start | bytes 1142792 | tf_op jit(solution)/shard_map/ppermute | solution.py:56
  15.7 1.7 %collective-permute-start.5 = (bf16[1488,128]{1,0:T(8,128)(2,1)S(1)}, bf16[1488,128]{1,0:T(8,128)(2,1)S(1)}, u32[]{:S(2)}, u32[]{:S(2)}) collective-permute-start(bf16[1488,128]{1,0:T(8,128)(2,1)S(1)} %collective-permute-done.2.refs_1_.refs_4_), channel_id=1, source_target_pairs={{0,4},{1,3},{4,8},{5,1},{8,12},{9,5},{12,14},{13,9},{14,10},{15,13... | collective-permute-start | bytes 1142792 | tf_op jit(solution)/shard_map/ppermute | solution.py:52
  17.4 0.8 %stage.8 = (f32[256,1024]{1,0:T(8,128)S(1)}, f32[128,256]{1,0:T(8,128)S(1)}) custom-call(s32[1]{0:T(128)} %bitcast.me_ref, bf16[1488,128]{1,0:T(8,128)(2,1)S(1)} %collective-permute-done.refs_0_.refs_2_, bf16[1488,128]{1,0:T(8,128)(2,1)S(1)} %collective-permute-done.2.refs_1_.refs_4_, ...), custom_call_target="tpu_custom_call", output_to_operand_aliasing={{0}: (10, {}), {1}: (11, {})} | custom-call | flops 167772160 | bytes 2097152 | tf_op jit(solution)/shard_map/stage/pallas_call | solution.py:441
  18.2 2.0 %collective-permute-done.1.refs_0_.refs_6_ = bf16[1488,128]{1,0:T(8,128)(2,1)S(1)} collective-permute-done((bf16[1488,128]{1,0:T(8,128)(2,1)S(1)}, bf16[1488,128]{1,0:T(8,128)(2,1)S(1)}, u32[]{:S(2)}, u32[]{:S(2)}) %collective-permute-start.1) | collective-permute-done | bytes 380960 | tf_op jit(solution)/shard_map/ppermute | solution.py:52
  20.2 1.4 %collective-permute-start.4 = (bf16[1488,128]{1,0:T(8,128)(2,1)S(1)}, bf16[1488,128]{1,0:T(8,128)(2,1)S(1)}, u32[]{:S(2)}, u32[]{:S(2)}) collective-permute-start(bf16[1488,128]{1,0:T(8,128)(2,1)S(1)} %collective-permute-done.1.refs_0_.refs_6_), channel_id=1, source_target_pairs={{0,4},{1,3},{4,8},{5,1},{8,12},{9,5},{12,14},{13,9},{14,10},{15,13... | collective-permute-start | bytes 1142792 | tf_op jit(solution)/shard_map/ppermute | solution.py:52
  21.6 0.8 %stage.9 = (f32[256,1024]{1,0:T(8,128)S(1)}, f32[128,256]{1,0:T(8,128)S(1)}) custom-call(s32[1]{0:T(128)} %bitcast.me_ref, bf16[1488,128]{1,0:T(8,128)(2,1)S(1)} %collective-permute-done.6.refs_0_.refs_3_, bf16[1488,128]{1,0:T(8,128)(2,1)S(1)} %collective-permute-done.7.refs_1_.refs_5_, ...), custom_call_target="tpu_custom_call", output_to_operand_aliasing={{0}: (10, {}), {1}: (11, {})} | custom-call | flops 167772160 | bytes 2097152 | tf_op jit(solution)/shard_map/stage/pallas_call | solution.py:441
  22.4 1.9 %collective-permute-done.5.refs_1_.block_ref.refs_8_ = bf16[1488,128]{1,0:T(8,128)(2,1)S(1)} collective-permute-done((bf16[1488,128]{1,0:T(8,128)(2,1)S(1)}, bf16[1488,128]{1,0:T(8,128)(2,1)S(1)}, u32[]{:S(2)}, u32[]{:S(2)}) %collective-permute-start.5) | collective-permute-done | bytes 380960 | tf_op jit(solution)/shard_map/ppermute | solution.py:52
  24.3 0.2 collective-permute-start.12
  24.5 0.4 collective-permute-start.11
  24.8 1.4 %collective-permute-start.10 = (bf16[960,128]{1,0:T(8,128)(2,1)S(1)}, bf16[960,128]{1,0:T(8,128)(2,1)S(1)}, u32[]{:S(2)}, u32[]{:S(2)}) collective-permute-start(bf16[960,128]{1,0:T(8,128)(2,1)S(1)} %get-tuple-element.102), channel_id=1, source_target_pairs={{0,4},{1,3},{4,8},{5,1},{8,12},{9,5},{12,14},{13,9},{14,10},{15,13... | collective-permute-start | bytes 737288 | tf_op jit(solution)/shard_map/ppermute | solution.py:52
  26.3 0.8 %stage.10 = (f32[256,1024]{1,0:T(8,128)S(1)}, f32[128,256]{1,0:T(8,128)S(1)}) custom-call(s32[1]{0:T(128)} %bitcast.me_ref, bf16[1488,128]{1,0:T(8,128)(2,1)S(1)} %collective-permute-done.1.refs_0_.refs_6_, bf16[1488,128]{1,0:T(8,128)(2,1)S(1)} %collective-permute-done.5.refs_1_.block_ref.refs_8_, ...), custom_call_target="tpu_custom_call", output_to_operand_aliasing={{0}: (10, {}), {1}: (11, {})} | custom-call | flops 167772160 | bytes 2097152 | tf_op jit(solution)/shard_map/stage/pallas_call | solution.py:441
  27.1 1.3 %collective-permute-done.4.block_ref.refs_0_.refs_10_ = bf16[1488,128]{1,0:T(8,128)(2,1)S(1)} collective-permute-done((bf16[1488,128]{1,0:T(8,128)(2,1)S(1)}, bf16[1488,128]{1,0:T(8,128)(2,1)S(1)}, u32[]{:S(2)}, u32[]{:S(2)}) %collective-permute-start.4) | collective-permute-done | bytes 380960 | tf_op jit(solution)/shard_map/ppermute | solution.py:52
  28.4 1.4 %collective-permute-start.9 = (bf16[960,128]{1,0:T(8,128)(2,1)S(1)}, bf16[960,128]{1,0:T(8,128)(2,1)S(1)}, u32[]{:S(2)}, u32[]{:S(2)}) collective-permute-start(bf16[960,128]{1,0:T(8,128)(2,1)S(1)} %get-tuple-element.101), channel_id=1, source_target_pairs={{0,4},{1,3},{4,8},{5,1},{8,12},{9,5},{12,14},{13,9},{14,10},{15,13... | collective-permute-start | bytes 737288 | tf_op jit(solution)/shard_map/ppermute | solution.py:52
  29.9 1.6 %collective-permute-start.8 = (bf16[1056,128]{1,0:T(8,128)(2,1)S(1)}, bf16[1056,128]{1,0:T(8,128)(2,1)S(1)}, u32[]{:S(2)}, u32[]{:S(2)}) collective-permute-start(bf16[1056,128]{1,0:T(8,128)(2,1)S(1)} %get-tuple-element.100), channel_id=1, source_target_pairs={{0,4},{1,3},{4,8},{5,1},{8,12},{9,5},{12,14},{13,9},{14,10},{15,13... | collective-permute-start | bytes 811016 | tf_op jit(solution)/shard_map/ppermute | solution.py:52
  31.4 0.8 %stage.11 = (f32[256,1024]{1,0:T(8,128)S(1)}, f32[128,256]{1,0:T(8,128)S(1)}) custom-call(s32[1]{0:T(128)} %bitcast.me_ref, bf16[1488,128]{1,0:T(8,128)(2,1)S(1)} %collective-permute-done.11.refs_0_.refs_7_, bf16[1488,128]{1,0:T(8,128)(2,1)S(1)} %collective-permute-done.12.refs_1_.refs_9_, ...), custom_call_target="tpu_custom_call", output_to_operand_aliasing={{0}: (10, {}), {1}: (11, {})} | custom-call | flops 167772160 | bytes 2097152 | tf_op jit(solution)/shard_map/stage/pallas_call | solution.py:441
  32.3 0.8 %stage.12 = (f32[256,1024]{1,0:T(8,128)S(1)}, f32[128,256]{1,0:T(8,128)S(1)}) custom-call(s32[1]{0:T(128)} %bitcast.me_ref, bf16[1488,128]{1,0:T(8,128)(2,1)S(1)} %collective-permute-done.4.block_ref.refs_0_.refs_10_, bf16[960,128]{1,0:T(8,128)(2,1)S(1)} %collective-permute-done.10.refs_1_, ...), custom_call_target="tpu_custom_call", output_to_operand_aliasing={{0}: (10, {}), {1}: (11, {})} | custom-call | flops 167772160 | bytes 2097152 | tf_op jit(solution)/shard_map/stage/pallas_call | solution.py:441
  33.2 1.5 %collective-permute-done.9.refs_0_ = bf16[960,128]{1,0:T(8,128)(2,1)S(1)} collective-permute-done((bf16[960,128]{1,0:T(8,128)(2,1)S(1)}, bf16[960,128]{1,0:T(8,128)(2,1)S(1)}, u32[]{:S(2)}, u32[]{:S(2)}) %collective-permute-start.9) | collective-permute-done | bytes 245792 | tf_op jit(solution)/shard_map/ppermute | solution.py:52
  34.7 0.8 %stage.13 = (f32[256,1024]{1,0:T(8,128)S(1)}, f32[128,256]{1,0:T(8,128)S(1)}) custom-call(s32[1]{0:T(128)} %bitcast.me_ref, bf16[1488,128]{1,0:T(8,128)(2,1)S(1)} %collective-permute-done.14.refs_0_.refs_11_, bf16[960,128]{1,0:T(8,128)(2,1)S(1)} %collective-permute-done.15.refs_1_, ...), custom_call_target="tpu_custom_call", output_to_operand_aliasing={{0}: (10, {}), {1}: (11, {})} | custom-call | flops 167772160 | bytes 2097152 | tf_op jit(solution)/shard_map/stage/pallas_call | solution.py:441
  35.5 0.7 %collective-permute-done.13.refs_1_ = bf16[960,128]{1,0:T(8,128)(2,1)S(1)} collective-permute-done((bf16[960,128]{1,0:T(8,128)(2,1)S(1)}, bf16[960,128]{1,0:T(8,128)(2,1)S(1)}, u32[]{:S(2)}, u32[]{:S(2)}) %collective-permute-start.13) | collective-permute-done | bytes 245792 | tf_op jit(solution)/shard_map/ppermute | solution.py:56
  36.2 2.5 %features.1.unit_ref = f32[128,128]{1,0:T(8,128)S(1)} custom-call(s32[1]{0:T(128)} %bitcast.me_ref, s32[1,2]{1,0:T(1,128)S(1)} %copy-done, bf16[960,128]{1,0:T(8,128)(2,1)S(1)} %collective-permute-done.9.refs_0_, bf16[960,128]{1,0:T(8,128)(2,1)S(1)} %collective-permute-done.13.refs_1_, bf16[256,5120]{1,0:T(8,128)(2,1)S(1)} %get-tuple-element.74.refs_2_, ...), custom_call_target="tpu_custom_call" | custom-call | flops 1 | bytes 1 | tf_op jit(solution)/shard_map/features/pallas_call | solution.py:495
  38.7 0.2 collective-permute-start.16
  38.9 0.9 %scores.1.best_ref = f32[2,3,8,128]{3,2,1,0:T(8,128)S(1)} custom-call(f32[128,128]{1,0:T(8,128)S(1)} %features.1.unit_ref, bf16[1488,128]{1,0:T(8,128)(2,1)S(1)} %pack.1.refs_0_, bf16[1488,128]{1,0:T(8,128)(2,1)S(1)} %collective-permute-done.3.refs_1_, bf16[1488,128]{1,0:T(8,128)(2,1)S(1)} %collective-permute-done.refs_0_.refs_2_, ...), custom_call_target="tpu_custom_call" | custom-call | flops 4194304 | bytes 2097152 | tf_op jit(solution)/shard_map/scores/pallas_call | solution.py:518
  39.7 0.6 %collective-permute-done.16.block_ref = bf16[1056,128]{1,0:T(8,128)(2,1)S(1)} collective-permute-done((bf16[1056,128]{1,0:T(8,128)(2,1)S(1)}, bf16[1056,128]{1,0:T(8,128)(2,1)S(1)}, u32[]{:S(2)}, u32[]{:S(2)}) %collective-permute-start.16) | collective-permute-done | bytes 270368 | tf_op jit(solution)/shard_map/ppermute | solution.py:56
  40.3 0.8 %last_scores.1 = (f32[2,3]{1,0:T(2,128)}, f32[1,2]{1,0:T(1,128)}) custom-call(f32[128,128]{1,0:T(8,128)S(1)} %features.1.unit_ref, bf16[1056,128]{1,0:T(8,128)(2,1)S(1)} %collective-permute-done.16.block_ref, f32[2,3,8,128]{3,2,1,0:T(8,128)S(1)} %scores.1.best_ref), custom_call_target="tpu_custom_call" | custom-call | tf_op jit(solution)/shard_map/last_scores/pallas_call | solution.py:527
  (19 shorter events, 0.3 us)
Async XLA Ops:
  2.1 10.5 %collective-permute-start = (bf16[1488,128]{1,0:T(8,128)(2,1)S(1)}, bf16[1488,128]{1,0:T(8,128)(2,1)S(1)}, u32[]{:S(2)}, u32[]{:S(2)}) collective-permute-start(bf16[1488,128]{1,0:T(8,128)(2,1)S(1)} %pack.1.refs_0_), channel_id=1, source_target_pairs={{0,4},{1,3},{4,8},{5,1},{8,12},{9,5},{12,14},{13,9},{14,10},{15,13... | collective-permute-start | bytes 1142792 | tf_op jit(solution)/shard_map/ppermute | solution.py:52
  7.9 6.0 %collective-permute-start.3 = (bf16[1488,128]{1,0:T(8,128)(2,1)S(1)}, bf16[1488,128]{1,0:T(8,128)(2,1)S(1)}, u32[]{:S(2)}, u32[]{:S(2)}) collective-permute-start(bf16[1488,128]{1,0:T(8,128)(2,1)S(1)} %pack.1.refs_0_), channel_id=1, source_target_pairs={{0,1},{1,0},{2,3},{3,2},{4,5},{5,4},{6,7},{7,6},{8,9},{9,8},{10,11... | collective-permute-start | bytes 1142792 | tf_op jit(solution)/shard_map/ppermute | solution.py:56
  8.0 7.1 %collective-permute-start.2 = (bf16[1488,128]{1,0:T(8,128)(2,1)S(1)}, bf16[1488,128]{1,0:T(8,128)(2,1)S(1)}, u32[]{:S(2)}, u32[]{:S(2)}) collective-permute-start(bf16[1488,128]{1,0:T(8,128)(2,1)S(1)} %pack.1.refs_0_), channel_id=1, source_target_pairs={{1,4},{0,3},{5,8},{4,1},{9,12},{8,5},{13,14},{12,9},{15,10},{14,13... | collective-permute-start | bytes 1142792 | tf_op jit(solution)/shard_map/ppermute | solution.py:52
  12.5 7.7 %collective-permute-start.1 = (bf16[1488,128]{1,0:T(8,128)(2,1)S(1)}, bf16[1488,128]{1,0:T(8,128)(2,1)S(1)}, u32[]{:S(2)}, u32[]{:S(2)}) collective-permute-start(bf16[1488,128]{1,0:T(8,128)(2,1)S(1)} %collective-permute-done.refs_0_.refs_2_), channel_id=1, source_target_pairs={{0,4},{1,3},{4,8},{5,1},{8,12},{9,5},{12,14},{13,9},{14,10},{15,13... | collective-permute-start | bytes 1142792 | tf_op jit(solution)/shard_map/ppermute | solution.py:52
  15.1 6.5 %collective-permute-start.7 = (bf16[1488,128]{1,0:T(8,128)(2,1)S(1)}, bf16[1488,128]{1,0:T(8,128)(2,1)S(1)}, u32[]{:S(2)}, u32[]{:S(2)}) collective-permute-start(bf16[1488,128]{1,0:T(8,128)(2,1)S(1)} %collective-permute-done.2.refs_1_.refs_4_), channel_id=1, source_target_pairs={{0,1},{1,0},{2,3},{3,2},{4,5},{5,4},{6,7},{7,6},{8,9},{9,8},{10,11... | collective-permute-start | bytes 1142792 | tf_op jit(solution)/shard_map/ppermute | solution.py:56
  15.6 6.0 %collective-permute-start.6 = (bf16[1488,128]{1,0:T(8,128)(2,1)S(1)}, bf16[1488,128]{1,0:T(8,128)(2,1)S(1)}, u32[]{:S(2)}, u32[]{:S(2)}) collective-permute-start(bf16[1488,128]{1,0:T(8,128)(2,1)S(1)} %collective-permute-done.refs_0_.refs_2_), channel_id=1, source_target_pairs={{0,1},{1,0},{2,3},{3,2},{4,5},{5,4},{6,7},{7,6},{8,9},{9,8},{10,11... | collective-permute-start | bytes 1142792 | tf_op jit(solution)/shard_map/ppermute | solution.py:56
  15.7 8.6 %collective-permute-start.5 = (bf16[1488,128]{1,0:T(8,128)(2,1)S(1)}, bf16[1488,128]{1,0:T(8,128)(2,1)S(1)}, u32[]{:S(2)}, u32[]{:S(2)}) collective-permute-start(bf16[1488,128]{1,0:T(8,128)(2,1)S(1)} %collective-permute-done.2.refs_1_.refs_4_), channel_id=1, source_target_pairs={{0,4},{1,3},{4,8},{5,1},{8,12},{9,5},{12,14},{13,9},{14,10},{15,13... | collective-permute-start | bytes 1142792 | tf_op jit(solution)/shard_map/ppermute | solution.py:52
  20.2 8.2 %collective-permute-start.4 = (bf16[1488,128]{1,0:T(8,128)(2,1)S(1)}, bf16[1488,128]{1,0:T(8,128)(2,1)S(1)}, u32[]{:S(2)}, u32[]{:S(2)}) collective-permute-start(bf16[1488,128]{1,0:T(8,128)(2,1)S(1)} %collective-permute-done.1.refs_0_.refs_6_), channel_id=1, source_target_pairs={{0,4},{1,3},{4,8},{5,1},{8,12},{9,5},{12,14},{13,9},{14,10},{15,13... | collective-permute-start | bytes 1142792 | tf_op jit(solution)/shard_map/ppermute | solution.py:52
  24.3 5.6 %collective-permute-start.12 = (bf16[1488,128]{1,0:T(8,128)(2,1)S(1)}, bf16[1488,128]{1,0:T(8,128)(2,1)S(1)}, u32[]{:S(2)}, u32[]{:S(2)}) collective-permute-start(bf16[1488,128]{1,0:T(8,128)(2,1)S(1)} %collective-permute-done.5.refs_1_.block_ref.refs_8_), channel_id=1, source_target_pairs={{0,1},{1,0},{2,3},{3,2},{4,5},{5,4},{6,7},{7,6},{8,9},{9,8},{10,11... | collective-permute-start | bytes 1142792 | tf_op jit(solution)/shard_map/ppermute | solution.py:56
  24.5 7.0 %collective-permute-start.11 = (bf16[1488,128]{1,0:T(8,128)(2,1)S(1)}, bf16[1488,128]{1,0:T(8,128)(2,1)S(1)}, u32[]{:S(2)}, u32[]{:S(2)}) collective-permute-start(bf16[1488,128]{1,0:T(8,128)(2,1)S(1)} %collective-permute-done.1.refs_0_.refs_6_), channel_id=1, source_target_pairs={{0,1},{1,0},{2,3},{3,2},{4,5},{5,4},{6,7},{7,6},{8,9},{9,8},{10,11... | collective-permute-start | bytes 1142792 | tf_op jit(solution)/shard_map/ppermute | solution.py:56
  24.8 7.4 %collective-permute-start.10 = (bf16[960,128]{1,0:T(8,128)(2,1)S(1)}, bf16[960,128]{1,0:T(8,128)(2,1)S(1)}, u32[]{:S(2)}, u32[]{:S(2)}) collective-permute-start(bf16[960,128]{1,0:T(8,128)(2,1)S(1)} %get-tuple-element.102), channel_id=1, source_target_pairs={{0,4},{1,3},{4,8},{5,1},{8,12},{9,5},{12,14},{13,9},{14,10},{15,13... | collective-permute-start | bytes 737288 | tf_op jit(solution)/shard_map/ppermute | solution.py:52
  28.4 6.2 %collective-permute-start.9 = (bf16[960,128]{1,0:T(8,128)(2,1)S(1)}, bf16[960,128]{1,0:T(8,128)(2,1)S(1)}, u32[]{:S(2)}, u32[]{:S(2)}) collective-permute-start(bf16[960,128]{1,0:T(8,128)(2,1)S(1)} %get-tuple-element.101), channel_id=1, source_target_pairs={{0,4},{1,3},{4,8},{5,1},{8,12},{9,5},{12,14},{13,9},{14,10},{15,13... | collective-permute-start | bytes 737288 | tf_op jit(solution)/shard_map/ppermute | solution.py:52
  29.9 4.8 %collective-permute-start.14 = (bf16[1488,128]{1,0:T(8,128)(2,1)S(1)}, bf16[1488,128]{1,0:T(8,128)(2,1)S(1)}, u32[]{:S(2)}, u32[]{:S(2)}) collective-permute-start(bf16[1488,128]{1,0:T(8,128)(2,1)S(1)} %collective-permute-done.4.block_ref.refs_0_.refs_10_), channel_id=1, source_target_pairs={{0,1},{1,0},{2,3},{3,2},{4,5},{5,4},{6,7},{7,6},{8,9},{9,8},{10,11... | collective-permute-start | bytes 1142792 | tf_op jit(solution)/shard_map/ppermute | solution.py:56
  29.9 8.8 %collective-permute-start.8 = (bf16[1056,128]{1,0:T(8,128)(2,1)S(1)}, bf16[1056,128]{1,0:T(8,128)(2,1)S(1)}, u32[]{:S(2)}, u32[]{:S(2)}) collective-permute-start(bf16[1056,128]{1,0:T(8,128)(2,1)S(1)} %get-tuple-element.100), channel_id=1, source_target_pairs={{0,4},{1,3},{4,8},{5,1},{8,12},{9,5},{12,14},{13,9},{14,10},{15,13... | collective-permute-start | bytes 811016 | tf_op jit(solution)/shard_map/ppermute | solution.py:52
  32.3 2.4 %collective-permute-start.15 = (bf16[960,128]{1,0:T(8,128)(2,1)S(1)}, bf16[960,128]{1,0:T(8,128)(2,1)S(1)}, u32[]{:S(2)}, u32[]{:S(2)}) collective-permute-start(bf16[960,128]{1,0:T(8,128)(2,1)S(1)} %collective-permute-done.10.refs_1_), channel_id=1, source_target_pairs={{0,1},{1,0},{2,3},{3,2},{4,5},{5,4},{6,7},{7,6},{8,9},{9,8},{10,11... | collective-permute-start | bytes 737288 | tf_op jit(solution)/shard_map/ppermute | solution.py:56
  34.7 1.5 %copy-start = (s32[1,2]{1,0:T(1,128)S(1)}, s32[1,2]{1,0:T(1,128)}, u32[]{:S(2)}) copy-start(s32[1,2]{1,0:T(1,128)} %counts_ref.1) | copy-start | bytes 28
  34.7 1.5 %collective-permute-start.13 = (bf16[960,128]{1,0:T(8,128)(2,1)S(1)}, bf16[960,128]{1,0:T(8,128)(2,1)S(1)}, u32[]{:S(2)}, u32[]{:S(2)}) collective-permute-start(bf16[960,128]{1,0:T(8,128)(2,1)S(1)} %collective-permute-done.9.refs_0_), channel_id=1, source_target_pairs={{0,1},{1,0},{2,3},{3,2},{4,5},{5,4},{6,7},{7,6},{8,9},{9,8},{10,11... | collective-permute-start | bytes 737288 | tf_op jit(solution)/shard_map/ppermute | solution.py:56
  38.7 1.6 %collective-permute-start.16 = (bf16[1056,128]{1,0:T(8,128)(2,1)S(1)}, bf16[1056,128]{1,0:T(8,128)(2,1)S(1)}, u32[]{:S(2)}, u32[]{:S(2)}) collective-permute-start(bf16[1056,128]{1,0:T(8,128)(2,1)S(1)} %collective-permute-done.8.refs_12_), channel_id=1, source_target_pairs={{0,1},{1,0},{2,3},{3,2},{4,5},{5,4},{6,7},{7,6},{8,9},{9,8},{10,11... | collective-permute-start | bytes 811016 | tf_op jit(solution)/shard_map/ppermute | solution.py:56

commit v13 on v9

--- a/solution.py
+++ b/solution.py
@@ -14,7 +14,7 @@
 RING_CHIPS = 8
 LANES = 128
 STEPS = 4
-X_DOWN, X_LOW, J_LOW, J_TARGET, M_DOWN, M_SOURCE, VALUES, V_TARGET, SUMS = range(9)
+VALUES, V_TARGET, X_DOWN, X_LOW, J_LOW, J_TARGET, M_DOWN, M_SOURCE, SUMS = range(9)
 INVERSE, LEFT_ONE, X_TARGET, LOCAL_SUMS = range(4)
 MIB = 1 << 20
 
@@ -189,16 +189,16 @@
     weights = both[...]
     down_up = weights[:, :LANES]
     lows = jnp.concatenate([weights[:, LANES:], target_ref[mine, :]], axis=1)
+    bridge = mm_cols(down_up, lows)
     products = []
     for activation, factor in (
+        (values_ref[:, values_part], up[...]),
         (x_ref[:, mine], weights),
         (adjoint_ref[:, mine], lows),
         (mixed_ref[:, mine], jnp.concatenate([down[...], source_ref[mine, :]], axis=1)),
-        (values_ref[:, values_part], up[...]),
     ):
         product = mm(activation, factor)
         products += [product[:, :LANES], product[:, LANES:]]
-    bridge = mm_cols(down_up, lows)
     if old:
         old_sums, old_bridge = old
         products = [p + old_sums[:, i * LANES : (i + 1) * LANES] for i, p in enumerate(products)]
@@ -226,24 +226,25 @@
     for copy in more:
         copy.wait()
     inverse = local[INVERSE]
+    returned = products[VALUES].astype(BF16)
+    back = mm(returned, jnp.concatenate([bridge.astype(BF16), sketch_ref[...]], axis=1))
+    right_one = ALPHA * back[:, 2 * LANES :]
     reduced = inverse * products[X_DOWN]
     expand = expand_ref[...]
     left_two = mm_rows(reduced.astype(BF16), jnp.concatenate([expand, expand], axis=0))
-    returned = products[VALUES].astype(BF16)
-    right_one = ALPHA * mm(returned, sketch_ref[...])
     along = (ALPHA / width) * jnp.sum(returned.astype(F32) * reduced, axis=1, keepdims=True)
-    back = mm(returned, bridge.astype(BF16))
     along = along * inverse
     right_three = products[J_LOW] + inverse * (ALPHA * back[:, :LANES] - along * products[X_LOW])
-    right_four = products[J_TARGET] + inverse * (ALPHA * back[:, LANES:] - along * local[X_TARGET])
+    right_four = products[J_TARGET] + inverse * (ALPHA * back[:, LANES : 2 * LANES] - along * local[X_TARGET])
     rights = (right_one, ALPHA * products[V_TARGET], ALPHA * right_three, ALPHA * right_four)
     lefts = (local[LEFT_ONE], left_two, products[M_SOURCE], products[M_DOWN])
     place = lax.broadcasted_iota(jnp.int32, (tokens, LANES), 0)
     one, two = counts_ref[0, 0], counts_ref[0, 1]
     lower = half_lanes((tokens, LANES))
     member = (place >= jnp.where(lower, 0, one)) & (place < jnp.where(lower, one, one + two))
-    spread = jnp.concatenate([jnp.where(member, left, 0.0).astype(BF16) for left in lefts], axis=0)
-    feats = mm_cols(spread, jnp.concatenate([right.astype(BF16) for right in rights], axis=0))
+    feats = jnp.zeros((LANES, LANES), F32)
+    for left, right in zip(lefts, rights):
+        feats = feats + mm_cols(jnp.where(member, left, 0.0).astype(BF16), right.astype(BF16))
     for e in range(2):
         own = feats[e * half : (e + 1) * half]
         squares = jnp.sum(own * own, keepdims=True)
@@ -304,11 +305,14 @@
 def last_score_kernel(count, unit_ref, block_ref, best_ref, out_ref, mean_ref):
     best = [[best_ref[e, t] for t in range(TASKS)] for e in range(2)]
     best_of(places_of([block_ref], count), count, unit_ref, best)
+    lane = lax.broadcasted_iota(jnp.int32, (1, LANES), 1)
+    means = []
     for e in range(2):
-        values = [jnp.max(best[e][t]) for t in range(TASKS)]
-        for t in range(TASKS):
-            out_ref[e, t] = values[t]
-        mean_ref[e] = (values[0] + values[1] + values[2]) * (1.0 / TASKS)
+        values = [jnp.max(best[e][t], axis=0, keepdims=True) for t in range(TASKS)]
+        row = jnp.where(lane == 0, values[0], jnp.where(lane == 1, values[1], values[2]))
+        out_ref[pl.ds(e, 1), :] = row[:, :TASKS]
+        means.append((values[0] + values[1] + values[2]) * (1.0 / TASKS))
+    mean_ref[...] = jnp.where(lane == 0, means[0], means[1])[:, :2]
 
 
 VMEM = pl.BlockSpec(memory_space=pltpu.VMEM)
@@ -461,6 +465,7 @@
             blocks += [second, crossed[1]]
         else:
             first, tails = split(first, tail)
+            tails, sums = tie((tails, sums))
         first = hop(first)
         sums = stage(k, held, sums)
         first, sums = tie((first, sums))
@@ -507,13 +512,13 @@
     )(unit, *blocks)
     task_best, scores = pl.pallas_call(
         functools.partial(last_score_kernel, count),
-        out_shape=(jax.ShapeDtypeStruct((2, TASKS), F32), jax.ShapeDtypeStruct((2,), F32)),
+        out_shape=(jax.ShapeDtypeStruct((2, TASKS), F32), jax.ShapeDtypeStruct((1, 2), F32)),
         in_specs=[VMEM] * 3,
-        out_specs=(SMEM, SMEM),
+        out_specs=(VMEM, VMEM),
         compiler_params=params(8),
         name="last_scores",
     )(unit, other_core(tails), best)
-    return (scores, task_best)
+    return (scores.reshape(2), task_best)
 
 
 def shards_of_any_slice(

time: 40.4 us -> 40 us (0.990)
  Pallas kernels: 15.9 us -> 15.1 us
  transfers between devices with their start and end apart: 17 -> 17, of which waited for: 7 -> 7; matrix products, arithmetic and copies ran while one was open for 0% -> 0% of each run, Pallas kernels for 34% -> 33%
where the time goes in v13:
time: 40 us; the launch traced here: 39.7 us
  starting transfers between devices  16.1 us (40%)
  Pallas kernels  15.1 us (38%)
  waiting for transfers between devices  7.63 us (19%)
  between operations  0.78 us (2%)
    ppermute x8, starting transfers between devices, hop(): return lax.ppermute(value, 'dp', pairs)  15.4 us
    ppermute x8, waiting for transfers between devices, hop(): return lax.ppermute(value, 'dp', pairs)  6.36 us
    pallas_call x7, Pallas kernels, stage(): pl.pallas_call(functools.partial(stage_kernel, away, first), out_shape=[j...  5.29 us
    pallas_call x1, Pallas kernels, shards(): pl.pallas_call(local_kernel, out_shape=[jax.ShapeDtypeStruct(a.shape, a.d...  4.6 us
    pallas_call x1, Pallas kernels, shards(): pl.pallas_call(functools.partial(feature_kernel, half), out_shape=jax.Sha...  2.16 us
    pallas_call x1, Pallas kernels, shards(): pl.pallas_call(pack_kernel, out_shape=jax.ShapeDtypeStruct((3 * rows + (L...  1.41 us
    ppermute x9, waiting for transfers between devices, other_core(): lax.ppermute(value, 'dp', [(d, d ^ 1) for d in range(2 * RING_CHIPS)])  1.27 us
    pallas_call x1, Pallas kernels, shards(): pl.pallas_call(functools.partial(score_kernel, len(blocks), count), out_s...  0.87 us
  transfers between devices with their start and end apart: 17, of which 7 were waited for; matrix products, arithmetic and copies ran while one was open for 0% of the time, Pallas kernels for 33%

profile of v13, /device:TPU:0, one launch (start us, length us, event | category | flops | bytes accessed | tf_op | source)
XLA Modules:
  0.0 39.7 jit_solution(3326221023762671828)
XLA Ops:
  0.6 1.4 %pack.1.refs_0_ = bf16[1488,128]{1,0:T(8,128)(2,1)S(1)} custom-call(s32[1]{0:T(128)} %bitcast.me_ref, f32[40,128]{1,0:T(8,128)} %bitcast.11, bf16[320,128]{1,0:T(8,128)(2,1)} %refs_1_.2, bf16[320,128]{1,0:T(8,128)(2,1)} %bitcast.13, bf16[128,128]{1,0:T(8,128)(2,1)} %refs_3_.2, bf16[160,128]{1,0:T(8,128)(2,1)} %bitcast.14, bf16[320,128]{1,0:T(8,128)(2,1)} %refs_5_.2, ...), custom_call_target="tpu_custom_call" | custom-call | tf_op jit(solution)/shard_map/pack/pallas_call | solution.py:379
  2.1 0.5 %collective-permute-start.2 = (bf16[1488,128]{1,0:T(8,128)(2,1)S(1)}, bf16[1488,128]{1,0:T(8,128)(2,1)S(1)}, u32[]{:S(2)}, u32[]{:S(2)}) collective-permute-start(bf16[1488,128]{1,0:T(8,128)(2,1)S(1)} %pack.1.refs_0_), channel_id=1, source_target_pairs={{0,1},{1,0},{2,3},{3,2},{4,5},{5,4},{6,7},{7,6},{8,9},{9,8},{10,11... | collective-permute-start | bytes 1142792 | tf_op jit(solution)/shard_map/ppermute | solution.py:55
  2.6 2.6 %collective-permute-start = (bf16[1488,128]{1,0:T(8,128)(2,1)S(1)}, bf16[1488,128]{1,0:T(8,128)(2,1)S(1)}, u32[]{:S(2)}, u32[]{:S(2)}) collective-permute-start(bf16[1488,128]{1,0:T(8,128)(2,1)S(1)} %pack.1.refs_0_), channel_id=1, source_target_pairs={{0,4},{1,3},{4,8},{5,1},{8,12},{9,5},{12,14},{13,9},{14,10},{15,13... | collective-permute-start | bytes 1142792 | tf_op jit(solution)/shard_map/ppermute | solution.py:51
  5.2 1.6 %collective-permute-start.3 = (bf16[1488,128]{1,0:T(8,128)(2,1)S(1)}, bf16[1488,128]{1,0:T(8,128)(2,1)S(1)}, u32[]{:S(2)}, u32[]{:S(2)}) collective-permute-start(bf16[1488,128]{1,0:T(8,128)(2,1)S(1)} %collective-permute-done.2.refs_1_), channel_id=1, source_target_pairs={{0,4},{1,3},{4,8},{5,1},{8,12},{9,5},{12,14},{13,9},{14,10},{15,13... | collective-permute-start | bytes 1142792 | tf_op jit(solution)/shard_map/ppermute | solution.py:51
  6.8 4.6 %local_products.1 = (bf16[256,5120]{1,0:T(8,128)(2,1)S(1)}, bf16[256,5120]{1,0:T(8,128)(2,1)S(1)}, bf16[256,5120]{1,0:T(8,128)(2,1)S(1)}, bf16[256,2560]{1,0:T(8...) custom-call(bf16[256,5120]{1,0:T(8,128)(2,1)} %refs_0_.1, ...), custom_call_target="tpu_custom_call" | custom-call | flops 1006632960 | bytes 14680064 | tf_op jit(solution)/shard_map/local_products/pallas_call | solution.py:400
  11.5 0.0 collective-permute-done.refs_0_.refs_2_
  11.5 1.6 %collective-permute-start.1 = (bf16[1488,128]{1,0:T(8,128)(2,1)S(1)}, bf16[1488,128]{1,0:T(8,128)(2,1)S(1)}, u32[]{:S(2)}, u32[]{:S(2)}) collective-permute-start(bf16[1488,128]{1,0:T(8,128)(2,1)S(1)} %collective-permute-done.refs_0_.refs_2_), channel_id=1, source_target_pairs={{0,4},{1,3},{4,8},{5,1},{8,12},{9,5},{12,14},{13,9},{14,10},{15,13... | collective-permute-start | bytes 1142792 | tf_op jit(solution)/shard_map/ppermute | solution.py:51
  13.1 0.7 %stage.7 = (f32[256,1024]{1,0:T(8,128)S(1)}, f32[128,256]{1,0:T(8,128)S(1)}) custom-call(s32[1]{0:T(128)} %bitcast.me_ref, bf16[1488,128]{1,0:T(8,128)(2,1)S(1)} %pack.1.refs_0_, bf16[1488,128]{1,0:T(8,128)(2,1)S(1)} %collective-permute-done.2.refs_1_, bf16[256,5120]{1,0:T(8,128)(2,1)S(1)} %get-tuple-element.69.refs_2_, ...), custom_call_target="tpu_custom_call" | custom-call | flops 167772160 | bytes 2097152 | tf_op jit(solution)/shard_map/stage/pallas_call | solution.py:425
  13.8 1.1 %collective-permute-done.3.refs_1_.refs_4_ = bf16[1488,128]{1,0:T(8,128)(2,1)S(1)} collective-permute-done((bf16[1488,128]{1,0:T(8,128)(2,1)S(1)}, bf16[1488,128]{1,0:T(8,128)(2,1)S(1)}, u32[]{:S(2)}, u32[]{:S(2)}) %collective-permute-start.3) | collective-permute-done | bytes 380960 | tf_op jit(solution)/shard_map/ppermute | solution.py:51
  14.9 0.0 collective-permute-start.7
  14.9 2.1 %collective-permute-start.5 = (bf16[1488,128]{1,0:T(8,128)(2,1)S(1)}, bf16[1488,128]{1,0:T(8,128)(2,1)S(1)}, u32[]{:S(2)}, u32[]{:S(2)}) collective-permute-start(bf16[1488,128]{1,0:T(8,128)(2,1)S(1)} %collective-permute-done.3.refs_1_.refs_4_), channel_id=1, source_target_pairs={{0,4},{1,3},{4,8},{5,1},{8,12},{9,5},{12,14},{13,9},{14,10},{15,13... | collective-permute-start | bytes 1142792 | tf_op jit(solution)/shard_map/ppermute | solution.py:51
  16.9 0.8 %stage.8 = (f32[256,1024]{1,0:T(8,128)S(1)}, f32[128,256]{1,0:T(8,128)S(1)}) custom-call(s32[1]{0:T(128)} %bitcast.me_ref, bf16[1488,128]{1,0:T(8,128)(2,1)S(1)} %collective-permute-done.refs_0_.refs_2_, bf16[1488,128]{1,0:T(8,128)(2,1)S(1)} %collective-permute-done.3.refs_1_.refs_4_, ...), custom_call_target="tpu_custom_call", output_to_operand_aliasing={{0}: (10, {}), {1}: (11, {})} | custom-call | flops 167772160 | bytes 2097152 | tf_op jit(solution)/shard_map/stage/pallas_call | solution.py:425
  17.7 1.4 %collective-permute-done.1.refs_0_.refs_6_ = bf16[1488,128]{1,0:T(8,128)(2,1)S(1)} collective-permute-done((bf16[1488,128]{1,0:T(8,128)(2,1)S(1)}, bf16[1488,128]{1,0:T(8,128)(2,1)S(1)}, u32[]{:S(2)}, u32[]{:S(2)}) %collective-permute-start.1) | collective-permute-done | bytes 380960 | tf_op jit(solution)/shard_map/ppermute | solution.py:51
  19.2 1.9 %collective-permute-start.4 = (bf16[1488,128]{1,0:T(8,128)(2,1)S(1)}, bf16[1488,128]{1,0:T(8,128)(2,1)S(1)}, u32[]{:S(2)}, u32[]{:S(2)}) collective-permute-start(bf16[1488,128]{1,0:T(8,128)(2,1)S(1)} %collective-permute-done.1.refs_0_.refs_6_), channel_id=1, source_target_pairs={{0,4},{1,3},{4,8},{5,1},{8,12},{9,5},{12,14},{13,9},{14,10},{15,13... | collective-permute-start | bytes 1142792 | tf_op jit(solution)/shard_map/ppermute | solution.py:51
  21.0 0.0 collective-permute-start.9
  21.0 0.8 %stage.9 = (f32[256,1024]{1,0:T(8,128)S(1)}, f32[128,256]{1,0:T(8,128)S(1)}) custom-call(s32[1]{0:T(128)} %bitcast.me_ref, bf16[1488,128]{1,0:T(8,128)(2,1)S(1)} %collective-permute-done.6.refs_0_.refs_3_, bf16[1488,128]{1,0:T(8,128)(2,1)S(1)} %collective-permute-done.7.refs_1_.refs_5_, ...), custom_call_target="tpu_custom_call", output_to_operand_aliasing={{0}: (10, {}), {1}: (11, {})} | custom-call | flops 167772160 | bytes 2097152 | tf_op jit(solution)/shard_map/stage/pallas_call | solution.py:425
  21.8 1.4 %collective-permute-done.5.refs_1_.block_ref.refs_8_ = bf16[1488,128]{1,0:T(8,128)(2,1)S(1)} collective-permute-done((bf16[1488,128]{1,0:T(8,128)(2,1)S(1)}, bf16[1488,128]{1,0:T(8,128)(2,1)S(1)}, u32[]{:S(2)}, u32[]{:S(2)}) %collective-permute-start.5) | collective-permute-done | bytes 380960 | tf_op jit(solution)/shard_map/ppermute | solution.py:51
  23.3 1.9 %collective-permute-start.8 = (bf16[960,128]{1,0:T(8,128)(2,1)S(1)}, bf16[960,128]{1,0:T(8,128)(2,1)S(1)}, u32[]{:S(2)}, u32[]{:S(2)}) collective-permute-start(bf16[960,128]{1,0:T(8,128)(2,1)S(1)} %get-tuple-element.96), channel_id=1, source_target_pairs={{0,4},{1,3},{4,8},{5,1},{8,12},{9,5},{12,14},{13,9},{14,10},{15,13... | collective-permute-start | bytes 737288 | tf_op jit(solution)/shard_map/ppermute | solution.py:51
  25.2 0.8 %stage.10 = (f32[256,1024]{1,0:T(8,128)S(1)}, f32[128,256]{1,0:T(8,128)S(1)}) custom-call(s32[1]{0:T(128)} %bitcast.me_ref, bf16[1488,128]{1,0:T(8,128)(2,1)S(1)} %collective-permute-done.1.refs_0_.refs_6_, bf16[1488,128]{1,0:T(8,128)(2,1)S(1)} %collective-permute-done.5.refs_1_.block_ref.refs_8_, ...), custom_call_target="tpu_custom_call", output_to_operand_aliasing={{0}: (10, {}), {1}: (11, {})} | custom-call | flops 167772160 | bytes 2097152 | tf_op jit(solution)/shard_map/stage/pallas_call | solution.py:425
  26.0 1.4 %collective-permute-done.4.block_ref.refs_0_.refs_10_ = bf16[1488,128]{1,0:T(8,128)(2,1)S(1)} collective-permute-done((bf16[1488,128]{1,0:T(8,128)(2,1)S(1)}, bf16[1488,128]{1,0:T(8,128)(2,1)S(1)}, u32[]{:S(2)}, u32[]{:S(2)}) %collective-permute-start.4) | collective-permute-done | bytes 380960 | tf_op jit(solution)/shard_map/ppermute | solution.py:51
  27.4 1.9 %collective-permute-start.12 = (bf16[960,128]{1,0:T(8,128)(2,1)S(1)}, bf16[960,128]{1,0:T(8,128)(2,1)S(1)}, u32[]{:S(2)}, u32[]{:S(2)}) collective-permute-start(bf16[960,128]{1,0:T(8,128)(2,1)S(1)} %get-tuple-element.104), channel_id=1, source_target_pairs={{0,4},{1,3},{4,8},{5,1},{8,12},{9,5},{12,14},{13,9},{14,10},{15,13... | collective-permute-start | bytes 737288 | tf_op jit(solution)/shard_map/ppermute | solution.py:51
  29.3 0.8 %stage.11 = (f32[256,1024]{1,0:T(8,128)S(1)}, f32[128,256]{1,0:T(8,128)S(1)}) custom-call(s32[1]{0:T(128)} %bitcast.me_ref, bf16[1488,128]{1,0:T(8,128)(2,1)S(1)} %collective-permute-done.9.refs_0_.refs_7_, bf16[1488,128]{1,0:T(8,128)(2,1)S(1)} %collective-permute-done.10.refs_1_.refs_9_, ...), custom_call_target="tpu_custom_call", output_to_operand_aliasing={{0}: (10, {}), {1}: (11, {})} | custom-call | flops 167772160 | bytes 2097152 | tf_op jit(solution)/shard_map/stage/pallas_call | solution.py:425
  30.1 1.7 %collective-permute-start.11 = (bf16[1056,128]{1,0:T(8,128)(2,1)S(1)}, bf16[1056,128]{1,0:T(8,128)(2,1)S(1)}, u32[]{:S(2)}, u32[]{:S(2)}) collective-permute-start(bf16[1056,128]{1,0:T(8,128)(2,1)S(1)} %get-tuple-element.103), channel_id=1, source_target_pairs={{0,4},{1,3},{4,8},{5,1},{8,12},{9,5},{12,14},{13,9},{14,10},{15,13... | collective-permute-start | bytes 811016 | tf_op jit(solution)/shard_map/ppermute | solution.py:51
  31.8 0.8 %stage.12 = (f32[256,1024]{1,0:T(8,128)S(1)}, f32[128,256]{1,0:T(8,128)S(1)}) custom-call(s32[1]{0:T(128)} %bitcast.me_ref, bf16[1488,128]{1,0:T(8,128)(2,1)S(1)} %collective-permute-done.4.block_ref.refs_0_.refs_10_, bf16[960,128]{1,0:T(8,128)(2,1)S(1)} %collective-permute-done.8.refs_1_, ...), custom_call_target="tpu_custom_call", output_to_operand_aliasing={{0}: (10, {}), {1}: (11, {})} | custom-call | flops 167772160 | bytes 2097152 | tf_op jit(solution)/shard_map/stage/pallas_call | solution.py:425
  32.6 1.0 %collective-permute-done.12.refs_0_ = bf16[960,128]{1,0:T(8,128)(2,1)S(1)} collective-permute-done((bf16[960,128]{1,0:T(8,128)(2,1)S(1)}, bf16[960,128]{1,0:T(8,128)(2,1)S(1)}, u32[]{:S(2)}, u32[]{:S(2)}) %collective-permute-start.12) | collective-permute-done | bytes 245792 | tf_op jit(solution)/shard_map/ppermute | solution.py:51
  33.6 0.8 %stage.13 = (f32[256,1024]{1,0:T(8,128)S(1)}, f32[128,256]{1,0:T(8,128)S(1)}) custom-call(s32[1]{0:T(128)} %bitcast.me_ref, bf16[1488,128]{1,0:T(8,128)(2,1)S(1)} %collective-permute-done.14.refs_0_.refs_11_, bf16[960,128]{1,0:T(8,128)(2,1)S(1)} %collective-permute-done.15.refs_1_, ...), custom_call_target="tpu_custom_call", output_to_operand_aliasing={{0}: (10, {}), {1}: (11, {})} | custom-call | flops 167772160 | bytes 2097152 | tf_op jit(solution)/shard_map/stage/pallas_call | solution.py:425
  34.4 0.7 %collective-permute-done.13.refs_1_ = bf16[960,128]{1,0:T(8,128)(2,1)S(1)} collective-permute-done((bf16[960,128]{1,0:T(8,128)(2,1)S(1)}, bf16[960,128]{1,0:T(8,128)(2,1)S(1)}, u32[]{:S(2)}, u32[]{:S(2)}) %collective-permute-start.13) | collective-permute-done | bytes 245792 | tf_op jit(solution)/shard_map/ppermute | solution.py:55
  35.1 2.2 %features.1.unit_ref = f32[128,128]{1,0:T(8,128)S(1)} custom-call(s32[1]{0:T(128)} %bitcast.me_ref, s32[1,2]{1,0:T(1,128)S(1)} %copy-done, bf16[960,128]{1,0:T(8,128)(2,1)S(1)} %collective-permute-done.12.refs_0_, bf16[960,128]{1,0:T(8,128)(2,1)S(1)} %collective-permute-done.13.refs_1_, bf16[256,5120]{1,0:T(8,128)(2,1)S(1)} %get-tuple-element.69.refs_2_, ...), custom_call_target="tpu_custom_call" | custom-call | flops 1 | bytes 1 | tf_op jit(solution)/shard_map/features/pallas_call | solution.py:481
  37.3 0.2 collective-permute-start.16
  37.5 0.9 %scores.1.best_ref = f32[2,3,8,128]{3,2,1,0:T(8,128)S(1)} custom-call(f32[128,128]{1,0:T(8,128)S(1)} %features.1.unit_ref, bf16[1488,128]{1,0:T(8,128)(2,1)S(1)} %pack.1.refs_0_, bf16[1488,128]{1,0:T(8,128)(2,1)S(1)} %collective-permute-done.2.refs_1_, bf16[1488,128]{1,0:T(8,128)(2,1)S(1)} %collective-permute-done.refs_0_.refs_2_, ...), custom_call_target="tpu_custom_call" | custom-call | flops 4194304 | bytes 2097152 | tf_op jit(solution)/shard_map/scores/pallas_call | solution.py:504
  38.4 0.5 %collective-permute-done.16.block_ref = bf16[1056,128]{1,0:T(8,128)(2,1)S(1)} collective-permute-done((bf16[1056,128]{1,0:T(8,128)(2,1)S(1)}, bf16[1056,128]{1,0:T(8,128)(2,1)S(1)}, u32[]{:S(2)}, u32[]{:S(2)}) %collective-permute-start.16) | collective-permute-done | bytes 270368 | tf_op jit(solution)/shard_map/ppermute | solution.py:55
  38.9 0.8 %last_scores.1 = (f32[2,3]{1,0:T(2,128)}, f32[1,2]{1,0:T(1,128)}) custom-call(f32[128,128]{1,0:T(8,128)S(1)} %features.1.unit_ref, bf16[1056,128]{1,0:T(8,128)(2,1)S(1)} %collective-permute-done.16.block_ref, f32[2,3,8,128]{3,2,1,0:T(8,128)S(1)} %scores.1.best_ref), custom_call_target="tpu_custom_call" | custom-call | tf_op jit(solution)/shard_map/last_scores/pallas_call | solution.py:513
  (18 shorter events, 0.1 us)
Async XLA Ops:
  2.1 3.2 %collective-permute-start.2 = (bf16[1488,128]{1,0:T(8,128)(2,1)S(1)}, bf16[1488,128]{1,0:T(8,128)(2,1)S(1)}, u32[]{:S(2)}, u32[]{:S(2)}) collective-permute-start(bf16[1488,128]{1,0:T(8,128)(2,1)S(1)} %pack.1.refs_0_), channel_id=1, source_target_pairs={{0,1},{1,0},{2,3},{3,2},{4,5},{5,4},{6,7},{7,6},{8,9},{9,8},{10,11... | collective-permute-start | bytes 1142792 | tf_op jit(solution)/shard_map/ppermute | solution.py:55
  2.6 8.9 %collective-permute-start = (bf16[1488,128]{1,0:T(8,128)(2,1)S(1)}, bf16[1488,128]{1,0:T(8,128)(2,1)S(1)}, u32[]{:S(2)}, u32[]{:S(2)}) collective-permute-start(bf16[1488,128]{1,0:T(8,128)(2,1)S(1)} %pack.1.refs_0_), channel_id=1, source_target_pairs={{0,4},{1,3},{4,8},{5,1},{8,12},{9,5},{12,14},{13,9},{14,10},{15,13... | collective-permute-start | bytes 1142792 | tf_op jit(solution)/shard_map/ppermute | solution.py:51
  5.2 9.6 %collective-permute-start.3 = (bf16[1488,128]{1,0:T(8,128)(2,1)S(1)}, bf16[1488,128]{1,0:T(8,128)(2,1)S(1)}, u32[]{:S(2)}, u32[]{:S(2)}) collective-permute-start(bf16[1488,128]{1,0:T(8,128)(2,1)S(1)} %collective-permute-done.2.refs_1_), channel_id=1, source_target_pairs={{0,4},{1,3},{4,8},{5,1},{8,12},{9,5},{12,14},{13,9},{14,10},{15,13... | collective-permute-start | bytes 1142792 | tf_op jit(solution)/shard_map/ppermute | solution.py:51
  11.5 7.7 %collective-permute-start.1 = (bf16[1488,128]{1,0:T(8,128)(2,1)S(1)}, bf16[1488,128]{1,0:T(8,128)(2,1)S(1)}, u32[]{:S(2)}, u32[]{:S(2)}) collective-permute-start(bf16[1488,128]{1,0:T(8,128)(2,1)S(1)} %collective-permute-done.refs_0_.refs_2_), channel_id=1, source_target_pairs={{0,4},{1,3},{4,8},{5,1},{8,12},{9,5},{12,14},{13,9},{14,10},{15,13... | collective-permute-start | bytes 1142792 | tf_op jit(solution)/shard_map/ppermute | solution.py:51
  13.1 7.9 %collective-permute-start.6 = (bf16[1488,128]{1,0:T(8,128)(2,1)S(1)}, bf16[1488,128]{1,0:T(8,128)(2,1)S(1)}, u32[]{:S(2)}, u32[]{:S(2)}) collective-permute-start(bf16[1488,128]{1,0:T(8,128)(2,1)S(1)} %collective-permute-done.refs_0_.refs_2_), channel_id=1, source_target_pairs={{0,1},{1,0},{2,3},{3,2},{4,5},{5,4},{6,7},{7,6},{8,9},{9,8},{10,11... | collective-permute-start | bytes 1142792 | tf_op jit(solution)/shard_map/ppermute | solution.py:55
  14.9 6.2 %collective-permute-start.7 = (bf16[1488,128]{1,0:T(8,128)(2,1)S(1)}, bf16[1488,128]{1,0:T(8,128)(2,1)S(1)}, u32[]{:S(2)}, u32[]{:S(2)}) collective-permute-start(bf16[1488,128]{1,0:T(8,128)(2,1)S(1)} %collective-permute-done.3.refs_1_.refs_4_), channel_id=1, source_target_pairs={{0,1},{1,0},{2,3},{3,2},{4,5},{5,4},{6,7},{7,6},{8,9},{9,8},{10,11... | collective-permute-start | bytes 1142792 | tf_op jit(solution)/shard_map/ppermute | solution.py:55
  14.9 8.4 %collective-permute-start.5 = (bf16[1488,128]{1,0:T(8,128)(2,1)S(1)}, bf16[1488,128]{1,0:T(8,128)(2,1)S(1)}, u32[]{:S(2)}, u32[]{:S(2)}) collective-permute-start(bf16[1488,128]{1,0:T(8,128)(2,1)S(1)} %collective-permute-done.3.refs_1_.refs_4_), channel_id=1, source_target_pairs={{0,4},{1,3},{4,8},{5,1},{8,12},{9,5},{12,14},{13,9},{14,10},{15,13... | collective-permute-start | bytes 1142792 | tf_op jit(solution)/shard_map/ppermute | solution.py:51
  19.2 8.2 %collective-permute-start.4 = (bf16[1488,128]{1,0:T(8,128)(2,1)S(1)}, bf16[1488,128]{1,0:T(8,128)(2,1)S(1)}, u32[]{:S(2)}, u32[]{:S(2)}) collective-permute-start(bf16[1488,128]{1,0:T(8,128)(2,1)S(1)} %collective-permute-done.1.refs_0_.refs_6_), channel_id=1, source_target_pairs={{0,4},{1,3},{4,8},{5,1},{8,12},{9,5},{12,14},{13,9},{14,10},{15,13... | collective-permute-start | bytes 1142792 | tf_op jit(solution)/shard_map/ppermute | solution.py:51
  21.0 8.3 %collective-permute-start.9 = (bf16[1488,128]{1,0:T(8,128)(2,1)S(1)}, bf16[1488,128]{1,0:T(8,128)(2,1)S(1)}, u32[]{:S(2)}, u32[]{:S(2)}) collective-permute-start(bf16[1488,128]{1,0:T(8,128)(2,1)S(1)} %collective-permute-done.1.refs_0_.refs_6_), channel_id=1, source_target_pairs={{0,1},{1,0},{2,3},{3,2},{4,5},{5,4},{6,7},{7,6},{8,9},{9,8},{10,11... | collective-permute-start | bytes 1142792 | tf_op jit(solution)/shard_map/ppermute | solution.py:55
  23.2 6.0 %collective-permute-start.10 = (bf16[1488,128]{1,0:T(8,128)(2,1)S(1)}, bf16[1488,128]{1,0:T(8,128)(2,1)S(1)}, u32[]{:S(2)}, u32[]{:S(2)}) collective-permute-start(bf16[1488,128]{1,0:T(8,128)(2,1)S(1)} %collective-permute-done.5.refs_1_.block_ref.refs_8_), channel_id=1, source_target_pairs={{0,1},{1,0},{2,3},{3,2},{4,5},{5,4},{6,7},{7,6},{8,9},{9,8},{10,11... | collective-permute-start | bytes 1142792 | tf_op jit(solution)/shard_map/ppermute | solution.py:55
  23.3 6.8 %collective-permute-start.8 = (bf16[960,128]{1,0:T(8,128)(2,1)S(1)}, bf16[960,128]{1,0:T(8,128)(2,1)S(1)}, u32[]{:S(2)}, u32[]{:S(2)}) collective-permute-start(bf16[960,128]{1,0:T(8,128)(2,1)S(1)} %get-tuple-element.96), channel_id=1, source_target_pairs={{0,4},{1,3},{4,8},{5,1},{8,12},{9,5},{12,14},{13,9},{14,10},{15,13... | collective-permute-start | bytes 737288 | tf_op jit(solution)/shard_map/ppermute | solution.py:51
  27.4 6.2 %collective-permute-start.12 = (bf16[960,128]{1,0:T(8,128)(2,1)S(1)}, bf16[960,128]{1,0:T(8,128)(2,1)S(1)}, u32[]{:S(2)}, u32[]{:S(2)}) collective-permute-start(bf16[960,128]{1,0:T(8,128)(2,1)S(1)} %get-tuple-element.104), channel_id=1, source_target_pairs={{0,4},{1,3},{4,8},{5,1},{8,12},{9,5},{12,14},{13,9},{14,10},{15,13... | collective-permute-start | bytes 737288 | tf_op jit(solution)/shard_map/ppermute | solution.py:51
  29.3 4.4 %collective-permute-start.14 = (bf16[1488,128]{1,0:T(8,128)(2,1)S(1)}, bf16[1488,128]{1,0:T(8,128)(2,1)S(1)}, u32[]{:S(2)}, u32[]{:S(2)}) collective-permute-start(bf16[1488,128]{1,0:T(8,128)(2,1)S(1)} %collective-permute-done.4.block_ref.refs_0_.refs_10_), channel_id=1, source_target_pairs={{0,1},{1,0},{2,3},{3,2},{4,5},{5,4},{6,7},{7,6},{8,9},{9,8},{10,11... | collective-permute-start | bytes 1142792 | tf_op jit(solution)/shard_map/ppermute | solution.py:55
  30.1 7.2 %collective-permute-start.11 = (bf16[1056,128]{1,0:T(8,128)(2,1)S(1)}, bf16[1056,128]{1,0:T(8,128)(2,1)S(1)}, u32[]{:S(2)}, u32[]{:S(2)}) collective-permute-start(bf16[1056,128]{1,0:T(8,128)(2,1)S(1)} %get-tuple-element.103), channel_id=1, source_target_pairs={{0,4},{1,3},{4,8},{5,1},{8,12},{9,5},{12,14},{13,9},{14,10},{15,13... | collective-permute-start | bytes 811016 | tf_op jit(solution)/shard_map/ppermute | solution.py:51
  31.8 1.8 %collective-permute-start.15 = (bf16[960,128]{1,0:T(8,128)(2,1)S(1)}, bf16[960,128]{1,0:T(8,128)(2,1)S(1)}, u32[]{:S(2)}, u32[]{:S(2)}) collective-permute-start(bf16[960,128]{1,0:T(8,128)(2,1)S(1)} %collective-permute-done.8.refs_1_), channel_id=1, source_target_pairs={{0,1},{1,0},{2,3},{3,2},{4,5},{5,4},{6,7},{7,6},{8,9},{9,8},{10,11... | collective-permute-start | bytes 737288 | tf_op jit(solution)/shard_map/ppermute | solution.py:55
  33.6 1.5 %copy-start = (s32[1,2]{1,0:T(1,128)S(1)}, s32[1,2]{1,0:T(1,128)}, u32[]{:S(2)}) copy-start(s32[1,2]{1,0:T(1,128)} %counts_ref.1) | copy-start | bytes 28
  33.6 1.5 %collective-permute-start.13 = (bf16[960,128]{1,0:T(8,128)(2,1)S(1)}, bf16[960,128]{1,0:T(8,128)(2,1)S(1)}, u32[]{:S(2)}, u32[]{:S(2)}) collective-permute-start(bf16[960,128]{1,0:T(8,128)(2,1)S(1)} %collective-permute-done.12.refs_0_), channel_id=1, source_target_pairs={{0,1},{1,0},{2,3},{3,2},{4,5},{5,4},{6,7},{7,6},{8,9},{9,8},{10,11... | collective-permute-start | bytes 737288 | tf_op jit(solution)/shard_map/ppermute | solution.py:55
  37.3 1.6 %collective-permute-start.16 = (bf16[1056,128]{1,0:T(8,128)(2,1)S(1)}, bf16[1056,128]{1,0:T(8,128)(2,1)S(1)}, u32[]{:S(2)}, u32[]{:S(2)}) collective-permute-start(bf16[1056,128]{1,0:T(8,128)(2,1)S(1)} %collective-permute-done.11.refs_12_), channel_id=1, source_target_pairs={{0,1},{1,0},{2,3},{3,2},{4,5},{5,4},{6,7},{7,6},{8,9},{9,8},{10,11... | collective-permute-start | bytes 811016 | tf_op jit(solution)/shard_map/ppermute | solution.py:55

commit v14 on v13

--- a/solution.py
+++ b/solution.py
@@ -74,12 +74,12 @@
 
 
 def pack_kernel(me_ref, *refs):
-    hbm, out_ref, held, sems = refs[:9], refs[9], refs[10:19], refs[19]
-    gain_ref, down_up_ref, up_low_ref, sketch_ref, up_up_ref, down_low_ref, expand_ref, val_ref, label_ref = held
-    copies = load(zip(hbm, held), sems)
+    up_up_hbm, hbm, out_ref, held, sems = refs[0], refs[1:9], refs[9], refs[10:18], refs[18]
+    val_ref, down_up_ref, up_low_ref, down_low_ref, gain_ref, sketch_ref, expand_ref, label_ref = held
     rows = down_up_ref.shape[0]
     half = LANES // 2
-    for copy in copies:
+    direct = (up_up_hbm, out_ref.at[pl.ds(2 * rows, rows // 2)])
+    for copy in load((*zip(hbm, held), direct), sems):
         copy.wait()
     for b in range(rows // half):
         place = me_ref[0] * (rows // half) + b
@@ -89,9 +89,7 @@
         out_ref[pl.ds(b * half, half), :] = (column * part).astype(BF16)
     at = rows
     out_ref[pl.ds(at, rows), :] = mm(up_low_ref[...], sketch_ref[...]).astype(BF16)
-    at += rows
-    out_ref[pl.ds(at, rows // 2), :] = up_up_ref[...]
-    at += rows // 2
+    at += rows + rows // 2
     expand = expand_ref[...]
     low = mm_rows(down_low_ref[...], jnp.concatenate([expand, expand], axis=0))
     first, second = low[: rows // 2], low[rows // 2 :]
@@ -366,14 +364,14 @@
     count = heldout_sketched_signals.shape[0]
 
     inputs = (
-        top_rmsnorm_weights.reshape(width // LANES, LANES),
+        top_expander_matrix.T,
+        heldout_sketched_signals,
         top_reducer_matrix,
         bottom_expander_matrix.T,
+        bottom_reducer_matrix,
+        top_rmsnorm_weights.reshape(width // LANES, LANES),
         bottom_reducer_sketch,
-        top_expander_matrix.T,
-        bottom_reducer_matrix,
         bottom_expander_sketch.T,
-        heldout_sketched_signals,
         benchmark_labels.T,
     )
     own = pl.pallas_call(
@@ -381,7 +379,7 @@
         out_shape=jax.ShapeDtypeStruct((3 * rows + (LANES // 2 + 2) * count, LANES), BF16),
         in_specs=[SMEM] + [HBM] * len(inputs),
         out_specs=VMEM,
-        scratch_shapes=[pltpu.VMEM(a.shape, a.dtype) for a in inputs]
+        scratch_shapes=[pltpu.VMEM(a.shape, a.dtype) for a in inputs[1:]]
         + [pltpu.SemaphoreType.DMA((len(inputs),))],
         compiler_params=params(8),
         name="pack",
@@ -465,9 +463,10 @@
             blocks += [second, crossed[1]]
         else:
             first, tails = split(first, tail)
-            tails, sums = tie((tails, sums))
         first = hop(first)
         sums = stage(k, held, sums)
+        if k == half - 1:
+            tails, sums = tie((tails, sums))
         first, sums = tie((first, sums))
         if k == half - 2:
             second, tail = split(second)

time: 40 us -> 39.9 us (level)
  transfers between devices with their start and end apart: 17 -> 17, of which waited for: 7 -> 9; matrix products, arithmetic and copies ran while one was open for 0% -> 0% of each run, Pallas kernels for 33% -> 33%
where the time goes in v14:
time: 39.9 us; the launch traced here: 39.6 us
  starting transfers between devices  16.1 us (40%)
  Pallas kernels  15.1 us (38%)
  waiting for transfers between devices  7.65 us (19%)
  between operations  0.77 us (2%)
    ppermute x8, starting transfers between devices, hop(): return lax.ppermute(value, 'dp', pairs)  15.4 us
    ppermute x8, waiting for transfers between devices, hop(): return lax.ppermute(value, 'dp', pairs)  6.36 us
    pallas_call x7, Pallas kernels, stage(): pl.pallas_call(functools.partial(stage_kernel, away, first), out_shape=[j...  5.28 us
    pallas_call x1, Pallas kernels, shards(): pl.pallas_call(local_kernel, out_shape=[jax.ShapeDtypeStruct(a.shape, a.d...  4.6 us
    pallas_call x1, Pallas kernels, shards(): pl.pallas_call(functools.partial(feature_kernel, half), out_shape=jax.Sha...  2.16 us
    pallas_call x1, Pallas kernels, shards(): pl.pallas_call(pack_kernel, out_shape=jax.ShapeDtypeStruct((3 * rows + (L...  1.35 us
    ppermute x9, waiting for transfers between devices, other_core(): lax.ppermute(value, 'dp', [(d, d ^ 1) for d in range(2 * RING_CHIPS)])  1.29 us
    pallas_call x1, Pallas kernels, shards(): pl.pallas_call(functools.partial(score_kernel, len(blocks), count), out_s...  0.87 us
  transfers between devices with their start and end apart: 17, of which 9 were waited for; matrix products, arithmetic and copies ran while one was open for 0% of the time, Pallas kernels for 33%

profile of v14, /device:TPU:0, one launch (start us, length us, event | category | flops | bytes accessed | tf_op | source)
XLA Modules:
  0.0 39.6 jit_solution(13354274095790781480)
XLA Ops:
  0.6 1.3 %pack.1.refs_0_ = bf16[1488,128]{1,0:T(8,128)(2,1)S(1)} custom-call(s32[1]{0:T(128)} %bitcast.me_ref, bf16[160,128]{1,0:T(8,128)(2,1)} %bitcast.14, bf16[8,8192]{1,0:T(8,128)(2,1)} %refs_1_.2, bf16[320,128]{1,0:T(8,128)(2,1)} %refs_2_.2, bf16[320,128]{1,0:T(8,128)(2,1)} %bitcast.13, bf16[320,128]{1,0:T(8,128)(2,1)} %refs_4_.2, f32[40,128]{1,0:T(8,128)} %bitcast.11, ...), custom_call_target="tpu_custom_call" | custom-call | tf_op jit(solution)/shard_map/pack/pallas_call | solution.py:377
  2.0 0.5 %collective-permute-start.2 = (bf16[1488,128]{1,0:T(8,128)(2,1)S(1)}, bf16[1488,128]{1,0:T(8,128)(2,1)S(1)}, u32[]{:S(2)}, u32[]{:S(2)}) collective-permute-start(bf16[1488,128]{1,0:T(8,128)(2,1)S(1)} %pack.1.refs_0_), channel_id=1, source_target_pairs={{0,1},{1,0},{2,3},{3,2},{4,5},{5,4},{6,7},{7,6},{8,9},{9,8},{10,11... | collective-permute-start | bytes 1142792 | tf_op jit(solution)/shard_map/ppermute | solution.py:55
  2.5 2.6 %collective-permute-start = (bf16[1488,128]{1,0:T(8,128)(2,1)S(1)}, bf16[1488,128]{1,0:T(8,128)(2,1)S(1)}, u32[]{:S(2)}, u32[]{:S(2)}) collective-permute-start(bf16[1488,128]{1,0:T(8,128)(2,1)S(1)} %pack.1.refs_0_), channel_id=1, source_target_pairs={{0,4},{1,3},{4,8},{5,1},{8,12},{9,5},{12,14},{13,9},{14,10},{15,13... | collective-permute-start | bytes 1142792 | tf_op jit(solution)/shard_map/ppermute | solution.py:51
  5.1 1.6 %collective-permute-start.3 = (bf16[1488,128]{1,0:T(8,128)(2,1)S(1)}, bf16[1488,128]{1,0:T(8,128)(2,1)S(1)}, u32[]{:S(2)}, u32[]{:S(2)}) collective-permute-start(bf16[1488,128]{1,0:T(8,128)(2,1)S(1)} %collective-permute-done.2.refs_1_), channel_id=1, source_target_pairs={{0,4},{1,3},{4,8},{5,1},{8,12},{9,5},{12,14},{13,9},{14,10},{15,13... | collective-permute-start | bytes 1142792 | tf_op jit(solution)/shard_map/ppermute | solution.py:51
  6.8 4.6 %local_products.1 = (bf16[256,5120]{1,0:T(8,128)(2,1)S(1)}, bf16[256,5120]{1,0:T(8,128)(2,1)S(1)}, bf16[256,5120]{1,0:T(8,128)(2,1)S(1)}, bf16[256,2560]{1,0:T(8...) custom-call(bf16[256,5120]{1,0:T(8,128)(2,1)} %refs_0_.1, ...), custom_call_target="tpu_custom_call" | custom-call | flops 1006632960 | bytes 14680064 | tf_op jit(solution)/shard_map/local_products/pallas_call | solution.py:398
  11.4 1.6 %collective-permute-start.1 = (bf16[1488,128]{1,0:T(8,128)(2,1)S(1)}, bf16[1488,128]{1,0:T(8,128)(2,1)S(1)}, u32[]{:S(2)}, u32[]{:S(2)}) collective-permute-start(bf16[1488,128]{1,0:T(8,128)(2,1)S(1)} %collective-permute-done.refs_0_.refs_2_), channel_id=1, source_target_pairs={{0,4},{1,3},{4,8},{5,1},{8,12},{9,5},{12,14},{13,9},{14,10},{15,13... | collective-permute-start | bytes 1142792 | tf_op jit(solution)/shard_map/ppermute | solution.py:51
  13.0 0.7 %stage.7 = (f32[256,1024]{1,0:T(8,128)S(1)}, f32[128,256]{1,0:T(8,128)S(1)}) custom-call(s32[1]{0:T(128)} %bitcast.me_ref, bf16[1488,128]{1,0:T(8,128)(2,1)S(1)} %pack.1.refs_0_, bf16[1488,128]{1,0:T(8,128)(2,1)S(1)} %collective-permute-done.2.refs_1_, bf16[256,5120]{1,0:T(8,128)(2,1)S(1)} %get-tuple-element.69.refs_2_, ...), custom_call_target="tpu_custom_call" | custom-call | flops 167772160 | bytes 2097152 | tf_op jit(solution)/shard_map/stage/pallas_call | solution.py:423
  13.7 1.1 %collective-permute-done.3.refs_1_.refs_4_ = bf16[1488,128]{1,0:T(8,128)(2,1)S(1)} collective-permute-done((bf16[1488,128]{1,0:T(8,128)(2,1)S(1)}, bf16[1488,128]{1,0:T(8,128)(2,1)S(1)}, u32[]{:S(2)}, u32[]{:S(2)}) %collective-permute-start.3) | collective-permute-done | bytes 380960 | tf_op jit(solution)/shard_map/ppermute | solution.py:51
  14.8 2.1 %collective-permute-start.5 = (bf16[1488,128]{1,0:T(8,128)(2,1)S(1)}, bf16[1488,128]{1,0:T(8,128)(2,1)S(1)}, u32[]{:S(2)}, u32[]{:S(2)}) collective-permute-start(bf16[1488,128]{1,0:T(8,128)(2,1)S(1)} %collective-permute-done.3.refs_1_.refs_4_), channel_id=1, source_target_pairs={{0,4},{1,3},{4,8},{5,1},{8,12},{9,5},{12,14},{13,9},{14,10},{15,13... | collective-permute-start | bytes 1142792 | tf_op jit(solution)/shard_map/ppermute | solution.py:51
  16.9 0.8 %stage.8 = (f32[256,1024]{1,0:T(8,128)S(1)}, f32[128,256]{1,0:T(8,128)S(1)}) custom-call(s32[1]{0:T(128)} %bitcast.me_ref, bf16[1488,128]{1,0:T(8,128)(2,1)S(1)} %collective-permute-done.refs_0_.refs_2_, bf16[1488,128]{1,0:T(8,128)(2,1)S(1)} %collective-permute-done.3.refs_1_.refs_4_, ...), custom_call_target="tpu_custom_call", output_to_operand_aliasing={{0}: (10, {}), {1}: (11, {})} | custom-call | flops 167772160 | bytes 2097152 | tf_op jit(solution)/shard_map/stage/pallas_call | solution.py:423
  17.6 1.4 %collective-permute-done.1.refs_0_.refs_6_ = bf16[1488,128]{1,0:T(8,128)(2,1)S(1)} collective-permute-done((bf16[1488,128]{1,0:T(8,128)(2,1)S(1)}, bf16[1488,128]{1,0:T(8,128)(2,1)S(1)}, u32[]{:S(2)}, u32[]{:S(2)}) %collective-permute-start.1) | collective-permute-done | bytes 380960 | tf_op jit(solution)/shard_map/ppermute | solution.py:51
  19.1 1.9 %collective-permute-start.4 = (bf16[1488,128]{1,0:T(8,128)(2,1)S(1)}, bf16[1488,128]{1,0:T(8,128)(2,1)S(1)}, u32[]{:S(2)}, u32[]{:S(2)}) collective-permute-start(bf16[1488,128]{1,0:T(8,128)(2,1)S(1)} %collective-permute-done.1.refs_0_.refs_6_), channel_id=1, source_target_pairs={{0,4},{1,3},{4,8},{5,1},{8,12},{9,5},{12,14},{13,9},{14,10},{15,13... | collective-permute-start | bytes 1142792 | tf_op jit(solution)/shard_map/ppermute | solution.py:51
  21.0 0.8 %stage.9 = (f32[256,1024]{1,0:T(8,128)S(1)}, f32[128,256]{1,0:T(8,128)S(1)}) custom-call(s32[1]{0:T(128)} %bitcast.me_ref, bf16[1488,128]{1,0:T(8,128)(2,1)S(1)} %collective-permute-done.6.refs_0_.refs_3_, bf16[1488,128]{1,0:T(8,128)(2,1)S(1)} %collective-permute-done.7.refs_1_.refs_5_, ...), custom_call_target="tpu_custom_call", output_to_operand_aliasing={{0}: (10, {}), {1}: (11, {})} | custom-call | flops 167772160 | bytes 2097152 | tf_op jit(solution)/shard_map/stage/pallas_call | solution.py:423
  21.7 1.4 %collective-permute-done.5.refs_1_.block_ref.refs_8_ = bf16[1488,128]{1,0:T(8,128)(2,1)S(1)} collective-permute-done((bf16[1488,128]{1,0:T(8,128)(2,1)S(1)}, bf16[1488,128]{1,0:T(8,128)(2,1)S(1)}, u32[]{:S(2)}, u32[]{:S(2)}) %collective-permute-start.5) | collective-permute-done | bytes 380960 | tf_op jit(solution)/shard_map/ppermute | solution.py:51
  23.2 1.9 %collective-permute-start.8 = (bf16[960,128]{1,0:T(8,128)(2,1)S(1)}, bf16[960,128]{1,0:T(8,128)(2,1)S(1)}, u32[]{:S(2)}, u32[]{:S(2)}) collective-permute-start(bf16[960,128]{1,0:T(8,128)(2,1)S(1)} %get-tuple-element.96), channel_id=1, source_target_pairs={{0,4},{1,3},{4,8},{5,1},{8,12},{9,5},{12,14},{13,9},{14,10},{15,13... | collective-permute-start | bytes 737288 | tf_op jit(solution)/shard_map/ppermute | solution.py:51
  25.1 0.8 %stage.10 = (f32[256,1024]{1,0:T(8,128)S(1)}, f32[128,256]{1,0:T(8,128)S(1)}) custom-call(s32[1]{0:T(128)} %bitcast.me_ref, bf16[1488,128]{1,0:T(8,128)(2,1)S(1)} %collective-permute-done.1.refs_0_.refs_6_, bf16[1488,128]{1,0:T(8,128)(2,1)S(1)} %collective-permute-done.5.refs_1_.block_ref.refs_8_, ...), custom_call_target="tpu_custom_call", output_to_operand_aliasing={{0}: (10, {}), {1}: (11, {})} | custom-call | flops 167772160 | bytes 2097152 | tf_op jit(solution)/shard_map/stage/pallas_call | solution.py:423
  25.9 1.4 %collective-permute-done.4.block_ref.refs_0_.refs_10_ = bf16[1488,128]{1,0:T(8,128)(2,1)S(1)} collective-permute-done((bf16[1488,128]{1,0:T(8,128)(2,1)S(1)}, bf16[1488,128]{1,0:T(8,128)(2,1)S(1)}, u32[]{:S(2)}, u32[]{:S(2)}) %collective-permute-start.4) | collective-permute-done | bytes 380960 | tf_op jit(solution)/shard_map/ppermute | solution.py:51
  27.3 1.9 %collective-permute-start.12 = (bf16[960,128]{1,0:T(8,128)(2,1)S(1)}, bf16[960,128]{1,0:T(8,128)(2,1)S(1)}, u32[]{:S(2)}, u32[]{:S(2)}) collective-permute-start(bf16[960,128]{1,0:T(8,128)(2,1)S(1)} %get-tuple-element.107), channel_id=1, source_target_pairs={{0,4},{1,3},{4,8},{5,1},{8,12},{9,5},{12,14},{13,9},{14,10},{15,13... | collective-permute-start | bytes 737288 | tf_op jit(solution)/shard_map/ppermute | solution.py:51
  29.2 0.8 %stage.11 = (f32[256,1024]{1,0:T(8,128)S(1)}, f32[128,256]{1,0:T(8,128)S(1)}) custom-call(s32[1]{0:T(128)} %bitcast.me_ref, bf16[1488,128]{1,0:T(8,128)(2,1)S(1)} %collective-permute-done.9.refs_0_.refs_7_, bf16[1488,128]{1,0:T(8,128)(2,1)S(1)} %collective-permute-done.10.refs_1_.refs_9_, ...), custom_call_target="tpu_custom_call", output_to_operand_aliasing={{0}: (10, {}), {1}: (11, {})} | custom-call | flops 167772160 | bytes 2097152 | tf_op jit(solution)/shard_map/stage/pallas_call | solution.py:423
  30.0 0.8 %stage.12 = (f32[256,1024]{1,0:T(8,128)S(1)}, f32[128,256]{1,0:T(8,128)S(1)}) custom-call(s32[1]{0:T(128)} %bitcast.me_ref, bf16[1488,128]{1,0:T(8,128)(2,1)S(1)} %collective-permute-done.4.block_ref.refs_0_.refs_10_, bf16[960,128]{1,0:T(8,128)(2,1)S(1)} %collective-permute-done.8.refs_1_, ...), custom_call_target="tpu_custom_call", output_to_operand_aliasing={{0}: (10, {}), {1}: (11, {})} | custom-call | flops 167772160 | bytes 2097152 | tf_op jit(solution)/shard_map/stage/pallas_call | solution.py:423
  30.8 0.0 copy-start
  30.8 1.8 %collective-permute-start.11 = (bf16[1056,128]{1,0:T(8,128)(2,1)S(1)}, bf16[1056,128]{1,0:T(8,128)(2,1)S(1)}, u32[]{:S(2)}, u32[]{:S(2)}) collective-permute-start(bf16[1056,128]{1,0:T(8,128)(2,1)S(1)} %get-tuple-element.106), channel_id=1, source_target_pairs={{0,4},{1,3},{4,8},{5,1},{8,12},{9,5},{12,14},{13,9},{14,10},{15,13... | collective-permute-start | bytes 811016 | tf_op jit(solution)/shard_map/ppermute | solution.py:51
  32.6 1.0 %collective-permute-done.12.refs_0_ = bf16[960,128]{1,0:T(8,128)(2,1)S(1)} collective-permute-done((bf16[960,128]{1,0:T(8,128)(2,1)S(1)}, bf16[960,128]{1,0:T(8,128)(2,1)S(1)}, u32[]{:S(2)}, u32[]{:S(2)}) %collective-permute-start.12) | collective-permute-done | bytes 245792 | tf_op jit(solution)/shard_map/ppermute | solution.py:51
  33.6 0.5 %collective-permute-done.15.refs_1_ = bf16[960,128]{1,0:T(8,128)(2,1)S(1)} collective-permute-done((bf16[960,128]{1,0:T(8,128)(2,1)S(1)}, bf16[960,128]{1,0:T(8,128)(2,1)S(1)}, u32[]{:S(2)}, u32[]{:S(2)}) %collective-permute-start.15) | collective-permute-done | bytes 245792 | tf_op jit(solution)/shard_map/ppermute | solution.py:55
  34.1 0.8 %stage.13 = (f32[256,1024]{1,0:T(8,128)S(1)}, f32[128,256]{1,0:T(8,128)S(1)}) custom-call(s32[1]{0:T(128)} %bitcast.me_ref, bf16[1488,128]{1,0:T(8,128)(2,1)S(1)} %collective-permute-done.14.refs_0_.refs_11_, bf16[960,128]{1,0:T(8,128)(2,1)S(1)} %collective-permute-done.15.refs_1_, ...), custom_call_target="tpu_custom_call", output_to_operand_aliasing={{0}: (10, {}), {1}: (11, {})} | custom-call | flops 167772160 | bytes 2097152 | tf_op jit(solution)/shard_map/stage/pallas_call | solution.py:423
  34.9 0.2 collective-permute-done.13.refs_1_
  35.1 2.2 %features.1.unit_ref = f32[128,128]{1,0:T(8,128)S(1)} custom-call(s32[1]{0:T(128)} %bitcast.me_ref, s32[1,2]{1,0:T(1,128)S(1)} %copy-done, bf16[960,128]{1,0:T(8,128)(2,1)S(1)} %collective-permute-done.12.refs_0_, bf16[960,128]{1,0:T(8,128)(2,1)S(1)} %collective-permute-done.13.refs_1_, bf16[256,5120]{1,0:T(8,128)(2,1)S(1)} %get-tuple-element.69.refs_2_, ...), custom_call_target="tpu_custom_call" | custom-call | flops 1 | bytes 1 | tf_op jit(solution)/shard_map/features/pallas_call | solution.py:480
  37.2 0.1 collective-permute-done.11.refs_12_
  37.3 0.1 collective-permute-start.16
  37.4 0.9 %scores.1.best_ref = f32[2,3,8,128]{3,2,1,0:T(8,128)S(1)} custom-call(f32[128,128]{1,0:T(8,128)S(1)} %features.1.unit_ref, bf16[1488,128]{1,0:T(8,128)(2,1)S(1)} %pack.1.refs_0_, bf16[1488,128]{1,0:T(8,128)(2,1)S(1)} %collective-permute-done.2.refs_1_, bf16[1488,128]{1,0:T(8,128)(2,1)S(1)} %collective-permute-done.refs_0_.refs_2_, ...), custom_call_target="tpu_custom_call" | custom-call | flops 4194304 | bytes 2097152 | tf_op jit(solution)/shard_map/scores/pallas_call | solution.py:503
  38.3 0.5 %collective-permute-done.16.block_ref = bf16[1056,128]{1,0:T(8,128)(2,1)S(1)} collective-permute-done((bf16[1056,128]{1,0:T(8,128)(2,1)S(1)}, bf16[1056,128]{1,0:T(8,128)(2,1)S(1)}, u32[]{:S(2)}, u32[]{:S(2)}) %collective-permute-start.16) | collective-permute-done | bytes 270368 | tf_op jit(solution)/shard_map/ppermute | solution.py:55
  38.9 0.8 %last_scores.1 = (f32[2,3]{1,0:T(2,128)}, f32[1,2]{1,0:T(1,128)}) custom-call(f32[128,128]{1,0:T(8,128)S(1)} %features.1.unit_ref, bf16[1056,128]{1,0:T(8,128)(2,1)S(1)} %collective-permute-done.16.block_ref, f32[2,3,8,128]{3,2,1,0:T(8,128)S(1)} %scores.1.best_ref), custom_call_target="tpu_custom_call" | custom-call | tf_op jit(solution)/shard_map/last_scores/pallas_call | solution.py:512
  (18 shorter events, 0.1 us)
Async XLA Ops:
  2.0 3.2 %collective-permute-start.2 = (bf16[1488,128]{1,0:T(8,128)(2,1)S(1)}, bf16[1488,128]{1,0:T(8,128)(2,1)S(1)}, u32[]{:S(2)}, u32[]{:S(2)}) collective-permute-start(bf16[1488,128]{1,0:T(8,128)(2,1)S(1)} %pack.1.refs_0_), channel_id=1, source_target_pairs={{0,1},{1,0},{2,3},{3,2},{4,5},{5,4},{6,7},{7,6},{8,9},{9,8},{10,11... | collective-permute-start | bytes 1142792 | tf_op jit(solution)/shard_map/ppermute | solution.py:55
  2.5 8.9 %collective-permute-start = (bf16[1488,128]{1,0:T(8,128)(2,1)S(1)}, bf16[1488,128]{1,0:T(8,128)(2,1)S(1)}, u32[]{:S(2)}, u32[]{:S(2)}) collective-permute-start(bf16[1488,128]{1,0:T(8,128)(2,1)S(1)} %pack.1.refs_0_), channel_id=1, source_target_pairs={{0,4},{1,3},{4,8},{5,1},{8,12},{9,5},{12,14},{13,9},{14,10},{15,13... | collective-permute-start | bytes 1142792 | tf_op jit(solution)/shard_map/ppermute | solution.py:51
  5.1 9.6 %collective-permute-start.3 = (bf16[1488,128]{1,0:T(8,128)(2,1)S(1)}, bf16[1488,128]{1,0:T(8,128)(2,1)S(1)}, u32[]{:S(2)}, u32[]{:S(2)}) collective-permute-start(bf16[1488,128]{1,0:T(8,128)(2,1)S(1)} %collective-permute-done.2.refs_1_), channel_id=1, source_target_pairs={{0,4},{1,3},{4,8},{5,1},{8,12},{9,5},{12,14},{13,9},{14,10},{15,13... | collective-permute-start | bytes 1142792 | tf_op jit(solution)/shard_map/ppermute | solution.py:51
  11.4 7.7 %collective-permute-start.1 = (bf16[1488,128]{1,0:T(8,128)(2,1)S(1)}, bf16[1488,128]{1,0:T(8,128)(2,1)S(1)}, u32[]{:S(2)}, u32[]{:S(2)}) collective-permute-start(bf16[1488,128]{1,0:T(8,128)(2,1)S(1)} %collective-permute-done.refs_0_.refs_2_), channel_id=1, source_target_pairs={{0,4},{1,3},{4,8},{5,1},{8,12},{9,5},{12,14},{13,9},{14,10},{15,13... | collective-permute-start | bytes 1142792 | tf_op jit(solution)/shard_map/ppermute | solution.py:51
  13.0 7.9 %collective-permute-start.6 = (bf16[1488,128]{1,0:T(8,128)(2,1)S(1)}, bf16[1488,128]{1,0:T(8,128)(2,1)S(1)}, u32[]{:S(2)}, u32[]{:S(2)}) collective-permute-start(bf16[1488,128]{1,0:T(8,128)(2,1)S(1)} %collective-permute-done.refs_0_.refs_2_), channel_id=1, source_target_pairs={{0,1},{1,0},{2,3},{3,2},{4,5},{5,4},{6,7},{7,6},{8,9},{9,8},{10,11... | collective-permute-start | bytes 1142792 | tf_op jit(solution)/shard_map/ppermute | solution.py:55
  14.8 6.2 %collective-permute-start.7 = (bf16[1488,128]{1,0:T(8,128)(2,1)S(1)}, bf16[1488,128]{1,0:T(8,128)(2,1)S(1)}, u32[]{:S(2)}, u32[]{:S(2)}) collective-permute-start(bf16[1488,128]{1,0:T(8,128)(2,1)S(1)} %collective-permute-done.3.refs_1_.refs_4_), channel_id=1, source_target_pairs={{0,1},{1,0},{2,3},{3,2},{4,5},{5,4},{6,7},{7,6},{8,9},{9,8},{10,11... | collective-permute-start | bytes 1142792 | tf_op jit(solution)/shard_map/ppermute | solution.py:55
  14.8 8.4 %collective-permute-start.5 = (bf16[1488,128]{1,0:T(8,128)(2,1)S(1)}, bf16[1488,128]{1,0:T(8,128)(2,1)S(1)}, u32[]{:S(2)}, u32[]{:S(2)}) collective-permute-start(bf16[1488,128]{1,0:T(8,128)(2,1)S(1)} %collective-permute-done.3.refs_1_.refs_4_), channel_id=1, source_target_pairs={{0,4},{1,3},{4,8},{5,1},{8,12},{9,5},{12,14},{13,9},{14,10},{15,13... | collective-permute-start | bytes 1142792 | tf_op jit(solution)/shard_map/ppermute | solution.py:51
  19.1 8.2 %collective-permute-start.4 = (bf16[1488,128]{1,0:T(8,128)(2,1)S(1)}, bf16[1488,128]{1,0:T(8,128)(2,1)S(1)}, u32[]{:S(2)}, u32[]{:S(2)}) collective-permute-start(bf16[1488,128]{1,0:T(8,128)(2,1)S(1)} %collective-permute-done.1.refs_0_.refs_6_), channel_id=1, source_target_pairs={{0,4},{1,3},{4,8},{5,1},{8,12},{9,5},{12,14},{13,9},{14,10},{15,13... | collective-permute-start | bytes 1142792 | tf_op jit(solution)/shard_map/ppermute | solution.py:51
  21.0 8.3 %collective-permute-start.9 = (bf16[1488,128]{1,0:T(8,128)(2,1)S(1)}, bf16[1488,128]{1,0:T(8,128)(2,1)S(1)}, u32[]{:S(2)}, u32[]{:S(2)}) collective-permute-start(bf16[1488,128]{1,0:T(8,128)(2,1)S(1)} %collective-permute-done.1.refs_0_.refs_6_), channel_id=1, source_target_pairs={{0,1},{1,0},{2,3},{3,2},{4,5},{5,4},{6,7},{7,6},{8,9},{9,8},{10,11... | collective-permute-start | bytes 1142792 | tf_op jit(solution)/shard_map/ppermute | solution.py:55
  23.2 6.0 %collective-permute-start.10 = (bf16[1488,128]{1,0:T(8,128)(2,1)S(1)}, bf16[1488,128]{1,0:T(8,128)(2,1)S(1)}, u32[]{:S(2)}, u32[]{:S(2)}) collective-permute-start(bf16[1488,128]{1,0:T(8,128)(2,1)S(1)} %collective-permute-done.5.refs_1_.block_ref.refs_8_), channel_id=1, source_target_pairs={{0,1},{1,0},{2,3},{3,2},{4,5},{5,4},{6,7},{7,6},{8,9},{9,8},{10,11... | collective-permute-start | bytes 1142792 | tf_op jit(solution)/shard_map/ppermute | solution.py:55
  23.2 6.8 %collective-permute-start.8 = (bf16[960,128]{1,0:T(8,128)(2,1)S(1)}, bf16[960,128]{1,0:T(8,128)(2,1)S(1)}, u32[]{:S(2)}, u32[]{:S(2)}) collective-permute-start(bf16[960,128]{1,0:T(8,128)(2,1)S(1)} %get-tuple-element.96), channel_id=1, source_target_pairs={{0,4},{1,3},{4,8},{5,1},{8,12},{9,5},{12,14},{13,9},{14,10},{15,13... | collective-permute-start | bytes 737288 | tf_op jit(solution)/shard_map/ppermute | solution.py:51
  27.3 6.2 %collective-permute-start.12 = (bf16[960,128]{1,0:T(8,128)(2,1)S(1)}, bf16[960,128]{1,0:T(8,128)(2,1)S(1)}, u32[]{:S(2)}, u32[]{:S(2)}) collective-permute-start(bf16[960,128]{1,0:T(8,128)(2,1)S(1)} %get-tuple-element.107), channel_id=1, source_target_pairs={{0,4},{1,3},{4,8},{5,1},{8,12},{9,5},{12,14},{13,9},{14,10},{15,13... | collective-permute-start | bytes 737288 | tf_op jit(solution)/shard_map/ppermute | solution.py:51
  29.2 4.3 %collective-permute-start.14 = (bf16[1488,128]{1,0:T(8,128)(2,1)S(1)}, bf16[1488,128]{1,0:T(8,128)(2,1)S(1)}, u32[]{:S(2)}, u32[]{:S(2)}) collective-permute-start(bf16[1488,128]{1,0:T(8,128)(2,1)S(1)} %collective-permute-done.4.block_ref.refs_0_.refs_10_), channel_id=1, source_target_pairs={{0,1},{1,0},{2,3},{3,2},{4,5},{5,4},{6,7},{7,6},{8,9},{9,8},{10,11... | collective-permute-start | bytes 1142792 | tf_op jit(solution)/shard_map/ppermute | solution.py:55
  30.8 4.3 %copy-start = (s32[1,2]{1,0:T(1,128)S(1)}, s32[1,2]{1,0:T(1,128)}, u32[]{:S(2)}) copy-start(s32[1,2]{1,0:T(1,128)} %counts_ref.1) | copy-start | bytes 28
  30.8 6.5 %collective-permute-start.11 = (bf16[1056,128]{1,0:T(8,128)(2,1)S(1)}, bf16[1056,128]{1,0:T(8,128)(2,1)S(1)}, u32[]{:S(2)}, u32[]{:S(2)}) collective-permute-start(bf16[1056,128]{1,0:T(8,128)(2,1)S(1)} %get-tuple-element.106), channel_id=1, source_target_pairs={{0,4},{1,3},{4,8},{5,1},{8,12},{9,5},{12,14},{13,9},{14,10},{15,13... | collective-permute-start | bytes 811016 | tf_op jit(solution)/shard_map/ppermute | solution.py:51
  32.6 1.5 %collective-permute-start.15 = (bf16[960,128]{1,0:T(8,128)(2,1)S(1)}, bf16[960,128]{1,0:T(8,128)(2,1)S(1)}, u32[]{:S(2)}, u32[]{:S(2)}) collective-permute-start(bf16[960,128]{1,0:T(8,128)(2,1)S(1)} %collective-permute-done.8.refs_1_), channel_id=1, source_target_pairs={{0,1},{1,0},{2,3},{3,2},{4,5},{5,4},{6,7},{7,6},{8,9},{9,8},{10,11... | collective-permute-start | bytes 737288 | tf_op jit(solution)/shard_map/ppermute | solution.py:55
  33.5 1.5 %collective-permute-start.13 = (bf16[960,128]{1,0:T(8,128)(2,1)S(1)}, bf16[960,128]{1,0:T(8,128)(2,1)S(1)}, u32[]{:S(2)}, u32[]{:S(2)}) collective-permute-start(bf16[960,128]{1,0:T(8,128)(2,1)S(1)} %collective-permute-done.12.refs_0_), channel_id=1, source_target_pairs={{0,1},{1,0},{2,3},{3,2},{4,5},{5,4},{6,7},{7,6},{8,9},{9,8},{10,11... | collective-permute-start | bytes 737288 | tf_op jit(solution)/shard_map/ppermute | solution.py:55
  37.3 1.6 %collective-permute-start.16 = (bf16[1056,128]{1,0:T(8,128)(2,1)S(1)}, bf16[1056,128]{1,0:T(8,128)(2,1)S(1)}, u32[]{:S(2)}, u32[]{:S(2)}) collective-permute-start(bf16[1056,128]{1,0:T(8,128)(2,1)S(1)} %collective-permute-done.11.refs_12_), channel_id=1, source_target_pairs={{0,1},{1,0},{2,3},{3,2},{4,5},{5,4},{6,7},{7,6},{8,9},{9,8},{10,11... | collective-permute-start | bytes 811016 | tf_op jit(solution)/shard_map/ppermute | solution.py:55

commit v15 on v14

--- a/solution.py
+++ b/solution.py
@@ -109,9 +109,11 @@
 
 
 def local_kernel(*refs):
-    x_hbm, mixed_hbm, adjoint_hbm, values_hbm, target_hbm, top_target_hbm, gain_hbm, source_hbm = refs[:8]
-    x_ref, mixed_ref, adjoint_ref, values_ref, target_ref, top_target_ref, turned_ref, sums_ref = refs[8:16]
-    gain_ref, source_ref, sems = refs[16:]
+    x_hbm, mixed_hbm, adjoint_hbm, values_hbm, target_hbm, top_target_hbm = refs[:6]
+    small_hbm, gain_hbm, source_hbm = refs[6:8], refs[8], refs[9]
+    x_ref, mixed_ref, adjoint_ref, values_ref, target_ref, top_target_ref = refs[10:16]
+    small_refs, turned_ref, sums_ref = refs[16:18], refs[18], refs[19]
+    gain_ref, source_ref, sems = refs[20:]
     tokens, width = x_ref.shape
     span = width // STEPS
     copies = []
@@ -129,6 +131,7 @@
         (mixed_hbm, mixed_ref),
         (values_hbm, values_ref),
         (top_target_hbm, top_target_ref),
+        *zip(small_hbm, small_refs),
     )
     later = load(pairs, sems.at[STEPS])
     products = jnp.zeros((tokens, 2 * LANES), F32)
@@ -204,6 +207,66 @@
     return products, bridge
 
 
+def add_half(away, other, me_ref, piece, held, old, scratch):
+    x_ref, mixed_ref, adjoint_ref, values_ref, target_ref, top_target_ref, source_ref = held
+    wide, down, up = scratch
+    pad = LANES // 2
+    rows = wide.shape[0] - pad
+    half, span = rows // 2, 2 * rows
+    me = me_ref[0]
+    pos, core = ring_pos(me // 2), me % 2
+    chip = ring_chip((pos + away * (2 * core - 1) + RING_CHIPS) % RING_CHIPS)
+    side = 1 - core if other else core
+    odd = chip % 2
+    mine = pl.ds(pl.multiple_of(chip * span + side * (rows - pad), LANES), rows + pad)
+    inside = pl.ds(pl.multiple_of(side * pad, 16), rows)
+    outside = pl.ds(pl.multiple_of((1 - side) * rows, 16), pad)
+    block = pl.ds(pl.multiple_of(chip * span + side * rows, 16), rows)
+    values_start = (chip // 2) * span + odd * (rows - pad)
+    values_part = pl.ds(pl.multiple_of(values_start, LANES), rows + pad)
+    values_inside = pl.ds(pl.multiple_of(odd * pad + side * half, 16), half)
+    values_block = pl.ds(pl.multiple_of(chip * rows + side * half, 16), half)
+    wide[outside, :] = jnp.zeros((pad, wide.shape[1]), BF16)
+    down[outside, :] = jnp.zeros((pad, down.shape[1]), BF16)
+    up[...] = jnp.zeros(up.shape, BF16)
+    wide[inside, pl.ds(0, LANES)] = piece[pl.ds(0, rows), :]
+    wide[inside, pl.ds(LANES, LANES)] = piece[pl.ds(rows, rows), :]
+    wide[inside, pl.ds(2 * LANES, LANES)] = target_ref[block, :]
+    up[values_inside, pl.ds(0, LANES)] = piece[pl.ds(2 * rows, half), :]
+    up[values_inside, pl.ds(LANES, LANES)] = top_target_ref[values_block, :]
+    packed = piece[pl.ds(2 * rows + half, half), :].astype(F32)
+    turned = pltpu.roll(packed, pad, 1)
+    lower = half_lanes(packed.shape)
+    at = side * pad
+    down[pl.ds(pl.multiple_of(at, 16), half), pl.ds(0, LANES)] = jnp.where(lower, packed, turned).astype(BF16)
+    down[pl.ds(pl.multiple_of(at + half, 16), half), pl.ds(0, LANES)] = jnp.where(lower, turned, packed).astype(BF16)
+    down[inside, pl.ds(LANES, LANES)] = source_ref[block, :]
+
+    weights = wide[...]
+    bridge = mm_cols(weights[:, :LANES], weights[:, LANES:])
+    products = []
+    for activation, factor in (
+        (values_ref[:, values_part], up[...]),
+        (x_ref[:, mine], weights[:, : 2 * LANES]),
+        (adjoint_ref[:, mine], weights[:, LANES:]),
+        (mixed_ref[:, mine], down[...]),
+    ):
+        product = mm(activation, factor)
+        products += [product[:, :LANES], product[:, LANES:]]
+    old_sums, old_bridge = old
+    products = [p + old_sums[:, i * LANES : (i + 1) * LANES] for i, p in enumerate(products)]
+    return products, bridge + old_bridge[...]
+
+
+def half_kernel(away, me_ref, *refs):
+    piece, held, old = refs[0], refs[1:8], refs[8:10]
+    (new_sums, new_bridge), scratch = refs[10:12], refs[12:]
+    products, bridge = add_half(away, False, me_ref, piece, held, old, scratch)
+    for i in range(SUMS):
+        new_sums[:, i * LANES : (i + 1) * LANES] = products[i]
+    new_bridge[...] = bridge
+
+
 def stage_kernel(away, first, me_ref, *refs):
     pieces, held, old = refs[:2], refs[2:9], refs[9:-5]
     (new_sums, new_bridge), scratch = refs[-5:-3], refs[-3:]
@@ -214,15 +277,12 @@
 
 
 def feature_kernel(away, me_ref, counts_ref, *refs):
-    pieces, held, old, local_ref, small_hbm, refs = refs[:2], refs[2:9], refs[9:11], refs[11], refs[12:14], refs[14:]
-    out_ref, scratch, (expand_ref, sketch_ref, sems) = refs[0], refs[1:4], refs[4:]
-    more = load(zip(small_hbm, (expand_ref, sketch_ref)), sems)
-    products, bridge = add_stage(away, me_ref, pieces, held, old, scratch)
+    piece, held, old, local_ref, expand_ref, sketch_ref = refs[0], refs[1:8], refs[8:10], *refs[10:13]
+    out_ref, scratch = refs[13], refs[14:]
+    products, bridge = add_half(away, True, me_ref, piece, held, old, scratch)
     local = [local_ref[:, i * LANES : (i + 1) * LANES] for i in range(LOCAL_SUMS)]
     tokens, width = held[0].shape
     half = LANES // 2
-    for copy in more:
-        copy.wait()
     inverse = local[INVERSE]
     returned = products[VALUES].astype(BF16)
     back = mm(returned, jnp.concatenate([bridge.astype(BF16), sketch_ref[...]], axis=1))
@@ -392,24 +452,27 @@
         values,
         bottom_target_sketch,
         top_target_sketch,
+        top_expander_sketch.T,
+        top_reducer_sketch,
         top_rmsnorm_weights.reshape(1, width),
         source_sketch.T,
     )
     *activations, local = pl.pallas_call(
         local_kernel,
-        out_shape=[jax.ShapeDtypeStruct(a.shape, a.dtype) for a in inputs[:6]]
+        out_shape=[jax.ShapeDtypeStruct(a.shape, a.dtype) for a in inputs[:8]]
         + [
             jax.ShapeDtypeStruct((width, LANES), BF16),
             jax.ShapeDtypeStruct((tokens, LOCAL_SUMS * LANES), F32),
         ],
         in_specs=[HBM] * len(inputs),
-        out_specs=[VMEM] * 8,
-        scratch_shapes=[pltpu.VMEM(a.shape, a.dtype) for a in inputs[6:]]
-        + [pltpu.SemaphoreType.DMA((STEPS + 1, 4))],
+        out_specs=[VMEM] * 10,
+        scratch_shapes=[pltpu.VMEM(a.shape, a.dtype) for a in inputs[8:]]
+        + [pltpu.SemaphoreType.DMA((STEPS + 1, 6))],
         compiler_params=params(24),
         cost_estimate=cost(tokens * width * LANES * 6, 14 * MIB),
         name="local_products",
     )(*in_hbm(inputs))
+    activations, small = [*activations[:6], activations[8]], activations[6:8]
 
     stage_scratch = [
         pltpu.VMEM((2 * rows, 2 * LANES), BF16),
@@ -476,28 +539,34 @@
         if k < half - 1:
             second, sums = tie((second, sums))
     tails = hop(tails)
-    small = (top_expander_sketch.T, top_reducer_sketch)
+    half_scratch = [
+        pltpu.VMEM((rows + LANES // 2, 3 * LANES), BF16),
+        pltpu.VMEM((rows + LANES // 2, 2 * LANES), BF16),
+        pltpu.VMEM((rows + LANES // 2, 2 * LANES), BF16),
+    ]
+    crossed = other_core(first)
+    start = 2 + len(activations)
+    sums = pl.pallas_call(
+        functools.partial(half_kernel, half),
+        out_shape=[jax.ShapeDtypeStruct(a.shape, a.dtype) for a in sums],
+        in_specs=[SMEM] + [VMEM] * (1 + len(activations) + 2),
+        out_specs=[VMEM, VMEM],
+        scratch_shapes=half_scratch,
+        input_output_aliases={start: 0, start + 1: 1},
+        compiler_params=params(16),
+        cost_estimate=cost(tokens * rows * LANES * 8, MIB),
+        name="half_stage",
+    )(me.reshape(1), first, *activations, *sums)
     unit = pl.pallas_call(
         functools.partial(feature_kernel, half),
         out_shape=jax.ShapeDtypeStruct((LANES, LANES), F32),
-        in_specs=[SMEM] * 2 + [VMEM] * (2 + len(activations) + 3) + [HBM] * 2,
+        in_specs=[SMEM] * 2 + [VMEM] * (1 + len(activations) + 5),
         out_specs=VMEM,
-        scratch_shapes=stage_scratch
-        + [pltpu.VMEM(a.shape, a.dtype) for a in small]
-        + [pltpu.SemaphoreType.DMA((2,))],
+        scratch_shapes=half_scratch,
         compiler_params=params(16),
         cost_estimate=cost(1, 1),
         name="features",
-    )(
-        me.reshape(1),
-        sequence_token_counts,
-        first,
-        other_core(first),
-        *activations,
-        *sums,
-        local,
-        *in_hbm(small),
-    )
+    )(me.reshape(1), sequence_token_counts, crossed, *activations, *sums, local, *small)
     tails, unit = tie((tails, unit))
     blocks.append(tails)
     best = pl.pallas_call(

time: 39.9 us -> 39.9 us (level)
    pallas_call x0 -> x1, Pallas kernels: none -> 0.62 us  [shards(): pl.pallas_call(functools.partial(half_kernel, half), out_shape=[jax.Shape...]
  transfers between devices with their start and end apart: 17 -> 17, of which waited for: 9 -> 7; matrix products, arithmetic and copies ran while one was open for 0% -> 0% of each run, Pallas kernels for 33% -> 33%
where the time goes in v15:
time: 39.9 us; the launch traced here: 39.7 us
  starting transfers between devices  15.9 us (40%)
  Pallas kernels  15.4 us (39%)
  waiting for transfers between devices  7.6 us (19%)
  between operations  0.79 us (2%)
    ppermute x8, starting transfers between devices, hop(): return lax.ppermute(value, 'dp', pairs)  15.2 us
    ppermute x8, waiting for transfers between devices, hop(): return lax.ppermute(value, 'dp', pairs)  6.61 us
    pallas_call x7, Pallas kernels, stage(): pl.pallas_call(functools.partial(stage_kernel, away, first), out_shape=[j...  5.25 us
    pallas_call x1, Pallas kernels, shards(): pl.pallas_call(local_kernel, out_shape=[jax.ShapeDtypeStruct(a.shape, a.d...  4.69 us
    pallas_call x1, Pallas kernels, shards(): pl.pallas_call(functools.partial(feature_kernel, half), out_shape=jax.Sha...  1.79 us
    pallas_call x1, Pallas kernels, shards(): pl.pallas_call(pack_kernel, out_shape=jax.ShapeDtypeStruct((3 * rows + (L...  1.35 us
    ppermute x9, waiting for transfers between devices, other_core(): lax.ppermute(value, 'dp', [(d, d ^ 1) for d in range(2 * RING_CHIPS)])  0.98 us
    pallas_call x1, Pallas kernels, shards(): pl.pallas_call(functools.partial(score_kernel, len(blocks), count), out_s...  0.86 us
  transfers between devices with their start and end apart: 17, of which 7 were waited for; matrix products, arithmetic and copies ran while one was open for 0% of the time, Pallas kernels for 33%

profile of v15, /device:TPU:0, one launch (start us, length us, event | category | flops | bytes accessed | tf_op | source)
XLA Modules:
  0.0 39.7 jit_solution(8512271519138618856)
XLA Ops:
  0.6 1.3 %pack.1.refs_0_ = bf16[1488,128]{1,0:T(8,128)(2,1)S(1)} custom-call(s32[1]{0:T(128)} %bitcast.me_ref, bf16[160,128]{1,0:T(8,128)(2,1)} %bitcast.14, bf16[8,8192]{1,0:T(8,128)(2,1)} %refs_1_.2, bf16[320,128]{1,0:T(8,128)(2,1)} %refs_2_.2, bf16[320,128]{1,0:T(8,128)(2,1)} %bitcast.13, bf16[320,128]{1,0:T(8,128)(2,1)} %refs_4_.2, f32[40,128]{1,0:T(8,128)} %bitcast.11, ...), custom_call_target="tpu_custom_call" | custom-call | tf_op jit(solution)/shard_map/pack/pallas_call | solution.py:437
  2.0 0.5 %collective-permute-start.2 = (bf16[1488,128]{1,0:T(8,128)(2,1)S(1)}, bf16[1488,128]{1,0:T(8,128)(2,1)S(1)}, u32[]{:S(2)}, u32[]{:S(2)}) collective-permute-start(bf16[1488,128]{1,0:T(8,128)(2,1)S(1)} %pack.1.refs_0_), channel_id=1, source_target_pairs={{0,1},{1,0},{2,3},{3,2},{4,5},{5,4},{6,7},{7,6},{8,9},{9,8},{10,11... | collective-permute-start | bytes 1142792 | tf_op jit(solution)/shard_map/ppermute | solution.py:55
  2.5 2.6 %collective-permute-start = (bf16[1488,128]{1,0:T(8,128)(2,1)S(1)}, bf16[1488,128]{1,0:T(8,128)(2,1)S(1)}, u32[]{:S(2)}, u32[]{:S(2)}) collective-permute-start(bf16[1488,128]{1,0:T(8,128)(2,1)S(1)} %pack.1.refs_0_), channel_id=1, source_target_pairs={{0,4},{1,3},{4,8},{5,1},{8,12},{9,5},{12,14},{13,9},{14,10},{15,13... | collective-permute-start | bytes 1142792 | tf_op jit(solution)/shard_map/ppermute | solution.py:51
  5.1 1.6 %collective-permute-start.3 = (bf16[1488,128]{1,0:T(8,128)(2,1)S(1)}, bf16[1488,128]{1,0:T(8,128)(2,1)S(1)}, u32[]{:S(2)}, u32[]{:S(2)}) collective-permute-start(bf16[1488,128]{1,0:T(8,128)(2,1)S(1)} %collective-permute-done.2.refs_1_), channel_id=1, source_target_pairs={{0,4},{1,3},{4,8},{5,1},{8,12},{9,5},{12,14},{13,9},{14,10},{15,13... | collective-permute-start | bytes 1142792 | tf_op jit(solution)/shard_map/ppermute | solution.py:51
  6.8 4.7 %local_products.1 = (bf16[256,5120]{1,0:T(8,128)(2,1)S(1)}, bf16[256,5120]{1,0:T(8,128)(2,1)S(1)}, bf16[256,5120]{1,0:T(8,128)(2,1)S(1)}, bf16[256,2560]{1,0:T(8...) custom-call(bf16[256,5120]{1,0:T(8,128)(2,1)} %refs_0_.1, ...), custom_call_target="tpu_custom_call" | custom-call | flops 1006632960 | bytes 14680064 | tf_op jit(solution)/shard_map/local_products/pallas_call | solution.py:460
  11.5 1.6 %collective-permute-start.1 = (bf16[1488,128]{1,0:T(8,128)(2,1)S(1)}, bf16[1488,128]{1,0:T(8,128)(2,1)S(1)}, u32[]{:S(2)}, u32[]{:S(2)}) collective-permute-start(bf16[1488,128]{1,0:T(8,128)(2,1)S(1)} %collective-permute-done.refs_0_.refs_2_), channel_id=1, source_target_pairs={{0,4},{1,3},{4,8},{5,1},{8,12},{9,5},{12,14},{13,9},{14,10},{15,13... | collective-permute-start | bytes 1142792 | tf_op jit(solution)/shard_map/ppermute | solution.py:51
  13.1 0.7 %stage.7 = (f32[256,1024]{1,0:T(8,128)S(1)}, f32[128,256]{1,0:T(8,128)S(1)}) custom-call(s32[1]{0:T(128)} %bitcast.me_ref, bf16[1488,128]{1,0:T(8,128)(2,1)S(1)} %pack.1.refs_0_, bf16[1488,128]{1,0:T(8,128)(2,1)S(1)} %collective-permute-done.2.refs_1_, bf16[256,5120]{1,0:T(8,128)(2,1)S(1)} %get-tuple-element.73.refs_2_.refs_1_, ...), custom_call_target="tpu_custom_call" | custom-call | flops 167772160 | bytes 2097152 | tf_op jit(solution)/shard_map/stage/pallas_call | solution.py:486
  13.8 1.0 %collective-permute-done.3.refs_1_.refs_4_ = bf16[1488,128]{1,0:T(8,128)(2,1)S(1)} collective-permute-done((bf16[1488,128]{1,0:T(8,128)(2,1)S(1)}, bf16[1488,128]{1,0:T(8,128)(2,1)S(1)}, u32[]{:S(2)}, u32[]{:S(2)}) %collective-permute-start.3) | collective-permute-done | bytes 380960 | tf_op jit(solution)/shard_map/ppermute | solution.py:51
  14.8 2.1 %collective-permute-start.5 = (bf16[1488,128]{1,0:T(8,128)(2,1)S(1)}, bf16[1488,128]{1,0:T(8,128)(2,1)S(1)}, u32[]{:S(2)}, u32[]{:S(2)}) collective-permute-start(bf16[1488,128]{1,0:T(8,128)(2,1)S(1)} %collective-permute-done.3.refs_1_.refs_4_), channel_id=1, source_target_pairs={{0,4},{1,3},{4,8},{5,1},{8,12},{9,5},{12,14},{13,9},{14,10},{15,13... | collective-permute-start | bytes 1142792 | tf_op jit(solution)/shard_map/ppermute | solution.py:51
  16.9 0.8 %stage.8 = (f32[256,1024]{1,0:T(8,128)S(1)}, f32[128,256]{1,0:T(8,128)S(1)}) custom-call(s32[1]{0:T(128)} %bitcast.me_ref, bf16[1488,128]{1,0:T(8,128)(2,1)S(1)} %collective-permute-done.refs_0_.refs_2_, bf16[1488,128]{1,0:T(8,128)(2,1)S(1)} %collective-permute-done.3.refs_1_.refs_4_, ...), custom_call_target="tpu_custom_call", output_to_operand_aliasing={{0}: (10, {}), {1}: (11, {})} | custom-call | flops 167772160 | bytes 2097152 | tf_op jit(solution)/shard_map/stage/pallas_call | solution.py:486
  17.6 1.5 %collective-permute-done.1.refs_0_.refs_6_ = bf16[1488,128]{1,0:T(8,128)(2,1)S(1)} collective-permute-done((bf16[1488,128]{1,0:T(8,128)(2,1)S(1)}, bf16[1488,128]{1,0:T(8,128)(2,1)S(1)}, u32[]{:S(2)}, u32[]{:S(2)}) %collective-permute-start.1) | collective-permute-done | bytes 380960 | tf_op jit(solution)/shard_map/ppermute | solution.py:51
  19.2 1.8 %collective-permute-start.4 = (bf16[1488,128]{1,0:T(8,128)(2,1)S(1)}, bf16[1488,128]{1,0:T(8,128)(2,1)S(1)}, u32[]{:S(2)}, u32[]{:S(2)}) collective-permute-start(bf16[1488,128]{1,0:T(8,128)(2,1)S(1)} %collective-permute-done.1.refs_0_.refs_6_), channel_id=1, source_target_pairs={{0,4},{1,3},{4,8},{5,1},{8,12},{9,5},{12,14},{13,9},{14,10},{15,13... | collective-permute-start | bytes 1142792 | tf_op jit(solution)/shard_map/ppermute | solution.py:51
  21.0 0.8 %stage.9 = (f32[256,1024]{1,0:T(8,128)S(1)}, f32[128,256]{1,0:T(8,128)S(1)}) custom-call(s32[1]{0:T(128)} %bitcast.me_ref, bf16[1488,128]{1,0:T(8,128)(2,1)S(1)} %collective-permute-done.6.refs_0_.refs_3_, bf16[1488,128]{1,0:T(8,128)(2,1)S(1)} %collective-permute-done.7.refs_1_.refs_5_, ...), custom_call_target="tpu_custom_call", output_to_operand_aliasing={{0}: (10, {}), {1}: (11, {})} | custom-call | flops 167772160 | bytes 2097152 | tf_op jit(solution)/shard_map/stage/pallas_call | solution.py:486
  21.7 1.5 %collective-permute-done.5.refs_1_.block_ref.refs_8_ = bf16[1488,128]{1,0:T(8,128)(2,1)S(1)} collective-permute-done((bf16[1488,128]{1,0:T(8,128)(2,1)S(1)}, bf16[1488,128]{1,0:T(8,128)(2,1)S(1)}, u32[]{:S(2)}, u32[]{:S(2)}) %collective-permute-start.5) | collective-permute-done | bytes 380960 | tf_op jit(solution)/shard_map/ppermute | solution.py:51
  23.3 1.8 %collective-permute-start.8 = (bf16[960,128]{1,0:T(8,128)(2,1)S(1)}, bf16[960,128]{1,0:T(8,128)(2,1)S(1)}, u32[]{:S(2)}, u32[]{:S(2)}) collective-permute-start(bf16[960,128]{1,0:T(8,128)(2,1)S(1)} %get-tuple-element.100), channel_id=1, source_target_pairs={{0,4},{1,3},{4,8},{5,1},{8,12},{9,5},{12,14},{13,9},{14,10},{15,13... | collective-permute-start | bytes 737288 | tf_op jit(solution)/shard_map/ppermute | solution.py:51
  25.1 0.7 %stage.10 = (f32[256,1024]{1,0:T(8,128)S(1)}, f32[128,256]{1,0:T(8,128)S(1)}) custom-call(s32[1]{0:T(128)} %bitcast.me_ref, bf16[1488,128]{1,0:T(8,128)(2,1)S(1)} %collective-permute-done.1.refs_0_.refs_6_, bf16[1488,128]{1,0:T(8,128)(2,1)S(1)} %collective-permute-done.5.refs_1_.block_ref.refs_8_, ...), custom_call_target="tpu_custom_call", output_to_operand_aliasing={{0}: (10, {}), {1}: (11, {})} | custom-call | flops 167772160 | bytes 2097152 | tf_op jit(solution)/shard_map/stage/pallas_call | solution.py:486
  25.9 1.5 %collective-permute-done.4.block_ref.refs_0_.refs_10_ = bf16[1488,128]{1,0:T(8,128)(2,1)S(1)} collective-permute-done((bf16[1488,128]{1,0:T(8,128)(2,1)S(1)}, bf16[1488,128]{1,0:T(8,128)(2,1)S(1)}, u32[]{:S(2)}, u32[]{:S(2)}) %collective-permute-start.4) | collective-permute-done | bytes 380960 | tf_op jit(solution)/shard_map/ppermute | solution.py:51
  27.4 1.8 %collective-permute-start.12 = (bf16[960,128]{1,0:T(8,128)(2,1)S(1)}, bf16[960,128]{1,0:T(8,128)(2,1)S(1)}, u32[]{:S(2)}, u32[]{:S(2)}) collective-permute-start(bf16[960,128]{1,0:T(8,128)(2,1)S(1)} %get-tuple-element.111), channel_id=1, source_target_pairs={{0,4},{1,3},{4,8},{5,1},{8,12},{9,5},{12,14},{13,9},{14,10},{15,13... | collective-permute-start | bytes 737288 | tf_op jit(solution)/shard_map/ppermute | solution.py:51
  29.2 0.8 %stage.11 = (f32[256,1024]{1,0:T(8,128)S(1)}, f32[128,256]{1,0:T(8,128)S(1)}) custom-call(s32[1]{0:T(128)} %bitcast.me_ref, bf16[1488,128]{1,0:T(8,128)(2,1)S(1)} %collective-permute-done.9.refs_0_.refs_7_, bf16[1488,128]{1,0:T(8,128)(2,1)S(1)} %collective-permute-done.10.refs_1_.refs_9_, ...), custom_call_target="tpu_custom_call", output_to_operand_aliasing={{0}: (10, {}), {1}: (11, {})} | custom-call | flops 167772160 | bytes 2097152 | tf_op jit(solution)/shard_map/stage/pallas_call | solution.py:486
  30.0 0.8 %stage.12 = (f32[256,1024]{1,0:T(8,128)S(1)}, f32[128,256]{1,0:T(8,128)S(1)}) custom-call(s32[1]{0:T(128)} %bitcast.me_ref, bf16[1488,128]{1,0:T(8,128)(2,1)S(1)} %collective-permute-done.4.block_ref.refs_0_.refs_10_, bf16[960,128]{1,0:T(8,128)(2,1)S(1)} %collective-permute-done.8.refs_1_, ...), custom_call_target="tpu_custom_call", output_to_operand_aliasing={{0}: (10, {}), {1}: (11, {})} | custom-call | flops 167772160 | bytes 2097152 | tf_op jit(solution)/shard_map/stage/pallas_call | solution.py:486
  30.8 1.8 %collective-permute-start.11 = (bf16[1056,128]{1,0:T(8,128)(2,1)S(1)}, bf16[1056,128]{1,0:T(8,128)(2,1)S(1)}, u32[]{:S(2)}, u32[]{:S(2)}) collective-permute-start(bf16[1056,128]{1,0:T(8,128)(2,1)S(1)} %get-tuple-element.110), channel_id=1, source_target_pairs={{0,4},{1,3},{4,8},{5,1},{8,12},{9,5},{12,14},{13,9},{14,10},{15,13... | collective-permute-start | bytes 811016 | tf_op jit(solution)/shard_map/ppermute | solution.py:51
  32.6 1.1 %collective-permute-done.12.refs_0_ = bf16[960,128]{1,0:T(8,128)(2,1)S(1)} collective-permute-done((bf16[960,128]{1,0:T(8,128)(2,1)S(1)}, bf16[960,128]{1,0:T(8,128)(2,1)S(1)}, u32[]{:S(2)}, u32[]{:S(2)}) %collective-permute-start.12) | collective-permute-done | bytes 245792 | tf_op jit(solution)/shard_map/ppermute | solution.py:51
  33.6 0.4 %collective-permute-done.15.refs_1_ = bf16[960,128]{1,0:T(8,128)(2,1)S(1)} collective-permute-done((bf16[960,128]{1,0:T(8,128)(2,1)S(1)}, bf16[960,128]{1,0:T(8,128)(2,1)S(1)}, u32[]{:S(2)}, u32[]{:S(2)}) %collective-permute-start.15) | collective-permute-done | bytes 245792 | tf_op jit(solution)/shard_map/ppermute | solution.py:55
  34.1 0.8 %stage.13 = (f32[256,1024]{1,0:T(8,128)S(1)}, f32[128,256]{1,0:T(8,128)S(1)}) custom-call(s32[1]{0:T(128)} %bitcast.me_ref, bf16[1488,128]{1,0:T(8,128)(2,1)S(1)} %collective-permute-done.14.refs_0_.refs_11_, bf16[960,128]{1,0:T(8,128)(2,1)S(1)} %collective-permute-done.15.refs_1_, ...), custom_call_target="tpu_custom_call", output_to_operand_aliasing={{0}: (10, {}), {1}: (11, {})} | custom-call | flops 167772160 | bytes 2097152 | tf_op jit(solution)/shard_map/stage/pallas_call | solution.py:486
  34.8 0.0 copy-start
  34.8 0.6 %half_stage.1 = (f32[256,1024]{1,0:T(8,128)S(1)}, f32[128,256]{1,0:T(8,128)S(1)}) custom-call(s32[1]{0:T(128)} %bitcast.me_ref, bf16[960,128]{1,0:T(8,128)(2,1)S(1)} %collective-permute-done.12.refs_0_, bf16[256,5120]{1,0:T(8,128)(2,1)S(1)} %get-tuple-element.73.refs_2_.refs_1_, ...), custom_call_target="tpu_custom_call", output_to_operand_aliasing={{0}: (9, {}), {1}: (10, {})} | custom-call | flops 83886080 | bytes 1048576 | tf_op jit(solution)/shard_map/half_stage/pallas_call | solution.py:549
  35.5 0.0 copy-done
  35.5 1.8 %features.1.unit_ref = f32[128,128]{1,0:T(8,128)S(1)} custom-call(s32[1]{0:T(128)} %bitcast.me_ref, s32[1,2]{1,0:T(1,128)S(1)} %copy-done, bf16[960,128]{1,0:T(8,128)(2,1)S(1)} %collective-permute-done.13.refs_0_, bf16[256,5120]{1,0:T(8,128)(2,1)S(1)} %get-tuple-element.73.refs_2_.refs_1_, bf16[256,5120]{1,0:T(8,128)(2,1)S(1)} %get-tuple-element.74.refs_3_.refs_2_, ...), custom_call_target="tpu_custom_call" | custom-call | flops 1 | bytes 1 | tf_op jit(solution)/shard_map/features/pallas_call | solution.py:560
  37.3 0.2 collective-permute-start.16
  37.5 0.9 %scores.1.best_ref = f32[2,3,8,128]{3,2,1,0:T(8,128)S(1)} custom-call(f32[128,128]{1,0:T(8,128)S(1)} %features.1.unit_ref, bf16[1488,128]{1,0:T(8,128)(2,1)S(1)} %pack.1.refs_0_, bf16[1488,128]{1,0:T(8,128)(2,1)S(1)} %collective-permute-done.2.refs_1_, bf16[1488,128]{1,0:T(8,128)(2,1)S(1)} %collective-permute-done.refs_0_.refs_2_, ...), custom_call_target="tpu_custom_call" | custom-call | flops 4194304 | bytes 2097152 | tf_op jit(solution)/shard_map/scores/pallas_call | solution.py:572
  38.4 0.5 %collective-permute-done.16.block_ref = bf16[1056,128]{1,0:T(8,128)(2,1)S(1)} collective-permute-done((bf16[1056,128]{1,0:T(8,128)(2,1)S(1)}, bf16[1056,128]{1,0:T(8,128)(2,1)S(1)}, u32[]{:S(2)}, u32[]{:S(2)}) %collective-permute-start.16) | collective-permute-done | bytes 270368 | tf_op jit(solution)/shard_map/ppermute | solution.py:55
  38.9 0.8 %last_scores.1 = (f32[2,3]{1,0:T(2,128)}, f32[1,2]{1,0:T(1,128)}) custom-call(f32[128,128]{1,0:T(8,128)S(1)} %features.1.unit_ref, bf16[1056,128]{1,0:T(8,128)(2,1)S(1)} %collective-permute-done.16.block_ref, f32[2,3,8,128]{3,2,1,0:T(8,128)S(1)} %scores.1.best_ref), custom_call_target="tpu_custom_call" | custom-call | tf_op jit(solution)/shard_map/last_scores/pallas_call | solution.py:581
  (19 shorter events, 0.1 us)
Async XLA Ops:
  2.0 3.2 %collective-permute-start.2 = (bf16[1488,128]{1,0:T(8,128)(2,1)S(1)}, bf16[1488,128]{1,0:T(8,128)(2,1)S(1)}, u32[]{:S(2)}, u32[]{:S(2)}) collective-permute-start(bf16[1488,128]{1,0:T(8,128)(2,1)S(1)} %pack.1.refs_0_), channel_id=1, source_target_pairs={{0,1},{1,0},{2,3},{3,2},{4,5},{5,4},{6,7},{7,6},{8,9},{9,8},{10,11... | collective-permute-start | bytes 1142792 | tf_op jit(solution)/shard_map/ppermute | solution.py:55
  2.5 9.0 %collective-permute-start = (bf16[1488,128]{1,0:T(8,128)(2,1)S(1)}, bf16[1488,128]{1,0:T(8,128)(2,1)S(1)}, u32[]{:S(2)}, u32[]{:S(2)}) collective-permute-start(bf16[1488,128]{1,0:T(8,128)(2,1)S(1)} %pack.1.refs_0_), channel_id=1, source_target_pairs={{0,4},{1,3},{4,8},{5,1},{8,12},{9,5},{12,14},{13,9},{14,10},{15,13... | collective-permute-start | bytes 1142792 | tf_op jit(solution)/shard_map/ppermute | solution.py:51
  5.1 9.6 %collective-permute-start.3 = (bf16[1488,128]{1,0:T(8,128)(2,1)S(1)}, bf16[1488,128]{1,0:T(8,128)(2,1)S(1)}, u32[]{:S(2)}, u32[]{:S(2)}) collective-permute-start(bf16[1488,128]{1,0:T(8,128)(2,1)S(1)} %collective-permute-done.2.refs_1_), channel_id=1, source_target_pairs={{0,4},{1,3},{4,8},{5,1},{8,12},{9,5},{12,14},{13,9},{14,10},{15,13... | collective-permute-start | bytes 1142792 | tf_op jit(solution)/shard_map/ppermute | solution.py:51
  11.5 7.7 %collective-permute-start.1 = (bf16[1488,128]{1,0:T(8,128)(2,1)S(1)}, bf16[1488,128]{1,0:T(8,128)(2,1)S(1)}, u32[]{:S(2)}, u32[]{:S(2)}) collective-permute-start(bf16[1488,128]{1,0:T(8,128)(2,1)S(1)} %collective-permute-done.refs_0_.refs_2_), channel_id=1, source_target_pairs={{0,4},{1,3},{4,8},{5,1},{8,12},{9,5},{12,14},{13,9},{14,10},{15,13... | collective-permute-start | bytes 1142792 | tf_op jit(solution)/shard_map/ppermute | solution.py:51
  13.1 7.8 %collective-permute-start.6 = (bf16[1488,128]{1,0:T(8,128)(2,1)S(1)}, bf16[1488,128]{1,0:T(8,128)(2,1)S(1)}, u32[]{:S(2)}, u32[]{:S(2)}) collective-permute-start(bf16[1488,128]{1,0:T(8,128)(2,1)S(1)} %collective-permute-done.refs_0_.refs_2_), channel_id=1, source_target_pairs={{0,1},{1,0},{2,3},{3,2},{4,5},{5,4},{6,7},{7,6},{8,9},{9,8},{10,11... | collective-permute-start | bytes 1142792 | tf_op jit(solution)/shard_map/ppermute | solution.py:55
  14.8 6.2 %collective-permute-start.7 = (bf16[1488,128]{1,0:T(8,128)(2,1)S(1)}, bf16[1488,128]{1,0:T(8,128)(2,1)S(1)}, u32[]{:S(2)}, u32[]{:S(2)}) collective-permute-start(bf16[1488,128]{1,0:T(8,128)(2,1)S(1)} %collective-permute-done.3.refs_1_.refs_4_), channel_id=1, source_target_pairs={{0,1},{1,0},{2,3},{3,2},{4,5},{5,4},{6,7},{7,6},{8,9},{9,8},{10,11... | collective-permute-start | bytes 1142792 | tf_op jit(solution)/shard_map/ppermute | solution.py:55
  14.8 8.5 %collective-permute-start.5 = (bf16[1488,128]{1,0:T(8,128)(2,1)S(1)}, bf16[1488,128]{1,0:T(8,128)(2,1)S(1)}, u32[]{:S(2)}, u32[]{:S(2)}) collective-permute-start(bf16[1488,128]{1,0:T(8,128)(2,1)S(1)} %collective-permute-done.3.refs_1_.refs_4_), channel_id=1, source_target_pairs={{0,4},{1,3},{4,8},{5,1},{8,12},{9,5},{12,14},{13,9},{14,10},{15,13... | collective-permute-start | bytes 1142792 | tf_op jit(solution)/shard_map/ppermute | solution.py:51
  19.2 8.2 %collective-permute-start.4 = (bf16[1488,128]{1,0:T(8,128)(2,1)S(1)}, bf16[1488,128]{1,0:T(8,128)(2,1)S(1)}, u32[]{:S(2)}, u32[]{:S(2)}) collective-permute-start(bf16[1488,128]{1,0:T(8,128)(2,1)S(1)} %collective-permute-done.1.refs_0_.refs_6_), channel_id=1, source_target_pairs={{0,4},{1,3},{4,8},{5,1},{8,12},{9,5},{12,14},{13,9},{14,10},{15,13... | collective-permute-start | bytes 1142792 | tf_op jit(solution)/shard_map/ppermute | solution.py:51
  21.0 8.3 %collective-permute-start.9 = (bf16[1488,128]{1,0:T(8,128)(2,1)S(1)}, bf16[1488,128]{1,0:T(8,128)(2,1)S(1)}, u32[]{:S(2)}, u32[]{:S(2)}) collective-permute-start(bf16[1488,128]{1,0:T(8,128)(2,1)S(1)} %collective-permute-done.1.refs_0_.refs_6_), channel_id=1, source_target_pairs={{0,1},{1,0},{2,3},{3,2},{4,5},{5,4},{6,7},{7,6},{8,9},{9,8},{10,11... | collective-permute-start | bytes 1142792 | tf_op jit(solution)/shard_map/ppermute | solution.py:55
  23.3 5.9 %collective-permute-start.10 = (bf16[1488,128]{1,0:T(8,128)(2,1)S(1)}, bf16[1488,128]{1,0:T(8,128)(2,1)S(1)}, u32[]{:S(2)}, u32[]{:S(2)}) collective-permute-start(bf16[1488,128]{1,0:T(8,128)(2,1)S(1)} %collective-permute-done.5.refs_1_.block_ref.refs_8_), channel_id=1, source_target_pairs={{0,1},{1,0},{2,3},{3,2},{4,5},{5,4},{6,7},{7,6},{8,9},{9,8},{10,11... | collective-permute-start | bytes 1142792 | tf_op jit(solution)/shard_map/ppermute | solution.py:55
  23.3 6.7 %collective-permute-start.8 = (bf16[960,128]{1,0:T(8,128)(2,1)S(1)}, bf16[960,128]{1,0:T(8,128)(2,1)S(1)}, u32[]{:S(2)}, u32[]{:S(2)}) collective-permute-start(bf16[960,128]{1,0:T(8,128)(2,1)S(1)} %get-tuple-element.100), channel_id=1, source_target_pairs={{0,4},{1,3},{4,8},{5,1},{8,12},{9,5},{12,14},{13,9},{14,10},{15,13... | collective-permute-start | bytes 737288 | tf_op jit(solution)/shard_map/ppermute | solution.py:51
  27.4 6.2 %collective-permute-start.12 = (bf16[960,128]{1,0:T(8,128)(2,1)S(1)}, bf16[960,128]{1,0:T(8,128)(2,1)S(1)}, u32[]{:S(2)}, u32[]{:S(2)}) collective-permute-start(bf16[960,128]{1,0:T(8,128)(2,1)S(1)} %get-tuple-element.111), channel_id=1, source_target_pairs={{0,4},{1,3},{4,8},{5,1},{8,12},{9,5},{12,14},{13,9},{14,10},{15,13... | collective-permute-start | bytes 737288 | tf_op jit(solution)/shard_map/ppermute | solution.py:51
  29.2 4.4 %collective-permute-start.14 = (bf16[1488,128]{1,0:T(8,128)(2,1)S(1)}, bf16[1488,128]{1,0:T(8,128)(2,1)S(1)}, u32[]{:S(2)}, u32[]{:S(2)}) collective-permute-start(bf16[1488,128]{1,0:T(8,128)(2,1)S(1)} %collective-permute-done.4.block_ref.refs_0_.refs_10_), channel_id=1, source_target_pairs={{0,1},{1,0},{2,3},{3,2},{4,5},{5,4},{6,7},{7,6},{8,9},{9,8},{10,11... | collective-permute-start | bytes 1142792 | tf_op jit(solution)/shard_map/ppermute | solution.py:55
  30.8 6.5 %collective-permute-start.11 = (bf16[1056,128]{1,0:T(8,128)(2,1)S(1)}, bf16[1056,128]{1,0:T(8,128)(2,1)S(1)}, u32[]{:S(2)}, u32[]{:S(2)}) collective-permute-start(bf16[1056,128]{1,0:T(8,128)(2,1)S(1)} %get-tuple-element.110), channel_id=1, source_target_pairs={{0,4},{1,3},{4,8},{5,1},{8,12},{9,5},{12,14},{13,9},{14,10},{15,13... | collective-permute-start | bytes 811016 | tf_op jit(solution)/shard_map/ppermute | solution.py:51
  32.6 1.5 %collective-permute-start.15 = (bf16[960,128]{1,0:T(8,128)(2,1)S(1)}, bf16[960,128]{1,0:T(8,128)(2,1)S(1)}, u32[]{:S(2)}, u32[]{:S(2)}) collective-permute-start(bf16[960,128]{1,0:T(8,128)(2,1)S(1)} %collective-permute-done.8.refs_1_), channel_id=1, source_target_pairs={{0,1},{1,0},{2,3},{3,2},{4,5},{5,4},{6,7},{7,6},{8,9},{9,8},{10,11... | collective-permute-start | bytes 737288 | tf_op jit(solution)/shard_map/ppermute | solution.py:55
  33.6 1.8 %collective-permute-start.13 = (bf16[960,128]{1,0:T(8,128)(2,1)S(1)}, bf16[960,128]{1,0:T(8,128)(2,1)S(1)}, u32[]{:S(2)}, u32[]{:S(2)}) collective-permute-start(bf16[960,128]{1,0:T(8,128)(2,1)S(1)} %collective-permute-done.12.refs_0_), channel_id=1, source_target_pairs={{0,1},{1,0},{2,3},{3,2},{4,5},{5,4},{6,7},{7,6},{8,9},{9,8},{10,11... | collective-permute-start | bytes 737288 | tf_op jit(solution)/shard_map/ppermute | solution.py:55
  34.8 0.7 %copy-start = (s32[1,2]{1,0:T(1,128)S(1)}, s32[1,2]{1,0:T(1,128)}, u32[]{:S(2)}) copy-start(s32[1,2]{1,0:T(1,128)} %counts_ref.1) | copy-start | bytes 28
  37.3 1.6 %collective-permute-start.16 = (bf16[1056,128]{1,0:T(8,128)(2,1)S(1)}, bf16[1056,128]{1,0:T(8,128)(2,1)S(1)}, u32[]{:S(2)}, u32[]{:S(2)}) collective-permute-start(bf16[1056,128]{1,0:T(8,128)(2,1)S(1)} %collective-permute-done.11.refs_12_), channel_id=1, source_target_pairs={{0,1},{1,0},{2,3},{3,2},{4,5},{5,4},{6,7},{7,6},{8,9},{9,8},{10,11... | collective-permute-start | bytes 811016 | tf_op jit(solution)/shard_map/ppermute | solution.py:55

commit v16 on v15

--- a/solution.py
+++ b/solution.py
@@ -526,10 +526,9 @@
             blocks += [second, crossed[1]]
         else:
             first, tails = split(first, tail)
+            tails, sums = tie((tails, sums))
         first = hop(first)
         sums = stage(k, held, sums)
-        if k == half - 1:
-            tails, sums = tie((tails, sums))
         first, sums = tie((first, sums))
         if k == half - 2:
             second, tail = split(second)

time: 39.9 us -> 39.6 us (level)
  waiting for transfers between devices: 7.6 us -> 7.09 us
    ppermute x9, waiting for transfers between devices: 0.98 us -> 0.42 us  [other_core(): lax.ppermute(value, 'dp', [(d, d ^ 1) for d in range(2 * RING_CHIPS)])]
  transfers between devices with their start and end apart: 17 -> 17, of which waited for: 7 -> 7; matrix products, arithmetic and copies ran while one was open for 0% -> 0% of each run, Pallas kernels for 33% -> 34%
where the time goes in v16:
time: 39.6 us; the launch traced here: 39.4 us
  starting transfers between devices  16.1 us (41%)
  Pallas kernels  15.4 us (39%)
  waiting for transfers between devices  7.09 us (18%)
  between operations  0.79 us (2%)
    ppermute x8, starting transfers between devices, hop(): return lax.ppermute(value, 'dp', pairs)  15.1 us
    ppermute x8, waiting for transfers between devices, hop(): return lax.ppermute(value, 'dp', pairs)  6.66 us
    pallas_call x7, Pallas kernels, stage(): pl.pallas_call(functools.partial(stage_kernel, away, first), out_shape=[j...  5.25 us
    pallas_call x1, Pallas kernels, shards(): pl.pallas_call(local_kernel, out_shape=[jax.ShapeDtypeStruct(a.shape, a.d...  4.69 us
    pallas_call x1, Pallas kernels, shards(): pl.pallas_call(functools.partial(feature_kernel, half), out_shape=jax.Sha...  1.78 us
    pallas_call x1, Pallas kernels, shards(): pl.pallas_call(pack_kernel, out_shape=jax.ShapeDtypeStruct((3 * rows + (L...  1.35 us
    ppermute x9, starting transfers between devices, other_core(): lax.ppermute(value, 'dp', [(d, d ^ 1) for d in range(2 * RING_CHIPS)])  1.04 us
    pallas_call x1, Pallas kernels, shards(): pl.pallas_call(functools.partial(score_kernel, len(blocks), count), out_s...  0.86 us
  transfers between devices with their start and end apart: 17, of which 7 were waited for; matrix products, arithmetic and copies ran while one was open for 0% of the time, Pallas kernels for 34%

profile of v16, /device:TPU:0, one launch (start us, length us, event | category | flops | bytes accessed | tf_op | source)
XLA Modules:
  0.0 39.4 jit_solution(14628274558296298344)
XLA Ops:
  0.6 1.3 %pack.1.refs_0_ = bf16[1488,128]{1,0:T(8,128)(2,1)S(1)} custom-call(s32[1]{0:T(128)} %bitcast.me_ref, bf16[160,128]{1,0:T(8,128)(2,1)} %bitcast.14, bf16[8,8192]{1,0:T(8,128)(2,1)} %refs_1_.2, bf16[320,128]{1,0:T(8,128)(2,1)} %refs_2_.2, bf16[320,128]{1,0:T(8,128)(2,1)} %bitcast.13, bf16[320,128]{1,0:T(8,128)(2,1)} %refs_4_.2, f32[40,128]{1,0:T(8,128)} %bitcast.11, ...), custom_call_target="tpu_custom_call" | custom-call | tf_op jit(solution)/shard_map/pack/pallas_call | solution.py:437
  2.0 0.5 %collective-permute-start.2 = (bf16[1488,128]{1,0:T(8,128)(2,1)S(1)}, bf16[1488,128]{1,0:T(8,128)(2,1)S(1)}, u32[]{:S(2)}, u32[]{:S(2)}) collective-permute-start(bf16[1488,128]{1,0:T(8,128)(2,1)S(1)} %pack.1.refs_0_), channel_id=1, source_target_pairs={{0,1},{1,0},{2,3},{3,2},{4,5},{5,4},{6,7},{7,6},{8,9},{9,8},{10,11... | collective-permute-start | bytes 1142792 | tf_op jit(solution)/shard_map/ppermute | solution.py:55
  2.5 2.6 %collective-permute-start = (bf16[1488,128]{1,0:T(8,128)(2,1)S(1)}, bf16[1488,128]{1,0:T(8,128)(2,1)S(1)}, u32[]{:S(2)}, u32[]{:S(2)}) collective-permute-start(bf16[1488,128]{1,0:T(8,128)(2,1)S(1)} %pack.1.refs_0_), channel_id=1, source_target_pairs={{0,4},{1,3},{4,8},{5,1},{8,12},{9,5},{12,14},{13,9},{14,10},{15,13... | collective-permute-start | bytes 1142792 | tf_op jit(solution)/shard_map/ppermute | solution.py:51
  5.1 0.0 collective-permute-done.2.refs_1_
  5.1 1.6 %collective-permute-start.3 = (bf16[1488,128]{1,0:T(8,128)(2,1)S(1)}, bf16[1488,128]{1,0:T(8,128)(2,1)S(1)}, u32[]{:S(2)}, u32[]{:S(2)}) collective-permute-start(bf16[1488,128]{1,0:T(8,128)(2,1)S(1)} %collective-permute-done.2.refs_1_), channel_id=1, source_target_pairs={{0,4},{1,3},{4,8},{5,1},{8,12},{9,5},{12,14},{13,9},{14,10},{15,13... | collective-permute-start | bytes 1142792 | tf_op jit(solution)/shard_map/ppermute | solution.py:51
  6.8 4.7 %local_products.1 = (bf16[256,5120]{1,0:T(8,128)(2,1)S(1)}, bf16[256,5120]{1,0:T(8,128)(2,1)S(1)}, bf16[256,5120]{1,0:T(8,128)(2,1)S(1)}, bf16[256,2560]{1,0:T(8...) custom-call(bf16[256,5120]{1,0:T(8,128)(2,1)} %refs_0_.1, ...), custom_call_target="tpu_custom_call" | custom-call | flops 1006632960 | bytes 14680064 | tf_op jit(solution)/shard_map/local_products/pallas_call | solution.py:460
  11.5 1.6 %collective-permute-start.1 = (bf16[1488,128]{1,0:T(8,128)(2,1)S(1)}, bf16[1488,128]{1,0:T(8,128)(2,1)S(1)}, u32[]{:S(2)}, u32[]{:S(2)}) collective-permute-start(bf16[1488,128]{1,0:T(8,128)(2,1)S(1)} %collective-permute-done.refs_0_.refs_2_), channel_id=1, source_target_pairs={{0,4},{1,3},{4,8},{5,1},{8,12},{9,5},{12,14},{13,9},{14,10},{15,13... | collective-permute-start | bytes 1142792 | tf_op jit(solution)/shard_map/ppermute | solution.py:51
  13.1 0.7 %stage.7 = (f32[256,1024]{1,0:T(8,128)S(1)}, f32[128,256]{1,0:T(8,128)S(1)}) custom-call(s32[1]{0:T(128)} %bitcast.me_ref, bf16[1488,128]{1,0:T(8,128)(2,1)S(1)} %pack.1.refs_0_, bf16[1488,128]{1,0:T(8,128)(2,1)S(1)} %collective-permute-done.2.refs_1_, bf16[256,5120]{1,0:T(8,128)(2,1)S(1)} %get-tuple-element.73.refs_2_.refs_1_, ...), custom_call_target="tpu_custom_call" | custom-call | flops 167772160 | bytes 2097152 | tf_op jit(solution)/shard_map/stage/pallas_call | solution.py:486
  13.8 1.0 %collective-permute-done.3.refs_1_.refs_4_ = bf16[1488,128]{1,0:T(8,128)(2,1)S(1)} collective-permute-done((bf16[1488,128]{1,0:T(8,128)(2,1)S(1)}, bf16[1488,128]{1,0:T(8,128)(2,1)S(1)}, u32[]{:S(2)}, u32[]{:S(2)}) %collective-permute-start.3) | collective-permute-done | bytes 380960 | tf_op jit(solution)/shard_map/ppermute | solution.py:51
  14.8 2.1 %collective-permute-start.5 = (bf16[1488,128]{1,0:T(8,128)(2,1)S(1)}, bf16[1488,128]{1,0:T(8,128)(2,1)S(1)}, u32[]{:S(2)}, u32[]{:S(2)}) collective-permute-start(bf16[1488,128]{1,0:T(8,128)(2,1)S(1)} %collective-permute-done.3.refs_1_.refs_4_), channel_id=1, source_target_pairs={{0,4},{1,3},{4,8},{5,1},{8,12},{9,5},{12,14},{13,9},{14,10},{15,13... | collective-permute-start | bytes 1142792 | tf_op jit(solution)/shard_map/ppermute | solution.py:51
  16.9 0.8 %stage.8 = (f32[256,1024]{1,0:T(8,128)S(1)}, f32[128,256]{1,0:T(8,128)S(1)}) custom-call(s32[1]{0:T(128)} %bitcast.me_ref, bf16[1488,128]{1,0:T(8,128)(2,1)S(1)} %collective-permute-done.refs_0_.refs_2_, bf16[1488,128]{1,0:T(8,128)(2,1)S(1)} %collective-permute-done.3.refs_1_.refs_4_, ...), custom_call_target="tpu_custom_call", output_to_operand_aliasing={{0}: (10, {}), {1}: (11, {})} | custom-call | flops 167772160 | bytes 2097152 | tf_op jit(solution)/shard_map/stage/pallas_call | solution.py:486
  17.6 1.5 %collective-permute-done.1.refs_0_.refs_6_ = bf16[1488,128]{1,0:T(8,128)(2,1)S(1)} collective-permute-done((bf16[1488,128]{1,0:T(8,128)(2,1)S(1)}, bf16[1488,128]{1,0:T(8,128)(2,1)S(1)}, u32[]{:S(2)}, u32[]{:S(2)}) %collective-permute-start.1) | collective-permute-done | bytes 380960 | tf_op jit(solution)/shard_map/ppermute | solution.py:51
  19.2 1.8 %collective-permute-start.4 = (bf16[1488,128]{1,0:T(8,128)(2,1)S(1)}, bf16[1488,128]{1,0:T(8,128)(2,1)S(1)}, u32[]{:S(2)}, u32[]{:S(2)}) collective-permute-start(bf16[1488,128]{1,0:T(8,128)(2,1)S(1)} %collective-permute-done.1.refs_0_.refs_6_), channel_id=1, source_target_pairs={{0,4},{1,3},{4,8},{5,1},{8,12},{9,5},{12,14},{13,9},{14,10},{15,13... | collective-permute-start | bytes 1142792 | tf_op jit(solution)/shard_map/ppermute | solution.py:51
  21.0 0.8 %stage.9 = (f32[256,1024]{1,0:T(8,128)S(1)}, f32[128,256]{1,0:T(8,128)S(1)}) custom-call(s32[1]{0:T(128)} %bitcast.me_ref, bf16[1488,128]{1,0:T(8,128)(2,1)S(1)} %collective-permute-done.6.refs_0_.refs_3_, bf16[1488,128]{1,0:T(8,128)(2,1)S(1)} %collective-permute-done.7.refs_1_.refs_5_, ...), custom_call_target="tpu_custom_call", output_to_operand_aliasing={{0}: (10, {}), {1}: (11, {})} | custom-call | flops 167772160 | bytes 2097152 | tf_op jit(solution)/shard_map/stage/pallas_call | solution.py:486
  21.7 1.5 %collective-permute-done.5.refs_1_.block_ref.refs_8_ = bf16[1488,128]{1,0:T(8,128)(2,1)S(1)} collective-permute-done((bf16[1488,128]{1,0:T(8,128)(2,1)S(1)}, bf16[1488,128]{1,0:T(8,128)(2,1)S(1)}, u32[]{:S(2)}, u32[]{:S(2)}) %collective-permute-start.5) | collective-permute-done | bytes 380960 | tf_op jit(solution)/shard_map/ppermute | solution.py:51
  23.3 1.8 %collective-permute-start.8 = (bf16[960,128]{1,0:T(8,128)(2,1)S(1)}, bf16[960,128]{1,0:T(8,128)(2,1)S(1)}, u32[]{:S(2)}, u32[]{:S(2)}) collective-permute-start(bf16[960,128]{1,0:T(8,128)(2,1)S(1)} %get-tuple-element.100), channel_id=1, source_target_pairs={{0,4},{1,3},{4,8},{5,1},{8,12},{9,5},{12,14},{13,9},{14,10},{15,13... | collective-permute-start | bytes 737288 | tf_op jit(solution)/shard_map/ppermute | solution.py:51
  25.1 0.7 %stage.10 = (f32[256,1024]{1,0:T(8,128)S(1)}, f32[128,256]{1,0:T(8,128)S(1)}) custom-call(s32[1]{0:T(128)} %bitcast.me_ref, bf16[1488,128]{1,0:T(8,128)(2,1)S(1)} %collective-permute-done.1.refs_0_.refs_6_, bf16[1488,128]{1,0:T(8,128)(2,1)S(1)} %collective-permute-done.5.refs_1_.block_ref.refs_8_, ...), custom_call_target="tpu_custom_call", output_to_operand_aliasing={{0}: (10, {}), {1}: (11, {})} | custom-call | flops 167772160 | bytes 2097152 | tf_op jit(solution)/shard_map/stage/pallas_call | solution.py:486
  25.9 1.5 %collective-permute-done.4.block_ref.refs_0_.refs_10_ = bf16[1488,128]{1,0:T(8,128)(2,1)S(1)} collective-permute-done((bf16[1488,128]{1,0:T(8,128)(2,1)S(1)}, bf16[1488,128]{1,0:T(8,128)(2,1)S(1)}, u32[]{:S(2)}, u32[]{:S(2)}) %collective-permute-start.4) | collective-permute-done | bytes 380960 | tf_op jit(solution)/shard_map/ppermute | solution.py:51
  27.4 1.8 %collective-permute-start.12 = (bf16[960,128]{1,0:T(8,128)(2,1)S(1)}, bf16[960,128]{1,0:T(8,128)(2,1)S(1)}, u32[]{:S(2)}, u32[]{:S(2)}) collective-permute-start(bf16[960,128]{1,0:T(8,128)(2,1)S(1)} %get-tuple-element.108), channel_id=1, source_target_pairs={{0,4},{1,3},{4,8},{5,1},{8,12},{9,5},{12,14},{13,9},{14,10},{15,13... | collective-permute-start | bytes 737288 | tf_op jit(solution)/shard_map/ppermute | solution.py:51
  29.2 0.8 %stage.11 = (f32[256,1024]{1,0:T(8,128)S(1)}, f32[128,256]{1,0:T(8,128)S(1)}) custom-call(s32[1]{0:T(128)} %bitcast.me_ref, bf16[1488,128]{1,0:T(8,128)(2,1)S(1)} %collective-permute-done.9.refs_0_.refs_7_, bf16[1488,128]{1,0:T(8,128)(2,1)S(1)} %collective-permute-done.10.refs_1_.refs_9_, ...), custom_call_target="tpu_custom_call", output_to_operand_aliasing={{0}: (10, {}), {1}: (11, {})} | custom-call | flops 167772160 | bytes 2097152 | tf_op jit(solution)/shard_map/stage/pallas_call | solution.py:486
  30.0 1.7 %collective-permute-start.11 = (bf16[1056,128]{1,0:T(8,128)(2,1)S(1)}, bf16[1056,128]{1,0:T(8,128)(2,1)S(1)}, u32[]{:S(2)}, u32[]{:S(2)}) collective-permute-start(bf16[1056,128]{1,0:T(8,128)(2,1)S(1)} %get-tuple-element.107), channel_id=1, source_target_pairs={{0,4},{1,3},{4,8},{5,1},{8,12},{9,5},{12,14},{13,9},{14,10},{15,13... | collective-permute-start | bytes 811016 | tf_op jit(solution)/shard_map/ppermute | solution.py:51
  31.8 0.8 %stage.12 = (f32[256,1024]{1,0:T(8,128)S(1)}, f32[128,256]{1,0:T(8,128)S(1)}) custom-call(s32[1]{0:T(128)} %bitcast.me_ref, bf16[1488,128]{1,0:T(8,128)(2,1)S(1)} %collective-permute-done.4.block_ref.refs_0_.refs_10_, bf16[960,128]{1,0:T(8,128)(2,1)S(1)} %collective-permute-done.8.refs_1_, ...), custom_call_target="tpu_custom_call", output_to_operand_aliasing={{0}: (10, {}), {1}: (11, {})} | custom-call | flops 167772160 | bytes 2097152 | tf_op jit(solution)/shard_map/stage/pallas_call | solution.py:486
  32.5 1.1 %collective-permute-done.12.refs_0_ = bf16[960,128]{1,0:T(8,128)(2,1)S(1)} collective-permute-done((bf16[960,128]{1,0:T(8,128)(2,1)S(1)}, bf16[960,128]{1,0:T(8,128)(2,1)S(1)}, u32[]{:S(2)}, u32[]{:S(2)}) %collective-permute-start.12) | collective-permute-done | bytes 245792 | tf_op jit(solution)/shard_map/ppermute | solution.py:51
  33.7 0.8 %stage.13 = (f32[256,1024]{1,0:T(8,128)S(1)}, f32[128,256]{1,0:T(8,128)S(1)}) custom-call(s32[1]{0:T(128)} %bitcast.me_ref, bf16[1488,128]{1,0:T(8,128)(2,1)S(1)} %collective-permute-done.14.refs_0_.refs_11_, bf16[960,128]{1,0:T(8,128)(2,1)S(1)} %collective-permute-done.15.refs_1_, ...), custom_call_target="tpu_custom_call", output_to_operand_aliasing={{0}: (10, {}), {1}: (11, {})} | custom-call | flops 167772160 | bytes 2097152 | tf_op jit(solution)/shard_map/stage/pallas_call | solution.py:486
  34.4 0.0 copy-start
  34.4 0.6 %half_stage.1 = (f32[256,1024]{1,0:T(8,128)S(1)}, f32[128,256]{1,0:T(8,128)S(1)}) custom-call(s32[1]{0:T(128)} %bitcast.me_ref, bf16[960,128]{1,0:T(8,128)(2,1)S(1)} %collective-permute-done.12.refs_0_, bf16[256,5120]{1,0:T(8,128)(2,1)S(1)} %get-tuple-element.73.refs_2_.refs_1_, ...), custom_call_target="tpu_custom_call", output_to_operand_aliasing={{0}: (9, {}), {1}: (10, {})} | custom-call | flops 83886080 | bytes 1048576 | tf_op jit(solution)/shard_map/half_stage/pallas_call | solution.py:548
  35.1 0.1 collective-permute-done.13.refs_0_
  35.2 1.8 %features.1.unit_ref = f32[128,128]{1,0:T(8,128)S(1)} custom-call(s32[1]{0:T(128)} %bitcast.me_ref, s32[1,2]{1,0:T(1,128)S(1)} %copy-done, bf16[960,128]{1,0:T(8,128)(2,1)S(1)} %collective-permute-done.13.refs_0_, bf16[256,5120]{1,0:T(8,128)(2,1)S(1)} %get-tuple-element.73.refs_2_.refs_1_, bf16[256,5120]{1,0:T(8,128)(2,1)S(1)} %get-tuple-element.74.refs_3_.refs_2_, ...), custom_call_target="tpu_custom_call" | custom-call | flops 1 | bytes 1 | tf_op jit(solution)/shard_map/features/pallas_call | solution.py:559
  37.0 0.5 %collective-permute-start.16 = (bf16[1056,128]{1,0:T(8,128)(2,1)S(1)}, bf16[1056,128]{1,0:T(8,128)(2,1)S(1)}, u32[]{:S(2)}, u32[]{:S(2)}) collective-permute-start(bf16[1056,128]{1,0:T(8,128)(2,1)S(1)} %collective-permute-done.11.refs_12_), channel_id=1, source_target_pairs={{0,1},{1,0},{2,3},{3,2},{4,5},{5,4},{6,7},{7,6},{8,9},{9,8},{10,11... | collective-permute-start | bytes 811016 | tf_op jit(solution)/shard_map/ppermute | solution.py:55
  37.5 0.9 %scores.1.best_ref = f32[2,3,8,128]{3,2,1,0:T(8,128)S(1)} custom-call(f32[128,128]{1,0:T(8,128)S(1)} %features.1.unit_ref, bf16[1488,128]{1,0:T(8,128)(2,1)S(1)} %pack.1.refs_0_, bf16[1488,128]{1,0:T(8,128)(2,1)S(1)} %collective-permute-done.2.refs_1_, bf16[1488,128]{1,0:T(8,128)(2,1)S(1)} %collective-permute-done.refs_0_.refs_2_, ...), custom_call_target="tpu_custom_call" | custom-call | flops 4194304 | bytes 2097152 | tf_op jit(solution)/shard_map/scores/pallas_call | solution.py:571
  38.3 0.3 collective-permute-done.16.block_ref
  38.6 0.8 %last_scores.1 = (f32[2,3]{1,0:T(2,128)}, f32[1,2]{1,0:T(1,128)}) custom-call(f32[128,128]{1,0:T(8,128)S(1)} %features.1.unit_ref, bf16[1056,128]{1,0:T(8,128)(2,1)S(1)} %collective-permute-done.16.block_ref, f32[2,3,8,128]{3,2,1,0:T(8,128)S(1)} %scores.1.best_ref), custom_call_target="tpu_custom_call" | custom-call | tf_op jit(solution)/shard_map/last_scores/pallas_call | solution.py:580
  (19 shorter events, 0.1 us)
Async XLA Ops:
  2.0 3.2 %collective-permute-start.2 = (bf16[1488,128]{1,0:T(8,128)(2,1)S(1)}, bf16[1488,128]{1,0:T(8,128)(2,1)S(1)}, u32[]{:S(2)}, u32[]{:S(2)}) collective-permute-start(bf16[1488,128]{1,0:T(8,128)(2,1)S(1)} %pack.1.refs_0_), channel_id=1, source_target_pairs={{0,1},{1,0},{2,3},{3,2},{4,5},{5,4},{6,7},{7,6},{8,9},{9,8},{10,11... | collective-permute-start | bytes 1142792 | tf_op jit(solution)/shard_map/ppermute | solution.py:55
  2.5 9.0 %collective-permute-start = (bf16[1488,128]{1,0:T(8,128)(2,1)S(1)}, bf16[1488,128]{1,0:T(8,128)(2,1)S(1)}, u32[]{:S(2)}, u32[]{:S(2)}) collective-permute-start(bf16[1488,128]{1,0:T(8,128)(2,1)S(1)} %pack.1.refs_0_), channel_id=1, source_target_pairs={{0,4},{1,3},{4,8},{5,1},{8,12},{9,5},{12,14},{13,9},{14,10},{15,13... | collective-permute-start | bytes 1142792 | tf_op jit(solution)/shard_map/ppermute | solution.py:51
  5.1 9.6 %collective-permute-start.3 = (bf16[1488,128]{1,0:T(8,128)(2,1)S(1)}, bf16[1488,128]{1,0:T(8,128)(2,1)S(1)}, u32[]{:S(2)}, u32[]{:S(2)}) collective-permute-start(bf16[1488,128]{1,0:T(8,128)(2,1)S(1)} %collective-permute-done.2.refs_1_), channel_id=1, source_target_pairs={{0,4},{1,3},{4,8},{5,1},{8,12},{9,5},{12,14},{13,9},{14,10},{15,13... | collective-permute-start | bytes 1142792 | tf_op jit(solution)/shard_map/ppermute | solution.py:51
  11.5 7.7 %collective-permute-start.1 = (bf16[1488,128]{1,0:T(8,128)(2,1)S(1)}, bf16[1488,128]{1,0:T(8,128)(2,1)S(1)}, u32[]{:S(2)}, u32[]{:S(2)}) collective-permute-start(bf16[1488,128]{1,0:T(8,128)(2,1)S(1)} %collective-permute-done.refs_0_.refs_2_), channel_id=1, source_target_pairs={{0,4},{1,3},{4,8},{5,1},{8,12},{9,5},{12,14},{13,9},{14,10},{15,13... | collective-permute-start | bytes 1142792 | tf_op jit(solution)/shard_map/ppermute | solution.py:51
  13.1 7.8 %collective-permute-start.6 = (bf16[1488,128]{1,0:T(8,128)(2,1)S(1)}, bf16[1488,128]{1,0:T(8,128)(2,1)S(1)}, u32[]{:S(2)}, u32[]{:S(2)}) collective-permute-start(bf16[1488,128]{1,0:T(8,128)(2,1)S(1)} %collective-permute-done.refs_0_.refs_2_), channel_id=1, source_target_pairs={{0,1},{1,0},{2,3},{3,2},{4,5},{5,4},{6,7},{7,6},{8,9},{9,8},{10,11... | collective-permute-start | bytes 1142792 | tf_op jit(solution)/shard_map/ppermute | solution.py:55
  14.8 6.2 %collective-permute-start.7 = (bf16[1488,128]{1,0:T(8,128)(2,1)S(1)}, bf16[1488,128]{1,0:T(8,128)(2,1)S(1)}, u32[]{:S(2)}, u32[]{:S(2)}) collective-permute-start(bf16[1488,128]{1,0:T(8,128)(2,1)S(1)} %collective-permute-done.3.refs_1_.refs_4_), channel_id=1, source_target_pairs={{0,1},{1,0},{2,3},{3,2},{4,5},{5,4},{6,7},{7,6},{8,9},{9,8},{10,11... | collective-permute-start | bytes 1142792 | tf_op jit(solution)/shard_map/ppermute | solution.py:55
  14.8 8.5 %collective-permute-start.5 = (bf16[1488,128]{1,0:T(8,128)(2,1)S(1)}, bf16[1488,128]{1,0:T(8,128)(2,1)S(1)}, u32[]{:S(2)}, u32[]{:S(2)}) collective-permute-start(bf16[1488,128]{1,0:T(8,128)(2,1)S(1)} %collective-permute-done.3.refs_1_.refs_4_), channel_id=1, source_target_pairs={{0,4},{1,3},{4,8},{5,1},{8,12},{9,5},{12,14},{13,9},{14,10},{15,13... | collective-permute-start | bytes 1142792 | tf_op jit(solution)/shard_map/ppermute | solution.py:51
  19.2 8.2 %collective-permute-start.4 = (bf16[1488,128]{1,0:T(8,128)(2,1)S(1)}, bf16[1488,128]{1,0:T(8,128)(2,1)S(1)}, u32[]{:S(2)}, u32[]{:S(2)}) collective-permute-start(bf16[1488,128]{1,0:T(8,128)(2,1)S(1)} %collective-permute-done.1.refs_0_.refs_6_), channel_id=1, source_target_pairs={{0,4},{1,3},{4,8},{5,1},{8,12},{9,5},{12,14},{13,9},{14,10},{15,13... | collective-permute-start | bytes 1142792 | tf_op jit(solution)/shard_map/ppermute | solution.py:51
  21.0 8.3 %collective-permute-start.9 = (bf16[1488,128]{1,0:T(8,128)(2,1)S(1)}, bf16[1488,128]{1,0:T(8,128)(2,1)S(1)}, u32[]{:S(2)}, u32[]{:S(2)}) collective-permute-start(bf16[1488,128]{1,0:T(8,128)(2,1)S(1)} %collective-permute-done.1.refs_0_.refs_6_), channel_id=1, source_target_pairs={{0,1},{1,0},{2,3},{3,2},{4,5},{5,4},{6,7},{7,6},{8,9},{9,8},{10,11... | collective-permute-start | bytes 1142792 | tf_op jit(solution)/shard_map/ppermute | solution.py:55
  23.3 5.9 %collective-permute-start.10 = (bf16[1488,128]{1,0:T(8,128)(2,1)S(1)}, bf16[1488,128]{1,0:T(8,128)(2,1)S(1)}, u32[]{:S(2)}, u32[]{:S(2)}) collective-permute-start(bf16[1488,128]{1,0:T(8,128)(2,1)S(1)} %collective-permute-done.5.refs_1_.block_ref.refs_8_), channel_id=1, source_target_pairs={{0,1},{1,0},{2,3},{3,2},{4,5},{5,4},{6,7},{7,6},{8,9},{9,8},{10,11... | collective-permute-start | bytes 1142792 | tf_op jit(solution)/shard_map/ppermute | solution.py:55
  23.3 6.7 %collective-permute-start.8 = (bf16[960,128]{1,0:T(8,128)(2,1)S(1)}, bf16[960,128]{1,0:T(8,128)(2,1)S(1)}, u32[]{:S(2)}, u32[]{:S(2)}) collective-permute-start(bf16[960,128]{1,0:T(8,128)(2,1)S(1)} %get-tuple-element.100), channel_id=1, source_target_pairs={{0,4},{1,3},{4,8},{5,1},{8,12},{9,5},{12,14},{13,9},{14,10},{15,13... | collective-permute-start | bytes 737288 | tf_op jit(solution)/shard_map/ppermute | solution.py:51
  27.4 6.2 %collective-permute-start.12 = (bf16[960,128]{1,0:T(8,128)(2,1)S(1)}, bf16[960,128]{1,0:T(8,128)(2,1)S(1)}, u32[]{:S(2)}, u32[]{:S(2)}) collective-permute-start(bf16[960,128]{1,0:T(8,128)(2,1)S(1)} %get-tuple-element.108), channel_id=1, source_target_pairs={{0,4},{1,3},{4,8},{5,1},{8,12},{9,5},{12,14},{13,9},{14,10},{15,13... | collective-permute-start | bytes 737288 | tf_op jit(solution)/shard_map/ppermute | solution.py:51
  29.2 4.4 %collective-permute-start.14 = (bf16[1488,128]{1,0:T(8,128)(2,1)S(1)}, bf16[1488,128]{1,0:T(8,128)(2,1)S(1)}, u32[]{:S(2)}, u32[]{:S(2)}) collective-permute-start(bf16[1488,128]{1,0:T(8,128)(2,1)S(1)} %collective-permute-done.4.block_ref.refs_0_.refs_10_), channel_id=1, source_target_pairs={{0,1},{1,0},{2,3},{3,2},{4,5},{5,4},{6,7},{7,6},{8,9},{9,8},{10,11... | collective-permute-start | bytes 1142792 | tf_op jit(solution)/shard_map/ppermute | solution.py:55
  30.0 6.9 %collective-permute-start.11 = (bf16[1056,128]{1,0:T(8,128)(2,1)S(1)}, bf16[1056,128]{1,0:T(8,128)(2,1)S(1)}, u32[]{:S(2)}, u32[]{:S(2)}) collective-permute-start(bf16[1056,128]{1,0:T(8,128)(2,1)S(1)} %get-tuple-element.107), channel_id=1, source_target_pairs={{0,4},{1,3},{4,8},{5,1},{8,12},{9,5},{12,14},{13,9},{14,10},{15,13... | collective-permute-start | bytes 811016 | tf_op jit(solution)/shard_map/ppermute | solution.py:51
  31.7 1.9 %collective-permute-start.15 = (bf16[960,128]{1,0:T(8,128)(2,1)S(1)}, bf16[960,128]{1,0:T(8,128)(2,1)S(1)}, u32[]{:S(2)}, u32[]{:S(2)}) collective-permute-start(bf16[960,128]{1,0:T(8,128)(2,1)S(1)} %collective-permute-done.8.refs_1_), channel_id=1, source_target_pairs={{0,1},{1,0},{2,3},{3,2},{4,5},{5,4},{6,7},{7,6},{8,9},{9,8},{10,11... | collective-permute-start | bytes 737288 | tf_op jit(solution)/shard_map/ppermute | solution.py:55
  33.6 1.5 %collective-permute-start.13 = (bf16[960,128]{1,0:T(8,128)(2,1)S(1)}, bf16[960,128]{1,0:T(8,128)(2,1)S(1)}, u32[]{:S(2)}, u32[]{:S(2)}) collective-permute-start(bf16[960,128]{1,0:T(8,128)(2,1)S(1)} %collective-permute-done.12.refs_0_), channel_id=1, source_target_pairs={{0,1},{1,0},{2,3},{3,2},{4,5},{5,4},{6,7},{7,6},{8,9},{9,8},{10,11... | collective-permute-start | bytes 737288 | tf_op jit(solution)/shard_map/ppermute | solution.py:55
  34.4 0.7 %copy-start = (s32[1,2]{1,0:T(1,128)S(1)}, s32[1,2]{1,0:T(1,128)}, u32[]{:S(2)}) copy-start(s32[1,2]{1,0:T(1,128)} %counts_ref.1) | copy-start | bytes 28
  37.0 1.7 %collective-permute-start.16 = (bf16[1056,128]{1,0:T(8,128)(2,1)S(1)}, bf16[1056,128]{1,0:T(8,128)(2,1)S(1)}, u32[]{:S(2)}, u32[]{:S(2)}) collective-permute-start(bf16[1056,128]{1,0:T(8,128)(2,1)S(1)} %collective-permute-done.11.refs_12_), channel_id=1, source_target_pairs={{0,1},{1,0},{2,3},{3,2},{4,5},{5,4},{6,7},{7,6},{8,9},{9,8},{10,11... | collective-permute-start | bytes 811016 | tf_op jit(solution)/shard_map/ppermute | solution.py:55

commit v17 on v16

--- a/solution.py
+++ b/solution.py
@@ -201,10 +201,13 @@
         product = mm(activation, factor)
         products += [product[:, :LANES], product[:, LANES:]]
     if old:
-        old_sums, old_bridge = old
-        products = [p + old_sums[:, i * LANES : (i + 1) * LANES] for i, p in enumerate(products)]
-        bridge = bridge + old_bridge[...]
+        products = [p + q for p, q in zip(products, old[0])]
+        bridge = bridge + old[1]
     return products, bridge
+
+
+def read_sums(refs):
+    return [refs[0][:, i * LANES : (i + 1) * LANES] for i in range(SUMS)], refs[1][...]
 
 
 def add_half(away, other, me_ref, piece, held, old, scratch):
@@ -253,15 +256,14 @@
     ):
         product = mm(activation, factor)
         products += [product[:, :LANES], product[:, LANES:]]
-    old_sums, old_bridge = old
-    products = [p + old_sums[:, i * LANES : (i + 1) * LANES] for i, p in enumerate(products)]
-    return products, bridge + old_bridge[...]
-
-
-def half_kernel(away, me_ref, *refs):
-    piece, held, old = refs[0], refs[1:8], refs[8:10]
-    (new_sums, new_bridge), scratch = refs[10:12], refs[12:]
-    products, bridge = add_half(away, False, me_ref, piece, held, old, scratch)
+    return [p + q for p, q in zip(products, old[0])], bridge + old[1]
+
+
+def stage_and_half_kernel(away, half_away, me_ref, *refs):
+    pieces, piece, held, old = refs[:2], refs[2], refs[3:10], refs[10:12]
+    (new_sums, new_bridge), scratch, half_scratch = refs[12:14], refs[14:17], refs[17:]
+    sums = add_stage(away, me_ref, pieces, held, read_sums(old), scratch)
+    products, bridge = add_half(half_away, False, me_ref, piece, held, sums, half_scratch)
     for i in range(SUMS):
         new_sums[:, i * LANES : (i + 1) * LANES] = products[i]
     new_bridge[...] = bridge
@@ -270,7 +272,7 @@
 def stage_kernel(away, first, me_ref, *refs):
     pieces, held, old = refs[:2], refs[2:9], refs[9:-5]
     (new_sums, new_bridge), scratch = refs[-5:-3], refs[-3:]
-    products, bridge = add_stage(away, me_ref, pieces, held, old, scratch)
+    products, bridge = add_stage(away, me_ref, pieces, held, read_sums(old) if old else (), scratch)
     for i in range(SUMS):
         new_sums[:, i * LANES : (i + 1) * LANES] = products[i]
     new_bridge[...] = bridge
@@ -279,7 +281,7 @@
 def feature_kernel(away, me_ref, counts_ref, *refs):
     piece, held, old, local_ref, expand_ref, sketch_ref = refs[0], refs[1:8], refs[8:10], *refs[10:13]
     out_ref, scratch = refs[13], refs[14:]
-    products, bridge = add_half(away, True, me_ref, piece, held, old, scratch)
+    products, bridge = add_half(away, True, me_ref, piece, held, read_sums(old), scratch)
     local = [local_ref[:, i * LANES : (i + 1) * LANES] for i in range(LOCAL_SUMS)]
     tokens, width = held[0].shape
     half = LANES // 2
@@ -534,8 +536,8 @@
             second, tail = split(second)
         if k < half - 1:
             second = hop(second)
-        sums = stage(-k, crossed, sums)
         if k < half - 1:
+            sums = stage(-k, crossed, sums)
             second, sums = tie((second, sums))
     tails = hop(tails)
     half_scratch = [
@@ -543,19 +545,19 @@
         pltpu.VMEM((rows + LANES // 2, 2 * LANES), BF16),
         pltpu.VMEM((rows + LANES // 2, 2 * LANES), BF16),
     ]
-    crossed = other_core(first)
-    start = 2 + len(activations)
+    start = 4 + len(activations)
     sums = pl.pallas_call(
-        functools.partial(half_kernel, half),
+        functools.partial(stage_and_half_kernel, 1 - half, half),
         out_shape=[jax.ShapeDtypeStruct(a.shape, a.dtype) for a in sums],
-        in_specs=[SMEM] + [VMEM] * (1 + len(activations) + 2),
+        in_specs=[SMEM] + [VMEM] * (3 + len(activations) + 2),
         out_specs=[VMEM, VMEM],
-        scratch_shapes=half_scratch,
+        scratch_shapes=stage_scratch + half_scratch,
         input_output_aliases={start: 0, start + 1: 1},
         compiler_params=params(16),
-        cost_estimate=cost(tokens * rows * LANES * 8, MIB),
-        name="half_stage",
-    )(me.reshape(1), first, *activations, *sums)
+        cost_estimate=cost(tokens * rows * LANES * 24, 3 * MIB),
+        name="stage_and_half",
+    )(me.reshape(1), *crossed, first, *activations, *sums)
+    crossed = other_core(first)
     unit = pl.pallas_call(
         functools.partial(feature_kernel, half),
         out_shape=jax.ShapeDtypeStruct((LANES, LANES), F32),

time: 39.6 us -> 39.6 us (level)
    pallas_call x7 -> x6, Pallas kernels: 5.25 us -> 4.51 us  [stage(): pl.pallas_call(functools.partial(stage_kernel, away, first), out_shape=[j...]
    pallas_call x1, Pallas kernels: 0.62 us -> 1.18 us  [shards(): pl.pallas_call(functools.partial(stage_and_half_kernel, 1 - half, half),...]
  transfers between devices with their start and end apart: 17 -> 17, of which waited for: 7 -> 7; matrix products, arithmetic and copies ran while one was open for 0% -> 0% of each run, Pallas kernels for 34% -> 33%
where the time goes in v17:
time: 39.6 us; the launch traced here: 39.4 us
  starting transfers between devices  15.9 us (40%)
  Pallas kernels  15.2 us (38%)
  waiting for transfers between devices  7.44 us (19%)
  between operations  0.78 us (2%)
    ppermute x8, starting transfers between devices, hop(): return lax.ppermute(value, 'dp', pairs)  15.1 us
    ppermute x8, waiting for transfers between devices, hop(): return lax.ppermute(value, 'dp', pairs)  6.63 us
    pallas_call x1, Pallas kernels, shards(): pl.pallas_call(local_kernel, out_shape=[jax.ShapeDtypeStruct(a.shape, a.d...  4.69 us
    pallas_call x6, Pallas kernels, stage(): pl.pallas_call(functools.partial(stage_kernel, away, first), out_shape=[j...  4.51 us
    pallas_call x1, Pallas kernels, shards(): pl.pallas_call(functools.partial(feature_kernel, half), out_shape=jax.Sha...  1.79 us
    pallas_call x1, Pallas kernels, shards(): pl.pallas_call(pack_kernel, out_shape=jax.ShapeDtypeStruct((3 * rows + (L...  1.35 us
    pallas_call x1, Pallas kernels, shards(): pl.pallas_call(functools.partial(stage_and_half_kernel, 1 - half, half),...  1.18 us
    pallas_call x1, Pallas kernels, shards(): pl.pallas_call(functools.partial(score_kernel, len(blocks), count), out_s...  0.86 us
  transfers between devices with their start and end apart: 17, of which 7 were waited for; matrix products, arithmetic and copies ran while one was open for 0% of the time, Pallas kernels for 33%

profile of v17, /device:TPU:0, one launch (start us, length us, event | category | flops | bytes accessed | tf_op | source)
XLA Modules:
  0.0 39.4 jit_solution(15179587268396225846)
XLA Ops:
  0.6 1.3 %pack.1.refs_0_ = bf16[1488,128]{1,0:T(8,128)(2,1)S(1)} custom-call(s32[1]{0:T(128)} %bitcast.me_ref, bf16[160,128]{1,0:T(8,128)(2,1)} %bitcast.14, bf16[8,8192]{1,0:T(8,128)(2,1)} %refs_1_.2, bf16[320,128]{1,0:T(8,128)(2,1)} %refs_2_.2, bf16[320,128]{1,0:T(8,128)(2,1)} %bitcast.13, bf16[320,128]{1,0:T(8,128)(2,1)} %refs_4_.2, f32[40,128]{1,0:T(8,128)} %bitcast.11, ...), custom_call_target="tpu_custom_call" | custom-call | tf_op jit(solution)/shard_map/pack/pallas_call | solution.py:439
  2.0 0.5 %collective-permute-start.2 = (bf16[1488,128]{1,0:T(8,128)(2,1)S(1)}, bf16[1488,128]{1,0:T(8,128)(2,1)S(1)}, u32[]{:S(2)}, u32[]{:S(2)}) collective-permute-start(bf16[1488,128]{1,0:T(8,128)(2,1)S(1)} %pack.1.refs_0_), channel_id=1, source_target_pairs={{0,1},{1,0},{2,3},{3,2},{4,5},{5,4},{6,7},{7,6},{8,9},{9,8},{10,11... | collective-permute-start | bytes 1142792 | tf_op jit(solution)/shard_map/ppermute | solution.py:55
  2.5 2.6 %collective-permute-start = (bf16[1488,128]{1,0:T(8,128)(2,1)S(1)}, bf16[1488,128]{1,0:T(8,128)(2,1)S(1)}, u32[]{:S(2)}, u32[]{:S(2)}) collective-permute-start(bf16[1488,128]{1,0:T(8,128)(2,1)S(1)} %pack.1.refs_0_), channel_id=1, source_target_pairs={{0,4},{1,3},{4,8},{5,1},{8,12},{9,5},{12,14},{13,9},{14,10},{15,13... | collective-permute-start | bytes 1142792 | tf_op jit(solution)/shard_map/ppermute | solution.py:51
  5.1 1.6 %collective-permute-start.3 = (bf16[1488,128]{1,0:T(8,128)(2,1)S(1)}, bf16[1488,128]{1,0:T(8,128)(2,1)S(1)}, u32[]{:S(2)}, u32[]{:S(2)}) collective-permute-start(bf16[1488,128]{1,0:T(8,128)(2,1)S(1)} %collective-permute-done.2.refs_1_), channel_id=1, source_target_pairs={{0,4},{1,3},{4,8},{5,1},{8,12},{9,5},{12,14},{13,9},{14,10},{15,13... | collective-permute-start | bytes 1142792 | tf_op jit(solution)/shard_map/ppermute | solution.py:51
  6.8 4.7 %local_products.1 = (bf16[256,5120]{1,0:T(8,128)(2,1)S(1)}, bf16[256,5120]{1,0:T(8,128)(2,1)S(1)}, bf16[256,5120]{1,0:T(8,128)(2,1)S(1)}, bf16[256,2560]{1,0:T(8...) custom-call(bf16[256,5120]{1,0:T(8,128)(2,1)} %refs_0_.1, ...), custom_call_target="tpu_custom_call" | custom-call | flops 1006632960 | bytes 14680064 | tf_op jit(solution)/shard_map/local_products/pallas_call | solution.py:462
  11.5 1.6 %collective-permute-start.1 = (bf16[1488,128]{1,0:T(8,128)(2,1)S(1)}, bf16[1488,128]{1,0:T(8,128)(2,1)S(1)}, u32[]{:S(2)}, u32[]{:S(2)}) collective-permute-start(bf16[1488,128]{1,0:T(8,128)(2,1)S(1)} %collective-permute-done.refs_0_.refs_2_), channel_id=1, source_target_pairs={{0,4},{1,3},{4,8},{5,1},{8,12},{9,5},{12,14},{13,9},{14,10},{15,13... | collective-permute-start | bytes 1142792 | tf_op jit(solution)/shard_map/ppermute | solution.py:51
  13.1 0.7 %stage.6 = (f32[256,1024]{1,0:T(8,128)S(1)}, f32[128,256]{1,0:T(8,128)S(1)}) custom-call(s32[1]{0:T(128)} %bitcast.me_ref, bf16[1488,128]{1,0:T(8,128)(2,1)S(1)} %pack.1.refs_0_, bf16[1488,128]{1,0:T(8,128)(2,1)S(1)} %collective-permute-done.2.refs_1_, bf16[256,5120]{1,0:T(8,128)(2,1)S(1)} %get-tuple-element.71.refs_2_.refs_3_.refs_1_, ...), custom_call_target="tpu_custom_call" | custom-call | flops 167772160 | bytes 2097152 | tf_op jit(solution)/shard_map/stage/pallas_call | solution.py:488
  13.8 1.0 %collective-permute-done.3.refs_1_.refs_4_ = bf16[1488,128]{1,0:T(8,128)(2,1)S(1)} collective-permute-done((bf16[1488,128]{1,0:T(8,128)(2,1)S(1)}, bf16[1488,128]{1,0:T(8,128)(2,1)S(1)}, u32[]{:S(2)}, u32[]{:S(2)}) %collective-permute-start.3) | collective-permute-done | bytes 380960 | tf_op jit(solution)/shard_map/ppermute | solution.py:51
  14.8 0.0 collective-permute-start.7
  14.8 2.1 %collective-permute-start.5 = (bf16[1488,128]{1,0:T(8,128)(2,1)S(1)}, bf16[1488,128]{1,0:T(8,128)(2,1)S(1)}, u32[]{:S(2)}, u32[]{:S(2)}) collective-permute-start(bf16[1488,128]{1,0:T(8,128)(2,1)S(1)} %collective-permute-done.3.refs_1_.refs_4_), channel_id=1, source_target_pairs={{0,4},{1,3},{4,8},{5,1},{8,12},{9,5},{12,14},{13,9},{14,10},{15,13... | collective-permute-start | bytes 1142792 | tf_op jit(solution)/shard_map/ppermute | solution.py:51
  16.9 0.8 %stage.7 = (f32[256,1024]{1,0:T(8,128)S(1)}, f32[128,256]{1,0:T(8,128)S(1)}) custom-call(s32[1]{0:T(128)} %bitcast.me_ref, bf16[1488,128]{1,0:T(8,128)(2,1)S(1)} %collective-permute-done.refs_0_.refs_2_, bf16[1488,128]{1,0:T(8,128)(2,1)S(1)} %collective-permute-done.3.refs_1_.refs_4_, ...), custom_call_target="tpu_custom_call", output_to_operand_aliasing={{0}: (10, {}), {1}: (11, {})} | custom-call | flops 167772160 | bytes 2097152 | tf_op jit(solution)/shard_map/stage/pallas_call | solution.py:488
  17.6 1.5 %collective-permute-done.1.refs_0_.refs_6_ = bf16[1488,128]{1,0:T(8,128)(2,1)S(1)} collective-permute-done((bf16[1488,128]{1,0:T(8,128)(2,1)S(1)}, bf16[1488,128]{1,0:T(8,128)(2,1)S(1)}, u32[]{:S(2)}, u32[]{:S(2)}) %collective-permute-start.1) | collective-permute-done | bytes 380960 | tf_op jit(solution)/shard_map/ppermute | solution.py:51
  19.2 1.8 %collective-permute-start.4 = (bf16[1488,128]{1,0:T(8,128)(2,1)S(1)}, bf16[1488,128]{1,0:T(8,128)(2,1)S(1)}, u32[]{:S(2)}, u32[]{:S(2)}) collective-permute-start(bf16[1488,128]{1,0:T(8,128)(2,1)S(1)} %collective-permute-done.1.refs_0_.refs_6_), channel_id=1, source_target_pairs={{0,4},{1,3},{4,8},{5,1},{8,12},{9,5},{12,14},{13,9},{14,10},{15,13... | collective-permute-start | bytes 1142792 | tf_op jit(solution)/shard_map/ppermute | solution.py:51
  21.0 0.0 collective-permute-start.9
  21.0 0.0 collective-permute-done.6.refs_0_.refs_3_
  21.0 0.8 %stage.8 = (f32[256,1024]{1,0:T(8,128)S(1)}, f32[128,256]{1,0:T(8,128)S(1)}) custom-call(s32[1]{0:T(128)} %bitcast.me_ref, bf16[1488,128]{1,0:T(8,128)(2,1)S(1)} %collective-permute-done.6.refs_0_.refs_3_, bf16[1488,128]{1,0:T(8,128)(2,1)S(1)} %collective-permute-done.7.refs_1_.refs_5_, ...), custom_call_target="tpu_custom_call", output_to_operand_aliasing={{0}: (10, {}), {1}: (11, {})} | custom-call | flops 167772160 | bytes 2097152 | tf_op jit(solution)/shard_map/stage/pallas_call | solution.py:488
  21.7 1.5 %collective-permute-done.5.refs_1_.block_ref.refs_8_ = bf16[1488,128]{1,0:T(8,128)(2,1)S(1)} collective-permute-done((bf16[1488,128]{1,0:T(8,128)(2,1)S(1)}, bf16[1488,128]{1,0:T(8,128)(2,1)S(1)}, u32[]{:S(2)}, u32[]{:S(2)}) %collective-permute-start.5) | collective-permute-done | bytes 380960 | tf_op jit(solution)/shard_map/ppermute | solution.py:51
  23.3 1.8 %collective-permute-start.8 = (bf16[960,128]{1,0:T(8,128)(2,1)S(1)}, bf16[960,128]{1,0:T(8,128)(2,1)S(1)}, u32[]{:S(2)}, u32[]{:S(2)}) collective-permute-start(bf16[960,128]{1,0:T(8,128)(2,1)S(1)} %get-tuple-element.98), channel_id=1, source_target_pairs={{0,4},{1,3},{4,8},{5,1},{8,12},{9,5},{12,14},{13,9},{14,10},{15,13... | collective-permute-start | bytes 737288 | tf_op jit(solution)/shard_map/ppermute | solution.py:51
  25.1 0.8 %stage.9 = (f32[256,1024]{1,0:T(8,128)S(1)}, f32[128,256]{1,0:T(8,128)S(1)}) custom-call(s32[1]{0:T(128)} %bitcast.me_ref, bf16[1488,128]{1,0:T(8,128)(2,1)S(1)} %collective-permute-done.1.refs_0_.refs_6_, bf16[1488,128]{1,0:T(8,128)(2,1)S(1)} %collective-permute-done.5.refs_1_.block_ref.refs_8_, ...), custom_call_target="tpu_custom_call", output_to_operand_aliasing={{0}: (10, {}), {1}: (11, {})} | custom-call | flops 167772160 | bytes 2097152 | tf_op jit(solution)/shard_map/stage/pallas_call | solution.py:488
  25.9 1.5 %collective-permute-done.4.block_ref.refs_0_.refs_10_ = bf16[1488,128]{1,0:T(8,128)(2,1)S(1)} collective-permute-done((bf16[1488,128]{1,0:T(8,128)(2,1)S(1)}, bf16[1488,128]{1,0:T(8,128)(2,1)S(1)}, u32[]{:S(2)}, u32[]{:S(2)}) %collective-permute-start.4) | collective-permute-done | bytes 380960 | tf_op jit(solution)/shard_map/ppermute | solution.py:51
  27.4 1.8 %collective-permute-start.12 = (bf16[960,128]{1,0:T(8,128)(2,1)S(1)}, bf16[960,128]{1,0:T(8,128)(2,1)S(1)}, u32[]{:S(2)}, u32[]{:S(2)}) collective-permute-start(bf16[960,128]{1,0:T(8,128)(2,1)S(1)} %get-tuple-element.106), channel_id=1, source_target_pairs={{0,4},{1,3},{4,8},{5,1},{8,12},{9,5},{12,14},{13,9},{14,10},{15,13... | collective-permute-start | bytes 737288 | tf_op jit(solution)/shard_map/ppermute | solution.py:51
  29.2 0.8 %stage.10 = (f32[256,1024]{1,0:T(8,128)S(1)}, f32[128,256]{1,0:T(8,128)S(1)}) custom-call(s32[1]{0:T(128)} %bitcast.me_ref, bf16[1488,128]{1,0:T(8,128)(2,1)S(1)} %collective-permute-done.9.refs_0_.refs_7_, bf16[1488,128]{1,0:T(8,128)(2,1)S(1)} %collective-permute-done.10.refs_1_.refs_9_, ...), custom_call_target="tpu_custom_call", output_to_operand_aliasing={{0}: (10, {}), {1}: (11, {})} | custom-call | flops 167772160 | bytes 2097152 | tf_op jit(solution)/shard_map/stage/pallas_call | solution.py:488
  30.0 1.7 %collective-permute-start.11 = (bf16[1056,128]{1,0:T(8,128)(2,1)S(1)}, bf16[1056,128]{1,0:T(8,128)(2,1)S(1)}, u32[]{:S(2)}, u32[]{:S(2)}) collective-permute-start(bf16[1056,128]{1,0:T(8,128)(2,1)S(1)} %get-tuple-element.105), channel_id=1, source_target_pairs={{0,4},{1,3},{4,8},{5,1},{8,12},{9,5},{12,14},{13,9},{14,10},{15,13... | collective-permute-start | bytes 811016 | tf_op jit(solution)/shard_map/ppermute | solution.py:51
  31.8 0.8 %stage.11 = (f32[256,1024]{1,0:T(8,128)S(1)}, f32[128,256]{1,0:T(8,128)S(1)}) custom-call(s32[1]{0:T(128)} %bitcast.me_ref, bf16[1488,128]{1,0:T(8,128)(2,1)S(1)} %collective-permute-done.4.block_ref.refs_0_.refs_10_, bf16[960,128]{1,0:T(8,128)(2,1)S(1)} %collective-permute-done.8.refs_1_, ...), custom_call_target="tpu_custom_call", output_to_operand_aliasing={{0}: (10, {}), {1}: (11, {})} | custom-call | flops 167772160 | bytes 2097152 | tf_op jit(solution)/shard_map/stage/pallas_call | solution.py:488
  32.5 1.1 %collective-permute-done.12.refs_2_ = bf16[960,128]{1,0:T(8,128)(2,1)S(1)} collective-permute-done((bf16[960,128]{1,0:T(8,128)(2,1)S(1)}, bf16[960,128]{1,0:T(8,128)(2,1)S(1)}, u32[]{:S(2)}, u32[]{:S(2)}) %collective-permute-start.12) | collective-permute-done | bytes 245792 | tf_op jit(solution)/shard_map/ppermute | solution.py:51
  33.7 1.2 %stage_and_half.1 = (f32[256,1024]{1,0:T(8,128)S(1)}, f32[128,256]{1,0:T(8,128)S(1)}) custom-call(s32[1]{0:T(128)} %bitcast.me_ref, bf16[1488,128]{1,0:T(8,128)(2,1)S(1)} %collective-permute-done.14.refs_0_.refs_11_, bf16[960,128]{1,0:T(8,128)(2,1)S(1)} %collective-permute-done.15.refs_1_, ...), custom_call_target="tpu_custom_call", output_to_operand_aliasing={{0}: (11, {}), {1}: (12, {})} | custom-call | flops 251658240 | bytes 3145728 | tf_op jit(solution)/shard_map/stage_and_half/pallas_call | solution.py:549
  34.9 0.3 collective-permute-done.13.refs_0_
  35.2 1.8 %features.1.unit_ref = f32[128,128]{1,0:T(8,128)S(1)} custom-call(s32[1]{0:T(128)} %bitcast.me_ref, s32[1,2]{1,0:T(1,128)S(1)} %copy-done, bf16[960,128]{1,0:T(8,128)(2,1)S(1)} %collective-permute-done.13.refs_0_, bf16[256,5120]{1,0:T(8,128)(2,1)S(1)} %get-tuple-element.71.refs_2_.refs_3_.refs_1_, ...), custom_call_target="tpu_custom_call" | custom-call | flops 1 | bytes 1 | tf_op jit(solution)/shard_map/features/pallas_call | solution.py:561
  37.0 0.3 collective-permute-start.16
  37.2 0.9 %scores.1.best_ref = f32[2,3,8,128]{3,2,1,0:T(8,128)S(1)} custom-call(f32[128,128]{1,0:T(8,128)S(1)} %features.1.unit_ref, bf16[1488,128]{1,0:T(8,128)(2,1)S(1)} %pack.1.refs_0_, bf16[1488,128]{1,0:T(8,128)(2,1)S(1)} %collective-permute-done.2.refs_1_, bf16[1488,128]{1,0:T(8,128)(2,1)S(1)} %collective-permute-done.refs_0_.refs_2_, ...), custom_call_target="tpu_custom_call" | custom-call | flops 4194304 | bytes 2097152 | tf_op jit(solution)/shard_map/scores/pallas_call | solution.py:573
  38.1 0.5 %collective-permute-done.16.block_ref = bf16[1056,128]{1,0:T(8,128)(2,1)S(1)} collective-permute-done((bf16[1056,128]{1,0:T(8,128)(2,1)S(1)}, bf16[1056,128]{1,0:T(8,128)(2,1)S(1)}, u32[]{:S(2)}, u32[]{:S(2)}) %collective-permute-start.16) | collective-permute-done | bytes 270368 | tf_op jit(solution)/shard_map/ppermute | solution.py:55
  38.6 0.8 %last_scores.1 = (f32[2,3]{1,0:T(2,128)}, f32[1,2]{1,0:T(1,128)}) custom-call(f32[128,128]{1,0:T(8,128)S(1)} %features.1.unit_ref, bf16[1056,128]{1,0:T(8,128)(2,1)S(1)} %collective-permute-done.16.block_ref, f32[2,3,8,128]{3,2,1,0:T(8,128)S(1)} %scores.1.best_ref), custom_call_target="tpu_custom_call" | custom-call | tf_op jit(solution)/shard_map/last_scores/pallas_call | solution.py:582
  (18 shorter events, 0.1 us)
Async XLA Ops:
  2.0 3.2 %collective-permute-start.2 = (bf16[1488,128]{1,0:T(8,128)(2,1)S(1)}, bf16[1488,128]{1,0:T(8,128)(2,1)S(1)}, u32[]{:S(2)}, u32[]{:S(2)}) collective-permute-start(bf16[1488,128]{1,0:T(8,128)(2,1)S(1)} %pack.1.refs_0_), channel_id=1, source_target_pairs={{0,1},{1,0},{2,3},{3,2},{4,5},{5,4},{6,7},{7,6},{8,9},{9,8},{10,11... | collective-permute-start | bytes 1142792 | tf_op jit(solution)/shard_map/ppermute | solution.py:55
  2.5 9.0 %collective-permute-start = (bf16[1488,128]{1,0:T(8,128)(2,1)S(1)}, bf16[1488,128]{1,0:T(8,128)(2,1)S(1)}, u32[]{:S(2)}, u32[]{:S(2)}) collective-permute-start(bf16[1488,128]{1,0:T(8,128)(2,1)S(1)} %pack.1.refs_0_), channel_id=1, source_target_pairs={{0,4},{1,3},{4,8},{5,1},{8,12},{9,5},{12,14},{13,9},{14,10},{15,13... | collective-permute-start | bytes 1142792 | tf_op jit(solution)/shard_map/ppermute | solution.py:51
  5.1 9.6 %collective-permute-start.3 = (bf16[1488,128]{1,0:T(8,128)(2,1)S(1)}, bf16[1488,128]{1,0:T(8,128)(2,1)S(1)}, u32[]{:S(2)}, u32[]{:S(2)}) collective-permute-start(bf16[1488,128]{1,0:T(8,128)(2,1)S(1)} %collective-permute-done.2.refs_1_), channel_id=1, source_target_pairs={{0,4},{1,3},{4,8},{5,1},{8,12},{9,5},{12,14},{13,9},{14,10},{15,13... | collective-permute-start | bytes 1142792 | tf_op jit(solution)/shard_map/ppermute | solution.py:51
  11.5 7.7 %collective-permute-start.1 = (bf16[1488,128]{1,0:T(8,128)(2,1)S(1)}, bf16[1488,128]{1,0:T(8,128)(2,1)S(1)}, u32[]{:S(2)}, u32[]{:S(2)}) collective-permute-start(bf16[1488,128]{1,0:T(8,128)(2,1)S(1)} %collective-permute-done.refs_0_.refs_2_), channel_id=1, source_target_pairs={{0,4},{1,3},{4,8},{5,1},{8,12},{9,5},{12,14},{13,9},{14,10},{15,13... | collective-permute-start | bytes 1142792 | tf_op jit(solution)/shard_map/ppermute | solution.py:51
  13.1 7.8 %collective-permute-start.6 = (bf16[1488,128]{1,0:T(8,128)(2,1)S(1)}, bf16[1488,128]{1,0:T(8,128)(2,1)S(1)}, u32[]{:S(2)}, u32[]{:S(2)}) collective-permute-start(bf16[1488,128]{1,0:T(8,128)(2,1)S(1)} %collective-permute-done.refs_0_.refs_2_), channel_id=1, source_target_pairs={{0,1},{1,0},{2,3},{3,2},{4,5},{5,4},{6,7},{7,6},{8,9},{9,8},{10,11... | collective-permute-start | bytes 1142792 | tf_op jit(solution)/shard_map/ppermute | solution.py:55
  14.8 6.2 %collective-permute-start.7 = (bf16[1488,128]{1,0:T(8,128)(2,1)S(1)}, bf16[1488,128]{1,0:T(8,128)(2,1)S(1)}, u32[]{:S(2)}, u32[]{:S(2)}) collective-permute-start(bf16[1488,128]{1,0:T(8,128)(2,1)S(1)} %collective-permute-done.3.refs_1_.refs_4_), channel_id=1, source_target_pairs={{0,1},{1,0},{2,3},{3,2},{4,5},{5,4},{6,7},{7,6},{8,9},{9,8},{10,11... | collective-permute-start | bytes 1142792 | tf_op jit(solution)/shard_map/ppermute | solution.py:55
  14.8 8.5 %collective-permute-start.5 = (bf16[1488,128]{1,0:T(8,128)(2,1)S(1)}, bf16[1488,128]{1,0:T(8,128)(2,1)S(1)}, u32[]{:S(2)}, u32[]{:S(2)}) collective-permute-start(bf16[1488,128]{1,0:T(8,128)(2,1)S(1)} %collective-permute-done.3.refs_1_.refs_4_), channel_id=1, source_target_pairs={{0,4},{1,3},{4,8},{5,1},{8,12},{9,5},{12,14},{13,9},{14,10},{15,13... | collective-permute-start | bytes 1142792 | tf_op jit(solution)/shard_map/ppermute | solution.py:51
  19.2 8.2 %collective-permute-start.4 = (bf16[1488,128]{1,0:T(8,128)(2,1)S(1)}, bf16[1488,128]{1,0:T(8,128)(2,1)S(1)}, u32[]{:S(2)}, u32[]{:S(2)}) collective-permute-start(bf16[1488,128]{1,0:T(8,128)(2,1)S(1)} %collective-permute-done.1.refs_0_.refs_6_), channel_id=1, source_target_pairs={{0,4},{1,3},{4,8},{5,1},{8,12},{9,5},{12,14},{13,9},{14,10},{15,13... | collective-permute-start | bytes 1142792 | tf_op jit(solution)/shard_map/ppermute | solution.py:51
  21.0 8.3 %collective-permute-start.9 = (bf16[1488,128]{1,0:T(8,128)(2,1)S(1)}, bf16[1488,128]{1,0:T(8,128)(2,1)S(1)}, u32[]{:S(2)}, u32[]{:S(2)}) collective-permute-start(bf16[1488,128]{1,0:T(8,128)(2,1)S(1)} %collective-permute-done.1.refs_0_.refs_6_), channel_id=1, source_target_pairs={{0,1},{1,0},{2,3},{3,2},{4,5},{5,4},{6,7},{7,6},{8,9},{9,8},{10,11... | collective-permute-start | bytes 1142792 | tf_op jit(solution)/shard_map/ppermute | solution.py:55
  23.3 5.9 %collective-permute-start.10 = (bf16[1488,128]{1,0:T(8,128)(2,1)S(1)}, bf16[1488,128]{1,0:T(8,128)(2,1)S(1)}, u32[]{:S(2)}, u32[]{:S(2)}) collective-permute-start(bf16[1488,128]{1,0:T(8,128)(2,1)S(1)} %collective-permute-done.5.refs_1_.block_ref.refs_8_), channel_id=1, source_target_pairs={{0,1},{1,0},{2,3},{3,2},{4,5},{5,4},{6,7},{7,6},{8,9},{9,8},{10,11... | collective-permute-start | bytes 1142792 | tf_op jit(solution)/shard_map/ppermute | solution.py:55
  23.3 6.7 %collective-permute-start.8 = (bf16[960,128]{1,0:T(8,128)(2,1)S(1)}, bf16[960,128]{1,0:T(8,128)(2,1)S(1)}, u32[]{:S(2)}, u32[]{:S(2)}) collective-permute-start(bf16[960,128]{1,0:T(8,128)(2,1)S(1)} %get-tuple-element.98), channel_id=1, source_target_pairs={{0,4},{1,3},{4,8},{5,1},{8,12},{9,5},{12,14},{13,9},{14,10},{15,13... | collective-permute-start | bytes 737288 | tf_op jit(solution)/shard_map/ppermute | solution.py:51
  27.4 6.2 %collective-permute-start.12 = (bf16[960,128]{1,0:T(8,128)(2,1)S(1)}, bf16[960,128]{1,0:T(8,128)(2,1)S(1)}, u32[]{:S(2)}, u32[]{:S(2)}) collective-permute-start(bf16[960,128]{1,0:T(8,128)(2,1)S(1)} %get-tuple-element.106), channel_id=1, source_target_pairs={{0,4},{1,3},{4,8},{5,1},{8,12},{9,5},{12,14},{13,9},{14,10},{15,13... | collective-permute-start | bytes 737288 | tf_op jit(solution)/shard_map/ppermute | solution.py:51
  29.2 4.4 %collective-permute-start.14 = (bf16[1488,128]{1,0:T(8,128)(2,1)S(1)}, bf16[1488,128]{1,0:T(8,128)(2,1)S(1)}, u32[]{:S(2)}, u32[]{:S(2)}) collective-permute-start(bf16[1488,128]{1,0:T(8,128)(2,1)S(1)} %collective-permute-done.4.block_ref.refs_0_.refs_10_), channel_id=1, source_target_pairs={{0,1},{1,0},{2,3},{3,2},{4,5},{5,4},{6,7},{7,6},{8,9},{9,8},{10,11... | collective-permute-start | bytes 1142792 | tf_op jit(solution)/shard_map/ppermute | solution.py:55
  30.0 7.0 %collective-permute-start.11 = (bf16[1056,128]{1,0:T(8,128)(2,1)S(1)}, bf16[1056,128]{1,0:T(8,128)(2,1)S(1)}, u32[]{:S(2)}, u32[]{:S(2)}) collective-permute-start(bf16[1056,128]{1,0:T(8,128)(2,1)S(1)} %get-tuple-element.105), channel_id=1, source_target_pairs={{0,4},{1,3},{4,8},{5,1},{8,12},{9,5},{12,14},{13,9},{14,10},{15,13... | collective-permute-start | bytes 811016 | tf_op jit(solution)/shard_map/ppermute | solution.py:51
  31.7 1.9 %collective-permute-start.15 = (bf16[960,128]{1,0:T(8,128)(2,1)S(1)}, bf16[960,128]{1,0:T(8,128)(2,1)S(1)}, u32[]{:S(2)}, u32[]{:S(2)}) collective-permute-start(bf16[960,128]{1,0:T(8,128)(2,1)S(1)} %collective-permute-done.8.refs_1_), channel_id=1, source_target_pairs={{0,1},{1,0},{2,3},{3,2},{4,5},{5,4},{6,7},{7,6},{8,9},{9,8},{10,11... | collective-permute-start | bytes 737288 | tf_op jit(solution)/shard_map/ppermute | solution.py:55
  33.6 1.5 %copy-start = (s32[1,2]{1,0:T(1,128)S(1)}, s32[1,2]{1,0:T(1,128)}, u32[]{:S(2)}) copy-start(s32[1,2]{1,0:T(1,128)} %counts_ref.1) | copy-start | bytes 28
  33.6 1.5 %collective-permute-start.13 = (bf16[960,128]{1,0:T(8,128)(2,1)S(1)}, bf16[960,128]{1,0:T(8,128)(2,1)S(1)}, u32[]{:S(2)}, u32[]{:S(2)}) collective-permute-start(bf16[960,128]{1,0:T(8,128)(2,1)S(1)} %collective-permute-done.12.refs_2_), channel_id=1, source_target_pairs={{0,1},{1,0},{2,3},{3,2},{4,5},{5,4},{6,7},{7,6},{8,9},{9,8},{10,11... | collective-permute-start | bytes 737288 | tf_op jit(solution)/shard_map/ppermute | solution.py:55
  37.0 1.6 %collective-permute-start.16 = (bf16[1056,128]{1,0:T(8,128)(2,1)S(1)}, bf16[1056,128]{1,0:T(8,128)(2,1)S(1)}, u32[]{:S(2)}, u32[]{:S(2)}) collective-permute-start(bf16[1056,128]{1,0:T(8,128)(2,1)S(1)} %collective-permute-done.11.refs_12_), channel_id=1, source_target_pairs={{0,1},{1,0},{2,3},{3,2},{4,5},{5,4},{6,7},{7,6},{8,9},{9,8},{10,11... | collective-permute-start | bytes 811016 | tf_op jit(solution)/shard_map/ppermute | solution.py:55

commit v18 on v17

--- a/solution.py
+++ b/solution.py
@@ -269,6 +269,15 @@
     new_bridge[...] = bridge
 
 
+def half_kernel(away, me_ref, *refs):
+    piece, held, old = refs[0], refs[1:8], refs[8:10]
+    (new_sums, new_bridge), scratch = refs[10:12], refs[12:]
+    products, bridge = add_half(away, True, me_ref, piece, held, read_sums(old), scratch)
+    for i in range(SUMS):
+        new_sums[:, i * LANES : (i + 1) * LANES] = products[i]
+    new_bridge[...] = bridge
+
+
 def stage_kernel(away, first, me_ref, *refs):
     pieces, held, old = refs[:2], refs[2:9], refs[9:-5]
     (new_sums, new_bridge), scratch = refs[-5:-3], refs[-3:]
@@ -278,12 +287,11 @@
     new_bridge[...] = bridge
 
 
-def feature_kernel(away, me_ref, counts_ref, *refs):
-    piece, held, old, local_ref, expand_ref, sketch_ref = refs[0], refs[1:8], refs[8:10], *refs[10:13]
-    out_ref, scratch = refs[13], refs[14:]
-    products, bridge = add_half(away, True, me_ref, piece, held, read_sums(old), scratch)
+def feature_kernel(width, counts_ref, *refs):
+    old, local_ref, expand_ref, sketch_ref, out_ref = refs[:2], *refs[2:]
+    products, bridge = read_sums(old)
     local = [local_ref[:, i * LANES : (i + 1) * LANES] for i in range(LOCAL_SUMS)]
-    tokens, width = held[0].shape
+    tokens = local_ref.shape[0]
     half = LANES // 2
     inverse = local[INVERSE]
     returned = products[VALUES].astype(BF16)
@@ -316,55 +324,33 @@
     cut, tail = head_ref.shape[0], block_ref.shape[0] - head_ref.shape[0]
     head_ref[...] = block_ref[pl.ds(0, cut), :]
     if len(refs) == 3:
-        tail_ref[pl.ds(0, tail), :] = refs[0][...]
+        tail_ref[pl.ds(0, refs[0].shape[0]), :] = refs[0][...]
     tail_ref[pl.ds(tail_ref.shape[0] - tail, tail), :] = block_ref[pl.ds(cut, tail), :]
 
 
-def best_of(places, count, unit_ref, best):
+def score_kernel(spans, count, unit_ref, *refs):
+    block_refs, (out_ref, mean_ref) = refs[:-2], refs[-2:]
     half = LANES // 2
     scale = float(half * LANES) ** 0.5
     shape = (count, LANES)
-    totals = [[jnp.zeros(shape, F32) for _ in range(2)] for _ in places]
+    totals = [[jnp.zeros(shape, F32) for _ in range(2)] for _ in spans]
     for i in range(0, half, 2):
         units = [
             [jnp.broadcast_to(unit_ref[pl.ds(e * half + i + k, 1), :], shape) for k in range(2)]
             for e in range(2)
         ]
-        for b, (block, start) in enumerate(places):
-            wide = block[pl.ds(start + i * count, 2 * count), :].astype(F32)
+        for b, (parts, _) in enumerate(spans):
+            ref, row, low, _ = next(part for part in parts if part[2] <= i < part[3])
+            wide = block_refs[ref][pl.ds(row + (i - low) * count, 2 * count), :].astype(F32)
             for e in range(2):
                 totals[b][e] = totals[b][e] + (wide[:count] * units[e][0] + wide[count:] * units[e][1])
-    for b, (block, start) in enumerate(places):
-        labels = block[pl.ds(start + half * count, 2 * count), :].astype(F32)[:count]
+    best = [[jnp.full(shape, -2.0 * scale, F32) for _ in range(TASKS)] for _ in range(2)]
+    for b, (_, (ref, row)) in enumerate(spans):
+        labels = block_refs[ref][pl.ds(row, 2 * count), :].astype(F32)[:count]
         for e in range(2):
             similar = scale * jnp.sum(totals[b][e], axis=1, keepdims=True)
             for t in range(TASKS):
                 best[e][t] = jnp.maximum(best[e][t], jnp.where(labels == float(t), similar, -2.0 * scale))
-
-
-def places_of(blocks, count):
-    size = (LANES // 2 + 2) * count
-    places = []
-    for block in blocks:
-        total = block.shape[0]
-        firsts = range(0, total, size) if total % size == 0 else [total - size]
-        places += [(block, first) for first in firsts]
-    return places
-
-
-def score_kernel(blocks, count, unit_ref, *refs):
-    block_refs, best_ref = refs[:blocks], refs[blocks]
-    lowest = -2.0 * float(LANES // 2 * LANES) ** 0.5
-    best = [[jnp.full((count, LANES), lowest, F32) for _ in range(TASKS)] for _ in range(2)]
-    best_of(places_of(block_refs, count), count, unit_ref, best)
-    for e in range(2):
-        for t in range(TASKS):
-            best_ref[e, t] = best[e][t]
-
-
-def last_score_kernel(count, unit_ref, block_ref, best_ref, out_ref, mean_ref):
-    best = [[best_ref[e, t] for t in range(TASKS)] for e in range(2)]
-    best_of(places_of([block_ref], count), count, unit_ref, best)
     lane = lax.broadcasted_iota(jnp.int32, (1, LANES), 1)
     means = []
     for e in range(2):
@@ -500,12 +486,15 @@
             name="stage",
         )(me.reshape(1), *pieces, *activations, *sums)
 
-    def split(block, *tails):
-        tail = block.shape[0] - 3 * rows
-        shapes = (3 * rows, LANES), ((1 + len(tails)) * tail, LANES)
+    def split(block, cut, *tails):
+        tail = block.shape[0] - cut
+        size = tail + sum(t.shape[0] for t in tails)
         return pl.pallas_call(
             split_kernel,
-            out_shape=[jax.ShapeDtypeStruct(shape, BF16) for shape in shapes],
+            out_shape=[
+                jax.ShapeDtypeStruct((cut, LANES), BF16),
+                jax.ShapeDtypeStruct((size, LANES), BF16),
+            ],
             in_specs=[VMEM] * (1 + len(tails)),
             out_specs=[VMEM, VMEM],
             compiler_params=params(8),
@@ -514,6 +503,8 @@
 
     tie = lax.optimization_barrier
     half = RING_CHIPS // 2
+    factor_rows, features = 3 * rows, LANES // 2
+    early = 10
     held = [own, other_core(own)]
     blocks = list(held)
     first, second = hop(held[0]), hop(held[1])
@@ -523,17 +514,15 @@
     for k in range(1, half):
         held = [first, second]
         crossed = [other_core(first), other_core(second)]
-        blocks += [first, crossed[0]]
-        if k < half - 1:
-            blocks += [second, crossed[1]]
-        else:
-            first, tails = split(first, tail)
+        blocks += [first, crossed[0], second, crossed[1]]
+        if k == half - 1:
+            first, tails = split(first, 3 * rows, tail)
             tails, sums = tie((tails, sums))
         first = hop(first)
         sums = stage(k, held, sums)
         first, sums = tie((first, sums))
         if k == half - 2:
-            second, tail = split(second)
+            second, tail = split(second, 3 * rows + early * count)
         if k < half - 1:
             second = hop(second)
         if k < half - 1:
@@ -554,39 +543,54 @@
         scratch_shapes=stage_scratch + half_scratch,
         input_output_aliases={start: 0, start + 1: 1},
         compiler_params=params(16),
-        cost_estimate=cost(tokens * rows * LANES * 24, 3 * MIB),
+        cost_estimate=cost(1, 1),
         name="stage_and_half",
     )(me.reshape(1), *crossed, first, *activations, *sums)
     crossed = other_core(first)
+    start = 2 + len(activations)
+    sums = pl.pallas_call(
+        functools.partial(half_kernel, half),
+        out_shape=[jax.ShapeDtypeStruct(a.shape, a.dtype) for a in sums],
+        in_specs=[SMEM] + [VMEM] * (1 + len(activations) + 2),
+        out_specs=[VMEM, VMEM],
+        scratch_shapes=half_scratch,
+        input_output_aliases={start: 0, start + 1: 1},
+        compiler_params=params(16),
+        cost_estimate=cost(1, 1),
+        name="half_stage",
+    )(me.reshape(1), crossed, *activations, *sums)
+    tails, sums = tie((tails, sums))
+    blocks += [tails, other_core(tails)]
     unit = pl.pallas_call(
-        functools.partial(feature_kernel, half),
+        functools.partial(feature_kernel, width),
         out_shape=jax.ShapeDtypeStruct((LANES, LANES), F32),
-        in_specs=[SMEM] * 2 + [VMEM] * (1 + len(activations) + 5),
+        in_specs=[SMEM] + [VMEM] * 5,
         out_specs=VMEM,
-        scratch_shapes=half_scratch,
         compiler_params=params(16),
         cost_estimate=cost(1, 1),
         name="features",
-    )(me.reshape(1), sequence_token_counts, crossed, *activations, *sums, local, *small)
-    tails, unit = tie((tails, unit))
-    blocks.append(tails)
-    best = pl.pallas_call(
-        functools.partial(score_kernel, len(blocks), count),
-        out_shape=jax.ShapeDtypeStruct((2, TASKS, count, LANES), F32),
+    )(sequence_token_counts, *sums, local, *small)
+    spans, rest = [], (features - early) * count
+    for b, block in enumerate(blocks[:-2]):
+        if block.shape == own.shape:
+            parts = ((b, factor_rows, 0, features),)
+            spans.append((parts, (b, factor_rows + features * count)))
+        else:
+            tail = len(blocks) - 2 + (b + 2 == len(blocks) - 1)
+            parts = ((b, factor_rows, 0, early), (tail, 0, early, features))
+            spans.append((parts, (tail, rest)))
+    for tail in (len(blocks) - 2, len(blocks) - 1):
+        first_row = rest + 2 * count
+        spans.append((((tail, first_row, 0, features),), (tail, first_row + features * count)))
+    task_best, scores = pl.pallas_call(
+        functools.partial(score_kernel, spans, count),
+        out_shape=(jax.ShapeDtypeStruct((2, TASKS), F32), jax.ShapeDtypeStruct((1, 2), F32)),
         in_specs=[VMEM] * (1 + len(blocks)),
-        out_specs=VMEM,
+        out_specs=(VMEM, VMEM),
         compiler_params=params(16),
         cost_estimate=cost(4 * MIB, 2 * MIB),
         name="scores",
     )(unit, *blocks)
-    task_best, scores = pl.pallas_call(
-        functools.partial(last_score_kernel, count),
-        out_shape=(jax.ShapeDtypeStruct((2, TASKS), F32), jax.ShapeDtypeStruct((1, 2), F32)),
-        in_specs=[VMEM] * 3,
-        out_specs=(VMEM, VMEM),
-        compiler_params=params(8),
-        name="last_scores",
-    )(unit, other_core(tails), best)
     return (scores.reshape(2), task_best)
 
 

time: 39.6 us -> 40.1 us (1.013)
  waiting for transfers between devices: 7.44 us -> 8.16 us
    ppermute x8, waiting for transfers between devices: 6.63 us -> 7.5 us  [hop(): return lax.ppermute(value, 'dp', pairs)]
  transfers between devices with their start and end apart: 17 -> 17, of which waited for: 7 -> 9; matrix products, arithmetic and copies ran while one was open for 0% -> 0% of each run, Pallas kernels for 33% -> 31%
where the time goes in v18:
time: 40.1 us; the launch traced here: 39.9 us
  starting transfers between devices  15.9 us (40%)
  Pallas kernels  15.1 us (38%)
  waiting for transfers between devices  8.16 us (20%)
  between operations  0.76 us (2%)
    ppermute x8, starting transfers between devices, hop(): return lax.ppermute(value, 'dp', pairs)  15 us
    ppermute x8, waiting for transfers between devices, hop(): return lax.ppermute(value, 'dp', pairs)  7.5 us
    pallas_call x1, Pallas kernels, shards(): pl.pallas_call(local_kernel, out_shape=[jax.ShapeDtypeStruct(a.shape, a.d...  4.69 us
    pallas_call x6, Pallas kernels, stage(): pl.pallas_call(functools.partial(stage_kernel, away, first), out_shape=[j...  4.5 us
    pallas_call x1, Pallas kernels, shards(): pl.pallas_call(functools.partial(score_kernel, spans, count), out_shape=(...  1.57 us
    pallas_call x1, Pallas kernels, shards(): pl.pallas_call(pack_kernel, out_shape=jax.ShapeDtypeStruct((3 * rows + (L...  1.35 us
    pallas_call x1, Pallas kernels, shards(): pl.pallas_call(functools.partial(stage_and_half_kernel, 1 - half, half),...  1.17 us
    pallas_call x1, Pallas kernels, shards(): pl.pallas_call(functools.partial(feature_kernel, width), out_shape=jax.Sh...  1.17 us
  transfers between devices with their start and end apart: 17, of which 9 were waited for; matrix products, arithmetic and copies ran while one was open for 0% of the time, Pallas kernels for 31%

profile of v18, /device:TPU:0, one launch (start us, length us, event | category | flops | bytes accessed | tf_op | source)
XLA Modules:
  0.0 39.9 jit_solution(15264532784072198990)
XLA Ops:
  0.6 1.3 %pack.1.refs_0_ = bf16[1488,128]{1,0:T(8,128)(2,1)S(1)} custom-call(s32[1]{0:T(128)} %bitcast.me_ref, bf16[160,128]{1,0:T(8,128)(2,1)} %bitcast.14, bf16[8,8192]{1,0:T(8,128)(2,1)} %refs_1_.2, bf16[320,128]{1,0:T(8,128)(2,1)} %refs_2_.2, bf16[320,128]{1,0:T(8,128)(2,1)} %bitcast.13, bf16[320,128]{1,0:T(8,128)(2,1)} %refs_4_.2, f32[40,128]{1,0:T(8,128)} %bitcast.11, ...), custom_call_target="tpu_custom_call" | custom-call | tf_op jit(solution)/shard_map/pack/pallas_call | solution.py:425
  2.0 0.5 %collective-permute-start.2 = (bf16[1488,128]{1,0:T(8,128)(2,1)S(1)}, bf16[1488,128]{1,0:T(8,128)(2,1)S(1)}, u32[]{:S(2)}, u32[]{:S(2)}) collective-permute-start(bf16[1488,128]{1,0:T(8,128)(2,1)S(1)} %pack.1.refs_0_), channel_id=1, source_target_pairs={{0,1},{1,0},{2,3},{3,2},{4,5},{5,4},{6,7},{7,6},{8,9},{9,8},{10,11... | collective-permute-start | bytes 1142792 | tf_op jit(solution)/shard_map/ppermute | solution.py:55
  2.5 2.6 %collective-permute-start = (bf16[1488,128]{1,0:T(8,128)(2,1)S(1)}, bf16[1488,128]{1,0:T(8,128)(2,1)S(1)}, u32[]{:S(2)}, u32[]{:S(2)}) collective-permute-start(bf16[1488,128]{1,0:T(8,128)(2,1)S(1)} %pack.1.refs_0_), channel_id=1, source_target_pairs={{0,4},{1,3},{4,8},{5,1},{8,12},{9,5},{12,14},{13,9},{14,10},{15,13... | collective-permute-start | bytes 1142792 | tf_op jit(solution)/shard_map/ppermute | solution.py:51
  5.1 0.0 collective-permute-done.2.refs_1_
  5.1 1.6 %collective-permute-start.3 = (bf16[1488,128]{1,0:T(8,128)(2,1)S(1)}, bf16[1488,128]{1,0:T(8,128)(2,1)S(1)}, u32[]{:S(2)}, u32[]{:S(2)}) collective-permute-start(bf16[1488,128]{1,0:T(8,128)(2,1)S(1)} %collective-permute-done.2.refs_1_), channel_id=1, source_target_pairs={{0,4},{1,3},{4,8},{5,1},{8,12},{9,5},{12,14},{13,9},{14,10},{15,13... | collective-permute-start | bytes 1142792 | tf_op jit(solution)/shard_map/ppermute | solution.py:51
  6.8 4.7 %local_products.1 = (bf16[256,5120]{1,0:T(8,128)(2,1)S(1)}, bf16[256,5120]{1,0:T(8,128)(2,1)S(1)}, bf16[256,5120]{1,0:T(8,128)(2,1)S(1)}, bf16[256,2560]{1,0:T(8...) custom-call(bf16[256,5120]{1,0:T(8,128)(2,1)} %refs_0_.1, ...), custom_call_target="tpu_custom_call" | custom-call | flops 1006632960 | bytes 14680064 | tf_op jit(solution)/shard_map/local_products/pallas_call | solution.py:448
  11.5 1.6 %collective-permute-start.1 = (bf16[1488,128]{1,0:T(8,128)(2,1)S(1)}, bf16[1488,128]{1,0:T(8,128)(2,1)S(1)}, u32[]{:S(2)}, u32[]{:S(2)}) collective-permute-start(bf16[1488,128]{1,0:T(8,128)(2,1)S(1)} %collective-permute-done.refs_0_.refs_2_), channel_id=1, source_target_pairs={{0,4},{1,3},{4,8},{5,1},{8,12},{9,5},{12,14},{13,9},{14,10},{15,13... | collective-permute-start | bytes 1142792 | tf_op jit(solution)/shard_map/ppermute | solution.py:51
  13.1 0.7 %stage.6 = (f32[256,1024]{1,0:T(8,128)S(1)}, f32[128,256]{1,0:T(8,128)S(1)}) custom-call(s32[1]{0:T(128)} %bitcast.me_ref, bf16[1488,128]{1,0:T(8,128)(2,1)S(1)} %pack.1.refs_0_, bf16[1488,128]{1,0:T(8,128)(2,1)S(1)} %collective-permute-done.2.refs_1_, bf16[256,5120]{1,0:T(8,128)(2,1)S(1)} %get-tuple-element.74.refs_2_.refs_3_.refs_1_, ...), custom_call_target="tpu_custom_call" | custom-call | flops 167772160 | bytes 2097152 | tf_op jit(solution)/shard_map/stage/pallas_call | solution.py:474
  13.8 1.0 %collective-permute-done.3.refs_1_.refs_4_ = bf16[1488,128]{1,0:T(8,128)(2,1)S(1)} collective-permute-done((bf16[1488,128]{1,0:T(8,128)(2,1)S(1)}, bf16[1488,128]{1,0:T(8,128)(2,1)S(1)}, u32[]{:S(2)}, u32[]{:S(2)}) %collective-permute-start.3) | collective-permute-done | bytes 380960 | tf_op jit(solution)/shard_map/ppermute | solution.py:51
  14.8 2.1 %collective-permute-start.5 = (bf16[1488,128]{1,0:T(8,128)(2,1)S(1)}, bf16[1488,128]{1,0:T(8,128)(2,1)S(1)}, u32[]{:S(2)}, u32[]{:S(2)}) collective-permute-start(bf16[1488,128]{1,0:T(8,128)(2,1)S(1)} %collective-permute-done.3.refs_1_.refs_4_), channel_id=1, source_target_pairs={{0,4},{1,3},{4,8},{5,1},{8,12},{9,5},{12,14},{13,9},{14,10},{15,13... | collective-permute-start | bytes 1142792 | tf_op jit(solution)/shard_map/ppermute | solution.py:51
  16.9 0.8 %stage.7 = (f32[256,1024]{1,0:T(8,128)S(1)}, f32[128,256]{1,0:T(8,128)S(1)}) custom-call(s32[1]{0:T(128)} %bitcast.me_ref, bf16[1488,128]{1,0:T(8,128)(2,1)S(1)} %collective-permute-done.refs_0_.refs_2_, bf16[1488,128]{1,0:T(8,128)(2,1)S(1)} %collective-permute-done.3.refs_1_.refs_4_, ...), custom_call_target="tpu_custom_call", output_to_operand_aliasing={{0}: (10, {}), {1}: (11, {})} | custom-call | flops 167772160 | bytes 2097152 | tf_op jit(solution)/shard_map/stage/pallas_call | solution.py:474
  17.6 1.5 %collective-permute-done.1.refs_0_.refs_6_ = bf16[1488,128]{1,0:T(8,128)(2,1)S(1)} collective-permute-done((bf16[1488,128]{1,0:T(8,128)(2,1)S(1)}, bf16[1488,128]{1,0:T(8,128)(2,1)S(1)}, u32[]{:S(2)}, u32[]{:S(2)}) %collective-permute-start.1) | collective-permute-done | bytes 380960 | tf_op jit(solution)/shard_map/ppermute | solution.py:51
  19.2 1.8 %collective-permute-start.4 = (bf16[1488,128]{1,0:T(8,128)(2,1)S(1)}, bf16[1488,128]{1,0:T(8,128)(2,1)S(1)}, u32[]{:S(2)}, u32[]{:S(2)}) collective-permute-start(bf16[1488,128]{1,0:T(8,128)(2,1)S(1)} %collective-permute-done.1.refs_0_.refs_6_), channel_id=1, source_target_pairs={{0,4},{1,3},{4,8},{5,1},{8,12},{9,5},{12,14},{13,9},{14,10},{15,13... | collective-permute-start | bytes 1142792 | tf_op jit(solution)/shard_map/ppermute | solution.py:51
  21.0 0.8 %stage.8 = (f32[256,1024]{1,0:T(8,128)S(1)}, f32[128,256]{1,0:T(8,128)S(1)}) custom-call(s32[1]{0:T(128)} %bitcast.me_ref, bf16[1488,128]{1,0:T(8,128)(2,1)S(1)} %collective-permute-done.6.refs_0_.refs_3_, bf16[1488,128]{1,0:T(8,128)(2,1)S(1)} %collective-permute-done.7.refs_1_.refs_5_, ...), custom_call_target="tpu_custom_call", output_to_operand_aliasing={{0}: (10, {}), {1}: (11, {})} | custom-call | flops 167772160 | bytes 2097152 | tf_op jit(solution)/shard_map/stage/pallas_call | solution.py:474
  21.7 1.5 %collective-permute-done.5.refs_1_.block_ref.refs_8_ = bf16[1488,128]{1,0:T(8,128)(2,1)S(1)} collective-permute-done((bf16[1488,128]{1,0:T(8,128)(2,1)S(1)}, bf16[1488,128]{1,0:T(8,128)(2,1)S(1)}, u32[]{:S(2)}, u32[]{:S(2)}) %collective-permute-start.5) | collective-permute-done | bytes 380960 | tf_op jit(solution)/shard_map/ppermute | solution.py:51
  23.3 1.8 %collective-permute-start.8 = (bf16[1040,128]{1,0:T(8,128)(2,1)S(1)}, bf16[1040,128]{1,0:T(8,128)(2,1)S(1)}, u32[]{:S(2)}, u32[]{:S(2)}) collective-permute-start(bf16[1040,128]{1,0:T(8,128)(2,1)S(1)} %get-tuple-element.101), channel_id=1, source_target_pairs={{0,4},{1,3},{4,8},{5,1},{8,12},{9,5},{12,14},{13,9},{14,10},{15,13... | collective-permute-start | bytes 798728 | tf_op jit(solution)/shard_map/ppermute | solution.py:51
  25.1 0.7 %stage.9 = (f32[256,1024]{1,0:T(8,128)S(1)}, f32[128,256]{1,0:T(8,128)S(1)}) custom-call(s32[1]{0:T(128)} %bitcast.me_ref, bf16[1488,128]{1,0:T(8,128)(2,1)S(1)} %collective-permute-done.1.refs_0_.refs_6_, bf16[1488,128]{1,0:T(8,128)(2,1)S(1)} %collective-permute-done.5.refs_1_.block_ref.refs_8_, ...), custom_call_target="tpu_custom_call", output_to_operand_aliasing={{0}: (10, {}), {1}: (11, {})} | custom-call | flops 167772160 | bytes 2097152 | tf_op jit(solution)/shard_map/stage/pallas_call | solution.py:474
  25.9 1.5 %collective-permute-done.4.block_ref.refs_0_.refs_10_ = bf16[1488,128]{1,0:T(8,128)(2,1)S(1)} collective-permute-done((bf16[1488,128]{1,0:T(8,128)(2,1)S(1)}, bf16[1488,128]{1,0:T(8,128)(2,1)S(1)}, u32[]{:S(2)}, u32[]{:S(2)}) %collective-permute-start.4) | collective-permute-done | bytes 380960 | tf_op jit(solution)/shard_map/ppermute | solution.py:51
  27.4 1.8 %collective-permute-start.12 = (bf16[960,128]{1,0:T(8,128)(2,1)S(1)}, bf16[960,128]{1,0:T(8,128)(2,1)S(1)}, u32[]{:S(2)}, u32[]{:S(2)}) collective-permute-start(bf16[960,128]{1,0:T(8,128)(2,1)S(1)} %get-tuple-element.109), channel_id=1, source_target_pairs={{0,4},{1,3},{4,8},{5,1},{8,12},{9,5},{12,14},{13,9},{14,10},{15,13... | collective-permute-start | bytes 737288 | tf_op jit(solution)/shard_map/ppermute | solution.py:51
  29.2 0.8 %stage.10 = (f32[256,1024]{1,0:T(8,128)S(1)}, f32[128,256]{1,0:T(8,128)S(1)}) custom-call(s32[1]{0:T(128)} %bitcast.me_ref, bf16[1488,128]{1,0:T(8,128)(2,1)S(1)} %collective-permute-done.9.refs_0_.refs_7_, bf16[1488,128]{1,0:T(8,128)(2,1)S(1)} %collective-permute-done.10.refs_1_.refs_9_, ...), custom_call_target="tpu_custom_call", output_to_operand_aliasing={{0}: (10, {}), {1}: (11, {})} | custom-call | flops 167772160 | bytes 2097152 | tf_op jit(solution)/shard_map/stage/pallas_call | solution.py:474
  30.0 0.2 collective-permute-done.8.refs_1_.refs_12_
  30.2 0.4 collective-permute-start.15
  30.6 1.6 %collective-permute-start.11 = (bf16[976,128]{1,0:T(8,128)(2,1)S(1)}, bf16[976,128]{1,0:T(8,128)(2,1)S(1)}, u32[]{:S(2)}, u32[]{:S(2)}) collective-permute-start(bf16[976,128]{1,0:T(8,128)(2,1)S(1)} %get-tuple-element.108), channel_id=1, source_target_pairs={{0,4},{1,3},{4,8},{5,1},{8,12},{9,5},{12,14},{13,9},{14,10},{15,13... | collective-permute-start | bytes 749576 | tf_op jit(solution)/shard_map/ppermute | solution.py:51
  32.2 0.8 %stage.11 = (f32[256,1024]{1,0:T(8,128)S(1)}, f32[128,256]{1,0:T(8,128)S(1)}) custom-call(s32[1]{0:T(128)} %bitcast.me_ref, bf16[1488,128]{1,0:T(8,128)(2,1)S(1)} %collective-permute-done.4.block_ref.refs_0_.refs_10_, bf16[1040,128]{1,0:T(8,128)(2,1)S(1)} %collective-permute-done.8.refs_1_.refs_12_, ...), custom_call_target="tpu_custom_call", output_to_operand_aliasing={{0}: (10, {}), {1}: (11, {})} | custom-call | flops 167772160 | bytes 2097152 | tf_op jit(solution)/shard_map/stage/pallas_call | solution.py:474
  32.9 0.7 %collective-permute-done.12.refs_2_ = bf16[960,128]{1,0:T(8,128)(2,1)S(1)} collective-permute-done((bf16[960,128]{1,0:T(8,128)(2,1)S(1)}, bf16[960,128]{1,0:T(8,128)(2,1)S(1)}, u32[]{:S(2)}, u32[]{:S(2)}) %collective-permute-start.12) | collective-permute-done | bytes 245792 | tf_op jit(solution)/shard_map/ppermute | solution.py:51
  33.7 1.2 %stage_and_half.1 = (f32[256,1024]{1,0:T(8,128)S(1)}, f32[128,256]{1,0:T(8,128)S(1)}) custom-call(s32[1]{0:T(128)} %bitcast.me_ref, bf16[1488,128]{1,0:T(8,128)(2,1)S(1)} %collective-permute-done.14.refs_0_.refs_11_, bf16[1040,128]{1,0:T(8,128)(2,1)S(1)} %collective-permute-done.15.refs_1_.refs_13_, ...), custom_call_target="tpu_custom_call", output_to_operand_aliasing={{0}: (11, {}), {1}: (12, {})} | custom-call | flops 1 | bytes 1 | tf_op jit(solution)/shard_map/stage_and_half/pallas_call | solution.py:538
  34.8 0.3 collective-permute-done.13.refs_0_
  35.2 0.6 %half_stage.1 = (f32[256,1024]{1,0:T(8,128)S(1)}, f32[128,256]{1,0:T(8,128)S(1)}) custom-call(s32[1]{0:T(128)} %bitcast.me_ref, bf16[960,128]{1,0:T(8,128)(2,1)S(1)} %collective-permute-done.13.refs_0_, bf16[256,5120]{1,0:T(8,128)(2,1)S(1)} %get-tuple-element.74.refs_2_.refs_3_.refs_1_, ...), custom_call_target="tpu_custom_call", output_to_operand_aliasing={{0}: (9, {}), {1}: (10, {})} | custom-call | flops 1 | bytes 1 | tf_op jit(solution)/shard_map/half_stage/pallas_call | solution.py:551
  35.8 1.0 %collective-permute-done.11.refs_14_ = bf16[976,128]{1,0:T(8,128)(2,1)S(1)} collective-permute-done((bf16[976,128]{1,0:T(8,128)(2,1)S(1)}, bf16[976,128]{1,0:T(8,128)(2,1)S(1)}, u32[]{:S(2)}, u32[]{:S(2)}) %collective-permute-start.11) | collective-permute-done | bytes 249888 | tf_op jit(solution)/shard_map/ppermute | solution.py:51
  36.8 1.2 %features.1.unit_ref = f32[128,128]{1,0:T(8,128)S(1)} custom-call(s32[1,2]{1,0:T(1,128)S(1)} %copy-done, f32[256,1024]{1,0:T(8,128)S(1)} %get-tuple-element.122.refs_0_, f32[128,256]{1,0:T(8,128)S(1)} %get-tuple-element.123.refs_1_, f32[256,384]{1,0:T(8,128)S(1)} %get-tuple-element.124.refs_2_, bf16[64,128]{1,0:T(8,128)(2,1)S(1)} %get-tuple-element.125.refs_3_, ...), custom_call_target="tpu_custom_call" | custom-call | flops 1 | bytes 1 | tf_op jit(solution)/shard_map/features/pallas_call | solution.py:564
  38.0 0.3 collective-permute-done.16.refs_15_
  38.3 1.6 %scores.1 = (f32[2,3]{1,0:T(2,128)}, f32[1,2]{1,0:T(1,128)}) custom-call(f32[128,128]{1,0:T(8,128)S(1)} %features.1.unit_ref, bf16[1488,128]{1,0:T(8,128)(2,1)S(1)} %pack.1.refs_0_, bf16[1488,128]{1,0:T(8,128)(2,1)S(1)} %collective-permute-done.2.refs_1_, bf16[1488,128]{1,0:T(8,128)(2,1)S(1)} %collective-permute-done.refs_0_.refs_2_, ...), custom_call_target="tpu_custom_call" | custom-call | flops 4194304 | bytes 2097152 | tf_op jit(solution)/shard_map/scores/pallas_call | solution.py:585
  (18 shorter events, 0.1 us)
Async XLA Ops:
  2.0 3.2 %collective-permute-start.2 = (bf16[1488,128]{1,0:T(8,128)(2,1)S(1)}, bf16[1488,128]{1,0:T(8,128)(2,1)S(1)}, u32[]{:S(2)}, u32[]{:S(2)}) collective-permute-start(bf16[1488,128]{1,0:T(8,128)(2,1)S(1)} %pack.1.refs_0_), channel_id=1, source_target_pairs={{0,1},{1,0},{2,3},{3,2},{4,5},{5,4},{6,7},{7,6},{8,9},{9,8},{10,11... | collective-permute-start | bytes 1142792 | tf_op jit(solution)/shard_map/ppermute | solution.py:55
  2.5 9.0 %collective-permute-start = (bf16[1488,128]{1,0:T(8,128)(2,1)S(1)}, bf16[1488,128]{1,0:T(8,128)(2,1)S(1)}, u32[]{:S(2)}, u32[]{:S(2)}) collective-permute-start(bf16[1488,128]{1,0:T(8,128)(2,1)S(1)} %pack.1.refs_0_), channel_id=1, source_target_pairs={{0,4},{1,3},{4,8},{5,1},{8,12},{9,5},{12,14},{13,9},{14,10},{15,13... | collective-permute-start | bytes 1142792 | tf_op jit(solution)/shard_map/ppermute | solution.py:51
  5.1 9.6 %collective-permute-start.3 = (bf16[1488,128]{1,0:T(8,128)(2,1)S(1)}, bf16[1488,128]{1,0:T(8,128)(2,1)S(1)}, u32[]{:S(2)}, u32[]{:S(2)}) collective-permute-start(bf16[1488,128]{1,0:T(8,128)(2,1)S(1)} %collective-permute-done.2.refs_1_), channel_id=1, source_target_pairs={{0,4},{1,3},{4,8},{5,1},{8,12},{9,5},{12,14},{13,9},{14,10},{15,13... | collective-permute-start | bytes 1142792 | tf_op jit(solution)/shard_map/ppermute | solution.py:51
  11.5 7.7 %collective-permute-start.1 = (bf16[1488,128]{1,0:T(8,128)(2,1)S(1)}, bf16[1488,128]{1,0:T(8,128)(2,1)S(1)}, u32[]{:S(2)}, u32[]{:S(2)}) collective-permute-start(bf16[1488,128]{1,0:T(8,128)(2,1)S(1)} %collective-permute-done.refs_0_.refs_2_), channel_id=1, source_target_pairs={{0,4},{1,3},{4,8},{5,1},{8,12},{9,5},{12,14},{13,9},{14,10},{15,13... | collective-permute-start | bytes 1142792 | tf_op jit(solution)/shard_map/ppermute | solution.py:51
  13.1 7.8 %collective-permute-start.6 = (bf16[1488,128]{1,0:T(8,128)(2,1)S(1)}, bf16[1488,128]{1,0:T(8,128)(2,1)S(1)}, u32[]{:S(2)}, u32[]{:S(2)}) collective-permute-start(bf16[1488,128]{1,0:T(8,128)(2,1)S(1)} %collective-permute-done.refs_0_.refs_2_), channel_id=1, source_target_pairs={{0,1},{1,0},{2,3},{3,2},{4,5},{5,4},{6,7},{7,6},{8,9},{9,8},{10,11... | collective-permute-start | bytes 1142792 | tf_op jit(solution)/shard_map/ppermute | solution.py:55
  14.8 6.2 %collective-permute-start.7 = (bf16[1488,128]{1,0:T(8,128)(2,1)S(1)}, bf16[1488,128]{1,0:T(8,128)(2,1)S(1)}, u32[]{:S(2)}, u32[]{:S(2)}) collective-permute-start(bf16[1488,128]{1,0:T(8,128)(2,1)S(1)} %collective-permute-done.3.refs_1_.refs_4_), channel_id=1, source_target_pairs={{0,1},{1,0},{2,3},{3,2},{4,5},{5,4},{6,7},{7,6},{8,9},{9,8},{10,11... | collective-permute-start | bytes 1142792 | tf_op jit(solution)/shard_map/ppermute | solution.py:55
  14.8 8.5 %collective-permute-start.5 = (bf16[1488,128]{1,0:T(8,128)(2,1)S(1)}, bf16[1488,128]{1,0:T(8,128)(2,1)S(1)}, u32[]{:S(2)}, u32[]{:S(2)}) collective-permute-start(bf16[1488,128]{1,0:T(8,128)(2,1)S(1)} %collective-permute-done.3.refs_1_.refs_4_), channel_id=1, source_target_pairs={{0,4},{1,3},{4,8},{5,1},{8,12},{9,5},{12,14},{13,9},{14,10},{15,13... | collective-permute-start | bytes 1142792 | tf_op jit(solution)/shard_map/ppermute | solution.py:51
  19.2 8.2 %collective-permute-start.4 = (bf16[1488,128]{1,0:T(8,128)(2,1)S(1)}, bf16[1488,128]{1,0:T(8,128)(2,1)S(1)}, u32[]{:S(2)}, u32[]{:S(2)}) collective-permute-start(bf16[1488,128]{1,0:T(8,128)(2,1)S(1)} %collective-permute-done.1.refs_0_.refs_6_), channel_id=1, source_target_pairs={{0,4},{1,3},{4,8},{5,1},{8,12},{9,5},{12,14},{13,9},{14,10},{15,13... | collective-permute-start | bytes 1142792 | tf_op jit(solution)/shard_map/ppermute | solution.py:51
  21.0 8.3 %collective-permute-start.9 = (bf16[1488,128]{1,0:T(8,128)(2,1)S(1)}, bf16[1488,128]{1,0:T(8,128)(2,1)S(1)}, u32[]{:S(2)}, u32[]{:S(2)}) collective-permute-start(bf16[1488,128]{1,0:T(8,128)(2,1)S(1)} %collective-permute-done.1.refs_0_.refs_6_), channel_id=1, source_target_pairs={{0,1},{1,0},{2,3},{3,2},{4,5},{5,4},{6,7},{7,6},{8,9},{9,8},{10,11... | collective-permute-start | bytes 1142792 | tf_op jit(solution)/shard_map/ppermute | solution.py:55
  23.3 5.9 %collective-permute-start.10 = (bf16[1488,128]{1,0:T(8,128)(2,1)S(1)}, bf16[1488,128]{1,0:T(8,128)(2,1)S(1)}, u32[]{:S(2)}, u32[]{:S(2)}) collective-permute-start(bf16[1488,128]{1,0:T(8,128)(2,1)S(1)} %collective-permute-done.5.refs_1_.block_ref.refs_8_), channel_id=1, source_target_pairs={{0,1},{1,0},{2,3},{3,2},{4,5},{5,4},{6,7},{7,6},{8,9},{9,8},{10,11... | collective-permute-start | bytes 1142792 | tf_op jit(solution)/shard_map/ppermute | solution.py:55
  23.3 6.9 %collective-permute-start.8 = (bf16[1040,128]{1,0:T(8,128)(2,1)S(1)}, bf16[1040,128]{1,0:T(8,128)(2,1)S(1)}, u32[]{:S(2)}, u32[]{:S(2)}) collective-permute-start(bf16[1040,128]{1,0:T(8,128)(2,1)S(1)} %get-tuple-element.101), channel_id=1, source_target_pairs={{0,4},{1,3},{4,8},{5,1},{8,12},{9,5},{12,14},{13,9},{14,10},{15,13... | collective-permute-start | bytes 798728 | tf_op jit(solution)/shard_map/ppermute | solution.py:51
  27.4 6.2 %collective-permute-start.12 = (bf16[960,128]{1,0:T(8,128)(2,1)S(1)}, bf16[960,128]{1,0:T(8,128)(2,1)S(1)}, u32[]{:S(2)}, u32[]{:S(2)}) collective-permute-start(bf16[960,128]{1,0:T(8,128)(2,1)S(1)} %get-tuple-element.109), channel_id=1, source_target_pairs={{0,4},{1,3},{4,8},{5,1},{8,12},{9,5},{12,14},{13,9},{14,10},{15,13... | collective-permute-start | bytes 737288 | tf_op jit(solution)/shard_map/ppermute | solution.py:51
  29.2 4.4 %collective-permute-start.14 = (bf16[1488,128]{1,0:T(8,128)(2,1)S(1)}, bf16[1488,128]{1,0:T(8,128)(2,1)S(1)}, u32[]{:S(2)}, u32[]{:S(2)}) collective-permute-start(bf16[1488,128]{1,0:T(8,128)(2,1)S(1)} %collective-permute-done.4.block_ref.refs_0_.refs_10_), channel_id=1, source_target_pairs={{0,1},{1,0},{2,3},{3,2},{4,5},{5,4},{6,7},{7,6},{8,9},{9,8},{10,11... | collective-permute-start | bytes 1142792 | tf_op jit(solution)/shard_map/ppermute | solution.py:55
  30.2 3.4 %collective-permute-start.15 = (bf16[1040,128]{1,0:T(8,128)(2,1)S(1)}, bf16[1040,128]{1,0:T(8,128)(2,1)S(1)}, u32[]{:S(2)}, u32[]{:S(2)}) collective-permute-start(bf16[1040,128]{1,0:T(8,128)(2,1)S(1)} %collective-permute-done.8.refs_1_.refs_12_), channel_id=1, source_target_pairs={{0,1},{1,0},{2,3},{3,2},{4,5},{5,4},{6,7},{7,6},{8,9},{9,8},{10,11... | collective-permute-start | bytes 798728 | tf_op jit(solution)/shard_map/ppermute | solution.py:55
  30.6 6.2 %collective-permute-start.11 = (bf16[976,128]{1,0:T(8,128)(2,1)S(1)}, bf16[976,128]{1,0:T(8,128)(2,1)S(1)}, u32[]{:S(2)}, u32[]{:S(2)}) collective-permute-start(bf16[976,128]{1,0:T(8,128)(2,1)S(1)} %get-tuple-element.108), channel_id=1, source_target_pairs={{0,4},{1,3},{4,8},{5,1},{8,12},{9,5},{12,14},{13,9},{14,10},{15,13... | collective-permute-start | bytes 749576 | tf_op jit(solution)/shard_map/ppermute | solution.py:51
  33.6 1.5 %collective-permute-start.13 = (bf16[960,128]{1,0:T(8,128)(2,1)S(1)}, bf16[960,128]{1,0:T(8,128)(2,1)S(1)}, u32[]{:S(2)}, u32[]{:S(2)}) collective-permute-start(bf16[960,128]{1,0:T(8,128)(2,1)S(1)} %collective-permute-done.12.refs_2_), channel_id=1, source_target_pairs={{0,1},{1,0},{2,3},{3,2},{4,5},{5,4},{6,7},{7,6},{8,9},{9,8},{10,11... | collective-permute-start | bytes 737288 | tf_op jit(solution)/shard_map/ppermute | solution.py:55
  35.2 1.7 %copy-start = (s32[1,2]{1,0:T(1,128)S(1)}, s32[1,2]{1,0:T(1,128)}, u32[]{:S(2)}) copy-start(s32[1,2]{1,0:T(1,128)} %counts_ref.1) | copy-start | bytes 28
  36.8 1.5 %collective-permute-start.16 = (bf16[976,128]{1,0:T(8,128)(2,1)S(1)}, bf16[976,128]{1,0:T(8,128)(2,1)S(1)}, u32[]{:S(2)}, u32[]{:S(2)}) collective-permute-start(bf16[976,128]{1,0:T(8,128)(2,1)S(1)} %collective-permute-done.11.refs_14_), channel_id=1, source_target_pairs={{0,1},{1,0},{2,3},{3,2},{4,5},{5,4},{6,7},{7,6},{8,9},{9,8},{10,11... | collective-permute-start | bytes 749576 | tf_op jit(solution)/shard_map/ppermute | solution.py:55

commit v19 on v17

--- a/solution.py
+++ b/solution.py
@@ -46,8 +46,8 @@
     place = [2 * q if q < half else 2 * (RING_CHIPS - 1 - q) + 1 for q in range(RING_CHIPS)]
     pairs = []
     for q in range(RING_CHIPS):
-        pairs.append((2 * place[q], 2 * place[(q + 1) % RING_CHIPS]))
-        pairs.append((2 * place[q] + 1, 2 * place[(q - 1) % RING_CHIPS] + 1))
+        pairs.append((2 * place[q], 2 * place[(q - 1) % RING_CHIPS]))
+        pairs.append((2 * place[q] + 1, 2 * place[(q + 1) % RING_CHIPS] + 1))
     return lax.ppermute(value, "dp", pairs)
 
 
@@ -164,7 +164,7 @@
     span = 2 * rows
     me = me_ref[0]
     pos, core = ring_pos(me // 2), me % 2
-    chip = ring_chip((pos + away * (2 * core - 1) + RING_CHIPS) % RING_CHIPS)
+    chip = ring_chip((pos + away * (1 - 2 * core) + RING_CHIPS) % RING_CHIPS)
     odd = chip % 2
     mine = pl.ds(pl.multiple_of(chip * span, LANES), span)
     values_start = (chip // 2) * span + odd * (rows - pad)
@@ -218,7 +218,7 @@
     half, span = rows // 2, 2 * rows
     me = me_ref[0]
     pos, core = ring_pos(me // 2), me % 2
-    chip = ring_chip((pos + away * (2 * core - 1) + RING_CHIPS) % RING_CHIPS)
+    chip = ring_chip((pos + away * (1 - 2 * core) + RING_CHIPS) % RING_CHIPS)
     side = 1 - core if other else core
     odd = chip % 2
     mine = pl.ds(pl.multiple_of(chip * span + side * (rows - pad), LANES), rows + pad)

time: 39.6 us -> 39.5 us (level)
  no operation moved by 1% of the time
where the time goes in v19:
time: 39.5 us; the launch traced here: 39.3 us
  starting transfers between devices  15.7 us (40%)
  Pallas kernels  15.2 us (38%)
  waiting for transfers between devices  7.55 us (19%)
  between operations  0.78 us (2%)
    ppermute x8, starting transfers between devices, hop(): return lax.ppermute(value, 'dp', pairs)  14.9 us
    ppermute x8, waiting for transfers between devices, hop(): return lax.ppermute(value, 'dp', pairs)  6.75 us
    pallas_call x1, Pallas kernels, shards(): pl.pallas_call(local_kernel, out_shape=[jax.ShapeDtypeStruct(a.shape, a.d...  4.69 us
    pallas_call x6, Pallas kernels, stage(): pl.pallas_call(functools.partial(stage_kernel, away, first), out_shape=[j...  4.53 us
    pallas_call x1, Pallas kernels, shards(): pl.pallas_call(functools.partial(feature_kernel, half), out_shape=jax.Sha...  1.79 us
    pallas_call x1, Pallas kernels, shards(): pl.pallas_call(pack_kernel, out_shape=jax.ShapeDtypeStruct((3 * rows + (L...  1.35 us
    pallas_call x1, Pallas kernels, shards(): pl.pallas_call(functools.partial(stage_and_half_kernel, 1 - half, half),...  1.18 us
    pallas_call x1, Pallas kernels, shards(): pl.pallas_call(functools.partial(score_kernel, len(blocks), count), out_s...  0.86 us
  transfers between devices with their start and end apart: 17, of which 7 were waited for; matrix products, arithmetic and copies ran while one was open for 0% of the time, Pallas kernels for 33%

profile of v19, /device:TPU:0, one launch (start us, length us, event | category | flops | bytes accessed | tf_op | source)
XLA Modules:
  0.0 39.3 jit_solution(13487829733323978864)
XLA Ops:
  0.6 1.3 %pack.1.refs_0_ = bf16[1488,128]{1,0:T(8,128)(2,1)S(1)} custom-call(s32[1]{0:T(128)} %bitcast.me_ref, bf16[160,128]{1,0:T(8,128)(2,1)} %bitcast.14, bf16[8,8192]{1,0:T(8,128)(2,1)} %refs_1_.2, bf16[320,128]{1,0:T(8,128)(2,1)} %refs_2_.2, bf16[320,128]{1,0:T(8,128)(2,1)} %bitcast.13, bf16[320,128]{1,0:T(8,128)(2,1)} %refs_4_.2, f32[40,128]{1,0:T(8,128)} %bitcast.11, ...), custom_call_target="tpu_custom_call" | custom-call | tf_op jit(solution)/shard_map/pack/pallas_call | solution.py:439
  2.0 0.5 %collective-permute-start.2 = (bf16[1488,128]{1,0:T(8,128)(2,1)S(1)}, bf16[1488,128]{1,0:T(8,128)(2,1)S(1)}, u32[]{:S(2)}, u32[]{:S(2)}) collective-permute-start(bf16[1488,128]{1,0:T(8,128)(2,1)S(1)} %pack.1.refs_0_), channel_id=1, source_target_pairs={{0,1},{1,0},{2,3},{3,2},{4,5},{5,4},{6,7},{7,6},{8,9},{9,8},{10,11... | collective-permute-start | bytes 1142792 | tf_op jit(solution)/shard_map/ppermute | solution.py:55
  2.5 2.6 %collective-permute-start = (bf16[1488,128]{1,0:T(8,128)(2,1)S(1)}, bf16[1488,128]{1,0:T(8,128)(2,1)S(1)}, u32[]{:S(2)}, u32[]{:S(2)}) collective-permute-start(bf16[1488,128]{1,0:T(8,128)(2,1)S(1)} %pack.1.refs_0_), channel_id=1, source_target_pairs={{0,2},{1,5},{4,0},{5,9},{8,4},{9,13},{12,8},{13,15},{14,12},{15,11... | collective-permute-start | bytes 1142792 | tf_op jit(solution)/shard_map/ppermute | solution.py:51
  5.1 1.6 %collective-permute-start.3 = (bf16[1488,128]{1,0:T(8,128)(2,1)S(1)}, bf16[1488,128]{1,0:T(8,128)(2,1)S(1)}, u32[]{:S(2)}, u32[]{:S(2)}) collective-permute-start(bf16[1488,128]{1,0:T(8,128)(2,1)S(1)} %collective-permute-done.2.refs_1_), channel_id=1, source_target_pairs={{0,2},{1,5},{4,0},{5,9},{8,4},{9,13},{12,8},{13,15},{14,12},{15,11... | collective-permute-start | bytes 1142792 | tf_op jit(solution)/shard_map/ppermute | solution.py:51
  6.7 4.7 %local_products.1 = (bf16[256,5120]{1,0:T(8,128)(2,1)S(1)}, bf16[256,5120]{1,0:T(8,128)(2,1)S(1)}, bf16[256,5120]{1,0:T(8,128)(2,1)S(1)}, bf16[256,2560]{1,0:T(8...) custom-call(bf16[256,5120]{1,0:T(8,128)(2,1)} %refs_0_.1, ...), custom_call_target="tpu_custom_call" | custom-call | flops 1006632960 | bytes 14680064 | tf_op jit(solution)/shard_map/local_products/pallas_call | solution.py:462
  11.4 1.6 %collective-permute-start.1 = (bf16[1488,128]{1,0:T(8,128)(2,1)S(1)}, bf16[1488,128]{1,0:T(8,128)(2,1)S(1)}, u32[]{:S(2)}, u32[]{:S(2)}) collective-permute-start(bf16[1488,128]{1,0:T(8,128)(2,1)S(1)} %collective-permute-done.refs_0_.refs_2_), channel_id=1, source_target_pairs={{0,2},{1,5},{4,0},{5,9},{8,4},{9,13},{12,8},{13,15},{14,12},{15,11... | collective-permute-start | bytes 1142792 | tf_op jit(solution)/shard_map/ppermute | solution.py:51
  13.1 0.7 %stage.6 = (f32[256,1024]{1,0:T(8,128)S(1)}, f32[128,256]{1,0:T(8,128)S(1)}) custom-call(s32[1]{0:T(128)} %bitcast.me_ref, bf16[1488,128]{1,0:T(8,128)(2,1)S(1)} %pack.1.refs_0_, bf16[1488,128]{1,0:T(8,128)(2,1)S(1)} %collective-permute-done.2.refs_1_, bf16[256,5120]{1,0:T(8,128)(2,1)S(1)} %get-tuple-element.71.refs_2_.refs_3_.refs_1_, ...), custom_call_target="tpu_custom_call" | custom-call | flops 167772160 | bytes 2097152 | tf_op jit(solution)/shard_map/stage/pallas_call | solution.py:488
  13.8 1.1 %collective-permute-done.3.refs_1_.refs_4_ = bf16[1488,128]{1,0:T(8,128)(2,1)S(1)} collective-permute-done((bf16[1488,128]{1,0:T(8,128)(2,1)S(1)}, bf16[1488,128]{1,0:T(8,128)(2,1)S(1)}, u32[]{:S(2)}, u32[]{:S(2)}) %collective-permute-start.3) | collective-permute-done | bytes 380960 | tf_op jit(solution)/shard_map/ppermute | solution.py:51
  14.9 0.0 collective-permute-start.7
  14.9 2.0 %collective-permute-start.5 = (bf16[1488,128]{1,0:T(8,128)(2,1)S(1)}, bf16[1488,128]{1,0:T(8,128)(2,1)S(1)}, u32[]{:S(2)}, u32[]{:S(2)}) collective-permute-start(bf16[1488,128]{1,0:T(8,128)(2,1)S(1)} %collective-permute-done.3.refs_1_.refs_4_), channel_id=1, source_target_pairs={{0,2},{1,5},{4,0},{5,9},{8,4},{9,13},{12,8},{13,15},{14,12},{15,11... | collective-permute-start | bytes 1142792 | tf_op jit(solution)/shard_map/ppermute | solution.py:51
  16.8 0.8 %stage.7 = (f32[256,1024]{1,0:T(8,128)S(1)}, f32[128,256]{1,0:T(8,128)S(1)}) custom-call(s32[1]{0:T(128)} %bitcast.me_ref, bf16[1488,128]{1,0:T(8,128)(2,1)S(1)} %collective-permute-done.refs_0_.refs_2_, bf16[1488,128]{1,0:T(8,128)(2,1)S(1)} %collective-permute-done.3.refs_1_.refs_4_, ...), custom_call_target="tpu_custom_call", output_to_operand_aliasing={{0}: (10, {}), {1}: (11, {})} | custom-call | flops 167772160 | bytes 2097152 | tf_op jit(solution)/shard_map/stage/pallas_call | solution.py:488
  17.6 1.5 %collective-permute-done.1.refs_0_.refs_6_ = bf16[1488,128]{1,0:T(8,128)(2,1)S(1)} collective-permute-done((bf16[1488,128]{1,0:T(8,128)(2,1)S(1)}, bf16[1488,128]{1,0:T(8,128)(2,1)S(1)}, u32[]{:S(2)}, u32[]{:S(2)}) %collective-permute-start.1) | collective-permute-done | bytes 380960 | tf_op jit(solution)/shard_map/ppermute | solution.py:51
  19.1 1.8 %collective-permute-start.4 = (bf16[1488,128]{1,0:T(8,128)(2,1)S(1)}, bf16[1488,128]{1,0:T(8,128)(2,1)S(1)}, u32[]{:S(2)}, u32[]{:S(2)}) collective-permute-start(bf16[1488,128]{1,0:T(8,128)(2,1)S(1)} %collective-permute-done.1.refs_0_.refs_6_), channel_id=1, source_target_pairs={{0,2},{1,5},{4,0},{5,9},{8,4},{9,13},{12,8},{13,15},{14,12},{15,11... | collective-permute-start | bytes 1142792 | tf_op jit(solution)/shard_map/ppermute | solution.py:51
  20.9 0.8 %stage.8 = (f32[256,1024]{1,0:T(8,128)S(1)}, f32[128,256]{1,0:T(8,128)S(1)}) custom-call(s32[1]{0:T(128)} %bitcast.me_ref, bf16[1488,128]{1,0:T(8,128)(2,1)S(1)} %collective-permute-done.6.refs_0_.refs_3_, bf16[1488,128]{1,0:T(8,128)(2,1)S(1)} %collective-permute-done.7.refs_1_.refs_5_, ...), custom_call_target="tpu_custom_call", output_to_operand_aliasing={{0}: (10, {}), {1}: (11, {})} | custom-call | flops 167772160 | bytes 2097152 | tf_op jit(solution)/shard_map/stage/pallas_call | solution.py:488
  21.7 1.5 %collective-permute-done.5.refs_1_.block_ref.refs_8_ = bf16[1488,128]{1,0:T(8,128)(2,1)S(1)} collective-permute-done((bf16[1488,128]{1,0:T(8,128)(2,1)S(1)}, bf16[1488,128]{1,0:T(8,128)(2,1)S(1)}, u32[]{:S(2)}, u32[]{:S(2)}) %collective-permute-start.5) | collective-permute-done | bytes 380960 | tf_op jit(solution)/shard_map/ppermute | solution.py:51
  23.3 1.8 %collective-permute-start.8 = (bf16[960,128]{1,0:T(8,128)(2,1)S(1)}, bf16[960,128]{1,0:T(8,128)(2,1)S(1)}, u32[]{:S(2)}, u32[]{:S(2)}) collective-permute-start(bf16[960,128]{1,0:T(8,128)(2,1)S(1)} %get-tuple-element.98), channel_id=1, source_target_pairs={{0,2},{1,5},{4,0},{5,9},{8,4},{9,13},{12,8},{13,15},{14,12},{15,11... | collective-permute-start | bytes 737288 | tf_op jit(solution)/shard_map/ppermute | solution.py:51
  25.1 0.8 %stage.9 = (f32[256,1024]{1,0:T(8,128)S(1)}, f32[128,256]{1,0:T(8,128)S(1)}) custom-call(s32[1]{0:T(128)} %bitcast.me_ref, bf16[1488,128]{1,0:T(8,128)(2,1)S(1)} %collective-permute-done.1.refs_0_.refs_6_, bf16[1488,128]{1,0:T(8,128)(2,1)S(1)} %collective-permute-done.5.refs_1_.block_ref.refs_8_, ...), custom_call_target="tpu_custom_call", output_to_operand_aliasing={{0}: (10, {}), {1}: (11, {})} | custom-call | flops 167772160 | bytes 2097152 | tf_op jit(solution)/shard_map/stage/pallas_call | solution.py:488
  25.8 1.5 %collective-permute-done.4.block_ref.refs_0_.refs_10_ = bf16[1488,128]{1,0:T(8,128)(2,1)S(1)} collective-permute-done((bf16[1488,128]{1,0:T(8,128)(2,1)S(1)}, bf16[1488,128]{1,0:T(8,128)(2,1)S(1)}, u32[]{:S(2)}, u32[]{:S(2)}) %collective-permute-start.4) | collective-permute-done | bytes 380960 | tf_op jit(solution)/shard_map/ppermute | solution.py:51
  27.3 1.8 %collective-permute-start.12 = (bf16[960,128]{1,0:T(8,128)(2,1)S(1)}, bf16[960,128]{1,0:T(8,128)(2,1)S(1)}, u32[]{:S(2)}, u32[]{:S(2)}) collective-permute-start(bf16[960,128]{1,0:T(8,128)(2,1)S(1)} %get-tuple-element.106), channel_id=1, source_target_pairs={{0,2},{1,5},{4,0},{5,9},{8,4},{9,13},{12,8},{13,15},{14,12},{15,11... | collective-permute-start | bytes 737288 | tf_op jit(solution)/shard_map/ppermute | solution.py:51
  29.2 0.8 %stage.10 = (f32[256,1024]{1,0:T(8,128)S(1)}, f32[128,256]{1,0:T(8,128)S(1)}) custom-call(s32[1]{0:T(128)} %bitcast.me_ref, bf16[1488,128]{1,0:T(8,128)(2,1)S(1)} %collective-permute-done.9.refs_0_.refs_7_, bf16[1488,128]{1,0:T(8,128)(2,1)S(1)} %collective-permute-done.10.refs_1_.refs_9_, ...), custom_call_target="tpu_custom_call", output_to_operand_aliasing={{0}: (10, {}), {1}: (11, {})} | custom-call | flops 167772160 | bytes 2097152 | tf_op jit(solution)/shard_map/stage/pallas_call | solution.py:488
  30.0 1.7 %collective-permute-start.11 = (bf16[1056,128]{1,0:T(8,128)(2,1)S(1)}, bf16[1056,128]{1,0:T(8,128)(2,1)S(1)}, u32[]{:S(2)}, u32[]{:S(2)}) collective-permute-start(bf16[1056,128]{1,0:T(8,128)(2,1)S(1)} %get-tuple-element.105), channel_id=1, source_target_pairs={{0,2},{1,5},{4,0},{5,9},{8,4},{9,13},{12,8},{13,15},{14,12},{15,11... | collective-permute-start | bytes 811016 | tf_op jit(solution)/shard_map/ppermute | solution.py:51
  31.7 0.8 %stage.11 = (f32[256,1024]{1,0:T(8,128)S(1)}, f32[128,256]{1,0:T(8,128)S(1)}) custom-call(s32[1]{0:T(128)} %bitcast.me_ref, bf16[1488,128]{1,0:T(8,128)(2,1)S(1)} %collective-permute-done.4.block_ref.refs_0_.refs_10_, bf16[960,128]{1,0:T(8,128)(2,1)S(1)} %collective-permute-done.8.refs_1_, ...), custom_call_target="tpu_custom_call", output_to_operand_aliasing={{0}: (10, {}), {1}: (11, {})} | custom-call | flops 167772160 | bytes 2097152 | tf_op jit(solution)/shard_map/stage/pallas_call | solution.py:488
  32.5 1.1 %collective-permute-done.12.refs_2_ = bf16[960,128]{1,0:T(8,128)(2,1)S(1)} collective-permute-done((bf16[960,128]{1,0:T(8,128)(2,1)S(1)}, bf16[960,128]{1,0:T(8,128)(2,1)S(1)}, u32[]{:S(2)}, u32[]{:S(2)}) %collective-permute-start.12) | collective-permute-done | bytes 245792 | tf_op jit(solution)/shard_map/ppermute | solution.py:51
  33.6 0.0 collective-permute-start.13
  33.6 0.0 collective-permute-done.14.refs_0_.refs_11_
  33.6 1.2 %stage_and_half.1 = (f32[256,1024]{1,0:T(8,128)S(1)}, f32[128,256]{1,0:T(8,128)S(1)}) custom-call(s32[1]{0:T(128)} %bitcast.me_ref, bf16[1488,128]{1,0:T(8,128)(2,1)S(1)} %collective-permute-done.14.refs_0_.refs_11_, bf16[960,128]{1,0:T(8,128)(2,1)S(1)} %collective-permute-done.15.refs_1_, ...), custom_call_target="tpu_custom_call", output_to_operand_aliasing={{0}: (11, {}), {1}: (12, {})} | custom-call | flops 251658240 | bytes 3145728 | tf_op jit(solution)/shard_map/stage_and_half/pallas_call | solution.py:549
  34.8 0.3 collective-permute-done.13.refs_0_
  35.1 1.8 %features.1.unit_ref = f32[128,128]{1,0:T(8,128)S(1)} custom-call(s32[1]{0:T(128)} %bitcast.me_ref, s32[1,2]{1,0:T(1,128)S(1)} %copy-done, bf16[960,128]{1,0:T(8,128)(2,1)S(1)} %collective-permute-done.13.refs_0_, bf16[256,5120]{1,0:T(8,128)(2,1)S(1)} %get-tuple-element.71.refs_2_.refs_3_.refs_1_, ...), custom_call_target="tpu_custom_call" | custom-call | flops 1 | bytes 1 | tf_op jit(solution)/shard_map/features/pallas_call | solution.py:561
  36.9 0.3 collective-permute-start.16
  37.2 0.9 %scores.1.best_ref = f32[2,3,8,128]{3,2,1,0:T(8,128)S(1)} custom-call(f32[128,128]{1,0:T(8,128)S(1)} %features.1.unit_ref, bf16[1488,128]{1,0:T(8,128)(2,1)S(1)} %pack.1.refs_0_, bf16[1488,128]{1,0:T(8,128)(2,1)S(1)} %collective-permute-done.2.refs_1_, bf16[1488,128]{1,0:T(8,128)(2,1)S(1)} %collective-permute-done.refs_0_.refs_2_, ...), custom_call_target="tpu_custom_call" | custom-call | flops 4194304 | bytes 2097152 | tf_op jit(solution)/shard_map/scores/pallas_call | solution.py:573
  38.0 0.5 %collective-permute-done.16.block_ref = bf16[1056,128]{1,0:T(8,128)(2,1)S(1)} collective-permute-done((bf16[1056,128]{1,0:T(8,128)(2,1)S(1)}, bf16[1056,128]{1,0:T(8,128)(2,1)S(1)}, u32[]{:S(2)}, u32[]{:S(2)}) %collective-permute-start.16) | collective-permute-done | bytes 270368 | tf_op jit(solution)/shard_map/ppermute | solution.py:55
  38.5 0.8 %last_scores.1 = (f32[2,3]{1,0:T(2,128)}, f32[1,2]{1,0:T(1,128)}) custom-call(f32[128,128]{1,0:T(8,128)S(1)} %features.1.unit_ref, bf16[1056,128]{1,0:T(8,128)(2,1)S(1)} %collective-permute-done.16.block_ref, f32[2,3,8,128]{3,2,1,0:T(8,128)S(1)} %scores.1.best_ref), custom_call_target="tpu_custom_call" | custom-call | tf_op jit(solution)/shard_map/last_scores/pallas_call | solution.py:582
  (18 shorter events, 0.1 us)
Async XLA Ops:
  2.0 3.1 %collective-permute-start.2 = (bf16[1488,128]{1,0:T(8,128)(2,1)S(1)}, bf16[1488,128]{1,0:T(8,128)(2,1)S(1)}, u32[]{:S(2)}, u32[]{:S(2)}) collective-permute-start(bf16[1488,128]{1,0:T(8,128)(2,1)S(1)} %pack.1.refs_0_), channel_id=1, source_target_pairs={{0,1},{1,0},{2,3},{3,2},{4,5},{5,4},{6,7},{7,6},{8,9},{9,8},{10,11... | collective-permute-start | bytes 1142792 | tf_op jit(solution)/shard_map/ppermute | solution.py:55
  2.5 8.9 %collective-permute-start = (bf16[1488,128]{1,0:T(8,128)(2,1)S(1)}, bf16[1488,128]{1,0:T(8,128)(2,1)S(1)}, u32[]{:S(2)}, u32[]{:S(2)}) collective-permute-start(bf16[1488,128]{1,0:T(8,128)(2,1)S(1)} %pack.1.refs_0_), channel_id=1, source_target_pairs={{0,2},{1,5},{4,0},{5,9},{8,4},{9,13},{12,8},{13,15},{14,12},{15,11... | collective-permute-start | bytes 1142792 | tf_op jit(solution)/shard_map/ppermute | solution.py:51
  5.1 9.8 %collective-permute-start.3 = (bf16[1488,128]{1,0:T(8,128)(2,1)S(1)}, bf16[1488,128]{1,0:T(8,128)(2,1)S(1)}, u32[]{:S(2)}, u32[]{:S(2)}) collective-permute-start(bf16[1488,128]{1,0:T(8,128)(2,1)S(1)} %collective-permute-done.2.refs_1_), channel_id=1, source_target_pairs={{0,2},{1,5},{4,0},{5,9},{8,4},{9,13},{12,8},{13,15},{14,12},{15,11... | collective-permute-start | bytes 1142792 | tf_op jit(solution)/shard_map/ppermute | solution.py:51
  11.4 7.7 %collective-permute-start.1 = (bf16[1488,128]{1,0:T(8,128)(2,1)S(1)}, bf16[1488,128]{1,0:T(8,128)(2,1)S(1)}, u32[]{:S(2)}, u32[]{:S(2)}) collective-permute-start(bf16[1488,128]{1,0:T(8,128)(2,1)S(1)} %collective-permute-done.refs_0_.refs_2_), channel_id=1, source_target_pairs={{0,2},{1,5},{4,0},{5,9},{8,4},{9,13},{12,8},{13,15},{14,12},{15,11... | collective-permute-start | bytes 1142792 | tf_op jit(solution)/shard_map/ppermute | solution.py:51
  13.1 7.8 %collective-permute-start.6 = (bf16[1488,128]{1,0:T(8,128)(2,1)S(1)}, bf16[1488,128]{1,0:T(8,128)(2,1)S(1)}, u32[]{:S(2)}, u32[]{:S(2)}) collective-permute-start(bf16[1488,128]{1,0:T(8,128)(2,1)S(1)} %collective-permute-done.refs_0_.refs_2_), channel_id=1, source_target_pairs={{0,1},{1,0},{2,3},{3,2},{4,5},{5,4},{6,7},{7,6},{8,9},{9,8},{10,11... | collective-permute-start | bytes 1142792 | tf_op jit(solution)/shard_map/ppermute | solution.py:55
  14.9 6.1 %collective-permute-start.7 = (bf16[1488,128]{1,0:T(8,128)(2,1)S(1)}, bf16[1488,128]{1,0:T(8,128)(2,1)S(1)}, u32[]{:S(2)}, u32[]{:S(2)}) collective-permute-start(bf16[1488,128]{1,0:T(8,128)(2,1)S(1)} %collective-permute-done.3.refs_1_.refs_4_), channel_id=1, source_target_pairs={{0,1},{1,0},{2,3},{3,2},{4,5},{5,4},{6,7},{7,6},{8,9},{9,8},{10,11... | collective-permute-start | bytes 1142792 | tf_op jit(solution)/shard_map/ppermute | solution.py:55
  14.9 8.4 %collective-permute-start.5 = (bf16[1488,128]{1,0:T(8,128)(2,1)S(1)}, bf16[1488,128]{1,0:T(8,128)(2,1)S(1)}, u32[]{:S(2)}, u32[]{:S(2)}) collective-permute-start(bf16[1488,128]{1,0:T(8,128)(2,1)S(1)} %collective-permute-done.3.refs_1_.refs_4_), channel_id=1, source_target_pairs={{0,2},{1,5},{4,0},{5,9},{8,4},{9,13},{12,8},{13,15},{14,12},{15,11... | collective-permute-start | bytes 1142792 | tf_op jit(solution)/shard_map/ppermute | solution.py:51
  19.1 8.2 %collective-permute-start.4 = (bf16[1488,128]{1,0:T(8,128)(2,1)S(1)}, bf16[1488,128]{1,0:T(8,128)(2,1)S(1)}, u32[]{:S(2)}, u32[]{:S(2)}) collective-permute-start(bf16[1488,128]{1,0:T(8,128)(2,1)S(1)} %collective-permute-done.1.refs_0_.refs_6_), channel_id=1, source_target_pairs={{0,2},{1,5},{4,0},{5,9},{8,4},{9,13},{12,8},{13,15},{14,12},{15,11... | collective-permute-start | bytes 1142792 | tf_op jit(solution)/shard_map/ppermute | solution.py:51
  20.9 8.3 %collective-permute-start.9 = (bf16[1488,128]{1,0:T(8,128)(2,1)S(1)}, bf16[1488,128]{1,0:T(8,128)(2,1)S(1)}, u32[]{:S(2)}, u32[]{:S(2)}) collective-permute-start(bf16[1488,128]{1,0:T(8,128)(2,1)S(1)} %collective-permute-done.1.refs_0_.refs_6_), channel_id=1, source_target_pairs={{0,1},{1,0},{2,3},{3,2},{4,5},{5,4},{6,7},{7,6},{8,9},{9,8},{10,11... | collective-permute-start | bytes 1142792 | tf_op jit(solution)/shard_map/ppermute | solution.py:55
  23.2 5.9 %collective-permute-start.10 = (bf16[1488,128]{1,0:T(8,128)(2,1)S(1)}, bf16[1488,128]{1,0:T(8,128)(2,1)S(1)}, u32[]{:S(2)}, u32[]{:S(2)}) collective-permute-start(bf16[1488,128]{1,0:T(8,128)(2,1)S(1)} %collective-permute-done.5.refs_1_.block_ref.refs_8_), channel_id=1, source_target_pairs={{0,1},{1,0},{2,3},{3,2},{4,5},{5,4},{6,7},{7,6},{8,9},{9,8},{10,11... | collective-permute-start | bytes 1142792 | tf_op jit(solution)/shard_map/ppermute | solution.py:55
  23.3 6.7 %collective-permute-start.8 = (bf16[960,128]{1,0:T(8,128)(2,1)S(1)}, bf16[960,128]{1,0:T(8,128)(2,1)S(1)}, u32[]{:S(2)}, u32[]{:S(2)}) collective-permute-start(bf16[960,128]{1,0:T(8,128)(2,1)S(1)} %get-tuple-element.98), channel_id=1, source_target_pairs={{0,2},{1,5},{4,0},{5,9},{8,4},{9,13},{12,8},{13,15},{14,12},{15,11... | collective-permute-start | bytes 737288 | tf_op jit(solution)/shard_map/ppermute | solution.py:51
  27.3 6.2 %collective-permute-start.12 = (bf16[960,128]{1,0:T(8,128)(2,1)S(1)}, bf16[960,128]{1,0:T(8,128)(2,1)S(1)}, u32[]{:S(2)}, u32[]{:S(2)}) collective-permute-start(bf16[960,128]{1,0:T(8,128)(2,1)S(1)} %get-tuple-element.106), channel_id=1, source_target_pairs={{0,2},{1,5},{4,0},{5,9},{8,4},{9,13},{12,8},{13,15},{14,12},{15,11... | collective-permute-start | bytes 737288 | tf_op jit(solution)/shard_map/ppermute | solution.py:51
  29.2 4.4 %collective-permute-start.14 = (bf16[1488,128]{1,0:T(8,128)(2,1)S(1)}, bf16[1488,128]{1,0:T(8,128)(2,1)S(1)}, u32[]{:S(2)}, u32[]{:S(2)}) collective-permute-start(bf16[1488,128]{1,0:T(8,128)(2,1)S(1)} %collective-permute-done.4.block_ref.refs_0_.refs_10_), channel_id=1, source_target_pairs={{0,1},{1,0},{2,3},{3,2},{4,5},{5,4},{6,7},{7,6},{8,9},{9,8},{10,11... | collective-permute-start | bytes 1142792 | tf_op jit(solution)/shard_map/ppermute | solution.py:55
  30.0 6.9 %collective-permute-start.11 = (bf16[1056,128]{1,0:T(8,128)(2,1)S(1)}, bf16[1056,128]{1,0:T(8,128)(2,1)S(1)}, u32[]{:S(2)}, u32[]{:S(2)}) collective-permute-start(bf16[1056,128]{1,0:T(8,128)(2,1)S(1)} %get-tuple-element.105), channel_id=1, source_target_pairs={{0,2},{1,5},{4,0},{5,9},{8,4},{9,13},{12,8},{13,15},{14,12},{15,11... | collective-permute-start | bytes 811016 | tf_op jit(solution)/shard_map/ppermute | solution.py:51
  31.7 1.9 %collective-permute-start.15 = (bf16[960,128]{1,0:T(8,128)(2,1)S(1)}, bf16[960,128]{1,0:T(8,128)(2,1)S(1)}, u32[]{:S(2)}, u32[]{:S(2)}) collective-permute-start(bf16[960,128]{1,0:T(8,128)(2,1)S(1)} %collective-permute-done.8.refs_1_), channel_id=1, source_target_pairs={{0,1},{1,0},{2,3},{3,2},{4,5},{5,4},{6,7},{7,6},{8,9},{9,8},{10,11... | collective-permute-start | bytes 737288 | tf_op jit(solution)/shard_map/ppermute | solution.py:55
  33.6 1.5 %copy-start = (s32[1,2]{1,0:T(1,128)S(1)}, s32[1,2]{1,0:T(1,128)}, u32[]{:S(2)}) copy-start(s32[1,2]{1,0:T(1,128)} %counts_ref.1) | copy-start | bytes 28
  33.6 1.5 %collective-permute-start.13 = (bf16[960,128]{1,0:T(8,128)(2,1)S(1)}, bf16[960,128]{1,0:T(8,128)(2,1)S(1)}, u32[]{:S(2)}, u32[]{:S(2)}) collective-permute-start(bf16[960,128]{1,0:T(8,128)(2,1)S(1)} %collective-permute-done.12.refs_2_), channel_id=1, source_target_pairs={{0,1},{1,0},{2,3},{3,2},{4,5},{5,4},{6,7},{7,6},{8,9},{9,8},{10,11... | collective-permute-start | bytes 737288 | tf_op jit(solution)/shard_map/ppermute | solution.py:55
  36.9 1.6 %collective-permute-start.16 = (bf16[1056,128]{1,0:T(8,128)(2,1)S(1)}, bf16[1056,128]{1,0:T(8,128)(2,1)S(1)}, u32[]{:S(2)}, u32[]{:S(2)}) collective-permute-start(bf16[1056,128]{1,0:T(8,128)(2,1)S(1)} %collective-permute-done.11.refs_12_), channel_id=1, source_target_pairs={{0,1},{1,0},{2,3},{3,2},{4,5},{5,4},{6,7},{7,6},{8,9},{9,8},{10,11... | collective-permute-start | bytes 811016 | tf_op jit(solution)/shard_map/ppermute | solution.py:55

commit v20 on v19

--- a/solution.py
+++ b/solution.py
@@ -324,16 +324,20 @@
     half = LANES // 2
     scale = float(half * LANES) ** 0.5
     shape = (count, LANES)
-    totals = [[jnp.zeros(shape, F32) for _ in range(2)] for _ in places]
+    chains = 4 if len(places) <= 4 else 1
+    partial = [[[None] * chains for _ in range(2)] for _ in places]
     for i in range(0, half, 2):
         units = [
             [jnp.broadcast_to(unit_ref[pl.ds(e * half + i + k, 1), :], shape) for k in range(2)]
             for e in range(2)
         ]
+        c = i // 2 % chains
         for b, (block, start) in enumerate(places):
             wide = block[pl.ds(start + i * count, 2 * count), :].astype(F32)
             for e in range(2):
-                totals[b][e] = totals[b][e] + (wide[:count] * units[e][0] + wide[count:] * units[e][1])
+                pair = wide[:count] * units[e][0] + wide[count:] * units[e][1]
+                partial[b][e][c] = pair if partial[b][e][c] is None else partial[b][e][c] + pair
+    totals = [[functools.reduce(jnp.add, parts) for parts in block] for block in partial]
     for b, (block, start) in enumerate(places):
         labels = block[pl.ds(start + half * count, 2 * count), :].astype(F32)[:count]
         for e in range(2):

time: 39.5 us -> 39.5 us (level)
  no operation moved by 1% of the time
where the time goes in v20:
time: 39.5 us; the launch traced here: 39.3 us
  starting transfers between devices  15.7 us (40%)
  Pallas kernels  15.2 us (38%)
  waiting for transfers between devices  7.55 us (19%)
  between operations  0.78 us (2%)
    ppermute x8, starting transfers between devices, hop(): return lax.ppermute(value, 'dp', pairs)  14.9 us
    ppermute x8, waiting for transfers between devices, hop(): return lax.ppermute(value, 'dp', pairs)  6.75 us
    pallas_call x1, Pallas kernels, shards(): pl.pallas_call(local_kernel, out_shape=[jax.ShapeDtypeStruct(a.shape, a.d...  4.69 us
    pallas_call x6, Pallas kernels, stage(): pl.pallas_call(functools.partial(stage_kernel, away, first), out_shape=[j...  4.53 us
    pallas_call x1, Pallas kernels, shards(): pl.pallas_call(functools.partial(feature_kernel, half), out_shape=jax.Sha...  1.79 us
    pallas_call x1, Pallas kernels, shards(): pl.pallas_call(pack_kernel, out_shape=jax.ShapeDtypeStruct((3 * rows + (L...  1.35 us
    pallas_call x1, Pallas kernels, shards(): pl.pallas_call(functools.partial(stage_and_half_kernel, 1 - half, half),...  1.18 us
    pallas_call x1, Pallas kernels, shards(): pl.pallas_call(functools.partial(score_kernel, len(blocks), count), out_s...  0.86 us
  transfers between devices with their start and end apart: 17, of which 7 were waited for; matrix products, arithmetic and copies ran while one was open for 0% of the time, Pallas kernels for 33%

profile of v20, /device:TPU:0, one launch (start us, length us, event | category | flops | bytes accessed | tf_op | source)
XLA Modules:
  0.0 39.3 jit_solution(8344449359316899692)
XLA Ops:
  0.6 1.3 %pack.1.refs_0_ = bf16[1488,128]{1,0:T(8,128)(2,1)S(1)} custom-call(s32[1]{0:T(128)} %bitcast.me_ref, bf16[160,128]{1,0:T(8,128)(2,1)} %bitcast.14, bf16[8,8192]{1,0:T(8,128)(2,1)} %refs_1_.2, bf16[320,128]{1,0:T(8,128)(2,1)} %refs_2_.2, bf16[320,128]{1,0:T(8,128)(2,1)} %bitcast.13, bf16[320,128]{1,0:T(8,128)(2,1)} %refs_4_.2, f32[40,128]{1,0:T(8,128)} %bitcast.11, ...), custom_call_target="tpu_custom_call" | custom-call | tf_op jit(solution)/shard_map/pack/pallas_call | solution.py:443
  2.0 0.5 %collective-permute-start.2 = (bf16[1488,128]{1,0:T(8,128)(2,1)S(1)}, bf16[1488,128]{1,0:T(8,128)(2,1)S(1)}, u32[]{:S(2)}, u32[]{:S(2)}) collective-permute-start(bf16[1488,128]{1,0:T(8,128)(2,1)S(1)} %pack.1.refs_0_), channel_id=1, source_target_pairs={{0,1},{1,0},{2,3},{3,2},{4,5},{5,4},{6,7},{7,6},{8,9},{9,8},{10,11... | collective-permute-start | bytes 1142792 | tf_op jit(solution)/shard_map/ppermute | solution.py:55
  2.5 2.6 %collective-permute-start = (bf16[1488,128]{1,0:T(8,128)(2,1)S(1)}, bf16[1488,128]{1,0:T(8,128)(2,1)S(1)}, u32[]{:S(2)}, u32[]{:S(2)}) collective-permute-start(bf16[1488,128]{1,0:T(8,128)(2,1)S(1)} %pack.1.refs_0_), channel_id=1, source_target_pairs={{0,2},{1,5},{4,0},{5,9},{8,4},{9,13},{12,8},{13,15},{14,12},{15,11... | collective-permute-start | bytes 1142792 | tf_op jit(solution)/shard_map/ppermute | solution.py:51
  5.1 1.6 %collective-permute-start.3 = (bf16[1488,128]{1,0:T(8,128)(2,1)S(1)}, bf16[1488,128]{1,0:T(8,128)(2,1)S(1)}, u32[]{:S(2)}, u32[]{:S(2)}) collective-permute-start(bf16[1488,128]{1,0:T(8,128)(2,1)S(1)} %collective-permute-done.2.refs_1_), channel_id=1, source_target_pairs={{0,2},{1,5},{4,0},{5,9},{8,4},{9,13},{12,8},{13,15},{14,12},{15,11... | collective-permute-start | bytes 1142792 | tf_op jit(solution)/shard_map/ppermute | solution.py:51
  6.7 4.7 %local_products.1 = (bf16[256,5120]{1,0:T(8,128)(2,1)S(1)}, bf16[256,5120]{1,0:T(8,128)(2,1)S(1)}, bf16[256,5120]{1,0:T(8,128)(2,1)S(1)}, bf16[256,2560]{1,0:T(8...) custom-call(bf16[256,5120]{1,0:T(8,128)(2,1)} %refs_0_.1, ...), custom_call_target="tpu_custom_call" | custom-call | flops 1006632960 | bytes 14680064 | tf_op jit(solution)/shard_map/local_products/pallas_call | solution.py:466
  11.4 1.6 %collective-permute-start.1 = (bf16[1488,128]{1,0:T(8,128)(2,1)S(1)}, bf16[1488,128]{1,0:T(8,128)(2,1)S(1)}, u32[]{:S(2)}, u32[]{:S(2)}) collective-permute-start(bf16[1488,128]{1,0:T(8,128)(2,1)S(1)} %collective-permute-done.refs_0_.refs_2_), channel_id=1, source_target_pairs={{0,2},{1,5},{4,0},{5,9},{8,4},{9,13},{12,8},{13,15},{14,12},{15,11... | collective-permute-start | bytes 1142792 | tf_op jit(solution)/shard_map/ppermute | solution.py:51
  13.1 0.7 %stage.6 = (f32[256,1024]{1,0:T(8,128)S(1)}, f32[128,256]{1,0:T(8,128)S(1)}) custom-call(s32[1]{0:T(128)} %bitcast.me_ref, bf16[1488,128]{1,0:T(8,128)(2,1)S(1)} %pack.1.refs_0_, bf16[1488,128]{1,0:T(8,128)(2,1)S(1)} %collective-permute-done.2.refs_1_, bf16[256,5120]{1,0:T(8,128)(2,1)S(1)} %get-tuple-element.71.refs_2_.refs_3_.refs_1_, ...), custom_call_target="tpu_custom_call" | custom-call | flops 167772160 | bytes 2097152 | tf_op jit(solution)/shard_map/stage/pallas_call | solution.py:492
  13.8 1.1 %collective-permute-done.3.refs_1_.refs_4_ = bf16[1488,128]{1,0:T(8,128)(2,1)S(1)} collective-permute-done((bf16[1488,128]{1,0:T(8,128)(2,1)S(1)}, bf16[1488,128]{1,0:T(8,128)(2,1)S(1)}, u32[]{:S(2)}, u32[]{:S(2)}) %collective-permute-start.3) | collective-permute-done | bytes 380960 | tf_op jit(solution)/shard_map/ppermute | solution.py:51
  14.9 0.0 collective-permute-start.7
  14.9 2.0 %collective-permute-start.5 = (bf16[1488,128]{1,0:T(8,128)(2,1)S(1)}, bf16[1488,128]{1,0:T(8,128)(2,1)S(1)}, u32[]{:S(2)}, u32[]{:S(2)}) collective-permute-start(bf16[1488,128]{1,0:T(8,128)(2,1)S(1)} %collective-permute-done.3.refs_1_.refs_4_), channel_id=1, source_target_pairs={{0,2},{1,5},{4,0},{5,9},{8,4},{9,13},{12,8},{13,15},{14,12},{15,11... | collective-permute-start | bytes 1142792 | tf_op jit(solution)/shard_map/ppermute | solution.py:51
  16.8 0.8 %stage.7 = (f32[256,1024]{1,0:T(8,128)S(1)}, f32[128,256]{1,0:T(8,128)S(1)}) custom-call(s32[1]{0:T(128)} %bitcast.me_ref, bf16[1488,128]{1,0:T(8,128)(2,1)S(1)} %collective-permute-done.refs_0_.refs_2_, bf16[1488,128]{1,0:T(8,128)(2,1)S(1)} %collective-permute-done.3.refs_1_.refs_4_, ...), custom_call_target="tpu_custom_call", output_to_operand_aliasing={{0}: (10, {}), {1}: (11, {})} | custom-call | flops 167772160 | bytes 2097152 | tf_op jit(solution)/shard_map/stage/pallas_call | solution.py:492
  17.6 1.5 %collective-permute-done.1.refs_0_.refs_6_ = bf16[1488,128]{1,0:T(8,128)(2,1)S(1)} collective-permute-done((bf16[1488,128]{1,0:T(8,128)(2,1)S(1)}, bf16[1488,128]{1,0:T(8,128)(2,1)S(1)}, u32[]{:S(2)}, u32[]{:S(2)}) %collective-permute-start.1) | collective-permute-done | bytes 380960 | tf_op jit(solution)/shard_map/ppermute | solution.py:51
  19.1 1.8 %collective-permute-start.4 = (bf16[1488,128]{1,0:T(8,128)(2,1)S(1)}, bf16[1488,128]{1,0:T(8,128)(2,1)S(1)}, u32[]{:S(2)}, u32[]{:S(2)}) collective-permute-start(bf16[1488,128]{1,0:T(8,128)(2,1)S(1)} %collective-permute-done.1.refs_0_.refs_6_), channel_id=1, source_target_pairs={{0,2},{1,5},{4,0},{5,9},{8,4},{9,13},{12,8},{13,15},{14,12},{15,11... | collective-permute-start | bytes 1142792 | tf_op jit(solution)/shard_map/ppermute | solution.py:51
  20.9 0.8 %stage.8 = (f32[256,1024]{1,0:T(8,128)S(1)}, f32[128,256]{1,0:T(8,128)S(1)}) custom-call(s32[1]{0:T(128)} %bitcast.me_ref, bf16[1488,128]{1,0:T(8,128)(2,1)S(1)} %collective-permute-done.6.refs_0_.refs_3_, bf16[1488,128]{1,0:T(8,128)(2,1)S(1)} %collective-permute-done.7.refs_1_.refs_5_, ...), custom_call_target="tpu_custom_call", output_to_operand_aliasing={{0}: (10, {}), {1}: (11, {})} | custom-call | flops 167772160 | bytes 2097152 | tf_op jit(solution)/shard_map/stage/pallas_call | solution.py:492
  21.7 1.5 %collective-permute-done.5.refs_1_.block_ref.refs_8_ = bf16[1488,128]{1,0:T(8,128)(2,1)S(1)} collective-permute-done((bf16[1488,128]{1,0:T(8,128)(2,1)S(1)}, bf16[1488,128]{1,0:T(8,128)(2,1)S(1)}, u32[]{:S(2)}, u32[]{:S(2)}) %collective-permute-start.5) | collective-permute-done | bytes 380960 | tf_op jit(solution)/shard_map/ppermute | solution.py:51
  23.3 1.8 %collective-permute-start.8 = (bf16[960,128]{1,0:T(8,128)(2,1)S(1)}, bf16[960,128]{1,0:T(8,128)(2,1)S(1)}, u32[]{:S(2)}, u32[]{:S(2)}) collective-permute-start(bf16[960,128]{1,0:T(8,128)(2,1)S(1)} %get-tuple-element.98), channel_id=1, source_target_pairs={{0,2},{1,5},{4,0},{5,9},{8,4},{9,13},{12,8},{13,15},{14,12},{15,11... | collective-permute-start | bytes 737288 | tf_op jit(solution)/shard_map/ppermute | solution.py:51
  25.1 0.8 %stage.9 = (f32[256,1024]{1,0:T(8,128)S(1)}, f32[128,256]{1,0:T(8,128)S(1)}) custom-call(s32[1]{0:T(128)} %bitcast.me_ref, bf16[1488,128]{1,0:T(8,128)(2,1)S(1)} %collective-permute-done.1.refs_0_.refs_6_, bf16[1488,128]{1,0:T(8,128)(2,1)S(1)} %collective-permute-done.5.refs_1_.block_ref.refs_8_, ...), custom_call_target="tpu_custom_call", output_to_operand_aliasing={{0}: (10, {}), {1}: (11, {})} | custom-call | flops 167772160 | bytes 2097152 | tf_op jit(solution)/shard_map/stage/pallas_call | solution.py:492
  25.8 1.5 %collective-permute-done.4.block_ref.refs_0_.refs_10_ = bf16[1488,128]{1,0:T(8,128)(2,1)S(1)} collective-permute-done((bf16[1488,128]{1,0:T(8,128)(2,1)S(1)}, bf16[1488,128]{1,0:T(8,128)(2,1)S(1)}, u32[]{:S(2)}, u32[]{:S(2)}) %collective-permute-start.4) | collective-permute-done | bytes 380960 | tf_op jit(solution)/shard_map/ppermute | solution.py:51
  27.3 1.8 %collective-permute-start.12 = (bf16[960,128]{1,0:T(8,128)(2,1)S(1)}, bf16[960,128]{1,0:T(8,128)(2,1)S(1)}, u32[]{:S(2)}, u32[]{:S(2)}) collective-permute-start(bf16[960,128]{1,0:T(8,128)(2,1)S(1)} %get-tuple-element.106), channel_id=1, source_target_pairs={{0,2},{1,5},{4,0},{5,9},{8,4},{9,13},{12,8},{13,15},{14,12},{15,11... | collective-permute-start | bytes 737288 | tf_op jit(solution)/shard_map/ppermute | solution.py:51
  29.2 0.8 %stage.10 = (f32[256,1024]{1,0:T(8,128)S(1)}, f32[128,256]{1,0:T(8,128)S(1)}) custom-call(s32[1]{0:T(128)} %bitcast.me_ref, bf16[1488,128]{1,0:T(8,128)(2,1)S(1)} %collective-permute-done.9.refs_0_.refs_7_, bf16[1488,128]{1,0:T(8,128)(2,1)S(1)} %collective-permute-done.10.refs_1_.refs_9_, ...), custom_call_target="tpu_custom_call", output_to_operand_aliasing={{0}: (10, {}), {1}: (11, {})} | custom-call | flops 167772160 | bytes 2097152 | tf_op jit(solution)/shard_map/stage/pallas_call | solution.py:492
  30.0 1.7 %collective-permute-start.11 = (bf16[1056,128]{1,0:T(8,128)(2,1)S(1)}, bf16[1056,128]{1,0:T(8,128)(2,1)S(1)}, u32[]{:S(2)}, u32[]{:S(2)}) collective-permute-start(bf16[1056,128]{1,0:T(8,128)(2,1)S(1)} %get-tuple-element.105), channel_id=1, source_target_pairs={{0,2},{1,5},{4,0},{5,9},{8,4},{9,13},{12,8},{13,15},{14,12},{15,11... | collective-permute-start | bytes 811016 | tf_op jit(solution)/shard_map/ppermute | solution.py:51
  31.7 0.8 %stage.11 = (f32[256,1024]{1,0:T(8,128)S(1)}, f32[128,256]{1,0:T(8,128)S(1)}) custom-call(s32[1]{0:T(128)} %bitcast.me_ref, bf16[1488,128]{1,0:T(8,128)(2,1)S(1)} %collective-permute-done.4.block_ref.refs_0_.refs_10_, bf16[960,128]{1,0:T(8,128)(2,1)S(1)} %collective-permute-done.8.refs_1_, ...), custom_call_target="tpu_custom_call", output_to_operand_aliasing={{0}: (10, {}), {1}: (11, {})} | custom-call | flops 167772160 | bytes 2097152 | tf_op jit(solution)/shard_map/stage/pallas_call | solution.py:492
  32.5 1.1 %collective-permute-done.12.refs_2_ = bf16[960,128]{1,0:T(8,128)(2,1)S(1)} collective-permute-done((bf16[960,128]{1,0:T(8,128)(2,1)S(1)}, bf16[960,128]{1,0:T(8,128)(2,1)S(1)}, u32[]{:S(2)}, u32[]{:S(2)}) %collective-permute-start.12) | collective-permute-done | bytes 245792 | tf_op jit(solution)/shard_map/ppermute | solution.py:51
  33.6 0.0 collective-permute-start.13
  33.6 0.0 collective-permute-done.14.refs_0_.refs_11_
  33.6 1.2 %stage_and_half.1 = (f32[256,1024]{1,0:T(8,128)S(1)}, f32[128,256]{1,0:T(8,128)S(1)}) custom-call(s32[1]{0:T(128)} %bitcast.me_ref, bf16[1488,128]{1,0:T(8,128)(2,1)S(1)} %collective-permute-done.14.refs_0_.refs_11_, bf16[960,128]{1,0:T(8,128)(2,1)S(1)} %collective-permute-done.15.refs_1_, ...), custom_call_target="tpu_custom_call", output_to_operand_aliasing={{0}: (11, {}), {1}: (12, {})} | custom-call | flops 251658240 | bytes 3145728 | tf_op jit(solution)/shard_map/stage_and_half/pallas_call | solution.py:553
  34.8 0.3 collective-permute-done.13.refs_0_
  35.1 1.8 %features.1.unit_ref = f32[128,128]{1,0:T(8,128)S(1)} custom-call(s32[1]{0:T(128)} %bitcast.me_ref, s32[1,2]{1,0:T(1,128)S(1)} %copy-done, bf16[960,128]{1,0:T(8,128)(2,1)S(1)} %collective-permute-done.13.refs_0_, bf16[256,5120]{1,0:T(8,128)(2,1)S(1)} %get-tuple-element.71.refs_2_.refs_3_.refs_1_, ...), custom_call_target="tpu_custom_call" | custom-call | flops 1 | bytes 1 | tf_op jit(solution)/shard_map/features/pallas_call | solution.py:565
  36.9 0.3 collective-permute-start.16
  37.2 0.9 %scores.1.best_ref = f32[2,3,8,128]{3,2,1,0:T(8,128)S(1)} custom-call(f32[128,128]{1,0:T(8,128)S(1)} %features.1.unit_ref, bf16[1488,128]{1,0:T(8,128)(2,1)S(1)} %pack.1.refs_0_, bf16[1488,128]{1,0:T(8,128)(2,1)S(1)} %collective-permute-done.2.refs_1_, bf16[1488,128]{1,0:T(8,128)(2,1)S(1)} %collective-permute-done.refs_0_.refs_2_, ...), custom_call_target="tpu_custom_call" | custom-call | flops 4194304 | bytes 2097152 | tf_op jit(solution)/shard_map/scores/pallas_call | solution.py:577
  38.0 0.5 %collective-permute-done.16.block_ref = bf16[1056,128]{1,0:T(8,128)(2,1)S(1)} collective-permute-done((bf16[1056,128]{1,0:T(8,128)(2,1)S(1)}, bf16[1056,128]{1,0:T(8,128)(2,1)S(1)}, u32[]{:S(2)}, u32[]{:S(2)}) %collective-permute-start.16) | collective-permute-done | bytes 270368 | tf_op jit(solution)/shard_map/ppermute | solution.py:55
  38.5 0.8 %last_scores.1 = (f32[2,3]{1,0:T(2,128)}, f32[1,2]{1,0:T(1,128)}) custom-call(f32[128,128]{1,0:T(8,128)S(1)} %features.1.unit_ref, bf16[1056,128]{1,0:T(8,128)(2,1)S(1)} %collective-permute-done.16.block_ref, f32[2,3,8,128]{3,2,1,0:T(8,128)S(1)} %scores.1.best_ref), custom_call_target="tpu_custom_call" | custom-call | tf_op jit(solution)/shard_map/last_scores/pallas_call | solution.py:586
  (18 shorter events, 0.1 us)
Async XLA Ops:
  2.0 3.1 %collective-permute-start.2 = (bf16[1488,128]{1,0:T(8,128)(2,1)S(1)}, bf16[1488,128]{1,0:T(8,128)(2,1)S(1)}, u32[]{:S(2)}, u32[]{:S(2)}) collective-permute-start(bf16[1488,128]{1,0:T(8,128)(2,1)S(1)} %pack.1.refs_0_), channel_id=1, source_target_pairs={{0,1},{1,0},{2,3},{3,2},{4,5},{5,4},{6,7},{7,6},{8,9},{9,8},{10,11... | collective-permute-start | bytes 1142792 | tf_op jit(solution)/shard_map/ppermute | solution.py:55
  2.5 8.9 %collective-permute-start = (bf16[1488,128]{1,0:T(8,128)(2,1)S(1)}, bf16[1488,128]{1,0:T(8,128)(2,1)S(1)}, u32[]{:S(2)}, u32[]{:S(2)}) collective-permute-start(bf16[1488,128]{1,0:T(8,128)(2,1)S(1)} %pack.1.refs_0_), channel_id=1, source_target_pairs={{0,2},{1,5},{4,0},{5,9},{8,4},{9,13},{12,8},{13,15},{14,12},{15,11... | collective-permute-start | bytes 1142792 | tf_op jit(solution)/shard_map/ppermute | solution.py:51
  5.1 9.8 %collective-permute-start.3 = (bf16[1488,128]{1,0:T(8,128)(2,1)S(1)}, bf16[1488,128]{1,0:T(8,128)(2,1)S(1)}, u32[]{:S(2)}, u32[]{:S(2)}) collective-permute-start(bf16[1488,128]{1,0:T(8,128)(2,1)S(1)} %collective-permute-done.2.refs_1_), channel_id=1, source_target_pairs={{0,2},{1,5},{4,0},{5,9},{8,4},{9,13},{12,8},{13,15},{14,12},{15,11... | collective-permute-start | bytes 1142792 | tf_op jit(solution)/shard_map/ppermute | solution.py:51
  11.4 7.7 %collective-permute-start.1 = (bf16[1488,128]{1,0:T(8,128)(2,1)S(1)}, bf16[1488,128]{1,0:T(8,128)(2,1)S(1)}, u32[]{:S(2)}, u32[]{:S(2)}) collective-permute-start(bf16[1488,128]{1,0:T(8,128)(2,1)S(1)} %collective-permute-done.refs_0_.refs_2_), channel_id=1, source_target_pairs={{0,2},{1,5},{4,0},{5,9},{8,4},{9,13},{12,8},{13,15},{14,12},{15,11... | collective-permute-start | bytes 1142792 | tf_op jit(solution)/shard_map/ppermute | solution.py:51
  13.1 7.8 %collective-permute-start.6 = (bf16[1488,128]{1,0:T(8,128)(2,1)S(1)}, bf16[1488,128]{1,0:T(8,128)(2,1)S(1)}, u32[]{:S(2)}, u32[]{:S(2)}) collective-permute-start(bf16[1488,128]{1,0:T(8,128)(2,1)S(1)} %collective-permute-done.refs_0_.refs_2_), channel_id=1, source_target_pairs={{0,1},{1,0},{2,3},{3,2},{4,5},{5,4},{6,7},{7,6},{8,9},{9,8},{10,11... | collective-permute-start | bytes 1142792 | tf_op jit(solution)/shard_map/ppermute | solution.py:55
  14.9 6.1 %collective-permute-start.7 = (bf16[1488,128]{1,0:T(8,128)(2,1)S(1)}, bf16[1488,128]{1,0:T(8,128)(2,1)S(1)}, u32[]{:S(2)}, u32[]{:S(2)}) collective-permute-start(bf16[1488,128]{1,0:T(8,128)(2,1)S(1)} %collective-permute-done.3.refs_1_.refs_4_), channel_id=1, source_target_pairs={{0,1},{1,0},{2,3},{3,2},{4,5},{5,4},{6,7},{7,6},{8,9},{9,8},{10,11... | collective-permute-start | bytes 1142792 | tf_op jit(solution)/shard_map/ppermute | solution.py:55
  14.9 8.4 %collective-permute-start.5 = (bf16[1488,128]{1,0:T(8,128)(2,1)S(1)}, bf16[1488,128]{1,0:T(8,128)(2,1)S(1)}, u32[]{:S(2)}, u32[]{:S(2)}) collective-permute-start(bf16[1488,128]{1,0:T(8,128)(2,1)S(1)} %collective-permute-done.3.refs_1_.refs_4_), channel_id=1, source_target_pairs={{0,2},{1,5},{4,0},{5,9},{8,4},{9,13},{12,8},{13,15},{14,12},{15,11... | collective-permute-start | bytes 1142792 | tf_op jit(solution)/shard_map/ppermute | solution.py:51
  19.1 8.2 %collective-permute-start.4 = (bf16[1488,128]{1,0:T(8,128)(2,1)S(1)}, bf16[1488,128]{1,0:T(8,128)(2,1)S(1)}, u32[]{:S(2)}, u32[]{:S(2)}) collective-permute-start(bf16[1488,128]{1,0:T(8,128)(2,1)S(1)} %collective-permute-done.1.refs_0_.refs_6_), channel_id=1, source_target_pairs={{0,2},{1,5},{4,0},{5,9},{8,4},{9,13},{12,8},{13,15},{14,12},{15,11... | collective-permute-start | bytes 1142792 | tf_op jit(solution)/shard_map/ppermute | solution.py:51
  20.9 8.3 %collective-permute-start.9 = (bf16[1488,128]{1,0:T(8,128)(2,1)S(1)}, bf16[1488,128]{1,0:T(8,128)(2,1)S(1)}, u32[]{:S(2)}, u32[]{:S(2)}) collective-permute-start(bf16[1488,128]{1,0:T(8,128)(2,1)S(1)} %collective-permute-done.1.refs_0_.refs_6_), channel_id=1, source_target_pairs={{0,1},{1,0},{2,3},{3,2},{4,5},{5,4},{6,7},{7,6},{8,9},{9,8},{10,11... | collective-permute-start | bytes 1142792 | tf_op jit(solution)/shard_map/ppermute | solution.py:55
  23.2 5.9 %collective-permute-start.10 = (bf16[1488,128]{1,0:T(8,128)(2,1)S(1)}, bf16[1488,128]{1,0:T(8,128)(2,1)S(1)}, u32[]{:S(2)}, u32[]{:S(2)}) collective-permute-start(bf16[1488,128]{1,0:T(8,128)(2,1)S(1)} %collective-permute-done.5.refs_1_.block_ref.refs_8_), channel_id=1, source_target_pairs={{0,1},{1,0},{2,3},{3,2},{4,5},{5,4},{6,7},{7,6},{8,9},{9,8},{10,11... | collective-permute-start | bytes 1142792 | tf_op jit(solution)/shard_map/ppermute | solution.py:55
  23.3 6.7 %collective-permute-start.8 = (bf16[960,128]{1,0:T(8,128)(2,1)S(1)}, bf16[960,128]{1,0:T(8,128)(2,1)S(1)}, u32[]{:S(2)}, u32[]{:S(2)}) collective-permute-start(bf16[960,128]{1,0:T(8,128)(2,1)S(1)} %get-tuple-element.98), channel_id=1, source_target_pairs={{0,2},{1,5},{4,0},{5,9},{8,4},{9,13},{12,8},{13,15},{14,12},{15,11... | collective-permute-start | bytes 737288 | tf_op jit(solution)/shard_map/ppermute | solution.py:51
  27.3 6.2 %collective-permute-start.12 = (bf16[960,128]{1,0:T(8,128)(2,1)S(1)}, bf16[960,128]{1,0:T(8,128)(2,1)S(1)}, u32[]{:S(2)}, u32[]{:S(2)}) collective-permute-start(bf16[960,128]{1,0:T(8,128)(2,1)S(1)} %get-tuple-element.106), channel_id=1, source_target_pairs={{0,2},{1,5},{4,0},{5,9},{8,4},{9,13},{12,8},{13,15},{14,12},{15,11... | collective-permute-start | bytes 737288 | tf_op jit(solution)/shard_map/ppermute | solution.py:51
  29.2 4.4 %collective-permute-start.14 = (bf16[1488,128]{1,0:T(8,128)(2,1)S(1)}, bf16[1488,128]{1,0:T(8,128)(2,1)S(1)}, u32[]{:S(2)}, u32[]{:S(2)}) collective-permute-start(bf16[1488,128]{1,0:T(8,128)(2,1)S(1)} %collective-permute-done.4.block_ref.refs_0_.refs_10_), channel_id=1, source_target_pairs={{0,1},{1,0},{2,3},{3,2},{4,5},{5,4},{6,7},{7,6},{8,9},{9,8},{10,11... | collective-permute-start | bytes 1142792 | tf_op jit(solution)/shard_map/ppermute | solution.py:55
  30.0 6.9 %collective-permute-start.11 = (bf16[1056,128]{1,0:T(8,128)(2,1)S(1)}, bf16[1056,128]{1,0:T(8,128)(2,1)S(1)}, u32[]{:S(2)}, u32[]{:S(2)}) collective-permute-start(bf16[1056,128]{1,0:T(8,128)(2,1)S(1)} %get-tuple-element.105), channel_id=1, source_target_pairs={{0,2},{1,5},{4,0},{5,9},{8,4},{9,13},{12,8},{13,15},{14,12},{15,11... | collective-permute-start | bytes 811016 | tf_op jit(solution)/shard_map/ppermute | solution.py:51
  31.7 1.9 %collective-permute-start.15 = (bf16[960,128]{1,0:T(8,128)(2,1)S(1)}, bf16[960,128]{1,0:T(8,128)(2,1)S(1)}, u32[]{:S(2)}, u32[]{:S(2)}) collective-permute-start(bf16[960,128]{1,0:T(8,128)(2,1)S(1)} %collective-permute-done.8.refs_1_), channel_id=1, source_target_pairs={{0,1},{1,0},{2,3},{3,2},{4,5},{5,4},{6,7},{7,6},{8,9},{9,8},{10,11... | collective-permute-start | bytes 737288 | tf_op jit(solution)/shard_map/ppermute | solution.py:55
  33.6 1.5 %copy-start = (s32[1,2]{1,0:T(1,128)S(1)}, s32[1,2]{1,0:T(1,128)}, u32[]{:S(2)}) copy-start(s32[1,2]{1,0:T(1,128)} %counts_ref.1) | copy-start | bytes 28
  33.6 1.5 %collective-permute-start.13 = (bf16[960,128]{1,0:T(8,128)(2,1)S(1)}, bf16[960,128]{1,0:T(8,128)(2,1)S(1)}, u32[]{:S(2)}, u32[]{:S(2)}) collective-permute-start(bf16[960,128]{1,0:T(8,128)(2,1)S(1)} %collective-permute-done.12.refs_2_), channel_id=1, source_target_pairs={{0,1},{1,0},{2,3},{3,2},{4,5},{5,4},{6,7},{7,6},{8,9},{9,8},{10,11... | collective-permute-start | bytes 737288 | tf_op jit(solution)/shard_map/ppermute | solution.py:55
  36.9 1.6 %collective-permute-start.16 = (bf16[1056,128]{1,0:T(8,128)(2,1)S(1)}, bf16[1056,128]{1,0:T(8,128)(2,1)S(1)}, u32[]{:S(2)}, u32[]{:S(2)}) collective-permute-start(bf16[1056,128]{1,0:T(8,128)(2,1)S(1)} %collective-permute-done.11.refs_12_), channel_id=1, source_target_pairs={{0,1},{1,0},{2,3},{3,2},{4,5},{5,4},{6,7},{7,6},{8,9},{9,8},{10,11... | collective-permute-start | bytes 811016 | tf_op jit(solution)/shard_map/ppermute | solution.py:55

commit v21 on v20

--- a/solution.py
+++ b/solution.py
@@ -308,7 +308,7 @@
     for e in range(2):
         own = feats[e * half : (e + 1) * half]
         squares = jnp.sum(own * own, keepdims=True)
-        out_ref[pl.ds(e * half, half), :] = (own * lax.rsqrt(squares + 1e-06)).astype(BF16).astype(F32)
+        out_ref[pl.ds(e * half, half), :] = own * lax.rsqrt(squares + 1e-06)
 
 
 def split_kernel(block_ref, *refs):

time: 39.5 us -> 39.5 us (level)
  no operation moved by 1% of the time
where the time goes in v21:
time: 39.5 us; the launch traced here: 39.3 us
  starting transfers between devices  15.7 us (40%)
  Pallas kernels  15.2 us (38%)
  waiting for transfers between devices  7.55 us (19%)
  between operations  0.78 us (2%)
    ppermute x8, starting transfers between devices, hop(): return lax.ppermute(value, 'dp', pairs)  14.9 us
    ppermute x8, waiting for transfers between devices, hop(): return lax.ppermute(value, 'dp', pairs)  6.75 us
    pallas_call x1, Pallas kernels, shards(): pl.pallas_call(local_kernel, out_shape=[jax.ShapeDtypeStruct(a.shape, a.d...  4.69 us
    pallas_call x6, Pallas kernels, stage(): pl.pallas_call(functools.partial(stage_kernel, away, first), out_shape=[j...  4.53 us
    pallas_call x1, Pallas kernels, shards(): pl.pallas_call(functools.partial(feature_kernel, half), out_shape=jax.Sha...  1.79 us
    pallas_call x1, Pallas kernels, shards(): pl.pallas_call(pack_kernel, out_shape=jax.ShapeDtypeStruct((3 * rows + (L...  1.35 us
    pallas_call x1, Pallas kernels, shards(): pl.pallas_call(functools.partial(stage_and_half_kernel, 1 - half, half),...  1.18 us
    pallas_call x1, Pallas kernels, shards(): pl.pallas_call(functools.partial(score_kernel, len(blocks), count), out_s...  0.86 us
  transfers between devices with their start and end apart: 17, of which 7 were waited for; matrix products, arithmetic and copies ran while one was open for 0% of the time, Pallas kernels for 33%

profile of v21, /device:TPU:0, one launch (start us, length us, event | category | flops | bytes accessed | tf_op | source)
XLA Modules:
  0.0 39.3 jit_solution(4851921975895607167)
XLA Ops:
  0.6 1.3 %pack.1.refs_0_ = bf16[1488,128]{1,0:T(8,128)(2,1)S(1)} custom-call(s32[1]{0:T(128)} %bitcast.me_ref, bf16[160,128]{1,0:T(8,128)(2,1)} %bitcast.14, bf16[8,8192]{1,0:T(8,128)(2,1)} %refs_1_.2, bf16[320,128]{1,0:T(8,128)(2,1)} %refs_2_.2, bf16[320,128]{1,0:T(8,128)(2,1)} %bitcast.13, bf16[320,128]{1,0:T(8,128)(2,1)} %refs_4_.2, f32[40,128]{1,0:T(8,128)} %bitcast.11, ...), custom_call_target="tpu_custom_call" | custom-call | tf_op jit(solution)/shard_map/pack/pallas_call | solution.py:443
  2.0 0.5 %collective-permute-start.2 = (bf16[1488,128]{1,0:T(8,128)(2,1)S(1)}, bf16[1488,128]{1,0:T(8,128)(2,1)S(1)}, u32[]{:S(2)}, u32[]{:S(2)}) collective-permute-start(bf16[1488,128]{1,0:T(8,128)(2,1)S(1)} %pack.1.refs_0_), channel_id=1, source_target_pairs={{0,1},{1,0},{2,3},{3,2},{4,5},{5,4},{6,7},{7,6},{8,9},{9,8},{10,11... | collective-permute-start | bytes 1142792 | tf_op jit(solution)/shard_map/ppermute | solution.py:55
  2.5 2.6 %collective-permute-start = (bf16[1488,128]{1,0:T(8,128)(2,1)S(1)}, bf16[1488,128]{1,0:T(8,128)(2,1)S(1)}, u32[]{:S(2)}, u32[]{:S(2)}) collective-permute-start(bf16[1488,128]{1,0:T(8,128)(2,1)S(1)} %pack.1.refs_0_), channel_id=1, source_target_pairs={{0,2},{1,5},{4,0},{5,9},{8,4},{9,13},{12,8},{13,15},{14,12},{15,11... | collective-permute-start | bytes 1142792 | tf_op jit(solution)/shard_map/ppermute | solution.py:51
  5.1 1.6 %collective-permute-start.3 = (bf16[1488,128]{1,0:T(8,128)(2,1)S(1)}, bf16[1488,128]{1,0:T(8,128)(2,1)S(1)}, u32[]{:S(2)}, u32[]{:S(2)}) collective-permute-start(bf16[1488,128]{1,0:T(8,128)(2,1)S(1)} %collective-permute-done.2.refs_1_), channel_id=1, source_target_pairs={{0,2},{1,5},{4,0},{5,9},{8,4},{9,13},{12,8},{13,15},{14,12},{15,11... | collective-permute-start | bytes 1142792 | tf_op jit(solution)/shard_map/ppermute | solution.py:51
  6.7 4.7 %local_products.1 = (bf16[256,5120]{1,0:T(8,128)(2,1)S(1)}, bf16[256,5120]{1,0:T(8,128)(2,1)S(1)}, bf16[256,5120]{1,0:T(8,128)(2,1)S(1)}, bf16[256,2560]{1,0:T(8...) custom-call(bf16[256,5120]{1,0:T(8,128)(2,1)} %refs_0_.1, ...), custom_call_target="tpu_custom_call" | custom-call | flops 1006632960 | bytes 14680064 | tf_op jit(solution)/shard_map/local_products/pallas_call | solution.py:466
  11.4 1.6 %collective-permute-start.1 = (bf16[1488,128]{1,0:T(8,128)(2,1)S(1)}, bf16[1488,128]{1,0:T(8,128)(2,1)S(1)}, u32[]{:S(2)}, u32[]{:S(2)}) collective-permute-start(bf16[1488,128]{1,0:T(8,128)(2,1)S(1)} %collective-permute-done.refs_0_.refs_2_), channel_id=1, source_target_pairs={{0,2},{1,5},{4,0},{5,9},{8,4},{9,13},{12,8},{13,15},{14,12},{15,11... | collective-permute-start | bytes 1142792 | tf_op jit(solution)/shard_map/ppermute | solution.py:51
  13.1 0.7 %stage.6 = (f32[256,1024]{1,0:T(8,128)S(1)}, f32[128,256]{1,0:T(8,128)S(1)}) custom-call(s32[1]{0:T(128)} %bitcast.me_ref, bf16[1488,128]{1,0:T(8,128)(2,1)S(1)} %pack.1.refs_0_, bf16[1488,128]{1,0:T(8,128)(2,1)S(1)} %collective-permute-done.2.refs_1_, bf16[256,5120]{1,0:T(8,128)(2,1)S(1)} %get-tuple-element.71.refs_2_.refs_3_.refs_1_, ...), custom_call_target="tpu_custom_call" | custom-call | flops 167772160 | bytes 2097152 | tf_op jit(solution)/shard_map/stage/pallas_call | solution.py:492
  13.8 1.1 %collective-permute-done.3.refs_1_.refs_4_ = bf16[1488,128]{1,0:T(8,128)(2,1)S(1)} collective-permute-done((bf16[1488,128]{1,0:T(8,128)(2,1)S(1)}, bf16[1488,128]{1,0:T(8,128)(2,1)S(1)}, u32[]{:S(2)}, u32[]{:S(2)}) %collective-permute-start.3) | collective-permute-done | bytes 380960 | tf_op jit(solution)/shard_map/ppermute | solution.py:51
  14.9 0.0 collective-permute-start.7
  14.9 2.0 %collective-permute-start.5 = (bf16[1488,128]{1,0:T(8,128)(2,1)S(1)}, bf16[1488,128]{1,0:T(8,128)(2,1)S(1)}, u32[]{:S(2)}, u32[]{:S(2)}) collective-permute-start(bf16[1488,128]{1,0:T(8,128)(2,1)S(1)} %collective-permute-done.3.refs_1_.refs_4_), channel_id=1, source_target_pairs={{0,2},{1,5},{4,0},{5,9},{8,4},{9,13},{12,8},{13,15},{14,12},{15,11... | collective-permute-start | bytes 1142792 | tf_op jit(solution)/shard_map/ppermute | solution.py:51
  16.8 0.8 %stage.7 = (f32[256,1024]{1,0:T(8,128)S(1)}, f32[128,256]{1,0:T(8,128)S(1)}) custom-call(s32[1]{0:T(128)} %bitcast.me_ref, bf16[1488,128]{1,0:T(8,128)(2,1)S(1)} %collective-permute-done.refs_0_.refs_2_, bf16[1488,128]{1,0:T(8,128)(2,1)S(1)} %collective-permute-done.3.refs_1_.refs_4_, ...), custom_call_target="tpu_custom_call", output_to_operand_aliasing={{0}: (10, {}), {1}: (11, {})} | custom-call | flops 167772160 | bytes 2097152 | tf_op jit(solution)/shard_map/stage/pallas_call | solution.py:492
  17.6 1.5 %collective-permute-done.1.refs_0_.refs_6_ = bf16[1488,128]{1,0:T(8,128)(2,1)S(1)} collective-permute-done((bf16[1488,128]{1,0:T(8,128)(2,1)S(1)}, bf16[1488,128]{1,0:T(8,128)(2,1)S(1)}, u32[]{:S(2)}, u32[]{:S(2)}) %collective-permute-start.1) | collective-permute-done | bytes 380960 | tf_op jit(solution)/shard_map/ppermute | solution.py:51
  19.1 1.8 %collective-permute-start.4 = (bf16[1488,128]{1,0:T(8,128)(2,1)S(1)}, bf16[1488,128]{1,0:T(8,128)(2,1)S(1)}, u32[]{:S(2)}, u32[]{:S(2)}) collective-permute-start(bf16[1488,128]{1,0:T(8,128)(2,1)S(1)} %collective-permute-done.1.refs_0_.refs_6_), channel_id=1, source_target_pairs={{0,2},{1,5},{4,0},{5,9},{8,4},{9,13},{12,8},{13,15},{14,12},{15,11... | collective-permute-start | bytes 1142792 | tf_op jit(solution)/shard_map/ppermute | solution.py:51
  20.9 0.8 %stage.8 = (f32[256,1024]{1,0:T(8,128)S(1)}, f32[128,256]{1,0:T(8,128)S(1)}) custom-call(s32[1]{0:T(128)} %bitcast.me_ref, bf16[1488,128]{1,0:T(8,128)(2,1)S(1)} %collective-permute-done.6.refs_0_.refs_3_, bf16[1488,128]{1,0:T(8,128)(2,1)S(1)} %collective-permute-done.7.refs_1_.refs_5_, ...), custom_call_target="tpu_custom_call", output_to_operand_aliasing={{0}: (10, {}), {1}: (11, {})} | custom-call | flops 167772160 | bytes 2097152 | tf_op jit(solution)/shard_map/stage/pallas_call | solution.py:492
  21.7 1.5 %collective-permute-done.5.refs_1_.block_ref.refs_8_ = bf16[1488,128]{1,0:T(8,128)(2,1)S(1)} collective-permute-done((bf16[1488,128]{1,0:T(8,128)(2,1)S(1)}, bf16[1488,128]{1,0:T(8,128)(2,1)S(1)}, u32[]{:S(2)}, u32[]{:S(2)}) %collective-permute-start.5) | collective-permute-done | bytes 380960 | tf_op jit(solution)/shard_map/ppermute | solution.py:51
  23.3 1.8 %collective-permute-start.8 = (bf16[960,128]{1,0:T(8,128)(2,1)S(1)}, bf16[960,128]{1,0:T(8,128)(2,1)S(1)}, u32[]{:S(2)}, u32[]{:S(2)}) collective-permute-start(bf16[960,128]{1,0:T(8,128)(2,1)S(1)} %get-tuple-element.98), channel_id=1, source_target_pairs={{0,2},{1,5},{4,0},{5,9},{8,4},{9,13},{12,8},{13,15},{14,12},{15,11... | collective-permute-start | bytes 737288 | tf_op jit(solution)/shard_map/ppermute | solution.py:51
  25.1 0.8 %stage.9 = (f32[256,1024]{1,0:T(8,128)S(1)}, f32[128,256]{1,0:T(8,128)S(1)}) custom-call(s32[1]{0:T(128)} %bitcast.me_ref, bf16[1488,128]{1,0:T(8,128)(2,1)S(1)} %collective-permute-done.1.refs_0_.refs_6_, bf16[1488,128]{1,0:T(8,128)(2,1)S(1)} %collective-permute-done.5.refs_1_.block_ref.refs_8_, ...), custom_call_target="tpu_custom_call", output_to_operand_aliasing={{0}: (10, {}), {1}: (11, {})} | custom-call | flops 167772160 | bytes 2097152 | tf_op jit(solution)/shard_map/stage/pallas_call | solution.py:492
  25.8 1.5 %collective-permute-done.4.block_ref.refs_0_.refs_10_ = bf16[1488,128]{1,0:T(8,128)(2,1)S(1)} collective-permute-done((bf16[1488,128]{1,0:T(8,128)(2,1)S(1)}, bf16[1488,128]{1,0:T(8,128)(2,1)S(1)}, u32[]{:S(2)}, u32[]{:S(2)}) %collective-permute-start.4) | collective-permute-done | bytes 380960 | tf_op jit(solution)/shard_map/ppermute | solution.py:51
  27.3 1.8 %collective-permute-start.12 = (bf16[960,128]{1,0:T(8,128)(2,1)S(1)}, bf16[960,128]{1,0:T(8,128)(2,1)S(1)}, u32[]{:S(2)}, u32[]{:S(2)}) collective-permute-start(bf16[960,128]{1,0:T(8,128)(2,1)S(1)} %get-tuple-element.106), channel_id=1, source_target_pairs={{0,2},{1,5},{4,0},{5,9},{8,4},{9,13},{12,8},{13,15},{14,12},{15,11... | collective-permute-start | bytes 737288 | tf_op jit(solution)/shard_map/ppermute | solution.py:51
  29.2 0.8 %stage.10 = (f32[256,1024]{1,0:T(8,128)S(1)}, f32[128,256]{1,0:T(8,128)S(1)}) custom-call(s32[1]{0:T(128)} %bitcast.me_ref, bf16[1488,128]{1,0:T(8,128)(2,1)S(1)} %collective-permute-done.9.refs_0_.refs_7_, bf16[1488,128]{1,0:T(8,128)(2,1)S(1)} %collective-permute-done.10.refs_1_.refs_9_, ...), custom_call_target="tpu_custom_call", output_to_operand_aliasing={{0}: (10, {}), {1}: (11, {})} | custom-call | flops 167772160 | bytes 2097152 | tf_op jit(solution)/shard_map/stage/pallas_call | solution.py:492
  30.0 1.7 %collective-permute-start.11 = (bf16[1056,128]{1,0:T(8,128)(2,1)S(1)}, bf16[1056,128]{1,0:T(8,128)(2,1)S(1)}, u32[]{:S(2)}, u32[]{:S(2)}) collective-permute-start(bf16[1056,128]{1,0:T(8,128)(2,1)S(1)} %get-tuple-element.105), channel_id=1, source_target_pairs={{0,2},{1,5},{4,0},{5,9},{8,4},{9,13},{12,8},{13,15},{14,12},{15,11... | collective-permute-start | bytes 811016 | tf_op jit(solution)/shard_map/ppermute | solution.py:51
  31.7 0.8 %stage.11 = (f32[256,1024]{1,0:T(8,128)S(1)}, f32[128,256]{1,0:T(8,128)S(1)}) custom-call(s32[1]{0:T(128)} %bitcast.me_ref, bf16[1488,128]{1,0:T(8,128)(2,1)S(1)} %collective-permute-done.4.block_ref.refs_0_.refs_10_, bf16[960,128]{1,0:T(8,128)(2,1)S(1)} %collective-permute-done.8.refs_1_, ...), custom_call_target="tpu_custom_call", output_to_operand_aliasing={{0}: (10, {}), {1}: (11, {})} | custom-call | flops 167772160 | bytes 2097152 | tf_op jit(solution)/shard_map/stage/pallas_call | solution.py:492
  32.5 1.1 %collective-permute-done.12.refs_2_ = bf16[960,128]{1,0:T(8,128)(2,1)S(1)} collective-permute-done((bf16[960,128]{1,0:T(8,128)(2,1)S(1)}, bf16[960,128]{1,0:T(8,128)(2,1)S(1)}, u32[]{:S(2)}, u32[]{:S(2)}) %collective-permute-start.12) | collective-permute-done | bytes 245792 | tf_op jit(solution)/shard_map/ppermute | solution.py:51
  33.6 0.0 collective-permute-start.13
  33.6 0.0 collective-permute-done.14.refs_0_.refs_11_
  33.6 1.2 %stage_and_half.1 = (f32[256,1024]{1,0:T(8,128)S(1)}, f32[128,256]{1,0:T(8,128)S(1)}) custom-call(s32[1]{0:T(128)} %bitcast.me_ref, bf16[1488,128]{1,0:T(8,128)(2,1)S(1)} %collective-permute-done.14.refs_0_.refs_11_, bf16[960,128]{1,0:T(8,128)(2,1)S(1)} %collective-permute-done.15.refs_1_, ...), custom_call_target="tpu_custom_call", output_to_operand_aliasing={{0}: (11, {}), {1}: (12, {})} | custom-call | flops 251658240 | bytes 3145728 | tf_op jit(solution)/shard_map/stage_and_half/pallas_call | solution.py:553
  34.8 0.3 collective-permute-done.13.refs_0_
  35.1 1.8 %features.1.unit_ref = f32[128,128]{1,0:T(8,128)S(1)} custom-call(s32[1]{0:T(128)} %bitcast.me_ref, s32[1,2]{1,0:T(1,128)S(1)} %copy-done, bf16[960,128]{1,0:T(8,128)(2,1)S(1)} %collective-permute-done.13.refs_0_, bf16[256,5120]{1,0:T(8,128)(2,1)S(1)} %get-tuple-element.71.refs_2_.refs_3_.refs_1_, ...), custom_call_target="tpu_custom_call" | custom-call | flops 1 | bytes 1 | tf_op jit(solution)/shard_map/features/pallas_call | solution.py:565
  36.9 0.3 collective-permute-start.16
  37.2 0.9 %scores.1.best_ref = f32[2,3,8,128]{3,2,1,0:T(8,128)S(1)} custom-call(f32[128,128]{1,0:T(8,128)S(1)} %features.1.unit_ref, bf16[1488,128]{1,0:T(8,128)(2,1)S(1)} %pack.1.refs_0_, bf16[1488,128]{1,0:T(8,128)(2,1)S(1)} %collective-permute-done.2.refs_1_, bf16[1488,128]{1,0:T(8,128)(2,1)S(1)} %collective-permute-done.refs_0_.refs_2_, ...), custom_call_target="tpu_custom_call" | custom-call | flops 4194304 | bytes 2097152 | tf_op jit(solution)/shard_map/scores/pallas_call | solution.py:577
  38.0 0.5 %collective-permute-done.16.block_ref = bf16[1056,128]{1,0:T(8,128)(2,1)S(1)} collective-permute-done((bf16[1056,128]{1,0:T(8,128)(2,1)S(1)}, bf16[1056,128]{1,0:T(8,128)(2,1)S(1)}, u32[]{:S(2)}, u32[]{:S(2)}) %collective-permute-start.16) | collective-permute-done | bytes 270368 | tf_op jit(solution)/shard_map/ppermute | solution.py:55
  38.5 0.8 %last_scores.1 = (f32[2,3]{1,0:T(2,128)}, f32[1,2]{1,0:T(1,128)}) custom-call(f32[128,128]{1,0:T(8,128)S(1)} %features.1.unit_ref, bf16[1056,128]{1,0:T(8,128)(2,1)S(1)} %collective-permute-done.16.block_ref, f32[2,3,8,128]{3,2,1,0:T(8,128)S(1)} %scores.1.best_ref), custom_call_target="tpu_custom_call" | custom-call | tf_op jit(solution)/shard_map/last_scores/pallas_call | solution.py:586
  (18 shorter events, 0.1 us)
Async XLA Ops:
  2.0 3.1 %collective-permute-start.2 = (bf16[1488,128]{1,0:T(8,128)(2,1)S(1)}, bf16[1488,128]{1,0:T(8,128)(2,1)S(1)}, u32[]{:S(2)}, u32[]{:S(2)}) collective-permute-start(bf16[1488,128]{1,0:T(8,128)(2,1)S(1)} %pack.1.refs_0_), channel_id=1, source_target_pairs={{0,1},{1,0},{2,3},{3,2},{4,5},{5,4},{6,7},{7,6},{8,9},{9,8},{10,11... | collective-permute-start | bytes 1142792 | tf_op jit(solution)/shard_map/ppermute | solution.py:55
  2.5 8.9 %collective-permute-start = (bf16[1488,128]{1,0:T(8,128)(2,1)S(1)}, bf16[1488,128]{1,0:T(8,128)(2,1)S(1)}, u32[]{:S(2)}, u32[]{:S(2)}) collective-permute-start(bf16[1488,128]{1,0:T(8,128)(2,1)S(1)} %pack.1.refs_0_), channel_id=1, source_target_pairs={{0,2},{1,5},{4,0},{5,9},{8,4},{9,13},{12,8},{13,15},{14,12},{15,11... | collective-permute-start | bytes 1142792 | tf_op jit(solution)/shard_map/ppermute | solution.py:51
  5.1 9.8 %collective-permute-start.3 = (bf16[1488,128]{1,0:T(8,128)(2,1)S(1)}, bf16[1488,128]{1,0:T(8,128)(2,1)S(1)}, u32[]{:S(2)}, u32[]{:S(2)}) collective-permute-start(bf16[1488,128]{1,0:T(8,128)(2,1)S(1)} %collective-permute-done.2.refs_1_), channel_id=1, source_target_pairs={{0,2},{1,5},{4,0},{5,9},{8,4},{9,13},{12,8},{13,15},{14,12},{15,11... | collective-permute-start | bytes 1142792 | tf_op jit(solution)/shard_map/ppermute | solution.py:51
  11.4 7.7 %collective-permute-start.1 = (bf16[1488,128]{1,0:T(8,128)(2,1)S(1)}, bf16[1488,128]{1,0:T(8,128)(2,1)S(1)}, u32[]{:S(2)}, u32[]{:S(2)}) collective-permute-start(bf16[1488,128]{1,0:T(8,128)(2,1)S(1)} %collective-permute-done.refs_0_.refs_2_), channel_id=1, source_target_pairs={{0,2},{1,5},{4,0},{5,9},{8,4},{9,13},{12,8},{13,15},{14,12},{15,11... | collective-permute-start | bytes 1142792 | tf_op jit(solution)/shard_map/ppermute | solution.py:51
  13.1 7.8 %collective-permute-start.6 = (bf16[1488,128]{1,0:T(8,128)(2,1)S(1)}, bf16[1488,128]{1,0:T(8,128)(2,1)S(1)}, u32[]{:S(2)}, u32[]{:S(2)}) collective-permute-start(bf16[1488,128]{1,0:T(8,128)(2,1)S(1)} %collective-permute-done.refs_0_.refs_2_), channel_id=1, source_target_pairs={{0,1},{1,0},{2,3},{3,2},{4,5},{5,4},{6,7},{7,6},{8,9},{9,8},{10,11... | collective-permute-start | bytes 1142792 | tf_op jit(solution)/shard_map/ppermute | solution.py:55
  14.9 6.1 %collective-permute-start.7 = (bf16[1488,128]{1,0:T(8,128)(2,1)S(1)}, bf16[1488,128]{1,0:T(8,128)(2,1)S(1)}, u32[]{:S(2)}, u32[]{:S(2)}) collective-permute-start(bf16[1488,128]{1,0:T(8,128)(2,1)S(1)} %collective-permute-done.3.refs_1_.refs_4_), channel_id=1, source_target_pairs={{0,1},{1,0},{2,3},{3,2},{4,5},{5,4},{6,7},{7,6},{8,9},{9,8},{10,11... | collective-permute-start | bytes 1142792 | tf_op jit(solution)/shard_map/ppermute | solution.py:55
  14.9 8.4 %collective-permute-start.5 = (bf16[1488,128]{1,0:T(8,128)(2,1)S(1)}, bf16[1488,128]{1,0:T(8,128)(2,1)S(1)}, u32[]{:S(2)}, u32[]{:S(2)}) collective-permute-start(bf16[1488,128]{1,0:T(8,128)(2,1)S(1)} %collective-permute-done.3.refs_1_.refs_4_), channel_id=1, source_target_pairs={{0,2},{1,5},{4,0},{5,9},{8,4},{9,13},{12,8},{13,15},{14,12},{15,11... | collective-permute-start | bytes 1142792 | tf_op jit(solution)/shard_map/ppermute | solution.py:51
  19.1 8.2 %collective-permute-start.4 = (bf16[1488,128]{1,0:T(8,128)(2,1)S(1)}, bf16[1488,128]{1,0:T(8,128)(2,1)S(1)}, u32[]{:S(2)}, u32[]{:S(2)}) collective-permute-start(bf16[1488,128]{1,0:T(8,128)(2,1)S(1)} %collective-permute-done.1.refs_0_.refs_6_), channel_id=1, source_target_pairs={{0,2},{1,5},{4,0},{5,9},{8,4},{9,13},{12,8},{13,15},{14,12},{15,11... | collective-permute-start | bytes 1142792 | tf_op jit(solution)/shard_map/ppermute | solution.py:51
  20.9 8.3 %collective-permute-start.9 = (bf16[1488,128]{1,0:T(8,128)(2,1)S(1)}, bf16[1488,128]{1,0:T(8,128)(2,1)S(1)}, u32[]{:S(2)}, u32[]{:S(2)}) collective-permute-start(bf16[1488,128]{1,0:T(8,128)(2,1)S(1)} %collective-permute-done.1.refs_0_.refs_6_), channel_id=1, source_target_pairs={{0,1},{1,0},{2,3},{3,2},{4,5},{5,4},{6,7},{7,6},{8,9},{9,8},{10,11... | collective-permute-start | bytes 1142792 | tf_op jit(solution)/shard_map/ppermute | solution.py:55
  23.2 5.9 %collective-permute-start.10 = (bf16[1488,128]{1,0:T(8,128)(2,1)S(1)}, bf16[1488,128]{1,0:T(8,128)(2,1)S(1)}, u32[]{:S(2)}, u32[]{:S(2)}) collective-permute-start(bf16[1488,128]{1,0:T(8,128)(2,1)S(1)} %collective-permute-done.5.refs_1_.block_ref.refs_8_), channel_id=1, source_target_pairs={{0,1},{1,0},{2,3},{3,2},{4,5},{5,4},{6,7},{7,6},{8,9},{9,8},{10,11... | collective-permute-start | bytes 1142792 | tf_op jit(solution)/shard_map/ppermute | solution.py:55
  23.3 6.7 %collective-permute-start.8 = (bf16[960,128]{1,0:T(8,128)(2,1)S(1)}, bf16[960,128]{1,0:T(8,128)(2,1)S(1)}, u32[]{:S(2)}, u32[]{:S(2)}) collective-permute-start(bf16[960,128]{1,0:T(8,128)(2,1)S(1)} %get-tuple-element.98), channel_id=1, source_target_pairs={{0,2},{1,5},{4,0},{5,9},{8,4},{9,13},{12,8},{13,15},{14,12},{15,11... | collective-permute-start | bytes 737288 | tf_op jit(solution)/shard_map/ppermute | solution.py:51
  27.3 6.2 %collective-permute-start.12 = (bf16[960,128]{1,0:T(8,128)(2,1)S(1)}, bf16[960,128]{1,0:T(8,128)(2,1)S(1)}, u32[]{:S(2)}, u32[]{:S(2)}) collective-permute-start(bf16[960,128]{1,0:T(8,128)(2,1)S(1)} %get-tuple-element.106), channel_id=1, source_target_pairs={{0,2},{1,5},{4,0},{5,9},{8,4},{9,13},{12,8},{13,15},{14,12},{15,11... | collective-permute-start | bytes 737288 | tf_op jit(solution)/shard_map/ppermute | solution.py:51
  29.2 4.4 %collective-permute-start.14 = (bf16[1488,128]{1,0:T(8,128)(2,1)S(1)}, bf16[1488,128]{1,0:T(8,128)(2,1)S(1)}, u32[]{:S(2)}, u32[]{:S(2)}) collective-permute-start(bf16[1488,128]{1,0:T(8,128)(2,1)S(1)} %collective-permute-done.4.block_ref.refs_0_.refs_10_), channel_id=1, source_target_pairs={{0,1},{1,0},{2,3},{3,2},{4,5},{5,4},{6,7},{7,6},{8,9},{9,8},{10,11... | collective-permute-start | bytes 1142792 | tf_op jit(solution)/shard_map/ppermute | solution.py:55
  30.0 6.9 %collective-permute-start.11 = (bf16[1056,128]{1,0:T(8,128)(2,1)S(1)}, bf16[1056,128]{1,0:T(8,128)(2,1)S(1)}, u32[]{:S(2)}, u32[]{:S(2)}) collective-permute-start(bf16[1056,128]{1,0:T(8,128)(2,1)S(1)} %get-tuple-element.105), channel_id=1, source_target_pairs={{0,2},{1,5},{4,0},{5,9},{8,4},{9,13},{12,8},{13,15},{14,12},{15,11... | collective-permute-start | bytes 811016 | tf_op jit(solution)/shard_map/ppermute | solution.py:51
  31.7 1.9 %collective-permute-start.15 = (bf16[960,128]{1,0:T(8,128)(2,1)S(1)}, bf16[960,128]{1,0:T(8,128)(2,1)S(1)}, u32[]{:S(2)}, u32[]{:S(2)}) collective-permute-start(bf16[960,128]{1,0:T(8,128)(2,1)S(1)} %collective-permute-done.8.refs_1_), channel_id=1, source_target_pairs={{0,1},{1,0},{2,3},{3,2},{4,5},{5,4},{6,7},{7,6},{8,9},{9,8},{10,11... | collective-permute-start | bytes 737288 | tf_op jit(solution)/shard_map/ppermute | solution.py:55
  33.6 1.5 %copy-start = (s32[1,2]{1,0:T(1,128)S(1)}, s32[1,2]{1,0:T(1,128)}, u32[]{:S(2)}) copy-start(s32[1,2]{1,0:T(1,128)} %counts_ref.1) | copy-start | bytes 28
  33.6 1.5 %collective-permute-start.13 = (bf16[960,128]{1,0:T(8,128)(2,1)S(1)}, bf16[960,128]{1,0:T(8,128)(2,1)S(1)}, u32[]{:S(2)}, u32[]{:S(2)}) collective-permute-start(bf16[960,128]{1,0:T(8,128)(2,1)S(1)} %collective-permute-done.12.refs_2_), channel_id=1, source_target_pairs={{0,1},{1,0},{2,3},{3,2},{4,5},{5,4},{6,7},{7,6},{8,9},{9,8},{10,11... | collective-permute-start | bytes 737288 | tf_op jit(solution)/shard_map/ppermute | solution.py:55
  36.9 1.6 %collective-permute-start.16 = (bf16[1056,128]{1,0:T(8,128)(2,1)S(1)}, bf16[1056,128]{1,0:T(8,128)(2,1)S(1)}, u32[]{:S(2)}, u32[]{:S(2)}) collective-permute-start(bf16[1056,128]{1,0:T(8,128)(2,1)S(1)} %collective-permute-done.11.refs_12_), channel_id=1, source_target_pairs={{0,1},{1,0},{2,3},{3,2},{4,5},{5,4},{6,7},{7,6},{8,9},{9,8},{10,11... | collective-permute-start | bytes 811016 | tf_op jit(solution)/shard_map/ppermute | solution.py:55
